TPU v7x, 32 devices: a whole 2x2x4 slice. The times are simulated.
32 devices in a mesh: groups: 2 (over x), batch: 8 (over z, y), head: 2 (over core).
Axes of the slice: x: 2, y: 2, z: 4, core: 2. Of those that a mesh axis runs over, the one named last changes fastest.
Arguments:
- x_in: bfloat16 [32, 256, 8192], P(('groups', 'batch'), None, 'head'), parts along dimension 0, may hold values from -6 to 6
- b_in: bfloat16 [32, 256, 1024], P(('groups', 'batch'), None, 'head'), parts along dimension 0, may hold values from -6 to 6
- c_in: bfloat16 [32, 256, 1024], P(('groups', 'batch'), None, 'head'), parts along dimension 0, may hold values from -6 to 6
- dt_in: float32 [32, 128, 256], P(('groups', 'batch'), 'head'), parts along dimension 0, may hold values from -6 to 6
- dt_bias: float32 [128], P('head'), may hold values from -6 to -3
- a_log: float32 [128], P('head'), may hold values from -3 to 1.1
- d_skip: float32 [128], P('head'), may hold values from 0.5 to 1.5
- conv_x: float32 [4, 8192], P(None, 'head'), may hold values from -3 to 3
- conv_bc: float32 [2, 4, 1024], P(None, None, 'head'), may hold values from -3 to 3
- par_state: float32 [16, 128, 64, 128], P(('groups', 'batch'), 'head'), parts along dimension 0, may hold values from -1.2 to 1.2
- tail_x: bfloat16 [16, 3, 8192], P(('groups', 'batch'), None, 'head'), parts along dimension 0, may hold values from -6 to 6
- tail_bc: bfloat16 [16, 2, 3, 1024], P(('groups', 'batch'), None, None, 'head'), parts along dimension 0, may hold values from -6 to 6
- counts: int32 [16], P('groups'), parts along dimension 0, may hold values from 1 to 8, 16 in all
- order: int32 [32], P('groups'), parts along dimension 0, may hold values from 0 to 15, as said below
Outputs:
- y_out: bfloat16 [32, 256, 8192], P(('groups', 'batch'), None, 'head'), parts along dimension 0
There are 2 independent parts, one for each index of `groups`. A program takes and returns all parts, laid end to end along the dimension named above; an argument that names none is the same for every part. Nothing has to cross between parts.
Inputs may be any that keep to these rules, and one draw needn't show every extreme that they name: `counts`: every parent has at least one child, 16 in all, and some parent has exactly 8. `order`: a permutation of the 16 slots; the child at position 7 takes the last slot.
All inputs are finite; a program needn't handle non-finite values.
Results may differ from a plain program's by a relative error of at most 0.0041.
Values may be sent and summed in bfloat16 or wider, within the bound.
No kernel may reach another device: no remote copies, remote signals or barrier semaphores. Data moves between devices by JAX's collectives and lax.ppermute only.
A program may use at most 128 MiB of HBM per device.

v0:
```python
import math

import jax
import jax.numpy as jnp
from jax import lax
from jax.sharding import PartitionSpec as P


def parent_rows(counts, order, children_all):
    bounds = jnp.cumsum(counts)
    slot_idx = jnp.arange(children_all, dtype=jnp.int32)
    slot_parent = jnp.sum((bounds[None, :] <= slot_idx[:, None]).astype(jnp.int32), axis=1)
    return jnp.take(slot_parent, order)


def conv_silu(tail_rows, sequence, weight):
    padded = jnp.concatenate([tail_rows, sequence], axis=1).astype(jnp.float32)
    length = sequence.shape[1]
    summed = padded[:, 0:length, :] * weight[0]
    for offset in range(1, weight.shape[0]):
        summed = summed + padded[:, offset : offset + length, :] * weight[offset]
    return jax.nn.silu(summed).astype(jnp.bfloat16)


def decay_terms(dt_raw, bias_part, alog_part):
    dt_step = jax.nn.softplus(dt_raw + bias_part[None, :, None])
    per_token = dt_step * (-jnp.exp(alog_part))[None, :, None]
    length = dt_raw.shape[2]
    position = jnp.arange(length)
    upper_ones = (position[:, None] <= position[None, :]).astype(jnp.float32)
    cumulative = jnp.einsum("chs,st->cht", per_token, upper_ones, precision=lax.Precision.HIGHEST)
    return (dt_step, cumulative)


def span_mix(x_rows, b_rows, c_rows, dt_step, cumulative):
    scores = jnp.einsum("ctn,csn->cts", c_rows, b_rows, preferred_element_type=jnp.float32)
    length = cumulative.shape[2]
    position = jnp.arange(length)
    causal = position[:, None] >= position[None, :]
    decay_gap = cumulative[:, :, :, None] - cumulative[:, :, None, :]
    factor = jnp.exp(jnp.where(causal, decay_gap, -1e30))
    mixing = (scores[:, None] * factor * dt_step[:, :, None, :]).astype(jnp.bfloat16)
    return jnp.einsum("crts,csrp->ctrp", mixing, x_rows, preferred_element_type=jnp.float32)


def state_term(c_rows, initial, cumulative):
    contracted = jnp.einsum(
        "ctn,chpn->cthp", c_rows.astype(jnp.float32), initial, precision=lax.Precision.HIGHEST
    )
    return (contracted * jnp.exp(jnp.swapaxes(cumulative, 1, 2))[..., None]).astype(jnp.bfloat16)


def local(
    x_in,
    b_in,
    c_in,
    dt_in,
    dt_bias,
    a_log,
    d_skip,
    conv_x,
    conv_bc,
    par_state,
    tail_x,
    tail_bc,
    counts,
    order,
):
    children_here, length, columns = x_in.shape
    wide_heads = dt_in.shape[1]
    head_size = columns // wide_heads
    state_size = par_state.shape[3]
    batch_ways = lax.axis_size("batch")
    head_count = wide_heads // batch_ways
    local_groups = b_in.shape[2] // state_size
    repeat_by = batch_ways // local_groups
    parents_all = counts.shape[0]
    children_all = children_here * batch_ways
    parent = parent_rows(counts, order, children_all)
    offset_row = lax.axis_index("batch") * children_here
    own_parent = lax.dynamic_slice_in_dim(parent, offset_row, children_here)
    catalog = jnp.arange(parents_all, dtype=jnp.int32)
    chooser = (own_parent[:, None] == catalog[None, :]).astype(jnp.bfloat16)
    tails_x, tails_bc = (
        lax.all_gather(tail_x, "batch", axis=0, tiled=True),
        lax.all_gather(tail_bc, "batch", axis=0, tiled=True),
    )
    near_x = jnp.dot(
        chooser, tails_x.reshape(parents_all, -1), preferred_element_type=jnp.float32
    ).astype(jnp.bfloat16)
    near_x = near_x.reshape(children_here, -1, columns)
    near_bc = jnp.dot(
        chooser, tails_bc.reshape(parents_all, -1), preferred_element_type=jnp.float32
    ).astype(jnp.bfloat16)
    near_bc = near_bc.reshape(children_here, 2, -1, local_groups * state_size)
    x_conv = conv_silu(near_x, x_in, conv_x)
    b_conv = conv_silu(near_bc[:, 0], b_in, conv_bc[0])
    c_conv = conv_silu(near_bc[:, 1], c_in, conv_bc[1])
    states, dt_heads = (
        lax.all_to_all(par_state, "batch", split_axis=1, concat_axis=0, tiled=True),
        lax.all_to_all(dt_in, "batch", split_axis=1, concat_axis=0, tiled=True),
    )
    head_start = lax.axis_index("batch") * head_count
    bias_part = lax.dynamic_slice_in_dim(dt_bias, head_start, head_count)
    alog_part = lax.dynamic_slice_in_dim(a_log, head_start, head_count)
    dt_head, cum_head = decay_terms(dt_heads, bias_part, alog_part)
    fanout = (parent[:, None] == catalog[None, :]).astype(jnp.float32)
    initial = jnp.dot(fanout, states.reshape(parents_all, -1), precision=lax.Precision.HIGHEST)
    initial = initial.reshape(children_all, head_count, head_size, state_size)
    c_wide = jnp.repeat(
        c_conv.reshape(children_here, length, local_groups, state_size), repeat_by, axis=2
    )
    skip_part = lax.dynamic_slice_in_dim(d_skip, head_start, head_count)
    x_split = x_conv.reshape(children_here, length, batch_ways, head_count * head_size)
    b_wide = jnp.repeat(
        b_conv.reshape(children_here, length, local_groups, state_size), repeat_by, axis=2
    )
    x_heads, b_heads, c_heads = (
        lax.all_to_all(x_split, "batch", split_axis=2, concat_axis=0, tiled=True),
        lax.all_to_all(b_wide, "batch", split_axis=2, concat_axis=0, tiled=True),
        lax.all_to_all(c_wide, "batch", split_axis=2, concat_axis=0, tiled=True),
    )
    c_heads = c_heads.reshape(children_all, length, state_size)
    b_heads = b_heads.reshape(children_all, length, state_size)
    x_heads = x_heads.reshape(children_all, length, head_count, head_size)
    carried = state_term(c_heads, initial, cum_head)
    carried = lax.optimization_barrier(carried).astype(jnp.float32)
    block_size = math.gcd(children_all, 8)
    within = lax.map(
        lambda operands: span_mix(*operands),
        (
            x_heads.reshape(-1, block_size, length, head_count, head_size),
            b_heads.reshape(-1, block_size, length, state_size),
            c_heads.reshape(-1, block_size, length, state_size),
            dt_head.reshape(-1, block_size, head_count, length),
            cum_head.reshape(-1, block_size, head_count, length),
        ),
    )
    within = within.reshape(children_all, length, head_count, head_size)
    mixed = within + carried + skip_part[None, None, :, None] * x_heads.astype(jnp.float32)
    mixed = mixed.astype(jnp.bfloat16).reshape(children_all, length, 1, head_count * head_size)
    returned = lax.all_to_all(mixed, "batch", split_axis=0, concat_axis=2, tiled=True)
    return returned.reshape(children_here, length, columns)


def solution(mesh):
    placed = (
        P(("groups", "batch"), None, "head"),
        P(("groups", "batch"), None, "head"),
        P(("groups", "batch"), None, "head"),
        P(("groups", "batch"), "head", None),
        P("head"),
        P("head"),
        P("head"),
        P(None, "head"),
        P(None, None, "head"),
        P(("groups", "batch"), "head", None, None),
        P(("groups", "batch"), None, "head"),
        P(("groups", "batch"), None, None, "head"),
        P("groups"),
        P("groups"),
    )
    return jax.shard_map(
        local,
        mesh=mesh,
        in_specs=placed,
        out_specs=P(("groups", "batch"), None, "head"),
        check_vma=False,
    )
```

profile of v0, /device:TPU:0, one launch (start us, length us, event | category | flops | bytes accessed | tf_op | source)
XLA Modules:
  0.0 397.2 jit_solution(10363734706234117650)
XLA Ops:
  0.0 1.7 copy.43
  1.7 7.3 %all-to-all-start.3 = ((f32[2,64,256]{2,0,1:T(2,128)}), f32[2,64,256]{2,0,1:T(2,128)S(1)}, u32[]{:S(2)}, u32[]{:S(2)}) async-start(f32[2,64,256]{2,0,1:T(2,128)} %copy.43), calls=%async_computation.3 | async-start | bytes 262144 | tf_op jit(solution)/shard_map/all_to_all | solution.py:101
  8.9 0.8 reduce-window.8
  9.8 0.1 convert_reduce_fusion
  9.9 0.7 compare_select_fusion.2
  10.5 0.7 gather_fusion
  11.2 0.7 and_select_fusion
  11.9 31.4 %all_gather.7 = bf16[8,2,3,512]{3,1,2,0:T(2,128)(2,1)S(1)} all-gather(bf16[1,2,3,512]{3,1,2,0:T(2,128)(2,1)} %param.27), channel_id=1, replica_groups=mesh['groups'=2,'batch'=8,'head'=2] {'batch'}, dimensions={0}, use_global_device_ids=true | all-gather | bytes 55296 | tf_op jit(solution)/shard_map/all_gather | solution.py:86
  43.3 0.1 reshape.131
  43.4 0.1 dynamic_slice.30
  43.5 0.2 convolution_convert_fusion.1
  43.7 0.9 fusion.55
  44.6 1.4 maximum_convert_fusion.1
  46.1 0.7 copy_bitcast_fusion.1
  46.7 1.2 broadcast_in_dim.21
  47.9 5.3 %all-to-all-start.1 = ((bf16[2,256,8,128]{3,1,0,2:T(8,128)(2,1)}), bf16[2,256,8,128]{3,1,0,2:T(8,128)(2,1)S(1)}, u32[]{:S(2)}, u32[]{:S(2)}) async-start(bf16[2,256,8,128]{3,1,0,2:T(8,128)(2,1)} %bitcast.21), calls=%async_computation.1 | async-start | bytes 2097152 | tf_op jit(solution)/shard_map/all_to_all | solution.py:121
  53.2 0.7 copy_bitcast_fusion
  53.9 18.4 %all-to-all-done.1 = bf16[2,256,8,128]{3,1,0,2:T(8,128)(2,1)S(1)} async-done(((bf16[2,256,8,128]{3,1,0,2:T(8,128)(2,1)}), bf16[2,256,8,128]{3,1,0,2:T(8,128)(2,1)S(1)}, u32[]{:S(2)}, u32[]{:S(2)}) %all-to-all-start.1) | async-done | bytes 1048608 | tf_op jit(solution)/shard_map/all_to_all | solution.py:121
  72.3 1.2 broadcast_in_dim.24
  73.4 3.6 all-to-all-start.2
  77.0 43.4 %all_gather.6 = bf16[8,3,4096]{2,1,0:T(4,128)(2,1)S(1)} all-gather(bf16[1,3,4096]{2,1,0:T(4,128)(2,1)S(1)} %copy-done.1), channel_id=1, replica_groups=mesh['groups'=2,'batch'=8,'head'=2] {'batch'}, dimensions={0}, use_global_device_ids=true | all-gather | bytes 221184 | tf_op jit(solution)/shard_map/all_gather | solution.py:85
  120.4 0.1 copy.54
  120.6 4.5 %all-to-all-start.4 = ((f32[1,64,64,128]{3,2,0,1:T(8,128)}), f32[1,64,64,128]{3,2,0,1:T(8,128)}, u32[]{:S(2)}, u32[]{:S(2)}) async-start(f32[1,64,64,128]{3,2,0,1:T(8,128)} %bitcast.142), calls=%async_computation.4 | async-start | bytes 4194304 | tf_op jit(solution)/shard_map/all_to_all | solution.py:100
  125.1 0.3 convolution_convert_fusion
  125.4 3.5 maximum_convert_fusion
  129.0 6.4 %multiply_convert_fusion.5 = bf16[2,256,4096]{2,1,0:T(8,128)(2,1)} fusion(f32[2,259,4096]{2,1,0:T(8,128)S(1)} %maximum_convert_fusion, f32[4096]{0:T(1024)S(1)} %bitcast.150, f32[4096]{0:T(1024)S(1)} %bitcast.151, f32[4096]{0:T(1024)S(1)} %bitcast.149, f32[4096]{0:T(1024)S(1)} %bitcast.148), kind=kLoop, calls=%fused_computation.36 | loop fusion | flops 25165824 | bytes 37814272 | tf_op jit(solution)/shard_map/convert_element_type | solution.py:22
  135.4 6.4 %copy.55 = bf16[64,8,8,512]{3,2,1,0:T(8,128)(2,1)} copy(bf16[64,8,8,512]{3,1,2,0:T(8,128)(2,1)} %bitcast.136) | data formatting | bytes 8388608
  141.8 7.5 %copy.39 = bf16[2,256,8,512]{1,3,0,2:T(8,128)(2,1)} copy(bf16[2,256,8,512]{3,2,1,0:T(8,128)(2,1)} %bitcast.137) | data formatting | bytes 8388608 | tf_op jit(solution)/shard_map/reshape | solution.py:114
  149.3 17.6 %all-to-all-done.4 = f32[1,64,64,128]{3,2,0,1:T(8,128)} async-done(((f32[1,64,64,128]{3,2,0,1:T(8,128)}), f32[1,64,64,128]{3,2,0,1:T(8,128)}, u32[]{:S(2)}, u32[]{:S(2)}) %all-to-all-start.4) | async-done | bytes 2097184 | tf_op jit(solution)/shard_map/all_to_all | solution.py:100
  166.9 4.8 %all-to-all-start = ((bf16[2,256,8,512]{1,3,0,2:T(8,128)(2,1)}), bf16[2,256,8,512]{1,3,0,2:T(8,128)(2,1)}, u32[]{:S(2)}, u32[]{:S(2)}) async-start(bf16[2,256,8,512]{1,3,0,2:T(8,128)(2,1)} %copy.39), calls=%async_computation | async-start | bytes 8388608 | tf_op jit(solution)/shard_map/all_to_all | solution.py:119
  171.7 0.1 dynamic_slice.31
  171.9 0.1 exponential_negate_fusion
  172.0 0.1 bitcast_add_fusion.2
  172.0 0.3 fusion.35
  172.4 0.1 compare_select_fusion
  172.5 3.3 reshape.140
  175.8 3.4 fusion.48
  179.2 6.1 %multiply_convert_fusion.4 = bf16[16,256,8,64]{1,3,2,0:T(8,128)(2,1)} fusion(f32[16,256,8]{1,2,0:T(8,128)S(1)} %exponential_bitcast_fusion, bf16[16,256,128,1]{2,1,3,0:T(8,128)(2,1)S(1)} %bitcast.134, f32[16,8,64,128]{3,0,2,1:T(8,128)S(1)} %fusion.48), kind=kOutput, calls=%fused_computation.35 | convolution fusion | flops 3225419776 | bytes 9568256 | tf_op jit(solution)/shard_map/ctn,chpn->cthp/dot_general | solution.py:47
  185.4 76.1 %all-to-all-done = bf16[2,256,8,512]{1,3,0,2:T(8,128)(2,1)} async-done(((bf16[2,256,8,512]{1,3,0,2:T(8,128)(2,1)}), bf16[2,256,8,512]{1,3,0,2:T(8,128)(2,1)}, u32[]{:S(2)}, u32[]{:S(2)}) %all-to-all-start) | async-done | bytes 4194336 | tf_op jit(solution)/shard_map/all_to_all | solution.py:119
  261.5 15.5 %while.10 = (s32[]{:T(128)}, f32[2,8,256,8,64]{2,4,3,1,0:T(8,128)}, bf16[2,8,256,8,64]{2,4,3,1,0:T(8,128)(2,1)}, bf16[2,8,256,128]{3,2,1,0:T(8,128)(2,1)S(1)}, b...) while((s32[]{:T(128)}, f32[2,8,256,8,64]{2,4,3,1,0:T(8,128)}, ...), condition=%wide.region_3.4_spmd, body=%wide.region_2.3_spmd.sunk | while | flops 692125696 | bytes 12126297 | solution.py:129
  261.5 0.4 fusion.69
  262.0 7.2 %bitcast_dynamic-update-slice_fusion.2 = f32[2,8,256,8,64]{2,4,3,1,0:T(8,128)} fusion(f32[2,8,256,8,64]{2,4,3,1,0:T(8,128)} %get-tuple-element.131, s32[]{:T(128)} %get-tuple-element.130, f32[8,8,256]{2,1,0:T(8,128)S(1)} %get-tuple-element.120, f32[8,8,256]{2,1,0:T(8,128)S(1)} %get-tuple-element.121, f32[8,256,256]{2,1,0:T(8,128)S(1)} %fusion.69, ...), kind=kOutput, calls=%fused_computation.9.clone.1 | convolution fusion | flops 557842432 | bytes 8651776 | tf_op jit(solution)/shard_map/while/body/eval_jaxpr/crts,csrp->ctrp/dot_general | solution.py:43
  269.2 0.4 fusion.69
  269.7 7.2 %bitcast_dynamic-update-slice_fusion.2 = f32[2,8,256,8,64]{2,4,3,1,0:T(8,128)} fusion(f32[2,8,256,8,64]{2,4,3,1,0:T(8,128)} %get-tuple-element.131, s32[]{:T(128)} %get-tuple-element.130, f32[8,8,256]{2,1,0:T(8,128)S(1)} %get-tuple-element.120, f32[8,8,256]{2,1,0:T(8,128)S(1)} %get-tuple-element.121, f32[8,256,256]{2,1,0:T(8,128)S(1)} %fusion.69, ...), kind=kOutput, calls=%fused_computation.9.clone.1 | convolution fusion | flops 557842432 | bytes 8651776 | tf_op jit(solution)/shard_map/while/body/eval_jaxpr/crts,csrp->ctrp/dot_general | solution.py:43
  276.9 8.2 %fusion.21 = bf16[16,256,8,64]{1,3,2,0:T(8,128)(2,1)S(1)} fusion(bf16[16,256,8,64]{1,3,2,0:T(8,128)(2,1)} %bitcast.68, f32[2,8,256,8,64]{2,4,3,1,0:T(8,128)} %get-tuple-element.42, bf16[16,256,8,64]{1,3,2,0:T(8,128)(2,1)} %multiply_convert_fusion.4, f32[8]{0:T(128)S(1)} %dynamic_slice.33), kind=kLoop, calls=%fused_computation.33 | loop fusion | flops 12582912 | bytes 20971552 | tf_op jit(solution)/shard_map/convert_element_type | solution.py:141
  285.1 96.8 %all_to_all.90 = bf16[16,256,1,512]{1,3,2,0:T(8,128)(2,1)} all-to-all(bf16[16,256,1,512]{1,3,2,0:T(8,128)(2,1)S(1)} %bitcast.139), channel_id=1, replica_groups=mesh['groups'=2,'batch'=8,'head'=2] {'batch'}, dimensions={0} | all-to-all | bytes 8388608 | tf_op jit(solution)/shard_map/all_to_all | solution.py:142
  381.9 7.9 %copy.49 = bf16[2,256,8,1,512]{4,2,1,0,3:T(8,128)(2,1)} copy(bf16[2,256,8,1,512]{1,4,0,2,3:T(8,128)(2,1)} %bitcast.138) | data formatting | bytes 8388608 | tf_op jit(solution)/shard_map/all_to_all | solution.py:142
  389.8 7.4 %reshape.142 = bf16[2,256,4096]{2,1,0:T(8,128)(2,1)} reshape(bf16[2,256,8,1,512]{4,2,1,0,3:T(8,128)(2,1)} %copy.49) | data formatting | bytes 8388608 | tf_op jit(solution)/shard_map/reshape | solution.py:143
  (26 shorter events, 0.4 us)
Async XLA Ops:
  1.7 45.1 %all-to-all-start.3 = ((f32[2,64,256]{2,0,1:T(2,128)}), f32[2,64,256]{2,0,1:T(2,128)S(1)}, u32[]{:S(2)}, u32[]{:S(2)}) async-start(f32[2,64,256]{2,0,1:T(2,128)} %copy.43), calls=%async_computation.3 | async-start | bytes 262144 | tf_op jit(solution)/shard_map/all_to_all | solution.py:101
  46.0 30.9 %copy-start.1 = (bf16[1,3,4096]{2,1,0:T(4,128)(2,1)S(1)}, bf16[1,3,4096]{2,1,0:T(4,128)(2,1)}, u32[]{:S(2)}) copy-start(bf16[1,3,4096]{2,1,0:T(4,128)(2,1)} %param.26) | copy-start | bytes 73732
  47.9 24.3 %all-to-all-start.1 = ((bf16[2,256,8,128]{3,1,0,2:T(8,128)(2,1)}), bf16[2,256,8,128]{3,1,0,2:T(8,128)(2,1)S(1)}, u32[]{:S(2)}, u32[]{:S(2)}) async-start(bf16[2,256,8,128]{3,1,0,2:T(8,128)(2,1)} %bitcast.21), calls=%async_computation.1 | async-start | bytes 2097152 | tf_op jit(solution)/shard_map/all_to_all | solution.py:121
  73.4 47.2 %all-to-all-start.2 = ((bf16[2,256,8,128]{3,1,0,2:T(8,128)(2,1)}), bf16[2,256,8,128]{3,1,0,2:T(8,128)(2,1)S(1)}, u32[]{:S(2)}, u32[]{:S(2)}) async-start(bf16[2,256,8,128]{3,1,0,2:T(8,128)(2,1)} %bitcast.30), calls=%async_computation.2 | async-start | bytes 2097152 | tf_op jit(solution)/shard_map/all_to_all | solution.py:120
  120.6 8.3 %copy-start = (f32[4,4096]{1,0:T(4,128)S(1)}, f32[4,4096]{1,0:T(4,128)}, u32[]{:S(2)}) copy-start(f32[4,4096]{1,0:T(4,128)} %param.23) | copy-start | bytes 196612
  120.6 46.3 %all-to-all-start.4 = ((f32[1,64,64,128]{3,2,0,1:T(8,128)}), f32[1,64,64,128]{3,2,0,1:T(8,128)}, u32[]{:S(2)}, u32[]{:S(2)}) async-start(f32[1,64,64,128]{3,2,0,1:T(8,128)} %bitcast.142), calls=%async_computation.4 | async-start | bytes 4194304 | tf_op jit(solution)/shard_map/all_to_all | solution.py:100
  141.8 29.9 %copy-start.2 = (f32[64]{0:T(128)S(1)}, f32[64]{0:T(128)}, u32[]{:S(2)}) copy-start(f32[64]{0:T(128)} %param.20) | copy-start | bytes 772
  141.8 30.0 %copy-start.3 = (f32[64]{0:T(128)S(1)}, f32[64]{0:T(128)}, u32[]{:S(2)}) copy-start(f32[64]{0:T(128)} %param.22) | copy-start | bytes 772
  141.8 30.1 %copy-start.4 = (f32[64]{0:T(128)S(1)}, f32[64]{0:T(128)}, u32[]{:S(2)}) copy-start(f32[64]{0:T(128)} %param.21) | copy-start | bytes 772
  166.9 94.6 %all-to-all-start = ((bf16[2,256,8,512]{1,3,0,2:T(8,128)(2,1)}), bf16[2,256,8,512]{1,3,0,2:T(8,128)(2,1)}, u32[]{:S(2)}, u32[]{:S(2)}) async-start(bf16[2,256,8,512]{1,3,0,2:T(8,128)(2,1)} %copy.39), calls=%async_computation | async-start | bytes 8388608 | tf_op jit(solution)/shard_map/all_to_all | solution.py:119
where the time goes:
time: 399 us; the launch traced here: 397 us
  blocking collectives  172 us (43%)
  waiting for transfers between devices  112 us (28%)
  local copies, waits for them, and re-layouts  38.7 us (10%)
  matrix products  25.7 us (6%)
  starting transfers between devices  25.4 us (6%)
  other arithmetic  23.5 us (6%)
    all_to_all x1, blocking collectives, local(): lax.all_to_all(mixed, 'batch', split_axis=0, concat_axis=2, tiled=True)  96.8 us
    all_to_all x1, waiting for transfers between devices, local(): lax.all_to_all(x_split, 'batch', split_axis=2, concat_axis=0, tiled=True)  76.1 us
    all_gather x1, blocking collectives, local(): lax.all_gather(tail_x, 'batch', axis=0, tiled=True)  43.4 us
    all_gather x1, blocking collectives, local(): lax.all_gather(tail_bc, 'batch', axis=0, tiled=True)  31.4 us
    all_to_all x1, waiting for transfers between devices, local(): lax.all_to_all(c_wide, 'batch', split_axis=2, concat_axis=0, tiled=True)  18.4 us
    all_to_all x1, waiting for transfers between devices, local(): lax.all_to_all(par_state, 'batch', split_axis=1, concat_axis=0, tiled=True)  17.6 us
    dot_general x2, matrix products, span_mix(): jnp.einsum('crts,csrp->ctrp', mixing, x_rows, preferred_element_type=jnp....  14.5 us
    unnamed x13, local copies, waits for them, and re-layouts  8.21 us
  transfers between devices with their start and end apart: 5, of which 3 were waited for; matrix products, arithmetic and copies ran while one was open for 11% of the time, Pallas kernels for 0%

commit v1 on v0

v1 whole, which is shorter than its diff:
```python
import functools

import jax
import jax.numpy as jnp
from jax import lax
from jax.experimental import pallas as pl
from jax.experimental.pallas import tpu as pltpu
from jax.sharding import PartitionSpec as P

VMEM_LIMIT = 48 * 1024 * 1024


def parent_of(counts, order):
    index = jnp.arange(counts.shape[0], dtype=jnp.int32)
    bounds = jnp.sum(jnp.where(index[None, :] <= index[:, None], counts[None, :], 0), axis=1)
    return jnp.sum((bounds[None, :] <= order[:, None]).astype(jnp.int32), axis=1)


def conv_silu(padded, tail, rows, taps):
    length = rows.shape[0]
    reach = taps.shape[0] - 1
    padded[8 - reach : 8, :] = tail.astype(jnp.float32)
    padded[8 : 8 + length, :] = rows.astype(jnp.float32)
    total = padded[8 - reach : 8 - reach + length, :] * taps[0:1, :]
    for k in range(1, reach + 1):
        total = total + padded[8 - reach + k : 8 - reach + k + length, :] * taps[k : k + 1, :]
    return (total / (1.0 + jnp.exp(-total))).astype(jnp.bfloat16)


def within_kernel(
    parent_ref,
    x_ref,
    b_ref,
    c_ref,
    dt_ref,
    bias_ref,
    alog_ref,
    skip_ref,
    taps_x_ref,
    taps_bc_ref,
    tail_x_ref,
    tail_bc_ref,
    mixed_ref,
    c_out_ref,
    grow_ref,
    padded,
):
    length = x_ref.shape[1]
    heads = dt_ref.shape[1]
    width = x_ref.shape[2] // heads
    b_conv = conv_silu(padded, tail_bc_ref[0, 0], b_ref[0], taps_bc_ref[0])
    c_conv = conv_silu(padded, tail_bc_ref[0, 1], c_ref[0], taps_bc_ref[1])
    c_out_ref[0] = c_conv
    scores = lax.dot_general(
        c_conv, b_conv, (((1,), (1,)), ((), ())), preferred_element_type=jnp.float32
    )
    raw = dt_ref[0] + bias_ref[...]
    step = jnp.maximum(raw, 0.0) + jnp.log1p(jnp.exp(-jnp.abs(raw)))
    per_token = step * (-jnp.exp(alog_ref[...]))
    row = lax.broadcasted_iota(jnp.int32, (length, length), 0)
    col = lax.broadcasted_iota(jnp.int32, (length, length), 1)
    upper = (row <= col).astype(jnp.float32)
    total = lax.dot_general(
        per_token,
        upper,
        (((1,), (0,)), ((), ())),
        precision=lax.Precision.HIGHEST,
        preferred_element_type=jnp.float32,
    )
    total_t = total.T
    grow_ref[0, 0] = jnp.exp(total_t)
    causal = row >= col
    low = lax.broadcasted_iota(jnp.int32, (length, 2 * width), 1) < width
    for pair in range(heads // 2):
        lanes = slice(pair * 2 * width, (pair + 1) * 2 * width)
        x_conv = conv_silu(
            padded, tail_x_ref[0, :, lanes], x_ref[0, :, lanes], taps_x_ref[:, lanes]
        )
        parts = []
        for head in (2 * pair, 2 * pair + 1):
            gap = total_t[:, head : head + 1] - total[head : head + 1, :]
            factor = jnp.exp(jnp.where(causal, gap, -1e30))
            mixing = (scores * factor * step[head : head + 1, :]).astype(jnp.bfloat16)
            parts.append(jnp.dot(mixing, x_conv, preferred_element_type=jnp.float32))
        mixed_ref[0, :, lanes] = (
            jnp.where(low, parts[0], parts[1]) + skip_ref[:, lanes] * x_conv.astype(jnp.float32)
        )


def carried_kernel(state_ref, c_ref, grow_ref, mixed_ref, y_ref):
    sources, _, part, width, size = state_ref.shape
    length = c_ref.shape[1]
    low = lax.broadcasted_iota(jnp.int32, (length, 2 * width), 1) < width
    c_conv = c_ref[0]
    for source in range(sources):
        state = state_ref[source, 0].reshape(part * width, size)
        term = lax.dot_general(
            c_conv, state, (((1,), (1,)), ((), ())), preferred_element_type=jnp.float32
        )
        for pair in range(part // 2):
            head = source * part + 2 * pair
            grow = jnp.where(
                low, grow_ref[0, 0, :, head : head + 1], grow_ref[0, 0, :, head + 1 : head + 2]
            )
            here = slice(2 * pair * width, (2 * pair + 2) * width)
            lanes = slice(head * width, (head + 2) * width)
            carried = (term[:, here] * grow).astype(jnp.bfloat16).astype(jnp.float32)
            y_ref[0, :, lanes] = (mixed_ref[0, :, lanes] + carried).astype(jnp.bfloat16)


def pick_kernel(parent_ref, state_ref, out_ref):
    out_ref[...] = state_ref[...]


def local(
    x_in,
    b_in,
    c_in,
    dt_in,
    dt_bias,
    a_log,
    d_skip,
    conv_x,
    conv_bc,
    par_state,
    tail_x,
    tail_bc,
    counts,
    order,
):
    kids, length, columns = x_in.shape
    heads = dt_in.shape[1]
    width, size = par_state.shape[2:]
    ways = lax.axis_size("batch")
    groups = b_in.shape[2] // size
    per_group = heads // groups
    part = heads // ways
    wide = per_group * width
    reach = tail_x.shape[1]
    parents_all = counts.shape[0]
    kids_all = order.shape[0]

    parent = parent_of(counts, order)
    own = lax.dynamic_slice_in_dim(parent, lax.axis_index("batch") * kids, kids)

    sent = par_state.astype(jnp.bfloat16).reshape(ways, part, width, size)
    shares = lax.all_to_all(sent, "batch", split_axis=0, concat_axis=0, tiled=True)

    tails = jnp.concatenate([tail_x.reshape(-1), tail_bc.reshape(-1)])
    tails = jnp.broadcast_to(tails[None], (ways, tails.shape[0]))
    tails = lax.all_to_all(tails, "batch", split_axis=0, concat_axis=0, tiled=True)
    tails_x = tails[:, : reach * columns].reshape(parents_all, reach, columns)
    tails_bc = tails[:, reach * columns :].reshape(parents_all, 2, reach, groups * size)

    picked = pl.pallas_call(
        pick_kernel,
        grid_spec=pltpu.PrefetchScalarGridSpec(
            num_scalar_prefetch=1,
            grid=(kids_all,),
            in_specs=[pl.BlockSpec((1, part, width, size), lambda i, p: (p[i], 0, 0, 0))],
            out_specs=pl.BlockSpec((1, part, width, size), lambda i, p: (i, 0, 0, 0)),
        ),
        out_shape=jax.ShapeDtypeStruct((kids_all, part, width, size), jnp.bfloat16),
        cost_estimate=pl.CostEstimate(
            flops=0, bytes_accessed=4 * kids_all * part * width * size, transcendentals=0
        ),
        name="pick_states",
    )(parent, shares)
    states = lax.all_to_all(
        picked.reshape(ways, kids, part, width, size), "batch", split_axis=0, concat_axis=0, tiled=True
    )

    skip_row = jnp.repeat(d_skip, width)[None, :]
    mixed, c_conv, grow = pl.pallas_call(
        within_kernel,
        grid_spec=pltpu.PrefetchScalarGridSpec(
            num_scalar_prefetch=1,
            grid=(kids, groups),
            in_specs=[
                pl.BlockSpec((1, length, wide), lambda c, q, p: (c, 0, q)),
                pl.BlockSpec((1, length, size), lambda c, q, p: (c, 0, q)),
                pl.BlockSpec((1, length, size), lambda c, q, p: (c, 0, q)),
                pl.BlockSpec((1, per_group, length), lambda c, q, p: (c, q, 0)),
                pl.BlockSpec((per_group, 1), lambda c, q, p: (q, 0)),
                pl.BlockSpec((per_group, 1), lambda c, q, p: (q, 0)),
                pl.BlockSpec((1, wide), lambda c, q, p: (0, q)),
                pl.BlockSpec((reach + 1, wide), lambda c, q, p: (0, q)),
                pl.BlockSpec((2, reach + 1, size), lambda c, q, p: (0, 0, q)),
                pl.BlockSpec((1, reach, wide), lambda c, q, p: (p[c], 0, q)),
                pl.BlockSpec((1, 2, reach, size), lambda c, q, p: (p[c], 0, 0, q)),
            ],
            out_specs=[
                pl.BlockSpec((1, length, wide), lambda c, q, p: (c, 0, q)),
                pl.BlockSpec((1, length, size), lambda c, q, p: (c, 0, q)),
                pl.BlockSpec((1, 1, length, per_group), lambda c, q, p: (c, q, 0, 0)),
            ],
            scratch_shapes=[pltpu.VMEM((8 + length, size), jnp.float32)],
        ),
        out_shape=[
            jax.ShapeDtypeStruct((kids, length, columns), jnp.float32),
            jax.ShapeDtypeStruct((kids, length, groups * size), jnp.bfloat16),
            jax.ShapeDtypeStruct((kids, groups, length, per_group), jnp.float32),
        ],
        compiler_params=pltpu.CompilerParams(vmem_limit_bytes=VMEM_LIMIT),
        cost_estimate=pl.CostEstimate(
            flops=4 * kids * heads * length * length * width,
            bytes_accessed=6 * kids * length * columns,
            transcendentals=kids * heads * length * length,
        ),
        name="within",
    )(
        own,
        x_in,
        b_in,
        c_in,
        dt_in,
        dt_bias[:, None],
        a_log[:, None],
        skip_row,
        conv_x,
        conv_bc,
        tails_x,
        tails_bc,
    )

    sources = per_group // part
    return pl.pallas_call(
        carried_kernel,
        grid=(kids, groups),
        in_specs=[
            pl.BlockSpec((sources, 1, part, width, size), lambda c, q: (q, c, 0, 0, 0)),
            pl.BlockSpec((1, length, size), lambda c, q: (c, 0, q)),
            pl.BlockSpec((1, 1, length, per_group), lambda c, q: (c, q, 0, 0)),
            pl.BlockSpec((1, length, wide), lambda c, q: (c, 0, q)),
        ],
        out_specs=pl.BlockSpec((1, length, wide), lambda c, q: (c, 0, q)),
        out_shape=jax.ShapeDtypeStruct((kids, length, columns), jnp.bfloat16),
        compiler_params=pltpu.CompilerParams(vmem_limit_bytes=VMEM_LIMIT),
        cost_estimate=pl.CostEstimate(
            flops=2 * kids * length * columns * size,
            bytes_accessed=8 * kids * length * columns,
            transcendentals=0,
        ),
        name="carried",
    )(states, c_conv, grow, mixed)


def solution(mesh):
    rows, cols = P(("groups", "batch"), None, "head"), P(("groups", "batch"), "head")
    placed = (
        rows,
        rows,
        rows,
        cols,
        P("head"),
        P("head"),
        P("head"),
        P(None, "head"),
        P(None, None, "head"),
        cols,
        rows,
        P(("groups", "batch"), None, None, "head"),
        P("groups"),
        P("groups"),
    )
    return jax.shard_map(local, mesh=mesh, in_specs=placed, out_specs=rows, check_vma=False)
```

time: 399 us -> 116 us (0.29)
  blocking collectives: 172 us -> 0 us
  waiting for transfers between devices: 112 us -> 40.2 us
  Pallas kernels: 0 us -> 42 us
  local copies, waits for them, and re-layouts: 38.7 us -> 10.6 us
  matrix products: 25.7 us -> 0 us
  other arithmetic: 23.5 us -> 5.58 us
  starting transfers between devices: 25.4 us -> 16.9 us
    all_to_all x1 -> x0, blocking collectives: 96.8 us -> none  [local(): lax.all_to_all(mixed, 'batch', split_axis=0, concat_axis=2, tiled=True)]
    all_gather x2 -> x0, blocking collectives: 74.9 us -> none  [the longest x1 43.4 us: local(): lax.all_gather(tail_x, 'batch', axis=0, tiled=True)]
    all_to_all x5 -> x3, waiting for transfers between devices: 112 us -> 40.2 us  [the longest x1 21.8 us: local(): lax.all_to_all(sent, 'batch', split_axis=0, concat_axis=0, tiled=True)]
    pallas_call x0 -> x3, Pallas kernels: none -> 42 us  [the longest x1 21.7 us: local(): pl.pallas_call(within_kernel, grid_spec=pltpu.PrefetchScalarGridSpec(num_...]
    dot_general x9 -> x0, matrix products: 25.7 us -> none  [the longest x2 14.5 us: span_mix(): jnp.einsum('crts,csrp->ctrp', mixing, x_rows, preferred_element_type=jnp....]
    reshape x6 -> x4, local copies, waits for them, and re-layouts: 18.3 us -> 0.43 us  [the longest x1 0.29 us: local(): tails_x = tails[:, :reach * columns].reshape(parents_all, reach, columns)]
    convert_element_type x4 -> x1, other arithmetic: 19.5 us -> 2.82 us  [local(): sent = par_state.astype(jnp.bfloat16).reshape(ways, part, width, size)]
    all_to_all x5 -> x3, starting transfers between devices: 25.4 us -> 16.9 us  [the longest x1 7.28 us: local(): lax.all_to_all(sent, 'batch', split_axis=0, concat_axis=0, tiled=True)]
  transfers between devices with their start and end apart: 5 -> 3, of which waited for: 3 -> 2; matrix products, arithmetic and copies ran while one was open for 11% -> 5% of each run, Pallas kernels for 0% -> 28%
where the time goes in v1:
time: 116 us; the launch traced here: 115 us
  Pallas kernels  42 us (36%)
  waiting for transfers between devices  40.2 us (35%)
  starting transfers between devices  16.9 us (15%)
  local copies, waits for them, and re-layouts  10.6 us (9%)
  other arithmetic  5.58 us (5%)
    all_to_all x1, waiting for transfers between devices, local(): lax.all_to_all(sent, 'batch', split_axis=0, concat_axis=0, tiled=True)  21.8 us
    pallas_call x1, Pallas kernels, local(): pl.pallas_call(within_kernel, grid_spec=pltpu.PrefetchScalarGridSpec(num_...  21.7 us
    all_to_all x1, waiting for transfers between devices, local(): lax.all_to_all(picked.reshape(ways, kids, part, width, size), 'batch', sp...  18.4 us
    pallas_call x1, Pallas kernels, local(): pl.pallas_call(pick_kernel, grid_spec=pltpu.PrefetchScalarGridSpec(num_sc...  10.3 us
    pallas_call x1, Pallas kernels, local(): pl.pallas_call(carried_kernel, grid=(kids, groups), in_specs=[pl.BlockSpe...  10 us
    unnamed x38, local copies, waits for them, and re-layouts  8.32 us
    all_to_all x1, starting transfers between devices, local(): lax.all_to_all(sent, 'batch', split_axis=0, concat_axis=0, tiled=True)  7.28 us
    all_to_all x1, starting transfers between devices, local(): lax.all_to_all(picked.reshape(ways, kids, part, width, size), 'batch', sp...  6 us
  transfers between devices with their start and end apart: 3, of which 2 were waited for; matrix products, arithmetic and copies ran while one was open for 5% of the time, Pallas kernels for 28%

profile of v1, /device:TPU:0, one launch (start us, length us, event | category | flops | bytes accessed | tf_op | source)
XLA Modules:
  0.0 115.4 jit_solution(15283755386302558950)
XLA Ops:
  0.0 0.0 copy-start.10
  0.0 0.0 copy-start.9
  0.0 2.8 %convert_element_type.7 = bf16[1,64,64,128]{3,2,1,0:T(8,128)(2,1)} convert(f32[1,64,64,128]{3,2,1,0:T(8,128)} %param.23) | non-fusion elementwise | flops 524288 | bytes 3145728 | tf_op jit(solution)/shard_map/convert_element_type | solution.py:146
  2.8 7.3 %all-to-all-start = ((bf16[8,8,64,128]{3,2,1,0:T(8,128)(2,1)}), bf16[8,8,64,128]{3,2,1,0:T(8,128)(2,1)S(1)}, u32[]{:S(2)}, u32[]{:S(2)}) async-start(bf16[8,8,64,128]{3,2,1,0:T(8,128)(2,1)} %bitcast), calls=%async_computation | async-start | bytes 2097152 | tf_op jit(solution)/shard_map/all_to_all | solution.py:147
  10.1 0.0 copy-done.10
  10.1 0.0 copy-done.9
  10.2 0.3 broadcast_in_dim.37
  10.5 0.6 broadcast.6
  11.1 2.1 %reduce = bf16[8,15360]{1,0:T(8,128)(2,1)S(1)} reduce(bf16[8,1,15360]{2,1,0:T(2,128)(2,1)S(1)} %broadcast_in_dim.37, bf16[]{:T(256)} %broadcast.6), dimensions={1}, to_apply=%broadcast_in_dim.37.reduce_sub_computation | reduce | bytes 491522 | tf_op jit(solution)/shard_map/broadcast_in_dim | solution.py:150
  13.1 0.0 copy-start.11
  13.1 0.0 copy-start.12
  13.1 0.0 copy-start.13
  13.2 0.9 reshape.33
  14.0 21.8 %all-to-all-done.state_ref = bf16[8,8,64,128]{3,2,1,0:T(8,128)(2,1)S(1)} async-done(((bf16[8,8,64,128]{3,2,1,0:T(8,128)(2,1)}), bf16[8,8,64,128]{3,2,1,0:T(8,128)(2,1)S(1)}, u32[]{:S(2)}, u32[]{:S(2)}) %all-to-all-start) | async-done | bytes 1048608 | tf_op jit(solution)/shard_map/all_to_all | solution.py:147
  35.9 3.6 %all-to-all-start.2 = ((bf16[8,2,7680]{2,1,0:T(2,128)(2,1)}), bf16[8,2,7680]{2,1,0:T(2,128)(2,1)S(1)}, u32[]{:S(2)}, u32[]{:S(2)}) async-start(bf16[8,2,7680]{2,1,0:T(2,128)(2,1)} %reshape.33), calls=%async_computation.2 | async-start | bytes 491520 | tf_op jit(solution)/shard_map/all_to_all | solution.py:151
  39.5 0.0 copy-done.15
  39.5 0.1 select_reduce_fusion
  39.6 0.0 copy-done.16
  39.6 0.6 convert_reduce_fusion.parent_ref
  40.2 0.0 copy-done.8
  40.2 10.3 %pick_states.1 = bf16[16,8,64,128]{3,2,1,0:T(8,128)(2,1)} custom-call(s32[16]{0:T(128)} %convert_reduce_fusion.parent_ref, bf16[8,8,64,128]{3,2,1,0:T(8,128)(2,1)} %copy-done.8), custom_call_target="tpu_custom_call" | custom-call | bytes 4194304 | tf_op jit(solution)/shard_map/pick_states/pallas_call | solution.py:155
  50.5 0.0 all-to-all-done.2
  50.5 6.0 %all-to-all-start.1 = ((bf16[8,2,8,64,128]{4,3,2,1,0:T(8,128)(2,1)}), bf16[8,2,8,64,128]{4,3,2,1,0:T(8,128)(2,1)S(1)}, u32[]{:S(2)}, u32[]{:S(2)}) async-start(bf16[8,2,8,64,128]{4,3,2,1,0:T(8,128)(2,1)} %bitcast.7), calls=%async_computation.1 | async-start | bytes 4194304 | tf_op jit(solution)/shard_map/all_to_all | solution.py:169
  56.5 0.0 copy-done.14
  56.5 0.6 dynamic_slice.3.parent_ref
  57.2 0.0 copy-done.11
  57.2 0.1 copy.27.bias_ref
  57.2 0.0 copy-done.12
  57.3 0.1 copy.28.alog_ref
  57.3 0.0 copy-done.13
  57.4 0.1 broadcast_in_dim.36
  57.4 0.1 broadcast_in_dim_reshape.3.skip_ref
  57.5 0.2 reshape.34
  57.8 0.1 copy.31
  57.9 0.1 reshape.32.tail_bc_ref
  58.0 0.3 reshape.31.tail_x_ref
  58.3 0.0 copy-start.2
  58.3 1.0 copy-done.2
  59.3 1.0 copy-done.3
  60.4 0.9 copy-done.4
  61.3 0.8 copy-done.5
  62.1 0.7 copy-done.6
  62.8 0.7 copy-done.7
  63.5 21.7 %within.1 = (f32[2,256,4096]{2,1,0:T(8,128)}, bf16[2,256,512]{2,1,0:T(8,128)(2,1)S(1)}, f32[2,4,256,16]{3,2,1,0:T(8,128)S(1)}) custom-call(s32[2]{0:T(128)S(1)} %copy-done.7, bf16[2,256,4096]{2,1,0:T(8,128)(2,1)} %x_ref.1, bf16[2,256,512]{2,1,0:T(8,128)(2,1)S(1)} %copy-done.2, bf16[2,256,512]{2,1,0:T(8,128)(2,1)S(1)} %copy-done.3, ...), custom_call_target="tpu_custom_call" | custom-call | flops 2147483648 | bytes 12582912 | tf_op jit(solution)/shard_map/within/pallas_call | solution.py:174
  85.1 0.8 copy-done
  86.0 18.4 %all-to-all-done.1.state_ref = bf16[8,2,8,64,128]{4,3,2,1,0:T(8,128)(2,1)S(1)} async-done(((bf16[8,2,8,64,128]{4,3,2,1,0:T(8,128)(2,1)}), bf16[8,2,8,64,128]{4,3,2,1,0:T(8,128)(2,1)S(1)}, u32[]{:S(2)}, u32[]{:S(2)}) %all-to-all-start.1) | async-done | bytes 2097184 | tf_op jit(solution)/shard_map/all_to_all | solution.py:169
  104.4 1.0 copy-done.1
  105.4 10.0 %carried.1 = bf16[2,256,4096]{2,1,0:T(8,128)(2,1)} custom-call(bf16[8,2,8,64,128]{4,3,2,1,0:T(8,128)(2,1)S(1)} %all-to-all-done.1.state_ref, bf16[2,256,512]{2,1,0:T(8,128)(2,1)S(1)} %copy-done.1, f32[2,4,256,16]{3,2,1,0:T(8,128)S(1)} %get-tuple-element.9.grow_ref, f32[2,256,4096]{2,1,0:T(8,128)} %get-tuple-element.10.mixed_ref), custom_call_target="tpu_custom_call" | custom-call | flops 536870912 | bytes 16777216 | tf_op jit(solution)/shard_map/carried/pallas_call | solution.py:227
  (17 shorter events, 0.1 us)
Async XLA Ops:
  0.0 10.1 %copy-start.10 = (bf16[1,2,3,512]{3,1,2,0:T(2,128)(2,1)S(1)}, bf16[1,2,3,512]{3,1,2,0:T(2,128)(2,1)}, u32[]{:S(2)}) copy-start(bf16[1,2,3,512]{3,1,2,0:T(2,128)(2,1)} %param.25) | copy-start | bytes 18436
  0.0 10.1 %copy-start.9 = (bf16[1,3,4096]{2,1,0:T(4,128)(2,1)S(1)}, bf16[1,3,4096]{2,1,0:T(4,128)(2,1)}, u32[]{:S(2)}) copy-start(bf16[1,3,4096]{2,1,0:T(4,128)(2,1)} %param.24) | copy-start | bytes 73732
  0.0 39.5 %copy-start.15 = (s32[8]{0:T(128)S(1)}, s32[8]{0:T(128)}, u32[]{:S(2)}) copy-start(s32[8]{0:T(128)} %param.26) | copy-start | bytes 100
  0.0 39.6 %copy-start.16 = (s32[16]{0:T(128)S(1)}, s32[16]{0:T(128)}, u32[]{:S(2)}) copy-start(s32[16]{0:T(128)} %param.27) | copy-start | bytes 196
  2.8 33.0 %all-to-all-start = ((bf16[8,8,64,128]{3,2,1,0:T(8,128)(2,1)}), bf16[8,8,64,128]{3,2,1,0:T(8,128)(2,1)S(1)}, u32[]{:S(2)}, u32[]{:S(2)}) async-start(bf16[8,8,64,128]{3,2,1,0:T(8,128)(2,1)} %bitcast), calls=%async_computation | async-start | bytes 2097152 | tf_op jit(solution)/shard_map/all_to_all | solution.py:147
  13.1 44.0 %copy-start.11 = (f32[64]{0:T(128)S(1)}, f32[64]{0:T(128)}, u32[]{:S(2)}) copy-start(f32[64]{0:T(128)} %param.18) | copy-start | bytes 772
  13.1 44.1 %copy-start.12 = (f32[64]{0:T(128)S(1)}, f32[64]{0:T(128)}, u32[]{:S(2)}) copy-start(f32[64]{0:T(128)} %param.19) | copy-start | bytes 772
  13.1 44.2 %copy-start.13 = (f32[64]{0:T(128)S(1)}, f32[64]{0:T(128)}, u32[]{:S(2)}) copy-start(f32[64]{0:T(128)} %param.20) | copy-start | bytes 772
  35.9 4.3 %copy-start.8 = (bf16[8,8,64,128]{3,2,1,0:T(8,128)(2,1)}, bf16[8,8,64,128]{3,2,1,0:T(8,128)(2,1)S(1)}, u32[]{:S(2)}) copy-start(bf16[8,8,64,128]{3,2,1,0:T(8,128)(2,1)S(1)} %all-to-all-done.state_ref) | copy-start | bytes 3145732
  35.9 14.6 %all-to-all-start.2 = ((bf16[8,2,7680]{2,1,0:T(2,128)(2,1)}), bf16[8,2,7680]{2,1,0:T(2,128)(2,1)S(1)}, u32[]{:S(2)}, u32[]{:S(2)}) async-start(bf16[8,2,7680]{2,1,0:T(2,128)(2,1)} %reshape.33), calls=%async_computation.2 | async-start | bytes 491520 | tf_op jit(solution)/shard_map/all_to_all | solution.py:151
  40.2 16.3 %copy-start.14 = (s32[16]{0:T(128)S(1)}, s32[16]{0:T(128)}, u32[]{:S(2)}) copy-start(s32[16]{0:T(128)} %convert_reduce_fusion.parent_ref) | copy-start | bytes 196
  50.5 53.9 %all-to-all-start.1 = ((bf16[8,2,8,64,128]{4,3,2,1,0:T(8,128)(2,1)}), bf16[8,2,8,64,128]{4,3,2,1,0:T(8,128)(2,1)S(1)}, u32[]{:S(2)}, u32[]{:S(2)}) async-start(bf16[8,2,8,64,128]{4,3,2,1,0:T(8,128)(2,1)} %bitcast.7), calls=%async_computation.1 | async-start | bytes 4194304 | tf_op jit(solution)/shard_map/all_to_all | solution.py:169
  58.3 1.0 copy-start.2
  59.3 1.0 copy-start.3
  60.4 0.9 copy-start.4
  61.3 0.8 copy-start.5
  62.1 0.7 copy-start.6
  62.8 0.7 copy-start.7
  85.1 0.8 copy-start
  104.4 1.0 copy-start.1

commit v2 on v1

--- a/solution.py
+++ b/solution.py
@@ -8,6 +8,8 @@
 from jax.sharding import PartitionSpec as P
 
 VMEM_LIMIT = 48 * 1024 * 1024
+CHUNKS = 4
+FIX = 16
 
 
 def parent_of(counts, order):
@@ -19,12 +21,185 @@
 def conv_silu(padded, tail, rows, taps):
     length = rows.shape[0]
     reach = taps.shape[0] - 1
-    padded[8 - reach : 8, :] = tail.astype(jnp.float32)
+    padded[8 - reach : 8, :] = jnp.broadcast_to(tail, (reach, rows.shape[1])).astype(jnp.float32)
     padded[8 : 8 + length, :] = rows.astype(jnp.float32)
     total = padded[8 - reach : 8 - reach + length, :] * taps[0:1, :]
     for k in range(1, reach + 1):
         total = total + padded[8 - reach + k : 8 - reach + k + length, :] * taps[k : k + 1, :]
-    return (total / (1.0 + jnp.exp(-total))).astype(jnp.bfloat16)
+    half = 0.5 * total
+    return (half + half * jnp.tanh(half)).astype(jnp.bfloat16)
+
+
+def conv_kernel(
+    x_ref, b_ref, c_ref, dt_ref, bias_ref, alog_ref, taps_x_ref, taps_bc_ref,
+    xc_ref, bc_ref, cc_ref, row_ref, column_ref, padded,
+):
+    length = x_ref.shape[1]
+    lanes_all = x_ref.shape[2]
+    bc_ref[0] = conv_silu(padded, 0.0, b_ref[0], taps_bc_ref[0])
+    cc_ref[0] = conv_silu(padded, 0.0, c_ref[0], taps_bc_ref[1])
+    for start in range(0, lanes_all, 128):
+        lanes = slice(start, start + 128)
+        xc_ref[0, :, lanes] = conv_silu(padded, 0.0, x_ref[0, :, lanes], taps_x_ref[:, lanes])
+    raw = dt_ref[0] + bias_ref[...]
+    step = jnp.maximum(raw, 0.0) + jnp.log1p(jnp.exp(-jnp.abs(raw)))
+    per_token = step * (-jnp.exp(alog_ref[...]))
+    row = lax.broadcasted_iota(jnp.int32, (length, length), 0)
+    col = lax.broadcasted_iota(jnp.int32, (length, length), 1)
+    total = lax.dot_general(
+        per_token,
+        (row <= col).astype(jnp.float32),
+        (((1,), (0,)), ((), ())),
+        precision=lax.Precision.HIGHEST,
+        preferred_element_type=jnp.float32,
+    )
+    row_ref[0] = total - jnp.log(step)
+    column_ref[0, 0] = total.T
+
+
+def out_kernel(offset, group_at, lines, flags_ref, *refs):
+    (
+        x_ref, xin_ref, b_ref, bin_ref, c_ref, cin_ref, row_ref, column_ref, skip_ref,
+        taps_x_ref, taps_bc_ref, tail_own, tail_a, tail_b, tail_c,
+        own_ref, a_ref, b2_ref, c2_ref,
+    ) = refs[:19]
+    y_ref, padded = refs[-2:]
+    length = x_ref.shape[1]
+    heads, width, size = own_ref.shape[1:]
+    half = length // 2
+    reach = taps_x_ref.shape[0] - 1
+    inner = flags_ref[0] == 1
+    same = flags_ref[1] == pl.program_id(1)
+
+    def choose(own, a, b, c):
+        return jnp.where(same, jnp.where(inner, own, a), jnp.where(inner, c, b))
+
+    tail = choose(tail_own[0, 0], tail_a[0, 0], tail_b[0, 0], tail_c[0, 0]).astype(jnp.float32)
+    state = choose(own_ref[0], a_ref[0], b2_ref[0], c2_ref[0]).reshape(heads * width, size)
+    def tail_rows(at):
+        return jnp.concatenate([tail[k * lines + at : k * lines + at + 1] for k in range(reach)])
+
+    def fixed(bulk, first, taps, at):
+        return jnp.concatenate([conv_silu(padded, tail_rows(at), first, taps), bulk])
+
+    blocks = lines - 4
+    b_conv = fixed(b_ref[0, FIX:], bin_ref[0], taps_bc_ref[0], blocks + group_at)
+    c_conv = fixed(c_ref[0, FIX:], cin_ref[0], taps_bc_ref[1], blocks + 2 + group_at)
+    scores = lax.dot_general(
+        c_conv, b_conv, (((1,), (1,)), ((), ())), preferred_element_type=jnp.float32
+    )
+    term = lax.dot_general(
+        c_conv, state, (((1,), (1,)), ((), ())), preferred_element_type=jnp.float32
+    )
+    causal = lax.broadcasted_iota(jnp.int32, (half, half), 0) >= lax.broadcasted_iota(
+        jnp.int32, (half, half), 1
+    )
+    low = lax.broadcasted_iota(jnp.int32, (length, 2 * width), 1) < width
+    for pair in range(heads // 2):
+        lanes = slice(pair * 2 * width, (pair + 1) * 2 * width)
+        x_conv = fixed(
+            x_ref[0, FIX:, lanes],
+            xin_ref[0, :, lanes],
+            taps_x_ref[:, lanes],
+            (offset + pair * 2) * width // 128,
+        )
+        parts, grow = [], []
+        for head in (2 * pair, 2 * pair + 1):
+            spot = offset % column_ref.shape[3] + head
+            column = jnp.broadcast_to(column_ref[0, 0, :, spot : spot + 1], (length, half))
+            rows = row_ref[0, head : head + 1, :]
+            near = jnp.exp(jnp.where(causal, column[:half] - rows[:, :half], -1e30))
+            far = jnp.exp(column[half:] - rows[:, :half])
+            last = jnp.exp(jnp.where(causal, column[half:] - rows[:, half:], -1e30))
+            top = (scores[:half, :half] * near).astype(jnp.bfloat16)
+            left = (scores[half:, :half] * far).astype(jnp.bfloat16)
+            right = (scores[half:, half:] * last).astype(jnp.bfloat16)
+            parts.append(
+                jnp.concatenate(
+                    [
+                        jnp.dot(top, x_conv[:half], preferred_element_type=jnp.float32),
+                        jnp.dot(
+                            jnp.concatenate([left, right], axis=1),
+                            x_conv,
+                            preferred_element_type=jnp.float32,
+                        ),
+                    ]
+                )
+            )
+            grow.append(column)
+        carried = term[:, lanes] * jnp.exp(jnp.where(low, grow[0], grow[1]))
+        carried = carried.astype(jnp.bfloat16).astype(jnp.float32)
+        y_ref[0, :, lanes] = (
+            jnp.where(low, parts[0], parts[1])
+            + carried
+            + skip_ref[:, lanes] * x_conv.astype(jnp.float32)
+        ).astype(jnp.bfloat16)
+
+
+def cast_kernel(inputs, flags_ref, *refs):
+    mine, other = refs[-2:]
+    sources = refs[:inputs]
+    part = sources[0].shape[1]
+    extra = mine.shape[0] - part
+    for at, out in enumerate((mine, other)):
+        if extra:
+            out[part] = sources[2 + at][0]
+        out[:part] = sources[at][0].astype(jnp.bfloat16)
+
+
+def select_kernel(slots_ref, *refs):
+    held, outs, sems = refs[:8], refs[-5:-1], refs[-1]
+    kids = outs[0].shape[0]
+
+    def copy(source, kind, kid):
+        return pltpu.make_async_copy(
+            held[source], outs[kind].at[kid], sems.at[kind, kid]
+        )
+
+    for kind in range(4):
+        for kid in range(kids):
+            for source in range(8):
+
+                @pl.when(slots_ref[kind * kids + kid] == source)
+                def _(source=source, kind=kind, kid=kid):
+                    copy(source, kind, kid).start()
+
+    for kind in range(4):
+        for kid in range(kids):
+            copy(0, kind, kid).wait()
+
+
+def routes():
+    at = lambda z, y: z * 2 + y
+    both = (0, 1)
+    near = [
+        [(at(0, y), at(1, y ^ f)) for y in both] + [(at(1, y), at(2, y ^ f)) for y in both]
+        for f in both
+    ]
+    back = [
+        [(at(3, y), at(2, y ^ f)) for y in both] + [(at(2, y), at(1, y ^ f)) for y in both]
+        for f in both
+    ]
+    leap = [
+        [(at(0, y), at(2, y ^ f)) for y in both] + [(at(3, y), at(1, y ^ f)) for y in both]
+        for f in both
+    ]
+    across = [(at(z, y), at(z, 1 - y)) for z in (1, 2) for y in both]
+    out = [
+        [(at(1, y), at(0, y ^ f)) for y in both] + [(at(2, y), at(3, y ^ f)) for y in both]
+        for f in both
+    ]
+    return near, back, leap, across, out
+
+
+def pack_tails(tail_x, tail_bc, width, size):
+    reach, columns = tail_x.shape[1:]
+    x_lines = tail_x.reshape(reach, 2, columns // 2 // 128, 128).transpose(1, 0, 2, 3)
+    bc_lines = tail_bc.reshape(2, reach, 2, -1, 128).transpose(2, 1, 0, 3, 4)
+    bc_lines = bc_lines.reshape(2, reach, -1, 128)
+    lines = jnp.concatenate([x_lines, bc_lines], axis=2)
+    lines = lines.reshape(2, -1, 128)
+    return jnp.pad(lines, ((0, 0), (0, width - lines.shape[1]), (0, 0)))
 
 
 def within_kernel(
@@ -112,7 +287,7 @@
     out_ref[...] = state_ref[...]
 
 
-def local(
+def local_any(
     x_in,
     b_in,
     c_in,
@@ -245,22 +420,225 @@
     )(states, c_conv, grow, mixed)
 
 
+def local_grid(
+    x_in, b_in, c_in, dt_in, dt_bias, a_log, d_skip, conv_x, conv_bc,
+    par_state, tail_x, tail_bc, counts, order,
+):
+    kids, length, columns = x_in.shape
+    heads = dt_in.shape[1]
+    width, size = par_state.shape[2:]
+    groups = b_in.shape[2] // size
+    per_group = heads // groups
+    wide = per_group * width
+    taps = conv_x.shape[0]
+    reach = taps - 1
+    half_heads = heads // 2
+    part = half_heads // CHUNKS
+
+    index = lax.axis_index("batch")
+    z, y = index // 2, index % 2
+    parent = parent_of(counts, order)
+    inner = (z == 1) | (z == 2)
+    flags = jnp.stack([inner.astype(jnp.int32), y.astype(jnp.int32)])
+
+    def slot(child):
+        owner = parent[child]
+        step = owner // 2 - z
+        place = jnp.where(step == 0, 0, jnp.where(step == -1, 1, jnp.where(step == 1, 2, 3)))
+        return place + 4 * (owner % 2 != y).astype(jnp.int32)
+
+    outer = jnp.where(z <= 1, 0, 3)
+    kid = jnp.arange(kids, dtype=jnp.int32)
+    wanted = jnp.concatenate(
+        [
+            (z * 2 + y) * kids + kid,
+            (outer * 2 + y) * kids + kid,
+            (outer * 2 + 1 - y) * kids + kid,
+            (z * 2 + 1 - y) * kids + kid,
+        ]
+    )
+    slots = slot(wanted)
+
+    near, back, leap, across, out = routes()
+    send = functools.partial(lax.ppermute, axis_name="batch")
+    halves = par_state.reshape(2, half_heads, width, size)
+    tails = pack_tails(tail_x, tail_bc, width, size)
+
+    def gather(k, tokens):
+        extra = 1 if k == 0 else 0
+        specs = [
+            pl.BlockSpec((1, part, width, size), lambda i, f: (f[1], k, 0, 0)),
+            pl.BlockSpec((1, part, width, size), lambda i, f: (1 - f[1], k, 0, 0)),
+        ]
+        operands = [halves, halves]
+        if extra:
+            specs += [
+                pl.BlockSpec((1, width, size), lambda i, f: (f[1], 0, 0)),
+                pl.BlockSpec((1, width, size), lambda i, f: (1 - f[1], 0, 0)),
+            ]
+            operands += [tails, tails]
+        inputs = len(operands)
+        operands += tokens
+        specs += [pl.BlockSpec(memory_space=pl.ANY)] * len(tokens)
+        block = (extra + part, width, size)
+        mine, other = pl.pallas_call(
+            functools.partial(cast_kernel, inputs),
+            grid_spec=pltpu.PrefetchScalarGridSpec(
+                num_scalar_prefetch=1,
+                grid=(1,),
+                in_specs=specs,
+                out_specs=[pl.BlockSpec(block, lambda i, f: (0, 0, 0))] * 2,
+            ),
+            out_shape=[jax.ShapeDtypeStruct(block, jnp.bfloat16)] * 2,
+            compiler_params=pltpu.CompilerParams(vmem_limit_bytes=VMEM_LIMIT),
+            cost_estimate=pl.CostEstimate(
+                flops=0, bytes_accessed=12 * part * width * size, transcendentals=0
+            ),
+            name="cast_states",
+        )(flags, *operands)
+        return (
+            mine,
+            send(mine, perm=near[0]),
+            send(mine, perm=back[0]),
+            send(mine, perm=leap[0]),
+            send(other, perm=across),
+            send(other, perm=near[1]),
+            send(other, perm=back[1]),
+            send(other, perm=leap[1]),
+        )
+
+    x_conv, b_conv, c_conv, row, column = pl.pallas_call(
+        conv_kernel,
+        grid=(kids, groups),
+        in_specs=[
+            pl.BlockSpec((1, length, wide), lambda c, q: (c, 0, q)),
+            pl.BlockSpec((1, length, size), lambda c, q: (c, 0, q)),
+            pl.BlockSpec((1, length, size), lambda c, q: (c, 0, q)),
+            pl.BlockSpec((1, per_group, length), lambda c, q: (c, q, 0)),
+            pl.BlockSpec((per_group, 1), lambda c, q: (q, 0)),
+            pl.BlockSpec((per_group, 1), lambda c, q: (q, 0)),
+            pl.BlockSpec((taps, wide), lambda c, q: (0, q)),
+            pl.BlockSpec((2, taps, size), lambda c, q: (0, 0, q)),
+        ],
+        out_specs=[
+            pl.BlockSpec((1, length, wide), lambda c, q: (c, 0, q)),
+            pl.BlockSpec((1, length, size), lambda c, q: (c, 0, q)),
+            pl.BlockSpec((1, length, size), lambda c, q: (c, 0, q)),
+            pl.BlockSpec((1, per_group, length), lambda c, q: (c, q, 0)),
+            pl.BlockSpec((1, 1, length, per_group), lambda c, q: (c, q, 0, 0)),
+        ],
+        out_shape=[
+            jax.ShapeDtypeStruct(x_in.shape, jnp.bfloat16),
+            jax.ShapeDtypeStruct(b_in.shape, jnp.bfloat16),
+            jax.ShapeDtypeStruct(c_in.shape, jnp.bfloat16),
+            jax.ShapeDtypeStruct(dt_in.shape, jnp.float32),
+            jax.ShapeDtypeStruct((kids, groups, length, per_group), jnp.float32),
+        ],
+        scratch_shapes=[pltpu.VMEM((8 + length, size), jnp.float32)],
+        compiler_params=pltpu.CompilerParams(vmem_limit_bytes=VMEM_LIMIT),
+        cost_estimate=pl.CostEstimate(
+            flops=20 * kids * length * columns,
+            bytes_accessed=4 * kids * length * columns,
+            transcendentals=kids * length * columns,
+        ),
+        name="conv",
+    )(x_in, b_in, c_in, dt_in, dt_bias[:, None], a_log[:, None], conv_x, conv_bc)
+
+    lines = (columns // 2 + groups * size) // 128
+    skip_row = jnp.repeat(d_skip, width)[None, :]
+    def select(k, tokens):
+        block = gathered[k][0].shape
+        own, to_a, to_b, to_c = pl.pallas_call(
+            select_kernel,
+            grid_spec=pltpu.PrefetchScalarGridSpec(
+                num_scalar_prefetch=1,
+                grid=(1,),
+                in_specs=[pl.BlockSpec(memory_space=pl.ANY)] * (8 + len(tokens)),
+                out_specs=[pl.BlockSpec(memory_space=pl.ANY)] * 4,
+                scratch_shapes=[pltpu.SemaphoreType.DMA((4, kids))],
+            ),
+            out_shape=[jax.ShapeDtypeStruct((kids,) + block, jnp.bfloat16)] * 4,
+            cost_estimate=pl.CostEstimate(
+                flops=0, bytes_accessed=16 * kids * part * width * size, transcendentals=0
+            ),
+            name="select_states",
+        )(slots, *gathered[k], *tokens)
+        return own, send(to_a, perm=out[0]), send(to_b, perm=out[1]), send(to_c, perm=across)
+
+    def mix(k, tails_here, states, result, tokens):
+        chunk_wide = part * width
+        group_at = k * part // per_group
+        half_groups = groups // 2
+        operands = [
+            x_conv, x_in, b_conv, b_in, c_conv, c_in, row, column, skip_row, conv_x, conv_bc,
+            *tails_here, *states,
+        ]
+        x_at = lambda c, h, f: (c, 0, h * CHUNKS + k)
+        bc_at = lambda c, h, f: (c, 0, h * half_groups + group_at)
+        state_spec = pl.BlockSpec((1, part, width, size), lambda c, h, f: (c, 0, 0, 0))
+        specs = [
+            pl.BlockSpec((1, length, chunk_wide), x_at),
+            pl.BlockSpec((1, FIX, chunk_wide), x_at),
+            pl.BlockSpec((1, length, size), bc_at),
+            pl.BlockSpec((1, FIX, size), bc_at),
+            pl.BlockSpec((1, length, size), bc_at),
+            pl.BlockSpec((1, FIX, size), bc_at),
+            pl.BlockSpec((1, part, length), lambda c, h, f: (c, h * CHUNKS + k, 0)),
+            pl.BlockSpec(
+                (1, 1, length, per_group), lambda c, h, f: (c, h * half_groups + group_at, 0, 0)
+            ),
+            pl.BlockSpec((1, chunk_wide), lambda c, h, f: (0, h * CHUNKS + k)),
+            pl.BlockSpec((taps, chunk_wide), lambda c, h, f: (0, h * CHUNKS + k)),
+            pl.BlockSpec((2, taps, size), lambda c, h, f: (0, 0, h * half_groups + group_at)),
+            *[pl.BlockSpec((1, 1, width, size), lambda c, h, f: (c, part, 0, 0))] * 4,
+            *[state_spec] * 4,
+        ]
+        operands += tokens
+        specs += [pl.BlockSpec(memory_space=pl.ANY)] * len(tokens)
+        alias = {}
+        if result is not None:
+            alias = {1 + len(operands): 0}
+            operands.append(result)
+            specs.append(pl.BlockSpec(memory_space=pl.ANY))
+        return pl.pallas_call(
+            functools.partial(out_kernel, k * part, group_at, lines),
+            grid_spec=pltpu.PrefetchScalarGridSpec(
+                num_scalar_prefetch=1,
+                grid=(kids, 2),
+                in_specs=specs,
+                out_specs=pl.BlockSpec((1, length, chunk_wide), x_at),
+                scratch_shapes=[pltpu.VMEM((8 + FIX, size), jnp.float32)],
+            ),
+            out_shape=jax.ShapeDtypeStruct(x_in.shape, jnp.bfloat16),
+            input_output_aliases=alias,
+            compiler_params=pltpu.CompilerParams(vmem_limit_bytes=VMEM_LIMIT),
+            cost_estimate=pl.CostEstimate(
+                flops=2 * kids * 2 * part * length * width * (length + size),
+                bytes_accessed=8 * kids * length * chunk_wide,
+                transcendentals=kids * 2 * part * length * length,
+            ),
+            name="mix",
+        )(flags, *operands)
+
+    gathered = [gather(0, [])]
+    gathered.append(gather(1, [gathered[0][0]]))
+    result, states = None, []
+    for k in range(CHUNKS):
+        states.append(select(k, [x_conv] if k == 0 else [] if k == 1 else [result]))
+        if k + 2 < CHUNKS:
+            gathered.append(gather(k + 2, [states[k][0]]))
+        if k > 0:
+            result = mix(k - 1, states[0], states[k - 1], result, [states[k][0]])
+    return mix(CHUNKS - 1, states[0], states[-1], result, [])
+
+
 def solution(mesh):
     rows, cols = P(("groups", "batch"), None, "head"), P(("groups", "batch"), "head")
     placed = (
-        rows,
-        rows,
-        rows,
-        cols,
-        P("head"),
-        P("head"),
-        P("head"),
-        P(None, "head"),
-        P(None, None, "head"),
-        cols,
-        rows,
-        P(("groups", "batch"), None, None, "head"),
-        P("groups"),
-        P("groups"),
-    )
+        rows, rows, rows, cols, P("head"), P("head"), P("head"), P(None, "head"),
+        P(None, None, "head"), cols, rows, P(("groups", "batch"), None, None, "head"),
+        P("groups"), P("groups"),
+    )
+    grid = mesh.shape["batch"] == 8
+    local = local_grid if grid else local_any
     return jax.shard_map(local, mesh=mesh, in_specs=placed, out_specs=rows, check_vma=False)

time: 116 us -> 325 us (2.80)
  the two profiles are of different devices: /device:TPU:0 before, /device:TPU:10 now
where the time goes in v2:
time: 325 us; the launch traced here: 323 us
  Pallas kernels  176 us (54%)
  starting transfers between devices  98.7 us (30%)
  local copies, waits for them, and re-layouts  30.6 us (9%)
  waiting for transfers between devices  15.1 us (5%)
    pallas_call x4, Pallas kernels, select(): pl.pallas_call(select_kernel, grid_spec=pltpu.PrefetchScalarGridSpec(num_...  139 us
    unnamed x131, local copies, waits for them, and re-layouts  28.9 us
    pallas_call x4, Pallas kernels, mix(): pl.pallas_call(functools.partial(out_kernel, k * part, group_at, lines),...  22.9 us
    ppermute x4, starting transfers between devices, gather(): send(other, perm=across)  15.6 us
    ppermute x4, starting transfers between devices, select(): send(to_b, perm=out[1])  15 us
    ppermute x4, starting transfers between devices, gather(): send(mine, perm=near[0])  14 us
    ppermute x4, starting transfers between devices, gather(): send(other, perm=near[1])  13.6 us
    pallas_call x1, Pallas kernels, local_grid(): pl.pallas_call(conv_kernel, grid=(kids, groups), in_specs=[pl.BlockSpec((...  11 us
  transfers between devices with their start and end apart: 40, of which 4 were waited for; matrix products, arithmetic and copies ran while one was open for 1% of the time, Pallas kernels for 52%

profile of v2, /device:TPU:10, one launch (start us, length us, event | category | flops | bytes accessed | tf_op | source)
XLA Modules:
  0.0 322.8 jit_solution(1368731021901892704)
XLA Ops:
  1.7 1.6 copy-done
  4.5 3.6 %collective-permute-start = (bf16[9,64,128]{2,1,0:T(8,128)(2,1)S(1)}, bf16[9,64,128]{2,1,0:T(8,128)(2,1)S(1)}, u32[]{:S(2)}, u32[]{:S(2)}) collective-permute-start(bf16[9,64,128]{2,1,0:T(8,128)(2,1)S(1)} %get-tuple-element.39.refs_0_.refs_2_), channel_id=1, source_target_pairs={{0,4},{2,6},{4,8},{6,10},{1,5},{3,7},{5,9},{7,11},{16,20},{18,22},... | collective-permute-start | bytes 442376 | tf_op jit(solution)/shard_map/ppermute | solution.py:501
  8.7 1.9 collective-permute-start.10
  10.7 1.3 collective-permute-start.11
  12.0 1.3 collective-permute-start.12
  13.3 3.4 %collective-permute-start.13 = (bf16[8,64,128]{2,1,0:T(8,128)(2,1)S(1)}, bf16[8,64,128]{2,1,0:T(8,128)(2,1)S(1)}, u32[]{:S(2)}, u32[]{:S(2)}) collective-permute-start(bf16[8,64,128]{2,1,0:T(8,128)(2,1)S(1)} %get-tuple-element.46), channel_id=1, source_target_pairs={{4,6},{6,4},{8,10},{10,8},{5,7},{7,5},{9,11},{11,9},{20,22},{22,20... | collective-permute-start | bytes 393224 | tf_op jit(solution)/shard_map/ppermute | solution.py:504
  17.0 1.3 collective-permute-start.1
  18.3 2.1 collective-permute-done.11.refs_2_
  20.3 3.1 collective-permute-start.14
  23.4 1.3 collective-permute-start.15
  24.7 1.3 collective-permute-start.16
  26.8 2.0 collective-permute-done.14.refs_5_
  30.1 5.7 %collective-permute-done.15.refs_6_ = bf16[8,64,128]{2,1,0:T(8,128)(2,1)} collective-permute-done((bf16[8,64,128]{2,1,0:T(8,128)(2,1)S(1)}, bf16[8,64,128]{2,1,0:T(8,128)(2,1)}, u32[]{:S(2)}, u32[]{:S(2)}) %collective-permute-start.15) | collective-permute-done | bytes 131104 | tf_op jit(solution)/shard_map/ppermute | solution.py:506
  35.8 4.9 %collective-permute-start.3 = (bf16[9,64,128]{2,1,0:T(8,128)(2,1)}, bf16[9,64,128]{2,1,0:T(8,128)(2,1)S(1)}, u32[]{:S(2)}, u32[]{:S(2)}) collective-permute-start(bf16[9,64,128]{2,1,0:T(8,128)(2,1)} %get-tuple-element.40), channel_id=1, source_target_pairs={{4,6},{6,4},{8,10},{10,8},{5,7},{7,5},{9,11},{11,9},{20,22},{22,20... | collective-permute-start | bytes 442376 | tf_op jit(solution)/shard_map/ppermute | solution.py:504
  40.7 1.9 collective-permute-start.4
  42.7 1.3 collective-permute-start.5
  44.0 1.3 collective-permute-start.6
  45.8 33.6 %select_states.5 = (bf16[2,8,64,128]{3,2,1,0:T(8,128)(2,1)}, bf16[2,8,64,128]{3,2,1,0:T(8,128)(2,1)}, bf16[2,8,64,128]{3,2,1,0:T(8,128)(2,1)}, bf16[2,8,64,128]{3,2,1,0:T(8,128)(2,1)}) custom-call(s32[8]{0:T(128)} %fusion.slots_ref, bf16[8,64,128]{2,1,0:T(8,128)(2,1)} %copy-done.41, bf16[8,64,128]{2,1,0:T(8,128)(2,1)} %collective-permute-done.10.refs_1_, ...), custom_call_target="tpu_custom_call" | custom-call | bytes 2097152 | tf_op jit(solution)/shard_map/select_states/pallas_call | solution.py:551
  82.3 4.0 %collective-permute-start.17 = (bf16[8,64,128]{2,1,0:T(8,128)(2,1)}, bf16[8,64,128]{2,1,0:T(8,128)(2,1)}, u32[]{:S(2)}, u32[]{:S(2)}) collective-permute-start(bf16[8,64,128]{2,1,0:T(8,128)(2,1)} %get-tuple-element.48.refs_0_), channel_id=1, source_target_pairs={{0,4},{2,6},{4,8},{6,10},{1,5},{3,7},{5,9},{7,11},{16,20},{18,22},... | collective-permute-start | bytes 393224 | tf_op jit(solution)/shard_map/ppermute | solution.py:501
  86.3 1.3 collective-permute-start.18
  91.2 11.0 %conv.1 = (bf16[2,256,4096]{2,1,0:T(8,128)(2,1)}, bf16[2,256,512]{2,1,0:T(8,128)(2,1)S(1)}, bf16[2,256,512]{2,1,0:T(8,128)(2,1)S(1)}, f32[2,64,256]{2,1,0:T(8,128)S(1)}, f32[2,4,256,16]{3,2,1,0:T(8,128)S(1)}) custom-call(bf16[2,256,4096]{2,1,0:T(8,128)(2,1)} %refs_1_.7, bf16[2,256,512]{2,1,0:T(8,128)(2,1)S(1)} %copy-done.2, ...), custom_call_target="tpu_custom_call" | custom-call | flops 41943040 | bytes 8388608 | tf_op jit(solution)/shard_map/conv/pallas_call | solution.py:510
  104.6 37.7 %select_states.4 = (bf16[2,9,64,128]{3,2,1,0:T(8,128)(2,1)}, bf16[2,9,64,128]{3,2,1,0:T(8,128)(2,1)}, bf16[2,9,64,128]{3,2,1,0:T(8,128)(2,1)}, bf16[2,9,64,128]{3,2,1,0:T(8,128)(2,1)}) custom-call(s32[8]{0:T(128)} %fusion.slots_ref, bf16[9,64,128]{2,1,0:T(8,128)(2,1)} %copy-done.37, bf16[9,64,128]{2,1,0:T(8,128)(2,1)} %copy-done.43, ...), custom_call_target="tpu_custom_call" | custom-call | bytes 2097152 | tf_op jit(solution)/shard_map/select_states/pallas_call | solution.py:551
  143.9 4.5 %collective-permute-start.27 = (bf16[8,64,128]{2,1,0:T(8,128)(2,1)S(1)}, bf16[8,64,128]{2,1,0:T(8,128)(2,1)S(1)}, u32[]{:S(2)}, u32[]{:S(2)}) collective-permute-start(bf16[8,64,128]{2,1,0:T(8,128)(2,1)S(1)} %get-tuple-element.53.refs_0_), channel_id=1, source_target_pairs={{0,4},{2,6},{4,8},{6,10},{1,5},{3,7},{5,9},{7,11},{16,20},{18,22},... | collective-permute-start | bytes 393224 | tf_op jit(solution)/shard_map/ppermute | solution.py:501
  149.7 1.3 collective-permute-start.29
  151.0 4.0 %collective-permute-start.30 = (bf16[8,64,128]{2,1,0:T(8,128)(2,1)S(1)}, bf16[8,64,128]{2,1,0:T(8,128)(2,1)S(1)}, u32[]{:S(2)}, u32[]{:S(2)}) collective-permute-start(bf16[8,64,128]{2,1,0:T(8,128)(2,1)S(1)} %get-tuple-element.54), channel_id=1, source_target_pairs={{4,6},{6,4},{8,10},{10,8},{5,7},{7,5},{9,11},{11,9},{20,22},{22,20... | collective-permute-start | bytes 393224 | tf_op jit(solution)/shard_map/ppermute | solution.py:504
  155.0 4.0 %collective-permute-start.31 = (bf16[8,64,128]{2,1,0:T(8,128)(2,1)S(1)}, bf16[8,64,128]{2,1,0:T(8,128)(2,1)S(1)}, u32[]{:S(2)}, u32[]{:S(2)}) collective-permute-start(bf16[8,64,128]{2,1,0:T(8,128)(2,1)S(1)} %get-tuple-element.54), channel_id=1, source_target_pairs={{0,6},{2,4},{4,10},{6,8},{1,7},{3,5},{5,11},{7,9},{16,22},{18,20},... | collective-permute-start | bytes 393224 | tf_op jit(solution)/shard_map/ppermute | solution.py:505
  159.0 1.3 collective-permute-start.7
  160.4 2.7 collective-permute-start.8
  163.1 2.5 collective-permute-start.9
  167.0 1.3 collective-permute-start.33
  168.3 5.2 %collective-permute-done.32.refs_6_ = bf16[8,64,128]{2,1,0:T(8,128)(2,1)S(1)} collective-permute-done((bf16[8,64,128]{2,1,0:T(8,128)(2,1)S(1)}, bf16[8,64,128]{2,1,0:T(8,128)(2,1)S(1)}, u32[]{:S(2)}, u32[]{:S(2)}) %collective-permute-start.32) | collective-permute-done | bytes 131104 | tf_op jit(solution)/shard_map/ppermute | solution.py:506
  173.5 3.0 collective-permute-start.24
  176.5 3.3 %collective-permute-start.20 = (bf16[8,64,128]{2,1,0:T(8,128)(2,1)}, bf16[8,64,128]{2,1,0:T(8,128)(2,1)}, u32[]{:S(2)}, u32[]{:S(2)}) collective-permute-start(bf16[8,64,128]{2,1,0:T(8,128)(2,1)} %copy-done.42), channel_id=1, source_target_pairs={{4,6},{6,4},{8,10},{10,8},{5,7},{7,5},{9,11},{11,9},{20,22},{22,20... | collective-permute-start | bytes 393224 | tf_op jit(solution)/shard_map/ppermute | solution.py:504
  179.9 2.0 collective-permute-start.25
  181.9 2.5 collective-permute-start.26
  184.7 4.6 %collective-permute-start.21 = (bf16[8,64,128]{2,1,0:T(8,128)(2,1)}, bf16[8,64,128]{2,1,0:T(8,128)(2,1)}, u32[]{:S(2)}, u32[]{:S(2)}) collective-permute-start(bf16[8,64,128]{2,1,0:T(8,128)(2,1)} %copy-done.42), channel_id=1, source_target_pairs={{0,6},{2,4},{4,10},{6,8},{1,7},{3,5},{5,11},{7,9},{16,22},{18,20},... | collective-permute-start | bytes 393224 | tf_op jit(solution)/shard_map/ppermute | solution.py:505
  195.3 5.6 %mix.4.refs_8_.refs_20_ = bf16[2,256,4096]{2,1,0:T(8,128)(2,1)} custom-call(s32[2]{0:T(128)S(1)} %pad_add_fusion.flags_ref, bf16[2,256,4096]{2,1,0:T(8,128)(2,1)} %get-tuple-element.34.refs_8_.refs_0_, bf16[2,256,4096]{2,1,0:T(8,128)(2,1)} %refs_1_.7, bf16[2,256,512]{2,1,0:T(8,128)(2,1)S(1)} %copy-done.11, bf16[2,256,512]{2,1,0:T(8,128)(2,1)S(1)} %copy-done.3, ...), custom_call_target="tpu_custom_call" | custom-call | flops 402653184 | bytes 2097152 | tf_op jit(solution)/shard_map/mix/pallas_call | solution.py:603
  203.0 33.8 %select_states.6 = (bf16[2,8,64,128]{3,2,1,0:T(8,128)(2,1)}, bf16[2,8,64,128]{3,2,1,0:T(8,128)(2,1)}, bf16[2,8,64,128]{3,2,1,0:T(8,128)(2,1)}, bf16[2,8,64,128]{3,2,1,0:T(8,128)(2,1)}) custom-call(s32[8]{0:T(128)} %fusion.slots_ref, bf16[8,64,128]{2,1,0:T(8,128)(2,1)} %copy-done.40, bf16[8,64,128]{2,1,0:T(8,128)(2,1)} %copy-done.48, ...), custom_call_target="tpu_custom_call" | custom-call | bytes 2097152 | tf_op jit(solution)/shard_map/select_states/pallas_call | solution.py:551
  236.8 3.5 %collective-permute-start.37 = (bf16[2,8,64,128]{3,2,1,0:T(8,128)(2,1)}, bf16[2,8,64,128]{3,2,1,0:T(8,128)(2,1)}, u32[]{:S(2)}, u32[]{:S(2)}) collective-permute-start(bf16[2,8,64,128]{3,2,1,0:T(8,128)(2,1)} %get-tuple-element.60), channel_id=1, source_target_pairs={{4,0},{6,2},{8,12},{10,14},{5,1},{7,3},{9,13},{11,15},{20,16},{22,... | collective-permute-start | bytes 786440 | tf_op jit(solution)/shard_map/ppermute | solution.py:566
  242.9 8.9 %collective-permute-start.38 = (bf16[2,8,64,128]{3,2,1,0:T(8,128)(2,1)}, bf16[2,8,64,128]{3,2,1,0:T(8,128)(2,1)}, u32[]{:S(2)}, u32[]{:S(2)}) collective-permute-start(bf16[2,8,64,128]{3,2,1,0:T(8,128)(2,1)} %get-tuple-element.61), channel_id=1, source_target_pairs={{4,2},{6,0},{8,14},{10,12},{5,3},{7,1},{9,15},{11,13},{20,18},{22,... | collective-permute-start | bytes 786440 | tf_op jit(solution)/shard_map/ppermute | solution.py:566
  251.8 3.3 %collective-permute-start.39 = (bf16[2,8,64,128]{3,2,1,0:T(8,128)(2,1)}, bf16[2,8,64,128]{3,2,1,0:T(8,128)(2,1)}, u32[]{:S(2)}, u32[]{:S(2)}) collective-permute-start(bf16[2,8,64,128]{3,2,1,0:T(8,128)(2,1)} %get-tuple-element.62), channel_id=1, source_target_pairs={{4,6},{6,4},{8,10},{10,8},{5,7},{7,5},{9,11},{11,9},{20,22},{22,20... | collective-permute-start | bytes 786440 | tf_op jit(solution)/shard_map/ppermute | solution.py:566
  260.9 5.9 %mix.5.refs_8_.refs_20_ = bf16[2,256,4096]{2,1,0:T(8,128)(2,1)} custom-call(s32[2]{0:T(128)S(1)} %pad_add_fusion.flags_ref, bf16[2,256,4096]{2,1,0:T(8,128)(2,1)} %get-tuple-element.34.refs_8_.refs_0_, bf16[2,256,4096]{2,1,0:T(8,128)(2,1)} %refs_1_.7, bf16[2,256,512]{2,1,0:T(8,128)(2,1)S(1)} %copy-done.12, ...), custom_call_target="tpu_custom_call", output_to_operand_aliasing={{}: (21, {})} | custom-call | flops 402653184 | bytes 2097152 | tf_op jit(solution)/shard_map/mix/pallas_call | solution.py:603
  266.8 33.6 %select_states.7 = (bf16[2,8,64,128]{3,2,1,0:T(8,128)(2,1)}, bf16[2,8,64,128]{3,2,1,0:T(8,128)(2,1)}, bf16[2,8,64,128]{3,2,1,0:T(8,128)(2,1)}, bf16[2,8,64,128]{3,2,1,0:T(8,128)(2,1)}) custom-call(s32[8]{0:T(128)} %fusion.slots_ref, bf16[8,64,128]{2,1,0:T(8,128)(2,1)} %get-tuple-element.48.refs_0_, bf16[8,64,128]{2,1,0:T(8,128)(2,1)} %collective-permute-done.17.refs_1_, ...), custom_call_target="tpu_custom_call" | custom-call | bytes 2097152 | tf_op jit(solution)/shard_map/select_states/pallas_call | solution.py:551
  300.4 1.3 collective-permute-start.34
  301.7 1.3 collective-permute-start.35
  303.1 2.5 collective-permute-start.36
  311.3 5.9 %mix.6.refs_19_ = bf16[2,256,4096]{2,1,0:T(8,128)(2,1)} custom-call(s32[2]{0:T(128)S(1)} %pad_add_fusion.flags_ref, bf16[2,256,4096]{2,1,0:T(8,128)(2,1)} %get-tuple-element.34.refs_8_.refs_0_, bf16[2,256,4096]{2,1,0:T(8,128)(2,1)} %refs_1_.7, bf16[2,256,512]{2,1,0:T(8,128)(2,1)S(1)} %copy-done.12, ...), custom_call_target="tpu_custom_call", output_to_operand_aliasing={{}: (21, {})} | custom-call | flops 402653184 | bytes 2097152 | tf_op jit(solution)/shard_map/mix/pallas_call | solution.py:603
  317.2 5.6 %mix.7 = bf16[2,256,4096]{2,1,0:T(8,128)(2,1)} custom-call(s32[2]{0:T(128)S(1)} %pad_add_fusion.flags_ref, bf16[2,256,4096]{2,1,0:T(8,128)(2,1)} %get-tuple-element.34.refs_8_.refs_0_, bf16[2,256,4096]{2,1,0:T(8,128)(2,1)} %refs_1_.7, bf16[2,256,512]{2,1,0:T(8,128)(2,1)S(1)} %copy-done.12, ...), custom_call_target="tpu_custom_call", output_to_operand_aliasing={{}: (20, {})} | custom-call | flops 402653184 | bytes 2097152 | tf_op jit(solution)/shard_map/mix/pallas_call | solution.py:603
  (195 shorter events, 41.4 us)
Async XLA Ops:
  3.3 76.2 %copy-start.1 = (f32[1,64,64,128]{3,2,1,0:T(8,128)S(1)}, f32[1,64,64,128]{3,2,1,0:T(8,128)}, u32[]{:S(2)}) copy-start(f32[1,64,64,128]{3,2,1,0:T(8,128)} %param.23) | copy-start | bytes 6291460
  4.5 77.1 %copy-start.37 = (bf16[9,64,128]{2,1,0:T(8,128)(2,1)}, bf16[9,64,128]{2,1,0:T(8,128)(2,1)S(1)}, u32[]{:S(2)}) copy-start(bf16[9,64,128]{2,1,0:T(8,128)(2,1)S(1)} %get-tuple-element.39.refs_0_.refs_2_) | copy-start | bytes 442372
  4.5 84.4 %copy-start.58 = (f32[64]{0:T(128)S(1)}, f32[64]{0:T(128)}, u32[]{:S(2)}) copy-start(f32[64]{0:T(128)} %param.18) | copy-start | bytes 772
  4.5 84.5 %copy-start.59 = (f32[64]{0:T(128)S(1)}, f32[64]{0:T(128)}, u32[]{:S(2)}) copy-start(f32[64]{0:T(128)} %param.19) | copy-start | bytes 772
  4.5 84.6 %copy-start.32 = (f32[4,4096]{1,0:T(4,128)S(1)}, f32[4,4096]{1,0:T(4,128)}, u32[]{:S(2)}) copy-start(f32[4,4096]{1,0:T(4,128)} %refs_9_.7) | copy-start | bytes 196612
  4.5 84.6 %copy-start.38 = (f32[2,4,512]{2,1,0:T(4,128)S(1)}, f32[2,4,512]{2,1,0:T(4,128)}, u32[]{:S(2)}) copy-start(f32[2,4,512]{2,1,0:T(4,128)} %refs_10_.7) | copy-start | bytes 49156
  4.5 84.6 %copy-start.39 = (f32[2,64,256]{2,1,0:T(8,128)S(1)}, f32[2,64,256]{2,1,0:T(8,128)}, u32[]{:S(2)}) copy-start(f32[2,64,256]{2,1,0:T(8,128)} %dt_ref.1) | copy-start | bytes 393220
  4.5 38.1 %collective-permute-start = (bf16[9,64,128]{2,1,0:T(8,128)(2,1)S(1)}, bf16[9,64,128]{2,1,0:T(8,128)(2,1)S(1)}, u32[]{:S(2)}, u32[]{:S(2)}) collective-permute-start(bf16[9,64,128]{2,1,0:T(8,128)(2,1)S(1)} %get-tuple-element.39.refs_0_.refs_2_), channel_id=1, source_target_pairs={{0,4},{2,6},{4,8},{6,10},{1,5},{3,7},{5,9},{7,11},{16,20},{18,22},... | collective-permute-start | bytes 442376 | tf_op jit(solution)/shard_map/ppermute | solution.py:501
  8.7 8.2 %collective-permute-start.10 = (bf16[8,64,128]{2,1,0:T(8,128)(2,1)S(1)}, bf16[8,64,128]{2,1,0:T(8,128)(2,1)}, u32[]{:S(2)}, u32[]{:S(2)}) collective-permute-start(bf16[8,64,128]{2,1,0:T(8,128)(2,1)S(1)} %get-tuple-element.45.refs_0_), channel_id=1, source_target_pairs={{0,4},{2,6},{4,8},{6,10},{1,5},{3,7},{5,9},{7,11},{16,20},{18,22},... | collective-permute-start | bytes 393224 | tf_op jit(solution)/shard_map/ppermute | solution.py:501
  10.7 9.7 %collective-permute-start.11 = (bf16[8,64,128]{2,1,0:T(8,128)(2,1)S(1)}, bf16[8,64,128]{2,1,0:T(8,128)(2,1)S(1)}, u32[]{:S(2)}, u32[]{:S(2)}) collective-permute-start(bf16[8,64,128]{2,1,0:T(8,128)(2,1)S(1)} %get-tuple-element.45.refs_0_), channel_id=1, source_target_pairs={{12,8},{14,10},{8,4},{10,6},{13,9},{15,11},{9,5},{11,7},{28,24},{3... | collective-permute-start | bytes 393224 | tf_op jit(solution)/shard_map/ppermute | solution.py:502
  12.0 11.4 %collective-permute-start.12 = (bf16[8,64,128]{2,1,0:T(8,128)(2,1)S(1)}, bf16[8,64,128]{2,1,0:T(8,128)(2,1)S(1)}, u32[]{:S(2)}, u32[]{:S(2)}) collective-permute-start(bf16[8,64,128]{2,1,0:T(8,128)(2,1)S(1)} %get-tuple-element.45.refs_0_), channel_id=1, source_target_pairs={{0,8},{2,10},{12,4},{14,6},{1,9},{3,11},{13,5},{15,7},{16,24},{18,... | collective-permute-start | bytes 393224 | tf_op jit(solution)/shard_map/ppermute | solution.py:503
  13.3 11.5 %collective-permute-start.13 = (bf16[8,64,128]{2,1,0:T(8,128)(2,1)S(1)}, bf16[8,64,128]{2,1,0:T(8,128)(2,1)S(1)}, u32[]{:S(2)}, u32[]{:S(2)}) collective-permute-start(bf16[8,64,128]{2,1,0:T(8,128)(2,1)S(1)} %get-tuple-element.46), channel_id=1, source_target_pairs={{4,6},{6,4},{8,10},{10,8},{5,7},{7,5},{9,11},{11,9},{20,22},{22,20... | collective-permute-start | bytes 393224 | tf_op jit(solution)/shard_map/ppermute | solution.py:504
  17.0 27.0 %collective-permute-start.1 = (bf16[9,64,128]{2,1,0:T(8,128)(2,1)S(1)}, bf16[9,64,128]{2,1,0:T(8,128)(2,1)S(1)}, u32[]{:S(2)}, u32[]{:S(2)}) collective-permute-start(bf16[9,64,128]{2,1,0:T(8,128)(2,1)S(1)} %get-tuple-element.39.refs_0_.refs_2_), channel_id=1, source_target_pairs={{12,8},{14,10},{8,4},{10,6},{13,9},{15,11},{9,5},{11,7},{28,24},{3... | collective-permute-start | bytes 442376 | tf_op jit(solution)/shard_map/ppermute | solution.py:502
  20.3 8.4 %collective-permute-start.14 = (bf16[8,64,128]{2,1,0:T(8,128)(2,1)S(1)}, bf16[8,64,128]{2,1,0:T(8,128)(2,1)}, u32[]{:S(2)}, u32[]{:S(2)}) collective-permute-start(bf16[8,64,128]{2,1,0:T(8,128)(2,1)S(1)} %get-tuple-element.46), channel_id=1, source_target_pairs={{0,6},{2,4},{4,10},{6,8},{1,7},{3,5},{5,11},{7,9},{16,22},{18,20},... | collective-permute-start | bytes 393224 | tf_op jit(solution)/shard_map/ppermute | solution.py:505
  23.4 12.4 %collective-permute-start.15 = (bf16[8,64,128]{2,1,0:T(8,128)(2,1)S(1)}, bf16[8,64,128]{2,1,0:T(8,128)(2,1)}, u32[]{:S(2)}, u32[]{:S(2)}) collective-permute-start(bf16[8,64,128]{2,1,0:T(8,128)(2,1)S(1)} %get-tuple-element.46), channel_id=1, source_target_pairs={{12,10},{14,8},{8,6},{10,4},{13,11},{15,9},{9,7},{11,5},{28,26},{3... | collective-permute-start | bytes 393224 | tf_op jit(solution)/shard_map/ppermute | solution.py:506
  24.7 15.9 %collective-permute-start.16 = (bf16[8,64,128]{2,1,0:T(8,128)(2,1)S(1)}, bf16[8,64,128]{2,1,0:T(8,128)(2,1)}, u32[]{:S(2)}, u32[]{:S(2)}) collective-permute-start(bf16[8,64,128]{2,1,0:T(8,128)(2,1)S(1)} %get-tuple-element.46), channel_id=1, source_target_pairs={{0,10},{2,8},{12,6},{14,4},{1,11},{3,9},{13,7},{15,5},{16,26},{18,... | collective-permute-start | bytes 393224 | tf_op jit(solution)/shard_map/ppermute | solution.py:507
  28.8 53.5 %collective-permute-start.2 = (bf16[9,64,128]{2,1,0:T(8,128)(2,1)S(1)}, bf16[9,64,128]{2,1,0:T(8,128)(2,1)S(1)}, u32[]{:S(2)}, u32[]{:S(2)}) collective-permute-start(bf16[9,64,128]{2,1,0:T(8,128)(2,1)S(1)} %get-tuple-element.39.refs_0_.refs_2_), channel_id=1, source_target_pairs={{0,8},{2,10},{12,4},{14,6},{1,9},{3,11},{13,5},{15,7},{16,24},{18,... | collective-permute-start | bytes 442376 | tf_op jit(solution)/shard_map/ppermute | solution.py:503
  35.8 50.5 %collective-permute-start.3 = (bf16[9,64,128]{2,1,0:T(8,128)(2,1)}, bf16[9,64,128]{2,1,0:T(8,128)(2,1)S(1)}, u32[]{:S(2)}, u32[]{:S(2)}) collective-permute-start(bf16[9,64,128]{2,1,0:T(8,128)(2,1)} %get-tuple-element.40), channel_id=1, source_target_pairs={{4,6},{6,4},{8,10},{10,8},{5,7},{7,5},{9,11},{11,9},{20,22},{22,20... | collective-permute-start | bytes 442376 | tf_op jit(solution)/shard_map/ppermute | solution.py:504
  40.7 46.9 %collective-permute-start.4 = (bf16[9,64,128]{2,1,0:T(8,128)(2,1)}, bf16[9,64,128]{2,1,0:T(8,128)(2,1)S(1)}, u32[]{:S(2)}, u32[]{:S(2)}) collective-permute-start(bf16[9,64,128]{2,1,0:T(8,128)(2,1)} %get-tuple-element.40), channel_id=1, source_target_pairs={{0,6},{2,4},{4,10},{6,8},{1,7},{3,5},{5,11},{7,9},{16,22},{18,20},... | collective-permute-start | bytes 442376 | tf_op jit(solution)/shard_map/ppermute | solution.py:505
  42.7 61.9 %collective-permute-start.5 = (bf16[9,64,128]{2,1,0:T(8,128)(2,1)}, bf16[9,64,128]{2,1,0:T(8,128)(2,1)}, u32[]{:S(2)}, u32[]{:S(2)}) collective-permute-start(bf16[9,64,128]{2,1,0:T(8,128)(2,1)} %get-tuple-element.40), channel_id=1, source_target_pairs={{12,10},{14,8},{8,6},{10,4},{13,11},{15,9},{9,7},{11,5},{28,26},{3... | collective-permute-start | bytes 442376 | tf_op jit(solution)/shard_map/ppermute | solution.py:506
  44.0 60.6 %collective-permute-start.6 = (bf16[9,64,128]{2,1,0:T(8,128)(2,1)}, bf16[9,64,128]{2,1,0:T(8,128)(2,1)}, u32[]{:S(2)}, u32[]{:S(2)}) collective-permute-start(bf16[9,64,128]{2,1,0:T(8,128)(2,1)} %get-tuple-element.40), channel_id=1, source_target_pairs={{0,10},{2,8},{12,6},{14,4},{1,11},{3,9},{13,7},{15,5},{16,26},{18,... | collective-permute-start | bytes 442376 | tf_op jit(solution)/shard_map/ppermute | solution.py:507
  82.3 67.4 %collective-permute-start.17 = (bf16[8,64,128]{2,1,0:T(8,128)(2,1)}, bf16[8,64,128]{2,1,0:T(8,128)(2,1)}, u32[]{:S(2)}, u32[]{:S(2)}) collective-permute-start(bf16[8,64,128]{2,1,0:T(8,128)(2,1)} %get-tuple-element.48.refs_0_), channel_id=1, source_target_pairs={{0,4},{2,6},{4,8},{6,10},{1,5},{3,7},{5,9},{7,11},{16,20},{18,22},... | collective-permute-start | bytes 393224 | tf_op jit(solution)/shard_map/ppermute | solution.py:501
  86.3 64.7 %collective-permute-start.18 = (bf16[8,64,128]{2,1,0:T(8,128)(2,1)}, bf16[8,64,128]{2,1,0:T(8,128)(2,1)}, u32[]{:S(2)}, u32[]{:S(2)}) collective-permute-start(bf16[8,64,128]{2,1,0:T(8,128)(2,1)} %get-tuple-element.48.refs_0_), channel_id=1, source_target_pairs={{12,8},{14,10},{8,4},{10,6},{13,9},{15,11},{9,5},{11,7},{28,24},{3... | collective-permute-start | bytes 393224 | tf_op jit(solution)/shard_map/ppermute | solution.py:502
  87.6 67.4 %collective-permute-start.19 = (bf16[8,64,128]{2,1,0:T(8,128)(2,1)}, bf16[8,64,128]{2,1,0:T(8,128)(2,1)}, u32[]{:S(2)}, u32[]{:S(2)}) collective-permute-start(bf16[8,64,128]{2,1,0:T(8,128)(2,1)} %get-tuple-element.48.refs_0_), channel_id=1, source_target_pairs={{0,8},{2,10},{12,4},{14,6},{1,9},{3,11},{13,5},{15,7},{16,24},{18,... | collective-permute-start | bytes 393224 | tf_op jit(solution)/shard_map/ppermute | solution.py:503
  104.6 79.9 %copy-start.60 = (f32[64]{0:T(128)S(1)}, f32[64]{0:T(128)}, u32[]{:S(2)}) copy-start(f32[64]{0:T(128)} %param.20) | copy-start | bytes 772
  143.9 15.2 %collective-permute-start.27 = (bf16[8,64,128]{2,1,0:T(8,128)(2,1)S(1)}, bf16[8,64,128]{2,1,0:T(8,128)(2,1)S(1)}, u32[]{:S(2)}, u32[]{:S(2)}) collective-permute-start(bf16[8,64,128]{2,1,0:T(8,128)(2,1)S(1)} %get-tuple-element.53.refs_0_), channel_id=1, source_target_pairs={{0,4},{2,6},{4,8},{6,10},{1,5},{3,7},{5,9},{7,11},{16,20},{18,22},... | collective-permute-start | bytes 393224 | tf_op jit(solution)/shard_map/ppermute | solution.py:501
  148.4 12.0 %collective-permute-start.28 = (bf16[8,64,128]{2,1,0:T(8,128)(2,1)S(1)}, bf16[8,64,128]{2,1,0:T(8,128)(2,1)S(1)}, u32[]{:S(2)}, u32[]{:S(2)}) collective-permute-start(bf16[8,64,128]{2,1,0:T(8,128)(2,1)S(1)} %get-tuple-element.53.refs_0_), channel_id=1, source_target_pairs={{12,8},{14,10},{8,4},{10,6},{13,9},{15,11},{9,5},{11,7},{28,24},{3... | collective-permute-start | bytes 393224 | tf_op jit(solution)/shard_map/ppermute | solution.py:502
  149.7 13.4 %collective-permute-start.29 = (bf16[8,64,128]{2,1,0:T(8,128)(2,1)S(1)}, bf16[8,64,128]{2,1,0:T(8,128)(2,1)S(1)}, u32[]{:S(2)}, u32[]{:S(2)}) collective-permute-start(bf16[8,64,128]{2,1,0:T(8,128)(2,1)S(1)} %get-tuple-element.53.refs_0_), channel_id=1, source_target_pairs={{0,8},{2,10},{12,4},{14,6},{1,9},{3,11},{13,5},{15,7},{16,24},{18,... | collective-permute-start | bytes 393224 | tf_op jit(solution)/shard_map/ppermute | solution.py:503
  151.0 14.6 %collective-permute-start.30 = (bf16[8,64,128]{2,1,0:T(8,128)(2,1)S(1)}, bf16[8,64,128]{2,1,0:T(8,128)(2,1)S(1)}, u32[]{:S(2)}, u32[]{:S(2)}) collective-permute-start(bf16[8,64,128]{2,1,0:T(8,128)(2,1)S(1)} %get-tuple-element.54), channel_id=1, source_target_pairs={{4,6},{6,4},{8,10},{10,8},{5,7},{7,5},{9,11},{11,9},{20,22},{22,20... | collective-permute-start | bytes 393224 | tf_op jit(solution)/shard_map/ppermute | solution.py:504
  155.0 12.0 %collective-permute-start.31 = (bf16[8,64,128]{2,1,0:T(8,128)(2,1)S(1)}, bf16[8,64,128]{2,1,0:T(8,128)(2,1)S(1)}, u32[]{:S(2)}, u32[]{:S(2)}) collective-permute-start(bf16[8,64,128]{2,1,0:T(8,128)(2,1)S(1)} %get-tuple-element.54), channel_id=1, source_target_pairs={{0,6},{2,4},{4,10},{6,8},{1,7},{3,5},{5,11},{7,9},{16,22},{18,20},... | collective-permute-start | bytes 393224 | tf_op jit(solution)/shard_map/ppermute | solution.py:505
  159.0 20.9 %collective-permute-start.7 = (bf16[2,9,64,128]{3,2,1,0:T(8,128)(2,1)S(1)}, bf16[2,9,64,128]{3,2,1,0:T(8,128)(2,1)S(1)}, u32[]{:S(2)}, u32[]{:S(2)}) collective-permute-start(bf16[2,9,64,128]{3,2,1,0:T(8,128)(2,1)S(1)} %copy-done.62), channel_id=1, source_target_pairs={{4,0},{6,2},{8,12},{10,14},{5,1},{7,3},{9,13},{11,15},{20,16},{22,... | collective-permute-start | bytes 884744 | tf_op jit(solution)/shard_map/ppermute | solution.py:566
  160.4 21.5 %collective-permute-start.8 = (bf16[2,9,64,128]{3,2,1,0:T(8,128)(2,1)S(1)}, bf16[2,9,64,128]{3,2,1,0:T(8,128)(2,1)S(1)}, u32[]{:S(2)}, u32[]{:S(2)}) collective-permute-start(bf16[2,9,64,128]{3,2,1,0:T(8,128)(2,1)S(1)} %copy-done.61), channel_id=1, source_target_pairs={{4,2},{6,0},{8,14},{10,12},{5,3},{7,1},{9,15},{11,13},{20,18},{22,... | collective-permute-start | bytes 884744 | tf_op jit(solution)/shard_map/ppermute | solution.py:566
  163.1 21.5 %collective-permute-start.9 = (bf16[2,9,64,128]{3,2,1,0:T(8,128)(2,1)}, bf16[2,9,64,128]{3,2,1,0:T(8,128)(2,1)S(1)}, u32[]{:S(2)}, u32[]{:S(2)}) collective-permute-start(bf16[2,9,64,128]{3,2,1,0:T(8,128)(2,1)} %get-tuple-element.44), channel_id=1, source_target_pairs={{4,6},{6,4},{8,10},{10,8},{5,7},{7,5},{9,11},{11,9},{20,22},{22,20... | collective-permute-start | bytes 884744 | tf_op jit(solution)/shard_map/ppermute | solution.py:566
  165.7 7.9 %collective-permute-start.32 = (bf16[8,64,128]{2,1,0:T(8,128)(2,1)S(1)}, bf16[8,64,128]{2,1,0:T(8,128)(2,1)S(1)}, u32[]{:S(2)}, u32[]{:S(2)}) collective-permute-start(bf16[8,64,128]{2,1,0:T(8,128)(2,1)S(1)} %get-tuple-element.54), channel_id=1, source_target_pairs={{12,10},{14,8},{8,6},{10,4},{13,11},{15,9},{9,7},{11,5},{28,26},{3... | collective-permute-start | bytes 393224 | tf_op jit(solution)/shard_map/ppermute | solution.py:506
  167.0 9.6 %collective-permute-start.33 = (bf16[8,64,128]{2,1,0:T(8,128)(2,1)S(1)}, bf16[8,64,128]{2,1,0:T(8,128)(2,1)S(1)}, u32[]{:S(2)}, u32[]{:S(2)}) collective-permute-start(bf16[8,64,128]{2,1,0:T(8,128)(2,1)S(1)} %get-tuple-element.54), channel_id=1, source_target_pairs={{0,10},{2,8},{12,6},{14,4},{1,11},{3,9},{13,7},{15,5},{16,26},{18,... | collective-permute-start | bytes 393224 | tf_op jit(solution)/shard_map/ppermute | solution.py:507
  173.5 68.0 %collective-permute-start.24 = (bf16[2,8,64,128]{3,2,1,0:T(8,128)(2,1)}, bf16[2,8,64,128]{3,2,1,0:T(8,128)(2,1)}, u32[]{:S(2)}, u32[]{:S(2)}) collective-permute-start(bf16[2,8,64,128]{3,2,1,0:T(8,128)(2,1)} %get-tuple-element.50), channel_id=1, source_target_pairs={{4,0},{6,2},{8,12},{10,14},{5,1},{7,3},{9,13},{11,15},{20,16},{22,... | collective-permute-start | bytes 786440 | tf_op jit(solution)/shard_map/ppermute | solution.py:566
  176.5 60.3 %collective-permute-start.20 = (bf16[8,64,128]{2,1,0:T(8,128)(2,1)}, bf16[8,64,128]{2,1,0:T(8,128)(2,1)}, u32[]{:S(2)}, u32[]{:S(2)}) collective-permute-start(bf16[8,64,128]{2,1,0:T(8,128)(2,1)} %copy-done.42), channel_id=1, source_target_pairs={{4,6},{6,4},{8,10},{10,8},{5,7},{7,5},{9,11},{11,9},{20,22},{22,20... | collective-permute-start | bytes 393224 | tf_op jit(solution)/shard_map/ppermute | solution.py:504
  179.9 63.0 %collective-permute-start.25 = (bf16[2,8,64,128]{3,2,1,0:T(8,128)(2,1)}, bf16[2,8,64,128]{3,2,1,0:T(8,128)(2,1)}, u32[]{:S(2)}, u32[]{:S(2)}) collective-permute-start(bf16[2,8,64,128]{3,2,1,0:T(8,128)(2,1)} %get-tuple-element.51), channel_id=1, source_target_pairs={{4,2},{6,0},{8,14},{10,12},{5,3},{7,1},{9,15},{11,13},{20,18},{22,... | collective-permute-start | bytes 786440 | tf_op jit(solution)/shard_map/ppermute | solution.py:566
  181.9 69.9 %collective-permute-start.26 = (bf16[2,8,64,128]{3,2,1,0:T(8,128)(2,1)}, bf16[2,8,64,128]{3,2,1,0:T(8,128)(2,1)}, u32[]{:S(2)}, u32[]{:S(2)}) collective-permute-start(bf16[2,8,64,128]{3,2,1,0:T(8,128)(2,1)} %get-tuple-element.52), channel_id=1, source_target_pairs={{4,6},{6,4},{8,10},{10,8},{5,7},{7,5},{9,11},{11,9},{20,22},{22,20... | collective-permute-start | bytes 786440 | tf_op jit(solution)/shard_map/ppermute | solution.py:566
  184.7 55.6 %collective-permute-start.21 = (bf16[8,64,128]{2,1,0:T(8,128)(2,1)}, bf16[8,64,128]{2,1,0:T(8,128)(2,1)}, u32[]{:S(2)}, u32[]{:S(2)}) collective-permute-start(bf16[8,64,128]{2,1,0:T(8,128)(2,1)} %copy-done.42), channel_id=1, source_target_pairs={{0,6},{2,4},{4,10},{6,8},{1,7},{3,5},{5,11},{7,9},{16,22},{18,20},... | collective-permute-start | bytes 393224 | tf_op jit(solution)/shard_map/ppermute | solution.py:505
  236.8 66.3 %collective-permute-start.37 = (bf16[2,8,64,128]{3,2,1,0:T(8,128)(2,1)}, bf16[2,8,64,128]{3,2,1,0:T(8,128)(2,1)}, u32[]{:S(2)}, u32[]{:S(2)}) collective-permute-start(bf16[2,8,64,128]{3,2,1,0:T(8,128)(2,1)} %get-tuple-element.60), channel_id=1, source_target_pairs={{4,0},{6,2},{8,12},{10,14},{5,1},{7,3},{9,13},{11,15},{20,16},{22,... | collective-permute-start | bytes 786440 | tf_op jit(solution)/shard_map/ppermute | solution.py:566
  240.3 26.5 %collective-permute-start.22 = (bf16[8,64,128]{2,1,0:T(8,128)(2,1)}, bf16[8,64,128]{2,1,0:T(8,128)(2,1)}, u32[]{:S(2)}, u32[]{:S(2)}) collective-permute-start(bf16[8,64,128]{2,1,0:T(8,128)(2,1)} %copy-done.42), channel_id=1, source_target_pairs={{12,10},{14,8},{8,6},{10,4},{13,11},{15,9},{9,7},{11,5},{28,26},{3... | collective-permute-start | bytes 393224 | tf_op jit(solution)/shard_map/ppermute | solution.py:506
  241.6 25.2 %collective-permute-start.23 = (bf16[8,64,128]{2,1,0:T(8,128)(2,1)}, bf16[8,64,128]{2,1,0:T(8,128)(2,1)}, u32[]{:S(2)}, u32[]{:S(2)}) collective-permute-start(bf16[8,64,128]{2,1,0:T(8,128)(2,1)} %copy-done.42), channel_id=1, source_target_pairs={{0,10},{2,8},{12,6},{14,4},{1,11},{3,9},{13,7},{15,5},{16,26},{18,... | collective-permute-start | bytes 393224 | tf_op jit(solution)/shard_map/ppermute | solution.py:507
  242.9 62.7 %collective-permute-start.38 = (bf16[2,8,64,128]{3,2,1,0:T(8,128)(2,1)}, bf16[2,8,64,128]{3,2,1,0:T(8,128)(2,1)}, u32[]{:S(2)}, u32[]{:S(2)}) collective-permute-start(bf16[2,8,64,128]{3,2,1,0:T(8,128)(2,1)} %get-tuple-element.61), channel_id=1, source_target_pairs={{4,2},{6,0},{8,14},{10,12},{5,3},{7,1},{9,15},{11,13},{20,18},{22,... | collective-permute-start | bytes 786440 | tf_op jit(solution)/shard_map/ppermute | solution.py:566
  251.8 53.8 %collective-permute-start.39 = (bf16[2,8,64,128]{3,2,1,0:T(8,128)(2,1)}, bf16[2,8,64,128]{3,2,1,0:T(8,128)(2,1)}, u32[]{:S(2)}, u32[]{:S(2)}) collective-permute-start(bf16[2,8,64,128]{3,2,1,0:T(8,128)(2,1)} %get-tuple-element.62), channel_id=1, source_target_pairs={{4,6},{6,4},{8,10},{10,8},{5,7},{7,5},{9,11},{11,9},{20,22},{22,20... | collective-permute-start | bytes 786440 | tf_op jit(solution)/shard_map/ppermute | solution.py:566
  300.4 16.7 %collective-permute-start.34 = (bf16[2,8,64,128]{3,2,1,0:T(8,128)(2,1)}, bf16[2,8,64,128]{3,2,1,0:T(8,128)(2,1)S(1)}, u32[]{:S(2)}, u32[]{:S(2)}) collective-permute-start(bf16[2,8,64,128]{3,2,1,0:T(8,128)(2,1)} %get-tuple-element.57), channel_id=1, source_target_pairs={{4,0},{6,2},{8,12},{10,14},{5,1},{7,3},{9,13},{11,15},{20,16},{22,... | collective-permute-start | bytes 786440 | tf_op jit(solution)/shard_map/ppermute | solution.py:566
  301.7 15.4 %collective-permute-start.35 = (bf16[2,8,64,128]{3,2,1,0:T(8,128)(2,1)}, bf16[2,8,64,128]{3,2,1,0:T(8,128)(2,1)S(1)}, u32[]{:S(2)}, u32[]{:S(2)}) collective-permute-start(bf16[2,8,64,128]{3,2,1,0:T(8,128)(2,1)} %get-tuple-element.58), channel_id=1, source_target_pairs={{4,2},{6,0},{8,14},{10,12},{5,3},{7,1},{9,15},{11,13},{20,18},{22,... | collective-permute-start | bytes 786440 | tf_op jit(solution)/shard_map/ppermute | solution.py:566
  303.1 14.1 %collective-permute-start.36 = (bf16[2,8,64,128]{3,2,1,0:T(8,128)(2,1)}, bf16[2,8,64,128]{3,2,1,0:T(8,128)(2,1)S(1)}, u32[]{:S(2)}, u32[]{:S(2)}) collective-permute-start(bf16[2,8,64,128]{3,2,1,0:T(8,128)(2,1)} %get-tuple-element.59), channel_id=1, source_target_pairs={{4,6},{6,4},{8,10},{10,8},{5,7},{7,5},{9,11},{11,9},{20,22},{22,20... | collective-permute-start | bytes 786440 | tf_op jit(solution)/shard_map/ppermute | solution.py:566
  (57 other events, 684.5 us)

commit v3 on v1

--- a/solution.py
+++ b/solution.py
@@ -7,7 +7,13 @@
 from jax.experimental.pallas import tpu as pltpu
 from jax.sharding import PartitionSpec as P
 
-VMEM_LIMIT = 48 * 1024 * 1024
+VMEM_LIMIT = 60 * 1024 * 1024
+SPLIT = (8, 8)
+FIX = 16
+
+
+def drop_tokens(kernel, keep, tokens, *refs):
+    kernel(*refs[:keep], *refs[keep + tokens :])
 
 
 def parent_of(counts, order):
@@ -19,12 +25,152 @@
 def conv_silu(padded, tail, rows, taps):
     length = rows.shape[0]
     reach = taps.shape[0] - 1
-    padded[8 - reach : 8, :] = tail.astype(jnp.float32)
+    padded[8 - reach : 8, :] = jnp.broadcast_to(tail, (reach, rows.shape[1])).astype(jnp.float32)
     padded[8 : 8 + length, :] = rows.astype(jnp.float32)
     total = padded[8 - reach : 8 - reach + length, :] * taps[0:1, :]
     for k in range(1, reach + 1):
         total = total + padded[8 - reach + k : 8 - reach + k + length, :] * taps[k : k + 1, :]
-    return (total / (1.0 + jnp.exp(-total))).astype(jnp.bfloat16)
+    half = 0.5 * total
+    return (half + half * jnp.tanh(half)).astype(jnp.bfloat16)
+
+
+def conv_kernel(
+    x_ref, b_ref, c_ref, dt_ref, bias_ref, alog_ref, taps_x_ref, taps_bc_ref,
+    xc_ref, bc_ref, cc_ref, row_ref, column_ref, padded,
+):
+    length = x_ref.shape[1]
+    lanes_all = x_ref.shape[2]
+    bc_ref[0] = conv_silu(padded, 0.0, b_ref[0], taps_bc_ref[0])
+    cc_ref[0] = conv_silu(padded, 0.0, c_ref[0], taps_bc_ref[1])
+    for start in range(0, lanes_all, 128):
+        lanes = slice(start, start + 128)
+        xc_ref[0, :, lanes] = conv_silu(padded, 0.0, x_ref[0, :, lanes], taps_x_ref[:, lanes])
+    raw = dt_ref[0] + bias_ref[...]
+    step = jnp.maximum(raw, 0.0) + jnp.log1p(jnp.exp(-jnp.abs(raw)))
+    per_token = step * (-jnp.exp(alog_ref[...]))
+    row = lax.broadcasted_iota(jnp.int32, (length, length), 0)
+    col = lax.broadcasted_iota(jnp.int32, (length, length), 1)
+    total = lax.dot_general(
+        per_token,
+        (row <= col).astype(jnp.float32),
+        (((1,), (0,)), ((), ())),
+        precision=lax.Precision.HIGHEST,
+        preferred_element_type=jnp.float32,
+    )
+    row_ref[0] = total - jnp.log(step)
+    column_ref[0, 0] = total.T
+
+
+def mix_kernel(
+    lines, x_ref, xin_ref, b_ref, bin_ref, c_ref, cin_ref, row_ref, column_ref, skip_ref,
+    taps_x_ref, taps_bc_ref, tail_ref, *refs,
+):
+    mixed_ref, c_out_ref, padded = refs[-3:]
+    length = x_ref.shape[1]
+    heads = row_ref.shape[1]
+    width = x_ref.shape[2] // heads
+    half = length // 2
+    reach = taps_x_ref.shape[0] - 1
+    tail = tail_ref[0, 0].astype(jnp.float32)
+
+    def fixed(bulk_ref, first_ref, lanes, taps, at):
+        rows = jnp.concatenate([tail[k * lines + at : k * lines + at + 1] for k in range(reach)])
+        first = conv_silu(padded, rows, first_ref[0, :, lanes], taps)
+        return jnp.concatenate([first, bulk_ref[0, FIX:, lanes]])
+
+    every = slice(0, b_ref.shape[2])
+    b_conv = fixed(b_ref, bin_ref, every, taps_bc_ref[0], lines - 2)
+    c_conv = fixed(c_ref, cin_ref, every, taps_bc_ref[1], lines - 1)
+    c_out_ref[0] = c_conv
+    scores = lax.dot_general(
+        c_conv, b_conv, (((1,), (1,)), ((), ())), preferred_element_type=jnp.float32
+    )
+    causal = lax.broadcasted_iota(jnp.int32, (half, half), 0) >= lax.broadcasted_iota(
+        jnp.int32, (half, half), 1
+    )
+    low = lax.broadcasted_iota(jnp.int32, (length, 2 * width), 1) < width
+    for pair in range(heads // 2):
+        lanes = slice(pair * 2 * width, (pair + 1) * 2 * width)
+        x_conv = fixed(x_ref, xin_ref, lanes, taps_x_ref[:, lanes], pair)
+        parts = []
+        for head in (2 * pair, 2 * pair + 1):
+            column = jnp.broadcast_to(column_ref[0, 0, :, head : head + 1], (length, half))
+            rows = row_ref[0, head : head + 1, :]
+            near = jnp.exp(jnp.where(causal, column[:half] - rows[:, :half], -1e30))
+            far = jnp.exp(column[half:] - rows[:, :half])
+            last = jnp.exp(jnp.where(causal, column[half:] - rows[:, half:], -1e30))
+            top = (scores[:half, :half] * near).astype(jnp.bfloat16)
+            left = (scores[half:, :half] * far).astype(jnp.bfloat16)
+            right = (scores[half:, half:] * last).astype(jnp.bfloat16)
+            below = jnp.concatenate([left, right], axis=1)
+            parts.append(
+                jnp.concatenate(
+                    [
+                        jnp.dot(top, x_conv[:half], preferred_element_type=jnp.float32),
+                        jnp.dot(below, x_conv, preferred_element_type=jnp.float32),
+                    ]
+                )
+            )
+        mixed_ref[0, :, lanes] = jnp.where(low, parts[0], parts[1]) + skip_ref[
+            :, lanes
+        ] * x_conv.astype(jnp.float32)
+
+
+def state_kernel(offset, state_ref, c_ref, column_ref, mixed_ref, *refs):
+    y_ref = refs[-1]
+    length, wide = y_ref.shape[1:]
+    pairs = wide // 128
+    width = 64
+    low = lax.broadcasted_iota(jnp.int32, (length, 128), 1) < width
+    term = lax.dot_general(
+        c_ref[0], state_ref[0, 0], (((1,), (1,)), ((), ())), preferred_element_type=jnp.float32
+    )
+    for pair in range(pairs):
+        lanes = slice(pair * 128, pair * 128 + 128)
+        head = offset + 2 * pair
+        grow = jnp.where(
+            low, column_ref[0, 0, :, head : head + 1], column_ref[0, 0, :, head + 1 : head + 2]
+        )
+        carried = (term[:, lanes] * jnp.exp(grow)).astype(jnp.bfloat16).astype(jnp.float32)
+        y_ref[0, :, lanes] = (mixed_ref[0, :, lanes] + carried).astype(jnp.bfloat16)
+
+
+def cast_kernel(state_ref, *refs):
+    out_ref = refs[-1]
+    rows = state_ref.shape[1] * state_ref.shape[2]
+    value = state_ref[0].reshape(rows, state_ref.shape[3]).astype(jnp.bfloat16)
+    for side in range(2):
+        out_ref[side, 0, :rows] = value
+    if len(refs) > 1:
+        x_tail, bc_tail = refs[0][0].astype(jnp.float32), refs[1][0].astype(jnp.float32)
+        reach, wide = x_tail.shape
+        lines = []
+        for k in range(reach):
+            lines += [x_tail[k : k + 1, at : at + 128] for at in range(0, wide, 128)]
+            lines += [bc_tail[0, k : k + 1], bc_tail[1, k : k + 1]]
+        spare = out_ref.shape[2] - rows - len(lines)
+        lines = jnp.concatenate(lines + [jnp.zeros((spare, 128), jnp.float32)])
+        for side in range(2):
+            out_ref[side, 0, rows:] = lines.astype(jnp.bfloat16)
+
+
+def pick_rows_kernel(slots_ref, held_ref, *refs):
+    outs, sems = refs[:-1], refs[-1]
+    spots = outs[0].shape[0]
+    starts = [0, outs[0].shape[1]]
+    copies = []
+    for at, out in enumerate(outs):
+        rows = pl.ds(starts[at], out.shape[1])
+        for i in range(spots):
+            copies.append(
+                pltpu.make_async_copy(
+                    held_ref.at[slots_ref[i], rows], out.at[i], sems.at[at, i]
+                )
+            )
+    for copy in copies:
+        copy.start()
+    for copy in copies:
+        copy.wait()
 
 
 def within_kernel(
@@ -112,7 +258,7 @@
     out_ref[...] = state_ref[...]
 
 
-def local(
+def local_any(
     x_in,
     b_in,
     c_in,
@@ -245,22 +391,215 @@
     )(states, c_conv, grow, mixed)
 
 
+def local_halves(
+    x_in, b_in, c_in, dt_in, dt_bias, a_log, d_skip, conv_x, conv_bc,
+    par_state, tail_x, tail_bc, counts, order,
+):
+    kids, length, columns = x_in.shape
+    heads = dt_in.shape[1]
+    width, size = par_state.shape[2:]
+    groups = b_in.shape[2] // size
+    per_group = heads // groups
+    wide = per_group * width
+    taps = conv_x.shape[0]
+    ways = lax.axis_size("batch")
+    side = ways // 2
+    halves = [list(range(side)), list(range(side, ways))]
+    lines = (wide + 2 * size) // 128
+    tail_lines = -(-lines * (taps - 1) // 16) * 16
+    exchange = functools.partial(
+        lax.all_to_all, axis_name="batch", split_axis=0, concat_axis=0, tiled=True
+    )
+
+    parent = parent_of(counts, order)
+    slots = lax.dynamic_slice_in_dim(
+        parent, lax.axis_index("batch") // side * side * kids, side * kids
+    )
+    state = par_state.reshape(groups, per_group, width, size)
+
+    offsets = [sum(SPLIT[:k]) for k in range(len(SPLIT))]
+
+    def spread(k, tokens):
+        part = SPLIT[k]
+        rows = part * width + (tail_lines if k == 0 else 0)
+        operands = [state] + ([tail_x, tail_bc] if k == 0 else [])
+        specs = [
+            pl.BlockSpec((1, part, width, size), lambda q: (q, offsets[k] // part, 0, 0)),
+            pl.BlockSpec((1, taps - 1, wide), lambda q: (0, 0, q)),
+            pl.BlockSpec((1, 2, taps - 1, size), lambda q: (0, 0, 0, q)),
+        ][: len(operands)]
+        sent = pl.pallas_call(
+            functools.partial(drop_tokens, cast_kernel, len(operands), len(tokens)),
+            grid=(groups,),
+            in_specs=specs + [pl.BlockSpec(memory_space=pl.ANY)] * len(tokens),
+            out_specs=pl.BlockSpec((2, 1, rows, size), lambda q: (0, q, 0, 0)),
+            out_shape=jax.ShapeDtypeStruct((2, groups, rows, size), jnp.bfloat16),
+            compiler_params=pltpu.CompilerParams(vmem_limit_bytes=VMEM_LIMIT),
+            cost_estimate=pl.CostEstimate(
+                flops=0, bytes_accessed=8 * groups * rows * size, transcendentals=0
+            ),
+            name="cast_states",
+        )(*operands, *tokens)
+        return sent, exchange(sent.reshape(ways, rows, size))
+
+    def pick(k, held, tokens):
+        rows = SPLIT[k] * width
+        sizes = [rows] + ([tail_lines] if k == 0 else [])
+        spots = side * kids
+        picked = pl.pallas_call(
+            functools.partial(drop_tokens, pick_rows_kernel, 2, len(tokens)),
+            grid_spec=pltpu.PrefetchScalarGridSpec(
+                num_scalar_prefetch=1,
+                grid=(1,),
+                in_specs=[pl.BlockSpec(held.shape, lambda i, s: (0, 0, 0))]
+                + [pl.BlockSpec(memory_space=pl.ANY)] * len(tokens),
+                out_specs=[pl.BlockSpec(memory_space=pl.ANY)] * len(sizes),
+                scratch_shapes=[pltpu.SemaphoreType.DMA((len(sizes), spots))],
+            ),
+            out_shape=[jax.ShapeDtypeStruct((spots, r, size), jnp.bfloat16) for r in sizes],
+            compiler_params=pltpu.CompilerParams(vmem_limit_bytes=VMEM_LIMIT),
+            cost_estimate=pl.CostEstimate(
+                flops=0, bytes_accessed=4 * spots * rows * size, transcendentals=0
+            ),
+            name="pick_states",
+        )(slots, held, *tokens)
+        return [exchange(p, axis_index_groups=halves) for p in picked[::-1]][::-1]
+
+    sent, held = [], []
+    for k in range(len(SPLIT)):
+        buffer, gathered = spread(k, sent[-1:])
+        sent.append(buffer)
+        held.append(gathered)
+
+    x_conv, b_conv, c_conv, row, column = pl.pallas_call(
+        conv_kernel,
+        grid=(kids, groups),
+        in_specs=[
+            pl.BlockSpec((1, length, wide), lambda c, q: (c, 0, q)),
+            pl.BlockSpec((1, length, size), lambda c, q: (c, 0, q)),
+            pl.BlockSpec((1, length, size), lambda c, q: (c, 0, q)),
+            pl.BlockSpec((1, per_group, length), lambda c, q: (c, q, 0)),
+            pl.BlockSpec((per_group, 1), lambda c, q: (q, 0)),
+            pl.BlockSpec((per_group, 1), lambda c, q: (q, 0)),
+            pl.BlockSpec((taps, wide), lambda c, q: (0, q)),
+            pl.BlockSpec((2, taps, size), lambda c, q: (0, 0, q)),
+        ],
+        out_specs=[
+            pl.BlockSpec((1, length, wide), lambda c, q: (c, 0, q)),
+            pl.BlockSpec((1, length, size), lambda c, q: (c, 0, q)),
+            pl.BlockSpec((1, length, size), lambda c, q: (c, 0, q)),
+            pl.BlockSpec((1, per_group, length), lambda c, q: (c, q, 0)),
+            pl.BlockSpec((1, 1, length, per_group), lambda c, q: (c, q, 0, 0)),
+        ],
+        out_shape=[
+            jax.ShapeDtypeStruct(x_in.shape, jnp.bfloat16),
+            jax.ShapeDtypeStruct(b_in.shape, jnp.bfloat16),
+            jax.ShapeDtypeStruct(c_in.shape, jnp.bfloat16),
+            jax.ShapeDtypeStruct(dt_in.shape, jnp.float32),
+            jax.ShapeDtypeStruct((kids, groups, length, per_group), jnp.float32),
+        ],
+        scratch_shapes=[pltpu.VMEM((8 + length, size), jnp.float32)],
+        compiler_params=pltpu.CompilerParams(vmem_limit_bytes=VMEM_LIMIT),
+        cost_estimate=pl.CostEstimate(
+            flops=20 * kids * length * columns,
+            bytes_accessed=4 * kids * length * columns,
+            transcendentals=kids * length * columns,
+        ),
+        name="conv",
+    )(x_in, b_in, c_in, dt_in, dt_bias[:, None], a_log[:, None], conv_x, conv_bc)
+
+    skip_row = jnp.repeat(d_skip, width)[None, :]
+
+    def mix(c, tails_here, before, tokens):
+        at = lambda q: (c, 0, q)
+        operands = [
+            x_conv, x_in, b_conv, b_in, c_conv, c_in, row, column, skip_row, conv_x, conv_bc,
+            tails_here.reshape(side, kids, tail_lines, size), *tokens, *before,
+        ]
+        first = len(operands) - len(before)
+        return pl.pallas_call(
+            functools.partial(mix_kernel, lines),
+            grid=(groups,),
+            in_specs=[
+                pl.BlockSpec((1, length, wide), at),
+                pl.BlockSpec((1, FIX, wide), at),
+                pl.BlockSpec((1, length, size), at),
+                pl.BlockSpec((1, FIX, size), at),
+                pl.BlockSpec((1, length, size), at),
+                pl.BlockSpec((1, FIX, size), at),
+                pl.BlockSpec((1, per_group, length), lambda q: (c, q, 0)),
+                pl.BlockSpec((1, 1, length, per_group), lambda q: (c, q, 0, 0)),
+                pl.BlockSpec((1, wide), lambda q: (0, q)),
+                pl.BlockSpec((taps, wide), lambda q: (0, q)),
+                pl.BlockSpec((2, taps, size), lambda q: (0, 0, q)),
+                pl.BlockSpec((1, 1, tail_lines, size), lambda q: (q, c, 0, 0)),
+                *[pl.BlockSpec(memory_space=pl.ANY)] * (len(tokens) + len(before)),
+            ],
+            out_specs=[pl.BlockSpec((1, length, wide), at), pl.BlockSpec((1, length, size), at)],
+            out_shape=[
+                jax.ShapeDtypeStruct(x_in.shape, jnp.float32),
+                jax.ShapeDtypeStruct(c_in.shape, jnp.bfloat16),
+            ],
+            input_output_aliases={first + i: i for i in range(len(before))},
+            scratch_shapes=[pltpu.VMEM((8 + FIX, size), jnp.float32)],
+            compiler_params=pltpu.CompilerParams(vmem_limit_bytes=VMEM_LIMIT),
+            cost_estimate=pl.CostEstimate(
+                flops=4 * heads * length * length * width,
+                bytes_accessed=6 * length * columns,
+                transcendentals=heads * length * length,
+            ),
+            name="mix",
+        )(*operands)
+
+    def finish(k, states, mixed, result):
+        part, offset = SPLIT[k], offsets[k]
+        chunk = part * width
+        blocks = per_group // part
+        at = lambda c, q: (c, 0, q * blocks + offset // part)
+        operands = [states.reshape(side, kids, chunk, size), mixed[1], column, mixed[0]]
+        specs = [
+            pl.BlockSpec((1, 1, chunk, size), lambda c, q: (q, c, 0, 0)),
+            pl.BlockSpec((1, length, size), lambda c, q: (c, 0, q)),
+            pl.BlockSpec((1, 1, length, per_group), lambda c, q: (c, q, 0, 0)),
+            pl.BlockSpec((1, length, chunk), at),
+        ]
+        alias = {}
+        if result is not None:
+            alias = {len(operands): 0}
+            operands.append(result)
+            specs.append(pl.BlockSpec(memory_space=pl.ANY))
+        return pl.pallas_call(
+            functools.partial(state_kernel, offset),
+            grid=(kids, groups),
+            in_specs=specs,
+            out_specs=pl.BlockSpec((1, length, chunk), at),
+            out_shape=jax.ShapeDtypeStruct(x_in.shape, jnp.bfloat16),
+            input_output_aliases=alias,
+            compiler_params=pltpu.CompilerParams(vmem_limit_bytes=VMEM_LIMIT),
+            cost_estimate=pl.CostEstimate(
+                flops=2 * kids * groups * length * chunk * size,
+                bytes_accessed=6 * kids * groups * length * chunk,
+                transcendentals=kids * groups * length * chunk,
+            ),
+            name="add_states",
+        )(*operands)
+
+    arrived, tails_here = pick(0, held[0], [x_conv])
+    mixed = mix(0, tails_here, [], [])
+    states = [arrived] + [pick(k, held[k], [mixed[0]])[0] for k in range(1, len(SPLIT))]
+    mixed = mix(1, tails_here, mixed, [])
+    result = None
+    for k in range(len(SPLIT)):
+        result = finish(k, states[k], mixed, result)
+    return result
+
+
 def solution(mesh):
     rows, cols = P(("groups", "batch"), None, "head"), P(("groups", "batch"), "head")
     placed = (
-        rows,
-        rows,
-        rows,
-        cols,
-        P("head"),
-        P("head"),
-        P("head"),
-        P(None, "head"),
-        P(None, None, "head"),
-        cols,
-        rows,
-        P(("groups", "batch"), None, None, "head"),
-        P("groups"),
-        P("groups"),
-    )
+        rows, rows, rows, cols, P("head"), P("head"), P("head"), P(None, "head"),
+        P(None, None, "head"), cols, rows, P(("groups", "batch"), None, None, "head"),
+        P("groups"), P("groups"),
+    )
+    local = local_halves if mesh.shape["batch"] == 8 else local_any
     return jax.shard_map(local, mesh=mesh, in_specs=placed, out_specs=rows, check_vma=False)

time: 116 us -> 122 us (1.052)
  Pallas kernels: 42 us -> 54.6 us
  blocking collectives: 0 us -> 8.8 us
  waiting for transfers between devices: 40.2 us -> 33.7 us
  local copies, waits for them, and re-layouts: 10.6 us -> 5.11 us
  other arithmetic: 5.58 us -> 0.2 us
    pallas_call x3 -> x9, Pallas kernels: 42 us -> 54.6 us  [the longest x2 16 us: finish(): pl.pallas_call(functools.partial(state_kernel, offset), grid=(kids, group...]
    all_to_all x0 -> x1, blocking collectives: none -> 8.8 us  [pick(): return [exchange(p, axis_index_groups=halves) for p in picked[::-1]][::-1]]
    all_to_all x3 -> x4, waiting for transfers between devices: 40.2 us -> 33.7 us  [the longest x2 32.8 us: spread(): return (sent, exchange(sent.reshape(ways, rows, size)))]
    unnamed x38 -> x19, local copies, waits for them, and re-layouts: 8.32 us -> 2.28 us
    convert_element_type x1 -> x0, other arithmetic: 2.82 us -> none  [local(): sent = par_state.astype(jnp.bfloat16).reshape(ways, part, width, size)]
    broadcast_in_dim x1 -> x0, other arithmetic: 2.06 us -> none  [local(): tails = jnp.broadcast_to(tails[None], (ways, tails.shape[0]))]
    all_to_all x3 -> x4, starting transfers between devices: 16.9 us -> 18.1 us  [the longest x2 11.1 us: spread(): return (sent, exchange(sent.reshape(ways, rows, size)))]
  transfers between devices with their start and end apart: 3 -> 4, of which waited for: 2 -> 3; matrix products, arithmetic and copies ran while one was open for 5% -> 3% of each run, Pallas kernels for 28% -> 36%
where the time goes in v3:
time: 122 us; the launch traced here: 121 us
  Pallas kernels  54.6 us (45%)
  waiting for transfers between devices  33.7 us (28%)
  starting transfers between devices  18.1 us (15%)
  blocking collectives  8.8 us (7%)
  local copies, waits for them, and re-layouts  5.11 us (4%)
    all_to_all x2, waiting for transfers between devices, spread(): return (sent, exchange(sent.reshape(ways, rows, size)))  32.8 us
    pallas_call x2, Pallas kernels, finish(): pl.pallas_call(functools.partial(state_kernel, offset), grid=(kids, group...  16 us
    pallas_call x2, Pallas kernels, mix(): pl.pallas_call(functools.partial(mix_kernel, lines), grid=(groups,), in_s...  14.2 us
    pallas_call x1, Pallas kernels, local_halves(): pl.pallas_call(conv_kernel, grid=(kids, groups), in_specs=[pl.BlockSpec((...  11.6 us
    all_to_all x2, starting transfers between devices, spread(): return (sent, exchange(sent.reshape(ways, rows, size)))  11.1 us
    all_to_all x1, blocking collectives, pick(): return [exchange(p, axis_index_groups=halves) for p in picked[::-1]][::-1]  8.8 us
    all_to_all x2, starting transfers between devices, pick(): return [exchange(p, axis_index_groups=halves) for p in picked[::-1]][::-1]  7.03 us
    pallas_call x2, Pallas kernels, spread(): pl.pallas_call(functools.partial(drop_tokens, cast_kernel, len(operands),...  6.82 us
  transfers between devices with their start and end apart: 4, of which 3 were waited for; matrix products, arithmetic and copies ran while one was open for 3% of the time, Pallas kernels for 36%

profile of v3, /device:TPU:0, one launch (start us, length us, event | category | flops | bytes accessed | tf_op | source)
XLA Modules:
  0.0 120.7 jit_solution(5847217282416496888)
XLA Ops:
  0.0 1.3 %copy.21.refs_2_ = bf16[1,2,3,512]{3,2,1,0:T(4,128)(2,1)} copy(bf16[1,2,3,512]{3,1,2,0:T(2,128)(2,1)} %param.25) | data formatting | bytes 12288 | tf_op args[11]
  1.3 3.4 %cast_states.2.refs_1_ = bf16[2,4,544,128]{3,2,1,0:T(8,128)(2,1)} custom-call(f32[4,16,64,128]{3,2,1,0:T(8,128)} %bitcast.9, bf16[1,3,4096]{2,1,0:T(4,128)(2,1)} %refs_1_.1, bf16[1,2,3,512]{3,2,1,0:T(4,128)(2,1)} %copy.21.refs_2_), custom_call_target="tpu_custom_call" | custom-call | bytes 2228224 | tf_op jit(solution)/shard_map/cast_states/pallas_call | solution.py:431
  4.7 0.0 copy-start.4
  4.7 0.0 copy-start.5
  4.7 0.0 copy-start.7
  4.7 0.0 copy-start.8
  4.7 7.4 %all-to-all-start.1 = ((bf16[8,544,128]{2,1,0:T(8,128)(2,1)}), bf16[8,544,128]{2,1,0:T(8,128)(2,1)S(1)}, u32[]{:S(2)}, u32[]{:S(2)}) async-start(bf16[8,544,128]{2,1,0:T(8,128)(2,1)} %bitcast.8), calls=%async_computation.1 | async-start | bytes 2228224 | tf_op jit(solution)/shard_map/all_to_all | solution.py:443
  12.2 3.4 %cast_states.3 = bf16[2,4,512,128]{3,2,1,0:T(8,128)(2,1)} custom-call(f32[4,16,64,128]{3,2,1,0:T(8,128)} %bitcast.10, bf16[2,4,544,128]{3,2,1,0:T(8,128)(2,1)} %cast_states.2.refs_1_), custom_call_target="tpu_custom_call" | custom-call | bytes 2097152 | tf_op jit(solution)/shard_map/cast_states/pallas_call | solution.py:431
  15.5 23.8 %all-to-all-done.1.refs_1_ = bf16[8,544,128]{2,1,0:T(8,128)(2,1)S(1)} async-done(((bf16[8,544,128]{2,1,0:T(8,128)(2,1)}), bf16[8,544,128]{2,1,0:T(8,128)(2,1)S(1)}, u32[]{:S(2)}, u32[]{:S(2)}) %all-to-all-start.1) | async-done | bytes 1114144 | tf_op jit(solution)/shard_map/all_to_all | solution.py:443
  39.3 0.0 copy-start
  39.3 3.6 %all-to-all-start = ((bf16[8,512,128]{2,1,0:T(8,128)(2,1)}), bf16[8,512,128]{2,1,0:T(8,128)(2,1)S(1)}, u32[]{:S(2)}, u32[]{:S(2)}) async-start(bf16[8,512,128]{2,1,0:T(8,128)(2,1)} %bitcast.12), calls=%async_computation | async-start | bytes 2097152 | tf_op jit(solution)/shard_map/all_to_all | solution.py:443
  43.0 0.0 copy-done.4
  43.0 0.7 copy.22.bias_ref
  43.7 0.0 copy-done.5
  43.7 0.7 copy.23.alog_ref
  44.4 0.0 copy-done.7
  44.4 0.1 select_reduce_fusion
  44.5 0.0 copy-done.8
  44.5 0.1 convert_reduce_fusion
  44.6 0.7 dynamic_slice.3.refs_0_
  45.2 11.6 %conv.1 = (bf16[2,256,4096]{2,1,0:T(8,128)(2,1)}, bf16[2,256,512]{2,1,0:T(8,128)(2,1)}, bf16[2,256,512]{2,1,0:T(8,128)(2,1)}, f32[2,64,256]{2,1,0:T(8,128)}, f32[2,4,256,16]{3,2,1,0:T(8,128)}) custom-call(bf16[2,256,4096]{2,1,0:T(8,128)(2,1)} %xin_ref.3, bf16[2,256,512]{2,1,0:T(8,128)(2,1)} %bin_ref.3, bf16[2,256,512]{2,1,0:T(8,128)(2,1)} %cin_ref.3, ...), custom_call_target="tpu_custom_call" | custom-call | flops 41943040 | bytes 8388608 | tf_op jit(solution)/shard_map/conv/pallas_call | solution.py:474
  56.9 0.0 copy-start.6
  56.9 0.0 copy-done
  56.9 3.1 %pick_states.2 = (bf16[8,512,128]{2,1,0:T(8,128)(2,1)}, bf16[8,32,128]{2,1,0:T(8,128)(2,1)}) custom-call(s32[8]{0:T(128)} %dynamic_slice.3.refs_0_, bf16[8,544,128]{2,1,0:T(8,128)(2,1)} %copy-done, bf16[2,256,4096]{2,1,0:T(8,128)(2,1)} %get-tuple-element.16.refs_2_.x_ref), custom_call_target="tpu_custom_call" | custom-call | bytes 2097152 | tf_op jit(solution)/shard_map/pick_states/pallas_call | solution.py:449
  59.9 9.0 %all-to-all-done.refs_1_ = bf16[8,512,128]{2,1,0:T(8,128)(2,1)S(1)} async-done(((bf16[8,512,128]{2,1,0:T(8,128)(2,1)}), bf16[8,512,128]{2,1,0:T(8,128)(2,1)S(1)}, u32[]{:S(2)}, u32[]{:S(2)}) %all-to-all-start) | async-done | bytes 1048608 | tf_op jit(solution)/shard_map/all_to_all | solution.py:443
  68.9 0.0 copy-start.2
  68.9 8.8 %all_to_all.25 = bf16[8,32,128]{2,1,0:T(8,128)(2,1)} all-to-all(bf16[8,32,128]{2,1,0:T(8,128)(2,1)} %get-tuple-element.21), channel_id=1, replica_groups={{0,2,4,6},{8,10,12,14},{1,3,5,7},{9,11,13,15},{16,18,20,22},{24,26,28,3..., dimensions={0} | all-to-all | bytes 131072 | tf_op jit(solution)/shard_map/all_to_all | solution.py:466
  77.7 3.5 %all-to-all-start.4 = ((bf16[8,512,128]{2,1,0:T(8,128)(2,1)}), bf16[8,512,128]{2,1,0:T(8,128)(2,1)S(1)}, u32[]{:S(2)}, u32[]{:S(2)}) async-start(bf16[8,512,128]{2,1,0:T(8,128)(2,1)} %get-tuple-element.26), calls=%async_computation.4 | async-start | bytes 2097152 | tf_op jit(solution)/shard_map/all_to_all | solution.py:466
  81.3 0.0 copy-done.6
  81.3 0.1 broadcast_in_dim.30
  81.3 0.7 broadcast_in_dim_reshape.3.skip_ref
  82.0 7.1 %mix.2 = (f32[2,256,4096]{2,1,0:T(8,128)}, bf16[2,256,512]{2,1,0:T(8,128)(2,1)}) custom-call(bf16[2,256,4096]{2,1,0:T(8,128)(2,1)} %get-tuple-element.16.refs_2_.x_ref, bf16[2,256,4096]{2,1,0:T(8,128)(2,1)} %xin_ref.3, bf16[2,256,512]{2,1,0:T(8,128)(2,1)} %get-tuple-element.17.b_ref, bf16[2,256,512]{2,1,0:T(8,128)(2,1)} %bin_ref.3, ...), custom_call_target="tpu_custom_call" | custom-call | flops 1073741824 | bytes 6291456 | tf_op jit(solution)/shard_map/mix/pallas_call | solution.py:520
  89.1 0.0 copy-done.2
  89.1 2.9 %pick_states.3 = bf16[8,512,128]{2,1,0:T(8,128)(2,1)} custom-call(s32[8]{0:T(128)} %dynamic_slice.3.refs_0_, bf16[8,512,128]{2,1,0:T(8,128)(2,1)} %copy-done.2, f32[2,256,4096]{2,1,0:T(8,128)} %get-tuple-element.22.refs_2_.refs_0_), custom_call_target="tpu_custom_call" | custom-call | bytes 2097152 | tf_op jit(solution)/shard_map/pick_states/pallas_call | solution.py:449
  92.1 1.0 all-to-all-done.4
  93.0 0.0 copy-start.3
  93.0 3.5 %all-to-all-start.3 = ((bf16[8,512,128]{2,1,0:T(8,128)(2,1)}), bf16[8,512,128]{2,1,0:T(8,128)(2,1)S(1)}, u32[]{:S(2)}, u32[]{:S(2)}) async-start(bf16[8,512,128]{2,1,0:T(8,128)(2,1)} %pick_states.3), calls=%async_computation.3 | async-start | bytes 2097152 | tf_op jit(solution)/shard_map/all_to_all | solution.py:466
  96.6 7.1 %mix.3 = (f32[2,256,4096]{2,1,0:T(8,128)}, bf16[2,256,512]{2,1,0:T(8,128)(2,1)}) custom-call(bf16[2,256,4096]{2,1,0:T(8,128)(2,1)} %get-tuple-element.16.refs_2_.x_ref, bf16[2,256,4096]{2,1,0:T(8,128)(2,1)} %xin_ref.3, bf16[2,256,512]{2,1,0:T(8,128)(2,1)} %get-tuple-element.17.b_ref, ...), custom_call_target="tpu_custom_call", output_to_operand_aliasing={{0}: (12, {}), {1}: (13, {})} | custom-call | flops 1073741824 | bytes 6291456 | tf_op jit(solution)/shard_map/mix/pallas_call | solution.py:520
  103.7 0.0 copy-done.3
  103.7 8.0 %add_states.2.refs_0_ = bf16[2,256,4096]{2,1,0:T(8,128)(2,1)} custom-call(bf16[4,2,512,128]{3,2,1,0:T(8,128)(2,1)} %bitcast.13, bf16[2,256,512]{2,1,0:T(8,128)(2,1)} %get-tuple-element.24.c_ref, f32[2,4,256,16]{3,2,1,0:T(8,128)} %get-tuple-element.20.column_ref, f32[2,256,4096]{2,1,0:T(8,128)} %get-tuple-element.25.mixed_ref), custom_call_target="tpu_custom_call" | custom-call | flops 268435456 | bytes 6291456 | tf_op jit(solution)/shard_map/add_states/pallas_call | solution.py:571
  111.7 0.0 all-to-all-done.3
  111.7 0.0 copy-start.1
  111.7 1.0 copy-done.1
  112.7 8.0 %add_states.3 = bf16[2,256,4096]{2,1,0:T(8,128)(2,1)} custom-call(bf16[4,2,512,128]{3,2,1,0:T(8,128)(2,1)} %bitcast.11, bf16[2,256,512]{2,1,0:T(8,128)(2,1)} %get-tuple-element.24.c_ref, f32[2,4,256,16]{3,2,1,0:T(8,128)} %get-tuple-element.20.column_ref, f32[2,256,4096]{2,1,0:T(8,128)} %get-tuple-element.25.mixed_ref, ...), custom_call_target="tpu_custom_call", output_to_operand_aliasing={{}: (4, {})} | custom-call | flops 268435456 | bytes 6291456 | tf_op jit(solution)/shard_map/add_states/pallas_call | solution.py:571
Async XLA Ops:
  4.7 38.3 %copy-start.4 = (f32[64]{0:T(128)S(1)}, f32[64]{0:T(128)}, u32[]{:S(2)}) copy-start(f32[64]{0:T(128)} %param.18) | copy-start | bytes 772
  4.7 39.0 %copy-start.5 = (f32[64]{0:T(128)S(1)}, f32[64]{0:T(128)}, u32[]{:S(2)}) copy-start(f32[64]{0:T(128)} %param.19) | copy-start | bytes 772
  4.7 39.7 %copy-start.7 = (s32[8]{0:T(128)S(1)}, s32[8]{0:T(128)}, u32[]{:S(2)}) copy-start(s32[8]{0:T(128)} %param.26) | copy-start | bytes 100
  4.7 39.8 %copy-start.8 = (s32[16]{0:T(128)S(1)}, s32[16]{0:T(128)}, u32[]{:S(2)}) copy-start(s32[16]{0:T(128)} %param.27) | copy-start | bytes 196
  4.7 34.6 %all-to-all-start.1 = ((bf16[8,544,128]{2,1,0:T(8,128)(2,1)}), bf16[8,544,128]{2,1,0:T(8,128)(2,1)S(1)}, u32[]{:S(2)}, u32[]{:S(2)}) async-start(bf16[8,544,128]{2,1,0:T(8,128)(2,1)} %bitcast.8), calls=%async_computation.1 | async-start | bytes 2228224 | tf_op jit(solution)/shard_map/all_to_all | solution.py:443
  39.3 17.5 %copy-start = (bf16[8,544,128]{2,1,0:T(8,128)(2,1)}, bf16[8,544,128]{2,1,0:T(8,128)(2,1)S(1)}, u32[]{:S(2)}) copy-start(bf16[8,544,128]{2,1,0:T(8,128)(2,1)S(1)} %all-to-all-done.1.refs_1_) | copy-start | bytes 3342340
  39.3 29.6 %all-to-all-start = ((bf16[8,512,128]{2,1,0:T(8,128)(2,1)}), bf16[8,512,128]{2,1,0:T(8,128)(2,1)S(1)}, u32[]{:S(2)}, u32[]{:S(2)}) async-start(bf16[8,512,128]{2,1,0:T(8,128)(2,1)} %bitcast.12), calls=%async_computation | async-start | bytes 2097152 | tf_op jit(solution)/shard_map/all_to_all | solution.py:443
  56.9 24.4 %copy-start.6 = (f32[64]{0:T(128)S(1)}, f32[64]{0:T(128)}, u32[]{:S(2)}) copy-start(f32[64]{0:T(128)} %param.20) | copy-start | bytes 772
  68.9 20.2 %copy-start.2 = (bf16[8,512,128]{2,1,0:T(8,128)(2,1)}, bf16[8,512,128]{2,1,0:T(8,128)(2,1)S(1)}, u32[]{:S(2)}) copy-start(bf16[8,512,128]{2,1,0:T(8,128)(2,1)S(1)} %all-to-all-done.refs_1_) | copy-start | bytes 3145732
  77.7 15.3 %all-to-all-start.4 = ((bf16[8,512,128]{2,1,0:T(8,128)(2,1)}), bf16[8,512,128]{2,1,0:T(8,128)(2,1)S(1)}, u32[]{:S(2)}, u32[]{:S(2)}) async-start(bf16[8,512,128]{2,1,0:T(8,128)(2,1)} %get-tuple-element.26), calls=%async_computation.4 | async-start | bytes 2097152 | tf_op jit(solution)/shard_map/all_to_all | solution.py:466
  93.0 10.6 %copy-start.3 = (bf16[8,512,128]{2,1,0:T(8,128)(2,1)}, bf16[8,512,128]{2,1,0:T(8,128)(2,1)S(1)}, u32[]{:S(2)}) copy-start(bf16[8,512,128]{2,1,0:T(8,128)(2,1)S(1)} %all-to-all-done.4) | copy-start | bytes 3145732
  93.0 18.7 %all-to-all-start.3 = ((bf16[8,512,128]{2,1,0:T(8,128)(2,1)}), bf16[8,512,128]{2,1,0:T(8,128)(2,1)S(1)}, u32[]{:S(2)}, u32[]{:S(2)}) async-start(bf16[8,512,128]{2,1,0:T(8,128)(2,1)} %pick_states.3), calls=%async_computation.3 | async-start | bytes 2097152 | tf_op jit(solution)/shard_map/all_to_all | solution.py:466
  111.7 1.0 copy-start.1

commit v4 on v1

--- a/solution.py
+++ b/solution.py
@@ -7,7 +7,13 @@
 from jax.experimental.pallas import tpu as pltpu
 from jax.sharding import PartitionSpec as P
 
-VMEM_LIMIT = 48 * 1024 * 1024
+VMEM_LIMIT = 20 * 1024 * 1024
+SPLIT = (8, 8)
+FIX = 16
+
+
+def drop_tokens(kernel, keep, tokens, *refs):
+    kernel(*refs[:keep], *refs[keep + tokens :])
 
 
 def parent_of(counts, order):
@@ -19,12 +25,164 @@
 def conv_silu(padded, tail, rows, taps):
     length = rows.shape[0]
     reach = taps.shape[0] - 1
-    padded[8 - reach : 8, :] = tail.astype(jnp.float32)
+    padded[8 - reach : 8, :] = jnp.broadcast_to(tail, (reach, rows.shape[1])).astype(jnp.float32)
     padded[8 : 8 + length, :] = rows.astype(jnp.float32)
     total = padded[8 - reach : 8 - reach + length, :] * taps[0:1, :]
     for k in range(1, reach + 1):
         total = total + padded[8 - reach + k : 8 - reach + k + length, :] * taps[k : k + 1, :]
-    return (total / (1.0 + jnp.exp(-total))).astype(jnp.bfloat16)
+    half = 0.5 * total
+    return (half + half * jnp.tanh(half)).astype(jnp.bfloat16)
+
+
+def conv_kernel(
+    x_ref, b_ref, c_ref, dt_ref, bias_ref, alog_ref, taps_x_ref, taps_bc_ref,
+    xc_ref, bc_ref, cc_ref, row_ref, column_ref, padded,
+):
+    length = x_ref.shape[1]
+    lanes_all = x_ref.shape[2]
+    bc_ref[...] = conv_silu(padded, 0.0, b_ref[0], taps_bc_ref[0])
+    cc_ref[...] = conv_silu(padded, 0.0, c_ref[0], taps_bc_ref[1])
+    for start in range(0, lanes_all, 128):
+        lanes = slice(start, start + 128)
+        xc_ref[:, lanes] = conv_silu(padded, 0.0, x_ref[0, :, lanes], taps_x_ref[:, lanes])
+    raw = dt_ref[0] + bias_ref[...]
+    step = jnp.maximum(raw, 0.0) + jnp.log1p(jnp.exp(-jnp.abs(raw)))
+    per_token = step * (-jnp.exp(alog_ref[...]))
+    row = lax.broadcasted_iota(jnp.int32, (length, length), 0)
+    col = lax.broadcasted_iota(jnp.int32, (length, length), 1)
+    total = lax.dot_general(
+        per_token,
+        (row <= col).astype(jnp.float32),
+        (((1,), (0,)), ((), ())),
+        precision=lax.Precision.HIGHEST,
+        preferred_element_type=jnp.float32,
+    )
+    row_ref[...] = total - jnp.log(step)
+    column_ref[0] = total.T
+
+
+def choose(refs, place):
+    j = place ^ pl.program_id(0)
+    near = jnp.where(j == 0, refs[0][0], refs[1][0])
+    return jnp.where(j <= 1, near, jnp.where(j == 2, refs[2][0], refs[3][0]))
+
+
+def mix_kernel(
+    lines, x_ref, xin_ref, b_ref, bin_ref, c_ref, cin_ref, row_ref, column_ref, skip_ref,
+    taps_x_ref, taps_bc_ref, place_ref, *refs,
+):
+    mixed_ref, c_out_ref, padded = refs[-3:]
+    length, wide = x_ref.shape
+    heads = row_ref.shape[0]
+    width = wide // heads
+    half = length // 2
+    reach = taps_x_ref.shape[0] - 1
+    tail = choose(refs[:4], place_ref[0]).astype(jnp.float32)
+
+    def fixed(bulk_ref, first_ref, lanes, taps, at):
+        rows = jnp.concatenate([tail[k * lines + at : k * lines + at + 1] for k in range(reach)])
+        first = conv_silu(padded, rows, first_ref[0, :, lanes], taps)
+        return jnp.concatenate([first, bulk_ref[FIX:, lanes]])
+
+    every = slice(0, b_ref.shape[1])
+    b_conv = fixed(b_ref, bin_ref, every, taps_bc_ref[0], lines - 2)
+    c_conv = fixed(c_ref, cin_ref, every, taps_bc_ref[1], lines - 1)
+    c_out_ref[...] = c_conv
+    scores = lax.dot_general(
+        c_conv, b_conv, (((1,), (1,)), ((), ())), preferred_element_type=jnp.float32
+    )
+    causal = lax.broadcasted_iota(jnp.int32, (half, half), 0) >= lax.broadcasted_iota(
+        jnp.int32, (half, half), 1
+    )
+    low = lax.broadcasted_iota(jnp.int32, (length, 2 * width), 1) < width
+    for pair in range(heads // 2):
+        lanes = slice(pair * 2 * width, (pair + 1) * 2 * width)
+        x_conv = fixed(x_ref, xin_ref, lanes, taps_x_ref[:, lanes], pair)
+        parts = []
+        for head in (2 * pair, 2 * pair + 1):
+            column = jnp.broadcast_to(column_ref[0, :, head : head + 1], (length, half))
+            rows = row_ref[head : head + 1, :]
+            near = jnp.exp(jnp.where(causal, column[:half] - rows[:, :half], -1e30))
+            far = jnp.exp(column[half:] - rows[:, :half])
+            last = jnp.exp(jnp.where(causal, column[half:] - rows[:, half:], -1e30))
+            top = (scores[:half, :half] * near).astype(jnp.bfloat16)
+            left = (scores[half:, :half] * far).astype(jnp.bfloat16)
+            right = (scores[half:, half:] * last).astype(jnp.bfloat16)
+            below = jnp.concatenate([left, right], axis=1)
+            parts.append(
+                jnp.concatenate(
+                    [
+                        jnp.dot(top, x_conv[:half], preferred_element_type=jnp.float32),
+                        jnp.dot(below, x_conv, preferred_element_type=jnp.float32),
+                    ]
+                )
+            )
+        mixed_ref[:, lanes] = jnp.where(low, parts[0], parts[1]) + skip_ref[
+            :, lanes
+        ] * x_conv.astype(jnp.float32)
+
+
+def state_kernel(offset, place_ref, *refs):
+    y_ref = refs[-1]
+    kids, length, wide = y_ref.shape
+    low = lax.broadcasted_iota(jnp.int32, (length, 128), 1) < 64
+    for kid in range(kids):
+        c_ref, column_ref, mixed_ref = refs[7 * kid + 4 : 7 * kid + 7]
+        state = choose(refs[7 * kid : 7 * kid + 4], place_ref[0])
+        term = lax.dot_general(
+            c_ref[...], state, (((1,), (1,)), ((), ())), preferred_element_type=jnp.float32
+        )
+        for pair in range(wide // 128):
+            lanes = slice(pair * 128, pair * 128 + 128)
+            head = offset + 2 * pair
+            grow = jnp.where(
+                low, column_ref[0, :, head : head + 1], column_ref[0, :, head + 1 : head + 2]
+            )
+            carried = (term[:, lanes] * jnp.exp(grow)).astype(jnp.bfloat16).astype(jnp.float32)
+            y_ref[kid, :, lanes] = (mixed_ref[:, lanes] + carried).astype(jnp.bfloat16)
+
+
+def cast_kernel(reach, lines, at_ref, *refs):
+    outs = refs[-4:]
+    for j, out_ref in enumerate(outs):
+        state = refs[j][0]
+        rows = state.shape[0] * state.shape[1]
+        out_ref[:rows] = state.reshape(rows, state.shape[2]).astype(jnp.bfloat16)
+        if lines:
+            x_tail = refs[4 + j][0].astype(jnp.float32)
+            bc_tail = refs[8 + j][0].astype(jnp.float32)
+            parts = []
+            for k in range(reach):
+                parts += [x_tail[k : k + 1, i * 128 : i * 128 + 128] for i in range(lines - 2)]
+                parts.append(bc_tail[k])
+            spare = out_ref.shape[0] - rows - lines * reach
+            parts.append(jnp.zeros((spare, 128), jnp.float32))
+            out_ref[rows:] = jnp.concatenate(parts).astype(jnp.bfloat16)
+
+
+def pick_rows_kernel(slots_ref, *refs):
+    count = 8
+    held, outs = refs[:count], refs[count:-3]
+    stage, in_sems, out_sems = refs[-3:]
+    kids = outs[0].shape[0]
+    loads = [
+        pltpu.make_async_copy(ref, stage.at[i], in_sems.at[i]) for i, ref in enumerate(held)
+    ]
+    for load in loads:
+        load.start()
+    for load in loads:
+        load.wait()
+    stores = [
+        pltpu.make_async_copy(
+            stage.at[slots_ref[j * kids + kid]], out.at[kid], out_sems.at[j, kid]
+        )
+        for j, out in enumerate(outs)
+        for kid in range(kids)
+    ]
+    for store in stores:
+        store.start()
+    for store in stores:
+        store.wait()
 
 
 def within_kernel(
@@ -112,7 +270,7 @@
     out_ref[...] = state_ref[...]
 
 
-def local(
+def local_any(
     x_in,
     b_in,
     c_in,
@@ -245,22 +403,250 @@
     )(states, c_conv, grow, mixed)
 
 
+def local_halves(
+    x_in, b_in, c_in, dt_in, dt_bias, a_log, d_skip, conv_x, conv_bc,
+    par_state, tail_x, tail_bc, counts, order,
+):
+    kids, length, columns = x_in.shape
+    heads = dt_in.shape[1]
+    width, size = par_state.shape[2:]
+    groups = b_in.shape[2] // size
+    per_group = heads // groups
+    wide = per_group * width
+    taps = conv_x.shape[0]
+    reach = taps - 1
+    lines = (wide + 2 * size) // 128
+    tail_lines = -(-lines * reach // 16) * 16
+    params = pltpu.CompilerParams(vmem_limit_bytes=VMEM_LIMIT)
+    anywhere = pl.BlockSpec(memory_space=pl.ANY)
+
+    stay = lambda x: pltpu.with_memory_space_constraint(x, pltpu.HBM)
+    x_in, b_in, c_in, dt_in, conv_x, conv_bc = map(stay, (x_in, b_in, c_in, dt_in, conv_x, conv_bc))
+
+    me = lax.axis_index("batch")
+    parent = parent_of(counts, order)
+    near = me ^ jnp.arange(4, dtype=jnp.int32)
+    children = (near[:, None] * kids + jnp.arange(kids, dtype=jnp.int32)[None, :]).reshape(-1)
+    slots = jnp.take(parent, children) ^ me
+    place = (me % 4).astype(jnp.int32)[None]
+
+    state = stay(par_state.reshape(groups, per_group, width, size))
+    x_tails, bc_tails = stay(tail_x), stay(tail_bc.transpose(0, 2, 1, 3))
+    offsets = [sum(SPLIT[:k]) for k in range(len(SPLIT))]
+
+    def swap(value, r):
+        return lax.ppermute(value, "batch", perm=[(i, i ^ r) for i in range(8)])
+
+    def spread(k, tokens):
+        part = SPLIT[k]
+        rows = part * width + (tail_lines if k == 0 else 0)
+        operands = [state] * 4
+        specs = [
+            pl.BlockSpec((1, part, width, size), lambda i, p, j=j: (p[0] ^ j, offsets[k] // part, 0, 0))
+            for j in range(4)
+        ]
+        if k == 0:
+            operands += [x_tails] * 4 + [bc_tails] * 4
+            specs += [
+                pl.BlockSpec((1, reach, wide), lambda i, p, j=j: (0, 0, p[0] ^ j)) for j in range(4)
+            ]
+            specs += [
+                pl.BlockSpec((1, reach, 2, size), lambda i, p, j=j: (0, 0, 0, p[0] ^ j))
+                for j in range(4)
+            ]
+        sent = pl.pallas_call(
+            functools.partial(
+                drop_tokens,
+                functools.partial(cast_kernel, reach, lines if k == 0 else 0),
+                1 + len(operands),
+                len(tokens),
+            ),
+            grid_spec=pltpu.PrefetchScalarGridSpec(
+                num_scalar_prefetch=1,
+                grid=(1,),
+                in_specs=specs + [anywhere] * len(tokens),
+                out_specs=[pl.BlockSpec((rows, size), lambda i, p: (0, 0))] * 4,
+            ),
+            out_shape=[jax.ShapeDtypeStruct((rows, size), jnp.bfloat16)] * 4,
+            compiler_params=params,
+            cost_estimate=pl.CostEstimate(
+                flops=0, bytes_accessed=24 * rows * size, transcendentals=0
+            ),
+            name="cast_states",
+        )(place, *operands, *tokens)
+        far = [swap(sent[j], j + 4) for j in range(4)]
+        return [sent[0]] + [swap(sent[j], j) for j in range(1, 4)] + far
+
+    def pick(k, held, tokens):
+        rows = held[0].shape[0]
+        picked = pl.pallas_call(
+            functools.partial(drop_tokens, pick_rows_kernel, 9, len(tokens)),
+            grid_spec=pltpu.PrefetchScalarGridSpec(
+                num_scalar_prefetch=1,
+                grid=(1,),
+                in_specs=[anywhere] * (8 + len(tokens)),
+                out_specs=[anywhere] * 4,
+                scratch_shapes=[
+                    pltpu.VMEM((8, rows, size), jnp.bfloat16),
+                    pltpu.SemaphoreType.DMA((8,)),
+                    pltpu.SemaphoreType.DMA((4, kids)),
+                ],
+            ),
+            out_shape=[jax.ShapeDtypeStruct((kids, rows, size), jnp.bfloat16)] * 4,
+            compiler_params=params,
+            cost_estimate=pl.CostEstimate(
+                flops=0, bytes_accessed=32 * kids * rows * size, transcendentals=0
+            ),
+            name="pick_states",
+        )(slots, *held, *tokens)
+        return [picked[0]] + [swap(picked[j], j) for j in range(1, 4)]
+
+    def convolve(c, tokens):
+        at = lambda q: (c, 0, q)
+        operands = [
+            x_in, b_in, c_in, dt_in, dt_bias[:, None], a_log[:, None], conv_x, conv_bc
+        ]
+        return pl.pallas_call(
+            functools.partial(drop_tokens, conv_kernel, len(operands), len(tokens)),
+            grid=(groups,),
+            in_specs=[
+                pl.BlockSpec((1, length, wide), at),
+                pl.BlockSpec((1, length, size), at),
+                pl.BlockSpec((1, length, size), at),
+                pl.BlockSpec((1, per_group, length), lambda q: (c, q, 0)),
+                pl.BlockSpec((per_group, 1), lambda q: (q, 0)),
+                pl.BlockSpec((per_group, 1), lambda q: (q, 0)),
+                pl.BlockSpec((taps, wide), lambda q: (0, q)),
+                pl.BlockSpec((2, taps, size), lambda q: (0, 0, q)),
+                *[anywhere] * len(tokens),
+            ],
+            out_specs=[
+                pl.BlockSpec((length, wide), lambda q: (0, q)),
+                pl.BlockSpec((length, size), lambda q: (0, q)),
+                pl.BlockSpec((length, size), lambda q: (0, q)),
+                pl.BlockSpec((per_group, length), lambda q: (q, 0)),
+                pl.BlockSpec((1, length, per_group), lambda q: (q, 0, 0)),
+            ],
+            out_shape=[
+                jax.ShapeDtypeStruct(x_in.shape[1:], jnp.bfloat16),
+                jax.ShapeDtypeStruct(b_in.shape[1:], jnp.bfloat16),
+                jax.ShapeDtypeStruct(c_in.shape[1:], jnp.bfloat16),
+                jax.ShapeDtypeStruct(dt_in.shape[1:], jnp.float32),
+                jax.ShapeDtypeStruct((groups, length, per_group), jnp.float32),
+            ],
+            scratch_shapes=[pltpu.VMEM((8 + length, size), jnp.float32)],
+            compiler_params=params,
+            cost_estimate=pl.CostEstimate(
+                flops=40 * length * columns,
+                bytes_accessed=4 * length * columns,
+                transcendentals=2 * length * columns,
+            ),
+            name="conv",
+        )(*operands, *tokens)
+
+    def mix(c, early, states, tokens):
+        x_conv, b_conv, c_conv, row, column = early
+        at = lambda q: (0, q)
+        tail_at = SPLIT[0] * width // tail_lines
+        operands = [
+            x_conv, x_in, b_conv, b_in, c_conv, c_in, row, column, skip_row, conv_x, conv_bc,
+            place, *states,
+        ]
+        return pl.pallas_call(
+            functools.partial(drop_tokens, functools.partial(mix_kernel, lines), 16, len(tokens)),
+            grid=(groups,),
+            in_specs=[
+                pl.BlockSpec((length, wide), at),
+                pl.BlockSpec((1, FIX, wide), lambda q: (c, 0, q)),
+                pl.BlockSpec((length, size), at),
+                pl.BlockSpec((1, FIX, size), lambda q: (c, 0, q)),
+                pl.BlockSpec((length, size), at),
+                pl.BlockSpec((1, FIX, size), lambda q: (c, 0, q)),
+                pl.BlockSpec((per_group, length), lambda q: (q, 0)),
+                pl.BlockSpec((1, length, per_group), lambda q: (q, 0, 0)),
+                pl.BlockSpec((1, wide), at),
+                pl.BlockSpec((taps, wide), at),
+                pl.BlockSpec((2, taps, size), lambda q: (0, 0, q)),
+                pl.BlockSpec(memory_space=pltpu.SMEM),
+                *[pl.BlockSpec((1, tail_lines, size), lambda q: (c, tail_at, 0))] * 4,
+                *[anywhere] * len(tokens),
+            ],
+            out_specs=[pl.BlockSpec((length, wide), at), pl.BlockSpec((length, size), at)],
+            out_shape=[
+                jax.ShapeDtypeStruct((length, columns), jnp.float32),
+                jax.ShapeDtypeStruct((length, groups * size), jnp.bfloat16),
+            ],
+            scratch_shapes=[
+                pltpu.VMEM((8 + FIX, size), jnp.float32),
+            ],
+            compiler_params=params,
+            cost_estimate=pl.CostEstimate(
+                flops=4 * heads * length * length * width,
+                bytes_accessed=6 * length * columns,
+                transcendentals=heads * length * length,
+            ),
+            name="mix",
+        )(*operands, *tokens)
+
+    def finish(k, states, early, mixed, result):
+        part, offset = SPLIT[k], offsets[k]
+        chunk = part * width
+        at = lambda q, p: (0, q * (per_group // part) + offset // part)
+        operands, specs = [], []
+        for c in range(kids):
+            operands += [*states, mixed[c][1], early[c][4], mixed[c][0]]
+            specs += [
+                *[pl.BlockSpec((1, chunk, size), lambda q, p, c=c: (c, 0, 0))] * 4,
+                pl.BlockSpec((length, size), lambda q, p: (0, q)),
+                pl.BlockSpec((1, length, per_group), lambda q, p: (q, 0, 0)),
+                pl.BlockSpec((length, chunk), at),
+            ]
+        alias = {}
+        if result is not None:
+            alias = {1 + len(operands): 0}
+            operands.append(result)
+            specs.append(anywhere)
+        return pl.pallas_call(
+            functools.partial(state_kernel, offset),
+            grid_spec=pltpu.PrefetchScalarGridSpec(
+                num_scalar_prefetch=1,
+                grid=(groups,),
+                in_specs=specs,
+                out_specs=pl.BlockSpec((kids, length, chunk), lambda q, p: (0, *at(q, p))),
+            ),
+            out_shape=jax.ShapeDtypeStruct(x_in.shape, jnp.bfloat16),
+            input_output_aliases=alias,
+            compiler_params=params,
+            cost_estimate=pl.CostEstimate(
+                flops=2 * kids * groups * length * chunk * size,
+                bytes_accessed=6 * kids * groups * length * chunk,
+                transcendentals=kids * groups * length * chunk,
+            ),
+            name="add_states",
+        )(place, *operands)
+
+    skip_row = jnp.repeat(d_skip, width)[None, :]
+    held, early = [], []
+    for k in range(len(SPLIT)):
+        held.append(spread(k, [held[-1][0]] if k else []))
+    early.append(convolve(0, [held[1][0]]))
+    states = [pick(0, held[0], [early[0][0]])]
+    early.append(convolve(1, [states[0][0]]))
+    mixed = [mix(0, early[0], states[0], [early[1][0]])]
+    states.append(pick(1, held[1], [mixed[0][1]]))
+    mixed.append(mix(1, early[1], states[0], [states[1][0]]))
+    result = None
+    for k in range(len(SPLIT)):
+        result = finish(k, states[k], early, mixed, result)
+    return result
+
+
 def solution(mesh):
     rows, cols = P(("groups", "batch"), None, "head"), P(("groups", "batch"), "head")
     placed = (
-        rows,
-        rows,
-        rows,
-        cols,
-        P("head"),
-        P("head"),
-        P("head"),
-        P(None, "head"),
-        P(None, None, "head"),
-        cols,
-        rows,
-        P(("groups", "batch"), None, None, "head"),
-        P("groups"),
-        P("groups"),
-    )
+        rows, rows, rows, cols, P("head"), P("head"), P("head"), P(None, "head"),
+        P(None, None, "head"), cols, rows, P(("groups", "batch"), None, None, "head"),
+        P("groups"), P("groups"),
+    )
+    local = local_halves if mesh.shape["batch"] == 8 else local_any
     return jax.shard_map(local, mesh=mesh, in_specs=placed, out_specs=rows, check_vma=False)

time: 116 us -> 102 us (0.88)
  waiting for transfers between devices: 40.2 us -> 15.5 us
  starting transfers between devices: 16.9 us -> 32.6 us
  other arithmetic: 5.58 us -> 0.3 us
  Pallas kernels: 42 us -> 43.2 us
    all_to_all x3 -> x0, waiting for transfers between devices: 40.2 us -> none  [the longest x1 21.8 us: local(): lax.all_to_all(sent, 'batch', split_axis=0, concat_axis=0, tiled=True)]
    ppermute x0 -> x20, starting transfers between devices: none -> 32.6 us  [swap(): return lax.ppermute(value, 'batch', perm=[(i, i ^ r) for i in range(8)])]
    all_to_all x3 -> x0, starting transfers between devices: 16.9 us -> none  [the longest x1 7.28 us: local(): lax.all_to_all(sent, 'batch', split_axis=0, concat_axis=0, tiled=True)]
    ppermute x0 -> x20, waiting for transfers between devices: none -> 15.5 us  [swap(): return lax.ppermute(value, 'batch', perm=[(i, i ^ r) for i in range(8)])]
    convert_element_type x1 -> x0, other arithmetic: 2.82 us -> none  [local(): sent = par_state.astype(jnp.bfloat16).reshape(ways, part, width, size)]
    broadcast_in_dim x1 -> x0, other arithmetic: 2.06 us -> none  [local(): tails = jnp.broadcast_to(tails[None], (ways, tails.shape[0]))]
    pallas_call x3 -> x10, Pallas kernels: 42 us -> 43.2 us  [the longest x2 12 us: convolve(): pl.pallas_call(functools.partial(drop_tokens, conv_kernel, len(operands),...]
    unnamed x38 -> x50, local copies, waits for them, and re-layouts: 8.32 us -> 7.23 us
  transfers between devices with their start and end apart: 3 -> 20, of which waited for: 2 -> 3; matrix products, arithmetic and copies ran while one was open for 5% -> 3% of each run, Pallas kernels for 28% -> 29%
where the time goes in v4:
time: 102 us
  Pallas kernels  43.2 us (42%)
  starting transfers between devices  32.6 us (32%)
  waiting for transfers between devices  15.5 us (15%)
  local copies, waits for them, and re-layouts  9.74 us (10%)
    ppermute x20, starting transfers between devices, swap(): return lax.ppermute(value, 'batch', perm=[(i, i ^ r) for i in range(8)])  32.6 us
    ppermute x20, waiting for transfers between devices, swap(): return lax.ppermute(value, 'batch', perm=[(i, i ^ r) for i in range(8)])  15.5 us
    pallas_call x2, Pallas kernels, convolve(): pl.pallas_call(functools.partial(drop_tokens, conv_kernel, len(operands),...  12 us
    pallas_call x2, Pallas kernels, mix(): pl.pallas_call(functools.partial(drop_tokens, functools.partial(mix_kerne...  11.4 us
    pallas_call x2, Pallas kernels, finish(): pl.pallas_call(functools.partial(state_kernel, offset), grid_spec=pltpu.P...  8.15 us
    pallas_call x2, Pallas kernels, pick(): pl.pallas_call(functools.partial(drop_tokens, pick_rows_kernel, 9, len(to...  7.53 us
    unnamed x50, local copies, waits for them, and re-layouts  7.23 us
    pallas_call x2, Pallas kernels, spread(): pl.pallas_call(functools.partial(drop_tokens, functools.partial(cast_kern...  3.99 us
  transfers between devices with their start and end apart: 20, of which 3 were waited for; matrix products, arithmetic and copies ran while one was open for 3% of the time, Pallas kernels for 29%

profile of v4, /device:TPU:0, one launch (start us, length us, event | category | flops | bytes accessed | tf_op | source)
XLA Modules:
  0.0 101.7 jit_solution(6237866365291826429)
XLA Ops:
  0.0 2.1 %cast_states.2 = (bf16[544,128]{1,0:T(8,128)(2,1)S(1)}, bf16[544,128]{1,0:T(8,128)(2,1)}, bf16[544,128]{1,0:T(8,128)(2,1)}, bf16[544,128]{1,0:T(8,128)(2,1)}) custom-call(s32[1]{0:T(128)} %bitcast.refs_0_.refs_11_.place_ref, f32[4,16,64,128]{3,2,1,0:T(8,128)} %bitcast.7, f32[4,16,64,128]{3,2,1,0:T(8,128)} %bitcast.8, f32[4,16,64,128]{3,2,1,0:T(8,128)} %bitcast.9, ...), custom_call_target="tpu_custom_call" | custom-call | bytes 1671168 | tf_op jit(solution)/shard_map/cast_states/pallas_call | solution.py:457
  2.1 5.0 %collective-permute-start.11 = (bf16[544,128]{1,0:T(8,128)(2,1)}, bf16[544,128]{1,0:T(8,128)(2,1)S(1)}, u32[]{:S(2)}, u32[]{:S(2)}) collective-permute-start(bf16[544,128]{1,0:T(8,128)(2,1)} %get-tuple-element.45), channel_id=1, source_target_pairs={{0,10},{2,8},{4,14},{6,12},{8,2},{10,0},{12,6},{14,4},{1,11},{3,9}... | collective-permute-start | bytes 417800 | tf_op jit(solution)/shard_map/ppermute | solution.py:438
  7.1 0.5 collective-permute-start.7
  7.6 1.3 %collective-permute-start.12 = (bf16[544,128]{1,0:T(8,128)(2,1)}, bf16[544,128]{1,0:T(8,128)(2,1)}, u32[]{:S(2)}, u32[]{:S(2)}) collective-permute-start(bf16[544,128]{1,0:T(8,128)(2,1)} %get-tuple-element.46), channel_id=1, source_target_pairs={{0,12},{2,14},{4,8},{6,10},{8,4},{10,6},{12,0},{14,2},{1,13},{3,15... | collective-permute-start | bytes 417800 | tf_op jit(solution)/shard_map/ppermute | solution.py:438
  8.9 0.2 collective-permute-start.8
  9.2 3.9 %collective-permute-start.13 = (bf16[544,128]{1,0:T(8,128)(2,1)}, bf16[544,128]{1,0:T(8,128)(2,1)}, u32[]{:S(2)}, u32[]{:S(2)}) collective-permute-start(bf16[544,128]{1,0:T(8,128)(2,1)} %get-tuple-element.47), channel_id=1, source_target_pairs={{0,14},{2,12},{4,10},{6,8},{8,6},{10,4},{12,2},{14,0},{1,15},{3,13... | collective-permute-start | bytes 417800 | tf_op jit(solution)/shard_map/ppermute | solution.py:438
  13.0 0.1 select_reduce_fusion
  13.4 0.1 copy.24.refs_4_
  13.5 0.1 copy.25.refs_5_
  13.6 1.9 %cast_states.3 = (bf16[512,128]{1,0:T(8,128)(2,1)S(1)}, bf16[512,128]{1,0:T(8,128)(2,1)S(1)}, bf16[512,128]{1,0:T(8,128)(2,1)}, bf16[512,128]{1,0:T(8,128)(2,1)}) custom-call(s32[1]{0:T(128)} %bitcast.refs_0_.refs_11_.place_ref, f32[4,16,64,128]{3,2,1,0:T(8,128)} %bitcast.11, f32[4,16,64,128]{3,2,1,0:T(8,128)} %bitcast.12, f32[4,16,64,128]{3,2,1,0:T(8,128)} %bitcast.13, ...), custom_call_target="tpu_custom_call" | custom-call | bytes 1572864 | tf_op jit(solution)/shard_map/cast_states/pallas_call | solution.py:457
  15.6 0.6 gather_fusion
  16.3 6.0 %conv.2 = (bf16[256,4096]{1,0:T(8,128)(2,1)S(1)}, bf16[256,512]{1,0:T(8,128)(2,1)S(1)}, bf16[256,512]{1,0:T(8,128)(2,1)S(1)}, f32[64,256]{1,0:T(8,128)S(1)}, f32[4,256,16]{2,1,0:T(8,128)S(1)}) custom-call(bf16[2,256,4096]{2,1,0:T(8,128)(2,1)} %refs_1_.7, bf16[2,256,512]{2,1,0:T(8,128)(2,1)} %refs_3_.7, bf16[2,256,512]{2,1,0:T(8,128)(2,1)} %refs_5_.5, ...), custom_call_target="tpu_custom_call" | custom-call | flops 41943040 | bytes 4194304 | tf_op jit(solution)/shard_map/conv/pallas_call | solution.py:509
  22.3 0.7 copy-done.4
  23.0 0.7 copy-done.6
  23.7 0.6 copy-done.16
  24.4 0.7 copy-done.8
  25.0 0.4 collective-permute-start.9
  25.4 0.7 copy-done.10
  26.1 1.0 collective-permute-start.10
  27.1 4.7 %collective-permute-done.9.refs_4_ = bf16[544,128]{1,0:T(8,128)(2,1)S(1)} collective-permute-done((bf16[544,128]{1,0:T(8,128)(2,1)}, bf16[544,128]{1,0:T(8,128)(2,1)S(1)}, u32[]{:S(2)}, u32[]{:S(2)}) %collective-permute-start.9) | collective-permute-done | bytes 139296 | tf_op jit(solution)/shard_map/ppermute | solution.py:438
  31.8 2.3 %collective-permute-done.10.refs_5_ = bf16[544,128]{1,0:T(8,128)(2,1)S(1)} collective-permute-done((bf16[544,128]{1,0:T(8,128)(2,1)S(1)}, bf16[544,128]{1,0:T(8,128)(2,1)S(1)}, u32[]{:S(2)}, u32[]{:S(2)}) %collective-permute-start.10) | collective-permute-done | bytes 139296 | tf_op jit(solution)/shard_map/ppermute | solution.py:438
  34.1 0.9 copy-done.9
  35.0 0.9 copy-done.11
  35.9 4.0 %pick_states.2 = (bf16[2,544,128]{2,1,0:T(8,128)(2,1)S(1)}, bf16[2,544,128]{2,1,0:T(8,128)(2,1)S(1)}, bf16[2,544,128]{2,1,0:T(8,128)(2,1)S(1)}, bf16[2,544,128]{2,1,0:T(8,128)(2,1)S(1)}) custom-call(s32[8]{0:T(128)S(1)} %fusion.1.refs_0_, bf16[544,128]{1,0:T(8,128)(2,1)S(1)} %get-tuple-element.35.refs_5_.refs_1_, bf16[544,128]{1,0:T(8,128)(2,1)S(1)} %copy-done.11, ...), custom_call_target="tpu_custom_call" | custom-call | bytes 4456448 | tf_op jit(solution)/shard_map/pick_states/pallas_call | solution.py:482
  39.9 1.6 %collective-permute-start.14 = (bf16[2,544,128]{2,1,0:T(8,128)(2,1)S(1)}, bf16[2,544,128]{2,1,0:T(8,128)(2,1)S(1)}, u32[]{:S(2)}, u32[]{:S(2)}) collective-permute-start(bf16[2,544,128]{2,1,0:T(8,128)(2,1)S(1)} %get-tuple-element.49), channel_id=1, source_target_pairs={{0,2},{2,0},{4,6},{6,4},{8,10},{10,8},{12,14},{14,12},{1,3},{3,1},... | collective-permute-start | bytes 835592 | tf_op jit(solution)/shard_map/ppermute | solution.py:438
  41.5 2.0 %collective-permute-start.16 = (bf16[2,544,128]{2,1,0:T(8,128)(2,1)S(1)}, bf16[2,544,128]{2,1,0:T(8,128)(2,1)S(1)}, u32[]{:S(2)}, u32[]{:S(2)}) collective-permute-start(bf16[2,544,128]{2,1,0:T(8,128)(2,1)S(1)} %get-tuple-element.51), channel_id=1, source_target_pairs={{0,6},{2,4},{4,2},{6,0},{8,14},{10,12},{12,10},{14,8},{1,7},{3,5},... | collective-permute-start | bytes 835592 | tf_op jit(solution)/shard_map/ppermute | solution.py:438
  43.5 0.6 collective-permute-start.4
  44.1 1.5 %collective-permute-start = (bf16[512,128]{1,0:T(8,128)(2,1)S(1)}, bf16[512,128]{1,0:T(8,128)(2,1)S(1)}, u32[]{:S(2)}, u32[]{:S(2)}) collective-permute-start(bf16[512,128]{1,0:T(8,128)(2,1)S(1)} %copy-done.19), channel_id=1, source_target_pairs={{0,2},{2,0},{4,6},{6,4},{8,10},{10,8},{12,14},{14,12},{1,3},{3,1},... | collective-permute-start | bytes 393224 | tf_op jit(solution)/shard_map/ppermute | solution.py:438
  45.5 8.5 %collective-permute-done.4.refs_6_ = bf16[512,128]{1,0:T(8,128)(2,1)S(1)} collective-permute-done((bf16[512,128]{1,0:T(8,128)(2,1)S(1)}, bf16[512,128]{1,0:T(8,128)(2,1)S(1)}, u32[]{:S(2)}, u32[]{:S(2)}) %collective-permute-start.4) | collective-permute-done | bytes 131104 | tf_op jit(solution)/shard_map/ppermute | solution.py:438
  54.0 0.6 copy-done.12
  54.7 4.3 %collective-permute-start.5 = (bf16[512,128]{1,0:T(8,128)(2,1)}, bf16[512,128]{1,0:T(8,128)(2,1)}, u32[]{:S(2)}, u32[]{:S(2)}) collective-permute-start(bf16[512,128]{1,0:T(8,128)(2,1)} %get-tuple-element.38), channel_id=1, source_target_pairs={{0,12},{2,14},{4,8},{6,10},{8,4},{10,6},{12,0},{14,2},{1,13},{3,15... | collective-permute-start | bytes 393224 | tf_op jit(solution)/shard_map/ppermute | solution.py:438
  59.0 0.6 copy-done.14
  59.6 1.5 %collective-permute-start.1 = (bf16[512,128]{1,0:T(8,128)(2,1)}, bf16[512,128]{1,0:T(8,128)(2,1)}, u32[]{:S(2)}, u32[]{:S(2)}) collective-permute-start(bf16[512,128]{1,0:T(8,128)(2,1)} %get-tuple-element.38), channel_id=1, source_target_pairs={{0,4},{2,6},{4,0},{6,2},{8,12},{10,14},{12,8},{14,10},{1,5},{3,7},... | collective-permute-start | bytes 393224 | tf_op jit(solution)/shard_map/ppermute | solution.py:438
  61.1 3.3 %collective-permute-start.6 = (bf16[512,128]{1,0:T(8,128)(2,1)}, bf16[512,128]{1,0:T(8,128)(2,1)}, u32[]{:S(2)}, u32[]{:S(2)}) collective-permute-start(bf16[512,128]{1,0:T(8,128)(2,1)} %get-tuple-element.39), channel_id=1, source_target_pairs={{0,14},{2,12},{4,10},{6,8},{8,6},{10,4},{12,2},{14,0},{1,15},{3,13... | collective-permute-start | bytes 393224 | tf_op jit(solution)/shard_map/ppermute | solution.py:438
  64.5 0.2 collective-permute-start.2
  64.7 0.7 copy-done
  65.4 1.8 %collective-permute-start.3 = (bf16[512,128]{1,0:T(8,128)(2,1)}, bf16[512,128]{1,0:T(8,128)(2,1)}, u32[]{:S(2)}, u32[]{:S(2)}) collective-permute-start(bf16[512,128]{1,0:T(8,128)(2,1)} %copy-done.2), channel_id=1, source_target_pairs={{0,8},{2,10},{4,12},{6,14},{8,0},{10,2},{12,4},{14,6},{1,9},{3,11}... | collective-permute-start | bytes 393224 | tf_op jit(solution)/shard_map/ppermute | solution.py:438
  67.2 0.7 broadcast_in_dim.40
  67.8 0.8 broadcast_in_dim_reshape.3.refs_8_
  68.7 6.0 %conv.3 = (bf16[256,4096]{1,0:T(8,128)(2,1)S(1)}, bf16[256,512]{1,0:T(8,128)(2,1)S(1)}, bf16[256,512]{1,0:T(8,128)(2,1)S(1)}, f32[64,256]{1,0:T(8,128)S(1)}, f32[4,256,16]{2,1,0:T(8,128)S(1)}) custom-call(bf16[2,256,4096]{2,1,0:T(8,128)(2,1)} %refs_1_.7, bf16[2,256,512]{2,1,0:T(8,128)(2,1)} %refs_3_.7, bf16[2,256,512]{2,1,0:T(8,128)(2,1)} %refs_5_.5, ...), custom_call_target="tpu_custom_call" | custom-call | flops 41943040 | bytes 4194304 | tf_op jit(solution)/shard_map/conv/pallas_call | solution.py:509
  74.8 5.8 %mix.2 = (f32[256,4096]{1,0:T(8,128)S(1)}, bf16[256,512]{1,0:T(8,128)(2,1)S(1)}) custom-call(bf16[256,4096]{1,0:T(8,128)(2,1)S(1)} %get-tuple-element.40.refs_9_.refs_0_, bf16[2,256,4096]{2,1,0:T(8,128)(2,1)} %refs_1_.7, bf16[256,512]{1,0:T(8,128)(2,1)S(1)} %copy-done.5, bf16[2,256,512]{2,1,0:T(8,128)(2,1)} %refs_3_.7, bf16[256,512]{1,0:T(8,128)(2,1)S(1)} %copy-done.7, ...), custom_call_target="tpu_custom_call" | custom-call | flops 1073741824 | bytes 6291456 | tf_op jit(solution)/shard_map/mix/pallas_call | solution.py:555
  80.7 3.5 %pick_states.3 = (bf16[2,512,128]{2,1,0:T(8,128)(2,1)S(1)}, bf16[2,512,128]{2,1,0:T(8,128)(2,1)S(1)}, bf16[2,512,128]{2,1,0:T(8,128)(2,1)S(1)}, bf16[2,512,128]{2,1,0:T(8,128)(2,1)S(1)}) custom-call(s32[8]{0:T(128)S(1)} %fusion.1.refs_0_, bf16[512,128]{1,0:T(8,128)(2,1)S(1)} %copy-done.3, bf16[512,128]{1,0:T(8,128)(2,1)S(1)} %copy-done.15, ...), custom_call_target="tpu_custom_call" | custom-call | bytes 4194304 | tf_op jit(solution)/shard_map/pick_states/pallas_call | solution.py:482
  84.3 1.0 %collective-permute-start.17 = (bf16[2,512,128]{2,1,0:T(8,128)(2,1)S(1)}, bf16[2,512,128]{2,1,0:T(8,128)(2,1)S(1)}, u32[]{:S(2)}, u32[]{:S(2)}) collective-permute-start(bf16[2,512,128]{2,1,0:T(8,128)(2,1)S(1)} %get-tuple-element.55), channel_id=1, source_target_pairs={{0,2},{2,0},{4,6},{6,4},{8,10},{10,8},{12,14},{14,12},{1,3},{3,1},... | collective-permute-start | bytes 786440 | tf_op jit(solution)/shard_map/ppermute | solution.py:438
  85.3 0.6 collective-permute-start.18
  85.9 2.0 %collective-permute-start.19 = (bf16[2,512,128]{2,1,0:T(8,128)(2,1)S(1)}, bf16[2,512,128]{2,1,0:T(8,128)(2,1)S(1)}, u32[]{:S(2)}, u32[]{:S(2)}) collective-permute-start(bf16[2,512,128]{2,1,0:T(8,128)(2,1)S(1)} %get-tuple-element.57), channel_id=1, source_target_pairs={{0,6},{2,4},{4,2},{6,0},{8,14},{10,12},{12,10},{14,8},{1,7},{3,5},... | collective-permute-start | bytes 786440 | tf_op jit(solution)/shard_map/ppermute | solution.py:438
  87.8 5.7 %mix.3 = (f32[256,4096]{1,0:T(8,128)S(1)}, bf16[256,512]{1,0:T(8,128)(2,1)S(1)}) custom-call(bf16[256,4096]{1,0:T(8,128)(2,1)S(1)} %get-tuple-element.52.refs_16_.refs_0_, bf16[2,256,4096]{2,1,0:T(8,128)(2,1)} %refs_1_.7, bf16[256,512]{1,0:T(8,128)(2,1)S(1)} %get-tuple-element.59.refs_2_, bf16[2,256,512]{2,1,0:T(8,128)(2,1)} %refs_3_.7, ...), custom_call_target="tpu_custom_call" | custom-call | flops 1073741824 | bytes 6291456 | tf_op jit(solution)/shard_map/mix/pallas_call | solution.py:555
  93.5 4.0 %add_states.2.refs_14_ = bf16[2,256,4096]{2,1,0:T(8,128)(2,1)} custom-call(s32[1]{0:T(128)} %bitcast.refs_0_.refs_11_.place_ref, bf16[2,544,128]{2,1,0:T(8,128)(2,1)S(1)} %get-tuple-element.48.refs_8_.refs_12_.refs_0_.refs_7_, bf16[2,544,128]{2,1,0:T(8,128)(2,1)S(1)} %collective-permute-done.14.refs_13_.refs_1_.refs_8_, ...), custom_call_target="tpu_custom_call" | custom-call | flops 268435456 | bytes 6291456 | tf_op jit(solution)/shard_map/add_states/pallas_call | solution.py:609
  97.5 4.1 %add_states.3 = bf16[2,256,4096]{2,1,0:T(8,128)(2,1)} custom-call(s32[1]{0:T(128)} %bitcast.refs_0_.refs_11_.place_ref, bf16[2,512,128]{2,1,0:T(8,128)(2,1)S(1)} %get-tuple-element.54.refs_16_.refs_0_.refs_7_, bf16[2,512,128]{2,1,0:T(8,128)(2,1)S(1)} %collective-permute-done.17.refs_1_.refs_8_, ...), custom_call_target="tpu_custom_call", output_to_operand_aliasing={{}: (15, {})} | custom-call | flops 268435456 | bytes 6291456 | tf_op jit(solution)/shard_map/add_states/pallas_call | solution.py:609
  (66 shorter events, 0.5 us)
Async XLA Ops:
  0.0 13.0 %copy-start.23 = (s32[8]{0:T(128)S(1)}, s32[8]{0:T(128)}, u32[]{:S(2)}) copy-start(s32[8]{0:T(128)} %param.26) | copy-start | bytes 100
  0.0 13.4 %copy-start.20 = (f32[64]{0:T(128)S(1)}, f32[64]{0:T(128)}, u32[]{:S(2)}) copy-start(f32[64]{0:T(128)} %param.18) | copy-start | bytes 772
  0.0 13.5 %copy-start.21 = (f32[64]{0:T(128)S(1)}, f32[64]{0:T(128)}, u32[]{:S(2)}) copy-start(f32[64]{0:T(128)} %param.19) | copy-start | bytes 772
  2.1 22.3 %collective-permute-start.11 = (bf16[544,128]{1,0:T(8,128)(2,1)}, bf16[544,128]{1,0:T(8,128)(2,1)S(1)}, u32[]{:S(2)}, u32[]{:S(2)}) collective-permute-start(bf16[544,128]{1,0:T(8,128)(2,1)} %get-tuple-element.45), channel_id=1, source_target_pairs={{0,10},{2,8},{4,14},{6,12},{8,2},{10,0},{12,6},{14,4},{1,11},{3,9}... | collective-permute-start | bytes 417800 | tf_op jit(solution)/shard_map/ppermute | solution.py:438
  7.1 18.4 %collective-permute-start.7 = (bf16[544,128]{1,0:T(8,128)(2,1)}, bf16[544,128]{1,0:T(8,128)(2,1)S(1)}, u32[]{:S(2)}, u32[]{:S(2)}) collective-permute-start(bf16[544,128]{1,0:T(8,128)(2,1)} %get-tuple-element.45), channel_id=1, source_target_pairs={{0,2},{2,0},{4,6},{6,4},{8,10},{10,8},{12,14},{14,12},{1,3},{3,1},... | collective-permute-start | bytes 417800 | tf_op jit(solution)/shard_map/ppermute | solution.py:438
  7.6 19.5 %collective-permute-start.12 = (bf16[544,128]{1,0:T(8,128)(2,1)}, bf16[544,128]{1,0:T(8,128)(2,1)}, u32[]{:S(2)}, u32[]{:S(2)}) collective-permute-start(bf16[544,128]{1,0:T(8,128)(2,1)} %get-tuple-element.46), channel_id=1, source_target_pairs={{0,12},{2,14},{4,8},{6,10},{8,4},{10,6},{12,0},{14,2},{1,13},{3,15... | collective-permute-start | bytes 417800 | tf_op jit(solution)/shard_map/ppermute | solution.py:438
  8.9 18.2 %collective-permute-start.8 = (bf16[544,128]{1,0:T(8,128)(2,1)}, bf16[544,128]{1,0:T(8,128)(2,1)}, u32[]{:S(2)}, u32[]{:S(2)}) collective-permute-start(bf16[544,128]{1,0:T(8,128)(2,1)} %get-tuple-element.46), channel_id=1, source_target_pairs={{0,4},{2,6},{4,0},{6,2},{8,12},{10,14},{12,8},{14,10},{1,5},{3,7},... | collective-permute-start | bytes 417800 | tf_op jit(solution)/shard_map/ppermute | solution.py:438
  9.2 18.0 %collective-permute-start.13 = (bf16[544,128]{1,0:T(8,128)(2,1)}, bf16[544,128]{1,0:T(8,128)(2,1)}, u32[]{:S(2)}, u32[]{:S(2)}) collective-permute-start(bf16[544,128]{1,0:T(8,128)(2,1)} %get-tuple-element.47), channel_id=1, source_target_pairs={{0,14},{2,12},{4,10},{6,8},{8,6},{10,4},{12,2},{14,0},{1,15},{3,13... | collective-permute-start | bytes 417800 | tf_op jit(solution)/shard_map/ppermute | solution.py:438
  13.6 1.9 %copy-start.24 = (s32[16]{0:T(128)S(1)}, s32[16]{0:T(128)}, u32[]{:S(2)}) copy-start(s32[16]{0:T(128)} %param.27) | copy-start | bytes 196
  15.5 0.7 copy-start.18
  15.5 18.6 %copy-start.2 = (bf16[512,128]{1,0:T(8,128)(2,1)}, bf16[512,128]{1,0:T(8,128)(2,1)S(1)}, u32[]{:S(2)}) copy-start(bf16[512,128]{1,0:T(8,128)(2,1)S(1)} %get-tuple-element.36.refs_8_.refs_1_) | copy-start | bytes 393220
  16.3 27.2 %copy-start.19 = (bf16[512,128]{1,0:T(8,128)(2,1)S(1)}, bf16[512,128]{1,0:T(8,128)(2,1)}, u32[]{:S(2)}) copy-start(bf16[512,128]{1,0:T(8,128)(2,1)} %copy-done.18) | copy-start | bytes 393220
  16.3 50.9 %copy-start.22 = (f32[64]{0:T(128)S(1)}, f32[64]{0:T(128)}, u32[]{:S(2)}) copy-start(f32[64]{0:T(128)} %param.20) | copy-start | bytes 772
  22.3 0.7 copy-start.4
  23.0 0.7 copy-start.6
  23.7 0.6 copy-start.16
  24.4 0.7 copy-start.8
  25.0 6.8 %collective-permute-start.9 = (bf16[544,128]{1,0:T(8,128)(2,1)}, bf16[544,128]{1,0:T(8,128)(2,1)S(1)}, u32[]{:S(2)}, u32[]{:S(2)}) collective-permute-start(bf16[544,128]{1,0:T(8,128)(2,1)} %get-tuple-element.47), channel_id=1, source_target_pairs={{0,6},{2,4},{4,2},{6,0},{8,14},{10,12},{12,10},{14,8},{1,7},{3,5},... | collective-permute-start | bytes 417800 | tf_op jit(solution)/shard_map/ppermute | solution.py:438
  25.4 0.7 copy-start.10
  26.1 8.0 %collective-permute-start.10 = (bf16[544,128]{1,0:T(8,128)(2,1)S(1)}, bf16[544,128]{1,0:T(8,128)(2,1)S(1)}, u32[]{:S(2)}, u32[]{:S(2)}) collective-permute-start(bf16[544,128]{1,0:T(8,128)(2,1)S(1)} %get-tuple-element.35.refs_5_.refs_1_), channel_id=1, source_target_pairs={{0,8},{2,10},{4,12},{6,14},{8,0},{10,2},{12,4},{14,6},{1,9},{3,11}... | collective-permute-start | bytes 417800 | tf_op jit(solution)/shard_map/ppermute | solution.py:438
  34.1 0.9 copy-start.9
  35.0 0.9 copy-start.11
  39.9 21.2 %collective-permute-start.14 = (bf16[2,544,128]{2,1,0:T(8,128)(2,1)S(1)}, bf16[2,544,128]{2,1,0:T(8,128)(2,1)S(1)}, u32[]{:S(2)}, u32[]{:S(2)}) collective-permute-start(bf16[2,544,128]{2,1,0:T(8,128)(2,1)S(1)} %get-tuple-element.49), channel_id=1, source_target_pairs={{0,2},{2,0},{4,6},{6,4},{8,10},{10,8},{12,14},{14,12},{1,3},{3,1},... | collective-permute-start | bytes 835592 | tf_op jit(solution)/shard_map/ppermute | solution.py:438
  41.5 23.0 %collective-permute-start.15 = (bf16[2,544,128]{2,1,0:T(8,128)(2,1)S(1)}, bf16[2,544,128]{2,1,0:T(8,128)(2,1)S(1)}, u32[]{:S(2)}, u32[]{:S(2)}) collective-permute-start(bf16[2,544,128]{2,1,0:T(8,128)(2,1)S(1)} %get-tuple-element.50), channel_id=1, source_target_pairs={{0,4},{2,6},{4,0},{6,2},{8,12},{10,14},{12,8},{14,10},{1,5},{3,7},... | collective-permute-start | bytes 835592 | tf_op jit(solution)/shard_map/ppermute | solution.py:438
  41.5 23.2 %collective-permute-start.16 = (bf16[2,544,128]{2,1,0:T(8,128)(2,1)S(1)}, bf16[2,544,128]{2,1,0:T(8,128)(2,1)S(1)}, u32[]{:S(2)}, u32[]{:S(2)}) collective-permute-start(bf16[2,544,128]{2,1,0:T(8,128)(2,1)S(1)} %get-tuple-element.51), channel_id=1, source_target_pairs={{0,6},{2,4},{4,2},{6,0},{8,14},{10,12},{12,10},{14,8},{1,7},{3,5},... | collective-permute-start | bytes 835592 | tf_op jit(solution)/shard_map/ppermute | solution.py:438
  43.5 10.5 %collective-permute-start.4 = (bf16[512,128]{1,0:T(8,128)(2,1)S(1)}, bf16[512,128]{1,0:T(8,128)(2,1)S(1)}, u32[]{:S(2)}, u32[]{:S(2)}) collective-permute-start(bf16[512,128]{1,0:T(8,128)(2,1)S(1)} %copy-done.19), channel_id=1, source_target_pairs={{0,10},{2,8},{4,14},{6,12},{8,2},{10,0},{12,6},{14,4},{1,11},{3,9}... | collective-permute-start | bytes 393224 | tf_op jit(solution)/shard_map/ppermute | solution.py:438
  44.1 14.9 %collective-permute-start = (bf16[512,128]{1,0:T(8,128)(2,1)S(1)}, bf16[512,128]{1,0:T(8,128)(2,1)S(1)}, u32[]{:S(2)}, u32[]{:S(2)}) collective-permute-start(bf16[512,128]{1,0:T(8,128)(2,1)S(1)} %copy-done.19), channel_id=1, source_target_pairs={{0,2},{2,0},{4,6},{6,4},{8,10},{10,8},{12,14},{14,12},{1,3},{3,1},... | collective-permute-start | bytes 393224 | tf_op jit(solution)/shard_map/ppermute | solution.py:438
  54.0 0.6 copy-start.12
  54.7 26.0 %collective-permute-start.5 = (bf16[512,128]{1,0:T(8,128)(2,1)}, bf16[512,128]{1,0:T(8,128)(2,1)}, u32[]{:S(2)}, u32[]{:S(2)}) collective-permute-start(bf16[512,128]{1,0:T(8,128)(2,1)} %get-tuple-element.38), channel_id=1, source_target_pairs={{0,12},{2,14},{4,8},{6,10},{8,4},{10,6},{12,0},{14,2},{1,13},{3,15... | collective-permute-start | bytes 393224 | tf_op jit(solution)/shard_map/ppermute | solution.py:438
  59.0 0.6 copy-start.14
  59.6 21.0 %collective-permute-start.1 = (bf16[512,128]{1,0:T(8,128)(2,1)}, bf16[512,128]{1,0:T(8,128)(2,1)}, u32[]{:S(2)}, u32[]{:S(2)}) collective-permute-start(bf16[512,128]{1,0:T(8,128)(2,1)} %get-tuple-element.38), channel_id=1, source_target_pairs={{0,4},{2,6},{4,0},{6,2},{8,12},{10,14},{12,8},{14,10},{1,5},{3,7},... | collective-permute-start | bytes 393224 | tf_op jit(solution)/shard_map/ppermute | solution.py:438
  61.1 19.5 %collective-permute-start.6 = (bf16[512,128]{1,0:T(8,128)(2,1)}, bf16[512,128]{1,0:T(8,128)(2,1)}, u32[]{:S(2)}, u32[]{:S(2)}) collective-permute-start(bf16[512,128]{1,0:T(8,128)(2,1)} %get-tuple-element.39), channel_id=1, source_target_pairs={{0,14},{2,12},{4,10},{6,8},{8,6},{10,4},{12,2},{14,0},{1,15},{3,13... | collective-permute-start | bytes 393224 | tf_op jit(solution)/shard_map/ppermute | solution.py:438
  64.5 16.2 %collective-permute-start.2 = (bf16[512,128]{1,0:T(8,128)(2,1)}, bf16[512,128]{1,0:T(8,128)(2,1)}, u32[]{:S(2)}, u32[]{:S(2)}) collective-permute-start(bf16[512,128]{1,0:T(8,128)(2,1)} %get-tuple-element.39), channel_id=1, source_target_pairs={{0,6},{2,4},{4,2},{6,0},{8,14},{10,12},{12,10},{14,8},{1,7},{3,5},... | collective-permute-start | bytes 393224 | tf_op jit(solution)/shard_map/ppermute | solution.py:438
  64.7 0.7 copy-start
  65.4 15.3 %collective-permute-start.3 = (bf16[512,128]{1,0:T(8,128)(2,1)}, bf16[512,128]{1,0:T(8,128)(2,1)}, u32[]{:S(2)}, u32[]{:S(2)}) collective-permute-start(bf16[512,128]{1,0:T(8,128)(2,1)} %copy-done.2), channel_id=1, source_target_pairs={{0,8},{2,10},{4,12},{6,14},{8,0},{10,2},{12,4},{14,6},{1,9},{3,11}... | collective-permute-start | bytes 393224 | tf_op jit(solution)/shard_map/ppermute | solution.py:438
  68.7 6.1 %copy-start.1 = (bf16[2,544,128]{2,1,0:T(8,128)(2,1)S(1)}, bf16[2,544,128]{2,1,0:T(8,128)(2,1)}, u32[]{:S(2)}) copy-start(bf16[2,544,128]{2,1,0:T(8,128)(2,1)} %copy-done) | copy-start | bytes 835588
  68.7 6.1 %copy-start.5 = (bf16[256,512]{1,0:T(8,128)(2,1)S(1)}, bf16[256,512]{1,0:T(8,128)(2,1)}, u32[]{:S(2)}) copy-start(bf16[256,512]{1,0:T(8,128)(2,1)} %copy-done.4) | copy-start | bytes 786436
  68.7 6.1 %copy-start.7 = (bf16[256,512]{1,0:T(8,128)(2,1)S(1)}, bf16[256,512]{1,0:T(8,128)(2,1)}, u32[]{:S(2)}) copy-start(bf16[256,512]{1,0:T(8,128)(2,1)} %copy-done.6) | copy-start | bytes 786436
  68.7 6.1 %copy-start.17 = (f32[64,256]{1,0:T(8,128)S(1)}, f32[64,256]{1,0:T(8,128)}, u32[]{:S(2)}) copy-start(f32[64,256]{1,0:T(8,128)} %copy-done.16) | copy-start | bytes 196612
  74.8 5.9 %copy-start.3 = (bf16[512,128]{1,0:T(8,128)(2,1)S(1)}, bf16[512,128]{1,0:T(8,128)(2,1)}, u32[]{:S(2)}) copy-start(bf16[512,128]{1,0:T(8,128)(2,1)} %copy-done.2) | copy-start | bytes 393220
  74.8 5.9 %copy-start.13 = (bf16[512,128]{1,0:T(8,128)(2,1)S(1)}, bf16[512,128]{1,0:T(8,128)(2,1)}, u32[]{:S(2)}) copy-start(bf16[512,128]{1,0:T(8,128)(2,1)} %copy-done.12) | copy-start | bytes 393220
  74.8 5.9 %copy-start.15 = (bf16[512,128]{1,0:T(8,128)(2,1)S(1)}, bf16[512,128]{1,0:T(8,128)(2,1)}, u32[]{:S(2)}) copy-start(bf16[512,128]{1,0:T(8,128)(2,1)} %copy-done.14) | copy-start | bytes 393220
  84.3 13.3 %collective-permute-start.17 = (bf16[2,512,128]{2,1,0:T(8,128)(2,1)S(1)}, bf16[2,512,128]{2,1,0:T(8,128)(2,1)S(1)}, u32[]{:S(2)}, u32[]{:S(2)}) collective-permute-start(bf16[2,512,128]{2,1,0:T(8,128)(2,1)S(1)} %get-tuple-element.55), channel_id=1, source_target_pairs={{0,2},{2,0},{4,6},{6,4},{8,10},{10,8},{12,14},{14,12},{1,3},{3,1},... | collective-permute-start | bytes 786440 | tf_op jit(solution)/shard_map/ppermute | solution.py:438
  85.3 12.2 %collective-permute-start.18 = (bf16[2,512,128]{2,1,0:T(8,128)(2,1)S(1)}, bf16[2,512,128]{2,1,0:T(8,128)(2,1)S(1)}, u32[]{:S(2)}, u32[]{:S(2)}) collective-permute-start(bf16[2,512,128]{2,1,0:T(8,128)(2,1)S(1)} %get-tuple-element.56), channel_id=1, source_target_pairs={{0,4},{2,6},{4,0},{6,2},{8,12},{10,14},{12,8},{14,10},{1,5},{3,7},... | collective-permute-start | bytes 786440 | tf_op jit(solution)/shard_map/ppermute | solution.py:438
  85.9 11.7 %collective-permute-start.19 = (bf16[2,512,128]{2,1,0:T(8,128)(2,1)S(1)}, bf16[2,512,128]{2,1,0:T(8,128)(2,1)S(1)}, u32[]{:S(2)}, u32[]{:S(2)}) collective-permute-start(bf16[2,512,128]{2,1,0:T(8,128)(2,1)S(1)} %get-tuple-element.57), channel_id=1, source_target_pairs={{0,6},{2,4},{4,2},{6,0},{8,14},{10,12},{12,10},{14,8},{1,7},{3,5},... | collective-permute-start | bytes 786440 | tf_op jit(solution)/shard_map/ppermute | solution.py:438

commit v5 on v4

--- a/solution.py
+++ b/solution.py
@@ -7,7 +7,7 @@
 from jax.experimental.pallas import tpu as pltpu
 from jax.sharding import PartitionSpec as P
 
-VMEM_LIMIT = 20 * 1024 * 1024
+VMEM_LIMIT = 10 * 1024 * 1024
 SPLIT = (8, 8)
 FIX = 16
 
@@ -61,15 +61,9 @@
     column_ref[0] = total.T
 
 
-def choose(refs, place):
-    j = place ^ pl.program_id(0)
-    near = jnp.where(j == 0, refs[0][0], refs[1][0])
-    return jnp.where(j <= 1, near, jnp.where(j == 2, refs[2][0], refs[3][0]))
-
-
 def mix_kernel(
     lines, x_ref, xin_ref, b_ref, bin_ref, c_ref, cin_ref, row_ref, column_ref, skip_ref,
-    taps_x_ref, taps_bc_ref, place_ref, *refs,
+    taps_x_ref, taps_bc_ref, tail_ref, *refs,
 ):
     mixed_ref, c_out_ref, padded = refs[-3:]
     length, wide = x_ref.shape
@@ -77,7 +71,7 @@
     width = wide // heads
     half = length // 2
     reach = taps_x_ref.shape[0] - 1
-    tail = choose(refs[:4], place_ref[0]).astype(jnp.float32)
+    tail = tail_ref[0, 0].astype(jnp.float32)
 
     def fixed(bulk_ref, first_ref, lanes, taps, at):
         rows = jnp.concatenate([tail[k * lines + at : k * lines + at + 1] for k in range(reach)])
@@ -122,13 +116,13 @@
         ] * x_conv.astype(jnp.float32)
 
 
-def state_kernel(offset, place_ref, *refs):
+def state_kernel(offset, *refs):
     y_ref = refs[-1]
     kids, length, wide = y_ref.shape
     low = lax.broadcasted_iota(jnp.int32, (length, 128), 1) < 64
     for kid in range(kids):
-        c_ref, column_ref, mixed_ref = refs[7 * kid + 4 : 7 * kid + 7]
-        state = choose(refs[7 * kid : 7 * kid + 4], place_ref[0])
+        state_ref, c_ref, column_ref, mixed_ref = refs[4 * kid : 4 * kid + 4]
+        state = state_ref[0, 0]
         term = lax.dot_general(
             c_ref[...], state, (((1,), (1,)), ((), ())), preferred_element_type=jnp.float32
         )
@@ -142,47 +136,46 @@
             y_ref[kid, :, lanes] = (mixed_ref[:, lanes] + carried).astype(jnp.bfloat16)
 
 
-def cast_kernel(reach, lines, at_ref, *refs):
-    outs = refs[-4:]
+def cast_kernel(parts, tailed, reach, lines, *refs):
+    count = len(tailed)
+    ins, outs = refs[:-count], refs[-count:]
+    states, tails = ins[: parts * count], ins[parts * count :]
     for j, out_ref in enumerate(outs):
-        state = refs[j][0]
-        rows = state.shape[0] * state.shape[1]
-        out_ref[:rows] = state.reshape(rows, state.shape[2]).astype(jnp.bfloat16)
-        if lines:
-            x_tail = refs[4 + j][0].astype(jnp.float32)
-            bc_tail = refs[8 + j][0].astype(jnp.float32)
-            parts = []
-            for k in range(reach):
-                parts += [x_tail[k : k + 1, i * 128 : i * 128 + 128] for i in range(lines - 2)]
-                parts.append(bc_tail[k])
-            spare = out_ref.shape[0] - rows - lines * reach
-            parts.append(jnp.zeros((spare, 128), jnp.float32))
-            out_ref[rows:] = jnp.concatenate(parts).astype(jnp.bfloat16)
-
-
-def pick_rows_kernel(slots_ref, *refs):
-    count = 8
-    held, outs = refs[:count], refs[count:-3]
-    stage, in_sems, out_sems = refs[-3:]
-    kids = outs[0].shape[0]
-    loads = [
-        pltpu.make_async_copy(ref, stage.at[i], in_sems.at[i]) for i, ref in enumerate(held)
-    ]
-    for load in loads:
-        load.start()
-    for load in loads:
-        load.wait()
-    stores = [
-        pltpu.make_async_copy(
-            stage.at[slots_ref[j * kids + kid]], out.at[kid], out_sems.at[j, kid]
-        )
-        for j, out in enumerate(outs)
-        for kid in range(kids)
-    ]
-    for store in stores:
-        store.start()
-    for store in stores:
-        store.wait()
+        start = 0
+        for at in range(parts):
+            state = states[parts * j + at][0]
+            rows = state.shape[0] * state.shape[1]
+            out_ref[start : start + rows] = state.reshape(rows, state.shape[2]).astype(jnp.bfloat16)
+            start += rows
+            if at == 0 and tailed[j]:
+                x_tail = tails[2 * j][0].astype(jnp.float32)
+                bc_tail = tails[2 * j + 1][0].astype(jnp.float32)
+                pieces = []
+                for k in range(reach):
+                    pieces += [x_tail[k : k + 1, i * 128 : i * 128 + 128] for i in range(lines - 2)]
+                    pieces.append(bc_tail[k])
+                spare = tailed[j] - lines * reach
+                pieces.append(jnp.zeros((spare, 128), jnp.float32))
+                out_ref[start : start + tailed[j]] = jnp.concatenate(pieces).astype(jnp.bfloat16)
+                start += tailed[j]
+
+
+def pick_rows_kernel(start, slots_ref, inside_ref, *refs):
+    crossed, out, sems = refs[:-2], refs[-2], refs[-1]
+    spots, rows = out.shape[:2]
+    for i in range(spots):
+        for source in range(4 + len(crossed)):
+            if source < 4:
+                held = inside_ref.at[source, pl.ds(start, rows)]
+            else:
+                held = crossed[source - 4]
+
+            @pl.when(slots_ref[i] == source)
+            def _(held=held, i=i):
+                pltpu.make_async_copy(held, out.at[i], sems.at[i]).start()
+
+    for i in range(spots):
+        pltpu.make_async_copy(crossed[0], out.at[i], sems.at[i]).wait()
 
 
 def within_kernel(
@@ -359,7 +352,7 @@
             jax.ShapeDtypeStruct((kids, length, groups * size), jnp.bfloat16),
             jax.ShapeDtypeStruct((kids, groups, length, per_group), jnp.float32),
         ],
-        compiler_params=pltpu.CompilerParams(vmem_limit_bytes=VMEM_LIMIT),
+        compiler_params=pltpu.CompilerParams(vmem_limit_bytes=4 * VMEM_LIMIT),
         cost_estimate=pl.CostEstimate(
             flops=4 * kids * heads * length * length * width,
             bytes_accessed=6 * kids * length * columns,
@@ -393,7 +386,7 @@
         ],
         out_specs=pl.BlockSpec((1, length, wide), lambda c, q: (c, 0, q)),
         out_shape=jax.ShapeDtypeStruct((kids, length, columns), jnp.bfloat16),
-        compiler_params=pltpu.CompilerParams(vmem_limit_bytes=VMEM_LIMIT),
+        compiler_params=pltpu.CompilerParams(vmem_limit_bytes=4 * VMEM_LIMIT),
         cost_estimate=pl.CostEstimate(
             flops=2 * kids * length * columns * size,
             bytes_accessed=8 * kids * length * columns,
@@ -425,9 +418,9 @@
 
     me = lax.axis_index("batch")
     parent = parent_of(counts, order)
-    near = me ^ jnp.arange(4, dtype=jnp.int32)
-    children = (near[:, None] * kids + jnp.arange(kids, dtype=jnp.int32)[None, :]).reshape(-1)
-    slots = jnp.take(parent, children) ^ me
+    side = me // 4 * 4
+    owner = lax.dynamic_slice_in_dim(parent, side * kids, 4 * kids)
+    slots = jnp.where(owner // 4 * 4 == side, owner % 4, 4 + ((owner ^ me) % 4))
     place = (me % 4).astype(jnp.int32)[None]
 
     state = stay(par_state.reshape(groups, per_group, width, size))
@@ -437,69 +430,104 @@
     def swap(value, r):
         return lax.ppermute(value, "batch", perm=[(i, i ^ r) for i in range(8)])
 
-    def spread(k, tokens):
-        part = SPLIT[k]
-        rows = part * width + (tail_lines if k == 0 else 0)
-        operands = [state] * 4
-        specs = [
-            pl.BlockSpec((1, part, width, size), lambda i, p, j=j: (p[0] ^ j, offsets[k] // part, 0, 0))
-            for j in range(4)
-        ]
-        if k == 0:
-            operands += [x_tails] * 4 + [bc_tails] * 4
-            specs += [
-                pl.BlockSpec((1, reach, wide), lambda i, p, j=j: (0, 0, p[0] ^ j)) for j in range(4)
-            ]
-            specs += [
-                pl.BlockSpec((1, reach, 2, size), lambda i, p, j=j: (0, 0, 0, p[0] ^ j))
-                for j in range(4)
-            ]
-        sent = pl.pallas_call(
+    def cast(quarters, chunks, tokens):
+        tailed = [tail_lines if chunks[0] == 0 else 0] * len(quarters)
+        rows = sum(SPLIT[k] for k in chunks) * width + tailed[0]
+        operands, specs = [], []
+        for j in quarters:
+            for k in chunks:
+                part, at = SPLIT[k], offsets[k] // SPLIT[k]
+                operands.append(state)
+                specs.append(
+                    pl.BlockSpec(
+                        (1, part, width, size), lambda i, p, j=j, at=at: (p[0] ^ j, at, 0, 0)
+                    )
+                )
+        if tailed[0]:
+            for j in quarters:
+                operands += [x_tails, bc_tails]
+                specs += [
+                    pl.BlockSpec((1, reach, wide), lambda i, p, j=j: (0, 0, p[0] ^ j)),
+                    pl.BlockSpec((1, reach, 2, size), lambda i, p, j=j: (0, 0, 0, p[0] ^ j)),
+                ]
+        kernel = functools.partial(cast_kernel, len(chunks), tailed, reach, lines)
+        return pl.pallas_call(
             functools.partial(
-                drop_tokens,
-                functools.partial(cast_kernel, reach, lines if k == 0 else 0),
-                1 + len(operands),
-                len(tokens),
+                drop_tokens, lambda place_ref, *refs: kernel(*refs), 1 + len(operands), len(tokens)
             ),
             grid_spec=pltpu.PrefetchScalarGridSpec(
                 num_scalar_prefetch=1,
                 grid=(1,),
                 in_specs=specs + [anywhere] * len(tokens),
-                out_specs=[pl.BlockSpec((rows, size), lambda i, p: (0, 0))] * 4,
-            ),
-            out_shape=[jax.ShapeDtypeStruct((rows, size), jnp.bfloat16)] * 4,
+                out_specs=[pl.BlockSpec((rows, size), lambda i, p: (0, 0))] * len(quarters),
+            ),
+            out_shape=[jax.ShapeDtypeStruct((rows, size), jnp.bfloat16)] * len(quarters),
             compiler_params=params,
             cost_estimate=pl.CostEstimate(
-                flops=0, bytes_accessed=24 * rows * size, transcendentals=0
+                flops=0, bytes_accessed=6 * len(quarters) * rows * size, transcendentals=0
             ),
             name="cast_states",
         )(place, *operands, *tokens)
-        far = [swap(sent[j], j + 4) for j in range(4)]
-        return [sent[0]] + [swap(sent[j], j) for j in range(1, 4)] + far
-
-    def pick(k, held, tokens):
-        rows = held[0].shape[0]
+
+    def cast_whole(tokens):
+        rows = per_group * width + tail_lines
+        operands = [state, state, x_tails, bc_tails]
+        kernel = functools.partial(cast_kernel, 2, [tail_lines], reach, lines)
+        return pl.pallas_call(
+            functools.partial(
+                drop_tokens,
+                lambda a, b, c, d, out_ref: kernel(a, b, c, d, out_ref.at[0]),
+                4,
+                len(tokens),
+            ),
+            grid=(groups,),
+            in_specs=[
+                pl.BlockSpec((1, SPLIT[0], width, size), lambda q: (q, 0, 0, 0)),
+                pl.BlockSpec((1, SPLIT[1], width, size), lambda q: (q, 1, 0, 0)),
+                pl.BlockSpec((1, reach, wide), lambda q: (0, 0, q)),
+                pl.BlockSpec((1, reach, 2, size), lambda q: (0, 0, 0, q)),
+                *[anywhere] * len(tokens),
+            ],
+            out_specs=pl.BlockSpec((1, rows, size), lambda q: (q, 0, 0)),
+            out_shape=jax.ShapeDtypeStruct((groups, rows, size), jnp.bfloat16),
+            compiler_params=params,
+            cost_estimate=pl.CostEstimate(
+                flops=0, bytes_accessed=6 * groups * rows * size, transcendentals=0
+            ),
+            name="cast_states",
+        )(*operands, *tokens)
+
+    def gather_half(value):
+        return lax.all_to_all(
+            value,
+            "batch",
+            split_axis=0,
+            concat_axis=0,
+            tiled=True,
+            axis_index_groups=[[0, 1, 2, 3], [4, 5, 6, 7]],
+        )
+
+    def pick(rows, start, inside, crossed, tokens):
+        spots = 4 * kids
         picked = pl.pallas_call(
-            functools.partial(drop_tokens, pick_rows_kernel, 9, len(tokens)),
+            functools.partial(
+                drop_tokens, functools.partial(pick_rows_kernel, start), 6, len(tokens)
+            ),
             grid_spec=pltpu.PrefetchScalarGridSpec(
                 num_scalar_prefetch=1,
                 grid=(1,),
-                in_specs=[anywhere] * (8 + len(tokens)),
-                out_specs=[anywhere] * 4,
-                scratch_shapes=[
-                    pltpu.VMEM((8, rows, size), jnp.bfloat16),
-                    pltpu.SemaphoreType.DMA((8,)),
-                    pltpu.SemaphoreType.DMA((4, kids)),
-                ],
-            ),
-            out_shape=[jax.ShapeDtypeStruct((kids, rows, size), jnp.bfloat16)] * 4,
+                in_specs=[anywhere] * (5 + len(tokens)),
+                out_specs=pl.BlockSpec((spots, rows, size), lambda i, s: (0, 0, 0)),
+                scratch_shapes=[pltpu.SemaphoreType.DMA((spots,))],
+            ),
+            out_shape=jax.ShapeDtypeStruct((spots, rows, size), jnp.bfloat16),
             compiler_params=params,
             cost_estimate=pl.CostEstimate(
-                flops=0, bytes_accessed=32 * kids * rows * size, transcendentals=0
+                flops=0, bytes_accessed=4 * spots * rows * size, transcendentals=0
             ),
             name="pick_states",
-        )(slots, *held, *tokens)
-        return [picked[0]] + [swap(picked[j], j) for j in range(1, 4)]
+        )(slots, inside, *crossed, *tokens)
+        return picked, gather_half(picked).reshape(4, kids, rows, size)
 
     def convolve(c, tokens):
         at = lambda q: (c, 0, q)
@@ -528,11 +556,11 @@
                 pl.BlockSpec((1, length, per_group), lambda q: (q, 0, 0)),
             ],
             out_shape=[
-                jax.ShapeDtypeStruct(x_in.shape[1:], jnp.bfloat16),
-                jax.ShapeDtypeStruct(b_in.shape[1:], jnp.bfloat16),
-                jax.ShapeDtypeStruct(c_in.shape[1:], jnp.bfloat16),
-                jax.ShapeDtypeStruct(dt_in.shape[1:], jnp.float32),
-                jax.ShapeDtypeStruct((groups, length, per_group), jnp.float32),
+                pltpu.HBM(x_in.shape[1:], jnp.bfloat16),
+                pltpu.HBM(b_in.shape[1:], jnp.bfloat16),
+                pltpu.HBM(c_in.shape[1:], jnp.bfloat16),
+                pltpu.HBM(dt_in.shape[1:], jnp.float32),
+                pltpu.HBM((groups, length, per_group), jnp.float32),
             ],
             scratch_shapes=[pltpu.VMEM((8 + length, size), jnp.float32)],
             compiler_params=params,
@@ -545,15 +573,15 @@
         )(*operands, *tokens)
 
     def mix(c, early, states, tokens):
-        x_conv, b_conv, c_conv, row, column = early
+        x_conv, b_conv, c_conv, row, column = map(stay, early)
         at = lambda q: (0, q)
         tail_at = SPLIT[0] * width // tail_lines
         operands = [
             x_conv, x_in, b_conv, b_in, c_conv, c_in, row, column, skip_row, conv_x, conv_bc,
-            place, *states,
+            states,
         ]
         return pl.pallas_call(
-            functools.partial(drop_tokens, functools.partial(mix_kernel, lines), 16, len(tokens)),
+            functools.partial(drop_tokens, functools.partial(mix_kernel, lines), 12, len(tokens)),
             grid=(groups,),
             in_specs=[
                 pl.BlockSpec((length, wide), at),
@@ -567,14 +595,13 @@
                 pl.BlockSpec((1, wide), at),
                 pl.BlockSpec((taps, wide), at),
                 pl.BlockSpec((2, taps, size), lambda q: (0, 0, q)),
-                pl.BlockSpec(memory_space=pltpu.SMEM),
-                *[pl.BlockSpec((1, tail_lines, size), lambda q: (c, tail_at, 0))] * 4,
+                pl.BlockSpec((1, 1, tail_lines, size), lambda q: (q, c, tail_at, 0)),
                 *[anywhere] * len(tokens),
             ],
             out_specs=[pl.BlockSpec((length, wide), at), pl.BlockSpec((length, size), at)],
             out_shape=[
-                jax.ShapeDtypeStruct((length, columns), jnp.float32),
-                jax.ShapeDtypeStruct((length, groups * size), jnp.bfloat16),
+                pltpu.HBM((length, columns), jnp.float32),
+                pltpu.HBM((length, groups * size), jnp.bfloat16),
             ],
             scratch_shapes=[
                 pltpu.VMEM((8 + FIX, size), jnp.float32),
@@ -591,29 +618,26 @@
     def finish(k, states, early, mixed, result):
         part, offset = SPLIT[k], offsets[k]
         chunk = part * width
-        at = lambda q, p: (0, q * (per_group // part) + offset // part)
+        at = lambda q: (0, q * (per_group // part) + offset // part)
         operands, specs = [], []
         for c in range(kids):
-            operands += [*states, mixed[c][1], early[c][4], mixed[c][0]]
+            operands += [states, *map(stay, (mixed[c][1], early[c][4], mixed[c][0]))]
             specs += [
-                *[pl.BlockSpec((1, chunk, size), lambda q, p, c=c: (c, 0, 0))] * 4,
-                pl.BlockSpec((length, size), lambda q, p: (0, q)),
-                pl.BlockSpec((1, length, per_group), lambda q, p: (q, 0, 0)),
+                pl.BlockSpec((1, 1, chunk, size), lambda q, c=c: (q, c, 0, 0)),
+                pl.BlockSpec((length, size), lambda q: (0, q)),
+                pl.BlockSpec((1, length, per_group), lambda q: (q, 0, 0)),
                 pl.BlockSpec((length, chunk), at),
             ]
         alias = {}
         if result is not None:
-            alias = {1 + len(operands): 0}
+            alias = {len(operands): 0}
             operands.append(result)
             specs.append(anywhere)
         return pl.pallas_call(
             functools.partial(state_kernel, offset),
-            grid_spec=pltpu.PrefetchScalarGridSpec(
-                num_scalar_prefetch=1,
-                grid=(groups,),
-                in_specs=specs,
-                out_specs=pl.BlockSpec((kids, length, chunk), lambda q, p: (0, *at(q, p))),
-            ),
+            grid=(groups,),
+            in_specs=specs,
+            out_specs=pl.BlockSpec((kids, length, chunk), lambda q: (0, *at(q))),
             out_shape=jax.ShapeDtypeStruct(x_in.shape, jnp.bfloat16),
             input_output_aliases=alias,
             compiler_params=params,
@@ -623,22 +647,25 @@
                 transcendentals=kids * groups * length * chunk,
             ),
             name="add_states",
-        )(place, *operands)
+        )(*operands)
 
     skip_row = jnp.repeat(d_skip, width)[None, :]
-    held, early = [], []
-    for k in range(len(SPLIT)):
-        held.append(spread(k, [held[-1][0]] if k else []))
-    early.append(convolve(0, [held[1][0]]))
-    states = [pick(0, held[0], [early[0][0]])]
-    early.append(convolve(1, [states[0][0]]))
-    mixed = [mix(0, early[0], states[0], [early[1][0]])]
-    states.append(pick(1, held[1], [mixed[0][1]]))
-    mixed.append(mix(1, early[1], states[0], [states[1][0]]))
-    result = None
-    for k in range(len(SPLIT)):
-        result = finish(k, states[k], early, mixed, result)
-    return result
+    rows = [SPLIT[0] * width + tail_lines, SPLIT[1] * width]
+    quarters = [0, 1, 2, 3]
+    sent_a = cast(quarters, [0], [])
+    crossed_a = [swap(sent_a[j], j + 4) for j in quarters]
+    whole = cast_whole([sent_a[0]])
+    inside = gather_half(whole)
+    early = [convolve(0, [whole])]
+    early.append(convolve(1, [stay(early[0][3])]))
+    sent_b = cast(quarters, [1], [*crossed_a, stay(early[1][3])])
+    crossed_b = [swap(sent_b[j], j + 4) for j in quarters]
+    picked_a, states_a = pick(rows[0], 0, inside, crossed_a, [sent_b[0]])
+    picked_b, states_b = pick(rows[1], rows[0], inside, crossed_b, [picked_a])
+    mixed = [mix(0, early[0], states_a, [picked_b])]
+    mixed.append(mix(1, early[1], states_a, [stay(mixed[0][1])]))
+    result = finish(0, states_a, early, mixed, None)
+    return finish(1, states_b, early, mixed, result)
 
 
 def solution(mesh):

time: 102 us -> 108 us (1.059)
  waiting for transfers between devices: 15.5 us -> 26.5 us
  local copies, waits for them, and re-layouts: 9.74 us -> 0.37 us
  Pallas kernels: 43.2 us -> 52.4 us
  starting transfers between devices: 32.6 us -> 27 us
    ppermute x20 -> x8, starting transfers between devices: 32.6 us -> 14.6 us  [swap(): return lax.ppermute(value, 'batch', perm=[(i, i ^ r) for i in range(8)])]
    all_to_all x0 -> x3, starting transfers between devices: none -> 12.5 us  [gather_half(): lax.all_to_all(value, 'batch', split_axis=0, concat_axis=0, tiled=True, a...]
    ppermute x20 -> x8, waiting for transfers between devices: 15.5 us -> 26.4 us  [swap(): return lax.ppermute(value, 'batch', perm=[(i, i ^ r) for i in range(8)])]
    unnamed x50 -> x10, local copies, waits for them, and re-layouts: 7.23 us -> 0.02 us
    pallas_call x6 -> x7, Pallas kernels: 19.7 us -> 25 us  [the longest x2 11.8 us: finish(): pl.pallas_call(functools.partial(state_kernel, offset), grid=(groups,), i...]
    pallas_call x2, Pallas kernels: 11.4 us -> 14.2 us  [mix(): pl.pallas_call(functools.partial(drop_tokens, functools.partial(mix_kerne...]
    pallas_call x2, Pallas kernels: 12 us -> 13.2 us  [convolve(): pl.pallas_call(functools.partial(drop_tokens, conv_kernel, len(operands),...]
  transfers between devices with their start and end apart: 20 -> 11, of which waited for: 3 -> 6; matrix products, arithmetic and copies ran while one was open for 3% -> 1% of each run, Pallas kernels for 29% -> 36%
where the time goes in v5:
time: 108 us; the launch traced here: 107 us
  Pallas kernels  52.4 us (49%)
  starting transfers between devices  27 us (25%)
  waiting for transfers between devices  26.5 us (25%)
    ppermute x8, waiting for transfers between devices, swap(): return lax.ppermute(value, 'batch', perm=[(i, i ^ r) for i in range(8)])  26.4 us
    ppermute x8, starting transfers between devices, swap(): return lax.ppermute(value, 'batch', perm=[(i, i ^ r) for i in range(8)])  14.6 us
    pallas_call x2, Pallas kernels, mix(): pl.pallas_call(functools.partial(drop_tokens, functools.partial(mix_kerne...  14.2 us
    pallas_call x2, Pallas kernels, convolve(): pl.pallas_call(functools.partial(drop_tokens, conv_kernel, len(operands),...  13.2 us
    all_to_all x3, starting transfers between devices, gather_half(): lax.all_to_all(value, 'batch', split_axis=0, concat_axis=0, tiled=True, a...  12.5 us
    pallas_call x2, Pallas kernels, finish(): pl.pallas_call(functools.partial(state_kernel, offset), grid=(groups,), i...  11.8 us
    pallas_call x2, Pallas kernels, pick(): pl.pallas_call(functools.partial(drop_tokens, functools.partial(pick_rows...  7.04 us
    pallas_call x1, Pallas kernels, cast_whole(): pl.pallas_call(functools.partial(drop_tokens, lambda a, b, c, d, out_ref:...  3.59 us
  transfers between devices with their start and end apart: 11, of which 6 were waited for; matrix products, arithmetic and copies ran while one was open for 1% of the time, Pallas kernels for 36%

profile of v5, /device:TPU:0, one launch (start us, length us, event | category | flops | bytes accessed | tf_op | source)
XLA Modules:
  0.0 106.6 jit_solution(17291581871798262320)
XLA Ops:
  0.0 1.3 %cast_states.3 = (bf16[544,128]{1,0:T(8,128)(2,1)S(1)}, bf16[544,128]{1,0:T(8,128)(2,1)S(1)}, bf16[544,128]{1,0:T(8,128)(2,1)S(1)}, bf16[544,128]{1,0:T(8,128)(2,1)S(1)}) custom-call(s32[1]{0:T(128)} %bitcast.2.refs_0_, f32[4,16,64,128]{3,2,1,0:T(8,128)} %bitcast.13, f32[4,16,64,128]{3,2,1,0:T(8,128)} %bitcast.14, f32[4,16,64,128]{3,2,1,0:T(8,128)} %bitcast.15, ...), custom_call_target="tpu_custom_call" | custom-call | bytes 1671168 | tf_op jit(solution)/shard_map/cast_states/pallas_call | solution.py:454
  1.3 3.6 %cast_states.4.refs_8_ = bf16[4,1056,128]{2,1,0:T(8,128)(2,1)} custom-call(f32[4,16,64,128]{3,2,1,0:T(8,128)} %bitcast.17, f32[4,16,64,128]{3,2,1,0:T(8,128)} %bitcast.18, bf16[1,3,4096]{2,1,0:T(4,128)(2,1)} %refs_2_.3, bf16[1,3,2,512]{3,2,1,0:T(2,128)(2,1)} %bitcast.27, bf16[544,128]{1,0:T(8,128)(2,1)S(1)} %get-tuple-element.27.refs_4_), custom_call_target="tpu_custom_call" | custom-call | bytes 3244032 | tf_op jit(solution)/shard_map/cast_states/pallas_call | solution.py:476
  4.9 0.0 copy-start.3
  4.9 0.0 copy-start.4
  4.9 0.0 copy-start.1
  4.9 5.4 %all-to-all-start = ((bf16[4,1056,128]{2,1,0:T(8,128)(2,1)}), bf16[4,1056,128]{2,1,0:T(8,128)(2,1)S(1)}, u32[]{:S(2)}, u32[]{:S(2)}) async-start(bf16[4,1056,128]{2,1,0:T(8,128)(2,1)} %cast_states.4.refs_8_), calls=%async_computation | async-start | bytes 2162688 | tf_op jit(solution)/shard_map/all_to_all | solution.py:501
  10.3 2.6 %collective-permute-start = (bf16[544,128]{1,0:T(8,128)(2,1)S(1)}, bf16[544,128]{1,0:T(8,128)(2,1)S(1)}, u32[]{:S(2)}, u32[]{:S(2)}) collective-permute-start(bf16[544,128]{1,0:T(8,128)(2,1)S(1)} %get-tuple-element.27.refs_4_), channel_id=1, source_target_pairs={{0,8},{2,10},{4,12},{6,14},{8,0},{10,2},{12,4},{14,6},{1,9},{3,11}... | collective-permute-start | bytes 417800 | tf_op jit(solution)/shard_map/ppermute | solution.py:431
  12.9 1.8 %collective-permute-start.1 = (bf16[544,128]{1,0:T(8,128)(2,1)S(1)}, bf16[544,128]{1,0:T(8,128)(2,1)S(1)}, u32[]{:S(2)}, u32[]{:S(2)}) collective-permute-start(bf16[544,128]{1,0:T(8,128)(2,1)S(1)} %get-tuple-element.28), channel_id=1, source_target_pairs={{0,10},{2,8},{4,14},{6,12},{8,2},{10,0},{12,6},{14,4},{1,11},{3,9}... | collective-permute-start | bytes 417800 | tf_op jit(solution)/shard_map/ppermute | solution.py:431
  14.7 3.5 %collective-permute-start.2 = (bf16[544,128]{1,0:T(8,128)(2,1)S(1)}, bf16[544,128]{1,0:T(8,128)(2,1)S(1)}, u32[]{:S(2)}, u32[]{:S(2)}) collective-permute-start(bf16[544,128]{1,0:T(8,128)(2,1)S(1)} %get-tuple-element.29), channel_id=1, source_target_pairs={{0,12},{2,14},{4,8},{6,10},{8,4},{10,6},{12,0},{14,2},{1,13},{3,15... | collective-permute-start | bytes 417800 | tf_op jit(solution)/shard_map/ppermute | solution.py:431
  18.2 0.0 collective-permute-start.3
  18.2 0.0 copy-done.3
  18.2 0.1 select_reduce_fusion
  18.3 0.0 copy-done.4
  18.3 0.1 convert_reduce_fusion
  18.4 0.0 copy-done
  18.4 0.1 copy.22.refs_4_
  18.5 0.0 copy-done.1
  18.5 0.1 copy.23.refs_5_
  18.6 6.6 %conv.2 = (bf16[256,4096]{1,0:T(8,128)(2,1)}, bf16[256,512]{1,0:T(8,128)(2,1)}, bf16[256,512]{1,0:T(8,128)(2,1)}, f32[64,256]{1,0:T(8,128)}, f32[4,256,16]{2,1,0:T(8,128)}) custom-call(bf16[2,256,4096]{2,1,0:T(8,128)(2,1)} %refs_1_.7, bf16[2,256,512]{2,1,0:T(8,128)(2,1)} %refs_3_.7, bf16[2,256,512]{2,1,0:T(8,128)(2,1)} %refs_5_.5, f32[2,64,256]{2,1,0:T(8,128)} %refs_3_.5, ...), custom_call_target="tpu_custom_call" | custom-call | flops 41943040 | bytes 4194304 | tf_op jit(solution)/shard_map/conv/pallas_call | solution.py:537
  25.2 6.6 %conv.3 = (bf16[256,4096]{1,0:T(8,128)(2,1)}, bf16[256,512]{1,0:T(8,128)(2,1)}, bf16[256,512]{1,0:T(8,128)(2,1)}, f32[64,256]{1,0:T(8,128)}, f32[4,256,16]{2,1,0:T(8,128)}) custom-call(bf16[2,256,4096]{2,1,0:T(8,128)(2,1)} %refs_1_.7, bf16[2,256,512]{2,1,0:T(8,128)(2,1)} %refs_3_.7, bf16[2,256,512]{2,1,0:T(8,128)(2,1)} %refs_5_.5, f32[2,64,256]{2,1,0:T(8,128)} %refs_3_.5, ...), custom_call_target="tpu_custom_call" | custom-call | flops 41943040 | bytes 4194304 | tf_op jit(solution)/shard_map/conv/pallas_call | solution.py:537
  31.8 0.1 compare_select_fusion.2.refs_0_
  31.9 0.0 collective-permute-done.1.refs_6_.refs_3_
  31.9 4.8 %collective-permute-done.2.refs_7_.refs_4_ = bf16[544,128]{1,0:T(8,128)(2,1)S(1)} collective-permute-done((bf16[544,128]{1,0:T(8,128)(2,1)S(1)}, bf16[544,128]{1,0:T(8,128)(2,1)S(1)}, u32[]{:S(2)}, u32[]{:S(2)}) %collective-permute-start.2) | collective-permute-done | bytes 139296 | tf_op jit(solution)/shard_map/ppermute | solution.py:431
  36.7 2.5 %collective-permute-done.3.refs_8_.refs_5_ = bf16[544,128]{1,0:T(8,128)(2,1)S(1)} collective-permute-done((bf16[544,128]{1,0:T(8,128)(2,1)S(1)}, bf16[544,128]{1,0:T(8,128)(2,1)S(1)}, u32[]{:S(2)}, u32[]{:S(2)}) %collective-permute-start.3) | collective-permute-done | bytes 139296 | tf_op jit(solution)/shard_map/ppermute | solution.py:431
  39.2 0.0 collective-permute-done.refs_5_.refs_2_
  39.2 1.2 %cast_states.5 = (bf16[512,128]{1,0:T(8,128)(2,1)S(1)}, bf16[512,128]{1,0:T(8,128)(2,1)S(1)}, bf16[512,128]{1,0:T(8,128)(2,1)S(1)}, bf16[512,128]{1,0:T(8,128)(2,1)S(1)}) custom-call(s32[1]{0:T(128)} %bitcast.2.refs_0_, f32[4,16,64,128]{3,2,1,0:T(8,128)} %bitcast.19, f32[4,16,64,128]{3,2,1,0:T(8,128)} %bitcast.20, f32[4,16,64,128]{3,2,1,0:T(8,128)} %bitcast.21, ...), custom_call_target="tpu_custom_call" | custom-call | bytes 1572864 | tf_op jit(solution)/shard_map/cast_states/pallas_call | solution.py:454
  40.4 0.0 all-to-all-done.refs_1_
  40.4 3.6 %pick_states.2.refs_6_ = bf16[8,544,128]{2,1,0:T(8,128)(2,1)} custom-call(s32[8]{0:T(128)S(1)} %compare_select_fusion.2.refs_0_, bf16[4,1056,128]{2,1,0:T(8,128)(2,1)S(1)} %all-to-all-done.refs_1_, bf16[544,128]{1,0:T(8,128)(2,1)S(1)} %collective-permute-done.refs_5_.refs_2_, bf16[544,128]{1,0:T(8,128)(2,1)S(1)} %collective-permute-done.1.refs_6_.refs_3_, ...), custom_call_target="tpu_custom_call" | custom-call | bytes 2228224 | tf_op jit(solution)/shard_map/pick_states/pallas_call | solution.py:512
  44.0 3.5 %all-to-all-start.2 = ((bf16[8,544,128]{2,1,0:T(8,128)(2,1)}), bf16[8,544,128]{2,1,0:T(8,128)(2,1)S(1)}, u32[]{:S(2)}, u32[]{:S(2)}) async-start(bf16[8,544,128]{2,1,0:T(8,128)(2,1)} %pick_states.2.refs_6_), calls=%async_computation.2 | async-start | bytes 2228224 | tf_op jit(solution)/shard_map/all_to_all | solution.py:501
  47.6 3.3 %collective-permute-start.5 = (bf16[512,128]{1,0:T(8,128)(2,1)S(1)}, bf16[512,128]{1,0:T(8,128)(2,1)S(1)}, u32[]{:S(2)}, u32[]{:S(2)}) collective-permute-start(bf16[512,128]{1,0:T(8,128)(2,1)S(1)} %get-tuple-element.34), channel_id=1, source_target_pairs={{0,10},{2,8},{4,14},{6,12},{8,2},{10,0},{12,6},{14,4},{1,11},{3,9}... | collective-permute-start | bytes 393224 | tf_op jit(solution)/shard_map/ppermute | solution.py:431
  50.9 1.9 %collective-permute-start.6 = (bf16[512,128]{1,0:T(8,128)(2,1)S(1)}, bf16[512,128]{1,0:T(8,128)(2,1)S(1)}, u32[]{:S(2)}, u32[]{:S(2)}) collective-permute-start(bf16[512,128]{1,0:T(8,128)(2,1)S(1)} %get-tuple-element.35), channel_id=1, source_target_pairs={{0,12},{2,14},{4,8},{6,10},{8,4},{10,6},{12,0},{14,2},{1,13},{3,15... | collective-permute-start | bytes 393224 | tf_op jit(solution)/shard_map/ppermute | solution.py:431
  52.8 1.4 %collective-permute-start.7 = (bf16[512,128]{1,0:T(8,128)(2,1)S(1)}, bf16[512,128]{1,0:T(8,128)(2,1)S(1)}, u32[]{:S(2)}, u32[]{:S(2)}) collective-permute-start(bf16[512,128]{1,0:T(8,128)(2,1)S(1)} %get-tuple-element.36), channel_id=1, source_target_pairs={{0,14},{2,12},{4,10},{6,8},{8,6},{10,4},{12,2},{14,0},{1,15},{3,13... | collective-permute-start | bytes 393224 | tf_op jit(solution)/shard_map/ppermute | solution.py:431
  54.3 0.0 collective-permute-start.4
  54.3 9.4 %collective-permute-done.5.refs_3_ = bf16[512,128]{1,0:T(8,128)(2,1)S(1)} collective-permute-done((bf16[512,128]{1,0:T(8,128)(2,1)S(1)}, bf16[512,128]{1,0:T(8,128)(2,1)S(1)}, u32[]{:S(2)}, u32[]{:S(2)}) %collective-permute-start.5) | collective-permute-done | bytes 131104 | tf_op jit(solution)/shard_map/ppermute | solution.py:431
  63.7 6.5 %collective-permute-done.6.refs_4_ = bf16[512,128]{1,0:T(8,128)(2,1)S(1)} collective-permute-done((bf16[512,128]{1,0:T(8,128)(2,1)S(1)}, bf16[512,128]{1,0:T(8,128)(2,1)S(1)}, u32[]{:S(2)}, u32[]{:S(2)}) %collective-permute-start.6) | collective-permute-done | bytes 131104 | tf_op jit(solution)/shard_map/ppermute | solution.py:431
  70.2 2.3 %collective-permute-done.7.refs_5_ = bf16[512,128]{1,0:T(8,128)(2,1)S(1)} collective-permute-done((bf16[512,128]{1,0:T(8,128)(2,1)S(1)}, bf16[512,128]{1,0:T(8,128)(2,1)S(1)}, u32[]{:S(2)}, u32[]{:S(2)}) %collective-permute-start.7) | collective-permute-done | bytes 131104 | tf_op jit(solution)/shard_map/ppermute | solution.py:431
  72.5 0.9 collective-permute-done.4.refs_2_
  73.4 3.5 %pick_states.3.refs_12_ = bf16[8,512,128]{2,1,0:T(8,128)(2,1)} custom-call(s32[8]{0:T(128)S(1)} %compare_select_fusion.2.refs_0_, bf16[4,1056,128]{2,1,0:T(8,128)(2,1)S(1)} %all-to-all-done.refs_1_, bf16[512,128]{1,0:T(8,128)(2,1)S(1)} %collective-permute-done.4.refs_2_, bf16[512,128]{1,0:T(8,128)(2,1)S(1)} %collective-permute-done.5.refs_3_, ...), custom_call_target="tpu_custom_call" | custom-call | bytes 2097152 | tf_op jit(solution)/shard_map/pick_states/pallas_call | solution.py:512
  76.9 0.0 all-to-all-done.2
  76.9 3.5 %all-to-all-start.1 = ((bf16[8,512,128]{2,1,0:T(8,128)(2,1)}), bf16[8,512,128]{2,1,0:T(8,128)(2,1)S(1)}, u32[]{:S(2)}, u32[]{:S(2)}) async-start(bf16[8,512,128]{2,1,0:T(8,128)(2,1)} %pick_states.3.refs_12_), calls=%async_computation.1 | async-start | bytes 2097152 | tf_op jit(solution)/shard_map/all_to_all | solution.py:501
  80.5 0.0 copy-done.2
  80.5 0.1 broadcast_in_dim.36
  80.5 0.1 broadcast_in_dim_reshape.3.refs_8_
  80.6 7.1 %mix.2 = (f32[256,4096]{1,0:T(8,128)}, bf16[256,512]{1,0:T(8,128)(2,1)}) custom-call(bf16[256,4096]{1,0:T(8,128)(2,1)} %get-tuple-element.37.refs_0_, bf16[2,256,4096]{2,1,0:T(8,128)(2,1)} %refs_1_.7, bf16[256,512]{1,0:T(8,128)(2,1)} %get-tuple-element.38.refs_2_, bf16[2,256,512]{2,1,0:T(8,128)(2,1)} %refs_3_.7, bf16[256,512]{1,0:T(8,128)(2,1)} %get-tuple-element.39.refs_4_, ...), custom_call_target="tpu_custom_call" | custom-call | flops 1073741824 | bytes 6291456 | tf_op jit(solution)/shard_map/mix/pallas_call | solution.py:583
  87.7 7.1 %mix.3 = (f32[256,4096]{1,0:T(8,128)}, bf16[256,512]{1,0:T(8,128)(2,1)}) custom-call(bf16[256,4096]{1,0:T(8,128)(2,1)} %get-tuple-element.43.refs_0_, bf16[2,256,4096]{2,1,0:T(8,128)(2,1)} %refs_1_.7, bf16[256,512]{1,0:T(8,128)(2,1)} %get-tuple-element.44.refs_2_, bf16[2,256,512]{2,1,0:T(8,128)(2,1)} %refs_3_.7, bf16[256,512]{1,0:T(8,128)(2,1)} %get-tuple-element.45.refs_4_, ...), custom_call_target="tpu_custom_call" | custom-call | flops 1073741824 | bytes 6291456 | tf_op jit(solution)/shard_map/mix/pallas_call | solution.py:583
  94.8 5.9 %add_states.2.refs_8_ = bf16[2,256,4096]{2,1,0:T(8,128)(2,1)} custom-call(bf16[4,2,544,128]{3,2,1,0:T(8,128)(2,1)S(1)} %bitcast.9, bf16[256,512]{1,0:T(8,128)(2,1)} %get-tuple-element.41.refs_12_.refs_1_, f32[4,256,16]{2,1,0:T(8,128)} %get-tuple-element.40.refs_7_.refs_2_, f32[256,4096]{1,0:T(8,128)} %get-tuple-element.42.refs_3_, ...), custom_call_target="tpu_custom_call" | custom-call | flops 268435456 | bytes 6291456 | tf_op jit(solution)/shard_map/add_states/pallas_call | solution.py:636
  100.7 0.0 all-to-all-done.1
  100.7 5.9 %add_states.3 = bf16[2,256,4096]{2,1,0:T(8,128)(2,1)} custom-call(bf16[4,2,512,128]{3,2,1,0:T(8,128)(2,1)S(1)} %bitcast.11, bf16[256,512]{1,0:T(8,128)(2,1)} %get-tuple-element.41.refs_12_.refs_1_, f32[4,256,16]{2,1,0:T(8,128)} %get-tuple-element.40.refs_7_.refs_2_, f32[256,4096]{1,0:T(8,128)} %get-tuple-element.42.refs_3_, ...), custom_call_target="tpu_custom_call", output_to_operand_aliasing={{}: (8, {})} | custom-call | flops 268435456 | bytes 6291456 | tf_op jit(solution)/shard_map/add_states/pallas_call | solution.py:636
  (2 shorter events, 0.0 us)
Async XLA Ops:
  4.9 13.3 %copy-start.3 = (s32[8]{0:T(128)S(1)}, s32[8]{0:T(128)}, u32[]{:S(2)}) copy-start(s32[8]{0:T(128)} %param.26) | copy-start | bytes 100
  4.9 13.4 %copy-start.4 = (s32[16]{0:T(128)S(1)}, s32[16]{0:T(128)}, u32[]{:S(2)}) copy-start(s32[16]{0:T(128)} %param.27) | copy-start | bytes 196
  4.9 13.5 %copy-start = (f32[64]{0:T(128)S(1)}, f32[64]{0:T(128)}, u32[]{:S(2)}) copy-start(f32[64]{0:T(128)} %param.18) | copy-start | bytes 772
  4.9 13.6 %copy-start.1 = (f32[64]{0:T(128)S(1)}, f32[64]{0:T(128)}, u32[]{:S(2)}) copy-start(f32[64]{0:T(128)} %param.19) | copy-start | bytes 772
  4.9 35.5 %all-to-all-start = ((bf16[4,1056,128]{2,1,0:T(8,128)(2,1)}), bf16[4,1056,128]{2,1,0:T(8,128)(2,1)S(1)}, u32[]{:S(2)}, u32[]{:S(2)}) async-start(bf16[4,1056,128]{2,1,0:T(8,128)(2,1)} %cast_states.4.refs_8_), calls=%async_computation | async-start | bytes 2162688 | tf_op jit(solution)/shard_map/all_to_all | solution.py:501
  10.3 28.9 %collective-permute-start = (bf16[544,128]{1,0:T(8,128)(2,1)S(1)}, bf16[544,128]{1,0:T(8,128)(2,1)S(1)}, u32[]{:S(2)}, u32[]{:S(2)}) collective-permute-start(bf16[544,128]{1,0:T(8,128)(2,1)S(1)} %get-tuple-element.27.refs_4_), channel_id=1, source_target_pairs={{0,8},{2,10},{4,12},{6,14},{8,0},{10,2},{12,4},{14,6},{1,9},{3,11}... | collective-permute-start | bytes 417800 | tf_op jit(solution)/shard_map/ppermute | solution.py:431
  12.9 19.0 %collective-permute-start.1 = (bf16[544,128]{1,0:T(8,128)(2,1)S(1)}, bf16[544,128]{1,0:T(8,128)(2,1)S(1)}, u32[]{:S(2)}, u32[]{:S(2)}) collective-permute-start(bf16[544,128]{1,0:T(8,128)(2,1)S(1)} %get-tuple-element.28), channel_id=1, source_target_pairs={{0,10},{2,8},{4,14},{6,12},{8,2},{10,0},{12,6},{14,4},{1,11},{3,9}... | collective-permute-start | bytes 417800 | tf_op jit(solution)/shard_map/ppermute | solution.py:431
  14.7 22.0 %collective-permute-start.2 = (bf16[544,128]{1,0:T(8,128)(2,1)S(1)}, bf16[544,128]{1,0:T(8,128)(2,1)S(1)}, u32[]{:S(2)}, u32[]{:S(2)}) collective-permute-start(bf16[544,128]{1,0:T(8,128)(2,1)S(1)} %get-tuple-element.29), channel_id=1, source_target_pairs={{0,12},{2,14},{4,8},{6,10},{8,4},{10,6},{12,0},{14,2},{1,13},{3,15... | collective-permute-start | bytes 417800 | tf_op jit(solution)/shard_map/ppermute | solution.py:431
  18.2 21.0 %collective-permute-start.3 = (bf16[544,128]{1,0:T(8,128)(2,1)S(1)}, bf16[544,128]{1,0:T(8,128)(2,1)S(1)}, u32[]{:S(2)}, u32[]{:S(2)}) collective-permute-start(bf16[544,128]{1,0:T(8,128)(2,1)S(1)} %get-tuple-element.30), channel_id=1, source_target_pairs={{0,14},{2,12},{4,10},{6,8},{8,6},{10,4},{12,2},{14,0},{1,15},{3,13... | collective-permute-start | bytes 417800 | tf_op jit(solution)/shard_map/ppermute | solution.py:431
  44.0 32.9 %all-to-all-start.2 = ((bf16[8,544,128]{2,1,0:T(8,128)(2,1)}), bf16[8,544,128]{2,1,0:T(8,128)(2,1)S(1)}, u32[]{:S(2)}, u32[]{:S(2)}) async-start(bf16[8,544,128]{2,1,0:T(8,128)(2,1)} %pick_states.2.refs_6_), calls=%async_computation.2 | async-start | bytes 2228224 | tf_op jit(solution)/shard_map/all_to_all | solution.py:501
  47.6 16.1 %collective-permute-start.5 = (bf16[512,128]{1,0:T(8,128)(2,1)S(1)}, bf16[512,128]{1,0:T(8,128)(2,1)S(1)}, u32[]{:S(2)}, u32[]{:S(2)}) collective-permute-start(bf16[512,128]{1,0:T(8,128)(2,1)S(1)} %get-tuple-element.34), channel_id=1, source_target_pairs={{0,10},{2,8},{4,14},{6,12},{8,2},{10,0},{12,6},{14,4},{1,11},{3,9}... | collective-permute-start | bytes 393224 | tf_op jit(solution)/shard_map/ppermute | solution.py:431
  50.9 19.3 %collective-permute-start.6 = (bf16[512,128]{1,0:T(8,128)(2,1)S(1)}, bf16[512,128]{1,0:T(8,128)(2,1)S(1)}, u32[]{:S(2)}, u32[]{:S(2)}) collective-permute-start(bf16[512,128]{1,0:T(8,128)(2,1)S(1)} %get-tuple-element.35), channel_id=1, source_target_pairs={{0,12},{2,14},{4,8},{6,10},{8,4},{10,6},{12,0},{14,2},{1,13},{3,15... | collective-permute-start | bytes 393224 | tf_op jit(solution)/shard_map/ppermute | solution.py:431
  52.8 27.6 %copy-start.2 = (f32[64]{0:T(128)S(1)}, f32[64]{0:T(128)}, u32[]{:S(2)}) copy-start(f32[64]{0:T(128)} %param.20) | copy-start | bytes 772
  52.8 19.7 %collective-permute-start.7 = (bf16[512,128]{1,0:T(8,128)(2,1)S(1)}, bf16[512,128]{1,0:T(8,128)(2,1)S(1)}, u32[]{:S(2)}, u32[]{:S(2)}) collective-permute-start(bf16[512,128]{1,0:T(8,128)(2,1)S(1)} %get-tuple-element.36), channel_id=1, source_target_pairs={{0,14},{2,12},{4,10},{6,8},{8,6},{10,4},{12,2},{14,0},{1,15},{3,13... | collective-permute-start | bytes 393224 | tf_op jit(solution)/shard_map/ppermute | solution.py:431
  54.3 19.2 %collective-permute-start.4 = (bf16[512,128]{1,0:T(8,128)(2,1)S(1)}, bf16[512,128]{1,0:T(8,128)(2,1)S(1)}, u32[]{:S(2)}, u32[]{:S(2)}) collective-permute-start(bf16[512,128]{1,0:T(8,128)(2,1)S(1)} %get-tuple-element.33.refs_6_), channel_id=1, source_target_pairs={{0,8},{2,10},{4,12},{6,14},{8,0},{10,2},{12,4},{14,6},{1,9},{3,11}... | collective-permute-start | bytes 393224 | tf_op jit(solution)/shard_map/ppermute | solution.py:431
  76.9 23.8 %all-to-all-start.1 = ((bf16[8,512,128]{2,1,0:T(8,128)(2,1)}), bf16[8,512,128]{2,1,0:T(8,128)(2,1)S(1)}, u32[]{:S(2)}, u32[]{:S(2)}) async-start(bf16[8,512,128]{2,1,0:T(8,128)(2,1)} %pick_states.3.refs_12_), calls=%async_computation.1 | async-start | bytes 2097152 | tf_op jit(solution)/shard_map/all_to_all | solution.py:501

commit v6 on v5

--- a/solution.py
+++ b/solution.py
@@ -34,71 +34,58 @@
     return (half + half * jnp.tanh(half)).astype(jnp.bfloat16)
 
 
-def conv_kernel(
-    x_ref, b_ref, c_ref, dt_ref, bias_ref, alog_ref, taps_x_ref, taps_bc_ref,
-    xc_ref, bc_ref, cc_ref, row_ref, column_ref, padded,
+def early_kernel(
+    x_ref, b_ref, c_ref, dt_ref, bias_ref, alog_ref, skip_ref, taps_x_ref, taps_bc_ref,
+    mixed_ref, c_out_ref, column_ref, first_ref, padded,
 ):
-    length = x_ref.shape[1]
-    lanes_all = x_ref.shape[2]
-    bc_ref[...] = conv_silu(padded, 0.0, b_ref[0], taps_bc_ref[0])
-    cc_ref[...] = conv_silu(padded, 0.0, c_ref[0], taps_bc_ref[1])
-    for start in range(0, lanes_all, 128):
-        lanes = slice(start, start + 128)
-        xc_ref[:, lanes] = conv_silu(padded, 0.0, x_ref[0, :, lanes], taps_x_ref[:, lanes])
+    length, wide = mixed_ref.shape
+    heads = dt_ref.shape[1]
+    width = wide // heads
+    half = length // 2
+
+    def convolve(rows, taps):
+        bulk = conv_silu(padded, 0.0, rows, taps)[FIX:]
+        return jnp.concatenate([jnp.zeros((FIX, rows.shape[1]), jnp.bfloat16), bulk])
+
+    b_conv = convolve(b_ref[0], taps_bc_ref[0])
+    c_conv = convolve(c_ref[0], taps_bc_ref[1])
+    c_out_ref[...] = c_conv
+    scores = lax.dot_general(
+        c_conv, b_conv, (((1,), (1,)), ((), ())), preferred_element_type=jnp.float32
+    )
     raw = dt_ref[0] + bias_ref[...]
     step = jnp.maximum(raw, 0.0) + jnp.log1p(jnp.exp(-jnp.abs(raw)))
     per_token = step * (-jnp.exp(alog_ref[...]))
-    row = lax.broadcasted_iota(jnp.int32, (length, length), 0)
-    col = lax.broadcasted_iota(jnp.int32, (length, length), 1)
+    upper = lax.broadcasted_iota(jnp.int32, (length, length), 0) <= lax.broadcasted_iota(
+        jnp.int32, (length, length), 1
+    )
     total = lax.dot_general(
         per_token,
-        (row <= col).astype(jnp.float32),
+        upper.astype(jnp.float32),
         (((1,), (0,)), ((), ())),
         precision=lax.Precision.HIGHEST,
         preferred_element_type=jnp.float32,
     )
-    row_ref[...] = total - jnp.log(step)
-    column_ref[0] = total.T
-
-
-def mix_kernel(
-    lines, x_ref, xin_ref, b_ref, bin_ref, c_ref, cin_ref, row_ref, column_ref, skip_ref,
-    taps_x_ref, taps_bc_ref, tail_ref, *refs,
-):
-    mixed_ref, c_out_ref, padded = refs[-3:]
-    length, wide = x_ref.shape
-    heads = row_ref.shape[0]
-    width = wide // heads
-    half = length // 2
-    reach = taps_x_ref.shape[0] - 1
-    tail = tail_ref[0, 0].astype(jnp.float32)
-
-    def fixed(bulk_ref, first_ref, lanes, taps, at):
-        rows = jnp.concatenate([tail[k * lines + at : k * lines + at + 1] for k in range(reach)])
-        first = conv_silu(padded, rows, first_ref[0, :, lanes], taps)
-        return jnp.concatenate([first, bulk_ref[FIX:, lanes]])
-
-    every = slice(0, b_ref.shape[1])
-    b_conv = fixed(b_ref, bin_ref, every, taps_bc_ref[0], lines - 2)
-    c_conv = fixed(c_ref, cin_ref, every, taps_bc_ref[1], lines - 1)
-    c_out_ref[...] = c_conv
-    scores = lax.dot_general(
-        c_conv, b_conv, (((1,), (1,)), ((), ())), preferred_element_type=jnp.float32
-    )
+    row = total - jnp.log(step)
+    columns = total.T
+    column_ref[0] = columns
     causal = lax.broadcasted_iota(jnp.int32, (half, half), 0) >= lax.broadcasted_iota(
         jnp.int32, (half, half), 1
     )
     low = lax.broadcasted_iota(jnp.int32, (length, 2 * width), 1) < width
     for pair in range(heads // 2):
         lanes = slice(pair * 2 * width, (pair + 1) * 2 * width)
-        x_conv = fixed(x_ref, xin_ref, lanes, taps_x_ref[:, lanes], pair)
+        x_conv = convolve(x_ref[0, :, lanes], taps_x_ref[:, lanes])
         parts = []
         for head in (2 * pair, 2 * pair + 1):
-            column = jnp.broadcast_to(column_ref[0, :, head : head + 1], (length, half))
-            rows = row_ref[head : head + 1, :]
+            column = jnp.broadcast_to(columns[:, head : head + 1], (length, half))
+            rows = row[head : head + 1, :]
             near = jnp.exp(jnp.where(causal, column[:half] - rows[:, :half], -1e30))
             far = jnp.exp(column[half:] - rows[:, :half])
             last = jnp.exp(jnp.where(causal, column[half:] - rows[:, half:], -1e30))
+            spot = slice(head * FIX, (head + 1) * FIX)
+            first_ref[0, :half, spot] = near[:, :FIX]
+            first_ref[0, half:, spot] = far[:, :FIX]
             top = (scores[:half, :half] * near).astype(jnp.bfloat16)
             left = (scores[half:, :half] * far).astype(jnp.bfloat16)
             right = (scores[half:, half:] * last).astype(jnp.bfloat16)
@@ -116,24 +103,59 @@
         ] * x_conv.astype(jnp.float32)
 
 
-def state_kernel(offset, *refs):
-    y_ref = refs[-1]
+def late_kernel(offset, lines, x_ref, b_ref, c_ref, skip_ref, taps_x_ref, taps_bc_ref, *refs):
+    y_ref, padded = refs[-2:]
     kids, length, wide = y_ref.shape
-    low = lax.broadcasted_iota(jnp.int32, (length, 128), 1) < 64
+    width = 64
+    heads = wide // width
+    reach = taps_x_ref.shape[0] - 1
+    low = lax.broadcasted_iota(jnp.int32, (length, 2 * width), 1) < width
+    low_first = lax.broadcasted_iota(jnp.int32, (FIX, 2 * width), 1) < width
+    contract = (((1,), (1,)), ((), ()))
     for kid in range(kids):
-        state_ref, c_ref, column_ref, mixed_ref = refs[4 * kid : 4 * kid + 4]
-        state = state_ref[0, 0]
+        state_ref, tail_ref, held_ref, column_ref, first_ref, mixed_ref = refs[6 * kid : 6 * kid + 6]
+        tail = tail_ref[0, 0].astype(jnp.float32)
+
+        def opening(rows, taps, at):
+            tap_rows = [tail[k * lines + at : k * lines + at + 1] for k in range(reach)]
+            return conv_silu(padded, jnp.concatenate(tap_rows), rows, taps)
+
+        b_first = opening(b_ref[kid], taps_bc_ref[0], lines - 2)
+        c_first = opening(c_ref[kid], taps_bc_ref[1], lines - 1)
+        c_conv = jnp.concatenate([c_first, held_ref[FIX:]])
         term = lax.dot_general(
-            c_ref[...], state, (((1,), (1,)), ((), ())), preferred_element_type=jnp.float32
+            c_conv, state_ref[0, 0], contract, preferred_element_type=jnp.float32
         )
-        for pair in range(wide // 128):
-            lanes = slice(pair * 128, pair * 128 + 128)
+        scores = lax.dot_general(
+            c_conv,
+            jnp.concatenate([b_first] * heads),
+            contract,
+            preferred_element_type=jnp.float32,
+        )
+        mixing = (scores * first_ref[0]).astype(jnp.bfloat16)
+        for pair in range(heads // 2):
+            lanes = slice(pair * 2 * width, (pair + 1) * 2 * width)
+            x_first = opening(
+                x_ref[kid, :, lanes], taps_x_ref[:, lanes], offset * width // 128 + pair
+            ).astype(jnp.float32)
+            stacked = [jnp.where(low_first, x_first, 0.0), jnp.where(low_first, 0.0, x_first)]
+            if pair > 0:
+                stacked = [jnp.zeros((2 * pair * FIX, 2 * width), jnp.float32)] + stacked
+            if 2 * pair + 2 < heads:
+                spare = (heads - 2 * pair - 2) * FIX
+                stacked = stacked + [jnp.zeros((spare, 2 * width), jnp.float32)]
+            part = jnp.dot(
+                mixing,
+                jnp.concatenate(stacked).astype(jnp.bfloat16),
+                preferred_element_type=jnp.float32,
+            )
+            part = jnp.concatenate([part[:FIX] + skip_ref[:, lanes] * x_first, part[FIX:]])
             head = offset + 2 * pair
             grow = jnp.where(
                 low, column_ref[0, :, head : head + 1], column_ref[0, :, head + 1 : head + 2]
             )
             carried = (term[:, lanes] * jnp.exp(grow)).astype(jnp.bfloat16).astype(jnp.float32)
-            y_ref[kid, :, lanes] = (mixed_ref[:, lanes] + carried).astype(jnp.bfloat16)
+            y_ref[kid, :, lanes] = (mixed_ref[:, lanes] + part + carried).astype(jnp.bfloat16)
 
 
 def cast_kernel(parts, tailed, reach, lines, *refs):
@@ -163,19 +185,23 @@
 def pick_rows_kernel(start, slots_ref, inside_ref, *refs):
     crossed, out, sems = refs[:-2], refs[-2], refs[-1]
     spots, rows = out.shape[:2]
+    held = [inside_ref.at[source, pl.ds(start, rows)] for source in range(4)]
+    held += list(crossed) if len(crossed) == 4 else [crossed[0].at[source] for source in range(4)]
     for i in range(spots):
-        for source in range(4 + len(crossed)):
-            if source < 4:
-                held = inside_ref.at[source, pl.ds(start, rows)]
-            else:
-                held = crossed[source - 4]
+        for source in range(8):
 
             @pl.when(slots_ref[i] == source)
-            def _(held=held, i=i):
-                pltpu.make_async_copy(held, out.at[i], sems.at[i]).start()
+            def _(source=source, i=i):
+                pltpu.make_async_copy(held[source], out.at[i], sems.at[i]).start()
 
     for i in range(spots):
-        pltpu.make_async_copy(crossed[0], out.at[i], sems.at[i]).wait()
+        pltpu.make_async_copy(held[0], out.at[i], sems.at[i]).wait()
+
+
+def slice_kernel(start, in_ref, out_ref, sem):
+    copy = pltpu.make_async_copy(in_ref.at[:, pl.ds(start, out_ref.shape[1])], out_ref, sem)
+    copy.start()
+    copy.wait()
 
 
 def within_kernel(
@@ -420,7 +446,9 @@
     parent = parent_of(counts, order)
     side = me // 4 * 4
     owner = lax.dynamic_slice_in_dim(parent, side * kids, 4 * kids)
-    slots = jnp.where(owner // 4 * 4 == side, owner % 4, 4 + ((owner ^ me) % 4))
+    here = owner // 4 * 4 == side
+    slots_a = jnp.where(here, owner % 4, 4 + (owner ^ me) % 4)
+    slots_b = jnp.where(here, owner % 4, 4 + owner % 4)
     place = (me % 4).astype(jnp.int32)[None]
 
     state = stay(par_state.reshape(groups, per_group, width, size))
@@ -471,24 +499,26 @@
 
     def cast_whole(tokens):
         rows = per_group * width + tail_lines
-        operands = [state, state, x_tails, bc_tails]
-        kernel = functools.partial(cast_kernel, 2, [tail_lines], reach, lines)
+
+        def kernel(*refs):
+            out_ref = refs[-1]
+            for q in range(groups):
+                cast_kernel(2, [tail_lines], reach, lines, *refs[4 * q : 4 * q + 4], out_ref.at[q])
+
+        operands, specs = [], []
+        for q in range(groups):
+            operands += [state, state, x_tails, bc_tails]
+            specs += [
+                pl.BlockSpec((1, SPLIT[0], width, size), lambda i, q=q: (q, 0, 0, 0)),
+                pl.BlockSpec((1, SPLIT[1], width, size), lambda i, q=q: (q, 1, 0, 0)),
+                pl.BlockSpec((1, reach, wide), lambda i, q=q: (0, 0, q)),
+                pl.BlockSpec((1, reach, 2, size), lambda i, q=q: (0, 0, 0, q)),
+            ]
         return pl.pallas_call(
-            functools.partial(
-                drop_tokens,
-                lambda a, b, c, d, out_ref: kernel(a, b, c, d, out_ref.at[0]),
-                4,
-                len(tokens),
-            ),
-            grid=(groups,),
-            in_specs=[
-                pl.BlockSpec((1, SPLIT[0], width, size), lambda q: (q, 0, 0, 0)),
-                pl.BlockSpec((1, SPLIT[1], width, size), lambda q: (q, 1, 0, 0)),
-                pl.BlockSpec((1, reach, wide), lambda q: (0, 0, q)),
-                pl.BlockSpec((1, reach, 2, size), lambda q: (0, 0, 0, q)),
-                *[anywhere] * len(tokens),
-            ],
-            out_specs=pl.BlockSpec((1, rows, size), lambda q: (q, 0, 0)),
+            functools.partial(drop_tokens, kernel, len(operands), len(tokens)),
+            grid=(1,),
+            in_specs=specs + [anywhere] * len(tokens),
+            out_specs=pl.BlockSpec((groups, rows, size), lambda i: (0, 0, 0)),
             out_shape=jax.ShapeDtypeStruct((groups, rows, size), jnp.bfloat16),
             compiler_params=params,
             cost_estimate=pl.CostEstimate(
@@ -496,6 +526,25 @@
             ),
             name="cast_states",
         )(*operands, *tokens)
+
+    def chunk_b(inside, tokens):
+        rows = SPLIT[1] * width
+        return pl.pallas_call(
+            functools.partial(
+                drop_tokens, functools.partial(slice_kernel, inside.shape[1] - rows), 1, len(tokens)
+            ),
+            grid=(1,),
+            in_specs=[anywhere]
+            + [anywhere] * len(tokens),
+            out_specs=pl.BlockSpec((4, rows, size), lambda i: (0, 0, 0)),
+            out_shape=jax.ShapeDtypeStruct((4, rows, size), jnp.bfloat16),
+            scratch_shapes=[pltpu.SemaphoreType.DMA],
+            compiler_params=params,
+            cost_estimate=pl.CostEstimate(
+                flops=0, bytes_accessed=16 * rows * size, transcendentals=0
+            ),
+            name="chunk_b",
+        )(inside, *tokens)
 
     def gather_half(value):
         return lax.all_to_all(
@@ -507,16 +556,16 @@
             axis_index_groups=[[0, 1, 2, 3], [4, 5, 6, 7]],
         )
 
-    def pick(rows, start, inside, crossed, tokens):
+    def pick(rows, start, slots, inside, crossed, tokens):
         spots = 4 * kids
         picked = pl.pallas_call(
             functools.partial(
-                drop_tokens, functools.partial(pick_rows_kernel, start), 6, len(tokens)
+                drop_tokens, functools.partial(pick_rows_kernel, start), 2 + len(crossed), len(tokens)
             ),
             grid_spec=pltpu.PrefetchScalarGridSpec(
                 num_scalar_prefetch=1,
                 grid=(1,),
-                in_specs=[anywhere] * (5 + len(tokens)),
+                in_specs=[anywhere] * (1 + len(crossed) + len(tokens)),
                 out_specs=pl.BlockSpec((spots, rows, size), lambda i, s: (0, 0, 0)),
                 scratch_shapes=[pltpu.SemaphoreType.DMA((spots,))],
             ),
@@ -529,13 +578,13 @@
         )(slots, inside, *crossed, *tokens)
         return picked, gather_half(picked).reshape(4, kids, rows, size)
 
-    def convolve(c, tokens):
+    def early(c, tokens):
         at = lambda q: (c, 0, q)
         operands = [
-            x_in, b_in, c_in, dt_in, dt_bias[:, None], a_log[:, None], conv_x, conv_bc
+            x_in, b_in, c_in, dt_in, dt_bias[:, None], a_log[:, None], skip_row, conv_x, conv_bc
         ]
         return pl.pallas_call(
-            functools.partial(drop_tokens, conv_kernel, len(operands), len(tokens)),
+            functools.partial(drop_tokens, early_kernel, len(operands), len(tokens)),
             grid=(groups,),
             in_specs=[
                 pl.BlockSpec((1, length, wide), at),
@@ -544,6 +593,7 @@
                 pl.BlockSpec((1, per_group, length), lambda q: (c, q, 0)),
                 pl.BlockSpec((per_group, 1), lambda q: (q, 0)),
                 pl.BlockSpec((per_group, 1), lambda q: (q, 0)),
+                pl.BlockSpec((1, wide), lambda q: (0, q)),
                 pl.BlockSpec((taps, wide), lambda q: (0, q)),
                 pl.BlockSpec((2, taps, size), lambda q: (0, 0, q)),
                 *[anywhere] * len(tokens),
@@ -551,102 +601,80 @@
             out_specs=[
                 pl.BlockSpec((length, wide), lambda q: (0, q)),
                 pl.BlockSpec((length, size), lambda q: (0, q)),
-                pl.BlockSpec((length, size), lambda q: (0, q)),
-                pl.BlockSpec((per_group, length), lambda q: (q, 0)),
                 pl.BlockSpec((1, length, per_group), lambda q: (q, 0, 0)),
+                pl.BlockSpec((1, length, per_group * FIX), lambda q: (q, 0, 0)),
             ],
             out_shape=[
-                pltpu.HBM(x_in.shape[1:], jnp.bfloat16),
-                pltpu.HBM(b_in.shape[1:], jnp.bfloat16),
-                pltpu.HBM(c_in.shape[1:], jnp.bfloat16),
-                pltpu.HBM(dt_in.shape[1:], jnp.float32),
-                pltpu.HBM((groups, length, per_group), jnp.float32),
+                jax.ShapeDtypeStruct((length, columns), jnp.float32),
+                jax.ShapeDtypeStruct((length, groups * size), jnp.bfloat16),
+                jax.ShapeDtypeStruct((groups, length, per_group), jnp.float32),
+                jax.ShapeDtypeStruct((groups, length, per_group * FIX), jnp.float32),
             ],
             scratch_shapes=[pltpu.VMEM((8 + length, size), jnp.float32)],
             compiler_params=params,
             cost_estimate=pl.CostEstimate(
-                flops=40 * length * columns,
-                bytes_accessed=4 * length * columns,
-                transcendentals=2 * length * columns,
-            ),
-            name="conv",
+                flops=4 * heads * length * length * width,
+                bytes_accessed=8 * length * columns,
+                transcendentals=heads * length * length,
+            ),
+            name="early",
         )(*operands, *tokens)
 
-    def mix(c, early, states, tokens):
-        x_conv, b_conv, c_conv, row, column = map(stay, early)
-        at = lambda q: (0, q)
-        tail_at = SPLIT[0] * width // tail_lines
-        operands = [
-            x_conv, x_in, b_conv, b_in, c_conv, c_in, row, column, skip_row, conv_x, conv_bc,
-            states,
-        ]
-        return pl.pallas_call(
-            functools.partial(drop_tokens, functools.partial(mix_kernel, lines), 12, len(tokens)),
-            grid=(groups,),
-            in_specs=[
-                pl.BlockSpec((length, wide), at),
-                pl.BlockSpec((1, FIX, wide), lambda q: (c, 0, q)),
-                pl.BlockSpec((length, size), at),
-                pl.BlockSpec((1, FIX, size), lambda q: (c, 0, q)),
-                pl.BlockSpec((length, size), at),
-                pl.BlockSpec((1, FIX, size), lambda q: (c, 0, q)),
-                pl.BlockSpec((per_group, length), lambda q: (q, 0)),
-                pl.BlockSpec((1, length, per_group), lambda q: (q, 0, 0)),
-                pl.BlockSpec((1, wide), at),
-                pl.BlockSpec((taps, wide), at),
-                pl.BlockSpec((2, taps, size), lambda q: (0, 0, q)),
-                pl.BlockSpec((1, 1, tail_lines, size), lambda q: (q, c, tail_at, 0)),
-                *[anywhere] * len(tokens),
-            ],
-            out_specs=[pl.BlockSpec((length, wide), at), pl.BlockSpec((length, size), at)],
-            out_shape=[
-                pltpu.HBM((length, columns), jnp.float32),
-                pltpu.HBM((length, groups * size), jnp.bfloat16),
-            ],
-            scratch_shapes=[
-                pltpu.VMEM((8 + FIX, size), jnp.float32),
-            ],
-            compiler_params=params,
-            cost_estimate=pl.CostEstimate(
-                flops=4 * heads * length * length * width,
-                bytes_accessed=6 * length * columns,
-                transcendentals=heads * length * length,
-            ),
-            name="mix",
-        )(*operands, *tokens)
-
-    def finish(k, states, early, mixed, result):
+    def late(k, states, states_first, parts, result, tokens):
         part, offset = SPLIT[k], offsets[k]
         chunk = part * width
-        at = lambda q: (0, q * (per_group // part) + offset // part)
-        operands, specs = [], []
+        unit = offset // part
+        at = lambda q: (0, q * (per_group // part) + unit)
+        lane = lambda q: (0, 0, q * (per_group // part) + unit)
+        tail_at = SPLIT[0] * width // tail_lines
+        operands = [x_in, b_in, c_in, skip_row, conv_x, conv_bc]
+        specs = [
+            pl.BlockSpec((kids, FIX, chunk), lane),
+            pl.BlockSpec((kids, FIX, size), lambda q: (0, 0, q)),
+            pl.BlockSpec((kids, FIX, size), lambda q: (0, 0, q)),
+            pl.BlockSpec((1, chunk), at),
+            pl.BlockSpec((taps, chunk), at),
+            pl.BlockSpec((2, taps, size), lambda q: (0, 0, q)),
+        ]
         for c in range(kids):
-            operands += [states, *map(stay, (mixed[c][1], early[c][4], mixed[c][0]))]
+            mixed, held, column, first = parts[c]
+            operands += [states, states_first, held, column, first, mixed]
             specs += [
                 pl.BlockSpec((1, 1, chunk, size), lambda q, c=c: (q, c, 0, 0)),
+                pl.BlockSpec((1, 1, tail_lines, size), lambda q, c=c: (q, c, tail_at, 0)),
                 pl.BlockSpec((length, size), lambda q: (0, q)),
                 pl.BlockSpec((1, length, per_group), lambda q: (q, 0, 0)),
+                pl.BlockSpec((1, length, part * FIX), lambda q: (q, 0, unit)),
                 pl.BlockSpec((length, chunk), at),
             ]
+        keep = len(operands)
+        operands += tokens
+        specs += [anywhere] * len(tokens)
         alias = {}
         if result is not None:
             alias = {len(operands): 0}
             operands.append(result)
             specs.append(anywhere)
         return pl.pallas_call(
-            functools.partial(state_kernel, offset),
+            functools.partial(
+                drop_tokens,
+                functools.partial(late_kernel, offset, lines),
+                keep,
+                len(operands) - keep,
+            ),
             grid=(groups,),
             in_specs=specs,
-            out_specs=pl.BlockSpec((kids, length, chunk), lambda q: (0, *at(q))),
+            out_specs=pl.BlockSpec((kids, length, chunk), lane),
             out_shape=jax.ShapeDtypeStruct(x_in.shape, jnp.bfloat16),
             input_output_aliases=alias,
+            scratch_shapes=[pltpu.VMEM((8 + FIX, size), jnp.float32)],
             compiler_params=params,
             cost_estimate=pl.CostEstimate(
-                flops=2 * kids * groups * length * chunk * size,
+                flops=4 * kids * groups * length * chunk * size,
                 bytes_accessed=6 * kids * groups * length * chunk,
                 transcendentals=kids * groups * length * chunk,
             ),
-            name="add_states",
+            name="late",
         )(*operands)
 
     skip_row = jnp.repeat(d_skip, width)[None, :]
@@ -656,16 +684,14 @@
     crossed_a = [swap(sent_a[j], j + 4) for j in quarters]
     whole = cast_whole([sent_a[0]])
     inside = gather_half(whole)
-    early = [convolve(0, [whole])]
-    early.append(convolve(1, [stay(early[0][3])]))
-    sent_b = cast(quarters, [1], [*crossed_a, stay(early[1][3])])
-    crossed_b = [swap(sent_b[j], j + 4) for j in quarters]
-    picked_a, states_a = pick(rows[0], 0, inside, crossed_a, [sent_b[0]])
-    picked_b, states_b = pick(rows[1], rows[0], inside, crossed_b, [picked_a])
-    mixed = [mix(0, early[0], states_a, [picked_b])]
-    mixed.append(mix(1, early[1], states_a, [stay(mixed[0][1])]))
-    result = finish(0, states_a, early, mixed, None)
-    return finish(1, states_b, early, mixed, result)
+    parts = [early(0, [whole])]
+    sent_b = chunk_b(inside, [parts[0][1]])
+    crossed_b = swap(sent_b, 4)
+    picked_a, states_a = pick(rows[0], 0, slots_a, inside, crossed_a, [sent_b])
+    parts.append(early(1, [picked_a]))
+    picked_b, states_b = pick(rows[1], rows[0], slots_b, inside, [crossed_b], [parts[1][1]])
+    result = late(0, states_a, states_a, parts, None, [picked_b])
+    return late(1, states_b, states_a, parts, result, [])
 
 
 def solution(mesh):

time: 108 us -> 108 us (level)
  local copies, waits for them, and re-layouts: 0.37 us -> 26.4 us
  waiting for transfers between devices: 26.5 us -> 11.3 us
  Pallas kernels: 52.4 us -> 43 us
  starting transfers between devices: 27 us -> 24.1 us
  other arithmetic: 0.29 us -> 1.41 us
    unnamed x10 -> x52, local copies, waits for them, and re-layouts: 0.02 us -> 26.1 us
    ppermute x8 -> x5, waiting for transfers between devices: 26.4 us -> 11.3 us  [swap(): return lax.ppermute(value, 'batch', perm=[(i, i ^ r) for i in range(8)])]
    pallas_call x7 -> x6, Pallas kernels: 42.8 us -> 34 us  [the longest x2 21.1 us: early(): pl.pallas_call(functools.partial(drop_tokens, early_kernel, len(operands)...]
    ppermute x8 -> x5, starting transfers between devices: 14.6 us -> 9.83 us  [swap(): return lax.ppermute(value, 'batch', perm=[(i, i ^ r) for i in range(8)])]
    all_to_all x3, starting transfers between devices: 12.5 us -> 14.3 us  [gather_half(): lax.all_to_all(value, 'batch', split_axis=0, concat_axis=0, tiled=True, a...]
    select_n x1 -> x2, other arithmetic: 0.09 us -> 1.21 us  [the longest x1 0.61 us: local_halves(): slots_b = jnp.where(here, owner % 4, 4 + owner % 4)]
    pallas_call x2 -> x1, Pallas kernels: 2.56 us -> 1.91 us  [cast(): pl.pallas_call(functools.partial(drop_tokens, lambda place_ref, *refs: ke...]
  transfers between devices with their start and end apart: 11 -> 8, of which waited for: 6 -> 3; matrix products, arithmetic and copies ran while one was open for 1% -> 2% of each run, Pallas kernels for 36% -> 28%
where the time goes in v6:
time: 108 us; the launch traced here: 106 us
  Pallas kernels  43 us (40%)
  local copies, waits for them, and re-layouts  26.4 us (24%)
  starting transfers between devices  24.1 us (22%)
  waiting for transfers between devices  11.3 us (10%)
  other arithmetic  1.41 us (1%)
    unnamed x52, local copies, waits for them, and re-layouts  26.1 us
    pallas_call x2, Pallas kernels, early(): pl.pallas_call(functools.partial(drop_tokens, early_kernel, len(operands)...  21.1 us
    all_to_all x3, starting transfers between devices, gather_half(): lax.all_to_all(value, 'batch', split_axis=0, concat_axis=0, tiled=True, a...  14.3 us
    ppermute x5, waiting for transfers between devices, swap(): return lax.ppermute(value, 'batch', perm=[(i, i ^ r) for i in range(8)])  11.3 us
    pallas_call x2, Pallas kernels, late(): pl.pallas_call(functools.partial(drop_tokens, functools.partial(late_kern...  10.2 us
    ppermute x5, starting transfers between devices, swap(): return lax.ppermute(value, 'batch', perm=[(i, i ^ r) for i in range(8)])  9.83 us
    pallas_call x2, Pallas kernels, pick(): pl.pallas_call(functools.partial(drop_tokens, functools.partial(pick_rows...  7.05 us
    pallas_call x1, Pallas kernels, cast_whole(): pl.pallas_call(functools.partial(drop_tokens, kernel, len(operands), len(...  2.7 us
  transfers between devices with their start and end apart: 8, of which 3 were waited for; matrix products, arithmetic and copies ran while one was open for 2% of the time, Pallas kernels for 28%

profile of v6, /device:TPU:0, one launch (start us, length us, event | category | flops | bytes accessed | tf_op | source)
XLA Modules:
  0.0 106.4 jit_solution(10825099671517569759)
XLA Ops:
  0.0 1.9 %cast_states.2 = (bf16[544,128]{1,0:T(8,128)(2,1)S(1)}, bf16[544,128]{1,0:T(8,128)(2,1)}, bf16[544,128]{1,0:T(8,128)(2,1)S(1)}, bf16[544,128]{1,0:T(8,128)(2,1)S(1)}) custom-call(s32[1]{0:T(128)} %bitcast.2.refs_0_, f32[4,16,64,128]{3,2,1,0:T(8,128)} %bitcast.15, f32[4,16,64,128]{3,2,1,0:T(8,128)} %bitcast.16, f32[4,16,64,128]{3,2,1,0:T(8,128)} %bitcast.17, ...), custom_call_target="tpu_custom_call" | custom-call | bytes 1671168 | tf_op jit(solution)/shard_map/cast_states/pallas_call | solution.py:482
  1.9 0.0 copy-start.24
  1.9 0.0 copy-start.25
  2.0 2.7 %cast_states.3.refs_9_ = bf16[4,1056,128]{2,1,0:T(8,128)(2,1)} custom-call(f32[4,16,64,128]{3,2,1,0:T(8,128)} %bitcast.19, f32[4,16,64,128]{3,2,1,0:T(8,128)} %bitcast.20, bf16[1,3,4096]{2,1,0:T(4,128)(2,1)} %refs_14_.1, bf16[1,3,2,512]{3,2,1,0:T(2,128)(2,1)} %bitcast.31, f32[4,16,64,128]{3,2,1,0:T(8,128)} %bitcast.21, f32[4,16,64,128]{3,2,1,0:T(8,128)} %bitcast.22, ...), custom_call_target="tpu_custom_call" | custom-call | bytes 3244032 | tf_op jit(solution)/shard_map/cast_states/pallas_call | solution.py:517
  4.7 5.2 %all-to-all-start = ((bf16[4,1056,128]{2,1,0:T(8,128)(2,1)}), bf16[4,1056,128]{2,1,0:T(8,128)(2,1)S(1)}, u32[]{:S(2)}, u32[]{:S(2)}) async-start(bf16[4,1056,128]{2,1,0:T(8,128)(2,1)} %cast_states.3.refs_9_), calls=%async_computation | async-start | bytes 2162688 | tf_op jit(solution)/shard_map/all_to_all | solution.py:550
  9.9 2.6 %collective-permute-start.1 = (bf16[544,128]{1,0:T(8,128)(2,1)S(1)}, bf16[544,128]{1,0:T(8,128)(2,1)S(1)}, u32[]{:S(2)}, u32[]{:S(2)}) collective-permute-start(bf16[544,128]{1,0:T(8,128)(2,1)S(1)} %get-tuple-element.17.refs_16_), channel_id=1, source_target_pairs={{0,8},{2,10},{4,12},{6,14},{8,0},{10,2},{12,4},{14,6},{1,9},{3,11}... | collective-permute-start | bytes 417800 | tf_op jit(solution)/shard_map/ppermute | solution.py:459
  12.5 1.8 %collective-permute-start.2 = (bf16[544,128]{1,0:T(8,128)(2,1)}, bf16[544,128]{1,0:T(8,128)(2,1)S(1)}, u32[]{:S(2)}, u32[]{:S(2)}) collective-permute-start(bf16[544,128]{1,0:T(8,128)(2,1)} %get-tuple-element.19), channel_id=1, source_target_pairs={{0,10},{2,8},{4,14},{6,12},{8,2},{10,0},{12,6},{14,4},{1,11},{3,9}... | collective-permute-start | bytes 417800 | tf_op jit(solution)/shard_map/ppermute | solution.py:459
  14.3 3.5 %collective-permute-start.3 = (bf16[544,128]{1,0:T(8,128)(2,1)S(1)}, bf16[544,128]{1,0:T(8,128)(2,1)S(1)}, u32[]{:S(2)}, u32[]{:S(2)}) collective-permute-start(bf16[544,128]{1,0:T(8,128)(2,1)S(1)} %get-tuple-element.20), channel_id=1, source_target_pairs={{0,12},{2,14},{4,8},{6,10},{8,4},{10,6},{12,0},{14,2},{1,13},{3,15... | collective-permute-start | bytes 417800 | tf_op jit(solution)/shard_map/ppermute | solution.py:459
  17.8 0.1 copy.20.refs_4_
  17.9 0.1 copy.21.refs_5_
  18.0 0.1 broadcast_in_dim.31
  18.1 0.1 broadcast_in_dim_reshape.3.refs_6_.refs_3_
  18.2 0.1 select_reduce_fusion
  18.3 0.1 convert_reduce_fusion
  18.4 10.6 %early.2 = (f32[256,4096]{1,0:T(8,128)S(1)}, bf16[256,512]{1,0:T(8,128)(2,1)S(1)}, f32[4,256,16]{2,1,0:T(8,128)S(1)}, f32[4,256,256]{2,1,0:T(8,128)S(1)}) custom-call(bf16[2,256,4096]{2,1,0:T(8,128)(2,1)} %refs_0_.7, bf16[2,256,512]{2,1,0:T(8,128)(2,1)} %refs_1_.7, bf16[2,256,512]{2,1,0:T(8,128)(2,1)} %refs_2_.9, f32[2,64,256]{2,1,0:T(8,128)} %refs_3_.3, ...), custom_call_target="tpu_custom_call" | custom-call | flops 1073741824 | bytes 8388608 | tf_op jit(solution)/shard_map/early/pallas_call | solution.py:586
  28.9 2.0 %copy-done = f32[256,4096]{1,0:T(8,128)} copy-done((f32[256,4096]{1,0:T(8,128)}, f32[256,4096]{1,0:T(8,128)S(1)}, u32[]{:S(2)}) %copy-start) | copy-done | bytes 4194328
  30.9 0.8 copy-done.12
  31.7 0.6 compare_select_fusion.5
  32.4 3.9 %collective-permute-done.3.refs_4_ = bf16[544,128]{1,0:T(8,128)(2,1)S(1)} collective-permute-done((bf16[544,128]{1,0:T(8,128)(2,1)S(1)}, bf16[544,128]{1,0:T(8,128)(2,1)S(1)}, u32[]{:S(2)}, u32[]{:S(2)}) %collective-permute-start.3) | collective-permute-done | bytes 139296 | tf_op jit(solution)/shard_map/ppermute | solution.py:459
  36.3 2.5 %collective-permute-done.4.refs_5_ = bf16[544,128]{1,0:T(8,128)(2,1)S(1)} collective-permute-done((bf16[544,128]{1,0:T(8,128)(2,1)S(1)}, bf16[544,128]{1,0:T(8,128)(2,1)S(1)}, u32[]{:S(2)}, u32[]{:S(2)}) %collective-permute-start.4) | collective-permute-done | bytes 139296 | tf_op jit(solution)/shard_map/ppermute | solution.py:459
  38.8 3.6 %pick_states.2.refs_9_ = bf16[8,544,128]{2,1,0:T(8,128)(2,1)} custom-call(s32[8]{0:T(128)S(1)} %get-tuple-element.29.refs_0_, bf16[4,1056,128]{2,1,0:T(8,128)(2,1)S(1)} %all-to-all-done.refs_0_.refs_1_, bf16[544,128]{1,0:T(8,128)(2,1)S(1)} %collective-permute-done.1.refs_2_, bf16[544,128]{1,0:T(8,128)(2,1)S(1)} %collective-permute-done.2.refs_3_, ...), custom_call_target="tpu_custom_call" | custom-call | bytes 2228224 | tf_op jit(solution)/shard_map/pick_states/pallas_call | solution.py:561
  42.3 0.8 copy-done.18
  43.1 3.5 %all-to-all-start.2 = ((bf16[8,544,128]{2,1,0:T(8,128)(2,1)}), bf16[8,544,128]{2,1,0:T(8,128)(2,1)S(1)}, u32[]{:S(2)}, u32[]{:S(2)}) async-start(bf16[8,544,128]{2,1,0:T(8,128)(2,1)} %pick_states.2.refs_9_), calls=%async_computation.2 | async-start | bytes 2228224 | tf_op jit(solution)/shard_map/all_to_all | solution.py:550
  46.6 2.0 %collective-permute-start = (bf16[4,512,128]{2,1,0:T(8,128)(2,1)}, bf16[4,512,128]{2,1,0:T(8,128)(2,1)S(1)}, u32[]{:S(2)}, u32[]{:S(2)}) collective-permute-start(bf16[4,512,128]{2,1,0:T(8,128)(2,1)} %copy-done.18), channel_id=1, source_target_pairs={{0,8},{2,10},{4,12},{6,14},{8,0},{10,2},{12,4},{14,6},{1,9},{3,11}... | collective-permute-start | bytes 1572872 | tf_op jit(solution)/shard_map/ppermute | solution.py:459
  48.6 0.6 compare_select_fusion.6.refs_0_
  49.2 0.8 copy-done.20
  50.0 10.6 %early.3 = (f32[256,4096]{1,0:T(8,128)S(1)}, bf16[256,512]{1,0:T(8,128)(2,1)S(1)}, f32[4,256,16]{2,1,0:T(8,128)S(1)}, f32[4,256,256]{2,1,0:T(8,128)S(1)}) custom-call(bf16[2,256,4096]{2,1,0:T(8,128)(2,1)} %refs_0_.7, bf16[2,256,512]{2,1,0:T(8,128)(2,1)} %refs_1_.7, bf16[2,256,512]{2,1,0:T(8,128)(2,1)} %refs_2_.9, f32[2,64,256]{2,1,0:T(8,128)} %refs_3_.3, ...), custom_call_target="tpu_custom_call" | custom-call | flops 1073741824 | bytes 8388608 | tf_op jit(solution)/shard_map/early/pallas_call | solution.py:586
  60.5 2.0 %copy-done.3 = f32[256,4096]{1,0:T(8,128)} copy-done((f32[256,4096]{1,0:T(8,128)}, f32[256,4096]{1,0:T(8,128)S(1)}, u32[]{:S(2)}) %copy-start.3) | copy-done | bytes 4194328
  62.5 1.0 copy-done.6
  63.6 0.8 copy-done.15
  64.4 4.9 %collective-permute-done.refs_2_ = bf16[4,512,128]{2,1,0:T(8,128)(2,1)S(1)} collective-permute-done((bf16[4,512,128]{2,1,0:T(8,128)(2,1)}, bf16[4,512,128]{2,1,0:T(8,128)(2,1)S(1)}, u32[]{:S(2)}, u32[]{:S(2)}) %collective-permute-start) | collective-permute-done | bytes 524320 | tf_op jit(solution)/shard_map/ppermute | solution.py:459
  69.3 3.5 %pick_states.3.refs_18_ = bf16[8,512,128]{2,1,0:T(8,128)(2,1)} custom-call(s32[8]{0:T(128)S(1)} %compare_select_fusion.6.refs_0_, bf16[4,1056,128]{2,1,0:T(8,128)(2,1)S(1)} %all-to-all-done.refs_0_.refs_1_, bf16[4,512,128]{2,1,0:T(8,128)(2,1)S(1)} %collective-permute-done.refs_2_, bf16[256,512]{1,0:T(8,128)(2,1)S(1)} %get-tuple-element.22.refs_3_.refs_14_), custom_call_target="tpu_custom_call" | custom-call | bytes 2097152 | tf_op jit(solution)/shard_map/pick_states/pallas_call | solution.py:561
  72.8 0.7 copy-done.9
  73.5 5.5 %all-to-all-start.1 = ((bf16[8,512,128]{2,1,0:T(8,128)(2,1)}), bf16[8,512,128]{2,1,0:T(8,128)(2,1)S(1)}, u32[]{:S(2)}, u32[]{:S(2)}) async-start(bf16[8,512,128]{2,1,0:T(8,128)(2,1)} %pick_states.3.refs_18_), calls=%async_computation.1 | async-start | bytes 2097152 | tf_op jit(solution)/shard_map/all_to_all | solution.py:550
  79.0 2.2 %copy-done.1 = f32[256,4096]{1,0:T(8,128)S(1)} copy-done((f32[256,4096]{1,0:T(8,128)S(1)}, f32[256,4096]{1,0:T(8,128)}, u32[]{:S(2)}) %copy-start.1) | copy-done | bytes 4194328
  81.2 2.2 %copy-done.4 = f32[256,4096]{1,0:T(8,128)S(1)} copy-done((f32[256,4096]{1,0:T(8,128)S(1)}, f32[256,4096]{1,0:T(8,128)}, u32[]{:S(2)}) %copy-start.4) | copy-done | bytes 4194328
  83.4 1.2 %copy-done.7 = f32[4,256,256]{2,1,0:T(8,128)S(1)} copy-done((f32[4,256,256]{2,1,0:T(8,128)S(1)}, f32[4,256,256]{2,1,0:T(8,128)}, u32[]{:S(2)}) %copy-start.7) | copy-done | bytes 1048600
  84.6 0.9 copy-done.10
  85.5 1.0 copy-done.13
  86.6 1.0 copy-done.16
  87.6 5.1 %late.2.refs_18_ = bf16[2,256,4096]{2,1,0:T(8,128)(2,1)} custom-call(bf16[2,256,4096]{2,1,0:T(8,128)(2,1)} %refs_0_.7, bf16[2,256,512]{2,1,0:T(8,128)(2,1)} %refs_1_.7, bf16[2,256,512]{2,1,0:T(8,128)(2,1)} %refs_2_.9, f32[1,4096]{1,0:T(1,128)S(1)} %broadcast_in_dim_reshape.3.refs_6_.refs_3_, f32[4,4096]{1,0:T(4,128)} %refs_4_.3, f32[2,4,512]{2,1,0:T(4,128)} %refs_5_.5, ...), custom_call_target="tpu_custom_call" | custom-call | flops 536870912 | bytes 6291456 | tf_op jit(solution)/shard_map/late/pallas_call | solution.py:658
  92.7 2.2 %copy-done.2 = f32[256,4096]{1,0:T(8,128)S(1)} copy-done((f32[256,4096]{1,0:T(8,128)S(1)}, f32[256,4096]{1,0:T(8,128)}, u32[]{:S(2)}) %copy-start.2) | copy-done | bytes 4194328
  94.9 2.2 %copy-done.5 = f32[256,4096]{1,0:T(8,128)S(1)} copy-done((f32[256,4096]{1,0:T(8,128)S(1)}, f32[256,4096]{1,0:T(8,128)}, u32[]{:S(2)}) %copy-start.5) | copy-done | bytes 4194328
  97.1 1.2 %copy-done.8 = f32[4,256,256]{2,1,0:T(8,128)S(1)} copy-done((f32[4,256,256]{2,1,0:T(8,128)S(1)}, f32[4,256,256]{2,1,0:T(8,128)}, u32[]{:S(2)}) %copy-start.8) | copy-done | bytes 1048600
  98.3 0.9 copy-done.11
  99.3 1.0 copy-done.14
  100.3 1.0 copy-done.17
  101.4 5.1 %late.3 = bf16[2,256,4096]{2,1,0:T(8,128)(2,1)} custom-call(bf16[2,256,4096]{2,1,0:T(8,128)(2,1)} %refs_0_.7, bf16[2,256,512]{2,1,0:T(8,128)(2,1)} %refs_1_.7, bf16[2,256,512]{2,1,0:T(8,128)(2,1)} %refs_2_.9, f32[1,4096]{1,0:T(1,128)S(1)} %broadcast_in_dim_reshape.3.refs_6_.refs_3_, f32[4,4096]{1,0:T(4,128)} %refs_4_.3, ...), custom_call_target="tpu_custom_call", output_to_operand_aliasing={{}: (18, {})} | custom-call | flops 536870912 | bytes 6291456 | tf_op jit(solution)/shard_map/late/pallas_call | solution.py:658
  (37 shorter events, 0.1 us)
Async XLA Ops:
  1.9 15.9 %copy-start.21 = (f32[64]{0:T(128)S(1)}, f32[64]{0:T(128)}, u32[]{:S(2)}) copy-start(f32[64]{0:T(128)} %param.18) | copy-start | bytes 772
  1.9 16.0 %copy-start.22 = (f32[64]{0:T(128)S(1)}, f32[64]{0:T(128)}, u32[]{:S(2)}) copy-start(f32[64]{0:T(128)} %param.19) | copy-start | bytes 772
  1.9 16.1 %copy-start.23 = (f32[64]{0:T(128)S(1)}, f32[64]{0:T(128)}, u32[]{:S(2)}) copy-start(f32[64]{0:T(128)} %param.20) | copy-start | bytes 772
  1.9 16.2 %copy-start.24 = (s32[8]{0:T(128)S(1)}, s32[8]{0:T(128)}, u32[]{:S(2)}) copy-start(s32[8]{0:T(128)} %param.26) | copy-start | bytes 100
  1.9 16.3 %copy-start.25 = (s32[16]{0:T(128)S(1)}, s32[16]{0:T(128)}, u32[]{:S(2)}) copy-start(s32[16]{0:T(128)} %param.27) | copy-start | bytes 196
  4.7 27.7 %all-to-all-start = ((bf16[4,1056,128]{2,1,0:T(8,128)(2,1)}), bf16[4,1056,128]{2,1,0:T(8,128)(2,1)S(1)}, u32[]{:S(2)}, u32[]{:S(2)}) async-start(bf16[4,1056,128]{2,1,0:T(8,128)(2,1)} %cast_states.3.refs_9_), calls=%async_computation | async-start | bytes 2162688 | tf_op jit(solution)/shard_map/all_to_all | solution.py:550
  9.9 28.9 %collective-permute-start.1 = (bf16[544,128]{1,0:T(8,128)(2,1)S(1)}, bf16[544,128]{1,0:T(8,128)(2,1)S(1)}, u32[]{:S(2)}, u32[]{:S(2)}) collective-permute-start(bf16[544,128]{1,0:T(8,128)(2,1)S(1)} %get-tuple-element.17.refs_16_), channel_id=1, source_target_pairs={{0,8},{2,10},{4,12},{6,14},{8,0},{10,2},{12,4},{14,6},{1,9},{3,11}... | collective-permute-start | bytes 417800 | tf_op jit(solution)/shard_map/ppermute | solution.py:459
  12.5 19.9 %collective-permute-start.2 = (bf16[544,128]{1,0:T(8,128)(2,1)}, bf16[544,128]{1,0:T(8,128)(2,1)S(1)}, u32[]{:S(2)}, u32[]{:S(2)}) collective-permute-start(bf16[544,128]{1,0:T(8,128)(2,1)} %get-tuple-element.19), channel_id=1, source_target_pairs={{0,10},{2,8},{4,14},{6,12},{8,2},{10,0},{12,6},{14,4},{1,11},{3,9}... | collective-permute-start | bytes 417800 | tf_op jit(solution)/shard_map/ppermute | solution.py:459
  14.3 22.0 %collective-permute-start.3 = (bf16[544,128]{1,0:T(8,128)(2,1)S(1)}, bf16[544,128]{1,0:T(8,128)(2,1)S(1)}, u32[]{:S(2)}, u32[]{:S(2)}) collective-permute-start(bf16[544,128]{1,0:T(8,128)(2,1)S(1)} %get-tuple-element.20), channel_id=1, source_target_pairs={{0,12},{2,14},{4,8},{6,10},{8,4},{10,6},{12,0},{14,2},{1,13},{3,15... | collective-permute-start | bytes 417800 | tf_op jit(solution)/shard_map/ppermute | solution.py:459
  17.8 21.0 %collective-permute-start.4 = (bf16[544,128]{1,0:T(8,128)(2,1)S(1)}, bf16[544,128]{1,0:T(8,128)(2,1)S(1)}, u32[]{:S(2)}, u32[]{:S(2)}) collective-permute-start(bf16[544,128]{1,0:T(8,128)(2,1)S(1)} %get-tuple-element.21), channel_id=1, source_target_pairs={{0,14},{2,12},{4,10},{6,8},{8,6},{10,4},{12,2},{14,0},{1,15},{3,13... | collective-permute-start | bytes 417800 | tf_op jit(solution)/shard_map/ppermute | solution.py:459
  18.0 14.4 %copy-start.19 = (f32[64,1]{1,0:T(8,128)}, f32[64,1]{1,0:T(8,128)S(1)}, u32[]{:S(2)}) copy-start(f32[64,1]{1,0:T(8,128)S(1)} %copy.21.refs_5_) | copy-start | bytes 772
  28.9 2.0 %copy-start = (f32[256,4096]{1,0:T(8,128)}, f32[256,4096]{1,0:T(8,128)S(1)}, u32[]{:S(2)}) copy-start(f32[256,4096]{1,0:T(8,128)S(1)} %get-tuple-element.25.refs_11_) | copy-start | bytes 12582916
  30.9 0.8 copy-start.12
  42.3 0.8 copy-start.18
  43.1 30.4 %all-to-all-start.2 = ((bf16[8,544,128]{2,1,0:T(8,128)(2,1)}), bf16[8,544,128]{2,1,0:T(8,128)(2,1)S(1)}, u32[]{:S(2)}, u32[]{:S(2)}) async-start(bf16[8,544,128]{2,1,0:T(8,128)(2,1)} %pick_states.2.refs_9_), calls=%async_computation.2 | async-start | bytes 2228224 | tf_op jit(solution)/shard_map/all_to_all | solution.py:550
  46.6 22.6 %collective-permute-start = (bf16[4,512,128]{2,1,0:T(8,128)(2,1)}, bf16[4,512,128]{2,1,0:T(8,128)(2,1)S(1)}, u32[]{:S(2)}, u32[]{:S(2)}) collective-permute-start(bf16[4,512,128]{2,1,0:T(8,128)(2,1)} %copy-done.18), channel_id=1, source_target_pairs={{0,8},{2,10},{4,12},{6,14},{8,0},{10,2},{12,4},{14,6},{1,9},{3,11}... | collective-permute-start | bytes 1572872 | tf_op jit(solution)/shard_map/ppermute | solution.py:459
  49.2 0.8 copy-start.20
  60.5 2.0 %copy-start.3 = (f32[256,4096]{1,0:T(8,128)}, f32[256,4096]{1,0:T(8,128)S(1)}, u32[]{:S(2)}) copy-start(f32[256,4096]{1,0:T(8,128)S(1)} %get-tuple-element.28.refs_17_) | copy-start | bytes 12582916
  62.5 1.0 copy-start.6
  63.6 0.8 copy-start.15
  72.8 0.7 copy-start.9
  73.5 19.2 %all-to-all-start.1 = ((bf16[8,512,128]{2,1,0:T(8,128)(2,1)}), bf16[8,512,128]{2,1,0:T(8,128)(2,1)S(1)}, u32[]{:S(2)}, u32[]{:S(2)}) async-start(bf16[8,512,128]{2,1,0:T(8,128)(2,1)} %pick_states.3.refs_18_), calls=%async_computation.1 | async-start | bytes 2097152 | tf_op jit(solution)/shard_map/all_to_all | solution.py:550
  79.0 2.2 %copy-start.1 = (f32[256,4096]{1,0:T(8,128)S(1)}, f32[256,4096]{1,0:T(8,128)}, u32[]{:S(2)}) copy-start(f32[256,4096]{1,0:T(8,128)} %copy-done) | copy-start | bytes 12582916
  81.2 2.2 %copy-start.4 = (f32[256,4096]{1,0:T(8,128)S(1)}, f32[256,4096]{1,0:T(8,128)}, u32[]{:S(2)}) copy-start(f32[256,4096]{1,0:T(8,128)} %copy-done.3) | copy-start | bytes 12582916
  83.4 1.2 %copy-start.7 = (f32[4,256,256]{2,1,0:T(8,128)S(1)}, f32[4,256,256]{2,1,0:T(8,128)}, u32[]{:S(2)}) copy-start(f32[4,256,256]{2,1,0:T(8,128)} %copy-done.6) | copy-start | bytes 3145732
  84.6 0.9 copy-start.10
  85.5 1.0 copy-start.13
  86.6 1.0 copy-start.16
  92.7 2.2 %copy-start.2 = (f32[256,4096]{1,0:T(8,128)S(1)}, f32[256,4096]{1,0:T(8,128)}, u32[]{:S(2)}) copy-start(f32[256,4096]{1,0:T(8,128)} %copy-done) | copy-start | bytes 12582916
  94.9 2.2 %copy-start.5 = (f32[256,4096]{1,0:T(8,128)S(1)}, f32[256,4096]{1,0:T(8,128)}, u32[]{:S(2)}) copy-start(f32[256,4096]{1,0:T(8,128)} %copy-done.3) | copy-start | bytes 12582916
  97.1 1.2 %copy-start.8 = (f32[4,256,256]{2,1,0:T(8,128)S(1)}, f32[4,256,256]{2,1,0:T(8,128)}, u32[]{:S(2)}) copy-start(f32[4,256,256]{2,1,0:T(8,128)} %copy-done.6) | copy-start | bytes 3145732
  98.3 0.9 copy-start.11
  99.3 1.0 copy-start.14
  100.3 1.0 copy-start.17

commit v7 on v6

--- a/solution.py
+++ b/solution.py
@@ -438,6 +438,7 @@
     tail_lines = -(-lines * reach // 16) * 16
     params = pltpu.CompilerParams(vmem_limit_bytes=VMEM_LIMIT)
     anywhere = pl.BlockSpec(memory_space=pl.ANY)
+    small = pl.CostEstimate(flops=1, bytes_accessed=1, transcendentals=0)
 
     stay = lambda x: pltpu.with_memory_space_constraint(x, pltpu.HBM)
     x_in, b_in, c_in, dt_in, conv_x, conv_bc = map(stay, (x_in, b_in, c_in, dt_in, conv_x, conv_bc))
@@ -491,9 +492,7 @@
             ),
             out_shape=[jax.ShapeDtypeStruct((rows, size), jnp.bfloat16)] * len(quarters),
             compiler_params=params,
-            cost_estimate=pl.CostEstimate(
-                flops=0, bytes_accessed=6 * len(quarters) * rows * size, transcendentals=0
-            ),
+            cost_estimate=small,
             name="cast_states",
         )(place, *operands, *tokens)
 
@@ -521,9 +520,7 @@
             out_specs=pl.BlockSpec((groups, rows, size), lambda i: (0, 0, 0)),
             out_shape=jax.ShapeDtypeStruct((groups, rows, size), jnp.bfloat16),
             compiler_params=params,
-            cost_estimate=pl.CostEstimate(
-                flops=0, bytes_accessed=6 * groups * rows * size, transcendentals=0
-            ),
+            cost_estimate=small,
             name="cast_states",
         )(*operands, *tokens)
 
@@ -540,9 +537,7 @@
             out_shape=jax.ShapeDtypeStruct((4, rows, size), jnp.bfloat16),
             scratch_shapes=[pltpu.SemaphoreType.DMA],
             compiler_params=params,
-            cost_estimate=pl.CostEstimate(
-                flops=0, bytes_accessed=16 * rows * size, transcendentals=0
-            ),
+            cost_estimate=small,
             name="chunk_b",
         )(inside, *tokens)
 
@@ -571,9 +566,7 @@
             ),
             out_shape=jax.ShapeDtypeStruct((spots, rows, size), jnp.bfloat16),
             compiler_params=params,
-            cost_estimate=pl.CostEstimate(
-                flops=0, bytes_accessed=4 * spots * rows * size, transcendentals=0
-            ),
+            cost_estimate=small,
             name="pick_states",
         )(slots, inside, *crossed, *tokens)
         return picked, gather_half(picked).reshape(4, kids, rows, size)
@@ -605,18 +598,14 @@
                 pl.BlockSpec((1, length, per_group * FIX), lambda q: (q, 0, 0)),
             ],
             out_shape=[
-                jax.ShapeDtypeStruct((length, columns), jnp.float32),
-                jax.ShapeDtypeStruct((length, groups * size), jnp.bfloat16),
-                jax.ShapeDtypeStruct((groups, length, per_group), jnp.float32),
-                jax.ShapeDtypeStruct((groups, length, per_group * FIX), jnp.float32),
+                pltpu.HBM((length, columns), jnp.float32),
+                pltpu.HBM((length, groups * size), jnp.bfloat16),
+                pltpu.HBM((groups, length, per_group), jnp.float32),
+                pltpu.HBM((groups, length, per_group * FIX), jnp.float32),
             ],
             scratch_shapes=[pltpu.VMEM((8 + length, size), jnp.float32)],
             compiler_params=params,
-            cost_estimate=pl.CostEstimate(
-                flops=4 * heads * length * length * width,
-                bytes_accessed=8 * length * columns,
-                transcendentals=heads * length * length,
-            ),
+            cost_estimate=small,
             name="early",
         )(*operands, *tokens)
 
@@ -637,7 +626,7 @@
             pl.BlockSpec((2, taps, size), lambda q: (0, 0, q)),
         ]
         for c in range(kids):
-            mixed, held, column, first = parts[c]
+            mixed, held, column, first = map(stay, parts[c])
             operands += [states, states_first, held, column, first, mixed]
             specs += [
                 pl.BlockSpec((1, 1, chunk, size), lambda q, c=c: (q, c, 0, 0)),
@@ -669,11 +658,7 @@
             input_output_aliases=alias,
             scratch_shapes=[pltpu.VMEM((8 + FIX, size), jnp.float32)],
             compiler_params=params,
-            cost_estimate=pl.CostEstimate(
-                flops=4 * kids * groups * length * chunk * size,
-                bytes_accessed=6 * kids * groups * length * chunk,
-                transcendentals=kids * groups * length * chunk,
-            ),
+            cost_estimate=small,
             name="late",
         )(*operands)
 
@@ -685,11 +670,11 @@
     whole = cast_whole([sent_a[0]])
     inside = gather_half(whole)
     parts = [early(0, [whole])]
-    sent_b = chunk_b(inside, [parts[0][1]])
+    sent_b = chunk_b(inside, [stay(parts[0][1])])
     crossed_b = swap(sent_b, 4)
     picked_a, states_a = pick(rows[0], 0, slots_a, inside, crossed_a, [sent_b])
     parts.append(early(1, [picked_a]))
-    picked_b, states_b = pick(rows[1], rows[0], slots_b, inside, [crossed_b], [parts[1][1]])
+    picked_b, states_b = pick(rows[1], rows[0], slots_b, inside, [crossed_b], [stay(parts[1][1])])
     result = late(0, states_a, states_a, parts, None, [picked_b])
     return late(1, states_b, states_a, parts, result, [])
 

time: 108 us -> 95.3 us (0.88)
  local copies, waits for them, and re-layouts: 26.4 us -> 0.39 us
  waiting for transfers between devices: 11.3 us -> 22.3 us
  Pallas kernels: 43 us -> 47.4 us
  other arithmetic: 1.41 us -> 0.29 us
    unnamed x52 -> x10, local copies, waits for them, and re-layouts: 26.1 us -> 0.03 us
    ppermute x5, waiting for transfers between devices: 11.3 us -> 17.9 us  [swap(): return lax.ppermute(value, 'batch', perm=[(i, i ^ r) for i in range(8)])]
    all_to_all x3, waiting for transfers between devices: 0.01 us -> 4.42 us  [gather_half(): lax.all_to_all(value, 'batch', split_axis=0, concat_axis=0, tiled=True, a...]
    pallas_call x2, Pallas kernels: 10.2 us -> 13.3 us  [late(): pl.pallas_call(functools.partial(drop_tokens, functools.partial(late_kern...]
    pallas_call x2, Pallas kernels: 21.1 us -> 22.9 us  [early(): pl.pallas_call(functools.partial(drop_tokens, early_kernel, len(operands)...]
  transfers between devices with their start and end apart: 8 -> 8, of which waited for: 3 -> 4; matrix products, arithmetic and copies ran while one was open for 2% -> 1% of each run, Pallas kernels for 28% -> 35%
where the time goes in v7:
time: 95.3 us; the launch traced here: 94.7 us
  Pallas kernels  47.4 us (50%)
  starting transfers between devices  24.2 us (25%)
  waiting for transfers between devices  22.3 us (23%)
    pallas_call x2, Pallas kernels, early(): pl.pallas_call(functools.partial(drop_tokens, early_kernel, len(operands)...  22.9 us
    ppermute x5, waiting for transfers between devices, swap(): return lax.ppermute(value, 'batch', perm=[(i, i ^ r) for i in range(8)])  17.9 us
    all_to_all x3, starting transfers between devices, gather_half(): lax.all_to_all(value, 'batch', split_axis=0, concat_axis=0, tiled=True, a...  14.4 us
    pallas_call x2, Pallas kernels, late(): pl.pallas_call(functools.partial(drop_tokens, functools.partial(late_kern...  13.3 us
    ppermute x5, starting transfers between devices, swap(): return lax.ppermute(value, 'batch', perm=[(i, i ^ r) for i in range(8)])  9.83 us
    pallas_call x2, Pallas kernels, pick(): pl.pallas_call(functools.partial(drop_tokens, functools.partial(pick_rows...  7.04 us
    all_to_all x3, waiting for transfers between devices, gather_half(): lax.all_to_all(value, 'batch', split_axis=0, concat_axis=0, tiled=True, a...  4.42 us
    pallas_call x1, Pallas kernels, cast_whole(): pl.pallas_call(functools.partial(drop_tokens, kernel, len(operands), len(...  2.7 us
  transfers between devices with their start and end apart: 8, of which 4 were waited for; matrix products, arithmetic and copies ran while one was open for 1% of the time, Pallas kernels for 35%

profile of v7, /device:TPU:0, one launch (start us, length us, event | category | flops | bytes accessed | tf_op | source)
XLA Modules:
  0.0 94.7 jit_solution(12033367551664685733)
XLA Ops:
  0.0 1.3 %cast_states.2 = (bf16[544,128]{1,0:T(8,128)(2,1)S(1)}, bf16[544,128]{1,0:T(8,128)(2,1)S(1)}, bf16[544,128]{1,0:T(8,128)(2,1)S(1)}, bf16[544,128]{1,0:T(8,128)(2,1)S(1)}) custom-call(s32[1]{0:T(128)} %bitcast.2.refs_0_, f32[4,16,64,128]{3,2,1,0:T(8,128)} %bitcast.15, f32[4,16,64,128]{3,2,1,0:T(8,128)} %bitcast.16, f32[4,16,64,128]{3,2,1,0:T(8,128)} %bitcast.17, ...), custom_call_target="tpu_custom_call" | custom-call | flops 1 | bytes 1 | tf_op jit(solution)/shard_map/cast_states/pallas_call | solution.py:483
  1.3 0.0 copy-start.3
  1.3 0.0 copy-start.4
  1.3 0.0 copy-start
  1.4 0.0 copy-start.1
  1.4 0.0 copy-start.2
  1.4 2.7 %cast_states.3.refs_9_ = bf16[4,1056,128]{2,1,0:T(8,128)(2,1)} custom-call(f32[4,16,64,128]{3,2,1,0:T(8,128)} %bitcast.19, f32[4,16,64,128]{3,2,1,0:T(8,128)} %bitcast.20, bf16[1,3,4096]{2,1,0:T(4,128)(2,1)} %refs_14_.1, bf16[1,3,2,512]{3,2,1,0:T(2,128)(2,1)} %bitcast.31, f32[4,16,64,128]{3,2,1,0:T(8,128)} %bitcast.21, f32[4,16,64,128]{3,2,1,0:T(8,128)} %bitcast.22, ...), custom_call_target="tpu_custom_call" | custom-call | flops 1 | bytes 1 | tf_op jit(solution)/shard_map/cast_states/pallas_call | solution.py:516
  4.1 5.2 %all-to-all-start = ((bf16[4,1056,128]{2,1,0:T(8,128)(2,1)}), bf16[4,1056,128]{2,1,0:T(8,128)(2,1)S(1)}, u32[]{:S(2)}, u32[]{:S(2)}) async-start(bf16[4,1056,128]{2,1,0:T(8,128)(2,1)} %cast_states.3.refs_9_), calls=%async_computation | async-start | bytes 2162688 | tf_op jit(solution)/shard_map/all_to_all | solution.py:545
  9.3 2.6 %collective-permute-start.1 = (bf16[544,128]{1,0:T(8,128)(2,1)S(1)}, bf16[544,128]{1,0:T(8,128)(2,1)S(1)}, u32[]{:S(2)}, u32[]{:S(2)}) collective-permute-start(bf16[544,128]{1,0:T(8,128)(2,1)S(1)} %get-tuple-element.17.refs_16_), channel_id=1, source_target_pairs={{0,8},{2,10},{4,12},{6,14},{8,0},{10,2},{12,4},{14,6},{1,9},{3,11}... | collective-permute-start | bytes 417800 | tf_op jit(solution)/shard_map/ppermute | solution.py:460
  11.9 1.8 %collective-permute-start.2 = (bf16[544,128]{1,0:T(8,128)(2,1)S(1)}, bf16[544,128]{1,0:T(8,128)(2,1)S(1)}, u32[]{:S(2)}, u32[]{:S(2)}) collective-permute-start(bf16[544,128]{1,0:T(8,128)(2,1)S(1)} %get-tuple-element.19), channel_id=1, source_target_pairs={{0,10},{2,8},{4,14},{6,12},{8,2},{10,0},{12,6},{14,4},{1,11},{3,9}... | collective-permute-start | bytes 417800 | tf_op jit(solution)/shard_map/ppermute | solution.py:460
  13.7 3.5 %collective-permute-start.3 = (bf16[544,128]{1,0:T(8,128)(2,1)S(1)}, bf16[544,128]{1,0:T(8,128)(2,1)S(1)}, u32[]{:S(2)}, u32[]{:S(2)}) collective-permute-start(bf16[544,128]{1,0:T(8,128)(2,1)S(1)} %get-tuple-element.20), channel_id=1, source_target_pairs={{0,12},{2,14},{4,8},{6,10},{8,4},{10,6},{12,0},{14,2},{1,13},{3,15... | collective-permute-start | bytes 417800 | tf_op jit(solution)/shard_map/ppermute | solution.py:460
  17.2 0.0 collective-permute-start.4
  17.2 0.0 copy-done.3
  17.2 0.1 select_reduce_fusion
  17.3 0.0 copy-done.4
  17.3 0.1 convert_reduce_fusion
  17.4 0.0 copy-done
  17.4 0.1 copy.20.refs_4_
  17.5 0.0 copy-done.1
  17.5 0.1 copy.21.refs_5_
  17.6 0.0 copy-done.2
  17.6 0.1 broadcast_in_dim.31
  17.7 0.1 broadcast_in_dim_reshape.3.refs_6_.refs_3_
  17.8 11.4 %early.2 = (f32[256,4096]{1,0:T(8,128)}, bf16[256,512]{1,0:T(8,128)(2,1)}, f32[4,256,16]{2,1,0:T(8,128)}, f32[4,256,256]{2,1,0:T(8,128)}) custom-call(bf16[2,256,4096]{2,1,0:T(8,128)(2,1)} %refs_0_.7, bf16[2,256,512]{2,1,0:T(8,128)(2,1)} %refs_1_.7, bf16[2,256,512]{2,1,0:T(8,128)(2,1)} %refs_2_.9, f32[2,64,256]{2,1,0:T(8,128)} %refs_3_.3, ...), custom_call_target="tpu_custom_call" | custom-call | flops 1 | bytes 1 | tf_op jit(solution)/shard_map/early/pallas_call | solution.py:579
  29.3 0.1 compare_select_fusion.5
  29.3 0.0 all-to-all-done.refs_0_.refs_1_
  29.4 0.0 collective-permute-done.2.refs_3_
  29.4 6.3 %collective-permute-done.3.refs_4_ = bf16[544,128]{1,0:T(8,128)(2,1)S(1)} collective-permute-done((bf16[544,128]{1,0:T(8,128)(2,1)S(1)}, bf16[544,128]{1,0:T(8,128)(2,1)S(1)}, u32[]{:S(2)}, u32[]{:S(2)}) %collective-permute-start.3) | collective-permute-done | bytes 139296 | tf_op jit(solution)/shard_map/ppermute | solution.py:460
  35.7 2.5 %collective-permute-done.4.refs_5_ = bf16[544,128]{1,0:T(8,128)(2,1)S(1)} collective-permute-done((bf16[544,128]{1,0:T(8,128)(2,1)S(1)}, bf16[544,128]{1,0:T(8,128)(2,1)S(1)}, u32[]{:S(2)}, u32[]{:S(2)}) %collective-permute-start.4) | collective-permute-done | bytes 139296 | tf_op jit(solution)/shard_map/ppermute | solution.py:460
  38.2 0.0 collective-permute-done.1.refs_2_
  38.2 3.6 %pick_states.2.refs_9_ = bf16[8,544,128]{2,1,0:T(8,128)(2,1)} custom-call(s32[8]{0:T(128)S(1)} %get-tuple-element.29.refs_0_, bf16[4,1056,128]{2,1,0:T(8,128)(2,1)S(1)} %all-to-all-done.refs_0_.refs_1_, bf16[544,128]{1,0:T(8,128)(2,1)S(1)} %collective-permute-done.1.refs_2_, bf16[544,128]{1,0:T(8,128)(2,1)S(1)} %collective-permute-done.2.refs_3_, ...), custom_call_target="tpu_custom_call" | custom-call | flops 1 | bytes 1 | tf_op jit(solution)/shard_map/pick_states/pallas_call | solution.py:556
  41.8 3.5 %all-to-all-start.2 = ((bf16[8,544,128]{2,1,0:T(8,128)(2,1)}), bf16[8,544,128]{2,1,0:T(8,128)(2,1)S(1)}, u32[]{:S(2)}, u32[]{:S(2)}) async-start(bf16[8,544,128]{2,1,0:T(8,128)(2,1)} %pick_states.2.refs_9_), calls=%async_computation.2 | async-start | bytes 2228224 | tf_op jit(solution)/shard_map/all_to_all | solution.py:545
  45.3 2.0 %collective-permute-start = (bf16[4,512,128]{2,1,0:T(8,128)(2,1)S(1)}, bf16[4,512,128]{2,1,0:T(8,128)(2,1)S(1)}, u32[]{:S(2)}, u32[]{:S(2)}) collective-permute-start(bf16[4,512,128]{2,1,0:T(8,128)(2,1)S(1)} %chunk_b.1.refs_6_), channel_id=1, source_target_pairs={{0,8},{2,10},{4,12},{6,14},{8,0},{10,2},{12,4},{14,6},{1,9},{3,11}... | collective-permute-start | bytes 1572872 | tf_op jit(solution)/shard_map/ppermute | solution.py:460
  47.3 11.5 %early.3 = (f32[256,4096]{1,0:T(8,128)}, bf16[256,512]{1,0:T(8,128)(2,1)}, f32[4,256,16]{2,1,0:T(8,128)}, f32[4,256,256]{2,1,0:T(8,128)}) custom-call(bf16[2,256,4096]{2,1,0:T(8,128)(2,1)} %refs_0_.7, bf16[2,256,512]{2,1,0:T(8,128)(2,1)} %refs_1_.7, bf16[2,256,512]{2,1,0:T(8,128)(2,1)} %refs_2_.9, f32[2,64,256]{2,1,0:T(8,128)} %refs_3_.3, ...), custom_call_target="tpu_custom_call" | custom-call | flops 1 | bytes 1 | tf_op jit(solution)/shard_map/early/pallas_call | solution.py:579
  58.8 9.1 %collective-permute-done.refs_2_ = bf16[4,512,128]{2,1,0:T(8,128)(2,1)S(1)} collective-permute-done((bf16[4,512,128]{2,1,0:T(8,128)(2,1)S(1)}, bf16[4,512,128]{2,1,0:T(8,128)(2,1)S(1)}, u32[]{:S(2)}, u32[]{:S(2)}) %collective-permute-start) | collective-permute-done | bytes 524320 | tf_op jit(solution)/shard_map/ppermute | solution.py:460
  67.8 3.5 %pick_states.3.refs_18_ = bf16[8,512,128]{2,1,0:T(8,128)(2,1)} custom-call(s32[8]{0:T(128)S(1)} %compare_select_fusion.6.refs_0_, bf16[4,1056,128]{2,1,0:T(8,128)(2,1)S(1)} %all-to-all-done.refs_0_.refs_1_, bf16[4,512,128]{2,1,0:T(8,128)(2,1)S(1)} %collective-permute-done.refs_2_, bf16[256,512]{1,0:T(8,128)(2,1)} %get-tuple-element.22.refs_3_.refs_14_), custom_call_target="tpu_custom_call" | custom-call | flops 1 | bytes 1 | tf_op jit(solution)/shard_map/pick_states/pallas_call | solution.py:556
  71.3 0.0 all-to-all-done.2
  71.3 5.6 %all-to-all-start.1 = ((bf16[8,512,128]{2,1,0:T(8,128)(2,1)}), bf16[8,512,128]{2,1,0:T(8,128)(2,1)S(1)}, u32[]{:S(2)}, u32[]{:S(2)}) async-start(bf16[8,512,128]{2,1,0:T(8,128)(2,1)} %pick_states.3.refs_18_), calls=%async_computation.1 | async-start | bytes 2097152 | tf_op jit(solution)/shard_map/all_to_all | solution.py:545
  77.0 6.7 %late.2.refs_18_ = bf16[2,256,4096]{2,1,0:T(8,128)(2,1)} custom-call(bf16[2,256,4096]{2,1,0:T(8,128)(2,1)} %refs_0_.7, bf16[2,256,512]{2,1,0:T(8,128)(2,1)} %refs_1_.7, bf16[2,256,512]{2,1,0:T(8,128)(2,1)} %refs_2_.9, f32[1,4096]{1,0:T(1,128)S(1)} %broadcast_in_dim_reshape.3.refs_6_.refs_3_, f32[4,4096]{1,0:T(4,128)} %refs_4_.3, f32[2,4,512]{2,1,0:T(4,128)} %refs_5_.5, ...), custom_call_target="tpu_custom_call" | custom-call | flops 1 | bytes 1 | tf_op jit(solution)/shard_map/late/pallas_call | solution.py:647
  83.6 4.4 %all-to-all-done.1 = bf16[8,512,128]{2,1,0:T(8,128)(2,1)S(1)} async-done(((bf16[8,512,128]{2,1,0:T(8,128)(2,1)}), bf16[8,512,128]{2,1,0:T(8,128)(2,1)S(1)}, u32[]{:S(2)}, u32[]{:S(2)}) %all-to-all-start.1) | async-done | bytes 1048608 | tf_op jit(solution)/shard_map/all_to_all | solution.py:545
  88.0 6.7 %late.3 = bf16[2,256,4096]{2,1,0:T(8,128)(2,1)} custom-call(bf16[2,256,4096]{2,1,0:T(8,128)(2,1)} %refs_0_.7, bf16[2,256,512]{2,1,0:T(8,128)(2,1)} %refs_1_.7, bf16[2,256,512]{2,1,0:T(8,128)(2,1)} %refs_2_.9, f32[1,4096]{1,0:T(1,128)S(1)} %broadcast_in_dim_reshape.3.refs_6_.refs_3_, f32[4,4096]{1,0:T(4,128)} %refs_4_.3, ...), custom_call_target="tpu_custom_call", output_to_operand_aliasing={{}: (18, {})} | custom-call | flops 1 | bytes 1 | tf_op jit(solution)/shard_map/late/pallas_call | solution.py:647
  (2 shorter events, 0.1 us)
Async XLA Ops:
  1.3 15.9 %copy-start.3 = (s32[8]{0:T(128)S(1)}, s32[8]{0:T(128)}, u32[]{:S(2)}) copy-start(s32[8]{0:T(128)} %param.26) | copy-start | bytes 100
  1.3 16.0 %copy-start.4 = (s32[16]{0:T(128)S(1)}, s32[16]{0:T(128)}, u32[]{:S(2)}) copy-start(s32[16]{0:T(128)} %param.27) | copy-start | bytes 196
  1.3 16.1 %copy-start = (f32[64]{0:T(128)S(1)}, f32[64]{0:T(128)}, u32[]{:S(2)}) copy-start(f32[64]{0:T(128)} %param.18) | copy-start | bytes 772
  1.4 16.2 %copy-start.1 = (f32[64]{0:T(128)S(1)}, f32[64]{0:T(128)}, u32[]{:S(2)}) copy-start(f32[64]{0:T(128)} %param.19) | copy-start | bytes 772
  1.4 16.2 %copy-start.2 = (f32[64]{0:T(128)S(1)}, f32[64]{0:T(128)}, u32[]{:S(2)}) copy-start(f32[64]{0:T(128)} %param.20) | copy-start | bytes 772
  4.1 25.3 %all-to-all-start = ((bf16[4,1056,128]{2,1,0:T(8,128)(2,1)}), bf16[4,1056,128]{2,1,0:T(8,128)(2,1)S(1)}, u32[]{:S(2)}, u32[]{:S(2)}) async-start(bf16[4,1056,128]{2,1,0:T(8,128)(2,1)} %cast_states.3.refs_9_), calls=%async_computation | async-start | bytes 2162688 | tf_op jit(solution)/shard_map/all_to_all | solution.py:545
  9.3 28.9 %collective-permute-start.1 = (bf16[544,128]{1,0:T(8,128)(2,1)S(1)}, bf16[544,128]{1,0:T(8,128)(2,1)S(1)}, u32[]{:S(2)}, u32[]{:S(2)}) collective-permute-start(bf16[544,128]{1,0:T(8,128)(2,1)S(1)} %get-tuple-element.17.refs_16_), channel_id=1, source_target_pairs={{0,8},{2,10},{4,12},{6,14},{8,0},{10,2},{12,4},{14,6},{1,9},{3,11}... | collective-permute-start | bytes 417800 | tf_op jit(solution)/shard_map/ppermute | solution.py:460
  11.9 17.5 %collective-permute-start.2 = (bf16[544,128]{1,0:T(8,128)(2,1)S(1)}, bf16[544,128]{1,0:T(8,128)(2,1)S(1)}, u32[]{:S(2)}, u32[]{:S(2)}) collective-permute-start(bf16[544,128]{1,0:T(8,128)(2,1)S(1)} %get-tuple-element.19), channel_id=1, source_target_pairs={{0,10},{2,8},{4,14},{6,12},{8,2},{10,0},{12,6},{14,4},{1,11},{3,9}... | collective-permute-start | bytes 417800 | tf_op jit(solution)/shard_map/ppermute | solution.py:460
  13.7 22.0 %collective-permute-start.3 = (bf16[544,128]{1,0:T(8,128)(2,1)S(1)}, bf16[544,128]{1,0:T(8,128)(2,1)S(1)}, u32[]{:S(2)}, u32[]{:S(2)}) collective-permute-start(bf16[544,128]{1,0:T(8,128)(2,1)S(1)} %get-tuple-element.20), channel_id=1, source_target_pairs={{0,12},{2,14},{4,8},{6,10},{8,4},{10,6},{12,0},{14,2},{1,13},{3,15... | collective-permute-start | bytes 417800 | tf_op jit(solution)/shard_map/ppermute | solution.py:460
  17.2 21.0 %collective-permute-start.4 = (bf16[544,128]{1,0:T(8,128)(2,1)S(1)}, bf16[544,128]{1,0:T(8,128)(2,1)S(1)}, u32[]{:S(2)}, u32[]{:S(2)}) collective-permute-start(bf16[544,128]{1,0:T(8,128)(2,1)S(1)} %get-tuple-element.21), channel_id=1, source_target_pairs={{0,14},{2,12},{4,10},{6,8},{8,6},{10,4},{12,2},{14,0},{1,15},{3,13... | collective-permute-start | bytes 417800 | tf_op jit(solution)/shard_map/ppermute | solution.py:460
  41.8 29.6 %all-to-all-start.2 = ((bf16[8,544,128]{2,1,0:T(8,128)(2,1)}), bf16[8,544,128]{2,1,0:T(8,128)(2,1)S(1)}, u32[]{:S(2)}, u32[]{:S(2)}) async-start(bf16[8,544,128]{2,1,0:T(8,128)(2,1)} %pick_states.2.refs_9_), calls=%async_computation.2 | async-start | bytes 2228224 | tf_op jit(solution)/shard_map/all_to_all | solution.py:545
  45.3 22.5 %collective-permute-start = (bf16[4,512,128]{2,1,0:T(8,128)(2,1)S(1)}, bf16[4,512,128]{2,1,0:T(8,128)(2,1)S(1)}, u32[]{:S(2)}, u32[]{:S(2)}) collective-permute-start(bf16[4,512,128]{2,1,0:T(8,128)(2,1)S(1)} %chunk_b.1.refs_6_), channel_id=1, source_target_pairs={{0,8},{2,10},{4,12},{6,14},{8,0},{10,2},{12,4},{14,6},{1,9},{3,11}... | collective-permute-start | bytes 1572872 | tf_op jit(solution)/shard_map/ppermute | solution.py:460
  71.3 16.7 %all-to-all-start.1 = ((bf16[8,512,128]{2,1,0:T(8,128)(2,1)}), bf16[8,512,128]{2,1,0:T(8,128)(2,1)S(1)}, u32[]{:S(2)}, u32[]{:S(2)}) async-start(bf16[8,512,128]{2,1,0:T(8,128)(2,1)} %pick_states.3.refs_18_), calls=%async_computation.1 | async-start | bytes 2097152 | tf_op jit(solution)/shard_map/all_to_all | solution.py:545

commit v8 on v7

--- a/solution.py
+++ b/solution.py
@@ -68,7 +68,7 @@
     )
     row = total - jnp.log(step)
     columns = total.T
-    column_ref[0] = columns
+    column_ref[0] = total
     causal = lax.broadcasted_iota(jnp.int32, (half, half), 0) >= lax.broadcasted_iota(
         jnp.int32, (half, half), 1
     )
@@ -103,7 +103,7 @@
         ] * x_conv.astype(jnp.float32)
 
 
-def late_kernel(offset, lines, x_ref, b_ref, c_ref, skip_ref, taps_x_ref, taps_bc_ref, *refs):
+def late_kernel(offset, lines, x_ref, b_ref, c_ref, skip_ref, taps_x_ref, taps_bc_ref, tail_ref, *refs):
     y_ref, padded = refs[-2:]
     kids, length, wide = y_ref.shape
     width = 64
@@ -112,17 +112,22 @@
     low = lax.broadcasted_iota(jnp.int32, (length, 2 * width), 1) < width
     low_first = lax.broadcasted_iota(jnp.int32, (FIX, 2 * width), 1) < width
     contract = (((1,), (1,)), ((), ()))
+    q = pl.program_id(0)
+    size = c_ref.shape[2] // pl.num_programs(0)
+    group_lanes = pl.ds(pl.multiple_of(q * size, 128), size)
+    stride = skip_ref.shape[1] // pl.num_programs(0)
     for kid in range(kids):
-        state_ref, tail_ref, held_ref, column_ref, first_ref, mixed_ref = refs[6 * kid : 6 * kid + 6]
-        tail = tail_ref[0, 0].astype(jnp.float32)
+        state_ref, held_ref, column_ref, first_ref, mixed_ref = refs[5 * kid : 5 * kid + 5]
+        tail = tail_ref[q, kid].astype(jnp.float32)
 
         def opening(rows, taps, at):
             tap_rows = [tail[k * lines + at : k * lines + at + 1] for k in range(reach)]
             return conv_silu(padded, jnp.concatenate(tap_rows), rows, taps)
 
-        b_first = opening(b_ref[kid], taps_bc_ref[0], lines - 2)
-        c_first = opening(c_ref[kid], taps_bc_ref[1], lines - 1)
+        b_first = opening(b_ref[kid, :, group_lanes], taps_bc_ref[0, :, group_lanes], lines - 2)
+        c_first = opening(c_ref[kid, :, group_lanes], taps_bc_ref[1, :, group_lanes], lines - 1)
         c_conv = jnp.concatenate([c_first, held_ref[FIX:]])
+        columns = column_ref[q].T
         term = lax.dot_general(
             c_conv, state_ref[0, 0], contract, preferred_element_type=jnp.float32
         )
@@ -135,8 +140,10 @@
         mixing = (scores * first_ref[0]).astype(jnp.bfloat16)
         for pair in range(heads // 2):
             lanes = slice(pair * 2 * width, (pair + 1) * 2 * width)
+            start = pl.multiple_of(q * stride + (offset + 2 * pair) * width, 128)
+            whole = pl.ds(start, 2 * width)
             x_first = opening(
-                x_ref[kid, :, lanes], taps_x_ref[:, lanes], offset * width // 128 + pair
+                x_ref[kid, :, whole], taps_x_ref[:, whole], offset * width // 128 + pair
             ).astype(jnp.float32)
             stacked = [jnp.where(low_first, x_first, 0.0), jnp.where(low_first, 0.0, x_first)]
             if pair > 0:
@@ -149,10 +156,10 @@
                 jnp.concatenate(stacked).astype(jnp.bfloat16),
                 preferred_element_type=jnp.float32,
             )
-            part = jnp.concatenate([part[:FIX] + skip_ref[:, lanes] * x_first, part[FIX:]])
+            part = jnp.concatenate([part[:FIX] + skip_ref[:, whole] * x_first, part[FIX:]])
             head = offset + 2 * pair
             grow = jnp.where(
-                low, column_ref[0, :, head : head + 1], column_ref[0, :, head + 1 : head + 2]
+                low, columns[:, head : head + 1], columns[:, head + 1 : head + 2]
             )
             carried = (term[:, lanes] * jnp.exp(grow)).astype(jnp.bfloat16).astype(jnp.float32)
             y_ref[kid, :, lanes] = (mixed_ref[:, lanes] + part + carried).astype(jnp.bfloat16)
@@ -198,7 +205,8 @@
         pltpu.make_async_copy(held[0], out.at[i], sems.at[i]).wait()
 
 
-def slice_kernel(start, in_ref, out_ref, sem):
+def slice_kernel(start, in_ref, out_ref, tick_ref, sem):
+    tick_ref[...] = jnp.zeros(tick_ref.shape, tick_ref.dtype)
     copy = pltpu.make_async_copy(in_ref.at[:, pl.ds(start, out_ref.shape[1])], out_ref, sem)
     copy.start()
     copy.wait()
@@ -479,7 +487,10 @@
                     pl.BlockSpec((1, reach, wide), lambda i, p, j=j: (0, 0, p[0] ^ j)),
                     pl.BlockSpec((1, reach, 2, size), lambda i, p, j=j: (0, 0, 0, p[0] ^ j)),
                 ]
-        kernel = functools.partial(cast_kernel, len(chunks), tailed, reach, lines)
+        def kernel(*refs):
+            cast_kernel(len(chunks), tailed, reach, lines, *refs[:-1])
+            refs[-1][...] = jnp.zeros(refs[-1].shape, jnp.bfloat16)
+
         return pl.pallas_call(
             functools.partial(
                 drop_tokens, lambda place_ref, *refs: kernel(*refs), 1 + len(operands), len(tokens)
@@ -488,9 +499,10 @@
                 num_scalar_prefetch=1,
                 grid=(1,),
                 in_specs=specs + [anywhere] * len(tokens),
-                out_specs=[pl.BlockSpec((rows, size), lambda i, p: (0, 0))] * len(quarters),
+                out_specs=[pl.BlockSpec(memory_space=pltpu.VMEM)] * (len(quarters) + 1),
             ),
-            out_shape=[jax.ShapeDtypeStruct((rows, size), jnp.bfloat16)] * len(quarters),
+            out_shape=[pltpu.VMEM((rows, size), jnp.bfloat16)] * len(quarters)
+            + [pltpu.VMEM((16, size), jnp.bfloat16)],
             compiler_params=params,
             cost_estimate=small,
             name="cast_states",
@@ -517,8 +529,8 @@
             functools.partial(drop_tokens, kernel, len(operands), len(tokens)),
             grid=(1,),
             in_specs=specs + [anywhere] * len(tokens),
-            out_specs=pl.BlockSpec((groups, rows, size), lambda i: (0, 0, 0)),
-            out_shape=jax.ShapeDtypeStruct((groups, rows, size), jnp.bfloat16),
+            out_specs=pl.BlockSpec(memory_space=pltpu.VMEM),
+            out_shape=pltpu.VMEM((groups, rows, size), jnp.bfloat16),
             compiler_params=params,
             cost_estimate=small,
             name="cast_states",
@@ -533,8 +545,11 @@
             grid=(1,),
             in_specs=[anywhere]
             + [anywhere] * len(tokens),
-            out_specs=pl.BlockSpec((4, rows, size), lambda i: (0, 0, 0)),
-            out_shape=jax.ShapeDtypeStruct((4, rows, size), jnp.bfloat16),
+            out_specs=[pl.BlockSpec(memory_space=pltpu.VMEM)] * 2,
+            out_shape=[
+                pltpu.VMEM((4, rows, size), jnp.bfloat16),
+                pltpu.VMEM((16, size), jnp.bfloat16),
+            ],
             scratch_shapes=[pltpu.SemaphoreType.DMA],
             compiler_params=params,
             cost_estimate=small,
@@ -561,10 +576,10 @@
                 num_scalar_prefetch=1,
                 grid=(1,),
                 in_specs=[anywhere] * (1 + len(crossed) + len(tokens)),
-                out_specs=pl.BlockSpec((spots, rows, size), lambda i, s: (0, 0, 0)),
+                out_specs=pl.BlockSpec(memory_space=pltpu.VMEM),
                 scratch_shapes=[pltpu.SemaphoreType.DMA((spots,))],
             ),
-            out_shape=jax.ShapeDtypeStruct((spots, rows, size), jnp.bfloat16),
+            out_shape=pltpu.VMEM((spots, rows, size), jnp.bfloat16),
             compiler_params=params,
             cost_estimate=small,
             name="pick_states",
@@ -594,13 +609,13 @@
             out_specs=[
                 pl.BlockSpec((length, wide), lambda q: (0, q)),
                 pl.BlockSpec((length, size), lambda q: (0, q)),
-                pl.BlockSpec((1, length, per_group), lambda q: (q, 0, 0)),
+                pl.BlockSpec((1, per_group, length), lambda q: (q, 0, 0)),
                 pl.BlockSpec((1, length, per_group * FIX), lambda q: (q, 0, 0)),
             ],
             out_shape=[
                 pltpu.HBM((length, columns), jnp.float32),
                 pltpu.HBM((length, groups * size), jnp.bfloat16),
-                pltpu.HBM((groups, length, per_group), jnp.float32),
+                pltpu.HBM((groups, per_group, length), jnp.float32),
                 pltpu.HBM((groups, length, per_group * FIX), jnp.float32),
             ],
             scratch_shapes=[pltpu.VMEM((8 + length, size), jnp.float32)],
@@ -616,23 +631,23 @@
         at = lambda q: (0, q * (per_group // part) + unit)
         lane = lambda q: (0, 0, q * (per_group // part) + unit)
         tail_at = SPLIT[0] * width // tail_lines
-        operands = [x_in, b_in, c_in, skip_row, conv_x, conv_bc]
+        operands = [x_in, b_in, c_in, skip_row, conv_x, conv_bc, states_first]
         specs = [
-            pl.BlockSpec((kids, FIX, chunk), lane),
-            pl.BlockSpec((kids, FIX, size), lambda q: (0, 0, q)),
-            pl.BlockSpec((kids, FIX, size), lambda q: (0, 0, q)),
-            pl.BlockSpec((1, chunk), at),
-            pl.BlockSpec((taps, chunk), at),
-            pl.BlockSpec((2, taps, size), lambda q: (0, 0, q)),
+            pl.BlockSpec((kids, FIX, columns), lambda q: (0, 0, 0)),
+            pl.BlockSpec((kids, FIX, groups * size), lambda q: (0, 0, 0)),
+            pl.BlockSpec((kids, FIX, groups * size), lambda q: (0, 0, 0)),
+            pl.BlockSpec((1, columns), lambda q: (0, 0)),
+            pl.BlockSpec((taps, columns), lambda q: (0, 0)),
+            pl.BlockSpec((2, taps, groups * size), lambda q: (0, 0, 0)),
+            pl.BlockSpec((groups, kids, tail_lines, size), lambda q: (0, 0, tail_at, 0)),
         ]
         for c in range(kids):
             mixed, held, column, first = map(stay, parts[c])
-            operands += [states, states_first, held, column, first, mixed]
+            operands += [states, held, column, first, mixed]
             specs += [
                 pl.BlockSpec((1, 1, chunk, size), lambda q, c=c: (q, c, 0, 0)),
-                pl.BlockSpec((1, 1, tail_lines, size), lambda q, c=c: (q, c, tail_at, 0)),
                 pl.BlockSpec((length, size), lambda q: (0, q)),
-                pl.BlockSpec((1, length, per_group), lambda q: (q, 0, 0)),
+                pl.BlockSpec((groups, per_group, length), lambda q: (0, 0, 0)),
                 pl.BlockSpec((1, length, part * FIX), lambda q: (q, 0, unit)),
                 pl.BlockSpec((length, chunk), at),
             ]
@@ -666,13 +681,14 @@
     rows = [SPLIT[0] * width + tail_lines, SPLIT[1] * width]
     quarters = [0, 1, 2, 3]
     sent_a = cast(quarters, [0], [])
+    *sent_a, tick = sent_a
     crossed_a = [swap(sent_a[j], j + 4) for j in quarters]
-    whole = cast_whole([sent_a[0]])
+    whole = cast_whole([swap(tick, 1)])
     inside = gather_half(whole)
     parts = [early(0, [whole])]
-    sent_b = chunk_b(inside, [stay(parts[0][1])])
+    sent_b, tick = chunk_b(inside, [stay(parts[0][1])])
     crossed_b = swap(sent_b, 4)
-    picked_a, states_a = pick(rows[0], 0, slots_a, inside, crossed_a, [sent_b])
+    picked_a, states_a = pick(rows[0], 0, slots_a, inside, crossed_a, [swap(tick, 1)])
     parts.append(early(1, [picked_a]))
     picked_b, states_b = pick(rows[1], rows[0], slots_b, inside, [crossed_b], [stay(parts[1][1])])
     result = late(0, states_a, states_a, parts, None, [picked_b])

time: 95.3 us -> 94.8 us (level)
  waiting for transfers between devices: 22.3 us -> 19.4 us
  starting transfers between devices: 24.2 us -> 26.8 us
    ppermute x5 -> x7, starting transfers between devices: 9.83 us -> 15.4 us  [swap(): return lax.ppermute(value, 'batch', perm=[(i, i ^ r) for i in range(8)])]
    all_to_all x3, starting transfers between devices: 14.4 us -> 11.4 us  [gather_half(): lax.all_to_all(value, 'batch', split_axis=0, concat_axis=0, tiled=True, a...]
    all_to_all x3, waiting for transfers between devices: 4.42 us -> 2.72 us  [gather_half(): lax.all_to_all(value, 'batch', split_axis=0, concat_axis=0, tiled=True, a...]
    ppermute x5 -> x7, waiting for transfers between devices: 17.9 us -> 16.7 us  [swap(): return lax.ppermute(value, 'batch', perm=[(i, i ^ r) for i in range(8)])]
  transfers between devices with their start and end apart: 8 -> 10, of which waited for: 4 -> 5; matrix products, arithmetic and copies ran while one was open for 1% -> 1% of each run, Pallas kernels for 35% -> 35%
where the time goes in v8:
time: 94.8 us; the launch traced here: 94.2 us
  Pallas kernels  47.2 us (50%)
  starting transfers between devices  26.8 us (28%)
  waiting for transfers between devices  19.4 us (20%)
    pallas_call x2, Pallas kernels, early(): pl.pallas_call(functools.partial(drop_tokens, early_kernel, len(operands)...  22.7 us
    ppermute x7, waiting for transfers between devices, swap(): return lax.ppermute(value, 'batch', perm=[(i, i ^ r) for i in range(8)])  16.7 us
    ppermute x7, starting transfers between devices, swap(): return lax.ppermute(value, 'batch', perm=[(i, i ^ r) for i in range(8)])  15.4 us
    pallas_call x2, Pallas kernels, late(): pl.pallas_call(functools.partial(drop_tokens, functools.partial(late_kern...  13.3 us
    all_to_all x3, starting transfers between devices, gather_half(): lax.all_to_all(value, 'batch', split_axis=0, concat_axis=0, tiled=True, a...  11.4 us
    pallas_call x2, Pallas kernels, pick(): pl.pallas_call(functools.partial(drop_tokens, functools.partial(pick_rows...  7.03 us
    all_to_all x3, waiting for transfers between devices, gather_half(): lax.all_to_all(value, 'batch', split_axis=0, concat_axis=0, tiled=True, a...  2.72 us
    pallas_call x1, Pallas kernels, cast_whole(): pl.pallas_call(functools.partial(drop_tokens, kernel, len(operands), len(...  2.68 us
  transfers between devices with their start and end apart: 10, of which 5 were waited for; matrix products, arithmetic and copies ran while one was open for 1% of the time, Pallas kernels for 35%

profile of v8, /device:TPU:0, one launch (start us, length us, event | category | flops | bytes accessed | tf_op | source)
XLA Modules:
  0.0 94.2 jit_solution(16714673568193115449)
XLA Ops:
  0.0 1.3 %cast_states.2 = (bf16[544,128]{1,0:T(8,128)(2,1)S(1)}, bf16[544,128]{1,0:T(8,128)(2,1)S(1)}, bf16[544,128]{1,0:T(8,128)(2,1)S(1)}, bf16[544,128]{1,0:T(8,128)(2,1)S(1)}, bf16[16,128]{1,0:T(8,128)(2,1)S(1)}) custom-call(s32[1]{0:T(128)} %bitcast.2.refs_0_, f32[4,16,64,128]{3,2,1,0:T(8,128)} %bitcast.13, f32[4,16,64,128]{3,2,1,0:T(8,128)} %bitcast.14, ...), custom_call_target="tpu_custom_call" | custom-call | flops 1 | bytes 1 | tf_op jit(solution)/shard_map/cast_states/pallas_call | solution.py:494
  1.3 0.0 copy-start
  1.3 0.0 copy-start.1
  1.4 0.0 copy-start.2
  1.4 0.0 copy-start.3
  1.4 0.0 copy-start.4
  1.4 3.0 %collective-permute-start = (bf16[16,128]{1,0:T(8,128)(2,1)S(1)}, bf16[16,128]{1,0:T(8,128)(2,1)S(1)}, u32[]{:S(2)}, u32[]{:S(2)}) collective-permute-start(bf16[16,128]{1,0:T(8,128)(2,1)S(1)} %get-tuple-element.20), channel_id=1, source_target_pairs={{0,2},{2,0},{4,6},{6,4},{8,10},{10,8},{12,14},{14,12},{1,3},{3,1},... | collective-permute-start | bytes 12296 | tf_op jit(solution)/shard_map/ppermute | solution.py:468
  4.4 1.6 %collective-permute-done.refs_16_ = bf16[16,128]{1,0:T(8,128)(2,1)S(1)} collective-permute-done((bf16[16,128]{1,0:T(8,128)(2,1)S(1)}, bf16[16,128]{1,0:T(8,128)(2,1)S(1)}, u32[]{:S(2)}, u32[]{:S(2)}) %collective-permute-start) | collective-permute-done | bytes 4128 | tf_op jit(solution)/shard_map/ppermute | solution.py:468
  6.0 2.7 %cast_states.3.refs_9_ = bf16[4,1056,128]{2,1,0:T(8,128)(2,1)} custom-call(f32[4,16,64,128]{3,2,1,0:T(8,128)} %bitcast.17, f32[4,16,64,128]{3,2,1,0:T(8,128)} %bitcast.18, bf16[1,3,4096]{2,1,0:T(4,128)(2,1)} %refs_14_.1, bf16[1,3,2,512]{3,2,1,0:T(2,128)(2,1)} %bitcast.29, f32[4,16,64,128]{3,2,1,0:T(8,128)} %bitcast.19, f32[4,16,64,128]{3,2,1,0:T(8,128)} %bitcast.20, ...), custom_call_target="tpu_custom_call" | custom-call | flops 1 | bytes 1 | tf_op jit(solution)/shard_map/cast_states/pallas_call | solution.py:528
  8.7 4.3 %all-to-all-start = ((bf16[4,1056,128]{2,1,0:T(8,128)(2,1)}), bf16[4,1056,128]{2,1,0:T(8,128)(2,1)S(1)}, u32[]{:S(2)}, u32[]{:S(2)}) async-start(bf16[4,1056,128]{2,1,0:T(8,128)(2,1)} %cast_states.3.refs_9_), calls=%async_computation | async-start | bytes 2162688 | tf_op jit(solution)/shard_map/all_to_all | solution.py:560
  13.0 2.6 %collective-permute-start.1 = (bf16[544,128]{1,0:T(8,128)(2,1)S(1)}, bf16[544,128]{1,0:T(8,128)(2,1)S(1)}, u32[]{:S(2)}, u32[]{:S(2)}) collective-permute-start(bf16[544,128]{1,0:T(8,128)(2,1)S(1)} %get-tuple-element.21), channel_id=1, source_target_pairs={{0,8},{2,10},{4,12},{6,14},{8,0},{10,2},{12,4},{14,6},{1,9},{3,11}... | collective-permute-start | bytes 417800 | tf_op jit(solution)/shard_map/ppermute | solution.py:468
  15.6 1.8 %collective-permute-start.2 = (bf16[544,128]{1,0:T(8,128)(2,1)S(1)}, bf16[544,128]{1,0:T(8,128)(2,1)S(1)}, u32[]{:S(2)}, u32[]{:S(2)}) collective-permute-start(bf16[544,128]{1,0:T(8,128)(2,1)S(1)} %get-tuple-element.22), channel_id=1, source_target_pairs={{0,10},{2,8},{4,14},{6,12},{8,2},{10,0},{12,6},{14,4},{1,11},{3,9}... | collective-permute-start | bytes 417800 | tf_op jit(solution)/shard_map/ppermute | solution.py:468
  17.4 3.5 %collective-permute-start.3 = (bf16[544,128]{1,0:T(8,128)(2,1)S(1)}, bf16[544,128]{1,0:T(8,128)(2,1)S(1)}, u32[]{:S(2)}, u32[]{:S(2)}) collective-permute-start(bf16[544,128]{1,0:T(8,128)(2,1)S(1)} %get-tuple-element.23), channel_id=1, source_target_pairs={{0,12},{2,14},{4,8},{6,10},{8,4},{10,6},{12,0},{14,2},{1,13},{3,15... | collective-permute-start | bytes 417800 | tf_op jit(solution)/shard_map/ppermute | solution.py:468
  20.9 0.0 collective-permute-start.4
  20.9 0.0 copy-done
  20.9 0.1 copy.20.refs_4_
  21.0 0.0 copy-done.1
  21.0 0.1 copy.21.refs_5_
  21.1 0.0 copy-done.2
  21.1 0.1 broadcast_in_dim.31
  21.1 0.1 broadcast_in_dim_reshape.3.refs_6_.refs_3_
  21.2 0.0 copy-done.3
  21.3 0.1 select_reduce_fusion
  21.4 0.0 copy-done.4
  21.4 0.1 convert_reduce_fusion
  21.5 0.1 compare_select_fusion.5
  21.5 11.4 %early.2 = (f32[256,4096]{1,0:T(8,128)}, bf16[256,512]{1,0:T(8,128)(2,1)}, f32[4,16,256]{2,1,0:T(8,128)}, f32[4,256,256]{2,1,0:T(8,128)}) custom-call(bf16[2,256,4096]{2,1,0:T(8,128)(2,1)} %refs_0_.7, bf16[2,256,512]{2,1,0:T(8,128)(2,1)} %refs_1_.7, bf16[2,256,512]{2,1,0:T(8,128)(2,1)} %refs_2_.9, f32[2,64,256]{2,1,0:T(8,128)} %refs_3_.3, ...), custom_call_target="tpu_custom_call" | custom-call | flops 1 | bytes 1 | tf_op jit(solution)/shard_map/early/pallas_call | solution.py:594
  32.9 0.0 all-to-all-done.refs_0_.refs_1_
  33.0 1.9 %collective-permute-start.5 = (bf16[16,128]{1,0:T(8,128)(2,1)S(1)}, bf16[16,128]{1,0:T(8,128)(2,1)S(1)}, u32[]{:S(2)}, u32[]{:S(2)}) collective-permute-start(bf16[16,128]{1,0:T(8,128)(2,1)S(1)} %get-tuple-element.26), channel_id=1, source_target_pairs={{0,2},{2,0},{4,6},{6,4},{8,10},{10,8},{12,14},{14,12},{1,3},{3,1},... | collective-permute-start | bytes 12296 | tf_op jit(solution)/shard_map/ppermute | solution.py:468
  34.9 0.1 compare_select_fusion.6.refs_0_
  34.9 0.0 collective-permute-done.1.refs_2_
  34.9 0.0 collective-permute-done.2.refs_3_
  35.0 3.4 %collective-permute-done.3.refs_4_ = bf16[544,128]{1,0:T(8,128)(2,1)S(1)} collective-permute-done((bf16[544,128]{1,0:T(8,128)(2,1)S(1)}, bf16[544,128]{1,0:T(8,128)(2,1)S(1)}, u32[]{:S(2)}, u32[]{:S(2)}) %collective-permute-start.3) | collective-permute-done | bytes 139296 | tf_op jit(solution)/shard_map/ppermute | solution.py:468
  38.4 2.3 %collective-permute-done.4.refs_5_ = bf16[544,128]{1,0:T(8,128)(2,1)S(1)} collective-permute-done((bf16[544,128]{1,0:T(8,128)(2,1)S(1)}, bf16[544,128]{1,0:T(8,128)(2,1)S(1)}, u32[]{:S(2)}, u32[]{:S(2)}) %collective-permute-start.4) | collective-permute-done | bytes 139296 | tf_op jit(solution)/shard_map/ppermute | solution.py:468
  40.7 0.0 collective-permute-done.5.refs_6_
  40.7 3.6 %pick_states.2.refs_9_ = bf16[8,544,128]{2,1,0:T(8,128)(2,1)} custom-call(s32[8]{0:T(128)S(1)} %compare_select_fusion.6.refs_0_, bf16[4,1056,128]{2,1,0:T(8,128)(2,1)S(1)} %all-to-all-done.refs_0_.refs_1_, bf16[544,128]{1,0:T(8,128)(2,1)S(1)} %collective-permute-done.1.refs_2_, bf16[544,128]{1,0:T(8,128)(2,1)S(1)} %collective-permute-done.2.refs_3_, ...), custom_call_target="tpu_custom_call" | custom-call | flops 1 | bytes 1 | tf_op jit(solution)/shard_map/pick_states/pallas_call | solution.py:571
  44.3 3.5 %all-to-all-start.1 = ((bf16[8,544,128]{2,1,0:T(8,128)(2,1)}), bf16[8,544,128]{2,1,0:T(8,128)(2,1)S(1)}, u32[]{:S(2)}, u32[]{:S(2)}) async-start(bf16[8,544,128]{2,1,0:T(8,128)(2,1)} %pick_states.2.refs_9_), calls=%async_computation.1 | async-start | bytes 2228224 | tf_op jit(solution)/shard_map/all_to_all | solution.py:560
  47.8 2.6 %collective-permute-start.6 = (bf16[4,512,128]{2,1,0:T(8,128)(2,1)S(1)}, bf16[4,512,128]{2,1,0:T(8,128)(2,1)S(1)}, u32[]{:S(2)}, u32[]{:S(2)}) collective-permute-start(bf16[4,512,128]{2,1,0:T(8,128)(2,1)S(1)} %get-tuple-element.27), channel_id=1, source_target_pairs={{0,8},{2,10},{4,12},{6,14},{8,0},{10,2},{12,4},{14,6},{1,9},{3,11}... | collective-permute-start | bytes 1572872 | tf_op jit(solution)/shard_map/ppermute | solution.py:468
  50.4 11.4 %early.3 = (f32[256,4096]{1,0:T(8,128)}, bf16[256,512]{1,0:T(8,128)(2,1)}, f32[4,16,256]{2,1,0:T(8,128)}, f32[4,256,256]{2,1,0:T(8,128)}) custom-call(bf16[2,256,4096]{2,1,0:T(8,128)(2,1)} %refs_0_.7, bf16[2,256,512]{2,1,0:T(8,128)(2,1)} %refs_1_.7, bf16[2,256,512]{2,1,0:T(8,128)(2,1)} %refs_2_.9, f32[2,64,256]{2,1,0:T(8,128)} %refs_3_.3, ...), custom_call_target="tpu_custom_call" | custom-call | flops 1 | bytes 1 | tf_op jit(solution)/shard_map/early/pallas_call | solution.py:594
  61.8 9.3 %collective-permute-done.6.refs_2_ = bf16[4,512,128]{2,1,0:T(8,128)(2,1)S(1)} collective-permute-done((bf16[4,512,128]{2,1,0:T(8,128)(2,1)S(1)}, bf16[4,512,128]{2,1,0:T(8,128)(2,1)S(1)}, u32[]{:S(2)}, u32[]{:S(2)}) %collective-permute-start.6) | collective-permute-done | bytes 524320 | tf_op jit(solution)/shard_map/ppermute | solution.py:468
  71.2 3.5 %pick_states.3.refs_17_ = bf16[8,512,128]{2,1,0:T(8,128)(2,1)} custom-call(s32[8]{0:T(128)S(1)} %get-tuple-element.35.refs_0_, bf16[4,1056,128]{2,1,0:T(8,128)(2,1)S(1)} %all-to-all-done.refs_0_.refs_1_, bf16[4,512,128]{2,1,0:T(8,128)(2,1)S(1)} %collective-permute-done.6.refs_2_, bf16[256,512]{1,0:T(8,128)(2,1)} %get-tuple-element.28.refs_3_.refs_13_), custom_call_target="tpu_custom_call" | custom-call | flops 1 | bytes 1 | tf_op jit(solution)/shard_map/pick_states/pallas_call | solution.py:571
  74.6 0.0 all-to-all-done.1
  74.6 3.5 %all-to-all-start.2 = ((bf16[8,512,128]{2,1,0:T(8,128)(2,1)}), bf16[8,512,128]{2,1,0:T(8,128)(2,1)S(1)}, u32[]{:S(2)}, u32[]{:S(2)}) async-start(bf16[8,512,128]{2,1,0:T(8,128)(2,1)} %pick_states.3.refs_17_), calls=%async_computation.2 | async-start | bytes 2097152 | tf_op jit(solution)/shard_map/all_to_all | solution.py:560
  78.2 6.7 %late.2.refs_17_ = bf16[2,256,4096]{2,1,0:T(8,128)(2,1)} custom-call(bf16[2,256,4096]{2,1,0:T(8,128)(2,1)} %refs_0_.7, bf16[2,256,512]{2,1,0:T(8,128)(2,1)} %refs_1_.7, bf16[2,256,512]{2,1,0:T(8,128)(2,1)} %refs_2_.9, f32[1,4096]{1,0:T(1,128)S(1)} %broadcast_in_dim_reshape.3.refs_6_.refs_3_, f32[4,4096]{1,0:T(4,128)} %refs_4_.3, f32[2,4,512]{2,1,0:T(4,128)} %refs_5_.5, ...), custom_call_target="tpu_custom_call" | custom-call | flops 1 | bytes 1 | tf_op jit(solution)/shard_map/late/pallas_call | solution.py:662
  84.9 2.7 %all-to-all-done.2 = bf16[8,512,128]{2,1,0:T(8,128)(2,1)S(1)} async-done(((bf16[8,512,128]{2,1,0:T(8,128)(2,1)}), bf16[8,512,128]{2,1,0:T(8,128)(2,1)S(1)}, u32[]{:S(2)}, u32[]{:S(2)}) %all-to-all-start.2) | async-done | bytes 1048608 | tf_op jit(solution)/shard_map/all_to_all | solution.py:560
  87.6 6.7 %late.3 = bf16[2,256,4096]{2,1,0:T(8,128)(2,1)} custom-call(bf16[2,256,4096]{2,1,0:T(8,128)(2,1)} %refs_0_.7, bf16[2,256,512]{2,1,0:T(8,128)(2,1)} %refs_1_.7, bf16[2,256,512]{2,1,0:T(8,128)(2,1)} %refs_2_.9, f32[1,4096]{1,0:T(1,128)S(1)} %broadcast_in_dim_reshape.3.refs_6_.refs_3_, f32[4,4096]{1,0:T(4,128)} %refs_4_.3, ...), custom_call_target="tpu_custom_call", output_to_operand_aliasing={{}: (17, {})} | custom-call | flops 1 | bytes 1 | tf_op jit(solution)/shard_map/late/pallas_call | solution.py:662
  (1 shorter events, 0.0 us)
Async XLA Ops:
  1.3 19.5 %copy-start = (f32[64]{0:T(128)S(1)}, f32[64]{0:T(128)}, u32[]{:S(2)}) copy-start(f32[64]{0:T(128)} %param.18) | copy-start | bytes 772
  1.3 19.6 %copy-start.1 = (f32[64]{0:T(128)S(1)}, f32[64]{0:T(128)}, u32[]{:S(2)}) copy-start(f32[64]{0:T(128)} %param.19) | copy-start | bytes 772
  1.4 19.7 %copy-start.2 = (f32[64]{0:T(128)S(1)}, f32[64]{0:T(128)}, u32[]{:S(2)}) copy-start(f32[64]{0:T(128)} %param.20) | copy-start | bytes 772
  1.4 19.9 %copy-start.3 = (s32[8]{0:T(128)S(1)}, s32[8]{0:T(128)}, u32[]{:S(2)}) copy-start(s32[8]{0:T(128)} %param.26) | copy-start | bytes 100
  1.4 20.0 %copy-start.4 = (s32[16]{0:T(128)S(1)}, s32[16]{0:T(128)}, u32[]{:S(2)}) copy-start(s32[16]{0:T(128)} %param.27) | copy-start | bytes 196
  1.4 4.6 %collective-permute-start = (bf16[16,128]{1,0:T(8,128)(2,1)S(1)}, bf16[16,128]{1,0:T(8,128)(2,1)S(1)}, u32[]{:S(2)}, u32[]{:S(2)}) collective-permute-start(bf16[16,128]{1,0:T(8,128)(2,1)S(1)} %get-tuple-element.20), channel_id=1, source_target_pairs={{0,2},{2,0},{4,6},{6,4},{8,10},{10,8},{12,14},{14,12},{1,3},{3,1},... | collective-permute-start | bytes 12296 | tf_op jit(solution)/shard_map/ppermute | solution.py:468
  8.7 24.2 %all-to-all-start = ((bf16[4,1056,128]{2,1,0:T(8,128)(2,1)}), bf16[4,1056,128]{2,1,0:T(8,128)(2,1)S(1)}, u32[]{:S(2)}, u32[]{:S(2)}) async-start(bf16[4,1056,128]{2,1,0:T(8,128)(2,1)} %cast_states.3.refs_9_), calls=%async_computation | async-start | bytes 2162688 | tf_op jit(solution)/shard_map/all_to_all | solution.py:560
  13.0 22.0 %collective-permute-start.1 = (bf16[544,128]{1,0:T(8,128)(2,1)S(1)}, bf16[544,128]{1,0:T(8,128)(2,1)S(1)}, u32[]{:S(2)}, u32[]{:S(2)}) collective-permute-start(bf16[544,128]{1,0:T(8,128)(2,1)S(1)} %get-tuple-element.21), channel_id=1, source_target_pairs={{0,8},{2,10},{4,12},{6,14},{8,0},{10,2},{12,4},{14,6},{1,9},{3,11}... | collective-permute-start | bytes 417800 | tf_op jit(solution)/shard_map/ppermute | solution.py:468
  15.6 19.4 %collective-permute-start.2 = (bf16[544,128]{1,0:T(8,128)(2,1)S(1)}, bf16[544,128]{1,0:T(8,128)(2,1)S(1)}, u32[]{:S(2)}, u32[]{:S(2)}) collective-permute-start(bf16[544,128]{1,0:T(8,128)(2,1)S(1)} %get-tuple-element.22), channel_id=1, source_target_pairs={{0,10},{2,8},{4,14},{6,12},{8,2},{10,0},{12,6},{14,4},{1,11},{3,9}... | collective-permute-start | bytes 417800 | tf_op jit(solution)/shard_map/ppermute | solution.py:468
  17.4 21.0 %collective-permute-start.3 = (bf16[544,128]{1,0:T(8,128)(2,1)S(1)}, bf16[544,128]{1,0:T(8,128)(2,1)S(1)}, u32[]{:S(2)}, u32[]{:S(2)}) collective-permute-start(bf16[544,128]{1,0:T(8,128)(2,1)S(1)} %get-tuple-element.23), channel_id=1, source_target_pairs={{0,12},{2,14},{4,8},{6,10},{8,4},{10,6},{12,0},{14,2},{1,13},{3,15... | collective-permute-start | bytes 417800 | tf_op jit(solution)/shard_map/ppermute | solution.py:468
  20.9 19.8 %collective-permute-start.4 = (bf16[544,128]{1,0:T(8,128)(2,1)S(1)}, bf16[544,128]{1,0:T(8,128)(2,1)S(1)}, u32[]{:S(2)}, u32[]{:S(2)}) collective-permute-start(bf16[544,128]{1,0:T(8,128)(2,1)S(1)} %get-tuple-element.24), channel_id=1, source_target_pairs={{0,14},{2,12},{4,10},{6,8},{8,6},{10,4},{12,2},{14,0},{1,15},{3,13... | collective-permute-start | bytes 417800 | tf_op jit(solution)/shard_map/ppermute | solution.py:468
  33.0 7.7 %collective-permute-start.5 = (bf16[16,128]{1,0:T(8,128)(2,1)S(1)}, bf16[16,128]{1,0:T(8,128)(2,1)S(1)}, u32[]{:S(2)}, u32[]{:S(2)}) collective-permute-start(bf16[16,128]{1,0:T(8,128)(2,1)S(1)} %get-tuple-element.26), channel_id=1, source_target_pairs={{0,2},{2,0},{4,6},{6,4},{8,10},{10,8},{12,14},{14,12},{1,3},{3,1},... | collective-permute-start | bytes 12296 | tf_op jit(solution)/shard_map/ppermute | solution.py:468
  44.3 30.4 %all-to-all-start.1 = ((bf16[8,544,128]{2,1,0:T(8,128)(2,1)}), bf16[8,544,128]{2,1,0:T(8,128)(2,1)S(1)}, u32[]{:S(2)}, u32[]{:S(2)}) async-start(bf16[8,544,128]{2,1,0:T(8,128)(2,1)} %pick_states.2.refs_9_), calls=%async_computation.1 | async-start | bytes 2228224 | tf_op jit(solution)/shard_map/all_to_all | solution.py:560
  47.8 23.4 %collective-permute-start.6 = (bf16[4,512,128]{2,1,0:T(8,128)(2,1)S(1)}, bf16[4,512,128]{2,1,0:T(8,128)(2,1)S(1)}, u32[]{:S(2)}, u32[]{:S(2)}) collective-permute-start(bf16[4,512,128]{2,1,0:T(8,128)(2,1)S(1)} %get-tuple-element.27), channel_id=1, source_target_pairs={{0,8},{2,10},{4,12},{6,14},{8,0},{10,2},{12,4},{14,6},{1,9},{3,11}... | collective-permute-start | bytes 1572872 | tf_op jit(solution)/shard_map/ppermute | solution.py:468
  74.6 12.9 %all-to-all-start.2 = ((bf16[8,512,128]{2,1,0:T(8,128)(2,1)}), bf16[8,512,128]{2,1,0:T(8,128)(2,1)S(1)}, u32[]{:S(2)}, u32[]{:S(2)}) async-start(bf16[8,512,128]{2,1,0:T(8,128)(2,1)} %pick_states.3.refs_17_), calls=%async_computation.2 | async-start | bytes 2097152 | tf_op jit(solution)/shard_map/all_to_all | solution.py:560

commit v9 on v7

--- a/solution.py
+++ b/solution.py
@@ -7,9 +7,10 @@
 from jax.experimental.pallas import tpu as pltpu
 from jax.sharding import PartitionSpec as P
 
-VMEM_LIMIT = 10 * 1024 * 1024
+VMEM_LIMIT = 16 * 1024 * 1024
 SPLIT = (8, 8)
 FIX = 16
+LOG2_E = 1.4426950408889634
 
 
 def drop_tokens(kernel, keep, tokens, *refs):
@@ -38,8 +39,9 @@
     x_ref, b_ref, c_ref, dt_ref, bias_ref, alog_ref, skip_ref, taps_x_ref, taps_bc_ref,
     mixed_ref, c_out_ref, column_ref, first_ref, padded,
 ):
-    length, wide = mixed_ref.shape
+    length, wide = x_ref.shape[1:]
     heads = dt_ref.shape[1]
+    q = pl.program_id(0)
     width = wide // heads
     half = length // 2
 
@@ -49,7 +51,7 @@
 
     b_conv = convolve(b_ref[0], taps_bc_ref[0])
     c_conv = convolve(c_ref[0], taps_bc_ref[1])
-    c_out_ref[...] = c_conv
+    c_out_ref[q] = c_conv
     scores = lax.dot_general(
         c_conv, b_conv, (((1,), (1,)), ((), ())), preferred_element_type=jnp.float32
     )
@@ -66,9 +68,10 @@
         precision=lax.Precision.HIGHEST,
         preferred_element_type=jnp.float32,
     )
-    row = total - jnp.log(step)
+    total = total * LOG2_E
+    row = total - jnp.log(step) * LOG2_E
     columns = total.T
-    column_ref[0] = columns
+    column_ref[q] = total
     causal = lax.broadcasted_iota(jnp.int32, (half, half), 0) >= lax.broadcasted_iota(
         jnp.int32, (half, half), 1
     )
@@ -80,12 +83,12 @@
         for head in (2 * pair, 2 * pair + 1):
             column = jnp.broadcast_to(columns[:, head : head + 1], (length, half))
             rows = row[head : head + 1, :]
-            near = jnp.exp(jnp.where(causal, column[:half] - rows[:, :half], -1e30))
-            far = jnp.exp(column[half:] - rows[:, :half])
-            last = jnp.exp(jnp.where(causal, column[half:] - rows[:, half:], -1e30))
+            near = jnp.exp2(jnp.where(causal, column[:half] - rows[:, :half], -1e30))
+            far = jnp.exp2(column[half:] - rows[:, :half])
+            last = jnp.exp2(jnp.where(causal, column[half:] - rows[:, half:], -1e30))
             spot = slice(head * FIX, (head + 1) * FIX)
-            first_ref[0, :half, spot] = near[:, :FIX]
-            first_ref[0, half:, spot] = far[:, :FIX]
+            first_ref[q, :half, spot] = near[:, :FIX]
+            first_ref[q, half:, spot] = far[:, :FIX]
             top = (scores[:half, :half] * near).astype(jnp.bfloat16)
             left = (scores[half:, :half] * far).astype(jnp.bfloat16)
             right = (scores[half:, half:] * last).astype(jnp.bfloat16)
@@ -98,45 +101,69 @@
                     ]
                 )
             )
-        mixed_ref[:, lanes] = jnp.where(low, parts[0], parts[1]) + skip_ref[
+        mixed_ref[q, :, lanes] = jnp.where(low, parts[0], parts[1]) + skip_ref[
             :, lanes
         ] * x_conv.astype(jnp.float32)
 
 
-def late_kernel(offset, lines, x_ref, b_ref, c_ref, skip_ref, taps_x_ref, taps_bc_ref, *refs):
-    y_ref, padded = refs[-2:]
+def late_kernel(
+    offset, lines, place_ref, x_ref, b_ref, c_ref, skip_ref, taps_x_ref, taps_bc_ref, *refs
+):
+    tails, states, parts, (y_ref, padded) = refs[:4], refs[4:8], refs[8:-2], refs[-2:]
     kids, length, wide = y_ref.shape
     width = 64
     heads = wide // width
     reach = taps_x_ref.shape[0] - 1
-    low = lax.broadcasted_iota(jnp.int32, (length, 2 * width), 1) < width
+    q = pl.program_id(0)
+    far = q ^ place_ref[0]
+    size = c_ref.shape[2] // pl.num_programs(0)
+    stride = skip_ref.shape[1] // pl.num_programs(0)
+    group_lanes = pl.ds(pl.multiple_of(q * size, 128), size)
     low_first = lax.broadcasted_iota(jnp.int32, (FIX, 2 * width), 1) < width
+    spread_row = lax.broadcasted_iota(jnp.int32, (4 * heads, wide), 0)
+    spread_lane = lax.broadcasted_iota(jnp.int32, (4 * heads, wide), 1)
+    spread = (spread_row % heads == spread_lane // width).astype(jnp.bfloat16)
     contract = (((1,), (1,)), ((), ()))
+
+    def choose(blocks):
+        near = jnp.where(far == 0, blocks[0], blocks[1])
+        return jnp.where(far <= 1, near, jnp.where(far == 2, blocks[2], blocks[3]))
+
     for kid in range(kids):
-        state_ref, tail_ref, held_ref, column_ref, first_ref, mixed_ref = refs[6 * kid : 6 * kid + 6]
-        tail = tail_ref[0, 0].astype(jnp.float32)
+        held_ref, column_ref, first_ref, mixed_ref = parts[4 * kid : 4 * kid + 4]
+        tail = choose([ref[kid] for ref in tails]).astype(jnp.float32)
+        state = choose([ref[kid] for ref in states])
 
         def opening(rows, taps, at):
             tap_rows = [tail[k * lines + at : k * lines + at + 1] for k in range(reach)]
             return conv_silu(padded, jnp.concatenate(tap_rows), rows, taps)
 
-        b_first = opening(b_ref[kid], taps_bc_ref[0], lines - 2)
-        c_first = opening(c_ref[kid], taps_bc_ref[1], lines - 1)
-        c_conv = jnp.concatenate([c_first, held_ref[FIX:]])
-        term = lax.dot_general(
-            c_conv, state_ref[0, 0], contract, preferred_element_type=jnp.float32
-        )
+        b_first = opening(b_ref[kid, :, group_lanes], taps_bc_ref[0, :, group_lanes], lines - 2)
+        c_first = opening(c_ref[kid, :, group_lanes], taps_bc_ref[1, :, group_lanes], lines - 1)
+        c_conv = jnp.concatenate([c_first, held_ref[q, FIX:]])
+        grow = jnp.exp2(column_ref[q, offset : offset + heads, :])
+        terms = []
+        for _ in range(3):
+            terms.append(grow.astype(jnp.bfloat16).astype(jnp.float32))
+            grow = grow - terms[-1]
+        terms = jnp.concatenate(terms + [jnp.zeros_like(grow)]).T.astype(jnp.bfloat16)
+        grow = jnp.dot(terms, spread, preferred_element_type=jnp.float32)
+        term = lax.dot_general(c_conv, state, contract, preferred_element_type=jnp.float32)
+        carried = (term * grow).astype(jnp.bfloat16)
         scores = lax.dot_general(
             c_conv,
             jnp.concatenate([b_first] * heads),
             contract,
             preferred_element_type=jnp.float32,
         )
-        mixing = (scores * first_ref[0]).astype(jnp.bfloat16)
+        unit = offset // heads * heads * FIX
+        mixing = (scores * first_ref[q, :, unit : unit + heads * FIX]).astype(jnp.bfloat16)
         for pair in range(heads // 2):
             lanes = slice(pair * 2 * width, (pair + 1) * 2 * width)
+            start = pl.multiple_of(q * stride + (offset + 2 * pair) * width, 128)
+            whole = pl.ds(start, 2 * width)
             x_first = opening(
-                x_ref[kid, :, lanes], taps_x_ref[:, lanes], offset * width // 128 + pair
+                x_ref[kid, :, whole], taps_x_ref[:, whole], offset * width // 128 + pair
             ).astype(jnp.float32)
             stacked = [jnp.where(low_first, x_first, 0.0), jnp.where(low_first, 0.0, x_first)]
             if pair > 0:
@@ -149,13 +176,11 @@
                 jnp.concatenate(stacked).astype(jnp.bfloat16),
                 preferred_element_type=jnp.float32,
             )
-            part = jnp.concatenate([part[:FIX] + skip_ref[:, lanes] * x_first, part[FIX:]])
-            head = offset + 2 * pair
-            grow = jnp.where(
-                low, column_ref[0, :, head : head + 1], column_ref[0, :, head + 1 : head + 2]
-            )
-            carried = (term[:, lanes] * jnp.exp(grow)).astype(jnp.bfloat16).astype(jnp.float32)
-            y_ref[kid, :, lanes] = (mixed_ref[:, lanes] + part + carried).astype(jnp.bfloat16)
+            part = jnp.concatenate([part[:FIX] + skip_ref[:, whole] * x_first, part[FIX:]])
+            here = slice(offset * width + lanes.start, offset * width + lanes.stop)
+            y_ref[kid, :, lanes] = (
+                mixed_ref[q, :, here] + part + carried[:, lanes].astype(jnp.float32)
+            ).astype(jnp.bfloat16)
 
 
 def cast_kernel(parts, tailed, reach, lines, *refs):
@@ -183,19 +208,21 @@
 
 
 def pick_rows_kernel(start, slots_ref, inside_ref, *refs):
-    crossed, out, sems = refs[:-2], refs[-2], refs[-1]
-    spots, rows = out.shape[:2]
+    crossed, outs, sems = refs[:-5], refs[-5:-1], refs[-1]
+    kids, rows = outs[0].shape[:2]
     held = [inside_ref.at[source, pl.ds(start, rows)] for source in range(4)]
     held += list(crossed) if len(crossed) == 4 else [crossed[0].at[source] for source in range(4)]
-    for i in range(spots):
-        for source in range(8):
-
-            @pl.when(slots_ref[i] == source)
-            def _(source=source, i=i):
-                pltpu.make_async_copy(held[source], out.at[i], sems.at[i]).start()
-
-    for i in range(spots):
-        pltpu.make_async_copy(held[0], out.at[i], sems.at[i]).wait()
+    for j, out in enumerate(outs):
+        for kid in range(kids):
+            for source in range(8):
+
+                @pl.when(slots_ref[j * kids + kid] == source)
+                def _(source=source, out=out, j=j, kid=kid):
+                    pltpu.make_async_copy(held[source], out.at[kid], sems.at[j, kid]).start()
+
+    for j, out in enumerate(outs):
+        for kid in range(kids):
+            pltpu.make_async_copy(held[0], out.at[kid], sems.at[j, kid]).wait()
 
 
 def slice_kernel(start, in_ref, out_ref, sem):
@@ -441,12 +468,16 @@
     small = pl.CostEstimate(flops=1, bytes_accessed=1, transcendentals=0)
 
     stay = lambda x: pltpu.with_memory_space_constraint(x, pltpu.HBM)
+    keep_in_vmem = lambda x: pltpu.with_memory_space_constraint(x, pltpu.VMEM)
     x_in, b_in, c_in, dt_in, conv_x, conv_bc = map(stay, (x_in, b_in, c_in, dt_in, conv_x, conv_bc))
 
     me = lax.axis_index("batch")
     parent = parent_of(counts, order)
     side = me // 4 * 4
-    owner = lax.dynamic_slice_in_dim(parent, side * kids, 4 * kids)
+    child = (jnp.arange(4 * kids, dtype=jnp.int32) // kids ^ me) * kids
+    child = child + jnp.arange(4 * kids, dtype=jnp.int32) % kids
+    catalog = jnp.arange(4 * 2 * kids, dtype=jnp.int32)
+    owner = jnp.sum(jnp.where(child[:, None] == catalog[None, :], parent[None, :], 0), axis=1)
     here = owner // 4 * 4 == side
     slots_a = jnp.where(here, owner % 4, 4 + (owner ^ me) % 4)
     slots_b = jnp.where(here, owner % 4, 4 + owner % 4)
@@ -459,70 +490,41 @@
     def swap(value, r):
         return lax.ppermute(value, "batch", perm=[(i, i ^ r) for i in range(8)])
 
-    def cast(quarters, chunks, tokens):
-        tailed = [tail_lines if chunks[0] == 0 else 0] * len(quarters)
-        rows = sum(SPLIT[k] for k in chunks) * width + tailed[0]
-        operands, specs = [], []
-        for j in quarters:
-            for k in chunks:
-                part, at = SPLIT[k], offsets[k] // SPLIT[k]
-                operands.append(state)
-                specs.append(
-                    pl.BlockSpec(
-                        (1, part, width, size), lambda i, p, j=j, at=at: (p[0] ^ j, at, 0, 0)
-                    )
-                )
-        if tailed[0]:
-            for j in quarters:
-                operands += [x_tails, bc_tails]
-                specs += [
-                    pl.BlockSpec((1, reach, wide), lambda i, p, j=j: (0, 0, p[0] ^ j)),
-                    pl.BlockSpec((1, reach, 2, size), lambda i, p, j=j: (0, 0, 0, p[0] ^ j)),
-                ]
-        kernel = functools.partial(cast_kernel, len(chunks), tailed, reach, lines)
-        return pl.pallas_call(
-            functools.partial(
-                drop_tokens, lambda place_ref, *refs: kernel(*refs), 1 + len(operands), len(tokens)
-            ),
-            grid_spec=pltpu.PrefetchScalarGridSpec(
-                num_scalar_prefetch=1,
-                grid=(1,),
-                in_specs=specs + [anywhere] * len(tokens),
-                out_specs=[pl.BlockSpec((rows, size), lambda i, p: (0, 0))] * len(quarters),
-            ),
-            out_shape=[jax.ShapeDtypeStruct((rows, size), jnp.bfloat16)] * len(quarters),
-            compiler_params=params,
-            cost_estimate=small,
-            name="cast_states",
-        )(place, *operands, *tokens)
-
-    def cast_whole(tokens):
+    def cast():
         rows = per_group * width + tail_lines
-
-        def kernel(*refs):
-            out_ref = refs[-1]
+        rows_a = SPLIT[0] * width + tail_lines
+
+        def kernel(place_ref, *refs):
+            whole_ref, outs = refs[-5], refs[-4:]
             for q in range(groups):
-                cast_kernel(2, [tail_lines], reach, lines, *refs[4 * q : 4 * q + 4], out_ref.at[q])
+                cast_kernel(2, [tail_lines], reach, lines, *refs[4 * q : 4 * q + 4], whole_ref.at[q])
+            for j, out_ref in enumerate(outs):
+                out_ref[...] = whole_ref[place_ref[0] ^ j, :rows_a]
 
         operands, specs = [], []
         for q in range(groups):
             operands += [state, state, x_tails, bc_tails]
             specs += [
-                pl.BlockSpec((1, SPLIT[0], width, size), lambda i, q=q: (q, 0, 0, 0)),
-                pl.BlockSpec((1, SPLIT[1], width, size), lambda i, q=q: (q, 1, 0, 0)),
-                pl.BlockSpec((1, reach, wide), lambda i, q=q: (0, 0, q)),
-                pl.BlockSpec((1, reach, 2, size), lambda i, q=q: (0, 0, 0, q)),
+                pl.BlockSpec((1, SPLIT[0], width, size), lambda i, p, q=q: (q, 0, 0, 0)),
+                pl.BlockSpec((1, SPLIT[1], width, size), lambda i, p, q=q: (q, 1, 0, 0)),
+                pl.BlockSpec((1, reach, wide), lambda i, p, q=q: (0, 0, q)),
+                pl.BlockSpec((1, reach, 2, size), lambda i, p, q=q: (0, 0, 0, q)),
             ]
         return pl.pallas_call(
-            functools.partial(drop_tokens, kernel, len(operands), len(tokens)),
-            grid=(1,),
-            in_specs=specs + [anywhere] * len(tokens),
-            out_specs=pl.BlockSpec((groups, rows, size), lambda i: (0, 0, 0)),
-            out_shape=jax.ShapeDtypeStruct((groups, rows, size), jnp.bfloat16),
+            kernel,
+            grid_spec=pltpu.PrefetchScalarGridSpec(
+                num_scalar_prefetch=1,
+                grid=(1,),
+                in_specs=specs,
+                out_specs=[pl.BlockSpec((groups, rows, size), lambda i, p: (0, 0, 0))]
+                + [pl.BlockSpec(memory_space=pltpu.VMEM)] * 4,
+            ),
+            out_shape=[jax.ShapeDtypeStruct((groups, rows, size), jnp.bfloat16)]
+            + [pltpu.VMEM((rows_a, size), jnp.bfloat16)] * 4,
             compiler_params=params,
             cost_estimate=small,
             name="cast_states",
-        )(*operands, *tokens)
+        )(place, *operands)
 
     def chunk_b(inside, tokens):
         rows = SPLIT[1] * width
@@ -533,8 +535,8 @@
             grid=(1,),
             in_specs=[anywhere]
             + [anywhere] * len(tokens),
-            out_specs=pl.BlockSpec((4, rows, size), lambda i: (0, 0, 0)),
-            out_shape=jax.ShapeDtypeStruct((4, rows, size), jnp.bfloat16),
+            out_specs=pl.BlockSpec(memory_space=pltpu.VMEM),
+            out_shape=pltpu.VMEM((4, rows, size), jnp.bfloat16),
             scratch_shapes=[pltpu.SemaphoreType.DMA],
             compiler_params=params,
             cost_estimate=small,
@@ -552,24 +554,26 @@
         )
 
     def pick(rows, start, slots, inside, crossed, tokens):
-        spots = 4 * kids
         picked = pl.pallas_call(
             functools.partial(
-                drop_tokens, functools.partial(pick_rows_kernel, start), 2 + len(crossed), len(tokens)
+                drop_tokens,
+                functools.partial(pick_rows_kernel, start),
+                2 + len(crossed),
+                len(tokens),
             ),
             grid_spec=pltpu.PrefetchScalarGridSpec(
                 num_scalar_prefetch=1,
                 grid=(1,),
                 in_specs=[anywhere] * (1 + len(crossed) + len(tokens)),
-                out_specs=pl.BlockSpec((spots, rows, size), lambda i, s: (0, 0, 0)),
-                scratch_shapes=[pltpu.SemaphoreType.DMA((spots,))],
+                out_specs=[pl.BlockSpec(memory_space=pltpu.VMEM)] * 4,
+                scratch_shapes=[pltpu.SemaphoreType.DMA((4, kids))],
             ),
-            out_shape=jax.ShapeDtypeStruct((spots, rows, size), jnp.bfloat16),
+            out_shape=[pltpu.VMEM((kids, rows, size), jnp.bfloat16)] * 4,
             compiler_params=params,
             cost_estimate=small,
             name="pick_states",
         )(slots, inside, *crossed, *tokens)
-        return picked, gather_half(picked).reshape(4, kids, rows, size)
+        return [picked[0]] + [swap(picked[j], j) for j in range(1, 4)]
 
     def early(c, tokens):
         at = lambda q: (c, 0, q)
@@ -591,17 +595,12 @@
                 pl.BlockSpec((2, taps, size), lambda q: (0, 0, q)),
                 *[anywhere] * len(tokens),
             ],
-            out_specs=[
-                pl.BlockSpec((length, wide), lambda q: (0, q)),
-                pl.BlockSpec((length, size), lambda q: (0, q)),
-                pl.BlockSpec((1, length, per_group), lambda q: (q, 0, 0)),
-                pl.BlockSpec((1, length, per_group * FIX), lambda q: (q, 0, 0)),
-            ],
+            out_specs=[pl.BlockSpec(memory_space=pltpu.VMEM)] * 4,
             out_shape=[
-                pltpu.HBM((length, columns), jnp.float32),
-                pltpu.HBM((length, groups * size), jnp.bfloat16),
-                pltpu.HBM((groups, length, per_group), jnp.float32),
-                pltpu.HBM((groups, length, per_group * FIX), jnp.float32),
+                pltpu.VMEM((groups, length, wide), jnp.float32),
+                pltpu.VMEM((groups, length, size), jnp.bfloat16),
+                pltpu.VMEM((groups, per_group, length), jnp.float32),
+                pltpu.VMEM((groups, length, per_group * FIX), jnp.float32),
             ],
             scratch_shapes=[pltpu.VMEM((8 + length, size), jnp.float32)],
             compiler_params=params,
@@ -613,35 +612,30 @@
         part, offset = SPLIT[k], offsets[k]
         chunk = part * width
         unit = offset // part
-        at = lambda q: (0, q * (per_group // part) + unit)
-        lane = lambda q: (0, 0, q * (per_group // part) + unit)
+        lane = lambda q, p: (0, 0, q * (per_group // part) + unit)
         tail_at = SPLIT[0] * width // tail_lines
-        operands = [x_in, b_in, c_in, skip_row, conv_x, conv_bc]
+        in_vmem = pl.BlockSpec(memory_space=pltpu.VMEM)
+        operands = [x_in, b_in, c_in, skip_row, conv_x, conv_bc, *states_first, *states]
         specs = [
-            pl.BlockSpec((kids, FIX, chunk), lane),
-            pl.BlockSpec((kids, FIX, size), lambda q: (0, 0, q)),
-            pl.BlockSpec((kids, FIX, size), lambda q: (0, 0, q)),
-            pl.BlockSpec((1, chunk), at),
-            pl.BlockSpec((taps, chunk), at),
-            pl.BlockSpec((2, taps, size), lambda q: (0, 0, q)),
+            pl.BlockSpec((kids, FIX, columns), lambda q, p: (0, 0, 0)),
+            pl.BlockSpec((kids, FIX, groups * size), lambda q, p: (0, 0, 0)),
+            pl.BlockSpec((kids, FIX, groups * size), lambda q, p: (0, 0, 0)),
+            pl.BlockSpec((1, columns), lambda q, p: (0, 0)),
+            pl.BlockSpec((taps, columns), lambda q, p: (0, 0)),
+            pl.BlockSpec((2, taps, groups * size), lambda q, p: (0, 0, 0)),
+            *[pl.BlockSpec((kids, tail_lines, size), lambda q, p: (0, tail_at, 0))] * 4,
+            *[pl.BlockSpec((kids, chunk, size), lambda q, p: (0, 0, 0))] * 4,
         ]
         for c in range(kids):
-            mixed, held, column, first = map(stay, parts[c])
-            operands += [states, states_first, held, column, first, mixed]
-            specs += [
-                pl.BlockSpec((1, 1, chunk, size), lambda q, c=c: (q, c, 0, 0)),
-                pl.BlockSpec((1, 1, tail_lines, size), lambda q, c=c: (q, c, tail_at, 0)),
-                pl.BlockSpec((length, size), lambda q: (0, q)),
-                pl.BlockSpec((1, length, per_group), lambda q: (q, 0, 0)),
-                pl.BlockSpec((1, length, part * FIX), lambda q: (q, 0, unit)),
-                pl.BlockSpec((length, chunk), at),
-            ]
-        keep = len(operands)
+            mixed, held, column, first = parts[c]
+            operands += [keep_in_vmem(a) for a in (held, column, first, mixed)]
+            specs += [in_vmem] * 4
+        keep = 1 + len(operands)
         operands += tokens
         specs += [anywhere] * len(tokens)
         alias = {}
         if result is not None:
-            alias = {len(operands): 0}
+            alias = {1 + len(operands): 0}
             operands.append(result)
             specs.append(anywhere)
         return pl.pallas_call(
@@ -649,33 +643,34 @@
                 drop_tokens,
                 functools.partial(late_kernel, offset, lines),
                 keep,
-                len(operands) - keep,
+                1 + len(operands) - keep,
             ),
-            grid=(groups,),
-            in_specs=specs,
-            out_specs=pl.BlockSpec((kids, length, chunk), lane),
+            grid_spec=pltpu.PrefetchScalarGridSpec(
+                num_scalar_prefetch=1,
+                grid=(groups,),
+                in_specs=specs,
+                out_specs=pl.BlockSpec((kids, length, chunk), lane),
+                scratch_shapes=[pltpu.VMEM((8 + FIX, size), jnp.float32)],
+            ),
             out_shape=jax.ShapeDtypeStruct(x_in.shape, jnp.bfloat16),
             input_output_aliases=alias,
-            scratch_shapes=[pltpu.VMEM((8 + FIX, size), jnp.float32)],
             compiler_params=params,
             cost_estimate=small,
             name="late",
-        )(*operands)
+        )(place, *operands)
 
     skip_row = jnp.repeat(d_skip, width)[None, :]
     rows = [SPLIT[0] * width + tail_lines, SPLIT[1] * width]
-    quarters = [0, 1, 2, 3]
-    sent_a = cast(quarters, [0], [])
-    crossed_a = [swap(sent_a[j], j + 4) for j in quarters]
-    whole = cast_whole([sent_a[0]])
+    whole, *sent_a = cast()
+    crossed_a = [swap(sent_a[j], j + 4) for j in range(4)]
     inside = gather_half(whole)
     parts = [early(0, [whole])]
-    sent_b = chunk_b(inside, [stay(parts[0][1])])
+    sent_b = chunk_b(inside, [parts[0][1]])
     crossed_b = swap(sent_b, 4)
-    picked_a, states_a = pick(rows[0], 0, slots_a, inside, crossed_a, [sent_b])
-    parts.append(early(1, [picked_a]))
-    picked_b, states_b = pick(rows[1], rows[0], slots_b, inside, [crossed_b], [stay(parts[1][1])])
-    result = late(0, states_a, states_a, parts, None, [picked_b])
+    states_a = pick(rows[0], 0, slots_a, inside, crossed_a, [sent_b])
+    parts.append(early(1, [states_a[0]]))
+    states_b = pick(rows[1], rows[0], slots_b, inside, [crossed_b], [parts[1][1]])
+    result = late(0, states_a, states_a, parts, None, [states_b[0]])
     return late(1, states_b, states_a, parts, result, [])
 
 

time: 95.3 us -> 88.7 us (0.931)
  Pallas kernels: 47.4 us -> 39.7 us
  waiting for transfers between devices: 22.3 us -> 16 us
  starting transfers between devices: 24.2 us -> 29.8 us
  local copies, waits for them, and re-layouts: 0.39 us -> 2.38 us
    ppermute x5 -> x11, starting transfers between devices: 9.83 us -> 24.4 us  [swap(): return lax.ppermute(value, 'batch', perm=[(i, i ^ r) for i in range(8)])]
    all_to_all x3 -> x1, starting transfers between devices: 14.4 us -> 5.39 us  [gather_half(): lax.all_to_all(value, 'batch', split_axis=0, concat_axis=0, tiled=True, a...]
    all_to_all x3 -> x1, waiting for transfers between devices: 4.42 us -> 0.01 us  [gather_half(): lax.all_to_all(value, 'batch', split_axis=0, concat_axis=0, tiled=True, a...]
    pallas_call x2, Pallas kernels: 22.9 us -> 20.4 us  [early(): pl.pallas_call(functools.partial(drop_tokens, early_kernel, len(operands)...]
    unnamed x10 -> x14, local copies, waits for them, and re-layouts: 0.03 us -> 2.03 us
    pallas_call x2, Pallas kernels: 7.04 us -> 5.06 us  [pick(): pl.pallas_call(functools.partial(drop_tokens, functools.partial(pick_rows...]
    pallas_call x2, Pallas kernels: 13.3 us -> 11.4 us  [late(): pl.pallas_call(functools.partial(drop_tokens, functools.partial(late_kern...]
    ppermute x5 -> x11, waiting for transfers between devices: 17.9 us -> 16 us  [swap(): return lax.ppermute(value, 'batch', perm=[(i, i ^ r) for i in range(8)])]
  transfers between devices with their start and end apart: 8 -> 12, of which waited for: 4 -> 4; matrix products, arithmetic and copies ran while one was open for 1% -> 1% of each run, Pallas kernels for 35% -> 35%
where the time goes in v9:
time: 88.7 us; the launch traced here: 88.4 us
  Pallas kernels  39.7 us (45%)
  starting transfers between devices  29.8 us (34%)
  waiting for transfers between devices  16 us (18%)
  local copies, waits for them, and re-layouts  2.38 us (3%)
    ppermute x11, starting transfers between devices, swap(): return lax.ppermute(value, 'batch', perm=[(i, i ^ r) for i in range(8)])  24.4 us
    pallas_call x2, Pallas kernels, early(): pl.pallas_call(functools.partial(drop_tokens, early_kernel, len(operands)...  20.4 us
    ppermute x11, waiting for transfers between devices, swap(): return lax.ppermute(value, 'batch', perm=[(i, i ^ r) for i in range(8)])  16 us
    pallas_call x2, Pallas kernels, late(): pl.pallas_call(functools.partial(drop_tokens, functools.partial(late_kern...  11.4 us
    all_to_all x1, starting transfers between devices, gather_half(): lax.all_to_all(value, 'batch', split_axis=0, concat_axis=0, tiled=True, a...  5.39 us
    pallas_call x2, Pallas kernels, pick(): pl.pallas_call(functools.partial(drop_tokens, functools.partial(pick_rows...  5.06 us
    pallas_call x1, Pallas kernels, cast(): pl.pallas_call(kernel, grid_spec=pltpu.PrefetchScalarGridSpec(num_scalar_...  2.78 us
    unnamed x14, local copies, waits for them, and re-layouts  2.03 us
  transfers between devices with their start and end apart: 12, of which 4 were waited for; matrix products, arithmetic and copies ran while one was open for 1% of the time, Pallas kernels for 35%

profile of v9, /device:TPU:0, one launch (start us, length us, event | category | flops | bytes accessed | tf_op | source)
XLA Modules:
  0.0 88.4 jit_solution(272767219791342246)
XLA Ops:
  0.0 0.0 copy-start.2
  0.0 2.8 %cast_states.1 = (bf16[4,1056,128]{2,1,0:T(8,128)(2,1)}, bf16[544,128]{1,0:T(8,128)(2,1)}, bf16[544,128]{1,0:T(8,128)(2,1)S(1)}, bf16[544,128]{1,0:T(8,128)(2,1)S(1)}, bf16[544,128]{1,0:T(8,128)(2,1)S(1)}) custom-call(s32[1]{0:T(128)} %bitcast.place_ref.refs_0_, f32[4,16,64,128]{3,2,1,0:T(8,128)} %bitcast.5, f32[4,16,64,128]{3,2,1,0:T(8,128)} %bitcast.6, ...), custom_call_target="tpu_custom_call" | custom-call | flops 1 | bytes 1 | tf_op jit(solution)/shard_map/cast_states/pallas_call | solution.py:513
  2.8 5.4 %all-to-all-start = ((bf16[4,1056,128]{2,1,0:T(8,128)(2,1)}), bf16[4,1056,128]{2,1,0:T(8,128)(2,1)S(1)}, u32[]{:S(2)}, u32[]{:S(2)}) async-start(bf16[4,1056,128]{2,1,0:T(8,128)(2,1)} %get-tuple-element.26.refs_9_), calls=%async_computation | async-start | bytes 2162688 | tf_op jit(solution)/shard_map/all_to_all | solution.py:547
  8.2 2.6 %collective-permute-start = (bf16[544,128]{1,0:T(8,128)(2,1)}, bf16[544,128]{1,0:T(8,128)(2,1)S(1)}, u32[]{:S(2)}, u32[]{:S(2)}) collective-permute-start(bf16[544,128]{1,0:T(8,128)(2,1)} %get-tuple-element.27), channel_id=1, source_target_pairs={{0,8},{2,10},{4,12},{6,14},{8,0},{10,2},{12,4},{14,6},{1,9},{3,11}... | collective-permute-start | bytes 417800 | tf_op jit(solution)/shard_map/ppermute | solution.py:491
  10.8 1.8 %collective-permute-start.1 = (bf16[544,128]{1,0:T(8,128)(2,1)S(1)}, bf16[544,128]{1,0:T(8,128)(2,1)S(1)}, u32[]{:S(2)}, u32[]{:S(2)}) collective-permute-start(bf16[544,128]{1,0:T(8,128)(2,1)S(1)} %get-tuple-element.28), channel_id=1, source_target_pairs={{0,10},{2,8},{4,14},{6,12},{8,2},{10,0},{12,6},{14,4},{1,11},{3,9}... | collective-permute-start | bytes 417800 | tf_op jit(solution)/shard_map/ppermute | solution.py:491
  12.6 3.5 %collective-permute-start.2 = (bf16[544,128]{1,0:T(8,128)(2,1)S(1)}, bf16[544,128]{1,0:T(8,128)(2,1)S(1)}, u32[]{:S(2)}, u32[]{:S(2)}) collective-permute-start(bf16[544,128]{1,0:T(8,128)(2,1)S(1)} %get-tuple-element.29), channel_id=1, source_target_pairs={{0,12},{2,14},{4,8},{6,10},{8,4},{10,6},{12,0},{14,2},{1,13},{3,15... | collective-permute-start | bytes 417800 | tf_op jit(solution)/shard_map/ppermute | solution.py:491
  16.1 0.0 collective-permute-start.3
  16.1 0.0 copy-done.2
  16.1 0.1 copy.20.refs_4_
  16.2 0.0 copy-done.3
  16.2 0.1 copy.21.refs_5_
  16.3 0.0 copy-done.4
  16.3 0.1 broadcast_in_dim.47
  16.3 0.1 broadcast_in_dim_reshape.3.refs_6_.refs_4_
  16.4 10.2 %early.2 = (f32[4,256,1024]{2,1,0:T(8,128)S(1)}, bf16[4,256,128]{2,1,0:T(8,128)(2,1)S(1)}, f32[4,16,256]{2,1,0:T(8,128)S(1)}, f32[4,256,256]{2,1,0:T(8,128)S(1)}) custom-call(bf16[2,256,4096]{2,1,0:T(8,128)(2,1)} %refs_1_.7, bf16[2,256,512]{2,1,0:T(8,128)(2,1)} %refs_2_.9, bf16[2,256,512]{2,1,0:T(8,128)(2,1)} %refs_3_.7, f32[2,64,256]{2,1,0:T(8,128)} %refs_3_.5, ...), custom_call_target="tpu_custom_call" | custom-call | flops 1 | bytes 1 | tf_op jit(solution)/shard_map/early/pallas_call | solution.py:583
  26.7 0.0 copy-start
  26.7 2.0 %copy-done = f32[4,256,1024]{2,1,0:T(8,128)} copy-done((f32[4,256,1024]{2,1,0:T(8,128)}, f32[4,256,1024]{2,1,0:T(8,128)S(1)}, u32[]{:S(2)}) %copy-start) | copy-done | bytes 4194328
  28.7 0.0 copy-done.5
  28.7 0.1 select_reduce_fusion.1
  28.8 0.0 copy-done.6
  28.8 0.1 convert_reduce_fusion
  28.9 0.2 select_reduce_fusion
  29.1 0.0 all-to-all-done.refs_0_.refs_1_
  29.2 0.7 collective-permute-start.7
  29.9 0.0 collective-permute-done.refs_2_
  29.9 0.0 collective-permute-done.1.refs_3_
  29.9 4.7 %collective-permute-done.2.refs_4_ = bf16[544,128]{1,0:T(8,128)(2,1)S(1)} collective-permute-done((bf16[544,128]{1,0:T(8,128)(2,1)S(1)}, bf16[544,128]{1,0:T(8,128)(2,1)S(1)}, u32[]{:S(2)}, u32[]{:S(2)}) %collective-permute-start.2) | collective-permute-done | bytes 139296 | tf_op jit(solution)/shard_map/ppermute | solution.py:491
  34.7 3.9 %collective-permute-done.3.refs_5_ = bf16[544,128]{1,0:T(8,128)(2,1)S(1)} collective-permute-done((bf16[544,128]{1,0:T(8,128)(2,1)S(1)}, bf16[544,128]{1,0:T(8,128)(2,1)S(1)}, u32[]{:S(2)}, u32[]{:S(2)}) %collective-permute-start.3) | collective-permute-done | bytes 139296 | tf_op jit(solution)/shard_map/ppermute | solution.py:491
  38.6 2.6 %pick_states.2 = (bf16[2,544,128]{2,1,0:T(8,128)(2,1)S(1)}, bf16[2,544,128]{2,1,0:T(8,128)(2,1)S(1)}, bf16[2,544,128]{2,1,0:T(8,128)(2,1)S(1)}, bf16[2,544,128]{2,1,0:T(8,128)(2,1)S(1)}) custom-call(s32[8]{0:T(128)S(1)} %compare_select_fusion.6.refs_0_, bf16[4,1056,128]{2,1,0:T(8,128)(2,1)S(1)} %all-to-all-done.refs_0_.refs_1_, ...), custom_call_target="tpu_custom_call" | custom-call | flops 1 | bytes 1 | tf_op jit(solution)/shard_map/pick_states/pallas_call | solution.py:557
  41.1 0.0 copy-start.1
  41.2 0.6 collective-permute-start.4
  41.8 11.6 %collective-permute-start.5 = (bf16[2,544,128]{2,1,0:T(8,128)(2,1)S(1)}, bf16[2,544,128]{2,1,0:T(8,128)(2,1)S(1)}, u32[]{:S(2)}, u32[]{:S(2)}) collective-permute-start(bf16[2,544,128]{2,1,0:T(8,128)(2,1)S(1)} %get-tuple-element.34), channel_id=1, source_target_pairs={{0,4},{2,6},{4,0},{6,2},{8,12},{10,14},{12,8},{14,10},{1,5},{3,7},... | collective-permute-start | bytes 835592 | tf_op jit(solution)/shard_map/ppermute | solution.py:491
  53.4 0.0 collective-permute-start.6
  53.4 10.2 %early.3 = (f32[4,256,1024]{2,1,0:T(8,128)S(1)}, bf16[4,256,128]{2,1,0:T(8,128)(2,1)S(1)}, f32[4,16,256]{2,1,0:T(8,128)S(1)}, f32[4,256,256]{2,1,0:T(8,128)S(1)}) custom-call(bf16[2,256,4096]{2,1,0:T(8,128)(2,1)} %refs_1_.7, bf16[2,256,512]{2,1,0:T(8,128)(2,1)} %refs_2_.9, bf16[2,256,512]{2,1,0:T(8,128)(2,1)} %refs_3_.7, f32[2,64,256]{2,1,0:T(8,128)} %refs_3_.5, ...), custom_call_target="tpu_custom_call" | custom-call | flops 1 | bytes 1 | tf_op jit(solution)/shard_map/early/pallas_call | solution.py:583
  63.6 0.0 collective-permute-done.7.refs_2_
  63.6 2.5 %pick_states.3 = (bf16[2,512,128]{2,1,0:T(8,128)(2,1)S(1)}, bf16[2,512,128]{2,1,0:T(8,128)(2,1)S(1)}, bf16[2,512,128]{2,1,0:T(8,128)(2,1)S(1)}, bf16[2,512,128]{2,1,0:T(8,128)(2,1)S(1)}) custom-call(s32[8]{0:T(128)S(1)} %get-tuple-element.47.refs_0_, bf16[4,1056,128]{2,1,0:T(8,128)(2,1)S(1)} %all-to-all-done.refs_0_.refs_1_, ...), custom_call_target="tpu_custom_call" | custom-call | flops 1 | bytes 1 | tf_op jit(solution)/shard_map/pick_states/pallas_call | solution.py:557
  66.1 1.5 %collective-permute-start.8 = (bf16[2,512,128]{2,1,0:T(8,128)(2,1)S(1)}, bf16[2,512,128]{2,1,0:T(8,128)(2,1)S(1)}, u32[]{:S(2)}, u32[]{:S(2)}) collective-permute-start(bf16[2,512,128]{2,1,0:T(8,128)(2,1)S(1)} %get-tuple-element.38), channel_id=1, source_target_pairs={{0,2},{2,0},{4,6},{6,4},{8,10},{10,8},{12,14},{14,12},{1,3},{3,1},... | collective-permute-start | bytes 786440 | tf_op jit(solution)/shard_map/ppermute | solution.py:491
  67.7 2.0 %collective-permute-start.9 = (bf16[2,512,128]{2,1,0:T(8,128)(2,1)S(1)}, bf16[2,512,128]{2,1,0:T(8,128)(2,1)S(1)}, u32[]{:S(2)}, u32[]{:S(2)}) collective-permute-start(bf16[2,512,128]{2,1,0:T(8,128)(2,1)S(1)} %get-tuple-element.39), channel_id=1, source_target_pairs={{0,4},{2,6},{4,0},{6,2},{8,12},{10,14},{12,8},{14,10},{1,5},{3,7},... | collective-permute-start | bytes 786440 | tf_op jit(solution)/shard_map/ppermute | solution.py:491
  69.7 0.0 collective-permute-done.4.refs_8_.refs_12_
  69.7 0.0 collective-permute-start.10
  69.7 0.0 collective-permute-done.5.refs_9_.refs_13_
  69.7 1.9 %collective-permute-done.6.refs_10_.refs_14_ = bf16[2,544,128]{2,1,0:T(8,128)(2,1)S(1)} collective-permute-done((bf16[2,544,128]{2,1,0:T(8,128)(2,1)S(1)}, bf16[2,544,128]{2,1,0:T(8,128)(2,1)S(1)}, u32[]{:S(2)}, u32[]{:S(2)}) %collective-permute-start.6) | collective-permute-done | bytes 278560 | tf_op jit(solution)/shard_map/ppermute | solution.py:491
  71.6 0.0 copy-done.1
  71.6 5.7 %late.2.refs_23_ = bf16[2,256,4096]{2,1,0:T(8,128)(2,1)} custom-call(s32[1]{0:T(128)} %bitcast.place_ref.refs_0_, bf16[2,256,4096]{2,1,0:T(8,128)(2,1)} %refs_1_.7, bf16[2,256,512]{2,1,0:T(8,128)(2,1)} %refs_2_.9, bf16[2,256,512]{2,1,0:T(8,128)(2,1)} %refs_3_.7, f32[1,4096]{1,0:T(1,128)S(1)} %broadcast_in_dim_reshape.3.refs_6_.refs_4_, f32[4,4096]{1,0:T(4,128)} %refs_5_.3, ...), custom_call_target="tpu_custom_call" | custom-call | flops 1 | bytes 1 | tf_op jit(solution)/shard_map/late/pallas_call | solution.py:641
  77.3 0.0 collective-permute-done.8.refs_12_
  77.3 0.0 collective-permute-done.9.refs_13_
  77.3 5.4 %collective-permute-done.10.refs_14_ = bf16[2,512,128]{2,1,0:T(8,128)(2,1)S(1)} collective-permute-done((bf16[2,512,128]{2,1,0:T(8,128)(2,1)S(1)}, bf16[2,512,128]{2,1,0:T(8,128)(2,1)S(1)}, u32[]{:S(2)}, u32[]{:S(2)}) %collective-permute-start.10) | collective-permute-done | bytes 262176 | tf_op jit(solution)/shard_map/ppermute | solution.py:491
  82.7 5.7 %late.3 = bf16[2,256,4096]{2,1,0:T(8,128)(2,1)} custom-call(s32[1]{0:T(128)} %bitcast.place_ref.refs_0_, bf16[2,256,4096]{2,1,0:T(8,128)(2,1)} %refs_1_.7, bf16[2,256,512]{2,1,0:T(8,128)(2,1)} %refs_2_.9, bf16[2,256,512]{2,1,0:T(8,128)(2,1)} %refs_3_.7, f32[1,4096]{1,0:T(1,128)S(1)} %broadcast_in_dim_reshape.3.refs_6_.refs_4_, ...), custom_call_target="tpu_custom_call", output_to_operand_aliasing={{}: (23, {})} | custom-call | flops 1 | bytes 1 | tf_op jit(solution)/shard_map/late/pallas_call | solution.py:641
  (8 shorter events, 0.1 us)
Async XLA Ops:
  0.0 16.1 %copy-start.2 = (f32[64]{0:T(128)S(1)}, f32[64]{0:T(128)}, u32[]{:S(2)}) copy-start(f32[64]{0:T(128)} %param.18) | copy-start | bytes 772
  0.0 16.2 %copy-start.3 = (f32[64]{0:T(128)S(1)}, f32[64]{0:T(128)}, u32[]{:S(2)}) copy-start(f32[64]{0:T(128)} %param.19) | copy-start | bytes 772
  0.0 16.3 %copy-start.4 = (f32[64]{0:T(128)S(1)}, f32[64]{0:T(128)}, u32[]{:S(2)}) copy-start(f32[64]{0:T(128)} %param.20) | copy-start | bytes 772
  2.8 25.9 %copy-start.5 = (s32[8]{0:T(128)S(1)}, s32[8]{0:T(128)}, u32[]{:S(2)}) copy-start(s32[8]{0:T(128)} %param.26) | copy-start | bytes 100
  2.8 26.0 %copy-start.6 = (s32[16]{0:T(128)S(1)}, s32[16]{0:T(128)}, u32[]{:S(2)}) copy-start(s32[16]{0:T(128)} %param.27) | copy-start | bytes 196
  2.8 26.3 %all-to-all-start = ((bf16[4,1056,128]{2,1,0:T(8,128)(2,1)}), bf16[4,1056,128]{2,1,0:T(8,128)(2,1)S(1)}, u32[]{:S(2)}, u32[]{:S(2)}) async-start(bf16[4,1056,128]{2,1,0:T(8,128)(2,1)} %get-tuple-element.26.refs_9_), calls=%async_computation | async-start | bytes 2162688 | tf_op jit(solution)/shard_map/all_to_all | solution.py:547
  8.2 21.7 %collective-permute-start = (bf16[544,128]{1,0:T(8,128)(2,1)}, bf16[544,128]{1,0:T(8,128)(2,1)S(1)}, u32[]{:S(2)}, u32[]{:S(2)}) collective-permute-start(bf16[544,128]{1,0:T(8,128)(2,1)} %get-tuple-element.27), channel_id=1, source_target_pairs={{0,8},{2,10},{4,12},{6,14},{8,0},{10,2},{12,4},{14,6},{1,9},{3,11}... | collective-permute-start | bytes 417800 | tf_op jit(solution)/shard_map/ppermute | solution.py:491
  10.8 19.2 %collective-permute-start.1 = (bf16[544,128]{1,0:T(8,128)(2,1)S(1)}, bf16[544,128]{1,0:T(8,128)(2,1)S(1)}, u32[]{:S(2)}, u32[]{:S(2)}) collective-permute-start(bf16[544,128]{1,0:T(8,128)(2,1)S(1)} %get-tuple-element.28), channel_id=1, source_target_pairs={{0,10},{2,8},{4,14},{6,12},{8,2},{10,0},{12,6},{14,4},{1,11},{3,9}... | collective-permute-start | bytes 417800 | tf_op jit(solution)/shard_map/ppermute | solution.py:491
  12.6 22.1 %collective-permute-start.2 = (bf16[544,128]{1,0:T(8,128)(2,1)S(1)}, bf16[544,128]{1,0:T(8,128)(2,1)S(1)}, u32[]{:S(2)}, u32[]{:S(2)}) collective-permute-start(bf16[544,128]{1,0:T(8,128)(2,1)S(1)} %get-tuple-element.29), channel_id=1, source_target_pairs={{0,12},{2,14},{4,8},{6,10},{8,4},{10,6},{12,0},{14,2},{1,13},{3,15... | collective-permute-start | bytes 417800 | tf_op jit(solution)/shard_map/ppermute | solution.py:491
  16.1 22.5 %collective-permute-start.3 = (bf16[544,128]{1,0:T(8,128)(2,1)S(1)}, bf16[544,128]{1,0:T(8,128)(2,1)S(1)}, u32[]{:S(2)}, u32[]{:S(2)}) collective-permute-start(bf16[544,128]{1,0:T(8,128)(2,1)S(1)} %get-tuple-element.30), channel_id=1, source_target_pairs={{0,14},{2,12},{4,10},{6,8},{8,6},{10,4},{12,2},{14,0},{1,15},{3,13... | collective-permute-start | bytes 417800 | tf_op jit(solution)/shard_map/ppermute | solution.py:491
  26.7 2.0 %copy-start = (f32[4,256,1024]{2,1,0:T(8,128)}, f32[4,256,1024]{2,1,0:T(8,128)S(1)}, u32[]{:S(2)}) copy-start(f32[4,256,1024]{2,1,0:T(8,128)S(1)} %get-tuple-element.43.refs_18_) | copy-start | bytes 12582916
  29.2 34.5 %collective-permute-start.7 = (bf16[4,512,128]{2,1,0:T(8,128)(2,1)S(1)}, bf16[4,512,128]{2,1,0:T(8,128)(2,1)S(1)}, u32[]{:S(2)}, u32[]{:S(2)}) collective-permute-start(bf16[4,512,128]{2,1,0:T(8,128)(2,1)S(1)} %chunk_b.1.refs_6_), channel_id=1, source_target_pairs={{0,8},{2,10},{4,12},{6,14},{8,0},{10,2},{12,4},{14,6},{1,9},{3,11}... | collective-permute-start | bytes 1572872 | tf_op jit(solution)/shard_map/ppermute | solution.py:491
  41.1 30.4 %copy-start.1 = (f32[4,256,1024]{2,1,0:T(8,128)S(1)}, f32[4,256,1024]{2,1,0:T(8,128)}, u32[]{:S(2)}) copy-start(f32[4,256,1024]{2,1,0:T(8,128)} %copy-done) | copy-start | bytes 12582916
  41.2 28.5 %collective-permute-start.4 = (bf16[2,544,128]{2,1,0:T(8,128)(2,1)S(1)}, bf16[2,544,128]{2,1,0:T(8,128)(2,1)S(1)}, u32[]{:S(2)}, u32[]{:S(2)}) collective-permute-start(bf16[2,544,128]{2,1,0:T(8,128)(2,1)S(1)} %get-tuple-element.33), channel_id=1, source_target_pairs={{0,2},{2,0},{4,6},{6,4},{8,10},{10,8},{12,14},{14,12},{1,3},{3,1},... | collective-permute-start | bytes 835592 | tf_op jit(solution)/shard_map/ppermute | solution.py:491
  41.8 27.9 %collective-permute-start.5 = (bf16[2,544,128]{2,1,0:T(8,128)(2,1)S(1)}, bf16[2,544,128]{2,1,0:T(8,128)(2,1)S(1)}, u32[]{:S(2)}, u32[]{:S(2)}) collective-permute-start(bf16[2,544,128]{2,1,0:T(8,128)(2,1)S(1)} %get-tuple-element.34), channel_id=1, source_target_pairs={{0,4},{2,6},{4,0},{6,2},{8,12},{10,14},{12,8},{14,10},{1,5},{3,7},... | collective-permute-start | bytes 835592 | tf_op jit(solution)/shard_map/ppermute | solution.py:491
  53.4 18.2 %collective-permute-start.6 = (bf16[2,544,128]{2,1,0:T(8,128)(2,1)S(1)}, bf16[2,544,128]{2,1,0:T(8,128)(2,1)S(1)}, u32[]{:S(2)}, u32[]{:S(2)}) collective-permute-start(bf16[2,544,128]{2,1,0:T(8,128)(2,1)S(1)} %get-tuple-element.35), channel_id=1, source_target_pairs={{0,6},{2,4},{4,2},{6,0},{8,14},{10,12},{12,10},{14,8},{1,7},{3,5},... | collective-permute-start | bytes 835592 | tf_op jit(solution)/shard_map/ppermute | solution.py:491
  66.1 11.2 %collective-permute-start.8 = (bf16[2,512,128]{2,1,0:T(8,128)(2,1)S(1)}, bf16[2,512,128]{2,1,0:T(8,128)(2,1)S(1)}, u32[]{:S(2)}, u32[]{:S(2)}) collective-permute-start(bf16[2,512,128]{2,1,0:T(8,128)(2,1)S(1)} %get-tuple-element.38), channel_id=1, source_target_pairs={{0,2},{2,0},{4,6},{6,4},{8,10},{10,8},{12,14},{14,12},{1,3},{3,1},... | collective-permute-start | bytes 786440 | tf_op jit(solution)/shard_map/ppermute | solution.py:491
  67.7 9.6 %collective-permute-start.9 = (bf16[2,512,128]{2,1,0:T(8,128)(2,1)S(1)}, bf16[2,512,128]{2,1,0:T(8,128)(2,1)S(1)}, u32[]{:S(2)}, u32[]{:S(2)}) collective-permute-start(bf16[2,512,128]{2,1,0:T(8,128)(2,1)S(1)} %get-tuple-element.39), channel_id=1, source_target_pairs={{0,4},{2,6},{4,0},{6,2},{8,12},{10,14},{12,8},{14,10},{1,5},{3,7},... | collective-permute-start | bytes 786440 | tf_op jit(solution)/shard_map/ppermute | solution.py:491
  69.7 13.0 %collective-permute-start.10 = (bf16[2,512,128]{2,1,0:T(8,128)(2,1)S(1)}, bf16[2,512,128]{2,1,0:T(8,128)(2,1)S(1)}, u32[]{:S(2)}, u32[]{:S(2)}) collective-permute-start(bf16[2,512,128]{2,1,0:T(8,128)(2,1)S(1)} %get-tuple-element.40), channel_id=1, source_target_pairs={{0,6},{2,4},{4,2},{6,0},{8,14},{10,12},{12,10},{14,8},{1,7},{3,5},... | collective-permute-start | bytes 786440 | tf_op jit(solution)/shard_map/ppermute | solution.py:491

commit v10 on v9

--- a/solution.py
+++ b/solution.py
@@ -664,8 +664,8 @@
     whole, *sent_a = cast()
     crossed_a = [swap(sent_a[j], j + 4) for j in range(4)]
     inside = gather_half(whole)
-    parts = [early(0, [whole])]
-    sent_b = chunk_b(inside, [parts[0][1]])
+    parts = [early(0, [whole, slots_a, slots_b])]
+    sent_b = chunk_b(inside, [parts[0][1], *crossed_a])
     crossed_b = swap(sent_b, 4)
     states_a = pick(rows[0], 0, slots_a, inside, crossed_a, [sent_b])
     parts.append(early(1, [states_a[0]]))

time: 88.7 us -> 83.7 us (0.944)
  starting transfers between devices: 29.8 us -> 22.6 us
  waiting for transfers between devices: 16 us -> 18.2 us
    ppermute x11, starting transfers between devices: 24.4 us -> 17.4 us  [swap(): return lax.ppermute(value, 'batch', perm=[(i, i ^ r) for i in range(8)])]
    ppermute x11, waiting for transfers between devices: 16 us -> 18.2 us  [swap(): return lax.ppermute(value, 'batch', perm=[(i, i ^ r) for i in range(8)])]
  transfers between devices with their start and end apart: 12 -> 12, of which waited for: 4 -> 7; matrix products, arithmetic and copies ran while one was open for 1% -> 1% of each run, Pallas kernels for 35% -> 37%
where the time goes in v10:
time: 83.7 us; the launch traced here: 83.4 us
  Pallas kernels  39.7 us (47%)
  starting transfers between devices  22.6 us (27%)
  waiting for transfers between devices  18.2 us (22%)
  local copies, waits for them, and re-layouts  2.38 us (3%)
    pallas_call x2, Pallas kernels, early(): pl.pallas_call(functools.partial(drop_tokens, early_kernel, len(operands)...  20.4 us
    ppermute x11, waiting for transfers between devices, swap(): return lax.ppermute(value, 'batch', perm=[(i, i ^ r) for i in range(8)])  18.2 us
    ppermute x11, starting transfers between devices, swap(): return lax.ppermute(value, 'batch', perm=[(i, i ^ r) for i in range(8)])  17.4 us
    pallas_call x2, Pallas kernels, late(): pl.pallas_call(functools.partial(drop_tokens, functools.partial(late_kern...  11.4 us
    all_to_all x1, starting transfers between devices, gather_half(): lax.all_to_all(value, 'batch', split_axis=0, concat_axis=0, tiled=True, a...  5.26 us
    pallas_call x2, Pallas kernels, pick(): pl.pallas_call(functools.partial(drop_tokens, functools.partial(pick_rows...  5.06 us
    pallas_call x1, Pallas kernels, cast(): pl.pallas_call(kernel, grid_spec=pltpu.PrefetchScalarGridSpec(num_scalar_...  2.8 us
    unnamed x14, local copies, waits for them, and re-layouts  2.03 us
  transfers between devices with their start and end apart: 12, of which 7 were waited for; matrix products, arithmetic and copies ran while one was open for 1% of the time, Pallas kernels for 37%

profile of v10, /device:TPU:0, one launch (start us, length us, event | category | flops | bytes accessed | tf_op | source)
XLA Modules:
  0.0 83.4 jit_solution(16661666942355703616)
XLA Ops:
  0.0 0.0 copy-start.2
  0.0 2.8 %cast_states.1 = (bf16[4,1056,128]{2,1,0:T(8,128)(2,1)}, bf16[544,128]{1,0:T(8,128)(2,1)}, bf16[544,128]{1,0:T(8,128)(2,1)S(1)}, bf16[544,128]{1,0:T(8,128)(2,1)S(1)}, bf16[544,128]{1,0:T(8,128)(2,1)S(1)}) custom-call(s32[1]{0:T(128)} %bitcast.place_ref.refs_0_, f32[4,16,64,128]{3,2,1,0:T(8,128)} %bitcast.5, f32[4,16,64,128]{3,2,1,0:T(8,128)} %bitcast.6, ...), custom_call_target="tpu_custom_call" | custom-call | flops 1 | bytes 1 | tf_op jit(solution)/shard_map/cast_states/pallas_call | solution.py:513
  2.8 5.3 %all-to-all-start = ((bf16[4,1056,128]{2,1,0:T(8,128)(2,1)}), bf16[4,1056,128]{2,1,0:T(8,128)(2,1)S(1)}, u32[]{:S(2)}, u32[]{:S(2)}) async-start(bf16[4,1056,128]{2,1,0:T(8,128)(2,1)} %get-tuple-element.26.refs_9_), calls=%async_computation | async-start | bytes 2162688 | tf_op jit(solution)/shard_map/all_to_all | solution.py:547
  8.1 2.6 %collective-permute-start = (bf16[544,128]{1,0:T(8,128)(2,1)}, bf16[544,128]{1,0:T(8,128)(2,1)S(1)}, u32[]{:S(2)}, u32[]{:S(2)}) collective-permute-start(bf16[544,128]{1,0:T(8,128)(2,1)} %get-tuple-element.27), channel_id=1, source_target_pairs={{0,8},{2,10},{4,12},{6,14},{8,0},{10,2},{12,4},{14,6},{1,9},{3,11}... | collective-permute-start | bytes 417800 | tf_op jit(solution)/shard_map/ppermute | solution.py:491
  10.7 1.8 %collective-permute-start.1 = (bf16[544,128]{1,0:T(8,128)(2,1)S(1)}, bf16[544,128]{1,0:T(8,128)(2,1)S(1)}, u32[]{:S(2)}, u32[]{:S(2)}) collective-permute-start(bf16[544,128]{1,0:T(8,128)(2,1)S(1)} %get-tuple-element.28), channel_id=1, source_target_pairs={{0,10},{2,8},{4,14},{6,12},{8,2},{10,0},{12,6},{14,4},{1,11},{3,9}... | collective-permute-start | bytes 417800 | tf_op jit(solution)/shard_map/ppermute | solution.py:491
  12.5 3.5 %collective-permute-start.2 = (bf16[544,128]{1,0:T(8,128)(2,1)S(1)}, bf16[544,128]{1,0:T(8,128)(2,1)S(1)}, u32[]{:S(2)}, u32[]{:S(2)}) collective-permute-start(bf16[544,128]{1,0:T(8,128)(2,1)S(1)} %get-tuple-element.29), channel_id=1, source_target_pairs={{0,12},{2,14},{4,8},{6,10},{8,4},{10,6},{12,0},{14,2},{1,13},{3,15... | collective-permute-start | bytes 417800 | tf_op jit(solution)/shard_map/ppermute | solution.py:491
  15.9 0.0 collective-permute-start.3
  15.9 0.0 copy-done.2
  16.0 0.1 copy.20.refs_4_
  16.0 0.0 copy-done.3
  16.1 0.1 copy.21.refs_5_
  16.1 0.0 copy-done.4
  16.1 0.1 broadcast_in_dim.47
  16.2 0.1 broadcast_in_dim_reshape.3.refs_6_.refs_4_
  16.3 0.0 copy-done.5
  16.3 0.1 select_reduce_fusion.1
  16.5 0.0 copy-done.6
  16.5 0.1 convert_reduce_fusion
  16.5 0.2 select_reduce_fusion
  16.8 10.2 %early.2 = (f32[4,256,1024]{2,1,0:T(8,128)S(1)}, bf16[4,256,128]{2,1,0:T(8,128)(2,1)S(1)}, f32[4,16,256]{2,1,0:T(8,128)S(1)}, f32[4,256,256]{2,1,0:T(8,128)S(1)}) custom-call(bf16[2,256,4096]{2,1,0:T(8,128)(2,1)} %refs_1_.7, bf16[2,256,512]{2,1,0:T(8,128)(2,1)} %refs_2_.9, bf16[2,256,512]{2,1,0:T(8,128)(2,1)} %refs_3_.7, f32[2,64,256]{2,1,0:T(8,128)} %refs_3_.5, ...), custom_call_target="tpu_custom_call" | custom-call | flops 1 | bytes 1 | tf_op jit(solution)/shard_map/early/pallas_call | solution.py:583
  27.0 0.0 copy-start
  27.0 2.0 %copy-done = f32[4,256,1024]{2,1,0:T(8,128)} copy-done((f32[4,256,1024]{2,1,0:T(8,128)}, f32[4,256,1024]{2,1,0:T(8,128)S(1)}, u32[]{:S(2)}) %copy-start) | copy-done | bytes 4194328
  29.0 0.0 collective-permute-done.refs_2_
  29.0 0.0 collective-permute-done.1.refs_3_
  29.0 5.4 %collective-permute-done.2.refs_4_ = bf16[544,128]{1,0:T(8,128)(2,1)S(1)} collective-permute-done((bf16[544,128]{1,0:T(8,128)(2,1)S(1)}, bf16[544,128]{1,0:T(8,128)(2,1)S(1)}, u32[]{:S(2)}, u32[]{:S(2)}) %collective-permute-start.2) | collective-permute-done | bytes 139296 | tf_op jit(solution)/shard_map/ppermute | solution.py:491
  34.5 2.5 %collective-permute-done.3.refs_5_ = bf16[544,128]{1,0:T(8,128)(2,1)S(1)} collective-permute-done((bf16[544,128]{1,0:T(8,128)(2,1)S(1)}, bf16[544,128]{1,0:T(8,128)(2,1)S(1)}, u32[]{:S(2)}, u32[]{:S(2)}) %collective-permute-start.3) | collective-permute-done | bytes 139296 | tf_op jit(solution)/shard_map/ppermute | solution.py:491
  36.9 0.0 all-to-all-done.refs_0_.refs_1_
  37.0 2.4 %collective-permute-start.7 = (bf16[4,512,128]{2,1,0:T(8,128)(2,1)S(1)}, bf16[4,512,128]{2,1,0:T(8,128)(2,1)S(1)}, u32[]{:S(2)}, u32[]{:S(2)}) collective-permute-start(bf16[4,512,128]{2,1,0:T(8,128)(2,1)S(1)} %chunk_b.1.refs_6_), channel_id=1, source_target_pairs={{0,8},{2,10},{4,12},{6,14},{8,0},{10,2},{12,4},{14,6},{1,9},{3,11}... | collective-permute-start | bytes 1572872 | tf_op jit(solution)/shard_map/ppermute | solution.py:491
  39.4 2.6 %pick_states.2 = (bf16[2,544,128]{2,1,0:T(8,128)(2,1)S(1)}, bf16[2,544,128]{2,1,0:T(8,128)(2,1)S(1)}, bf16[2,544,128]{2,1,0:T(8,128)(2,1)S(1)}, bf16[2,544,128]{2,1,0:T(8,128)(2,1)S(1)}) custom-call(s32[8]{0:T(128)S(1)} %compare_select_fusion.6.refs_10_.refs_0_, bf16[4,1056,128]{2,1,0:T(8,128)(2,1)S(1)} %all-to-all-done.refs_0_.refs_1_, ...), custom_call_target="tpu_custom_call" | custom-call | flops 1 | bytes 1 | tf_op jit(solution)/shard_map/pick_states/pallas_call | solution.py:557
  41.9 0.0 copy-start.1
  41.9 0.4 collective-permute-start.4
  42.4 0.0 collective-permute-start.5
  42.4 3.1 %collective-permute-start.6 = (bf16[2,544,128]{2,1,0:T(8,128)(2,1)S(1)}, bf16[2,544,128]{2,1,0:T(8,128)(2,1)S(1)}, u32[]{:S(2)}, u32[]{:S(2)}) collective-permute-start(bf16[2,544,128]{2,1,0:T(8,128)(2,1)S(1)} %get-tuple-element.35), channel_id=1, source_target_pairs={{0,6},{2,4},{4,2},{6,0},{8,14},{10,12},{12,10},{14,8},{1,7},{3,5},... | collective-permute-start | bytes 835592 | tf_op jit(solution)/shard_map/ppermute | solution.py:491
  45.5 10.2 %early.3 = (f32[4,256,1024]{2,1,0:T(8,128)S(1)}, bf16[4,256,128]{2,1,0:T(8,128)(2,1)S(1)}, f32[4,16,256]{2,1,0:T(8,128)S(1)}, f32[4,256,256]{2,1,0:T(8,128)S(1)}) custom-call(bf16[2,256,4096]{2,1,0:T(8,128)(2,1)} %refs_1_.7, bf16[2,256,512]{2,1,0:T(8,128)(2,1)} %refs_2_.9, bf16[2,256,512]{2,1,0:T(8,128)(2,1)} %refs_3_.7, f32[2,64,256]{2,1,0:T(8,128)} %refs_3_.5, ...), custom_call_target="tpu_custom_call" | custom-call | flops 1 | bytes 1 | tf_op jit(solution)/shard_map/early/pallas_call | solution.py:583
  55.7 4.5 %collective-permute-done.7.refs_2_ = bf16[4,512,128]{2,1,0:T(8,128)(2,1)S(1)} collective-permute-done((bf16[4,512,128]{2,1,0:T(8,128)(2,1)S(1)}, bf16[4,512,128]{2,1,0:T(8,128)(2,1)S(1)}, u32[]{:S(2)}, u32[]{:S(2)}) %collective-permute-start.7) | collective-permute-done | bytes 524320 | tf_op jit(solution)/shard_map/ppermute | solution.py:491
  60.2 2.5 %pick_states.3 = (bf16[2,512,128]{2,1,0:T(8,128)(2,1)S(1)}, bf16[2,512,128]{2,1,0:T(8,128)(2,1)S(1)}, bf16[2,512,128]{2,1,0:T(8,128)(2,1)S(1)}, bf16[2,512,128]{2,1,0:T(8,128)(2,1)S(1)}) custom-call(s32[8]{0:T(128)S(1)} %get-tuple-element.47.refs_11_.refs_0_, bf16[4,1056,128]{2,1,0:T(8,128)(2,1)S(1)} %all-to-all-done.refs_0_.refs_1_, ...), custom_call_target="tpu_custom_call" | custom-call | flops 1 | bytes 1 | tf_op jit(solution)/shard_map/pick_states/pallas_call | solution.py:557
  62.7 1.5 %collective-permute-start.8 = (bf16[2,512,128]{2,1,0:T(8,128)(2,1)S(1)}, bf16[2,512,128]{2,1,0:T(8,128)(2,1)S(1)}, u32[]{:S(2)}, u32[]{:S(2)}) collective-permute-start(bf16[2,512,128]{2,1,0:T(8,128)(2,1)S(1)} %get-tuple-element.38), channel_id=1, source_target_pairs={{0,2},{2,0},{4,6},{6,4},{8,10},{10,8},{12,14},{14,12},{1,3},{3,1},... | collective-permute-start | bytes 786440 | tf_op jit(solution)/shard_map/ppermute | solution.py:491
  64.3 0.0 collective-permute-start.9
  64.3 0.0 collective-permute-done.4.refs_8_.refs_12_
  64.3 2.0 %collective-permute-start.10 = (bf16[2,512,128]{2,1,0:T(8,128)(2,1)S(1)}, bf16[2,512,128]{2,1,0:T(8,128)(2,1)S(1)}, u32[]{:S(2)}, u32[]{:S(2)}) collective-permute-start(bf16[2,512,128]{2,1,0:T(8,128)(2,1)S(1)} %get-tuple-element.40), channel_id=1, source_target_pairs={{0,6},{2,4},{4,2},{6,0},{8,14},{10,12},{12,10},{14,8},{1,7},{3,5},... | collective-permute-start | bytes 786440 | tf_op jit(solution)/shard_map/ppermute | solution.py:491
  66.3 0.0 collective-permute-done.5.refs_9_.refs_13_
  66.3 0.3 collective-permute-done.6.refs_10_.refs_14_
  66.6 0.0 copy-done.1
  66.6 5.7 %late.2.refs_23_ = bf16[2,256,4096]{2,1,0:T(8,128)(2,1)} custom-call(s32[1]{0:T(128)} %bitcast.place_ref.refs_0_, bf16[2,256,4096]{2,1,0:T(8,128)(2,1)} %refs_1_.7, bf16[2,256,512]{2,1,0:T(8,128)(2,1)} %refs_2_.9, bf16[2,256,512]{2,1,0:T(8,128)(2,1)} %refs_3_.7, f32[1,4096]{1,0:T(1,128)S(1)} %broadcast_in_dim_reshape.3.refs_6_.refs_4_, f32[4,4096]{1,0:T(4,128)} %refs_5_.3, ...), custom_call_target="tpu_custom_call" | custom-call | flops 1 | bytes 1 | tf_op jit(solution)/shard_map/late/pallas_call | solution.py:641
  72.3 1.1 %collective-permute-done.8.refs_12_ = bf16[2,512,128]{2,1,0:T(8,128)(2,1)S(1)} collective-permute-done((bf16[2,512,128]{2,1,0:T(8,128)(2,1)S(1)}, bf16[2,512,128]{2,1,0:T(8,128)(2,1)S(1)}, u32[]{:S(2)}, u32[]{:S(2)}) %collective-permute-start.8) | collective-permute-done | bytes 262176 | tf_op jit(solution)/shard_map/ppermute | solution.py:491
  73.4 0.1 collective-permute-done.9.refs_13_
  73.5 4.3 %collective-permute-done.10.refs_14_ = bf16[2,512,128]{2,1,0:T(8,128)(2,1)S(1)} collective-permute-done((bf16[2,512,128]{2,1,0:T(8,128)(2,1)S(1)}, bf16[2,512,128]{2,1,0:T(8,128)(2,1)S(1)}, u32[]{:S(2)}, u32[]{:S(2)}) %collective-permute-start.10) | collective-permute-done | bytes 262176 | tf_op jit(solution)/shard_map/ppermute | solution.py:491
  77.8 5.7 %late.3 = bf16[2,256,4096]{2,1,0:T(8,128)(2,1)} custom-call(s32[1]{0:T(128)} %bitcast.place_ref.refs_0_, bf16[2,256,4096]{2,1,0:T(8,128)(2,1)} %refs_1_.7, bf16[2,256,512]{2,1,0:T(8,128)(2,1)} %refs_2_.9, bf16[2,256,512]{2,1,0:T(8,128)(2,1)} %refs_3_.7, f32[1,4096]{1,0:T(1,128)S(1)} %broadcast_in_dim_reshape.3.refs_6_.refs_4_, ...), custom_call_target="tpu_custom_call", output_to_operand_aliasing={{}: (23, {})} | custom-call | flops 1 | bytes 1 | tf_op jit(solution)/shard_map/late/pallas_call | solution.py:641
  (8 shorter events, 0.1 us)
Async XLA Ops:
  0.0 16.0 %copy-start.2 = (f32[64]{0:T(128)S(1)}, f32[64]{0:T(128)}, u32[]{:S(2)}) copy-start(f32[64]{0:T(128)} %param.18) | copy-start | bytes 772
  0.0 16.0 %copy-start.3 = (f32[64]{0:T(128)S(1)}, f32[64]{0:T(128)}, u32[]{:S(2)}) copy-start(f32[64]{0:T(128)} %param.19) | copy-start | bytes 772
  0.0 16.1 %copy-start.4 = (f32[64]{0:T(128)S(1)}, f32[64]{0:T(128)}, u32[]{:S(2)}) copy-start(f32[64]{0:T(128)} %param.20) | copy-start | bytes 772
  0.0 16.3 %copy-start.5 = (s32[8]{0:T(128)S(1)}, s32[8]{0:T(128)}, u32[]{:S(2)}) copy-start(s32[8]{0:T(128)} %param.26) | copy-start | bytes 100
  0.0 16.5 %copy-start.6 = (s32[16]{0:T(128)S(1)}, s32[16]{0:T(128)}, u32[]{:S(2)}) copy-start(s32[16]{0:T(128)} %param.27) | copy-start | bytes 196
  2.8 34.1 %all-to-all-start = ((bf16[4,1056,128]{2,1,0:T(8,128)(2,1)}), bf16[4,1056,128]{2,1,0:T(8,128)(2,1)S(1)}, u32[]{:S(2)}, u32[]{:S(2)}) async-start(bf16[4,1056,128]{2,1,0:T(8,128)(2,1)} %get-tuple-element.26.refs_9_), calls=%async_computation | async-start | bytes 2162688 | tf_op jit(solution)/shard_map/all_to_all | solution.py:547
  8.1 21.0 %collective-permute-start = (bf16[544,128]{1,0:T(8,128)(2,1)}, bf16[544,128]{1,0:T(8,128)(2,1)S(1)}, u32[]{:S(2)}, u32[]{:S(2)}) collective-permute-start(bf16[544,128]{1,0:T(8,128)(2,1)} %get-tuple-element.27), channel_id=1, source_target_pairs={{0,8},{2,10},{4,12},{6,14},{8,0},{10,2},{12,4},{14,6},{1,9},{3,11}... | collective-permute-start | bytes 417800 | tf_op jit(solution)/shard_map/ppermute | solution.py:491
  10.7 18.4 %collective-permute-start.1 = (bf16[544,128]{1,0:T(8,128)(2,1)S(1)}, bf16[544,128]{1,0:T(8,128)(2,1)S(1)}, u32[]{:S(2)}, u32[]{:S(2)}) collective-permute-start(bf16[544,128]{1,0:T(8,128)(2,1)S(1)} %get-tuple-element.28), channel_id=1, source_target_pairs={{0,10},{2,8},{4,14},{6,12},{8,2},{10,0},{12,6},{14,4},{1,11},{3,9}... | collective-permute-start | bytes 417800 | tf_op jit(solution)/shard_map/ppermute | solution.py:491
  12.5 22.0 %collective-permute-start.2 = (bf16[544,128]{1,0:T(8,128)(2,1)S(1)}, bf16[544,128]{1,0:T(8,128)(2,1)S(1)}, u32[]{:S(2)}, u32[]{:S(2)}) collective-permute-start(bf16[544,128]{1,0:T(8,128)(2,1)S(1)} %get-tuple-element.29), channel_id=1, source_target_pairs={{0,12},{2,14},{4,8},{6,10},{8,4},{10,6},{12,0},{14,2},{1,13},{3,15... | collective-permute-start | bytes 417800 | tf_op jit(solution)/shard_map/ppermute | solution.py:491
  15.9 21.0 %collective-permute-start.3 = (bf16[544,128]{1,0:T(8,128)(2,1)S(1)}, bf16[544,128]{1,0:T(8,128)(2,1)S(1)}, u32[]{:S(2)}, u32[]{:S(2)}) collective-permute-start(bf16[544,128]{1,0:T(8,128)(2,1)S(1)} %get-tuple-element.30), channel_id=1, source_target_pairs={{0,14},{2,12},{4,10},{6,8},{8,6},{10,4},{12,2},{14,0},{1,15},{3,13... | collective-permute-start | bytes 417800 | tf_op jit(solution)/shard_map/ppermute | solution.py:491
  27.0 2.0 %copy-start = (f32[4,256,1024]{2,1,0:T(8,128)}, f32[4,256,1024]{2,1,0:T(8,128)S(1)}, u32[]{:S(2)}) copy-start(f32[4,256,1024]{2,1,0:T(8,128)S(1)} %get-tuple-element.43.refs_18_) | copy-start | bytes 12582916
  37.0 23.2 %collective-permute-start.7 = (bf16[4,512,128]{2,1,0:T(8,128)(2,1)S(1)}, bf16[4,512,128]{2,1,0:T(8,128)(2,1)S(1)}, u32[]{:S(2)}, u32[]{:S(2)}) collective-permute-start(bf16[4,512,128]{2,1,0:T(8,128)(2,1)S(1)} %chunk_b.1.refs_6_), channel_id=1, source_target_pairs={{0,8},{2,10},{4,12},{6,14},{8,0},{10,2},{12,4},{14,6},{1,9},{3,11}... | collective-permute-start | bytes 1572872 | tf_op jit(solution)/shard_map/ppermute | solution.py:491
  41.9 24.6 %copy-start.1 = (f32[4,256,1024]{2,1,0:T(8,128)S(1)}, f32[4,256,1024]{2,1,0:T(8,128)}, u32[]{:S(2)}) copy-start(f32[4,256,1024]{2,1,0:T(8,128)} %copy-done) | copy-start | bytes 12582916
  41.9 22.3 %collective-permute-start.4 = (bf16[2,544,128]{2,1,0:T(8,128)(2,1)S(1)}, bf16[2,544,128]{2,1,0:T(8,128)(2,1)S(1)}, u32[]{:S(2)}, u32[]{:S(2)}) collective-permute-start(bf16[2,544,128]{2,1,0:T(8,128)(2,1)S(1)} %get-tuple-element.33), channel_id=1, source_target_pairs={{0,2},{2,0},{4,6},{6,4},{8,10},{10,8},{12,14},{14,12},{1,3},{3,1},... | collective-permute-start | bytes 835592 | tf_op jit(solution)/shard_map/ppermute | solution.py:491
  42.4 23.9 %collective-permute-start.5 = (bf16[2,544,128]{2,1,0:T(8,128)(2,1)S(1)}, bf16[2,544,128]{2,1,0:T(8,128)(2,1)S(1)}, u32[]{:S(2)}, u32[]{:S(2)}) collective-permute-start(bf16[2,544,128]{2,1,0:T(8,128)(2,1)S(1)} %get-tuple-element.34), channel_id=1, source_target_pairs={{0,4},{2,6},{4,0},{6,2},{8,12},{10,14},{12,8},{14,10},{1,5},{3,7},... | collective-permute-start | bytes 835592 | tf_op jit(solution)/shard_map/ppermute | solution.py:491
  42.4 24.2 %collective-permute-start.6 = (bf16[2,544,128]{2,1,0:T(8,128)(2,1)S(1)}, bf16[2,544,128]{2,1,0:T(8,128)(2,1)S(1)}, u32[]{:S(2)}, u32[]{:S(2)}) collective-permute-start(bf16[2,544,128]{2,1,0:T(8,128)(2,1)S(1)} %get-tuple-element.35), channel_id=1, source_target_pairs={{0,6},{2,4},{4,2},{6,0},{8,14},{10,12},{12,10},{14,8},{1,7},{3,5},... | collective-permute-start | bytes 835592 | tf_op jit(solution)/shard_map/ppermute | solution.py:491
  62.7 10.7 %collective-permute-start.8 = (bf16[2,512,128]{2,1,0:T(8,128)(2,1)S(1)}, bf16[2,512,128]{2,1,0:T(8,128)(2,1)S(1)}, u32[]{:S(2)}, u32[]{:S(2)}) collective-permute-start(bf16[2,512,128]{2,1,0:T(8,128)(2,1)S(1)} %get-tuple-element.38), channel_id=1, source_target_pairs={{0,2},{2,0},{4,6},{6,4},{8,10},{10,8},{12,14},{14,12},{1,3},{3,1},... | collective-permute-start | bytes 786440 | tf_op jit(solution)/shard_map/ppermute | solution.py:491
  64.3 9.2 %collective-permute-start.9 = (bf16[2,512,128]{2,1,0:T(8,128)(2,1)S(1)}, bf16[2,512,128]{2,1,0:T(8,128)(2,1)S(1)}, u32[]{:S(2)}, u32[]{:S(2)}) collective-permute-start(bf16[2,512,128]{2,1,0:T(8,128)(2,1)S(1)} %get-tuple-element.39), channel_id=1, source_target_pairs={{0,4},{2,6},{4,0},{6,2},{8,12},{10,14},{12,8},{14,10},{1,5},{3,7},... | collective-permute-start | bytes 786440 | tf_op jit(solution)/shard_map/ppermute | solution.py:491
  64.3 13.5 %collective-permute-start.10 = (bf16[2,512,128]{2,1,0:T(8,128)(2,1)S(1)}, bf16[2,512,128]{2,1,0:T(8,128)(2,1)S(1)}, u32[]{:S(2)}, u32[]{:S(2)}) collective-permute-start(bf16[2,512,128]{2,1,0:T(8,128)(2,1)S(1)} %get-tuple-element.40), channel_id=1, source_target_pairs={{0,6},{2,4},{4,2},{6,0},{8,14},{10,12},{12,10},{14,8},{1,7},{3,5},... | collective-permute-start | bytes 786440 | tf_op jit(solution)/shard_map/ppermute | solution.py:491

commit v11 on v10

--- a/solution.py
+++ b/solution.py
@@ -7,7 +7,7 @@
 from jax.experimental.pallas import tpu as pltpu
 from jax.sharding import PartitionSpec as P
 
-VMEM_LIMIT = 16 * 1024 * 1024
+VMEM_LIMIT = 12 * 1024 * 1024
 SPLIT = (8, 8)
 FIX = 16
 LOG2_E = 1.4426950408889634
@@ -36,12 +36,12 @@
 
 
 def early_kernel(
-    x_ref, b_ref, c_ref, dt_ref, bias_ref, alog_ref, skip_ref, taps_x_ref, taps_bc_ref,
+    base, x_ref, b_ref, c_ref, dt_ref, bias_ref, alog_ref, skip_ref, taps_x_ref, taps_bc_ref,
     mixed_ref, c_out_ref, column_ref, first_ref, padded,
 ):
     length, wide = x_ref.shape[1:]
     heads = dt_ref.shape[1]
-    q = pl.program_id(0)
+    q = base + pl.program_id(0)
     width = wide // heads
     half = length // 2
 
@@ -205,30 +205,6 @@
                 pieces.append(jnp.zeros((spare, 128), jnp.float32))
                 out_ref[start : start + tailed[j]] = jnp.concatenate(pieces).astype(jnp.bfloat16)
                 start += tailed[j]
-
-
-def pick_rows_kernel(start, slots_ref, inside_ref, *refs):
-    crossed, outs, sems = refs[:-5], refs[-5:-1], refs[-1]
-    kids, rows = outs[0].shape[:2]
-    held = [inside_ref.at[source, pl.ds(start, rows)] for source in range(4)]
-    held += list(crossed) if len(crossed) == 4 else [crossed[0].at[source] for source in range(4)]
-    for j, out in enumerate(outs):
-        for kid in range(kids):
-            for source in range(8):
-
-                @pl.when(slots_ref[j * kids + kid] == source)
-                def _(source=source, out=out, j=j, kid=kid):
-                    pltpu.make_async_copy(held[source], out.at[kid], sems.at[j, kid]).start()
-
-    for j, out in enumerate(outs):
-        for kid in range(kids):
-            pltpu.make_async_copy(held[0], out.at[kid], sems.at[j, kid]).wait()
-
-
-def slice_kernel(start, in_ref, out_ref, sem):
-    copy = pltpu.make_async_copy(in_ref.at[:, pl.ds(start, out_ref.shape[1])], out_ref, sem)
-    copy.start()
-    copy.wait()
 
 
 def within_kernel(
@@ -473,14 +449,11 @@
 
     me = lax.axis_index("batch")
     parent = parent_of(counts, order)
-    side = me // 4 * 4
     child = (jnp.arange(4 * kids, dtype=jnp.int32) // kids ^ me) * kids
     child = child + jnp.arange(4 * kids, dtype=jnp.int32) % kids
     catalog = jnp.arange(4 * 2 * kids, dtype=jnp.int32)
     owner = jnp.sum(jnp.where(child[:, None] == catalog[None, :], parent[None, :], 0), axis=1)
-    here = owner // 4 * 4 == side
-    slots_a = jnp.where(here, owner % 4, 4 + (owner ^ me) % 4)
-    slots_b = jnp.where(here, owner % 4, 4 + owner % 4)
+    slots = owner ^ me
     place = (me % 4).astype(jnp.int32)[None]
 
     state = stay(par_state.reshape(groups, per_group, width, size))
@@ -490,109 +463,123 @@
     def swap(value, r):
         return lax.ppermute(value, "batch", perm=[(i, i ^ r) for i in range(8)])
 
-    def cast():
-        rows = per_group * width + tail_lines
-        rows_a = SPLIT[0] * width + tail_lines
+    def cast(quarters, chunks, stacked, tokens):
+        part = sum(SPLIT[k] for k in chunks)
+        rows = part * width + tail_lines
+        block = [SPLIT[k] for k in chunks]
 
         def kernel(place_ref, *refs):
-            whole_ref, outs = refs[-5], refs[-4:]
-            for q in range(groups):
-                cast_kernel(2, [tail_lines], reach, lines, *refs[4 * q : 4 * q + 4], whole_ref.at[q])
-            for j, out_ref in enumerate(outs):
-                out_ref[...] = whole_ref[place_ref[0] ^ j, :rows_a]
+            count = len(chunks) + 2
+            ins, outs = refs[: count * 4], refs[count * 4 :]
+            for n in range(4):
+                out_ref = outs[0].at[n] if stacked else outs[n]
+                cast_kernel(
+                    len(chunks), [tail_lines], reach, lines, *ins[count * n : count * n + count], out_ref
+                )
 
         operands, specs = [], []
-        for q in range(groups):
-            operands += [state, state, x_tails, bc_tails]
+        for n in range(4):
+            which = (lambda i, p, n=n: n) if stacked else (lambda i, p, n=n: p[0] ^ n)
+            for k in chunks:
+                operands.append(state)
+                specs.append(
+                    pl.BlockSpec(
+                        (1, SPLIT[k], width, size),
+                        lambda i, p, w=which, at=offsets[k] // SPLIT[k]: (w(i, p), at, 0, 0),
+                    )
+                )
+            operands += [x_tails, bc_tails]
             specs += [
-                pl.BlockSpec((1, SPLIT[0], width, size), lambda i, p, q=q: (q, 0, 0, 0)),
-                pl.BlockSpec((1, SPLIT[1], width, size), lambda i, p, q=q: (q, 1, 0, 0)),
-                pl.BlockSpec((1, reach, wide), lambda i, p, q=q: (0, 0, q)),
-                pl.BlockSpec((1, reach, 2, size), lambda i, p, q=q: (0, 0, 0, q)),
+                pl.BlockSpec((1, reach, wide), lambda i, p, w=which: (0, 0, w(i, p))),
+                pl.BlockSpec((1, reach, 2, size), lambda i, p, w=which: (0, 0, 0, w(i, p))),
             ]
+        shapes = [(4, rows, size)] if stacked else [(rows, size)] * 4
         return pl.pallas_call(
-            kernel,
+            functools.partial(drop_tokens, kernel, 1 + len(operands), len(tokens)),
             grid_spec=pltpu.PrefetchScalarGridSpec(
                 num_scalar_prefetch=1,
                 grid=(1,),
-                in_specs=specs,
-                out_specs=[pl.BlockSpec((groups, rows, size), lambda i, p: (0, 0, 0))]
-                + [pl.BlockSpec(memory_space=pltpu.VMEM)] * 4,
+                in_specs=specs + [anywhere] * len(tokens),
+                out_specs=[pl.BlockSpec(memory_space=pltpu.VMEM)] * len(shapes),
             ),
-            out_shape=[jax.ShapeDtypeStruct((groups, rows, size), jnp.bfloat16)]
-            + [pltpu.VMEM((rows_a, size), jnp.bfloat16)] * 4,
+            out_shape=[pltpu.VMEM(shape, jnp.bfloat16) for shape in shapes],
             compiler_params=params,
             cost_estimate=small,
             name="cast_states",
-        )(place, *operands)
-
-    def chunk_b(inside, tokens):
-        rows = SPLIT[1] * width
+        )(place, *operands, *tokens)
+
+    def rearrange(scalars, sources, moves, shapes, tokens, name):
+        def kernel(scalars_ref, *refs):
+            held, outs, sems = refs[: len(sources)], refs[len(sources) : -1], refs[-1]
+
+            def copy(move, source):
+                out, at, _, _ = moves[move]
+                number, take = source
+                ref = held[number].at[take] if take is not None else held[number]
+                target = outs[out].at[at] if at is not None else outs[out]
+                return pltpu.make_async_copy(ref, target, sems.at[move])
+
+            for move, (_, _, scalar, choices) in enumerate(moves):
+                if scalar is None:
+                    copy(move, choices[0]).start()
+                    continue
+                for value, source in enumerate(choices):
+
+                    @pl.when(scalars_ref[scalar] == value)
+                    def _(move=move, source=source):
+                        copy(move, source).start()
+
+            for move in range(len(moves)):
+                copy(move, moves[move][3][0]).wait()
+
         return pl.pallas_call(
-            functools.partial(
-                drop_tokens, functools.partial(slice_kernel, inside.shape[1] - rows), 1, len(tokens)
-            ),
-            grid=(1,),
-            in_specs=[anywhere]
-            + [anywhere] * len(tokens),
-            out_specs=pl.BlockSpec(memory_space=pltpu.VMEM),
-            out_shape=pltpu.VMEM((4, rows, size), jnp.bfloat16),
-            scratch_shapes=[pltpu.SemaphoreType.DMA],
-            compiler_params=params,
-            cost_estimate=small,
-            name="chunk_b",
-        )(inside, *tokens)
-
-    def gather_half(value):
-        return lax.all_to_all(
-            value,
-            "batch",
-            split_axis=0,
-            concat_axis=0,
-            tiled=True,
-            axis_index_groups=[[0, 1, 2, 3], [4, 5, 6, 7]],
-        )
-
-    def pick(rows, start, slots, inside, crossed, tokens):
-        picked = pl.pallas_call(
-            functools.partial(
-                drop_tokens,
-                functools.partial(pick_rows_kernel, start),
-                2 + len(crossed),
-                len(tokens),
-            ),
+            functools.partial(drop_tokens, kernel, 1 + len(sources), len(tokens)),
             grid_spec=pltpu.PrefetchScalarGridSpec(
                 num_scalar_prefetch=1,
                 grid=(1,),
-                in_specs=[anywhere] * (1 + len(crossed) + len(tokens)),
-                out_specs=[pl.BlockSpec(memory_space=pltpu.VMEM)] * 4,
-                scratch_shapes=[pltpu.SemaphoreType.DMA((4, kids))],
+                in_specs=[anywhere] * (len(sources) + len(tokens)),
+                out_specs=[pl.BlockSpec(memory_space=pltpu.VMEM)] * len(shapes),
+                scratch_shapes=[pltpu.SemaphoreType.DMA((len(moves),))],
             ),
-            out_shape=[pltpu.VMEM((kids, rows, size), jnp.bfloat16)] * 4,
+            out_shape=[pltpu.VMEM(shape, jnp.bfloat16) for shape in shapes],
             compiler_params=params,
             cost_estimate=small,
-            name="pick_states",
-        )(slots, inside, *crossed, *tokens)
+            name=name,
+        )(scalars, *sources, *tokens)
+
+    def pick(rows, sources, choices, tokens):
+        moves = [
+            (j, kid, j * kids + kid, choices) for j in range(4) for kid in range(kids)
+        ]
+        picked = rearrange(
+            slots, sources, moves, [(kids, rows, size)] * 4, tokens, "pick_states"
+        )
         return [picked[0]] + [swap(picked[j], j) for j in range(1, 4)]
 
-    def early(c, tokens):
-        at = lambda q: (c, 0, q)
+    def early(c, piece, before, tokens):
+        per = groups // 2
+        at = lambda q: (c, 0, per * piece + q)
         operands = [
             x_in, b_in, c_in, dt_in, dt_bias[:, None], a_log[:, None], skip_row, conv_x, conv_bc
         ]
+        keep = len(operands)
+        tokens = list(tokens) + [keep_in_vmem(a) for a in before]
+        first = keep + len(tokens) - len(before)
         return pl.pallas_call(
-            functools.partial(drop_tokens, early_kernel, len(operands), len(tokens)),
-            grid=(groups,),
+            functools.partial(
+                drop_tokens, functools.partial(early_kernel, per * piece), keep, len(tokens)
+            ),
+            grid=(per,),
             in_specs=[
                 pl.BlockSpec((1, length, wide), at),
                 pl.BlockSpec((1, length, size), at),
                 pl.BlockSpec((1, length, size), at),
-                pl.BlockSpec((1, per_group, length), lambda q: (c, q, 0)),
-                pl.BlockSpec((per_group, 1), lambda q: (q, 0)),
-                pl.BlockSpec((per_group, 1), lambda q: (q, 0)),
-                pl.BlockSpec((1, wide), lambda q: (0, q)),
-                pl.BlockSpec((taps, wide), lambda q: (0, q)),
-                pl.BlockSpec((2, taps, size), lambda q: (0, 0, q)),
+                pl.BlockSpec((1, per_group, length), lambda q: (c, per * piece + q, 0)),
+                pl.BlockSpec((per_group, 1), lambda q: (per * piece + q, 0)),
+                pl.BlockSpec((per_group, 1), lambda q: (per * piece + q, 0)),
+                pl.BlockSpec((1, wide), lambda q: (0, per * piece + q)),
+                pl.BlockSpec((taps, wide), lambda q: (0, per * piece + q)),
+                pl.BlockSpec((2, taps, size), lambda q: (0, 0, per * piece + q)),
                 *[anywhere] * len(tokens),
             ],
             out_specs=[pl.BlockSpec(memory_space=pltpu.VMEM)] * 4,
@@ -602,6 +589,7 @@
                 pltpu.VMEM((groups, per_group, length), jnp.float32),
                 pltpu.VMEM((groups, length, per_group * FIX), jnp.float32),
             ],
+            input_output_aliases={first + i: i for i in range(len(before))},
             scratch_shapes=[pltpu.VMEM((8 + length, size), jnp.float32)],
             compiler_params=params,
             cost_estimate=small,
@@ -661,15 +649,31 @@
 
     skip_row = jnp.repeat(d_skip, width)[None, :]
     rows = [SPLIT[0] * width + tail_lines, SPLIT[1] * width]
-    whole, *sent_a = cast()
-    crossed_a = [swap(sent_a[j], j + 4) for j in range(4)]
-    inside = gather_half(whole)
-    parts = [early(0, [whole, slots_a, slots_b])]
-    sent_b = chunk_b(inside, [parts[0][1], *crossed_a])
+    chunk_a, chunk_b = pl.ds(0, rows[0]), pl.ds(rows[0], rows[1])
+
+    (sent_a,) = cast(range(4), [0], True, [])
+    crossed_a = swap(sent_a, 4)
+    own = cast(range(4), [0, 1], False, [sent_a])
+    inside = [own[0]] + [swap(own[j], j) for j in range(1, 4)]
+    first = early(0, 0, [], [own[0], slots])
+    first = early(0, 1, first, [])
+    second = early(1, 0, [], [first[1]])
+    moves = [(0, j, None, [(j, chunk_b)]) for j in range(4)]
+    (sent_b,) = rearrange(
+        place, inside, moves, [(4, rows[1], size)], [second[1], crossed_a], "stack_b"
+    )
     crossed_b = swap(sent_b, 4)
-    states_a = pick(rows[0], 0, slots_a, inside, crossed_a, [sent_b])
-    parts.append(early(1, [states_a[0]]))
-    states_b = pick(rows[1], rows[0], slots_b, inside, [crossed_b], [parts[1][1]])
+    moves = [(j, None, 0, [(0, n ^ j) for n in range(4)]) for j in range(4)]
+    spread = rearrange(
+        place, [crossed_a], moves, [(rows[0], size)] * 4, [sent_b], "split_a"
+    )
+    spread = [spread[0]] + [swap(spread[j], j) for j in range(1, 4)]
+    second = early(1, 1, second, [spread[0]])
+    choices = [(j, chunk_a) for j in range(4)] + [(4 + j, None) for j in range(4)]
+    states_a = pick(rows[0], [*inside, *spread], choices, [second[1]])
+    choices = [(j, chunk_b) for j in range(4)] + [(4, j) for j in range(4)]
+    states_b = pick(rows[1], [*inside, crossed_b], choices, [states_a[0]])
+    parts = [first, second]
     result = late(0, states_a, states_a, parts, None, [states_b[0]])
     return late(1, states_b, states_a, parts, result, [])
 

time: 83.7 us -> 87.9 us (1.050)
  Pallas kernels: 39.7 us -> 43.7 us
  local copies, waits for them, and re-layouts: 2.38 us -> 0.39 us
  starting transfers between devices: 22.6 us -> 24.5 us
    ppermute x11 -> x14, starting transfers between devices: 17.4 us -> 24.5 us  [swap(): return lax.ppermute(value, 'batch', perm=[(i, i ^ r) for i in range(8)])]
    all_to_all x1 -> x0, starting transfers between devices: 5.26 us -> none  [gather_half(): lax.all_to_all(value, 'batch', split_axis=0, concat_axis=0, tiled=True, a...]
    pallas_call x6 -> x10, Pallas kernels: 28.3 us -> 32.3 us  [the longest x4 22.7 us: early(): pl.pallas_call(functools.partial(drop_tokens, functools.partial(early_ker...]
    unnamed x14 -> x10, local copies, waits for them, and re-layouts: 2.03 us -> 0.03 us
    ppermute x11 -> x14, waiting for transfers between devices: 18.2 us -> 18.5 us  [swap(): return lax.ppermute(value, 'batch', perm=[(i, i ^ r) for i in range(8)])]
  transfers between devices with their start and end apart: 12 -> 14, of which waited for: 7 -> 6; matrix products, arithmetic and copies ran while one was open for 1% -> 1% of each run, Pallas kernels for 37% -> 41%
where the time goes in v11:
time: 87.9 us; the launch traced here: 87.7 us
  Pallas kernels  43.7 us (50%)
  starting transfers between devices  24.5 us (28%)
  waiting for transfers between devices  18.5 us (21%)
    ppermute x14, starting transfers between devices, swap(): return lax.ppermute(value, 'batch', perm=[(i, i ^ r) for i in range(8)])  24.5 us
    pallas_call x4, Pallas kernels, early(): pl.pallas_call(functools.partial(drop_tokens, functools.partial(early_ker...  22.7 us
    ppermute x14, waiting for transfers between devices, swap(): return lax.ppermute(value, 'batch', perm=[(i, i ^ r) for i in range(8)])  18.5 us
    pallas_call x2, Pallas kernels, late(): pl.pallas_call(functools.partial(drop_tokens, functools.partial(late_kern...  11.4 us
    pallas_call x4, Pallas kernels, rearrange(): pl.pallas_call(functools.partial(drop_tokens, kernel, 1 + len(sources), l...  6.6 us
    pallas_call x2, Pallas kernels, cast(): pl.pallas_call(functools.partial(drop_tokens, kernel, 1 + len(operands),...  3.04 us
  transfers between devices with their start and end apart: 14, of which 6 were waited for; matrix products, arithmetic and copies ran while one was open for 1% of the time, Pallas kernels for 41%

profile of v11, /device:TPU:0, one launch (start us, length us, event | category | flops | bytes accessed | tf_op | source)
XLA Modules:
  0.0 87.7 jit_solution(13077002129579221060)
XLA Ops:
  0.0 1.3 %cast_states.2.refs_17_ = bf16[4,544,128]{2,1,0:T(8,128)(2,1)S(1)} custom-call(s32[1]{0:T(128)} %bitcast.refs_0_, f32[4,16,64,128]{3,2,1,0:T(8,128)} %bitcast.5, bf16[1,3,4096]{2,1,0:T(4,128)(2,1)} %refs_15_.1, bf16[1,3,2,512]{3,2,1,0:T(2,128)(2,1)} %bitcast.17, f32[4,16,64,128]{3,2,1,0:T(8,128)} %bitcast.6, bf16[1,3,4096]{2,1,0:T(4,128)(2,1)} %refs_15_.1, ...), custom_call_target="tpu_custom_call" | custom-call | flops 1 | bytes 1 | tf_op jit(solution)/shard_map/cast_states/pallas_call | solution.py:497
  1.4 0.0 copy-start.3
  1.4 0.0 copy-start.4
  1.4 0.0 copy-start
  1.4 0.0 copy-start.1
  1.4 0.0 copy-start.2
  1.4 4.1 %collective-permute-start.3 = (bf16[4,544,128]{2,1,0:T(8,128)(2,1)S(1)}, bf16[4,544,128]{2,1,0:T(8,128)(2,1)S(1)}, u32[]{:S(2)}, u32[]{:S(2)}) collective-permute-start(bf16[4,544,128]{2,1,0:T(8,128)(2,1)S(1)} %cast_states.2.refs_17_), channel_id=1, source_target_pairs={{0,8},{2,10},{4,12},{6,14},{8,0},{10,2},{12,4},{14,6},{1,9},{3,11}... | collective-permute-start | bytes 1671176 | tf_op jit(solution)/shard_map/ppermute | solution.py:464
  5.5 1.7 %cast_states.3 = (bf16[1056,128]{1,0:T(8,128)(2,1)S(1)}, bf16[1056,128]{1,0:T(8,128)(2,1)S(1)}, bf16[1056,128]{1,0:T(8,128)(2,1)S(1)}, bf16[1056,128]{1,0:T(8,128)(2,1)S(1)}) custom-call(s32[1]{0:T(128)} %bitcast.refs_0_, f32[4,16,64,128]{3,2,1,0:T(8,128)} %bitcast.9, f32[4,16,64,128]{3,2,1,0:T(8,128)} %bitcast.10, bf16[1,3,4096]{2,1,0:T(4,128)(2,1)} %refs_15_.1, ...), custom_call_target="tpu_custom_call" | custom-call | flops 1 | bytes 1 | tf_op jit(solution)/shard_map/cast_states/pallas_call | solution.py:497
  7.2 1.6 %collective-permute-start = (bf16[1056,128]{1,0:T(8,128)(2,1)S(1)}, bf16[1056,128]{1,0:T(8,128)(2,1)S(1)}, u32[]{:S(2)}, u32[]{:S(2)}) collective-permute-start(bf16[1056,128]{1,0:T(8,128)(2,1)S(1)} %get-tuple-element.38), channel_id=1, source_target_pairs={{0,2},{2,0},{4,6},{6,4},{8,10},{10,8},{12,14},{14,12},{1,3},{3,1},... | collective-permute-start | bytes 811016 | tf_op jit(solution)/shard_map/ppermute | solution.py:464
  8.8 1.6 %collective-permute-start.1 = (bf16[1056,128]{1,0:T(8,128)(2,1)S(1)}, bf16[1056,128]{1,0:T(8,128)(2,1)S(1)}, u32[]{:S(2)}, u32[]{:S(2)}) collective-permute-start(bf16[1056,128]{1,0:T(8,128)(2,1)S(1)} %get-tuple-element.39), channel_id=1, source_target_pairs={{0,4},{2,6},{4,0},{6,2},{8,12},{10,14},{12,8},{14,10},{1,5},{3,7},... | collective-permute-start | bytes 811016 | tf_op jit(solution)/shard_map/ppermute | solution.py:464
  10.4 0.4 collective-permute-start.2
  10.8 0.1 select_reduce_fusion.1
  10.9 0.1 convert_reduce_fusion
  11.0 0.2 select_reduce_fusion
  11.2 0.1 copy.36.refs_4_
  11.3 0.1 copy.37.refs_5_
  11.4 0.1 broadcast_in_dim.33
  11.4 0.1 broadcast_in_dim_reshape.3.refs_6_.refs_4_
  11.6 5.7 %early.4 = (f32[4,256,1024]{2,1,0:T(8,128)S(1)}, bf16[4,256,128]{2,1,0:T(8,128)(2,1)S(1)}, f32[4,16,256]{2,1,0:T(8,128)S(1)}, f32[4,256,256]{2,1,0:T(8,128)S(1)}) custom-call(bf16[2,256,4096]{2,1,0:T(8,128)(2,1)} %refs_1_.11, bf16[2,256,512]{2,1,0:T(8,128)(2,1)} %refs_2_.13, bf16[2,256,512]{2,1,0:T(8,128)(2,1)} %refs_3_.13, f32[2,64,256]{2,1,0:T(8,128)} %refs_3_.11, ...), custom_call_target="tpu_custom_call" | custom-call | flops 1 | bytes 1 | tf_op jit(solution)/shard_map/early/pallas_call | solution.py:568
  17.2 5.7 %early.5 = (f32[4,256,1024]{2,1,0:T(8,128)S(1)}, bf16[4,256,128]{2,1,0:T(8,128)(2,1)S(1)}, f32[4,16,256]{2,1,0:T(8,128)S(1)}, f32[4,256,256]{2,1,0:T(8,128)S(1)}) custom-call(bf16[2,256,4096]{2,1,0:T(8,128)(2,1)} %refs_1_.11, bf16[2,256,512]{2,1,0:T(8,128)(2,1)} %refs_2_.13, ...), custom_call_target="tpu_custom_call", output_to_operand_aliasing={{0}: (9, {}), {1}: (10, {}), {2}: (11, {}), {3}: (12, {})} | custom-call | flops 1 | bytes 1 | tf_op jit(solution)/shard_map/early/pallas_call | solution.py:568
  22.9 5.7 %early.6 = (f32[4,256,1024]{2,1,0:T(8,128)S(1)}, bf16[4,256,128]{2,1,0:T(8,128)(2,1)S(1)}, f32[4,16,256]{2,1,0:T(8,128)S(1)}, f32[4,256,256]{2,1,0:T(8,128)S(1)}) custom-call(bf16[2,256,4096]{2,1,0:T(8,128)(2,1)} %refs_1_.11, bf16[2,256,512]{2,1,0:T(8,128)(2,1)} %refs_2_.13, bf16[2,256,512]{2,1,0:T(8,128)(2,1)} %refs_3_.13, f32[2,64,256]{2,1,0:T(8,128)} %refs_3_.11, ...), custom_call_target="tpu_custom_call" | custom-call | flops 1 | bytes 1 | tf_op jit(solution)/shard_map/early/pallas_call | solution.py:568
  28.6 0.0 collective-permute-done.refs_2_
  28.6 0.0 collective-permute-done.1.refs_3_
  28.6 4.4 %collective-permute-done.2.refs_4_ = bf16[1056,128]{1,0:T(8,128)(2,1)S(1)} collective-permute-done((bf16[1056,128]{1,0:T(8,128)(2,1)S(1)}, bf16[1056,128]{1,0:T(8,128)(2,1)S(1)}, u32[]{:S(2)}, u32[]{:S(2)}) %collective-permute-start.2) | collective-permute-done | bytes 270368 | tf_op jit(solution)/shard_map/ppermute | solution.py:464
  33.0 0.0 collective-permute-done.3.refs_6_.refs_1_
  33.0 0.7 stack_b.1.refs_2_
  33.7 0.6 collective-permute-start.10
  34.3 0.8 split_a.1
  35.1 1.1 %collective-permute-start.4 = (bf16[544,128]{1,0:T(8,128)(2,1)S(1)}, bf16[544,128]{1,0:T(8,128)(2,1)S(1)}, u32[]{:S(2)}, u32[]{:S(2)}) collective-permute-start(bf16[544,128]{1,0:T(8,128)(2,1)S(1)} %get-tuple-element.48), channel_id=1, source_target_pairs={{0,2},{2,0},{4,6},{6,4},{8,10},{10,8},{12,14},{14,12},{1,3},{3,1},... | collective-permute-start | bytes 417800 | tf_op jit(solution)/shard_map/ppermute | solution.py:464
  36.2 2.9 %collective-permute-start.5 = (bf16[544,128]{1,0:T(8,128)(2,1)S(1)}, bf16[544,128]{1,0:T(8,128)(2,1)S(1)}, u32[]{:S(2)}, u32[]{:S(2)}) collective-permute-start(bf16[544,128]{1,0:T(8,128)(2,1)S(1)} %get-tuple-element.49), channel_id=1, source_target_pairs={{0,4},{2,6},{4,0},{6,2},{8,12},{10,14},{12,8},{14,10},{1,5},{3,7},... | collective-permute-start | bytes 417800 | tf_op jit(solution)/shard_map/ppermute | solution.py:464
  39.1 0.0 collective-permute-start.6
  39.1 5.6 %early.7 = (f32[4,256,1024]{2,1,0:T(8,128)S(1)}, bf16[4,256,128]{2,1,0:T(8,128)(2,1)S(1)}, f32[4,16,256]{2,1,0:T(8,128)S(1)}, f32[4,256,256]{2,1,0:T(8,128)S(1)}) custom-call(bf16[2,256,4096]{2,1,0:T(8,128)(2,1)} %refs_1_.11, bf16[2,256,512]{2,1,0:T(8,128)(2,1)} %refs_2_.13, ...), custom_call_target="tpu_custom_call", output_to_operand_aliasing={{0}: (10, {}), {1}: (11, {}), {2}: (12, {}), {3}: (13, {})} | custom-call | flops 1 | bytes 1 | tf_op jit(solution)/shard_map/early/pallas_call | solution.py:568
  44.8 3.5 %collective-permute-done.5.refs_7_ = bf16[544,128]{1,0:T(8,128)(2,1)S(1)} collective-permute-done((bf16[544,128]{1,0:T(8,128)(2,1)S(1)}, bf16[544,128]{1,0:T(8,128)(2,1)S(1)}, u32[]{:S(2)}, u32[]{:S(2)}) %collective-permute-start.5) | collective-permute-done | bytes 139296 | tf_op jit(solution)/shard_map/ppermute | solution.py:464
  48.3 1.5 %collective-permute-done.6.refs_8_ = bf16[544,128]{1,0:T(8,128)(2,1)S(1)} collective-permute-done((bf16[544,128]{1,0:T(8,128)(2,1)S(1)}, bf16[544,128]{1,0:T(8,128)(2,1)S(1)}, u32[]{:S(2)}, u32[]{:S(2)}) %collective-permute-start.6) | collective-permute-done | bytes 139296 | tf_op jit(solution)/shard_map/ppermute | solution.py:464
  49.8 2.6 %pick_states.2 = (bf16[2,544,128]{2,1,0:T(8,128)(2,1)S(1)}, bf16[2,544,128]{2,1,0:T(8,128)(2,1)S(1)}, bf16[2,544,128]{2,1,0:T(8,128)(2,1)S(1)}, bf16[2,544,128]{2,1,0:T(8,128)(2,1)S(1)}) custom-call(s32[8]{0:T(128)S(1)} %broadcast_xor_fusion.refs_10_.refs_0_, bf16[1056,128]{1,0:T(8,128)(2,1)S(1)} %get-tuple-element.37.refs_9_.refs_1_, ...), custom_call_target="tpu_custom_call" | custom-call | flops 1 | bytes 1 | tf_op jit(solution)/shard_map/pick_states/pallas_call | solution.py:535
  52.4 1.5 %collective-permute-start.7 = (bf16[2,544,128]{2,1,0:T(8,128)(2,1)S(1)}, bf16[2,544,128]{2,1,0:T(8,128)(2,1)S(1)}, u32[]{:S(2)}, u32[]{:S(2)}) collective-permute-start(bf16[2,544,128]{2,1,0:T(8,128)(2,1)S(1)} %get-tuple-element.56), channel_id=1, source_target_pairs={{0,2},{2,0},{4,6},{6,4},{8,10},{10,8},{12,14},{14,12},{1,3},{3,1},... | collective-permute-start | bytes 835592 | tf_op jit(solution)/shard_map/ppermute | solution.py:464
  53.9 2.5 %collective-permute-start.8 = (bf16[2,544,128]{2,1,0:T(8,128)(2,1)S(1)}, bf16[2,544,128]{2,1,0:T(8,128)(2,1)S(1)}, u32[]{:S(2)}, u32[]{:S(2)}) collective-permute-start(bf16[2,544,128]{2,1,0:T(8,128)(2,1)S(1)} %get-tuple-element.57), channel_id=1, source_target_pairs={{0,4},{2,6},{4,0},{6,2},{8,12},{10,14},{12,8},{14,10},{1,5},{3,7},... | collective-permute-start | bytes 835592 | tf_op jit(solution)/shard_map/ppermute | solution.py:464
  56.4 0.9 %collective-permute-start.9 = (bf16[2,544,128]{2,1,0:T(8,128)(2,1)S(1)}, bf16[2,544,128]{2,1,0:T(8,128)(2,1)S(1)}, u32[]{:S(2)}, u32[]{:S(2)}) collective-permute-start(bf16[2,544,128]{2,1,0:T(8,128)(2,1)S(1)} %get-tuple-element.58), channel_id=1, source_target_pairs={{0,6},{2,4},{4,2},{6,0},{8,14},{10,12},{12,10},{14,8},{1,7},{3,5},... | collective-permute-start | bytes 835592 | tf_op jit(solution)/shard_map/ppermute | solution.py:464
  57.3 0.6 collective-permute-done.10.refs_5_
  57.9 2.5 %pick_states.3 = (bf16[2,512,128]{2,1,0:T(8,128)(2,1)S(1)}, bf16[2,512,128]{2,1,0:T(8,128)(2,1)S(1)}, bf16[2,512,128]{2,1,0:T(8,128)(2,1)S(1)}, bf16[2,512,128]{2,1,0:T(8,128)(2,1)S(1)}) custom-call(s32[8]{0:T(128)S(1)} %broadcast_xor_fusion.refs_10_.refs_0_, bf16[1056,128]{1,0:T(8,128)(2,1)S(1)} %get-tuple-element.37.refs_9_.refs_1_, ...), custom_call_target="tpu_custom_call" | custom-call | flops 1 | bytes 1 | tf_op jit(solution)/shard_map/pick_states/pallas_call | solution.py:535
  60.4 1.6 %collective-permute-start.11 = (bf16[2,512,128]{2,1,0:T(8,128)(2,1)S(1)}, bf16[2,512,128]{2,1,0:T(8,128)(2,1)S(1)}, u32[]{:S(2)}, u32[]{:S(2)}) collective-permute-start(bf16[2,512,128]{2,1,0:T(8,128)(2,1)S(1)} %get-tuple-element.60), channel_id=1, source_target_pairs={{0,2},{2,0},{4,6},{6,4},{8,10},{10,8},{12,14},{14,12},{1,3},{3,1},... | collective-permute-start | bytes 786440 | tf_op jit(solution)/shard_map/ppermute | solution.py:464
  62.0 0.5 collective-permute-start.12
  62.4 5.3 %collective-permute-start.13 = (bf16[2,512,128]{2,1,0:T(8,128)(2,1)S(1)}, bf16[2,512,128]{2,1,0:T(8,128)(2,1)S(1)}, u32[]{:S(2)}, u32[]{:S(2)}) collective-permute-start(bf16[2,512,128]{2,1,0:T(8,128)(2,1)S(1)} %get-tuple-element.62), channel_id=1, source_target_pairs={{0,6},{2,4},{4,2},{6,0},{8,14},{10,12},{12,10},{14,8},{1,7},{3,5},... | collective-permute-start | bytes 786440 | tf_op jit(solution)/shard_map/ppermute | solution.py:464
  67.7 0.0 collective-permute-done.8.refs_9_.refs_13_
  67.7 3.1 %collective-permute-done.9.refs_10_.refs_14_ = bf16[2,544,128]{2,1,0:T(8,128)(2,1)S(1)} collective-permute-done((bf16[2,544,128]{2,1,0:T(8,128)(2,1)S(1)}, bf16[2,544,128]{2,1,0:T(8,128)(2,1)S(1)}, u32[]{:S(2)}, u32[]{:S(2)}) %collective-permute-start.9) | collective-permute-done | bytes 278560 | tf_op jit(solution)/shard_map/ppermute | solution.py:464
  70.8 5.7 %late.2.refs_23_ = bf16[2,256,4096]{2,1,0:T(8,128)(2,1)} custom-call(s32[1]{0:T(128)} %bitcast.refs_0_, bf16[2,256,4096]{2,1,0:T(8,128)(2,1)} %refs_1_.11, bf16[2,256,512]{2,1,0:T(8,128)(2,1)} %refs_2_.13, bf16[2,256,512]{2,1,0:T(8,128)(2,1)} %refs_3_.13, f32[1,4096]{1,0:T(1,128)S(1)} %broadcast_in_dim_reshape.3.refs_6_.refs_4_, f32[4,4096]{1,0:T(4,128)} %refs_5_.5, ...), custom_call_target="tpu_custom_call" | custom-call | flops 1 | bytes 1 | tf_op jit(solution)/shard_map/late/pallas_call | solution.py:629
  76.5 5.4 %collective-permute-done.13.refs_14_ = bf16[2,512,128]{2,1,0:T(8,128)(2,1)S(1)} collective-permute-done((bf16[2,512,128]{2,1,0:T(8,128)(2,1)S(1)}, bf16[2,512,128]{2,1,0:T(8,128)(2,1)S(1)}, u32[]{:S(2)}, u32[]{:S(2)}) %collective-permute-start.13) | collective-permute-done | bytes 262176 | tf_op jit(solution)/shard_map/ppermute | solution.py:464
  81.9 5.7 %late.3 = bf16[2,256,4096]{2,1,0:T(8,128)(2,1)} custom-call(s32[1]{0:T(128)} %bitcast.refs_0_, bf16[2,256,4096]{2,1,0:T(8,128)(2,1)} %refs_1_.11, bf16[2,256,512]{2,1,0:T(8,128)(2,1)} %refs_2_.13, bf16[2,256,512]{2,1,0:T(8,128)(2,1)} %refs_3_.13, f32[1,4096]{1,0:T(1,128)S(1)} %broadcast_in_dim_reshape.3.refs_6_.refs_4_, ...), custom_call_target="tpu_custom_call", output_to_operand_aliasing={{}: (23, {})} | custom-call | flops 1 | bytes 1 | tf_op jit(solution)/shard_map/late/pallas_call | solution.py:629
  (11 shorter events, 0.0 us)
Async XLA Ops:
  1.4 9.4 %copy-start.3 = (s32[8]{0:T(128)S(1)}, s32[8]{0:T(128)}, u32[]{:S(2)}) copy-start(s32[8]{0:T(128)} %param.26) | copy-start | bytes 100
  1.4 9.5 %copy-start.4 = (s32[16]{0:T(128)S(1)}, s32[16]{0:T(128)}, u32[]{:S(2)}) copy-start(s32[16]{0:T(128)} %param.27) | copy-start | bytes 196
  1.4 9.8 %copy-start = (f32[64]{0:T(128)S(1)}, f32[64]{0:T(128)}, u32[]{:S(2)}) copy-start(f32[64]{0:T(128)} %param.18) | copy-start | bytes 772
  1.4 9.9 %copy-start.1 = (f32[64]{0:T(128)S(1)}, f32[64]{0:T(128)}, u32[]{:S(2)}) copy-start(f32[64]{0:T(128)} %param.19) | copy-start | bytes 772
  1.4 10.0 %copy-start.2 = (f32[64]{0:T(128)S(1)}, f32[64]{0:T(128)}, u32[]{:S(2)}) copy-start(f32[64]{0:T(128)} %param.20) | copy-start | bytes 772
  1.4 31.6 %collective-permute-start.3 = (bf16[4,544,128]{2,1,0:T(8,128)(2,1)S(1)}, bf16[4,544,128]{2,1,0:T(8,128)(2,1)S(1)}, u32[]{:S(2)}, u32[]{:S(2)}) collective-permute-start(bf16[4,544,128]{2,1,0:T(8,128)(2,1)S(1)} %cast_states.2.refs_17_), channel_id=1, source_target_pairs={{0,8},{2,10},{4,12},{6,14},{8,0},{10,2},{12,4},{14,6},{1,9},{3,11}... | collective-permute-start | bytes 1671176 | tf_op jit(solution)/shard_map/ppermute | solution.py:464
  7.2 21.4 %collective-permute-start = (bf16[1056,128]{1,0:T(8,128)(2,1)S(1)}, bf16[1056,128]{1,0:T(8,128)(2,1)S(1)}, u32[]{:S(2)}, u32[]{:S(2)}) collective-permute-start(bf16[1056,128]{1,0:T(8,128)(2,1)S(1)} %get-tuple-element.38), channel_id=1, source_target_pairs={{0,2},{2,0},{4,6},{6,4},{8,10},{10,8},{12,14},{14,12},{1,3},{3,1},... | collective-permute-start | bytes 811016 | tf_op jit(solution)/shard_map/ppermute | solution.py:464
  8.8 19.8 %collective-permute-start.1 = (bf16[1056,128]{1,0:T(8,128)(2,1)S(1)}, bf16[1056,128]{1,0:T(8,128)(2,1)S(1)}, u32[]{:S(2)}, u32[]{:S(2)}) collective-permute-start(bf16[1056,128]{1,0:T(8,128)(2,1)S(1)} %get-tuple-element.39), channel_id=1, source_target_pairs={{0,4},{2,6},{4,0},{6,2},{8,12},{10,14},{12,8},{14,10},{1,5},{3,7},... | collective-permute-start | bytes 811016 | tf_op jit(solution)/shard_map/ppermute | solution.py:464
  10.4 22.6 %collective-permute-start.2 = (bf16[1056,128]{1,0:T(8,128)(2,1)S(1)}, bf16[1056,128]{1,0:T(8,128)(2,1)S(1)}, u32[]{:S(2)}, u32[]{:S(2)}) collective-permute-start(bf16[1056,128]{1,0:T(8,128)(2,1)S(1)} %get-tuple-element.40), channel_id=1, source_target_pairs={{0,6},{2,4},{4,2},{6,0},{8,14},{10,12},{12,10},{14,8},{1,7},{3,5},... | collective-permute-start | bytes 811016 | tf_op jit(solution)/shard_map/ppermute | solution.py:464
  33.7 24.1 %collective-permute-start.10 = (bf16[4,512,128]{2,1,0:T(8,128)(2,1)S(1)}, bf16[4,512,128]{2,1,0:T(8,128)(2,1)S(1)}, u32[]{:S(2)}, u32[]{:S(2)}) collective-permute-start(bf16[4,512,128]{2,1,0:T(8,128)(2,1)S(1)} %stack_b.1.refs_2_), channel_id=1, source_target_pairs={{0,8},{2,10},{4,12},{6,14},{8,0},{10,2},{12,4},{14,6},{1,9},{3,11}... | collective-permute-start | bytes 1572872 | tf_op jit(solution)/shard_map/ppermute | solution.py:464
  35.1 9.6 %collective-permute-start.4 = (bf16[544,128]{1,0:T(8,128)(2,1)S(1)}, bf16[544,128]{1,0:T(8,128)(2,1)S(1)}, u32[]{:S(2)}, u32[]{:S(2)}) collective-permute-start(bf16[544,128]{1,0:T(8,128)(2,1)S(1)} %get-tuple-element.48), channel_id=1, source_target_pairs={{0,2},{2,0},{4,6},{6,4},{8,10},{10,8},{12,14},{14,12},{1,3},{3,1},... | collective-permute-start | bytes 417800 | tf_op jit(solution)/shard_map/ppermute | solution.py:464
  36.2 12.1 %collective-permute-start.5 = (bf16[544,128]{1,0:T(8,128)(2,1)S(1)}, bf16[544,128]{1,0:T(8,128)(2,1)S(1)}, u32[]{:S(2)}, u32[]{:S(2)}) collective-permute-start(bf16[544,128]{1,0:T(8,128)(2,1)S(1)} %get-tuple-element.49), channel_id=1, source_target_pairs={{0,4},{2,6},{4,0},{6,2},{8,12},{10,14},{12,8},{14,10},{1,5},{3,7},... | collective-permute-start | bytes 417800 | tf_op jit(solution)/shard_map/ppermute | solution.py:464
  39.1 10.7 %collective-permute-start.6 = (bf16[544,128]{1,0:T(8,128)(2,1)S(1)}, bf16[544,128]{1,0:T(8,128)(2,1)S(1)}, u32[]{:S(2)}, u32[]{:S(2)}) collective-permute-start(bf16[544,128]{1,0:T(8,128)(2,1)S(1)} %get-tuple-element.50), channel_id=1, source_target_pairs={{0,6},{2,4},{4,2},{6,0},{8,14},{10,12},{12,10},{14,8},{1,7},{3,5},... | collective-permute-start | bytes 417800 | tf_op jit(solution)/shard_map/ppermute | solution.py:464
  52.4 10.1 %collective-permute-start.7 = (bf16[2,544,128]{2,1,0:T(8,128)(2,1)S(1)}, bf16[2,544,128]{2,1,0:T(8,128)(2,1)S(1)}, u32[]{:S(2)}, u32[]{:S(2)}) collective-permute-start(bf16[2,544,128]{2,1,0:T(8,128)(2,1)S(1)} %get-tuple-element.56), channel_id=1, source_target_pairs={{0,2},{2,0},{4,6},{6,4},{8,10},{10,8},{12,14},{14,12},{1,3},{3,1},... | collective-permute-start | bytes 835592 | tf_op jit(solution)/shard_map/ppermute | solution.py:464
  53.9 13.8 %collective-permute-start.8 = (bf16[2,544,128]{2,1,0:T(8,128)(2,1)S(1)}, bf16[2,544,128]{2,1,0:T(8,128)(2,1)S(1)}, u32[]{:S(2)}, u32[]{:S(2)}) collective-permute-start(bf16[2,544,128]{2,1,0:T(8,128)(2,1)S(1)} %get-tuple-element.57), channel_id=1, source_target_pairs={{0,4},{2,6},{4,0},{6,2},{8,12},{10,14},{12,8},{14,10},{1,5},{3,7},... | collective-permute-start | bytes 835592 | tf_op jit(solution)/shard_map/ppermute | solution.py:464
  56.4 14.4 %collective-permute-start.9 = (bf16[2,544,128]{2,1,0:T(8,128)(2,1)S(1)}, bf16[2,544,128]{2,1,0:T(8,128)(2,1)S(1)}, u32[]{:S(2)}, u32[]{:S(2)}) collective-permute-start(bf16[2,544,128]{2,1,0:T(8,128)(2,1)S(1)} %get-tuple-element.58), channel_id=1, source_target_pairs={{0,6},{2,4},{4,2},{6,0},{8,14},{10,12},{12,10},{14,8},{1,7},{3,5},... | collective-permute-start | bytes 835592 | tf_op jit(solution)/shard_map/ppermute | solution.py:464
  60.4 16.1 %collective-permute-start.11 = (bf16[2,512,128]{2,1,0:T(8,128)(2,1)S(1)}, bf16[2,512,128]{2,1,0:T(8,128)(2,1)S(1)}, u32[]{:S(2)}, u32[]{:S(2)}) collective-permute-start(bf16[2,512,128]{2,1,0:T(8,128)(2,1)S(1)} %get-tuple-element.60), channel_id=1, source_target_pairs={{0,2},{2,0},{4,6},{6,4},{8,10},{10,8},{12,14},{14,12},{1,3},{3,1},... | collective-permute-start | bytes 786440 | tf_op jit(solution)/shard_map/ppermute | solution.py:464
  62.0 14.5 %collective-permute-start.12 = (bf16[2,512,128]{2,1,0:T(8,128)(2,1)S(1)}, bf16[2,512,128]{2,1,0:T(8,128)(2,1)S(1)}, u32[]{:S(2)}, u32[]{:S(2)}) collective-permute-start(bf16[2,512,128]{2,1,0:T(8,128)(2,1)S(1)} %get-tuple-element.61), channel_id=1, source_target_pairs={{0,4},{2,6},{4,0},{6,2},{8,12},{10,14},{12,8},{14,10},{1,5},{3,7},... | collective-permute-start | bytes 786440 | tf_op jit(solution)/shard_map/ppermute | solution.py:464
  62.4 19.5 %collective-permute-start.13 = (bf16[2,512,128]{2,1,0:T(8,128)(2,1)S(1)}, bf16[2,512,128]{2,1,0:T(8,128)(2,1)S(1)}, u32[]{:S(2)}, u32[]{:S(2)}) collective-permute-start(bf16[2,512,128]{2,1,0:T(8,128)(2,1)S(1)} %get-tuple-element.62), channel_id=1, source_target_pairs={{0,6},{2,4},{4,2},{6,0},{8,14},{10,12},{12,10},{14,8},{1,7},{3,5},... | collective-permute-start | bytes 786440 | tf_op jit(solution)/shard_map/ppermute | solution.py:464

commit v12 on v11

--- a/solution.py
+++ b/solution.py
@@ -21,6 +21,14 @@
     index = jnp.arange(counts.shape[0], dtype=jnp.int32)
     bounds = jnp.sum(jnp.where(index[None, :] <= index[:, None], counts[None, :], 0), axis=1)
     return jnp.sum((bounds[None, :] <= order[:, None]).astype(jnp.int32), axis=1)
+
+
+def three_terms(value):
+    terms = []
+    for _ in range(3):
+        terms.append(value.astype(jnp.bfloat16).astype(jnp.float32))
+        value = value - terms[-1]
+    return jnp.concatenate(terms)
 
 
 def conv_silu(padded, tail, rows, taps):
@@ -45,12 +53,12 @@
     width = wide // heads
     half = length // 2
 
-    def convolve(rows, taps):
-        bulk = conv_silu(padded, 0.0, rows, taps)[FIX:]
+    def convolve(rows, taps, slot):
+        bulk = conv_silu(padded.at[slot % 2], 0.0, rows, taps)[FIX:]
         return jnp.concatenate([jnp.zeros((FIX, rows.shape[1]), jnp.bfloat16), bulk])
 
-    b_conv = convolve(b_ref[0], taps_bc_ref[0])
-    c_conv = convolve(c_ref[0], taps_bc_ref[1])
+    b_conv = convolve(b_ref[0], taps_bc_ref[0], 0)
+    c_conv = convolve(c_ref[0], taps_bc_ref[1], 1)
     c_out_ref[q] = c_conv
     scores = lax.dot_general(
         c_conv, b_conv, (((1,), (1,)), ((), ())), preferred_element_type=jnp.float32
@@ -61,13 +69,12 @@
     upper = lax.broadcasted_iota(jnp.int32, (length, length), 0) <= lax.broadcasted_iota(
         jnp.int32, (length, length), 1
     )
-    total = lax.dot_general(
-        per_token,
-        upper.astype(jnp.float32),
-        (((1,), (0,)), ((), ())),
-        precision=lax.Precision.HIGHEST,
+    sums = jnp.dot(
+        three_terms(per_token).astype(jnp.bfloat16),
+        upper.astype(jnp.float32).astype(jnp.bfloat16),
         preferred_element_type=jnp.float32,
     )
+    total = (sums[:heads] + sums[heads : 2 * heads]) + sums[2 * heads :]
     total = total * LOG2_E
     row = total - jnp.log(step) * LOG2_E
     columns = total.T
@@ -78,7 +85,7 @@
     low = lax.broadcasted_iota(jnp.int32, (length, 2 * width), 1) < width
     for pair in range(heads // 2):
         lanes = slice(pair * 2 * width, (pair + 1) * 2 * width)
-        x_conv = convolve(x_ref[0, :, lanes], taps_x_ref[:, lanes])
+        x_conv = convolve(x_ref[0, :, lanes], taps_x_ref[:, lanes], pair)
         parts = []
         for head in (2 * pair, 2 * pair + 1):
             column = jnp.broadcast_to(columns[:, head : head + 1], (length, half))
@@ -134,19 +141,36 @@
         tail = choose([ref[kid] for ref in tails]).astype(jnp.float32)
         state = choose([ref[kid] for ref in states])
 
-        def opening(rows, taps, at):
-            tap_rows = [tail[k * lines + at : k * lines + at + 1] for k in range(reach)]
-            return conv_silu(padded, jnp.concatenate(tap_rows), rows, taps)
-
-        b_first = opening(b_ref[kid, :, group_lanes], taps_bc_ref[0, :, group_lanes], lines - 2)
-        c_first = opening(c_ref[kid, :, group_lanes], taps_bc_ref[1, :, group_lanes], lines - 1)
+        def opening(scratch, rows, taps, at, count):
+            tap_rows = []
+            for k in range(reach):
+                here = [tail[k * lines + at + n : k * lines + at + n + 1] for n in range(count)]
+                tap_rows.append(jnp.concatenate(here, axis=1))
+            return conv_silu(scratch, jnp.concatenate(tap_rows), rows, taps)
+
+        start = pl.multiple_of(q * stride + offset * width, 128)
+        chunk_lanes = pl.ds(start, wide)
+        blocks = wide // 128
+        bc_first = opening(
+            padded.at[kid, :, wide : wide + 2 * size],
+            jnp.concatenate([b_ref[kid, :, group_lanes], c_ref[kid, :, group_lanes]], axis=1),
+            jnp.concatenate([taps_bc_ref[0, :, group_lanes], taps_bc_ref[1, :, group_lanes]], axis=1),
+            lines - 2,
+            2,
+        )
+        b_first, c_first = bc_first[:, :size], bc_first[:, size:]
+        x_all = opening(
+            padded.at[kid, :, :wide],
+            x_ref[kid, :, chunk_lanes],
+            taps_x_ref[:, chunk_lanes],
+            offset * width // 128,
+            blocks,
+        ).astype(jnp.float32)
+        skipped = skip_ref[:, chunk_lanes] * x_all
         c_conv = jnp.concatenate([c_first, held_ref[q, FIX:]])
         grow = jnp.exp2(column_ref[q, offset : offset + heads, :])
-        terms = []
-        for _ in range(3):
-            terms.append(grow.astype(jnp.bfloat16).astype(jnp.float32))
-            grow = grow - terms[-1]
-        terms = jnp.concatenate(terms + [jnp.zeros_like(grow)]).T.astype(jnp.bfloat16)
+        terms = jnp.concatenate([three_terms(grow), jnp.zeros_like(grow)])
+        terms = terms.T.astype(jnp.bfloat16)
         grow = jnp.dot(terms, spread, preferred_element_type=jnp.float32)
         term = lax.dot_general(c_conv, state, contract, preferred_element_type=jnp.float32)
         carried = (term * grow).astype(jnp.bfloat16)
@@ -160,11 +184,7 @@
         mixing = (scores * first_ref[q, :, unit : unit + heads * FIX]).astype(jnp.bfloat16)
         for pair in range(heads // 2):
             lanes = slice(pair * 2 * width, (pair + 1) * 2 * width)
-            start = pl.multiple_of(q * stride + (offset + 2 * pair) * width, 128)
-            whole = pl.ds(start, 2 * width)
-            x_first = opening(
-                x_ref[kid, :, whole], taps_x_ref[:, whole], offset * width // 128 + pair
-            ).astype(jnp.float32)
+            x_first = x_all[:, lanes]
             stacked = [jnp.where(low_first, x_first, 0.0), jnp.where(low_first, 0.0, x_first)]
             if pair > 0:
                 stacked = [jnp.zeros((2 * pair * FIX, 2 * width), jnp.float32)] + stacked
@@ -176,7 +196,7 @@
                 jnp.concatenate(stacked).astype(jnp.bfloat16),
                 preferred_element_type=jnp.float32,
             )
-            part = jnp.concatenate([part[:FIX] + skip_ref[:, whole] * x_first, part[FIX:]])
+            part = jnp.concatenate([part[:FIX] + skipped[:, lanes], part[FIX:]])
             here = slice(offset * width + lanes.start, offset * width + lanes.stop)
             y_ref[kid, :, lanes] = (
                 mixed_ref[q, :, here] + part + carried[:, lanes].astype(jnp.float32)
@@ -463,7 +483,7 @@
     def swap(value, r):
         return lax.ppermute(value, "batch", perm=[(i, i ^ r) for i in range(8)])
 
-    def cast(quarters, chunks, stacked, tokens):
+    def cast(chunks, paired, tokens):
         part = sum(SPLIT[k] for k in chunks)
         rows = part * width + tail_lines
         block = [SPLIT[k] for k in chunks]
@@ -472,14 +492,14 @@
             count = len(chunks) + 2
             ins, outs = refs[: count * 4], refs[count * 4 :]
             for n in range(4):
-                out_ref = outs[0].at[n] if stacked else outs[n]
+                out_ref = outs[n // 2].at[n % 2] if paired else outs[n]
                 cast_kernel(
                     len(chunks), [tail_lines], reach, lines, *ins[count * n : count * n + count], out_ref
                 )
 
         operands, specs = [], []
         for n in range(4):
-            which = (lambda i, p, n=n: n) if stacked else (lambda i, p, n=n: p[0] ^ n)
+            which = lambda i, p, n=n: p[0] ^ n
             for k in chunks:
                 operands.append(state)
                 specs.append(
@@ -493,7 +513,7 @@
                 pl.BlockSpec((1, reach, wide), lambda i, p, w=which: (0, 0, w(i, p))),
                 pl.BlockSpec((1, reach, 2, size), lambda i, p, w=which: (0, 0, 0, w(i, p))),
             ]
-        shapes = [(4, rows, size)] if stacked else [(rows, size)] * 4
+        shapes = [(2, rows, size)] * 2 if paired else [(rows, size)] * 4
         return pl.pallas_call(
             functools.partial(drop_tokens, kernel, 1 + len(operands), len(tokens)),
             grid_spec=pltpu.PrefetchScalarGridSpec(
@@ -590,7 +610,7 @@
                 pltpu.VMEM((groups, length, per_group * FIX), jnp.float32),
             ],
             input_output_aliases={first + i: i for i in range(len(before))},
-            scratch_shapes=[pltpu.VMEM((8 + length, size), jnp.float32)],
+            scratch_shapes=[pltpu.VMEM((2, 8 + length, size), jnp.float32)],
             compiler_params=params,
             cost_estimate=small,
             name="early",
@@ -638,7 +658,7 @@
                 grid=(groups,),
                 in_specs=specs,
                 out_specs=pl.BlockSpec((kids, length, chunk), lane),
-                scratch_shapes=[pltpu.VMEM((8 + FIX, size), jnp.float32)],
+                scratch_shapes=[pltpu.VMEM((kids, 8 + FIX, chunk + 2 * size), jnp.float32)],
             ),
             out_shape=jax.ShapeDtypeStruct(x_in.shape, jnp.bfloat16),
             input_output_aliases=alias,
@@ -651,26 +671,26 @@
     rows = [SPLIT[0] * width + tail_lines, SPLIT[1] * width]
     chunk_a, chunk_b = pl.ds(0, rows[0]), pl.ds(rows[0], rows[1])
 
-    (sent_a,) = cast(range(4), [0], True, [])
-    crossed_a = swap(sent_a, 4)
-    own = cast(range(4), [0, 1], False, [sent_a])
+    sent_a = cast([0], True, [])
+    crossed_a = [swap(sent_a[0], 4), swap(sent_a[1], 6)]
+    own = cast([0, 1], False, [sent_a[0]])
     inside = [own[0]] + [swap(own[j], j) for j in range(1, 4)]
     first = early(0, 0, [], [own[0], slots])
     first = early(0, 1, first, [])
     second = early(1, 0, [], [first[1]])
     moves = [(0, j, None, [(j, chunk_b)]) for j in range(4)]
     (sent_b,) = rearrange(
-        place, inside, moves, [(4, rows[1], size)], [second[1], crossed_a], "stack_b"
+        place, inside, moves, [(4, rows[1], size)], [second[1], *crossed_a], "stack_b"
     )
     crossed_b = swap(sent_b, 4)
-    moves = [(j, None, 0, [(0, n ^ j) for n in range(4)]) for j in range(4)]
-    spread = rearrange(
-        place, [crossed_a], moves, [(rows[0], size)] * 4, [sent_b], "split_a"
-    )
-    spread = [spread[0]] + [swap(spread[j], j) for j in range(1, 4)]
-    second = early(1, 1, second, [spread[0]])
-    choices = [(j, chunk_a) for j in range(4)] + [(4 + j, None) for j in range(4)]
-    states_a = pick(rows[0], [*inside, *spread], choices, [second[1]])
+    moves = [(0, n, None, [(n, 1)]) for n in range(2)]
+    (spread,) = rearrange(
+        place, crossed_a, moves, [(2, rows[0], size)], [sent_b], "stack_a"
+    )
+    passed = swap(spread, 1)
+    second = early(1, 1, second, [spread])
+    choices = [(j, chunk_a) for j in range(4)] + [(4, 0), (6, 0), (5, 0), (6, 1)]
+    states_a = pick(rows[0], [*inside, *crossed_a, passed], choices, [second[1]])
     choices = [(j, chunk_b) for j in range(4)] + [(4, j) for j in range(4)]
     states_b = pick(rows[1], [*inside, crossed_b], choices, [states_a[0]])
     parts = [first, second]

time: 87.9 us -> 86.6 us (0.985)
  waiting for transfers between devices: 18.5 us -> 25 us
  starting transfers between devices: 24.5 us -> 18.1 us
  Pallas kernels: 43.7 us -> 42.3 us
    ppermute x14 -> x13, waiting for transfers between devices: 18.5 us -> 25 us  [swap(): return lax.ppermute(value, 'batch', perm=[(i, i ^ r) for i in range(8)])]
    ppermute x14 -> x13, starting transfers between devices: 24.5 us -> 18.1 us  [swap(): return lax.ppermute(value, 'batch', perm=[(i, i ^ r) for i in range(8)])]
    pallas_call x4, Pallas kernels: 22.7 us -> 21.5 us  [early(): pl.pallas_call(functools.partial(drop_tokens, functools.partial(early_ker...]
  transfers between devices with their start and end apart: 14 -> 13, of which waited for: 6 -> 5; matrix products, arithmetic and copies ran while one was open for 1% -> 1% of each run, Pallas kernels for 41% -> 39%
where the time goes in v12:
time: 86.6 us; the launch traced here: 86.3 us
  Pallas kernels  42.3 us (49%)
  waiting for transfers between devices  25 us (29%)
  starting transfers between devices  18.1 us (21%)
    ppermute x13, waiting for transfers between devices, swap(): return lax.ppermute(value, 'batch', perm=[(i, i ^ r) for i in range(8)])  25 us
    pallas_call x4, Pallas kernels, early(): pl.pallas_call(functools.partial(drop_tokens, functools.partial(early_ker...  21.5 us
    ppermute x13, starting transfers between devices, swap(): return lax.ppermute(value, 'batch', perm=[(i, i ^ r) for i in range(8)])  18.1 us
    pallas_call x2, Pallas kernels, late(): pl.pallas_call(functools.partial(drop_tokens, functools.partial(late_kern...  11.6 us
    pallas_call x4, Pallas kernels, rearrange(): pl.pallas_call(functools.partial(drop_tokens, kernel, 1 + len(sources), l...  6.16 us
    pallas_call x2, Pallas kernels, cast(): pl.pallas_call(functools.partial(drop_tokens, kernel, 1 + len(operands),...  3.07 us
  transfers between devices with their start and end apart: 13, of which 5 were waited for; matrix products, arithmetic and copies ran while one was open for 1% of the time, Pallas kernels for 39%

profile of v12, /device:TPU:0, one launch (start us, length us, event | category | flops | bytes accessed | tf_op | source)
XLA Modules:
  0.0 86.3 jit_solution(12134510359597952772)
XLA Ops:
  0.0 1.3 %cast_states.2 = (bf16[2,544,128]{2,1,0:T(8,128)(2,1)S(1)}, bf16[2,544,128]{2,1,0:T(8,128)(2,1)S(1)}) custom-call(s32[1]{0:T(128)} %bitcast.refs_0_, f32[4,16,64,128]{3,2,1,0:T(8,128)} %bitcast.5, bf16[1,3,4096]{2,1,0:T(4,128)(2,1)} %refs_15_.1, bf16[1,3,2,512]{3,2,1,0:T(2,128)(2,1)} %bitcast.17, f32[4,16,64,128]{3,2,1,0:T(8,128)} %bitcast.6, ...), custom_call_target="tpu_custom_call" | custom-call | flops 1 | bytes 1 | tf_op jit(solution)/shard_map/cast_states/pallas_call | solution.py:517
  1.4 5.1 %collective-permute-start.4 = (bf16[2,544,128]{2,1,0:T(8,128)(2,1)S(1)}, bf16[2,544,128]{2,1,0:T(8,128)(2,1)S(1)}, u32[]{:S(2)}, u32[]{:S(2)}) collective-permute-start(bf16[2,544,128]{2,1,0:T(8,128)(2,1)S(1)} %get-tuple-element.40), channel_id=1, source_target_pairs={{0,12},{2,14},{4,8},{6,10},{8,4},{10,6},{12,0},{14,2},{1,13},{3,15... | collective-permute-start | bytes 835592 | tf_op jit(solution)/shard_map/ppermute | solution.py:484
  6.5 0.0 copy-start.2
  6.5 0.1 collective-permute-start.3
  6.6 1.7 %cast_states.3 = (bf16[1056,128]{1,0:T(8,128)(2,1)S(1)}, bf16[1056,128]{1,0:T(8,128)(2,1)S(1)}, bf16[1056,128]{1,0:T(8,128)(2,1)S(1)}, bf16[1056,128]{1,0:T(8,128)(2,1)S(1)}) custom-call(s32[1]{0:T(128)} %bitcast.refs_0_, f32[4,16,64,128]{3,2,1,0:T(8,128)} %bitcast.9, f32[4,16,64,128]{3,2,1,0:T(8,128)} %bitcast.10, bf16[1,3,4096]{2,1,0:T(4,128)(2,1)} %refs_15_.1, ...), custom_call_target="tpu_custom_call" | custom-call | flops 1 | bytes 1 | tf_op jit(solution)/shard_map/cast_states/pallas_call | solution.py:517
  8.3 1.6 %collective-permute-start = (bf16[1056,128]{1,0:T(8,128)(2,1)S(1)}, bf16[1056,128]{1,0:T(8,128)(2,1)S(1)}, u32[]{:S(2)}, u32[]{:S(2)}) collective-permute-start(bf16[1056,128]{1,0:T(8,128)(2,1)S(1)} %get-tuple-element.37), channel_id=1, source_target_pairs={{0,2},{2,0},{4,6},{6,4},{8,10},{10,8},{12,14},{14,12},{1,3},{3,1},... | collective-permute-start | bytes 811016 | tf_op jit(solution)/shard_map/ppermute | solution.py:484
  9.9 0.7 collective-permute-start.1
  10.6 1.2 %collective-permute-start.2 = (bf16[1056,128]{1,0:T(8,128)(2,1)S(1)}, bf16[1056,128]{1,0:T(8,128)(2,1)S(1)}, u32[]{:S(2)}, u32[]{:S(2)}) collective-permute-start(bf16[1056,128]{1,0:T(8,128)(2,1)S(1)} %get-tuple-element.39), channel_id=1, source_target_pairs={{0,6},{2,4},{4,2},{6,0},{8,14},{10,12},{12,10},{14,8},{1,7},{3,5},... | collective-permute-start | bytes 811016 | tf_op jit(solution)/shard_map/ppermute | solution.py:484
  11.9 0.0 copy-done.3
  11.9 0.1 select_reduce_fusion.1
  12.0 0.0 copy-done.4
  12.0 0.1 convert_reduce_fusion
  12.1 0.2 select_reduce_fusion
  12.3 0.1 copy.36.refs_4_
  12.4 0.1 copy.37.refs_5_
  12.5 0.1 broadcast_in_dim.33
  12.5 0.1 broadcast_in_dim_reshape.3.refs_6_.refs_4_
  12.6 5.4 %early.4 = (f32[4,256,1024]{2,1,0:T(8,128)S(1)}, bf16[4,256,128]{2,1,0:T(8,128)(2,1)S(1)}, f32[4,16,256]{2,1,0:T(8,128)S(1)}, f32[4,256,256]{2,1,0:T(8,128)S(1)}) custom-call(bf16[2,256,4096]{2,1,0:T(8,128)(2,1)} %refs_1_.11, bf16[2,256,512]{2,1,0:T(8,128)(2,1)} %refs_2_.13, bf16[2,256,512]{2,1,0:T(8,128)(2,1)} %refs_3_.13, f32[2,64,256]{2,1,0:T(8,128)} %refs_3_.11, ...), custom_call_target="tpu_custom_call" | custom-call | flops 1 | bytes 1 | tf_op jit(solution)/shard_map/early/pallas_call | solution.py:588
  18.0 5.4 %early.5 = (f32[4,256,1024]{2,1,0:T(8,128)S(1)}, bf16[4,256,128]{2,1,0:T(8,128)(2,1)S(1)}, f32[4,16,256]{2,1,0:T(8,128)S(1)}, f32[4,256,256]{2,1,0:T(8,128)S(1)}) custom-call(bf16[2,256,4096]{2,1,0:T(8,128)(2,1)} %refs_1_.11, bf16[2,256,512]{2,1,0:T(8,128)(2,1)} %refs_2_.13, ...), custom_call_target="tpu_custom_call", output_to_operand_aliasing={{0}: (9, {}), {1}: (10, {}), {2}: (11, {}), {3}: (12, {})} | custom-call | flops 1 | bytes 1 | tf_op jit(solution)/shard_map/early/pallas_call | solution.py:588
  23.4 5.4 %early.6 = (f32[4,256,1024]{2,1,0:T(8,128)S(1)}, bf16[4,256,128]{2,1,0:T(8,128)(2,1)S(1)}, f32[4,16,256]{2,1,0:T(8,128)S(1)}, f32[4,256,256]{2,1,0:T(8,128)S(1)}) custom-call(bf16[2,256,4096]{2,1,0:T(8,128)(2,1)} %refs_1_.11, bf16[2,256,512]{2,1,0:T(8,128)(2,1)} %refs_2_.13, bf16[2,256,512]{2,1,0:T(8,128)(2,1)} %refs_3_.13, f32[2,64,256]{2,1,0:T(8,128)} %refs_3_.11, ...), custom_call_target="tpu_custom_call" | custom-call | flops 1 | bytes 1 | tf_op jit(solution)/shard_map/early/pallas_call | solution.py:588
  28.8 0.0 collective-permute-done.refs_2_
  28.8 0.0 collective-permute-done.1.refs_3_
  28.8 2.9 %collective-permute-done.2.refs_4_ = bf16[1056,128]{1,0:T(8,128)(2,1)S(1)} collective-permute-done((bf16[1056,128]{1,0:T(8,128)(2,1)S(1)}, bf16[1056,128]{1,0:T(8,128)(2,1)S(1)}, u32[]{:S(2)}, u32[]{:S(2)}) %collective-permute-start.2) | collective-permute-done | bytes 270368 | tf_op jit(solution)/shard_map/ppermute | solution.py:484
  31.7 0.0 collective-permute-done.4.refs_7_.refs_2_.refs_6_
  31.7 0.0 collective-permute-done.3.refs_6_.refs_1_.refs_5_
  31.7 0.7 stack_b.1.refs_3_
  32.5 0.4 stack_a.1.refs_9_
  32.9 0.6 collective-permute-start.5
  33.4 1.7 %collective-permute-start.9 = (bf16[4,512,128]{2,1,0:T(8,128)(2,1)S(1)}, bf16[4,512,128]{2,1,0:T(8,128)(2,1)S(1)}, u32[]{:S(2)}, u32[]{:S(2)}) collective-permute-start(bf16[4,512,128]{2,1,0:T(8,128)(2,1)S(1)} %stack_b.1.refs_3_), channel_id=1, source_target_pairs={{0,8},{2,10},{4,12},{6,14},{8,0},{10,2},{12,4},{14,6},{1,9},{3,11}... | collective-permute-start | bytes 1572872 | tf_op jit(solution)/shard_map/ppermute | solution.py:484
  35.1 5.4 %early.7 = (f32[4,256,1024]{2,1,0:T(8,128)S(1)}, bf16[4,256,128]{2,1,0:T(8,128)(2,1)S(1)}, f32[4,16,256]{2,1,0:T(8,128)S(1)}, f32[4,256,256]{2,1,0:T(8,128)S(1)}) custom-call(bf16[2,256,4096]{2,1,0:T(8,128)(2,1)} %refs_1_.11, bf16[2,256,512]{2,1,0:T(8,128)(2,1)} %refs_2_.13, ...), custom_call_target="tpu_custom_call", output_to_operand_aliasing={{0}: (10, {}), {1}: (11, {}), {2}: (12, {}), {3}: (13, {})} | custom-call | flops 1 | bytes 1 | tf_op jit(solution)/shard_map/early/pallas_call | solution.py:588
  40.5 1.0 %collective-permute-done.5.refs_7_ = bf16[2,544,128]{2,1,0:T(8,128)(2,1)S(1)} collective-permute-done((bf16[2,544,128]{2,1,0:T(8,128)(2,1)S(1)}, bf16[2,544,128]{2,1,0:T(8,128)(2,1)S(1)}, u32[]{:S(2)}, u32[]{:S(2)}) %collective-permute-start.5) | collective-permute-done | bytes 278560 | tf_op jit(solution)/shard_map/ppermute | solution.py:484
  41.5 2.6 %pick_states.2 = (bf16[2,544,128]{2,1,0:T(8,128)(2,1)S(1)}, bf16[2,544,128]{2,1,0:T(8,128)(2,1)S(1)}, bf16[2,544,128]{2,1,0:T(8,128)(2,1)S(1)}, bf16[2,544,128]{2,1,0:T(8,128)(2,1)S(1)}) custom-call(s32[8]{0:T(128)S(1)} %broadcast_xor_fusion.refs_10_.refs_0_, bf16[1056,128]{1,0:T(8,128)(2,1)S(1)} %get-tuple-element.36.refs_9_.refs_1_, ...), custom_call_target="tpu_custom_call" | custom-call | flops 1 | bytes 1 | tf_op jit(solution)/shard_map/pick_states/pallas_call | solution.py:555
  44.1 0.4 collective-permute-start.6
  44.4 2.7 %collective-permute-start.7 = (bf16[2,544,128]{2,1,0:T(8,128)(2,1)S(1)}, bf16[2,544,128]{2,1,0:T(8,128)(2,1)S(1)}, u32[]{:S(2)}, u32[]{:S(2)}) collective-permute-start(bf16[2,544,128]{2,1,0:T(8,128)(2,1)S(1)} %get-tuple-element.53), channel_id=1, source_target_pairs={{0,4},{2,6},{4,0},{6,2},{8,12},{10,14},{12,8},{14,10},{1,5},{3,7},... | collective-permute-start | bytes 835592 | tf_op jit(solution)/shard_map/ppermute | solution.py:484
  47.1 0.5 collective-permute-start.8
  47.6 11.5 %collective-permute-done.9.refs_5_ = bf16[4,512,128]{2,1,0:T(8,128)(2,1)S(1)} collective-permute-done((bf16[4,512,128]{2,1,0:T(8,128)(2,1)S(1)}, bf16[4,512,128]{2,1,0:T(8,128)(2,1)S(1)}, u32[]{:S(2)}, u32[]{:S(2)}) %collective-permute-start.9) | collective-permute-done | bytes 524320 | tf_op jit(solution)/shard_map/ppermute | solution.py:484
  59.1 2.5 %pick_states.3 = (bf16[2,512,128]{2,1,0:T(8,128)(2,1)S(1)}, bf16[2,512,128]{2,1,0:T(8,128)(2,1)S(1)}, bf16[2,512,128]{2,1,0:T(8,128)(2,1)S(1)}, bf16[2,512,128]{2,1,0:T(8,128)(2,1)S(1)}) custom-call(s32[8]{0:T(128)S(1)} %broadcast_xor_fusion.refs_10_.refs_0_, bf16[1056,128]{1,0:T(8,128)(2,1)S(1)} %get-tuple-element.36.refs_9_.refs_1_, ...), custom_call_target="tpu_custom_call" | custom-call | flops 1 | bytes 1 | tf_op jit(solution)/shard_map/pick_states/pallas_call | solution.py:555
  61.6 1.7 %collective-permute-start.10 = (bf16[2,512,128]{2,1,0:T(8,128)(2,1)S(1)}, bf16[2,512,128]{2,1,0:T(8,128)(2,1)S(1)}, u32[]{:S(2)}, u32[]{:S(2)}) collective-permute-start(bf16[2,512,128]{2,1,0:T(8,128)(2,1)S(1)} %get-tuple-element.56), channel_id=1, source_target_pairs={{0,2},{2,0},{4,6},{6,4},{8,10},{10,8},{12,14},{14,12},{1,3},{3,1},... | collective-permute-start | bytes 786440 | tf_op jit(solution)/shard_map/ppermute | solution.py:484
  63.3 0.0 collective-permute-start.11
  63.3 0.0 collective-permute-done.6.refs_8_.refs_12_
  63.3 1.8 %collective-permute-start.12 = (bf16[2,512,128]{2,1,0:T(8,128)(2,1)S(1)}, bf16[2,512,128]{2,1,0:T(8,128)(2,1)S(1)}, u32[]{:S(2)}, u32[]{:S(2)}) collective-permute-start(bf16[2,512,128]{2,1,0:T(8,128)(2,1)S(1)} %get-tuple-element.58), channel_id=1, source_target_pairs={{0,6},{2,4},{4,2},{6,0},{8,14},{10,12},{12,10},{14,8},{1,7},{3,5},... | collective-permute-start | bytes 786440 | tf_op jit(solution)/shard_map/ppermute | solution.py:484
  65.1 0.0 collective-permute-done.7.refs_9_.refs_13_
  65.1 6.2 %collective-permute-done.8.refs_10_.refs_14_ = bf16[2,544,128]{2,1,0:T(8,128)(2,1)S(1)} collective-permute-done((bf16[2,544,128]{2,1,0:T(8,128)(2,1)S(1)}, bf16[2,544,128]{2,1,0:T(8,128)(2,1)S(1)}, u32[]{:S(2)}, u32[]{:S(2)}) %collective-permute-start.8) | collective-permute-done | bytes 278560 | tf_op jit(solution)/shard_map/ppermute | solution.py:484
  71.4 5.8 %late.2.refs_23_ = bf16[2,256,4096]{2,1,0:T(8,128)(2,1)} custom-call(s32[1]{0:T(128)} %bitcast.refs_0_, bf16[2,256,4096]{2,1,0:T(8,128)(2,1)} %refs_1_.11, bf16[2,256,512]{2,1,0:T(8,128)(2,1)} %refs_2_.13, bf16[2,256,512]{2,1,0:T(8,128)(2,1)} %refs_3_.13, f32[1,4096]{1,0:T(1,128)S(1)} %broadcast_in_dim_reshape.3.refs_6_.refs_4_, f32[4,4096]{1,0:T(4,128)} %refs_5_.5, ...), custom_call_target="tpu_custom_call" | custom-call | flops 1 | bytes 1 | tf_op jit(solution)/shard_map/late/pallas_call | solution.py:649
  77.1 0.0 collective-permute-done.10.refs_12_
  77.1 0.0 collective-permute-done.11.refs_13_
  77.1 3.3 %collective-permute-done.12.refs_14_ = bf16[2,512,128]{2,1,0:T(8,128)(2,1)S(1)} collective-permute-done((bf16[2,512,128]{2,1,0:T(8,128)(2,1)S(1)}, bf16[2,512,128]{2,1,0:T(8,128)(2,1)S(1)}, u32[]{:S(2)}, u32[]{:S(2)}) %collective-permute-start.12) | collective-permute-done | bytes 262176 | tf_op jit(solution)/shard_map/ppermute | solution.py:484
  80.5 5.8 %late.3 = bf16[2,256,4096]{2,1,0:T(8,128)(2,1)} custom-call(s32[1]{0:T(128)} %bitcast.refs_0_, bf16[2,256,4096]{2,1,0:T(8,128)(2,1)} %refs_1_.11, bf16[2,256,512]{2,1,0:T(8,128)(2,1)} %refs_2_.13, bf16[2,256,512]{2,1,0:T(8,128)(2,1)} %refs_3_.13, f32[1,4096]{1,0:T(1,128)S(1)} %broadcast_in_dim_reshape.3.refs_6_.refs_4_, ...), custom_call_target="tpu_custom_call", output_to_operand_aliasing={{}: (23, {})} | custom-call | flops 1 | bytes 1 | tf_op jit(solution)/shard_map/late/pallas_call | solution.py:649
  (9 shorter events, 0.0 us)
Async XLA Ops:
  1.4 30.4 %collective-permute-start.4 = (bf16[2,544,128]{2,1,0:T(8,128)(2,1)S(1)}, bf16[2,544,128]{2,1,0:T(8,128)(2,1)S(1)}, u32[]{:S(2)}, u32[]{:S(2)}) collective-permute-start(bf16[2,544,128]{2,1,0:T(8,128)(2,1)S(1)} %get-tuple-element.40), channel_id=1, source_target_pairs={{0,12},{2,14},{4,8},{6,10},{8,4},{10,6},{12,0},{14,2},{1,13},{3,15... | collective-permute-start | bytes 835592 | tf_op jit(solution)/shard_map/ppermute | solution.py:484
  6.5 5.4 %copy-start.3 = (s32[8]{0:T(128)S(1)}, s32[8]{0:T(128)}, u32[]{:S(2)}) copy-start(s32[8]{0:T(128)} %param.26) | copy-start | bytes 100
  6.5 5.5 %copy-start.4 = (s32[16]{0:T(128)S(1)}, s32[16]{0:T(128)}, u32[]{:S(2)}) copy-start(s32[16]{0:T(128)} %param.27) | copy-start | bytes 196
  6.5 5.8 %copy-start = (f32[64]{0:T(128)S(1)}, f32[64]{0:T(128)}, u32[]{:S(2)}) copy-start(f32[64]{0:T(128)} %param.18) | copy-start | bytes 772
  6.5 5.9 %copy-start.1 = (f32[64]{0:T(128)S(1)}, f32[64]{0:T(128)}, u32[]{:S(2)}) copy-start(f32[64]{0:T(128)} %param.19) | copy-start | bytes 772
  6.5 6.0 %copy-start.2 = (f32[64]{0:T(128)S(1)}, f32[64]{0:T(128)}, u32[]{:S(2)}) copy-start(f32[64]{0:T(128)} %param.20) | copy-start | bytes 772
  6.5 25.3 %collective-permute-start.3 = (bf16[2,544,128]{2,1,0:T(8,128)(2,1)S(1)}, bf16[2,544,128]{2,1,0:T(8,128)(2,1)S(1)}, u32[]{:S(2)}, u32[]{:S(2)}) collective-permute-start(bf16[2,544,128]{2,1,0:T(8,128)(2,1)S(1)} %get-tuple-element.35.refs_17_), channel_id=1, source_target_pairs={{0,8},{2,10},{4,12},{6,14},{8,0},{10,2},{12,4},{14,6},{1,9},{3,11}... | collective-permute-start | bytes 835592 | tf_op jit(solution)/shard_map/ppermute | solution.py:484
  8.3 20.5 %collective-permute-start = (bf16[1056,128]{1,0:T(8,128)(2,1)S(1)}, bf16[1056,128]{1,0:T(8,128)(2,1)S(1)}, u32[]{:S(2)}, u32[]{:S(2)}) collective-permute-start(bf16[1056,128]{1,0:T(8,128)(2,1)S(1)} %get-tuple-element.37), channel_id=1, source_target_pairs={{0,2},{2,0},{4,6},{6,4},{8,10},{10,8},{12,14},{14,12},{1,3},{3,1},... | collective-permute-start | bytes 811016 | tf_op jit(solution)/shard_map/ppermute | solution.py:484
  9.9 18.9 %collective-permute-start.1 = (bf16[1056,128]{1,0:T(8,128)(2,1)S(1)}, bf16[1056,128]{1,0:T(8,128)(2,1)S(1)}, u32[]{:S(2)}, u32[]{:S(2)}) collective-permute-start(bf16[1056,128]{1,0:T(8,128)(2,1)S(1)} %get-tuple-element.38), channel_id=1, source_target_pairs={{0,4},{2,6},{4,0},{6,2},{8,12},{10,14},{12,8},{14,10},{1,5},{3,7},... | collective-permute-start | bytes 811016 | tf_op jit(solution)/shard_map/ppermute | solution.py:484
  10.6 21.1 %collective-permute-start.2 = (bf16[1056,128]{1,0:T(8,128)(2,1)S(1)}, bf16[1056,128]{1,0:T(8,128)(2,1)S(1)}, u32[]{:S(2)}, u32[]{:S(2)}) collective-permute-start(bf16[1056,128]{1,0:T(8,128)(2,1)S(1)} %get-tuple-element.39), channel_id=1, source_target_pairs={{0,6},{2,4},{4,2},{6,0},{8,14},{10,12},{12,10},{14,8},{1,7},{3,5},... | collective-permute-start | bytes 811016 | tf_op jit(solution)/shard_map/ppermute | solution.py:484
  32.9 8.6 %collective-permute-start.5 = (bf16[2,544,128]{2,1,0:T(8,128)(2,1)S(1)}, bf16[2,544,128]{2,1,0:T(8,128)(2,1)S(1)}, u32[]{:S(2)}, u32[]{:S(2)}) collective-permute-start(bf16[2,544,128]{2,1,0:T(8,128)(2,1)S(1)} %stack_a.1.refs_9_), channel_id=1, source_target_pairs={{0,2},{2,0},{4,6},{6,4},{8,10},{10,8},{12,14},{14,12},{1,3},{3,1},... | collective-permute-start | bytes 835592 | tf_op jit(solution)/shard_map/ppermute | solution.py:484
  33.4 25.6 %collective-permute-start.9 = (bf16[4,512,128]{2,1,0:T(8,128)(2,1)S(1)}, bf16[4,512,128]{2,1,0:T(8,128)(2,1)S(1)}, u32[]{:S(2)}, u32[]{:S(2)}) collective-permute-start(bf16[4,512,128]{2,1,0:T(8,128)(2,1)S(1)} %stack_b.1.refs_3_), channel_id=1, source_target_pairs={{0,8},{2,10},{4,12},{6,14},{8,0},{10,2},{12,4},{14,6},{1,9},{3,11}... | collective-permute-start | bytes 1572872 | tf_op jit(solution)/shard_map/ppermute | solution.py:484
  44.1 19.2 %collective-permute-start.6 = (bf16[2,544,128]{2,1,0:T(8,128)(2,1)S(1)}, bf16[2,544,128]{2,1,0:T(8,128)(2,1)S(1)}, u32[]{:S(2)}, u32[]{:S(2)}) collective-permute-start(bf16[2,544,128]{2,1,0:T(8,128)(2,1)S(1)} %get-tuple-element.52), channel_id=1, source_target_pairs={{0,2},{2,0},{4,6},{6,4},{8,10},{10,8},{12,14},{14,12},{1,3},{3,1},... | collective-permute-start | bytes 835592 | tf_op jit(solution)/shard_map/ppermute | solution.py:484
  44.4 20.7 %collective-permute-start.7 = (bf16[2,544,128]{2,1,0:T(8,128)(2,1)S(1)}, bf16[2,544,128]{2,1,0:T(8,128)(2,1)S(1)}, u32[]{:S(2)}, u32[]{:S(2)}) collective-permute-start(bf16[2,544,128]{2,1,0:T(8,128)(2,1)S(1)} %get-tuple-element.53), channel_id=1, source_target_pairs={{0,4},{2,6},{4,0},{6,2},{8,12},{10,14},{12,8},{14,10},{1,5},{3,7},... | collective-permute-start | bytes 835592 | tf_op jit(solution)/shard_map/ppermute | solution.py:484
  47.1 24.3 %collective-permute-start.8 = (bf16[2,544,128]{2,1,0:T(8,128)(2,1)S(1)}, bf16[2,544,128]{2,1,0:T(8,128)(2,1)S(1)}, u32[]{:S(2)}, u32[]{:S(2)}) collective-permute-start(bf16[2,544,128]{2,1,0:T(8,128)(2,1)S(1)} %get-tuple-element.54), channel_id=1, source_target_pairs={{0,6},{2,4},{4,2},{6,0},{8,14},{10,12},{12,10},{14,8},{1,7},{3,5},... | collective-permute-start | bytes 835592 | tf_op jit(solution)/shard_map/ppermute | solution.py:484
  61.6 15.6 %collective-permute-start.10 = (bf16[2,512,128]{2,1,0:T(8,128)(2,1)S(1)}, bf16[2,512,128]{2,1,0:T(8,128)(2,1)S(1)}, u32[]{:S(2)}, u32[]{:S(2)}) collective-permute-start(bf16[2,512,128]{2,1,0:T(8,128)(2,1)S(1)} %get-tuple-element.56), channel_id=1, source_target_pairs={{0,2},{2,0},{4,6},{6,4},{8,10},{10,8},{12,14},{14,12},{1,3},{3,1},... | collective-permute-start | bytes 786440 | tf_op jit(solution)/shard_map/ppermute | solution.py:484
  63.3 13.8 %collective-permute-start.11 = (bf16[2,512,128]{2,1,0:T(8,128)(2,1)S(1)}, bf16[2,512,128]{2,1,0:T(8,128)(2,1)S(1)}, u32[]{:S(2)}, u32[]{:S(2)}) collective-permute-start(bf16[2,512,128]{2,1,0:T(8,128)(2,1)S(1)} %get-tuple-element.57), channel_id=1, source_target_pairs={{0,4},{2,6},{4,0},{6,2},{8,12},{10,14},{12,8},{14,10},{1,5},{3,7},... | collective-permute-start | bytes 786440 | tf_op jit(solution)/shard_map/ppermute | solution.py:484
  63.3 17.2 %collective-permute-start.12 = (bf16[2,512,128]{2,1,0:T(8,128)(2,1)S(1)}, bf16[2,512,128]{2,1,0:T(8,128)(2,1)S(1)}, u32[]{:S(2)}, u32[]{:S(2)}) collective-permute-start(bf16[2,512,128]{2,1,0:T(8,128)(2,1)S(1)} %get-tuple-element.58), channel_id=1, source_target_pairs={{0,6},{2,4},{4,2},{6,0},{8,14},{10,12},{12,10},{14,8},{1,7},{3,5},... | collective-permute-start | bytes 786440 | tf_op jit(solution)/shard_map/ppermute | solution.py:484

commit v13 on v12

--- a/solution.py
+++ b/solution.py
@@ -8,7 +8,7 @@
 from jax.sharding import PartitionSpec as P
 
 VMEM_LIMIT = 12 * 1024 * 1024
-SPLIT = (8, 8)
+SPLIT = (8, 4, 4)
 FIX = 16
 LOG2_E = 1.4426950408889634
 
@@ -45,7 +45,7 @@
 
 def early_kernel(
     base, x_ref, b_ref, c_ref, dt_ref, bias_ref, alog_ref, skip_ref, taps_x_ref, taps_bc_ref,
-    mixed_ref, c_out_ref, column_ref, first_ref, padded,
+    mixed_ref, c_out_ref, column_ref, first_ref, opening_ref, weights_ref, padded,
 ):
     length, wide = x_ref.shape[1:]
     heads = dt_ref.shape[1]
@@ -60,6 +60,15 @@
     b_conv = convolve(b_ref[0], taps_bc_ref[0], 0)
     c_conv = convolve(c_ref[0], taps_bc_ref[1], 1)
     c_out_ref[q] = c_conv
+    size = b_ref.shape[2]
+    taps = taps_x_ref.shape[0]
+    opening_ref[q, :, :wide] = x_ref[0, :FIX]
+    opening_ref[q, :, wide : wide + size] = b_ref[0, :FIX]
+    opening_ref[q, :, wide + size :] = c_ref[0, :FIX]
+    weights_ref[q, :taps, :wide] = taps_x_ref[...]
+    weights_ref[q, :taps, wide : wide + size] = taps_bc_ref[0]
+    weights_ref[q, :taps, wide + size :] = taps_bc_ref[1]
+    weights_ref[q, taps : taps + 1, :wide] = skip_ref[...]
     scores = lax.dot_general(
         c_conv, b_conv, (((1,), (1,)), ((), ())), preferred_element_type=jnp.float32
     )
@@ -113,23 +122,13 @@
         ] * x_conv.astype(jnp.float32)
 
 
-def late_kernel(
-    offset, lines, place_ref, x_ref, b_ref, c_ref, skip_ref, taps_x_ref, taps_bc_ref, *refs
-):
+def late_kernel(offset, heads, lines, reach, tail_at, place_ref, *refs):
     tails, states, parts, (y_ref, padded) = refs[:4], refs[4:8], refs[8:-2], refs[-2:]
     kids, length, wide = y_ref.shape
-    width = 64
-    heads = wide // width
-    reach = taps_x_ref.shape[0] - 1
+    width = wide // heads
     q = pl.program_id(0)
     far = q ^ place_ref[0]
-    size = c_ref.shape[2] // pl.num_programs(0)
-    stride = skip_ref.shape[1] // pl.num_programs(0)
-    group_lanes = pl.ds(pl.multiple_of(q * size, 128), size)
     low_first = lax.broadcasted_iota(jnp.int32, (FIX, 2 * width), 1) < width
-    spread_row = lax.broadcasted_iota(jnp.int32, (4 * heads, wide), 0)
-    spread_lane = lax.broadcasted_iota(jnp.int32, (4 * heads, wide), 1)
-    spread = (spread_row % heads == spread_lane // width).astype(jnp.bfloat16)
     contract = (((1,), (1,)), ((), ()))
 
     def choose(blocks):
@@ -137,41 +136,46 @@
         return jnp.where(far <= 1, near, jnp.where(far == 2, blocks[2], blocks[3]))
 
     for kid in range(kids):
-        held_ref, column_ref, first_ref, mixed_ref = parts[4 * kid : 4 * kid + 4]
-        tail = choose([ref[kid] for ref in tails]).astype(jnp.float32)
-        state = choose([ref[kid] for ref in states])
-
-        def opening(scratch, rows, taps, at, count):
+        mixed_ref, held_ref, column_ref, first_ref, opening_ref, weights_ref = parts[
+            6 * kid : 6 * kid + 6
+        ]
+        size = held_ref.shape[2]
+        per_group = column_ref.shape[1]
+        group_wide = opening_ref.shape[2] - 2 * size
+        tail_rows = pl.ds(tail_at, -(-lines * reach // 16) * 16)
+        tail = choose([ref[kid, tail_rows] for ref in tails]).astype(jnp.float32)
+        state = choose([ref[kid, : heads * width] for ref in states])
+
+        def opening(start, stop, at):
             tap_rows = []
             for k in range(reach):
-                here = [tail[k * lines + at + n : k * lines + at + n + 1] for n in range(count)]
+                first = k * lines + at
+                count = (stop - start) // 128
+                here = [tail[first + n : first + n + 1] for n in range(count)]
                 tap_rows.append(jnp.concatenate(here, axis=1))
-            return conv_silu(scratch, jnp.concatenate(tap_rows), rows, taps)
-
-        start = pl.multiple_of(q * stride + offset * width, 128)
-        chunk_lanes = pl.ds(start, wide)
-        blocks = wide // 128
-        bc_first = opening(
-            padded.at[kid, :, wide : wide + 2 * size],
-            jnp.concatenate([b_ref[kid, :, group_lanes], c_ref[kid, :, group_lanes]], axis=1),
-            jnp.concatenate([taps_bc_ref[0, :, group_lanes], taps_bc_ref[1, :, group_lanes]], axis=1),
-            lines - 2,
-            2,
+            return conv_silu(
+                padded.at[kid, :, : stop - start],
+                jnp.concatenate(tap_rows),
+                opening_ref[q, :, start:stop],
+                weights_ref[q, : reach + 1, start:stop],
+            )
+
+        bc_first = opening(group_wide, group_wide + 2 * size, lines - 2)
+        b_first, c_first = bc_first[:, :size], bc_first[:, size:]
+        start = offset * width
+        x_all = opening(start, start + wide, start // 128).astype(jnp.float32)
+        skipped = weights_ref[q, reach + 1 : reach + 2, start : start + wide] * x_all
+        c_conv = jnp.concatenate([c_first, held_ref[q, FIX:]])
+        terms = three_terms(jnp.exp2(column_ref[q]))
+        terms = jnp.concatenate([terms, jnp.zeros((per_group, length), jnp.float32)])
+        spread_row = lax.broadcasted_iota(jnp.int32, (4 * per_group, wide), 0)
+        spread_lane = lax.broadcasted_iota(jnp.int32, (4 * per_group, wide), 1)
+        spread = spread_row % per_group == offset + spread_lane // width
+        grow = jnp.dot(
+            terms.T.astype(jnp.bfloat16),
+            spread.astype(jnp.float32).astype(jnp.bfloat16),
+            preferred_element_type=jnp.float32,
         )
-        b_first, c_first = bc_first[:, :size], bc_first[:, size:]
-        x_all = opening(
-            padded.at[kid, :, :wide],
-            x_ref[kid, :, chunk_lanes],
-            taps_x_ref[:, chunk_lanes],
-            offset * width // 128,
-            blocks,
-        ).astype(jnp.float32)
-        skipped = skip_ref[:, chunk_lanes] * x_all
-        c_conv = jnp.concatenate([c_first, held_ref[q, FIX:]])
-        grow = jnp.exp2(column_ref[q, offset : offset + heads, :])
-        terms = jnp.concatenate([three_terms(grow), jnp.zeros_like(grow)])
-        terms = terms.T.astype(jnp.bfloat16)
-        grow = jnp.dot(terms, spread, preferred_element_type=jnp.float32)
         term = lax.dot_general(c_conv, state, contract, preferred_element_type=jnp.float32)
         carried = (term * grow).astype(jnp.bfloat16)
         scores = lax.dot_general(
@@ -180,8 +184,8 @@
             contract,
             preferred_element_type=jnp.float32,
         )
-        unit = offset // heads * heads * FIX
-        mixing = (scores * first_ref[q, :, unit : unit + heads * FIX]).astype(jnp.bfloat16)
+        here = slice(offset * FIX, (offset + heads) * FIX)
+        mixing = (scores * first_ref[q, :, here]).astype(jnp.bfloat16)
         for pair in range(heads // 2):
             lanes = slice(pair * 2 * width, (pair + 1) * 2 * width)
             x_first = x_all[:, lanes]
@@ -197,9 +201,9 @@
                 preferred_element_type=jnp.float32,
             )
             part = jnp.concatenate([part[:FIX] + skipped[:, lanes], part[FIX:]])
-            here = slice(offset * width + lanes.start, offset * width + lanes.stop)
+            whole = slice(start + lanes.start, start + lanes.stop)
             y_ref[kid, :, lanes] = (
-                mixed_ref[q, :, here] + part + carried[:, lanes].astype(jnp.float32)
+                mixed_ref[q, :, whole] + part + carried[:, lanes].astype(jnp.float32)
             ).astype(jnp.bfloat16)
 
 
@@ -483,50 +487,48 @@
     def swap(value, r):
         return lax.ppermute(value, "batch", perm=[(i, i ^ r) for i in range(8)])
 
-    def cast(chunks, paired, tokens):
-        part = sum(SPLIT[k] for k in chunks)
-        rows = part * width + tail_lines
-        block = [SPLIT[k] for k in chunks]
+    def cast():
+        rows = per_group * width + tail_lines
+        rows_a = SPLIT[0] * width + tail_lines
+        count = len(SPLIT) + 2
 
         def kernel(place_ref, *refs):
-            count = len(chunks) + 2
-            ins, outs = refs[: count * 4], refs[count * 4 :]
+            ins, outs = refs[: 4 * count], refs[4 * count :]
             for n in range(4):
-                out_ref = outs[n // 2].at[n % 2] if paired else outs[n]
                 cast_kernel(
-                    len(chunks), [tail_lines], reach, lines, *ins[count * n : count * n + count], out_ref
+                    len(SPLIT), [tail_lines], reach, lines, *ins[count * n : count * n + count], outs[n]
                 )
+                outs[4 + n // 2][n % 2] = outs[n][:rows_a]
 
         operands, specs = [], []
         for n in range(4):
-            which = lambda i, p, n=n: p[0] ^ n
-            for k in chunks:
+            for part, offset in zip(SPLIT, offsets):
                 operands.append(state)
                 specs.append(
                     pl.BlockSpec(
-                        (1, SPLIT[k], width, size),
-                        lambda i, p, w=which, at=offsets[k] // SPLIT[k]: (w(i, p), at, 0, 0),
+                        (1, part, width, size),
+                        lambda i, p, n=n, at=offset // part: (p[0] ^ n, at, 0, 0),
                     )
                 )
             operands += [x_tails, bc_tails]
             specs += [
-                pl.BlockSpec((1, reach, wide), lambda i, p, w=which: (0, 0, w(i, p))),
-                pl.BlockSpec((1, reach, 2, size), lambda i, p, w=which: (0, 0, 0, w(i, p))),
+                pl.BlockSpec((1, reach, wide), lambda i, p, n=n: (0, 0, p[0] ^ n)),
+                pl.BlockSpec((1, reach, 2, size), lambda i, p, n=n: (0, 0, 0, p[0] ^ n)),
             ]
-        shapes = [(2, rows, size)] * 2 if paired else [(rows, size)] * 4
+        shapes = [(rows, size)] * 4 + [(2, rows_a, size)] * 2
         return pl.pallas_call(
-            functools.partial(drop_tokens, kernel, 1 + len(operands), len(tokens)),
+            kernel,
             grid_spec=pltpu.PrefetchScalarGridSpec(
                 num_scalar_prefetch=1,
                 grid=(1,),
-                in_specs=specs + [anywhere] * len(tokens),
+                in_specs=specs,
                 out_specs=[pl.BlockSpec(memory_space=pltpu.VMEM)] * len(shapes),
             ),
             out_shape=[pltpu.VMEM(shape, jnp.bfloat16) for shape in shapes],
             compiler_params=params,
             cost_estimate=small,
             name="cast_states",
-        )(place, *operands, *tokens)
+        )(place, *operands)
 
     def rearrange(scalars, sources, moves, shapes, tokens, name):
         def kernel(scalars_ref, *refs):
@@ -602,12 +604,14 @@
                 pl.BlockSpec((2, taps, size), lambda q: (0, 0, per * piece + q)),
                 *[anywhere] * len(tokens),
             ],
-            out_specs=[pl.BlockSpec(memory_space=pltpu.VMEM)] * 4,
+            out_specs=[pl.BlockSpec(memory_space=pltpu.VMEM)] * 6,
             out_shape=[
                 pltpu.VMEM((groups, length, wide), jnp.float32),
                 pltpu.VMEM((groups, length, size), jnp.bfloat16),
                 pltpu.VMEM((groups, per_group, length), jnp.float32),
                 pltpu.VMEM((groups, length, per_group * FIX), jnp.float32),
+                pltpu.VMEM((groups, FIX, wide + 2 * size), jnp.bfloat16),
+                pltpu.VMEM((groups, 8, wide + 2 * size), jnp.float32),
             ],
             input_output_aliases={first + i: i for i in range(len(before))},
             scratch_shapes=[pltpu.VMEM((2, 8 + length, size), jnp.float32)],
@@ -619,25 +623,9 @@
     def late(k, states, states_first, parts, result, tokens):
         part, offset = SPLIT[k], offsets[k]
         chunk = part * width
-        unit = offset // part
-        lane = lambda q, p: (0, 0, q * (per_group // part) + unit)
-        tail_at = SPLIT[0] * width // tail_lines
-        in_vmem = pl.BlockSpec(memory_space=pltpu.VMEM)
-        operands = [x_in, b_in, c_in, skip_row, conv_x, conv_bc, *states_first, *states]
-        specs = [
-            pl.BlockSpec((kids, FIX, columns), lambda q, p: (0, 0, 0)),
-            pl.BlockSpec((kids, FIX, groups * size), lambda q, p: (0, 0, 0)),
-            pl.BlockSpec((kids, FIX, groups * size), lambda q, p: (0, 0, 0)),
-            pl.BlockSpec((1, columns), lambda q, p: (0, 0)),
-            pl.BlockSpec((taps, columns), lambda q, p: (0, 0)),
-            pl.BlockSpec((2, taps, groups * size), lambda q, p: (0, 0, 0)),
-            *[pl.BlockSpec((kids, tail_lines, size), lambda q, p: (0, tail_at, 0))] * 4,
-            *[pl.BlockSpec((kids, chunk, size), lambda q, p: (0, 0, 0))] * 4,
-        ]
-        for c in range(kids):
-            mixed, held, column, first = parts[c]
-            operands += [keep_in_vmem(a) for a in (held, column, first, mixed)]
-            specs += [in_vmem] * 4
+        lane = lambda q, p: (0, 0, q * (per_group // part) + offset // part)
+        operands = [keep_in_vmem(a) for a in (*states_first, *states, *parts[0], *parts[1])]
+        specs = [pl.BlockSpec(memory_space=pltpu.VMEM)] * len(operands)
         keep = 1 + len(operands)
         operands += tokens
         specs += [anywhere] * len(tokens)
@@ -646,19 +634,15 @@
             alias = {1 + len(operands): 0}
             operands.append(result)
             specs.append(anywhere)
+        kernel = functools.partial(late_kernel, offset, part, lines, reach, SPLIT[0] * width)
         return pl.pallas_call(
-            functools.partial(
-                drop_tokens,
-                functools.partial(late_kernel, offset, lines),
-                keep,
-                1 + len(operands) - keep,
-            ),
+            functools.partial(drop_tokens, kernel, keep, 1 + len(operands) - keep),
             grid_spec=pltpu.PrefetchScalarGridSpec(
                 num_scalar_prefetch=1,
                 grid=(groups,),
                 in_specs=specs,
                 out_specs=pl.BlockSpec((kids, length, chunk), lane),
-                scratch_shapes=[pltpu.VMEM((kids, 8 + FIX, chunk + 2 * size), jnp.float32)],
+                scratch_shapes=[pltpu.VMEM((kids, 8 + FIX, max(chunk, 2 * size)), jnp.float32)],
             ),
             out_shape=jax.ShapeDtypeStruct(x_in.shape, jnp.bfloat16),
             input_output_aliases=alias,
@@ -668,34 +652,38 @@
         )(place, *operands)
 
     skip_row = jnp.repeat(d_skip, width)[None, :]
-    rows = [SPLIT[0] * width + tail_lines, SPLIT[1] * width]
-    chunk_a, chunk_b = pl.ds(0, rows[0]), pl.ds(rows[0], rows[1])
-
-    sent_a = cast([0], True, [])
-    crossed_a = [swap(sent_a[0], 4), swap(sent_a[1], 6)]
-    own = cast([0, 1], False, [sent_a[0]])
+    rows = [SPLIT[0] * width + tail_lines] + [part * width for part in SPLIT[1:]]
+    chunks = [pl.ds(sum(rows[:k]), rows[k]) for k in range(len(SPLIT))]
+    *own, sent_4, sent_6 = cast()
+    crossed_a = [swap(sent_4, 4), swap(sent_6, 6)]
     inside = [own[0]] + [swap(own[j], j) for j in range(1, 4)]
+
+    def cross(k, tokens):
+        moves = [(0, j, None, [(j, chunks[k])]) for j in range(4)]
+        (sent,) = rearrange(place, inside, moves, [(4, rows[k], size)], tokens, "stack_later")
+        return sent, swap(sent, 4)
+
+    def pick_later(k, crossed, tokens):
+        choices = [(j, chunks[k]) for j in range(4)] + [(4, j) for j in range(4)]
+        return pick(rows[k], [*inside, crossed], choices, tokens)
+
     first = early(0, 0, [], [own[0], slots])
     first = early(0, 1, first, [])
     second = early(1, 0, [], [first[1]])
-    moves = [(0, j, None, [(j, chunk_b)]) for j in range(4)]
-    (sent_b,) = rearrange(
-        place, inside, moves, [(4, rows[1], size)], [second[1], *crossed_a], "stack_b"
-    )
-    crossed_b = swap(sent_b, 4)
+    sent_b, crossed_b = cross(1, [second[1], *crossed_a])
     moves = [(0, n, None, [(n, 1)]) for n in range(2)]
-    (spread,) = rearrange(
-        place, crossed_a, moves, [(2, rows[0], size)], [sent_b], "stack_a"
-    )
+    (spread,) = rearrange(place, crossed_a, moves, [(2, rows[0], size)], [sent_b], "stack_first")
     passed = swap(spread, 1)
-    second = early(1, 1, second, [spread])
-    choices = [(j, chunk_a) for j in range(4)] + [(4, 0), (6, 0), (5, 0), (6, 1)]
-    states_a = pick(rows[0], [*inside, *crossed_a, passed], choices, [second[1]])
-    choices = [(j, chunk_b) for j in range(4)] + [(4, j) for j in range(4)]
-    states_b = pick(rows[1], [*inside, crossed_b], choices, [states_a[0]])
+    choices = [(j, chunks[0]) for j in range(4)] + [(4, 0), (6, 0), (5, 0), (6, 1)]
+    states_a = pick(rows[0], [*inside, *crossed_a, passed], choices, [])
+    sent_c, crossed_c = cross(2, [states_a[0], crossed_b])
+    states_b = pick_later(1, crossed_b, [sent_c])
+    second = early(1, 1, second, [states_b[0]])
+    states_c = pick_later(2, crossed_c, [second[1]])
     parts = [first, second]
-    result = late(0, states_a, states_a, parts, None, [states_b[0]])
-    return late(1, states_b, states_a, parts, result, [])
+    result = late(0, states_a, states_a, parts, None, [states_c[0]])
+    result = late(1, states_b, states_a, parts, result, [])
+    return late(2, states_c, states_a, parts, result, [])
 
 
 def solution(mesh):

time: 86.6 us -> 84.6 us (0.977)
  waiting for transfers between devices: 25 us -> 10.5 us
  starting transfers between devices: 18.1 us -> 30.5 us
    ppermute x13 -> x17, waiting for transfers between devices: 25 us -> 10.5 us  [swap(): return lax.ppermute(value, 'batch', perm=[(i, i ^ r) for i in range(8)])]
    ppermute x13 -> x17, starting transfers between devices: 18.1 us -> 30.5 us  [swap(): return lax.ppermute(value, 'batch', perm=[(i, i ^ r) for i in range(8)])]
    pallas_call x4 -> x6, Pallas kernels: 6.16 us -> 7.29 us  [rearrange(): pl.pallas_call(functools.partial(drop_tokens, kernel, 1 + len(sources), l...]
    pallas_call x4, Pallas kernels: 14.6 us -> 13.6 us  [the longest x3 11.8 us: late(): pl.pallas_call(functools.partial(drop_tokens, kernel, keep, 1 + len(opera...]
  transfers between devices with their start and end apart: 13 -> 17, of which waited for: 5 -> 4; matrix products, arithmetic and copies ran while one was open for 1% -> 1% of each run, Pallas kernels for 39% -> 43%
where the time goes in v13:
time: 84.6 us; the launch traced here: 84.3 us
  Pallas kernels  42.4 us (50%)
  starting transfers between devices  30.5 us (36%)
  waiting for transfers between devices  10.5 us (12%)
    ppermute x17, starting transfers between devices, swap(): return lax.ppermute(value, 'batch', perm=[(i, i ^ r) for i in range(8)])  30.5 us
    pallas_call x4, Pallas kernels, early(): pl.pallas_call(functools.partial(drop_tokens, functools.partial(early_ker...  21.5 us
    pallas_call x3, Pallas kernels, late(): pl.pallas_call(functools.partial(drop_tokens, kernel, keep, 1 + len(opera...  11.8 us
    ppermute x17, waiting for transfers between devices, swap(): return lax.ppermute(value, 'batch', perm=[(i, i ^ r) for i in range(8)])  10.5 us
    pallas_call x6, Pallas kernels, rearrange(): pl.pallas_call(functools.partial(drop_tokens, kernel, 1 + len(sources), l...  7.29 us
    pallas_call x1, Pallas kernels, cast(): pl.pallas_call(kernel, grid_spec=pltpu.PrefetchScalarGridSpec(num_scalar_...  1.82 us
  transfers between devices with their start and end apart: 17, of which 4 were waited for; matrix products, arithmetic and copies ran while one was open for 1% of the time, Pallas kernels for 43%

profile of v13, /device:TPU:0, one launch (start us, length us, event | category | flops | bytes accessed | tf_op | source)
XLA Modules:
  0.0 84.3 jit_solution(7259846602359967202)
XLA Ops:
  0.0 1.8 %cast_states.1 = (bf16[1056,128]{1,0:T(8,128)(2,1)S(1)}, bf16[1056,128]{1,0:T(8,128)(2,1)S(1)}, bf16[1056,128]{1,0:T(8,128)(2,1)S(1)}, bf16[1056,128]{1,0:T(8,12...) custom-call(s32[1]{0:T(128)} %bitcast.place_ref.refs_0_, f32[4,16,64,128]{3,2,1,0:T(8,128)} %bitcast.5, ...), custom_call_target="tpu_custom_call" | custom-call | flops 1 | bytes 1 | tf_op jit(solution)/shard_map/cast_states/pallas_call | solution.py:519
  1.8 3.1 %collective-permute-start = (bf16[1056,128]{1,0:T(8,128)(2,1)S(1)}, bf16[1056,128]{1,0:T(8,128)(2,1)S(1)}, u32[]{:S(2)}, u32[]{:S(2)}) collective-permute-start(bf16[1056,128]{1,0:T(8,128)(2,1)S(1)} %get-tuple-element.48), channel_id=1, source_target_pairs={{0,2},{2,0},{4,6},{6,4},{8,10},{10,8},{12,14},{14,12},{1,3},{3,1},... | collective-permute-start | bytes 811016 | tf_op jit(solution)/shard_map/ppermute | solution.py:488
  4.9 1.6 %collective-permute-start.1 = (bf16[1056,128]{1,0:T(8,128)(2,1)S(1)}, bf16[1056,128]{1,0:T(8,128)(2,1)S(1)}, u32[]{:S(2)}, u32[]{:S(2)}) collective-permute-start(bf16[1056,128]{1,0:T(8,128)(2,1)S(1)} %get-tuple-element.49), channel_id=1, source_target_pairs={{0,4},{2,6},{4,0},{6,2},{8,12},{10,14},{12,8},{14,10},{1,5},{3,7},... | collective-permute-start | bytes 811016 | tf_op jit(solution)/shard_map/ppermute | solution.py:488
  6.5 3.0 %collective-permute-start.3 = (bf16[2,544,128]{2,1,0:T(8,128)(2,1)S(1)}, bf16[2,544,128]{2,1,0:T(8,128)(2,1)S(1)}, u32[]{:S(2)}, u32[]{:S(2)}) collective-permute-start(bf16[2,544,128]{2,1,0:T(8,128)(2,1)S(1)} %get-tuple-element.51), channel_id=1, source_target_pairs={{0,8},{2,10},{4,12},{6,14},{8,0},{10,2},{12,4},{14,6},{1,9},{3,11}... | collective-permute-start | bytes 835592 | tf_op jit(solution)/shard_map/ppermute | solution.py:488
  9.4 1.3 %collective-permute-start.4 = (bf16[2,544,128]{2,1,0:T(8,128)(2,1)S(1)}, bf16[2,544,128]{2,1,0:T(8,128)(2,1)S(1)}, u32[]{:S(2)}, u32[]{:S(2)}) collective-permute-start(bf16[2,544,128]{2,1,0:T(8,128)(2,1)S(1)} %get-tuple-element.52), channel_id=1, source_target_pairs={{0,12},{2,14},{4,8},{6,10},{8,4},{10,6},{12,0},{14,2},{1,13},{3,15... | collective-permute-start | bytes 835592 | tf_op jit(solution)/shard_map/ppermute | solution.py:488
  10.8 0.1 select_reduce_fusion.1
  10.9 0.1 convert_reduce_fusion
  11.0 0.2 select_reduce_fusion
  11.2 0.1 copy.41.refs_4_
  11.3 0.1 copy.42.refs_5_
  11.4 0.1 broadcast_in_dim.57
  11.5 0.1 broadcast_in_dim_reshape.3.refs_6_
  11.6 5.4 %early.4 = (f32[4,256,1024]{2,1,0:T(8,128)S(1)}, bf16[4,256,128]{2,1,0:T(8,128)(2,1)S(1)}, f32[4,16,256]{2,1,0:T(8,128)S(1)}, f32[4,256,256]{2,1,0:T(8,128)S(1)}...) custom-call(bf16[2,256,4096]{2,1,0:T(8,128)(2,1)} %refs_0_.7, bf16[2,256,512]{2,1,0:T(8,128)(2,1)} %refs_1_.7, ...), custom_call_target="tpu_custom_call" | custom-call | flops 1 | bytes 1 | tf_op jit(solution)/shard_map/early/pallas_call | solution.py:590
  17.0 5.4 %early.5 = (f32[4,256,1024]{2,1,0:T(8,128)S(1)}, bf16[4,256,128]{2,1,0:T(8,128)(2,1)S(1)}, f32[4,16,256]{2,1,0:T(8,128)S(1)}, f32[4,256,256]{2,1,0:T(8,128)S(1)}...) custom-call(bf16[2,256,4096]{2,1,0:T(8,128)(2,1)} %refs_0_.7, ...), custom_call_target="tpu_custom_call", output_to_operand_aliasing={{0}: (9, {}), {1}: (10, {}), {2}: (11, {}), {3}: (12, {}), ... | custom-call | flops 1 | bytes 1 | tf_op jit(solution)/shard_map/early/pallas_call | solution.py:590
  22.4 5.4 %early.6 = (f32[4,256,1024]{2,1,0:T(8,128)S(1)}, bf16[4,256,128]{2,1,0:T(8,128)(2,1)S(1)}, f32[4,16,256]{2,1,0:T(8,128)S(1)}, f32[4,256,256]{2,1,0:T(8,128)S(1)}...) custom-call(bf16[2,256,4096]{2,1,0:T(8,128)(2,1)} %refs_0_.7, bf16[2,256,512]{2,1,0:T(8,128)(2,1)} %refs_1_.7, ...), custom_call_target="tpu_custom_call" | custom-call | flops 1 | bytes 1 | tf_op jit(solution)/shard_map/early/pallas_call | solution.py:590
  27.8 0.0 collective-permute-done.refs_2_
  27.8 0.0 collective-permute-done.2.refs_4_
  27.8 0.0 collective-permute-done.3.refs_6_.refs_1_.refs_5_
  27.8 4.9 %collective-permute-done.4.refs_7_.refs_2_.refs_6_ = bf16[2,544,128]{2,1,0:T(8,128)(2,1)S(1)} collective-permute-done((bf16[2,544,128]{2,1,0:T(8,128)(2,1)S(1)}, bf16[2,544,128]{2,1,0:T(8,128)(2,1)S(1)}, u32[]{:S(2)}, u32[]{:S(2)}) %collective-permute-start.4) | collective-permute-done | bytes 278560 | tf_op jit(solution)/shard_map/ppermute | solution.py:488
  32.7 0.4 stack_later.2.refs_3_
  33.1 0.4 stack_first.1
  33.4 0.6 collective-permute-start.5
  34.0 4.3 %collective-permute-start.9 = (bf16[4,256,128]{2,1,0:T(8,128)(2,1)S(1)}, bf16[4,256,128]{2,1,0:T(8,128)(2,1)S(1)}, u32[]{:S(2)}, u32[]{:S(2)}) collective-permute-start(bf16[4,256,128]{2,1,0:T(8,128)(2,1)S(1)} %stack_later.2.refs_3_), channel_id=1, source_target_pairs={{0,8},{2,10},{4,12},{6,14},{8,0},{10,2},{12,4},{14,6},{1,9},{3,11}... | collective-permute-start | bytes 786440 | tf_op jit(solution)/shard_map/ppermute | solution.py:488
  38.3 2.4 %collective-permute-done.5.refs_7_ = bf16[2,544,128]{2,1,0:T(8,128)(2,1)S(1)} collective-permute-done((bf16[2,544,128]{2,1,0:T(8,128)(2,1)S(1)}, bf16[2,544,128]{2,1,0:T(8,128)(2,1)S(1)}, u32[]{:S(2)}, u32[]{:S(2)}) %collective-permute-start.5) | collective-permute-done | bytes 278560 | tf_op jit(solution)/shard_map/ppermute | solution.py:488
  40.7 2.6 %pick_states.3 = (bf16[2,544,128]{2,1,0:T(8,128)(2,1)S(1)}, bf16[2,544,128]{2,1,0:T(8,128)(2,1)S(1)}, bf16[2,544,128]{2,1,0:T(8,128)(2,1)S(1)}, bf16[2,544,128]{2,1,0:T(8,128)(2,1)S(1)}) custom-call(s32[8]{0:T(128)S(1)} %broadcast_xor_fusion.refs_10_.refs_0_, bf16[1056,128]{1,0:T(8,128)(2,1)S(1)} %get-tuple-element.47.refs_9_.refs_1_, ...), custom_call_target="tpu_custom_call" | custom-call | flops 1 | bytes 1 | tf_op jit(solution)/shard_map/pick_states/pallas_call | solution.py:557
  43.2 0.6 collective-permute-start.6
  43.8 1.9 %collective-permute-start.7 = (bf16[2,544,128]{2,1,0:T(8,128)(2,1)S(1)}, bf16[2,544,128]{2,1,0:T(8,128)(2,1)S(1)}, u32[]{:S(2)}, u32[]{:S(2)}) collective-permute-start(bf16[2,544,128]{2,1,0:T(8,128)(2,1)S(1)} %get-tuple-element.63), channel_id=1, source_target_pairs={{0,4},{2,6},{4,0},{6,2},{8,12},{10,14},{12,8},{14,10},{1,5},{3,7},... | collective-permute-start | bytes 835592 | tf_op jit(solution)/shard_map/ppermute | solution.py:488
  45.7 1.1 %collective-permute-start.8 = (bf16[2,544,128]{2,1,0:T(8,128)(2,1)S(1)}, bf16[2,544,128]{2,1,0:T(8,128)(2,1)S(1)}, u32[]{:S(2)}, u32[]{:S(2)}) collective-permute-start(bf16[2,544,128]{2,1,0:T(8,128)(2,1)S(1)} %get-tuple-element.64), channel_id=1, source_target_pairs={{0,6},{2,4},{4,2},{6,0},{8,14},{10,12},{12,10},{14,8},{1,7},{3,5},... | collective-permute-start | bytes 835592 | tf_op jit(solution)/shard_map/ppermute | solution.py:488
  46.8 1.5 %collective-permute-done.9.refs_6_.refs_5_ = bf16[4,256,128]{2,1,0:T(8,128)(2,1)S(1)} collective-permute-done((bf16[4,256,128]{2,1,0:T(8,128)(2,1)S(1)}, bf16[4,256,128]{2,1,0:T(8,128)(2,1)S(1)}, u32[]{:S(2)}, u32[]{:S(2)}) %collective-permute-start.9) | collective-permute-done | bytes 262176 | tf_op jit(solution)/shard_map/ppermute | solution.py:488
  48.3 0.4 stack_later.3.refs_6_
  48.7 1.3 %collective-permute-start.10 = (bf16[4,256,128]{2,1,0:T(8,128)(2,1)S(1)}, bf16[4,256,128]{2,1,0:T(8,128)(2,1)S(1)}, u32[]{:S(2)}, u32[]{:S(2)}) collective-permute-start(bf16[4,256,128]{2,1,0:T(8,128)(2,1)S(1)} %stack_later.3.refs_6_), channel_id=1, source_target_pairs={{0,8},{2,10},{4,12},{6,14},{8,0},{10,2},{12,4},{14,6},{1,9},{3,11}... | collective-permute-start | bytes 786440 | tf_op jit(solution)/shard_map/ppermute | solution.py:488
  50.0 1.8 %pick_states.4 = (bf16[2,256,128]{2,1,0:T(8,128)(2,1)S(1)}, bf16[2,256,128]{2,1,0:T(8,128)(2,1)S(1)}, bf16[2,256,128]{2,1,0:T(8,128)(2,1)S(1)}, bf16[2,256,128]{2,1,0:T(8,128)(2,1)S(1)}) custom-call(s32[8]{0:T(128)S(1)} %broadcast_xor_fusion.refs_10_.refs_0_, bf16[1056,128]{1,0:T(8,128)(2,1)S(1)} %get-tuple-element.47.refs_9_.refs_1_, ...), custom_call_target="tpu_custom_call" | custom-call | flops 1 | bytes 1 | tf_op jit(solution)/shard_map/pick_states/pallas_call | solution.py:557
  51.9 1.6 %collective-permute-start.14 = (bf16[2,256,128]{2,1,0:T(8,128)(2,1)S(1)}, bf16[2,256,128]{2,1,0:T(8,128)(2,1)S(1)}, u32[]{:S(2)}, u32[]{:S(2)}) collective-permute-start(bf16[2,256,128]{2,1,0:T(8,128)(2,1)S(1)} %get-tuple-element.86), channel_id=1, source_target_pairs={{0,2},{2,0},{4,6},{6,4},{8,10},{10,8},{12,14},{14,12},{1,3},{3,1},... | collective-permute-start | bytes 393224 | tf_op jit(solution)/shard_map/ppermute | solution.py:488
  53.4 5.4 %early.7 = (f32[4,256,1024]{2,1,0:T(8,128)S(1)}, bf16[4,256,128]{2,1,0:T(8,128)(2,1)S(1)}, f32[4,16,256]{2,1,0:T(8,128)S(1)}, f32[4,256,256]{2,1,0:T(8,128)S(1)}...) custom-call(bf16[2,256,4096]{2,1,0:T(8,128)(2,1)} %refs_0_.7, ...), custom_call_target="tpu_custom_call", output_to_operand_aliasing={{0}: (10, {}), {1}: (11, {}), {2}: (12, {}), {3}: (13, {}),... | custom-call | flops 1 | bytes 1 | tf_op jit(solution)/shard_map/early/pallas_call | solution.py:590
  58.8 1.7 %collective-permute-done.10.refs_5_ = bf16[4,256,128]{2,1,0:T(8,128)(2,1)S(1)} collective-permute-done((bf16[4,256,128]{2,1,0:T(8,128)(2,1)S(1)}, bf16[4,256,128]{2,1,0:T(8,128)(2,1)S(1)}, u32[]{:S(2)}, u32[]{:S(2)}) %collective-permute-start.10) | collective-permute-done | bytes 262176 | tf_op jit(solution)/shard_map/ppermute | solution.py:488
  60.5 6.5 %collective-permute-start.15 = (bf16[2,256,128]{2,1,0:T(8,128)(2,1)S(1)}, bf16[2,256,128]{2,1,0:T(8,128)(2,1)S(1)}, u32[]{:S(2)}, u32[]{:S(2)}) collective-permute-start(bf16[2,256,128]{2,1,0:T(8,128)(2,1)S(1)} %get-tuple-element.87), channel_id=1, source_target_pairs={{0,4},{2,6},{4,0},{6,2},{8,12},{10,14},{12,8},{14,10},{1,5},{3,7},... | collective-permute-start | bytes 393224 | tf_op jit(solution)/shard_map/ppermute | solution.py:488
  67.1 1.8 %pick_states.5 = (bf16[2,256,128]{2,1,0:T(8,128)(2,1)S(1)}, bf16[2,256,128]{2,1,0:T(8,128)(2,1)S(1)}, bf16[2,256,128]{2,1,0:T(8,128)(2,1)S(1)}, bf16[2,256,128]{2,1,0:T(8,128)(2,1)S(1)}) custom-call(s32[8]{0:T(128)S(1)} %broadcast_xor_fusion.refs_10_.refs_0_, bf16[1056,128]{1,0:T(8,128)(2,1)S(1)} %get-tuple-element.47.refs_9_.refs_1_, ...), custom_call_target="tpu_custom_call" | custom-call | flops 1 | bytes 1 | tf_op jit(solution)/shard_map/pick_states/pallas_call | solution.py:557
  68.9 0.1 collective-permute-start.16
  69.0 1.4 %collective-permute-start.11 = (bf16[2,256,128]{2,1,0:T(8,128)(2,1)S(1)}, bf16[2,256,128]{2,1,0:T(8,128)(2,1)S(1)}, u32[]{:S(2)}, u32[]{:S(2)}) collective-permute-start(bf16[2,256,128]{2,1,0:T(8,128)(2,1)S(1)} %get-tuple-element.73), channel_id=1, source_target_pairs={{0,2},{2,0},{4,6},{6,4},{8,10},{10,8},{12,14},{14,12},{1,3},{3,1},... | collective-permute-start | bytes 393224 | tf_op jit(solution)/shard_map/ppermute | solution.py:488
  70.4 0.0 collective-permute-done.7.refs_3_.refs_7_
  70.4 2.0 %collective-permute-start.12 = (bf16[2,256,128]{2,1,0:T(8,128)(2,1)S(1)}, bf16[2,256,128]{2,1,0:T(8,128)(2,1)S(1)}, u32[]{:S(2)}, u32[]{:S(2)}) collective-permute-start(bf16[2,256,128]{2,1,0:T(8,128)(2,1)S(1)} %get-tuple-element.74), channel_id=1, source_target_pairs={{0,4},{2,6},{4,0},{6,2},{8,12},{10,14},{12,8},{14,10},{1,5},{3,7},... | collective-permute-start | bytes 393224 | tf_op jit(solution)/shard_map/ppermute | solution.py:488
  72.5 0.1 collective-permute-start.13
  72.5 4.6 %late.3.refs_21_ = bf16[2,256,4096]{2,1,0:T(8,128)(2,1)} custom-call(s32[1]{0:T(128)} %bitcast.place_ref.refs_0_, bf16[2,544,128]{2,1,0:T(8,128)(2,1)S(1)} %get-tuple-element.61.refs_5_.refs_1_, bf16[2,544,128]{2,1,0:T(8,128)(2,1)S(1)} %collective-permute-done.6.refs_2_.refs_6_, bf16[2,544,128]{2,1,0:T(8,128)(2,1)S(1)} %collective-permute-done.7.refs_3_.refs_7_, ...), custom_call_target="tpu_custom_call" | custom-call | flops 1 | bytes 1 | tf_op jit(solution)/shard_map/late/pallas_call | solution.py:638
  77.2 0.0 collective-permute-done.15.refs_7_
  77.2 0.0 collective-permute-done.16.refs_8_
  77.2 3.5 %late.4.refs_21_ = bf16[2,256,4096]{2,1,0:T(8,128)(2,1)} custom-call(s32[1]{0:T(128)} %bitcast.place_ref.refs_0_, bf16[2,544,128]{2,1,0:T(8,128)(2,1)S(1)} %get-tuple-element.61.refs_5_.refs_1_, bf16[2,544,128]{2,1,0:T(8,128)(2,1)S(1)} %collective-permute-done.6.refs_2_.refs_6_, ...), custom_call_target="tpu_custom_call", output_to_operand_aliasing={{}: (21, {})} | custom-call | flops 1 | bytes 1 | tf_op jit(solution)/shard_map/late/pallas_call | solution.py:638
  80.7 0.0 collective-permute-done.11.refs_6_
  80.8 3.6 %late.5 = bf16[2,256,4096]{2,1,0:T(8,128)(2,1)} custom-call(s32[1]{0:T(128)} %bitcast.place_ref.refs_0_, bf16[2,544,128]{2,1,0:T(8,128)(2,1)S(1)} %get-tuple-element.61.refs_5_.refs_1_, bf16[2,544,128]{2,1,0:T(8,128)(2,1)S(1)} %collective-permute-done.6.refs_2_.refs_6_, ...), custom_call_target="tpu_custom_call", output_to_operand_aliasing={{}: (21, {})} | custom-call | flops 1 | bytes 1 | tf_op jit(solution)/shard_map/late/pallas_call | solution.py:638
  (19 shorter events, 0.0 us)
Async XLA Ops:
  0.0 10.8 %copy-start.3 = (s32[8]{0:T(128)S(1)}, s32[8]{0:T(128)}, u32[]{:S(2)}) copy-start(s32[8]{0:T(128)} %param.26) | copy-start | bytes 100
  0.0 10.9 %copy-start.4 = (s32[16]{0:T(128)S(1)}, s32[16]{0:T(128)}, u32[]{:S(2)}) copy-start(s32[16]{0:T(128)} %param.27) | copy-start | bytes 196
  0.0 11.2 %copy-start = (f32[64]{0:T(128)S(1)}, f32[64]{0:T(128)}, u32[]{:S(2)}) copy-start(f32[64]{0:T(128)} %param.18) | copy-start | bytes 772
  0.0 11.3 %copy-start.1 = (f32[64]{0:T(128)S(1)}, f32[64]{0:T(128)}, u32[]{:S(2)}) copy-start(f32[64]{0:T(128)} %param.19) | copy-start | bytes 772
  0.0 11.4 %copy-start.2 = (f32[64]{0:T(128)S(1)}, f32[64]{0:T(128)}, u32[]{:S(2)}) copy-start(f32[64]{0:T(128)} %param.20) | copy-start | bytes 772
  1.8 25.9 %collective-permute-start = (bf16[1056,128]{1,0:T(8,128)(2,1)S(1)}, bf16[1056,128]{1,0:T(8,128)(2,1)S(1)}, u32[]{:S(2)}, u32[]{:S(2)}) collective-permute-start(bf16[1056,128]{1,0:T(8,128)(2,1)S(1)} %get-tuple-element.48), channel_id=1, source_target_pairs={{0,2},{2,0},{4,6},{6,4},{8,10},{10,8},{12,14},{14,12},{1,3},{3,1},... | collective-permute-start | bytes 811016 | tf_op jit(solution)/shard_map/ppermute | solution.py:488
  4.9 22.9 %collective-permute-start.1 = (bf16[1056,128]{1,0:T(8,128)(2,1)S(1)}, bf16[1056,128]{1,0:T(8,128)(2,1)S(1)}, u32[]{:S(2)}, u32[]{:S(2)}) collective-permute-start(bf16[1056,128]{1,0:T(8,128)(2,1)S(1)} %get-tuple-element.49), channel_id=1, source_target_pairs={{0,4},{2,6},{4,0},{6,2},{8,12},{10,14},{12,8},{14,10},{1,5},{3,7},... | collective-permute-start | bytes 811016 | tf_op jit(solution)/shard_map/ppermute | solution.py:488
  6.5 21.3 %collective-permute-start.2 = (bf16[1056,128]{1,0:T(8,128)(2,1)S(1)}, bf16[1056,128]{1,0:T(8,128)(2,1)S(1)}, u32[]{:S(2)}, u32[]{:S(2)}) collective-permute-start(bf16[1056,128]{1,0:T(8,128)(2,1)S(1)} %get-tuple-element.50), channel_id=1, source_target_pairs={{0,6},{2,4},{4,2},{6,0},{8,14},{10,12},{12,10},{14,8},{1,7},{3,5},... | collective-permute-start | bytes 811016 | tf_op jit(solution)/shard_map/ppermute | solution.py:488
  6.5 21.3 %collective-permute-start.3 = (bf16[2,544,128]{2,1,0:T(8,128)(2,1)S(1)}, bf16[2,544,128]{2,1,0:T(8,128)(2,1)S(1)}, u32[]{:S(2)}, u32[]{:S(2)}) collective-permute-start(bf16[2,544,128]{2,1,0:T(8,128)(2,1)S(1)} %get-tuple-element.51), channel_id=1, source_target_pairs={{0,8},{2,10},{4,12},{6,14},{8,0},{10,2},{12,4},{14,6},{1,9},{3,11}... | collective-permute-start | bytes 835592 | tf_op jit(solution)/shard_map/ppermute | solution.py:488
  9.4 23.2 %collective-permute-start.4 = (bf16[2,544,128]{2,1,0:T(8,128)(2,1)S(1)}, bf16[2,544,128]{2,1,0:T(8,128)(2,1)S(1)}, u32[]{:S(2)}, u32[]{:S(2)}) collective-permute-start(bf16[2,544,128]{2,1,0:T(8,128)(2,1)S(1)} %get-tuple-element.52), channel_id=1, source_target_pairs={{0,12},{2,14},{4,8},{6,10},{8,4},{10,6},{12,0},{14,2},{1,13},{3,15... | collective-permute-start | bytes 835592 | tf_op jit(solution)/shard_map/ppermute | solution.py:488
  33.4 7.2 %collective-permute-start.5 = (bf16[2,544,128]{2,1,0:T(8,128)(2,1)S(1)}, bf16[2,544,128]{2,1,0:T(8,128)(2,1)S(1)}, u32[]{:S(2)}, u32[]{:S(2)}) collective-permute-start(bf16[2,544,128]{2,1,0:T(8,128)(2,1)S(1)} %stack_first.1), channel_id=1, source_target_pairs={{0,2},{2,0},{4,6},{6,4},{8,10},{10,8},{12,14},{14,12},{1,3},{3,1},... | collective-permute-start | bytes 835592 | tf_op jit(solution)/shard_map/ppermute | solution.py:488
  34.0 14.3 %collective-permute-start.9 = (bf16[4,256,128]{2,1,0:T(8,128)(2,1)S(1)}, bf16[4,256,128]{2,1,0:T(8,128)(2,1)S(1)}, u32[]{:S(2)}, u32[]{:S(2)}) collective-permute-start(bf16[4,256,128]{2,1,0:T(8,128)(2,1)S(1)} %stack_later.2.refs_3_), channel_id=1, source_target_pairs={{0,8},{2,10},{4,12},{6,14},{8,0},{10,2},{12,4},{14,6},{1,9},{3,11}... | collective-permute-start | bytes 786440 | tf_op jit(solution)/shard_map/ppermute | solution.py:488
  43.2 25.7 %collective-permute-start.6 = (bf16[2,544,128]{2,1,0:T(8,128)(2,1)S(1)}, bf16[2,544,128]{2,1,0:T(8,128)(2,1)S(1)}, u32[]{:S(2)}, u32[]{:S(2)}) collective-permute-start(bf16[2,544,128]{2,1,0:T(8,128)(2,1)S(1)} %get-tuple-element.62), channel_id=1, source_target_pairs={{0,2},{2,0},{4,6},{6,4},{8,10},{10,8},{12,14},{14,12},{1,3},{3,1},... | collective-permute-start | bytes 835592 | tf_op jit(solution)/shard_map/ppermute | solution.py:488
  43.8 26.6 %collective-permute-start.7 = (bf16[2,544,128]{2,1,0:T(8,128)(2,1)S(1)}, bf16[2,544,128]{2,1,0:T(8,128)(2,1)S(1)}, u32[]{:S(2)}, u32[]{:S(2)}) collective-permute-start(bf16[2,544,128]{2,1,0:T(8,128)(2,1)S(1)} %get-tuple-element.63), channel_id=1, source_target_pairs={{0,4},{2,6},{4,0},{6,2},{8,12},{10,14},{12,8},{14,10},{1,5},{3,7},... | collective-permute-start | bytes 835592 | tf_op jit(solution)/shard_map/ppermute | solution.py:488
  45.7 26.8 %collective-permute-start.8 = (bf16[2,544,128]{2,1,0:T(8,128)(2,1)S(1)}, bf16[2,544,128]{2,1,0:T(8,128)(2,1)S(1)}, u32[]{:S(2)}, u32[]{:S(2)}) collective-permute-start(bf16[2,544,128]{2,1,0:T(8,128)(2,1)S(1)} %get-tuple-element.64), channel_id=1, source_target_pairs={{0,6},{2,4},{4,2},{6,0},{8,14},{10,12},{12,10},{14,8},{1,7},{3,5},... | collective-permute-start | bytes 835592 | tf_op jit(solution)/shard_map/ppermute | solution.py:488
  48.7 11.8 %collective-permute-start.10 = (bf16[4,256,128]{2,1,0:T(8,128)(2,1)S(1)}, bf16[4,256,128]{2,1,0:T(8,128)(2,1)S(1)}, u32[]{:S(2)}, u32[]{:S(2)}) collective-permute-start(bf16[4,256,128]{2,1,0:T(8,128)(2,1)S(1)} %stack_later.3.refs_6_), channel_id=1, source_target_pairs={{0,8},{2,10},{4,12},{6,14},{8,0},{10,2},{12,4},{14,6},{1,9},{3,11}... | collective-permute-start | bytes 786440 | tf_op jit(solution)/shard_map/ppermute | solution.py:488
  51.9 17.0 %collective-permute-start.14 = (bf16[2,256,128]{2,1,0:T(8,128)(2,1)S(1)}, bf16[2,256,128]{2,1,0:T(8,128)(2,1)S(1)}, u32[]{:S(2)}, u32[]{:S(2)}) collective-permute-start(bf16[2,256,128]{2,1,0:T(8,128)(2,1)S(1)} %get-tuple-element.86), channel_id=1, source_target_pairs={{0,2},{2,0},{4,6},{6,4},{8,10},{10,8},{12,14},{14,12},{1,3},{3,1},... | collective-permute-start | bytes 393224 | tf_op jit(solution)/shard_map/ppermute | solution.py:488
  60.5 16.7 %collective-permute-start.15 = (bf16[2,256,128]{2,1,0:T(8,128)(2,1)S(1)}, bf16[2,256,128]{2,1,0:T(8,128)(2,1)S(1)}, u32[]{:S(2)}, u32[]{:S(2)}) collective-permute-start(bf16[2,256,128]{2,1,0:T(8,128)(2,1)S(1)} %get-tuple-element.87), channel_id=1, source_target_pairs={{0,4},{2,6},{4,0},{6,2},{8,12},{10,14},{12,8},{14,10},{1,5},{3,7},... | collective-permute-start | bytes 393224 | tf_op jit(solution)/shard_map/ppermute | solution.py:488
  68.9 8.3 %collective-permute-start.16 = (bf16[2,256,128]{2,1,0:T(8,128)(2,1)S(1)}, bf16[2,256,128]{2,1,0:T(8,128)(2,1)S(1)}, u32[]{:S(2)}, u32[]{:S(2)}) collective-permute-start(bf16[2,256,128]{2,1,0:T(8,128)(2,1)S(1)} %get-tuple-element.88), channel_id=1, source_target_pairs={{0,6},{2,4},{4,2},{6,0},{8,14},{10,12},{12,10},{14,8},{1,7},{3,5},... | collective-permute-start | bytes 393224 | tf_op jit(solution)/shard_map/ppermute | solution.py:488
  69.0 11.8 %collective-permute-start.11 = (bf16[2,256,128]{2,1,0:T(8,128)(2,1)S(1)}, bf16[2,256,128]{2,1,0:T(8,128)(2,1)S(1)}, u32[]{:S(2)}, u32[]{:S(2)}) collective-permute-start(bf16[2,256,128]{2,1,0:T(8,128)(2,1)S(1)} %get-tuple-element.73), channel_id=1, source_target_pairs={{0,2},{2,0},{4,6},{6,4},{8,10},{10,8},{12,14},{14,12},{1,3},{3,1},... | collective-permute-start | bytes 393224 | tf_op jit(solution)/shard_map/ppermute | solution.py:488
  70.4 10.3 %collective-permute-start.12 = (bf16[2,256,128]{2,1,0:T(8,128)(2,1)S(1)}, bf16[2,256,128]{2,1,0:T(8,128)(2,1)S(1)}, u32[]{:S(2)}, u32[]{:S(2)}) collective-permute-start(bf16[2,256,128]{2,1,0:T(8,128)(2,1)S(1)} %get-tuple-element.74), channel_id=1, source_target_pairs={{0,4},{2,6},{4,0},{6,2},{8,12},{10,14},{12,8},{14,10},{1,5},{3,7},... | collective-permute-start | bytes 393224 | tf_op jit(solution)/shard_map/ppermute | solution.py:488
  72.5 8.3 %collective-permute-start.13 = (bf16[2,256,128]{2,1,0:T(8,128)(2,1)S(1)}, bf16[2,256,128]{2,1,0:T(8,128)(2,1)S(1)}, u32[]{:S(2)}, u32[]{:S(2)}) collective-permute-start(bf16[2,256,128]{2,1,0:T(8,128)(2,1)S(1)} %get-tuple-element.75), channel_id=1, source_target_pairs={{0,6},{2,4},{4,2},{6,0},{8,14},{10,12},{12,10},{14,8},{1,7},{3,5},... | collective-permute-start | bytes 393224 | tf_op jit(solution)/shard_map/ppermute | solution.py:488

commit v14 on v13

--- a/solution.py
+++ b/solution.py
@@ -123,19 +123,15 @@
 
 
 def late_kernel(offset, heads, lines, reach, tail_at, place_ref, *refs):
-    tails, states, parts, (y_ref, padded) = refs[:4], refs[4:8], refs[8:-2], refs[-2:]
-    kids, length, wide = y_ref.shape
+    tails, states, parts = refs[:4], refs[4:8], refs[8:-4]
+    y_ref, padded, y_part, sems = refs[-4:]
+    _, kids, length, wide = y_part.shape
     width = wide // heads
-    q = pl.program_id(0)
-    far = q ^ place_ref[0]
     low_first = lax.broadcasted_iota(jnp.int32, (FIX, 2 * width), 1) < width
     contract = (((1,), (1,)), ((), ()))
 
-    def choose(blocks):
-        near = jnp.where(far == 0, blocks[0], blocks[1])
-        return jnp.where(far <= 1, near, jnp.where(far == 2, blocks[2], blocks[3]))
-
-    for kid in range(kids):
+    def add(j, kid):
+        q = place_ref[0] ^ j
         mixed_ref, held_ref, column_ref, first_ref, opening_ref, weights_ref = parts[
             6 * kid : 6 * kid + 6
         ]
@@ -143,8 +139,8 @@
         per_group = column_ref.shape[1]
         group_wide = opening_ref.shape[2] - 2 * size
         tail_rows = pl.ds(tail_at, -(-lines * reach // 16) * 16)
-        tail = choose([ref[kid, tail_rows] for ref in tails]).astype(jnp.float32)
-        state = choose([ref[kid, : heads * width] for ref in states])
+        tail = tails[j][kid, tail_rows].astype(jnp.float32)
+        state = states[j][kid, : heads * width]
 
         def opening(start, stop, at):
             tap_rows = []
@@ -154,7 +150,7 @@
                 here = [tail[first + n : first + n + 1] for n in range(count)]
                 tap_rows.append(jnp.concatenate(here, axis=1))
             return conv_silu(
-                padded.at[kid, :, : stop - start],
+                padded.at[j, kid, :, : stop - start],
                 jnp.concatenate(tap_rows),
                 opening_ref[q, :, start:stop],
                 weights_ref[q, : reach + 1, start:stop],
@@ -202,9 +198,20 @@
             )
             part = jnp.concatenate([part[:FIX] + skipped[:, lanes], part[FIX:]])
             whole = slice(start + lanes.start, start + lanes.stop)
-            y_ref[kid, :, lanes] = (
+            y_part[j, kid, :, lanes] = (
                 mixed_ref[q, :, whole] + part + carried[:, lanes].astype(jnp.float32)
             ).astype(jnp.bfloat16)
+
+    copies = []
+    for j in range(4):
+        for kid in range(kids):
+            add(j, kid)
+        start = (place_ref[0] ^ j) * (y_ref.shape[2] // 4) + offset * width
+        lanes = pl.ds(pl.multiple_of(start, 128), wide)
+        copies.append(pltpu.make_async_copy(y_part.at[j], y_ref.at[:, :, lanes], sems.at[j]))
+        copies[-1].start()
+    for copy in copies:
+        copy.wait()
 
 
 def cast_kernel(parts, tailed, reach, lines, *refs):
@@ -532,42 +539,36 @@
 
     def rearrange(scalars, sources, moves, shapes, tokens, name):
         def kernel(scalars_ref, *refs):
-            held, outs, sems = refs[: len(sources)], refs[len(sources) : -1], refs[-1]
-
-            def copy(move, source):
-                out, at, _, _ = moves[move]
-                number, take = source
-                ref = held[number].at[take] if take is not None else held[number]
-                target = outs[out].at[at] if at is not None else outs[out]
-                return pltpu.make_async_copy(ref, target, sems.at[move])
-
-            for move, (_, _, scalar, choices) in enumerate(moves):
-                if scalar is None:
-                    copy(move, choices[0]).start()
-                    continue
-                for value, source in enumerate(choices):
-
-                    @pl.when(scalars_ref[scalar] == value)
-                    def _(move=move, source=source):
-                        copy(move, source).start()
-
-            for move in range(len(moves)):
-                copy(move, moves[move][3][0]).wait()
+            held, outs = refs[: len(sources)], refs[len(sources) :]
+            for out, at, scalar, choices in moves:
+                for value, (number, take) in enumerate(choices):
+
+                    def copy(out=out, at=at, number=number, take=take):
+                        rows = held[number][...] if take is None else held[number][take]
+                        if at is None:
+                            outs[out][...] = rows
+                        else:
+                            outs[out][at] = rows
+
+                    if scalar is None:
+                        copy()
+                    else:
+                        pl.when(scalars_ref[scalar] == value)(copy)
 
         return pl.pallas_call(
             functools.partial(drop_tokens, kernel, 1 + len(sources), len(tokens)),
             grid_spec=pltpu.PrefetchScalarGridSpec(
                 num_scalar_prefetch=1,
                 grid=(1,),
-                in_specs=[anywhere] * (len(sources) + len(tokens)),
+                in_specs=[pl.BlockSpec(memory_space=pltpu.VMEM)] * len(sources)
+                + [anywhere] * len(tokens),
                 out_specs=[pl.BlockSpec(memory_space=pltpu.VMEM)] * len(shapes),
-                scratch_shapes=[pltpu.SemaphoreType.DMA((len(moves),))],
             ),
             out_shape=[pltpu.VMEM(shape, jnp.bfloat16) for shape in shapes],
             compiler_params=params,
             cost_estimate=small,
             name=name,
-        )(scalars, *sources, *tokens)
+        )(scalars, *map(keep_in_vmem, sources), *tokens)
 
     def pick(rows, sources, choices, tokens):
         moves = [
@@ -623,7 +624,6 @@
     def late(k, states, states_first, parts, result, tokens):
         part, offset = SPLIT[k], offsets[k]
         chunk = part * width
-        lane = lambda q, p: (0, 0, q * (per_group // part) + offset // part)
         operands = [keep_in_vmem(a) for a in (*states_first, *states, *parts[0], *parts[1])]
         specs = [pl.BlockSpec(memory_space=pltpu.VMEM)] * len(operands)
         keep = 1 + len(operands)
@@ -639,10 +639,14 @@
             functools.partial(drop_tokens, kernel, keep, 1 + len(operands) - keep),
             grid_spec=pltpu.PrefetchScalarGridSpec(
                 num_scalar_prefetch=1,
-                grid=(groups,),
+                grid=(1,),
                 in_specs=specs,
-                out_specs=pl.BlockSpec((kids, length, chunk), lane),
-                scratch_shapes=[pltpu.VMEM((kids, 8 + FIX, max(chunk, 2 * size)), jnp.float32)],
+                out_specs=anywhere,
+                scratch_shapes=[
+                    pltpu.VMEM((groups, kids, 8 + FIX, max(chunk, 2 * size)), jnp.float32),
+                    pltpu.VMEM((groups, kids, length, chunk), jnp.bfloat16),
+                    pltpu.SemaphoreType.DMA((groups,)),
+                ],
             ),
             out_shape=jax.ShapeDtypeStruct(x_in.shape, jnp.bfloat16),
             input_output_aliases=alias,
@@ -679,10 +683,10 @@
     sent_c, crossed_c = cross(2, [states_a[0], crossed_b])
     states_b = pick_later(1, crossed_b, [sent_c])
     second = early(1, 1, second, [states_b[0]])
-    states_c = pick_later(2, crossed_c, [second[1]])
     parts = [first, second]
-    result = late(0, states_a, states_a, parts, None, [states_c[0]])
-    result = late(1, states_b, states_a, parts, result, [])
+    result = late(0, states_a, states_a, parts, None, [states_b[0]])
+    states_c = pick_later(2, crossed_c, [stay(result)])
+    result = late(1, states_b, states_a, parts, result, [states_c[0]])
     return late(2, states_c, states_a, parts, result, [])
 
 

time: 84.6 us -> 82.8 us (0.979)
  waiting for transfers between devices: 10.5 us -> 19.9 us
  Pallas kernels: 42.4 us -> 36.5 us
  starting transfers between devices: 30.5 us -> 25.1 us
    ppermute x17, waiting for transfers between devices: 10.5 us -> 19.9 us  [swap(): return lax.ppermute(value, 'batch', perm=[(i, i ^ r) for i in range(8)])]
    ppermute x17, starting transfers between devices: 30.5 us -> 25.1 us  [swap(): return lax.ppermute(value, 'batch', perm=[(i, i ^ r) for i in range(8)])]
    pallas_call x6, Pallas kernels: 7.29 us -> 3.43 us  [rearrange(): pl.pallas_call(functools.partial(drop_tokens, kernel, 1 + len(sources), l...]
    pallas_call x3, Pallas kernels: 11.8 us -> 9.74 us  [late(): pl.pallas_call(functools.partial(drop_tokens, kernel, keep, 1 + len(opera...]
  transfers between devices with their start and end apart: 17 -> 17, of which waited for: 4 -> 6; matrix products, arithmetic and copies ran while one was open for 1% -> 1% of each run, Pallas kernels for 43% -> 38%
where the time goes in v14:
time: 82.8 us; the launch traced here: 82.6 us
  Pallas kernels  36.5 us (44%)
  starting transfers between devices  25.1 us (30%)
  waiting for transfers between devices  19.9 us (24%)
    ppermute x17, starting transfers between devices, swap(): return lax.ppermute(value, 'batch', perm=[(i, i ^ r) for i in range(8)])  25.1 us
    pallas_call x4, Pallas kernels, early(): pl.pallas_call(functools.partial(drop_tokens, functools.partial(early_ker...  21.5 us
    ppermute x17, waiting for transfers between devices, swap(): return lax.ppermute(value, 'batch', perm=[(i, i ^ r) for i in range(8)])  19.9 us
    pallas_call x3, Pallas kernels, late(): pl.pallas_call(functools.partial(drop_tokens, kernel, keep, 1 + len(opera...  9.74 us
    pallas_call x6, Pallas kernels, rearrange(): pl.pallas_call(functools.partial(drop_tokens, kernel, 1 + len(sources), l...  3.43 us
    pallas_call x1, Pallas kernels, cast(): pl.pallas_call(kernel, grid_spec=pltpu.PrefetchScalarGridSpec(num_scalar_...  1.82 us
  transfers between devices with their start and end apart: 17, of which 6 were waited for; matrix products, arithmetic and copies ran while one was open for 1% of the time, Pallas kernels for 38%

profile of v14, /device:TPU:0, one launch (start us, length us, event | category | flops | bytes accessed | tf_op | source)
XLA Modules:
  0.0 82.6 jit_solution(1290905881959895145)
XLA Ops:
  0.0 1.8 %cast_states.1 = (bf16[1056,128]{1,0:T(8,128)(2,1)S(1)}, bf16[1056,128]{1,0:T(8,128)(2,1)S(1)}, bf16[1056,128]{1,0:T(8,128)(2,1)S(1)}, bf16[1056,128]{1,0:T(8,12...) custom-call(s32[1]{0:T(128)} %bitcast.place_ref.refs_0_, f32[4,16,64,128]{3,2,1,0:T(8,128)} %bitcast.5, ...), custom_call_target="tpu_custom_call" | custom-call | flops 1 | bytes 1 | tf_op jit(solution)/shard_map/cast_states/pallas_call | solution.py:526
  1.8 3.1 %collective-permute-start = (bf16[1056,128]{1,0:T(8,128)(2,1)S(1)}, bf16[1056,128]{1,0:T(8,128)(2,1)S(1)}, u32[]{:S(2)}, u32[]{:S(2)}) collective-permute-start(bf16[1056,128]{1,0:T(8,128)(2,1)S(1)} %get-tuple-element.48), channel_id=1, source_target_pairs={{0,2},{2,0},{4,6},{6,4},{8,10},{10,8},{12,14},{14,12},{1,3},{3,1},... | collective-permute-start | bytes 811016 | tf_op jit(solution)/shard_map/ppermute | solution.py:495
  4.9 1.6 %collective-permute-start.1 = (bf16[1056,128]{1,0:T(8,128)(2,1)S(1)}, bf16[1056,128]{1,0:T(8,128)(2,1)S(1)}, u32[]{:S(2)}, u32[]{:S(2)}) collective-permute-start(bf16[1056,128]{1,0:T(8,128)(2,1)S(1)} %get-tuple-element.49), channel_id=1, source_target_pairs={{0,4},{2,6},{4,0},{6,2},{8,12},{10,14},{12,8},{14,10},{1,5},{3,7},... | collective-permute-start | bytes 811016 | tf_op jit(solution)/shard_map/ppermute | solution.py:495
  6.5 3.0 %collective-permute-start.3 = (bf16[2,544,128]{2,1,0:T(8,128)(2,1)S(1)}, bf16[2,544,128]{2,1,0:T(8,128)(2,1)S(1)}, u32[]{:S(2)}, u32[]{:S(2)}) collective-permute-start(bf16[2,544,128]{2,1,0:T(8,128)(2,1)S(1)} %get-tuple-element.51), channel_id=1, source_target_pairs={{0,8},{2,10},{4,12},{6,14},{8,0},{10,2},{12,4},{14,6},{1,9},{3,11}... | collective-permute-start | bytes 835592 | tf_op jit(solution)/shard_map/ppermute | solution.py:495
  9.4 1.3 %collective-permute-start.4 = (bf16[2,544,128]{2,1,0:T(8,128)(2,1)S(1)}, bf16[2,544,128]{2,1,0:T(8,128)(2,1)S(1)}, u32[]{:S(2)}, u32[]{:S(2)}) collective-permute-start(bf16[2,544,128]{2,1,0:T(8,128)(2,1)S(1)} %get-tuple-element.52), channel_id=1, source_target_pairs={{0,12},{2,14},{4,8},{6,10},{8,4},{10,6},{12,0},{14,2},{1,13},{3,15... | collective-permute-start | bytes 835592 | tf_op jit(solution)/shard_map/ppermute | solution.py:495
  10.8 0.1 select_reduce_fusion.1
  10.9 0.1 convert_reduce_fusion
  11.0 0.2 select_reduce_fusion
  11.2 0.1 copy.41.refs_4_
  11.3 0.1 copy.42.refs_5_
  11.4 0.1 broadcast_in_dim.57
  11.5 0.1 broadcast_in_dim_reshape.3.refs_6_
  11.6 5.4 %early.4 = (f32[4,256,1024]{2,1,0:T(8,128)S(1)}, bf16[4,256,128]{2,1,0:T(8,128)(2,1)S(1)}, f32[4,16,256]{2,1,0:T(8,128)S(1)}, f32[4,256,256]{2,1,0:T(8,128)S(1)}...) custom-call(bf16[2,256,4096]{2,1,0:T(8,128)(2,1)} %refs_0_.7, bf16[2,256,512]{2,1,0:T(8,128)(2,1)} %refs_1_.7, ...), custom_call_target="tpu_custom_call" | custom-call | flops 1 | bytes 1 | tf_op jit(solution)/shard_map/early/pallas_call | solution.py:591
  17.0 5.4 %early.5 = (f32[4,256,1024]{2,1,0:T(8,128)S(1)}, bf16[4,256,128]{2,1,0:T(8,128)(2,1)S(1)}, f32[4,16,256]{2,1,0:T(8,128)S(1)}, f32[4,256,256]{2,1,0:T(8,128)S(1)}...) custom-call(bf16[2,256,4096]{2,1,0:T(8,128)(2,1)} %refs_0_.7, ...), custom_call_target="tpu_custom_call", output_to_operand_aliasing={{0}: (9, {}), {1}: (10, {}), {2}: (11, {}), {3}: (12, {}), ... | custom-call | flops 1 | bytes 1 | tf_op jit(solution)/shard_map/early/pallas_call | solution.py:591
  22.4 5.4 %early.6 = (f32[4,256,1024]{2,1,0:T(8,128)S(1)}, bf16[4,256,128]{2,1,0:T(8,128)(2,1)S(1)}, f32[4,16,256]{2,1,0:T(8,128)S(1)}, f32[4,256,256]{2,1,0:T(8,128)S(1)}...) custom-call(bf16[2,256,4096]{2,1,0:T(8,128)(2,1)} %refs_0_.7, bf16[2,256,512]{2,1,0:T(8,128)(2,1)} %refs_1_.7, ...), custom_call_target="tpu_custom_call" | custom-call | flops 1 | bytes 1 | tf_op jit(solution)/shard_map/early/pallas_call | solution.py:591
  27.8 0.0 collective-permute-done.refs_2_
  27.8 0.0 collective-permute-done.3.refs_6_.refs_1_.refs_5_
  27.8 4.9 %collective-permute-done.4.refs_7_.refs_2_.refs_6_ = bf16[2,544,128]{2,1,0:T(8,128)(2,1)S(1)} collective-permute-done((bf16[2,544,128]{2,1,0:T(8,128)(2,1)S(1)}, bf16[2,544,128]{2,1,0:T(8,128)(2,1)S(1)}, u32[]{:S(2)}, u32[]{:S(2)}) %collective-permute-start.4) | collective-permute-done | bytes 278560 | tf_op jit(solution)/shard_map/ppermute | solution.py:495
  32.7 0.6 collective-permute-start.5
  33.3 4.6 %collective-permute-start.9 = (bf16[4,256,128]{2,1,0:T(8,128)(2,1)S(1)}, bf16[4,256,128]{2,1,0:T(8,128)(2,1)S(1)}, u32[]{:S(2)}, u32[]{:S(2)}) collective-permute-start(bf16[4,256,128]{2,1,0:T(8,128)(2,1)S(1)} %stack_later.2.refs_3_), channel_id=1, source_target_pairs={{0,8},{2,10},{4,12},{6,14},{8,0},{10,2},{12,4},{14,6},{1,9},{3,11}... | collective-permute-start | bytes 786440 | tf_op jit(solution)/shard_map/ppermute | solution.py:495
  37.9 2.1 %collective-permute-done.5.refs_7_ = bf16[2,544,128]{2,1,0:T(8,128)(2,1)S(1)} collective-permute-done((bf16[2,544,128]{2,1,0:T(8,128)(2,1)S(1)}, bf16[2,544,128]{2,1,0:T(8,128)(2,1)S(1)}, u32[]{:S(2)}, u32[]{:S(2)}) %collective-permute-start.5) | collective-permute-done | bytes 278560 | tf_op jit(solution)/shard_map/ppermute | solution.py:495
  40.0 1.1 %pick_states.3 = (bf16[2,544,128]{2,1,0:T(8,128)(2,1)S(1)}, bf16[2,544,128]{2,1,0:T(8,128)(2,1)S(1)}, bf16[2,544,128]{2,1,0:T(8,128)(2,1)S(1)}, bf16[2,544,128]{2,1,0:T(8,128)(2,1)S(1)}) custom-call(s32[8]{0:T(128)S(1)} %broadcast_xor_fusion.refs_10_.refs_0_, bf16[1056,128]{1,0:T(8,128)(2,1)S(1)} %get-tuple-element.47.refs_9_.refs_1_, ...), custom_call_target="tpu_custom_call" | custom-call | flops 1 | bytes 1 | tf_op jit(solution)/shard_map/pick_states/pallas_call | solution.py:558
  41.1 0.6 collective-permute-start.6
  41.6 2.1 %collective-permute-start.7 = (bf16[2,544,128]{2,1,0:T(8,128)(2,1)S(1)}, bf16[2,544,128]{2,1,0:T(8,128)(2,1)S(1)}, u32[]{:S(2)}, u32[]{:S(2)}) collective-permute-start(bf16[2,544,128]{2,1,0:T(8,128)(2,1)S(1)} %get-tuple-element.63), channel_id=1, source_target_pairs={{0,4},{2,6},{4,0},{6,2},{8,12},{10,14},{12,8},{14,10},{1,5},{3,7},... | collective-permute-start | bytes 835592 | tf_op jit(solution)/shard_map/ppermute | solution.py:495
  43.7 0.9 %collective-permute-start.8 = (bf16[2,544,128]{2,1,0:T(8,128)(2,1)S(1)}, bf16[2,544,128]{2,1,0:T(8,128)(2,1)S(1)}, u32[]{:S(2)}, u32[]{:S(2)}) collective-permute-start(bf16[2,544,128]{2,1,0:T(8,128)(2,1)S(1)} %get-tuple-element.64), channel_id=1, source_target_pairs={{0,6},{2,4},{4,2},{6,0},{8,14},{10,12},{12,10},{14,8},{1,7},{3,5},... | collective-permute-start | bytes 835592 | tf_op jit(solution)/shard_map/ppermute | solution.py:495
  44.6 3.0 %collective-permute-done.9.refs_6_.refs_5_ = bf16[4,256,128]{2,1,0:T(8,128)(2,1)S(1)} collective-permute-done((bf16[4,256,128]{2,1,0:T(8,128)(2,1)S(1)}, bf16[4,256,128]{2,1,0:T(8,128)(2,1)S(1)}, u32[]{:S(2)}, u32[]{:S(2)}) %collective-permute-start.9) | collective-permute-done | bytes 262176 | tf_op jit(solution)/shard_map/ppermute | solution.py:495
  47.7 0.1 collective-permute-start.10
  47.7 1.2 %pick_states.4 = (bf16[2,256,128]{2,1,0:T(8,128)(2,1)S(1)}, bf16[2,256,128]{2,1,0:T(8,128)(2,1)S(1)}, bf16[2,256,128]{2,1,0:T(8,128)(2,1)S(1)}, bf16[2,256,128]{2,1,0:T(8,128)(2,1)S(1)}) custom-call(s32[8]{0:T(128)S(1)} %broadcast_xor_fusion.refs_10_.refs_0_, bf16[1056,128]{1,0:T(8,128)(2,1)S(1)} %get-tuple-element.47.refs_9_.refs_1_, ...), custom_call_target="tpu_custom_call" | custom-call | flops 1 | bytes 1 | tf_op jit(solution)/shard_map/pick_states/pallas_call | solution.py:558
  49.0 1.5 %collective-permute-start.14 = (bf16[2,256,128]{2,1,0:T(8,128)(2,1)S(1)}, bf16[2,256,128]{2,1,0:T(8,128)(2,1)S(1)}, u32[]{:S(2)}, u32[]{:S(2)}) collective-permute-start(bf16[2,256,128]{2,1,0:T(8,128)(2,1)S(1)} %get-tuple-element.86), channel_id=1, source_target_pairs={{0,2},{2,0},{4,6},{6,4},{8,10},{10,8},{12,14},{14,12},{1,3},{3,1},... | collective-permute-start | bytes 393224 | tf_op jit(solution)/shard_map/ppermute | solution.py:495
  50.5 5.4 %early.7 = (f32[4,256,1024]{2,1,0:T(8,128)S(1)}, bf16[4,256,128]{2,1,0:T(8,128)(2,1)S(1)}, f32[4,16,256]{2,1,0:T(8,128)S(1)}, f32[4,256,256]{2,1,0:T(8,128)S(1)}...) custom-call(bf16[2,256,4096]{2,1,0:T(8,128)(2,1)} %refs_0_.7, ...), custom_call_target="tpu_custom_call", output_to_operand_aliasing={{0}: (10, {}), {1}: (11, {}), {2}: (12, {}), {3}: (13, {}),... | custom-call | flops 1 | bytes 1 | tf_op jit(solution)/shard_map/early/pallas_call | solution.py:591
  55.9 1.3 %collective-permute-start.15 = (bf16[2,256,128]{2,1,0:T(8,128)(2,1)S(1)}, bf16[2,256,128]{2,1,0:T(8,128)(2,1)S(1)}, u32[]{:S(2)}, u32[]{:S(2)}) collective-permute-start(bf16[2,256,128]{2,1,0:T(8,128)(2,1)S(1)} %get-tuple-element.87), channel_id=1, source_target_pairs={{0,4},{2,6},{4,0},{6,2},{8,12},{10,14},{12,8},{14,10},{1,5},{3,7},... | collective-permute-start | bytes 393224 | tf_op jit(solution)/shard_map/ppermute | solution.py:495
  57.1 0.0 collective-permute-done.7.refs_3_.refs_7_
  57.1 1.0 %collective-permute-start.16 = (bf16[2,256,128]{2,1,0:T(8,128)(2,1)S(1)}, bf16[2,256,128]{2,1,0:T(8,128)(2,1)S(1)}, u32[]{:S(2)}, u32[]{:S(2)}) collective-permute-start(bf16[2,256,128]{2,1,0:T(8,128)(2,1)S(1)} %get-tuple-element.88), channel_id=1, source_target_pairs={{0,6},{2,4},{4,2},{6,0},{8,14},{10,12},{12,10},{14,8},{1,7},{3,5},... | collective-permute-start | bytes 393224 | tf_op jit(solution)/shard_map/ppermute | solution.py:495
  58.1 7.0 %collective-permute-done.8.refs_4_.refs_8_ = bf16[2,544,128]{2,1,0:T(8,128)(2,1)S(1)} collective-permute-done((bf16[2,544,128]{2,1,0:T(8,128)(2,1)S(1)}, bf16[2,544,128]{2,1,0:T(8,128)(2,1)S(1)}, u32[]{:S(2)}, u32[]{:S(2)}) %collective-permute-start.8) | collective-permute-done | bytes 278560 | tf_op jit(solution)/shard_map/ppermute | solution.py:495
  65.1 3.9 %late.3.refs_6_.refs_22_ = bf16[2,256,4096]{2,1,0:T(8,128)(2,1)} custom-call(s32[1]{0:T(128)} %bitcast.place_ref.refs_0_, bf16[2,544,128]{2,1,0:T(8,128)(2,1)S(1)} %get-tuple-element.61.refs_5_.refs_1_, bf16[2,544,128]{2,1,0:T(8,128)(2,1)S(1)} %collective-permute-done.6.refs_2_.refs_6_, bf16[2,544,128]{2,1,0:T(8,128)(2,1)S(1)} %collective-permute-done.7.refs_3_.refs_7_, ...), custom_call_target="tpu_custom_call" | custom-call | flops 1 | bytes 1 | tf_op jit(solution)/shard_map/late/pallas_call | solution.py:638
  69.0 0.0 collective-permute-done.10.refs_5_
  69.1 1.1 %pick_states.5 = (bf16[2,256,128]{2,1,0:T(8,128)(2,1)S(1)}, bf16[2,256,128]{2,1,0:T(8,128)(2,1)S(1)}, bf16[2,256,128]{2,1,0:T(8,128)(2,1)S(1)}, bf16[2,256,128]{2,1,0:T(8,128)(2,1)S(1)}) custom-call(s32[8]{0:T(128)S(1)} %broadcast_xor_fusion.refs_10_.refs_0_, bf16[1056,128]{1,0:T(8,128)(2,1)S(1)} %get-tuple-element.47.refs_9_.refs_1_, ...), custom_call_target="tpu_custom_call" | custom-call | flops 1 | bytes 1 | tf_op jit(solution)/shard_map/pick_states/pallas_call | solution.py:558
  70.1 1.7 %collective-permute-start.11 = (bf16[2,256,128]{2,1,0:T(8,128)(2,1)S(1)}, bf16[2,256,128]{2,1,0:T(8,128)(2,1)S(1)}, u32[]{:S(2)}, u32[]{:S(2)}) collective-permute-start(bf16[2,256,128]{2,1,0:T(8,128)(2,1)S(1)} %get-tuple-element.83), channel_id=1, source_target_pairs={{0,2},{2,0},{4,6},{6,4},{8,10},{10,8},{12,14},{14,12},{1,3},{3,1},... | collective-permute-start | bytes 393224 | tf_op jit(solution)/shard_map/ppermute | solution.py:495
  71.8 0.0 collective-permute-start.12
  71.8 0.0 collective-permute-done.14.refs_6_
  71.8 1.9 %collective-permute-start.13 = (bf16[2,256,128]{2,1,0:T(8,128)(2,1)S(1)}, bf16[2,256,128]{2,1,0:T(8,128)(2,1)S(1)}, u32[]{:S(2)}, u32[]{:S(2)}) collective-permute-start(bf16[2,256,128]{2,1,0:T(8,128)(2,1)S(1)} %get-tuple-element.85), channel_id=1, source_target_pairs={{0,6},{2,4},{4,2},{6,0},{8,14},{10,12},{12,10},{14,8},{1,7},{3,5},... | collective-permute-start | bytes 393224 | tf_op jit(solution)/shard_map/ppermute | solution.py:495
  73.7 0.0 collective-permute-done.15.refs_7_
  73.7 0.0 collective-permute-done.16.refs_8_
  73.7 2.9 %late.4.refs_21_ = bf16[2,256,4096]{2,1,0:T(8,128)(2,1)} custom-call(s32[1]{0:T(128)} %bitcast.place_ref.refs_0_, bf16[2,544,128]{2,1,0:T(8,128)(2,1)S(1)} %get-tuple-element.61.refs_5_.refs_1_, bf16[2,544,128]{2,1,0:T(8,128)(2,1)S(1)} %collective-permute-done.6.refs_2_.refs_6_, ...), custom_call_target="tpu_custom_call", output_to_operand_aliasing={{}: (22, {})} | custom-call | flops 1 | bytes 1 | tf_op jit(solution)/shard_map/late/pallas_call | solution.py:638
  76.6 0.0 collective-permute-done.11.refs_6_
  76.6 0.5 collective-permute-done.12.refs_7_
  77.0 2.5 %collective-permute-done.13.refs_8_ = bf16[2,256,128]{2,1,0:T(8,128)(2,1)S(1)} collective-permute-done((bf16[2,256,128]{2,1,0:T(8,128)(2,1)S(1)}, bf16[2,256,128]{2,1,0:T(8,128)(2,1)S(1)}, u32[]{:S(2)}, u32[]{:S(2)}) %collective-permute-start.13) | collective-permute-done | bytes 131104 | tf_op jit(solution)/shard_map/ppermute | solution.py:495
  79.5 2.9 %late.5 = bf16[2,256,4096]{2,1,0:T(8,128)(2,1)} custom-call(s32[1]{0:T(128)} %bitcast.place_ref.refs_0_, bf16[2,544,128]{2,1,0:T(8,128)(2,1)S(1)} %get-tuple-element.61.refs_5_.refs_1_, bf16[2,544,128]{2,1,0:T(8,128)(2,1)S(1)} %collective-permute-done.6.refs_2_.refs_6_, ...), custom_call_target="tpu_custom_call", output_to_operand_aliasing={{}: (21, {})} | custom-call | flops 1 | bytes 1 | tf_op jit(solution)/shard_map/late/pallas_call | solution.py:638
  (19 shorter events, 0.1 us)
Async XLA Ops:
  0.0 10.8 %copy-start.3 = (s32[8]{0:T(128)S(1)}, s32[8]{0:T(128)}, u32[]{:S(2)}) copy-start(s32[8]{0:T(128)} %param.26) | copy-start | bytes 100
  0.0 10.9 %copy-start.4 = (s32[16]{0:T(128)S(1)}, s32[16]{0:T(128)}, u32[]{:S(2)}) copy-start(s32[16]{0:T(128)} %param.27) | copy-start | bytes 196
  0.0 11.2 %copy-start = (f32[64]{0:T(128)S(1)}, f32[64]{0:T(128)}, u32[]{:S(2)}) copy-start(f32[64]{0:T(128)} %param.18) | copy-start | bytes 772
  0.0 11.3 %copy-start.1 = (f32[64]{0:T(128)S(1)}, f32[64]{0:T(128)}, u32[]{:S(2)}) copy-start(f32[64]{0:T(128)} %param.19) | copy-start | bytes 772
  0.0 11.4 %copy-start.2 = (f32[64]{0:T(128)S(1)}, f32[64]{0:T(128)}, u32[]{:S(2)}) copy-start(f32[64]{0:T(128)} %param.20) | copy-start | bytes 772
  1.8 25.9 %collective-permute-start = (bf16[1056,128]{1,0:T(8,128)(2,1)S(1)}, bf16[1056,128]{1,0:T(8,128)(2,1)S(1)}, u32[]{:S(2)}, u32[]{:S(2)}) collective-permute-start(bf16[1056,128]{1,0:T(8,128)(2,1)S(1)} %get-tuple-element.48), channel_id=1, source_target_pairs={{0,2},{2,0},{4,6},{6,4},{8,10},{10,8},{12,14},{14,12},{1,3},{3,1},... | collective-permute-start | bytes 811016 | tf_op jit(solution)/shard_map/ppermute | solution.py:495
  4.9 22.9 %collective-permute-start.1 = (bf16[1056,128]{1,0:T(8,128)(2,1)S(1)}, bf16[1056,128]{1,0:T(8,128)(2,1)S(1)}, u32[]{:S(2)}, u32[]{:S(2)}) collective-permute-start(bf16[1056,128]{1,0:T(8,128)(2,1)S(1)} %get-tuple-element.49), channel_id=1, source_target_pairs={{0,4},{2,6},{4,0},{6,2},{8,12},{10,14},{12,8},{14,10},{1,5},{3,7},... | collective-permute-start | bytes 811016 | tf_op jit(solution)/shard_map/ppermute | solution.py:495
  6.5 21.3 %collective-permute-start.2 = (bf16[1056,128]{1,0:T(8,128)(2,1)S(1)}, bf16[1056,128]{1,0:T(8,128)(2,1)S(1)}, u32[]{:S(2)}, u32[]{:S(2)}) collective-permute-start(bf16[1056,128]{1,0:T(8,128)(2,1)S(1)} %get-tuple-element.50), channel_id=1, source_target_pairs={{0,6},{2,4},{4,2},{6,0},{8,14},{10,12},{12,10},{14,8},{1,7},{3,5},... | collective-permute-start | bytes 811016 | tf_op jit(solution)/shard_map/ppermute | solution.py:495
  6.5 21.3 %collective-permute-start.3 = (bf16[2,544,128]{2,1,0:T(8,128)(2,1)S(1)}, bf16[2,544,128]{2,1,0:T(8,128)(2,1)S(1)}, u32[]{:S(2)}, u32[]{:S(2)}) collective-permute-start(bf16[2,544,128]{2,1,0:T(8,128)(2,1)S(1)} %get-tuple-element.51), channel_id=1, source_target_pairs={{0,8},{2,10},{4,12},{6,14},{8,0},{10,2},{12,4},{14,6},{1,9},{3,11}... | collective-permute-start | bytes 835592 | tf_op jit(solution)/shard_map/ppermute | solution.py:495
  9.4 23.2 %collective-permute-start.4 = (bf16[2,544,128]{2,1,0:T(8,128)(2,1)S(1)}, bf16[2,544,128]{2,1,0:T(8,128)(2,1)S(1)}, u32[]{:S(2)}, u32[]{:S(2)}) collective-permute-start(bf16[2,544,128]{2,1,0:T(8,128)(2,1)S(1)} %get-tuple-element.52), channel_id=1, source_target_pairs={{0,12},{2,14},{4,8},{6,10},{8,4},{10,6},{12,0},{14,2},{1,13},{3,15... | collective-permute-start | bytes 835592 | tf_op jit(solution)/shard_map/ppermute | solution.py:495
  32.7 7.2 %collective-permute-start.5 = (bf16[2,544,128]{2,1,0:T(8,128)(2,1)S(1)}, bf16[2,544,128]{2,1,0:T(8,128)(2,1)S(1)}, u32[]{:S(2)}, u32[]{:S(2)}) collective-permute-start(bf16[2,544,128]{2,1,0:T(8,128)(2,1)S(1)} %stack_first.1), channel_id=1, source_target_pairs={{0,2},{2,0},{4,6},{6,4},{8,10},{10,8},{12,14},{14,12},{1,3},{3,1},... | collective-permute-start | bytes 835592 | tf_op jit(solution)/shard_map/ppermute | solution.py:495
  33.3 14.3 %collective-permute-start.9 = (bf16[4,256,128]{2,1,0:T(8,128)(2,1)S(1)}, bf16[4,256,128]{2,1,0:T(8,128)(2,1)S(1)}, u32[]{:S(2)}, u32[]{:S(2)}) collective-permute-start(bf16[4,256,128]{2,1,0:T(8,128)(2,1)S(1)} %stack_later.2.refs_3_), channel_id=1, source_target_pairs={{0,8},{2,10},{4,12},{6,14},{8,0},{10,2},{12,4},{14,6},{1,9},{3,11}... | collective-permute-start | bytes 786440 | tf_op jit(solution)/shard_map/ppermute | solution.py:495
  41.1 14.8 %collective-permute-start.6 = (bf16[2,544,128]{2,1,0:T(8,128)(2,1)S(1)}, bf16[2,544,128]{2,1,0:T(8,128)(2,1)S(1)}, u32[]{:S(2)}, u32[]{:S(2)}) collective-permute-start(bf16[2,544,128]{2,1,0:T(8,128)(2,1)S(1)} %get-tuple-element.62), channel_id=1, source_target_pairs={{0,2},{2,0},{4,6},{6,4},{8,10},{10,8},{12,14},{14,12},{1,3},{3,1},... | collective-permute-start | bytes 835592 | tf_op jit(solution)/shard_map/ppermute | solution.py:495
  41.6 15.5 %collective-permute-start.7 = (bf16[2,544,128]{2,1,0:T(8,128)(2,1)S(1)}, bf16[2,544,128]{2,1,0:T(8,128)(2,1)S(1)}, u32[]{:S(2)}, u32[]{:S(2)}) collective-permute-start(bf16[2,544,128]{2,1,0:T(8,128)(2,1)S(1)} %get-tuple-element.63), channel_id=1, source_target_pairs={{0,4},{2,6},{4,0},{6,2},{8,12},{10,14},{12,8},{14,10},{1,5},{3,7},... | collective-permute-start | bytes 835592 | tf_op jit(solution)/shard_map/ppermute | solution.py:495
  43.7 21.4 %collective-permute-start.8 = (bf16[2,544,128]{2,1,0:T(8,128)(2,1)S(1)}, bf16[2,544,128]{2,1,0:T(8,128)(2,1)S(1)}, u32[]{:S(2)}, u32[]{:S(2)}) collective-permute-start(bf16[2,544,128]{2,1,0:T(8,128)(2,1)S(1)} %get-tuple-element.64), channel_id=1, source_target_pairs={{0,6},{2,4},{4,2},{6,0},{8,14},{10,12},{12,10},{14,8},{1,7},{3,5},... | collective-permute-start | bytes 835592 | tf_op jit(solution)/shard_map/ppermute | solution.py:495
  47.7 21.4 %collective-permute-start.10 = (bf16[4,256,128]{2,1,0:T(8,128)(2,1)S(1)}, bf16[4,256,128]{2,1,0:T(8,128)(2,1)S(1)}, u32[]{:S(2)}, u32[]{:S(2)}) collective-permute-start(bf16[4,256,128]{2,1,0:T(8,128)(2,1)S(1)} %stack_later.3.refs_6_), channel_id=1, source_target_pairs={{0,8},{2,10},{4,12},{6,14},{8,0},{10,2},{12,4},{14,6},{1,9},{3,11}... | collective-permute-start | bytes 786440 | tf_op jit(solution)/shard_map/ppermute | solution.py:495
  49.0 22.8 %collective-permute-start.14 = (bf16[2,256,128]{2,1,0:T(8,128)(2,1)S(1)}, bf16[2,256,128]{2,1,0:T(8,128)(2,1)S(1)}, u32[]{:S(2)}, u32[]{:S(2)}) collective-permute-start(bf16[2,256,128]{2,1,0:T(8,128)(2,1)S(1)} %get-tuple-element.86), channel_id=1, source_target_pairs={{0,2},{2,0},{4,6},{6,4},{8,10},{10,8},{12,14},{14,12},{1,3},{3,1},... | collective-permute-start | bytes 393224 | tf_op jit(solution)/shard_map/ppermute | solution.py:495
  55.9 17.8 %collective-permute-start.15 = (bf16[2,256,128]{2,1,0:T(8,128)(2,1)S(1)}, bf16[2,256,128]{2,1,0:T(8,128)(2,1)S(1)}, u32[]{:S(2)}, u32[]{:S(2)}) collective-permute-start(bf16[2,256,128]{2,1,0:T(8,128)(2,1)S(1)} %get-tuple-element.87), channel_id=1, source_target_pairs={{0,4},{2,6},{4,0},{6,2},{8,12},{10,14},{12,8},{14,10},{1,5},{3,7},... | collective-permute-start | bytes 393224 | tf_op jit(solution)/shard_map/ppermute | solution.py:495
  57.1 16.5 %collective-permute-start.16 = (bf16[2,256,128]{2,1,0:T(8,128)(2,1)S(1)}, bf16[2,256,128]{2,1,0:T(8,128)(2,1)S(1)}, u32[]{:S(2)}, u32[]{:S(2)}) collective-permute-start(bf16[2,256,128]{2,1,0:T(8,128)(2,1)S(1)} %get-tuple-element.88), channel_id=1, source_target_pairs={{0,6},{2,4},{4,2},{6,0},{8,14},{10,12},{12,10},{14,8},{1,7},{3,5},... | collective-permute-start | bytes 393224 | tf_op jit(solution)/shard_map/ppermute | solution.py:495
  70.1 6.5 %collective-permute-start.11 = (bf16[2,256,128]{2,1,0:T(8,128)(2,1)S(1)}, bf16[2,256,128]{2,1,0:T(8,128)(2,1)S(1)}, u32[]{:S(2)}, u32[]{:S(2)}) collective-permute-start(bf16[2,256,128]{2,1,0:T(8,128)(2,1)S(1)} %get-tuple-element.83), channel_id=1, source_target_pairs={{0,2},{2,0},{4,6},{6,4},{8,10},{10,8},{12,14},{14,12},{1,3},{3,1},... | collective-permute-start | bytes 393224 | tf_op jit(solution)/shard_map/ppermute | solution.py:495
  71.8 5.2 %collective-permute-start.12 = (bf16[2,256,128]{2,1,0:T(8,128)(2,1)S(1)}, bf16[2,256,128]{2,1,0:T(8,128)(2,1)S(1)}, u32[]{:S(2)}, u32[]{:S(2)}) collective-permute-start(bf16[2,256,128]{2,1,0:T(8,128)(2,1)S(1)} %get-tuple-element.84), channel_id=1, source_target_pairs={{0,4},{2,6},{4,0},{6,2},{8,12},{10,14},{12,8},{14,10},{1,5},{3,7},... | collective-permute-start | bytes 393224 | tf_op jit(solution)/shard_map/ppermute | solution.py:495
  71.8 7.7 %collective-permute-start.13 = (bf16[2,256,128]{2,1,0:T(8,128)(2,1)S(1)}, bf16[2,256,128]{2,1,0:T(8,128)(2,1)S(1)}, u32[]{:S(2)}, u32[]{:S(2)}) collective-permute-start(bf16[2,256,128]{2,1,0:T(8,128)(2,1)S(1)} %get-tuple-element.85), channel_id=1, source_target_pairs={{0,6},{2,4},{4,2},{6,0},{8,14},{10,12},{12,10},{14,8},{1,7},{3,5},... | collective-permute-start | bytes 393224 | tf_op jit(solution)/shard_map/ppermute | solution.py:495

commit v15 on v14

--- a/solution.py
+++ b/solution.py
@@ -44,12 +44,12 @@
 
 
 def early_kernel(
-    base, x_ref, b_ref, c_ref, dt_ref, bias_ref, alog_ref, skip_ref, taps_x_ref, taps_bc_ref,
+    x_ref, b_ref, c_ref, dt_ref, bias_ref, alog_ref, skip_ref, taps_x_ref, taps_bc_ref,
     mixed_ref, c_out_ref, column_ref, first_ref, opening_ref, weights_ref, padded,
 ):
     length, wide = x_ref.shape[1:]
     heads = dt_ref.shape[1]
-    q = base + pl.program_id(0)
+    q = pl.program_id(0)
     width = wide // heads
     half = length // 2
 
@@ -495,7 +495,7 @@
         return lax.ppermute(value, "batch", perm=[(i, i ^ r) for i in range(8)])
 
     def cast():
-        rows = per_group * width + tail_lines
+        rows = per_group * width + tail_lines + 48
         rows_a = SPLIT[0] * width + tail_lines
         count = len(SPLIT) + 2
 
@@ -579,30 +579,24 @@
         )
         return [picked[0]] + [swap(picked[j], j) for j in range(1, 4)]
 
-    def early(c, piece, before, tokens):
-        per = groups // 2
-        at = lambda q: (c, 0, per * piece + q)
+    def early(c, tokens):
+        at = lambda q: (c, 0, q)
         operands = [
             x_in, b_in, c_in, dt_in, dt_bias[:, None], a_log[:, None], skip_row, conv_x, conv_bc
         ]
-        keep = len(operands)
-        tokens = list(tokens) + [keep_in_vmem(a) for a in before]
-        first = keep + len(tokens) - len(before)
         return pl.pallas_call(
-            functools.partial(
-                drop_tokens, functools.partial(early_kernel, per * piece), keep, len(tokens)
-            ),
-            grid=(per,),
+            functools.partial(drop_tokens, early_kernel, len(operands), len(tokens)),
+            grid=(groups,),
             in_specs=[
                 pl.BlockSpec((1, length, wide), at),
                 pl.BlockSpec((1, length, size), at),
                 pl.BlockSpec((1, length, size), at),
-                pl.BlockSpec((1, per_group, length), lambda q: (c, per * piece + q, 0)),
-                pl.BlockSpec((per_group, 1), lambda q: (per * piece + q, 0)),
-                pl.BlockSpec((per_group, 1), lambda q: (per * piece + q, 0)),
-                pl.BlockSpec((1, wide), lambda q: (0, per * piece + q)),
-                pl.BlockSpec((taps, wide), lambda q: (0, per * piece + q)),
-                pl.BlockSpec((2, taps, size), lambda q: (0, 0, per * piece + q)),
+                pl.BlockSpec((1, per_group, length), lambda q: (c, q, 0)),
+                pl.BlockSpec((per_group, 1), lambda q: (q, 0)),
+                pl.BlockSpec((per_group, 1), lambda q: (q, 0)),
+                pl.BlockSpec((1, wide), lambda q: (0, q)),
+                pl.BlockSpec((taps, wide), lambda q: (0, q)),
+                pl.BlockSpec((2, taps, size), lambda q: (0, 0, q)),
                 *[anywhere] * len(tokens),
             ],
             out_specs=[pl.BlockSpec(memory_space=pltpu.VMEM)] * 6,
@@ -614,7 +608,6 @@
                 pltpu.VMEM((groups, FIX, wide + 2 * size), jnp.bfloat16),
                 pltpu.VMEM((groups, 8, wide + 2 * size), jnp.float32),
             ],
-            input_output_aliases={first + i: i for i in range(len(before))},
             scratch_shapes=[pltpu.VMEM((2, 8 + length, size), jnp.float32)],
             compiler_params=params,
             cost_estimate=small,
@@ -659,8 +652,8 @@
     rows = [SPLIT[0] * width + tail_lines] + [part * width for part in SPLIT[1:]]
     chunks = [pl.ds(sum(rows[:k]), rows[k]) for k in range(len(SPLIT))]
     *own, sent_4, sent_6 = cast()
+    inside = [own[0]] + [swap(own[j], j) for j in range(1, 4)]
     crossed_a = [swap(sent_4, 4), swap(sent_6, 6)]
-    inside = [own[0]] + [swap(own[j], j) for j in range(1, 4)]
 
     def cross(k, tokens):
         moves = [(0, j, None, [(j, chunks[k])]) for j in range(4)]
@@ -671,22 +664,21 @@
         choices = [(j, chunks[k]) for j in range(4)] + [(4, j) for j in range(4)]
         return pick(rows[k], [*inside, crossed], choices, tokens)
 
-    first = early(0, 0, [], [own[0], slots])
-    first = early(0, 1, first, [])
-    second = early(1, 0, [], [first[1]])
-    sent_b, crossed_b = cross(1, [second[1], *crossed_a])
+    parts = [early(0, [own[0], slots])]
+    parts.append(early(1, [parts[0][1]]))
     moves = [(0, n, None, [(n, 1)]) for n in range(2)]
-    (spread,) = rearrange(place, crossed_a, moves, [(2, rows[0], size)], [sent_b], "stack_first")
+    (spread,) = rearrange(
+        place, crossed_a, moves, [(2, rows[0], size)], [parts[1][1]], "stack_first"
+    )
     passed = swap(spread, 1)
+    sent_b, crossed_b = cross(1, [spread])
     choices = [(j, chunks[0]) for j in range(4)] + [(4, 0), (6, 0), (5, 0), (6, 1)]
-    states_a = pick(rows[0], [*inside, *crossed_a, passed], choices, [])
+    states_a = pick(rows[0], [*inside, *crossed_a, passed], choices, [sent_b])
     sent_c, crossed_c = cross(2, [states_a[0], crossed_b])
     states_b = pick_later(1, crossed_b, [sent_c])
-    second = early(1, 1, second, [states_b[0]])
-    parts = [first, second]
-    result = late(0, states_a, states_a, parts, None, [states_b[0]])
-    states_c = pick_later(2, crossed_c, [stay(result)])
-    result = late(1, states_b, states_a, parts, result, [states_c[0]])
+    states_c = pick_later(2, crossed_c, [states_b[0]])
+    result = late(0, states_a, states_a, parts, None, [states_c[0]])
+    result = late(1, states_b, states_a, parts, result, [])
     return late(2, states_c, states_a, parts, result, [])
 
 

time: 82.8 us -> 79.9 us (0.965)
  Pallas kernels: 36.5 us -> 34.4 us
  waiting for transfers between devices: 19.9 us -> 18 us
  starting transfers between devices: 25.1 us -> 26.2 us
    pallas_call x4 -> x2, Pallas kernels: 21.5 us -> 19.3 us  [early(): pl.pallas_call(functools.partial(drop_tokens, early_kernel, len(operands)...]
    ppermute x17, waiting for transfers between devices: 19.9 us -> 18 us  [swap(): return lax.ppermute(value, 'batch', perm=[(i, i ^ r) for i in range(8)])]
    ppermute x17, starting transfers between devices: 25.1 us -> 26.2 us  [swap(): return lax.ppermute(value, 'batch', perm=[(i, i ^ r) for i in range(8)])]
  transfers between devices with their start and end apart: 17 -> 17, of which waited for: 6 -> 4; matrix products, arithmetic and copies ran while one was open for 1% -> 1% of each run, Pallas kernels for 38% -> 37%
where the time goes in v15:
time: 79.9 us; the launch traced here: 79.7 us
  Pallas kernels  34.4 us (43%)
  starting transfers between devices  26.2 us (33%)
  waiting for transfers between devices  18 us (23%)
    ppermute x17, starting transfers between devices, swap(): return lax.ppermute(value, 'batch', perm=[(i, i ^ r) for i in range(8)])  26.2 us
    pallas_call x2, Pallas kernels, early(): pl.pallas_call(functools.partial(drop_tokens, early_kernel, len(operands)...  19.3 us
    ppermute x17, waiting for transfers between devices, swap(): return lax.ppermute(value, 'batch', perm=[(i, i ^ r) for i in range(8)])  18 us
    pallas_call x3, Pallas kernels, late(): pl.pallas_call(functools.partial(drop_tokens, kernel, keep, 1 + len(opera...  9.8 us
    pallas_call x6, Pallas kernels, rearrange(): pl.pallas_call(functools.partial(drop_tokens, kernel, 1 + len(sources), l...  3.43 us
    pallas_call x1, Pallas kernels, cast(): pl.pallas_call(kernel, grid_spec=pltpu.PrefetchScalarGridSpec(num_scalar_...  1.82 us
  transfers between devices with their start and end apart: 17, of which 4 were waited for; matrix products, arithmetic and copies ran while one was open for 1% of the time, Pallas kernels for 37%

profile of v15, /device:TPU:0, one launch (start us, length us, event | category | flops | bytes accessed | tf_op | source)
XLA Modules:
  0.0 79.7 jit_solution(10366414376910112817)
XLA Ops:
  0.0 1.8 %cast_states.1 = (bf16[1104,128]{1,0:T(8,128)(2,1)S(1)}, bf16[1104,128]{1,0:T(8,128)(2,1)S(1)}, bf16[1104,128]{1,0:T(8,128)(2,1)S(1)}, bf16[1104,128]{1,0:T(8,12...) custom-call(s32[1]{0:T(128)} %bitcast.place_ref.refs_0_, f32[4,16,64,128]{3,2,1,0:T(8,128)} %bitcast.5, ...), custom_call_target="tpu_custom_call" | custom-call | flops 1 | bytes 1 | tf_op jit(solution)/shard_map/cast_states/pallas_call | solution.py:526
  1.8 4.1 %collective-permute-start.3 = (bf16[2,544,128]{2,1,0:T(8,128)(2,1)S(1)}, bf16[2,544,128]{2,1,0:T(8,128)(2,1)S(1)}, u32[]{:S(2)}, u32[]{:S(2)}) collective-permute-start(bf16[2,544,128]{2,1,0:T(8,128)(2,1)S(1)} %get-tuple-element.39), channel_id=1, source_target_pairs={{0,8},{2,10},{4,12},{6,14},{8,0},{10,2},{12,4},{14,6},{1,9},{3,11}... | collective-permute-start | bytes 835592 | tf_op jit(solution)/shard_map/ppermute | solution.py:495
  6.0 1.3 %collective-permute-start.4 = (bf16[2,544,128]{2,1,0:T(8,128)(2,1)S(1)}, bf16[2,544,128]{2,1,0:T(8,128)(2,1)S(1)}, u32[]{:S(2)}, u32[]{:S(2)}) collective-permute-start(bf16[2,544,128]{2,1,0:T(8,128)(2,1)S(1)} %get-tuple-element.40), channel_id=1, source_target_pairs={{0,12},{2,14},{4,8},{6,10},{8,4},{10,6},{12,0},{14,2},{1,13},{3,15... | collective-permute-start | bytes 835592 | tf_op jit(solution)/shard_map/ppermute | solution.py:495
  7.3 1.5 %collective-permute-start = (bf16[1104,128]{1,0:T(8,128)(2,1)S(1)}, bf16[1104,128]{1,0:T(8,128)(2,1)S(1)}, u32[]{:S(2)}, u32[]{:S(2)}) collective-permute-start(bf16[1104,128]{1,0:T(8,128)(2,1)S(1)} %get-tuple-element.36), channel_id=1, source_target_pairs={{0,2},{2,0},{4,6},{6,4},{8,10},{10,8},{12,14},{14,12},{1,3},{3,1},... | collective-permute-start | bytes 847880 | tf_op jit(solution)/shard_map/ppermute | solution.py:495
  8.8 0.2 collective-permute-start.1
  9.1 1.7 %collective-permute-start.2 = (bf16[1104,128]{1,0:T(8,128)(2,1)S(1)}, bf16[1104,128]{1,0:T(8,128)(2,1)S(1)}, u32[]{:S(2)}, u32[]{:S(2)}) collective-permute-start(bf16[1104,128]{1,0:T(8,128)(2,1)S(1)} %get-tuple-element.38), channel_id=1, source_target_pairs={{0,6},{2,4},{4,2},{6,0},{8,14},{10,12},{12,10},{14,8},{1,7},{3,5},... | collective-permute-start | bytes 847880 | tf_op jit(solution)/shard_map/ppermute | solution.py:495
  10.8 0.1 select_reduce_fusion.1
  10.9 0.1 convert_reduce_fusion
  11.0 0.2 select_reduce_fusion
  11.2 0.1 copy.23.refs_4_
  11.3 0.1 copy.24.refs_5_
  11.4 0.1 broadcast_in_dim.53
  11.5 0.1 broadcast_in_dim_reshape.3.refs_6_
  11.6 9.7 %early.2 = (f32[4,256,1024]{2,1,0:T(8,128)S(1)}, bf16[4,256,128]{2,1,0:T(8,128)(2,1)S(1)}, f32[4,16,256]{2,1,0:T(8,128)S(1)}, f32[4,256,256]{2,1,0:T(8,128)S(1)}...) custom-call(bf16[2,256,4096]{2,1,0:T(8,128)(2,1)} %refs_0_.3, bf16[2,256,512]{2,1,0:T(8,128)(2,1)} %refs_1_.3, ...), custom_call_target="tpu_custom_call" | custom-call | flops 1 | bytes 1 | tf_op jit(solution)/shard_map/early/pallas_call | solution.py:587
  21.2 9.7 %early.3 = (f32[4,256,1024]{2,1,0:T(8,128)S(1)}, bf16[4,256,128]{2,1,0:T(8,128)(2,1)S(1)}, f32[4,16,256]{2,1,0:T(8,128)S(1)}, f32[4,256,256]{2,1,0:T(8,128)S(1)}...) custom-call(bf16[2,256,4096]{2,1,0:T(8,128)(2,1)} %refs_0_.3, bf16[2,256,512]{2,1,0:T(8,128)(2,1)} %refs_1_.3, ...), custom_call_target="tpu_custom_call" | custom-call | flops 1 | bytes 1 | tf_op jit(solution)/shard_map/early/pallas_call | solution.py:587
  30.9 0.0 collective-permute-done.3.refs_1_.refs_5_
  30.9 0.0 collective-permute-done.4.refs_2_.refs_6_
  31.0 1.6 %collective-permute-start.5 = (bf16[2,544,128]{2,1,0:T(8,128)(2,1)S(1)}, bf16[2,544,128]{2,1,0:T(8,128)(2,1)S(1)}, u32[]{:S(2)}, u32[]{:S(2)}) collective-permute-start(bf16[2,544,128]{2,1,0:T(8,128)(2,1)S(1)} %stack_first.1.refs_5_), channel_id=1, source_target_pairs={{0,2},{2,0},{4,6},{6,4},{8,10},{10,8},{12,14},{14,12},{1,3},{3,1},... | collective-permute-start | bytes 835592 | tf_op jit(solution)/shard_map/ppermute | solution.py:495
  32.5 0.0 collective-permute-done.refs_2_
  32.6 0.0 collective-permute-done.1.refs_3_
  32.6 0.9 %collective-permute-done.2.refs_4_ = bf16[1104,128]{1,0:T(8,128)(2,1)S(1)} collective-permute-done((bf16[1104,128]{1,0:T(8,128)(2,1)S(1)}, bf16[1104,128]{1,0:T(8,128)(2,1)S(1)}, u32[]{:S(2)}, u32[]{:S(2)}) %collective-permute-start.2) | collective-permute-done | bytes 282656 | tf_op jit(solution)/shard_map/ppermute | solution.py:495
  33.4 1.6 %collective-permute-start.9 = (bf16[4,256,128]{2,1,0:T(8,128)(2,1)S(1)}, bf16[4,256,128]{2,1,0:T(8,128)(2,1)S(1)}, u32[]{:S(2)}, u32[]{:S(2)}) collective-permute-start(bf16[4,256,128]{2,1,0:T(8,128)(2,1)S(1)} %stack_later.2.refs_8_), channel_id=1, source_target_pairs={{0,8},{2,10},{4,12},{6,14},{8,0},{10,2},{12,4},{14,6},{1,9},{3,11}... | collective-permute-start | bytes 786440 | tf_op jit(solution)/shard_map/ppermute | solution.py:495
  35.1 4.2 %collective-permute-done.5.refs_7_ = bf16[2,544,128]{2,1,0:T(8,128)(2,1)S(1)} collective-permute-done((bf16[2,544,128]{2,1,0:T(8,128)(2,1)S(1)}, bf16[2,544,128]{2,1,0:T(8,128)(2,1)S(1)}, u32[]{:S(2)}, u32[]{:S(2)}) %collective-permute-start.5) | collective-permute-done | bytes 278560 | tf_op jit(solution)/shard_map/ppermute | solution.py:495
  39.3 1.1 %pick_states.3 = (bf16[2,544,128]{2,1,0:T(8,128)(2,1)S(1)}, bf16[2,544,128]{2,1,0:T(8,128)(2,1)S(1)}, bf16[2,544,128]{2,1,0:T(8,128)(2,1)S(1)}, bf16[2,544,128]{2,1,0:T(8,128)(2,1)S(1)}) custom-call(s32[8]{0:T(128)S(1)} %broadcast_xor_fusion.refs_10_.refs_0_, bf16[1104,128]{1,0:T(8,128)(2,1)S(1)} %get-tuple-element.35.refs_9_.refs_1_, ...), custom_call_target="tpu_custom_call" | custom-call | flops 1 | bytes 1 | tf_op jit(solution)/shard_map/pick_states/pallas_call | solution.py:558
  40.4 1.5 %collective-permute-start.6 = (bf16[2,544,128]{2,1,0:T(8,128)(2,1)S(1)}, bf16[2,544,128]{2,1,0:T(8,128)(2,1)S(1)}, u32[]{:S(2)}, u32[]{:S(2)}) collective-permute-start(bf16[2,544,128]{2,1,0:T(8,128)(2,1)S(1)} %get-tuple-element.44), channel_id=1, source_target_pairs={{0,2},{2,0},{4,6},{6,4},{8,10},{10,8},{12,14},{14,12},{1,3},{3,1},... | collective-permute-start | bytes 835592 | tf_op jit(solution)/shard_map/ppermute | solution.py:495
  41.9 0.7 collective-permute-start.7
  42.6 1.3 %collective-permute-start.8 = (bf16[2,544,128]{2,1,0:T(8,128)(2,1)S(1)}, bf16[2,544,128]{2,1,0:T(8,128)(2,1)S(1)}, u32[]{:S(2)}, u32[]{:S(2)}) collective-permute-start(bf16[2,544,128]{2,1,0:T(8,128)(2,1)S(1)} %get-tuple-element.46), channel_id=1, source_target_pairs={{0,6},{2,4},{4,2},{6,0},{8,14},{10,12},{12,10},{14,8},{1,7},{3,5},... | collective-permute-start | bytes 835592 | tf_op jit(solution)/shard_map/ppermute | solution.py:495
  43.9 2.9 %collective-permute-done.9.refs_6_.refs_5_ = bf16[4,256,128]{2,1,0:T(8,128)(2,1)S(1)} collective-permute-done((bf16[4,256,128]{2,1,0:T(8,128)(2,1)S(1)}, bf16[4,256,128]{2,1,0:T(8,128)(2,1)S(1)}, u32[]{:S(2)}, u32[]{:S(2)}) %collective-permute-start.9) | collective-permute-done | bytes 262176 | tf_op jit(solution)/shard_map/ppermute | solution.py:495
  46.9 0.1 collective-permute-start.10
  47.0 1.1 %pick_states.4 = (bf16[2,256,128]{2,1,0:T(8,128)(2,1)S(1)}, bf16[2,256,128]{2,1,0:T(8,128)(2,1)S(1)}, bf16[2,256,128]{2,1,0:T(8,128)(2,1)S(1)}, bf16[2,256,128]{2,1,0:T(8,128)(2,1)S(1)}) custom-call(s32[8]{0:T(128)S(1)} %broadcast_xor_fusion.refs_10_.refs_0_, bf16[1104,128]{1,0:T(8,128)(2,1)S(1)} %get-tuple-element.35.refs_9_.refs_1_, ...), custom_call_target="tpu_custom_call" | custom-call | flops 1 | bytes 1 | tf_op jit(solution)/shard_map/pick_states/pallas_call | solution.py:558
  48.0 1.2 %collective-permute-start.14 = (bf16[2,256,128]{2,1,0:T(8,128)(2,1)S(1)}, bf16[2,256,128]{2,1,0:T(8,128)(2,1)S(1)}, u32[]{:S(2)}, u32[]{:S(2)}) collective-permute-start(bf16[2,256,128]{2,1,0:T(8,128)(2,1)S(1)} %get-tuple-element.62), channel_id=1, source_target_pairs={{0,2},{2,0},{4,6},{6,4},{8,10},{10,8},{12,14},{14,12},{1,3},{3,1},... | collective-permute-start | bytes 393224 | tf_op jit(solution)/shard_map/ppermute | solution.py:495
  49.3 10.0 %collective-permute-done.10.refs_5_ = bf16[4,256,128]{2,1,0:T(8,128)(2,1)S(1)} collective-permute-done((bf16[4,256,128]{2,1,0:T(8,128)(2,1)S(1)}, bf16[4,256,128]{2,1,0:T(8,128)(2,1)S(1)}, u32[]{:S(2)}, u32[]{:S(2)}) %collective-permute-start.10) | collective-permute-done | bytes 262176 | tf_op jit(solution)/shard_map/ppermute | solution.py:495
  59.2 5.5 %collective-permute-start.15 = (bf16[2,256,128]{2,1,0:T(8,128)(2,1)S(1)}, bf16[2,256,128]{2,1,0:T(8,128)(2,1)S(1)}, u32[]{:S(2)}, u32[]{:S(2)}) collective-permute-start(bf16[2,256,128]{2,1,0:T(8,128)(2,1)S(1)} %get-tuple-element.63), channel_id=1, source_target_pairs={{0,4},{2,6},{4,0},{6,2},{8,12},{10,14},{12,8},{14,10},{1,5},{3,7},... | collective-permute-start | bytes 393224 | tf_op jit(solution)/shard_map/ppermute | solution.py:495
  64.8 1.2 %pick_states.5 = (bf16[2,256,128]{2,1,0:T(8,128)(2,1)S(1)}, bf16[2,256,128]{2,1,0:T(8,128)(2,1)S(1)}, bf16[2,256,128]{2,1,0:T(8,128)(2,1)S(1)}, bf16[2,256,128]{2,1,0:T(8,128)(2,1)S(1)}) custom-call(s32[8]{0:T(128)S(1)} %broadcast_xor_fusion.refs_10_.refs_0_, bf16[1104,128]{1,0:T(8,128)(2,1)S(1)} %get-tuple-element.35.refs_9_.refs_1_, ...), custom_call_target="tpu_custom_call" | custom-call | flops 1 | bytes 1 | tf_op jit(solution)/shard_map/pick_states/pallas_call | solution.py:558
  66.0 0.0 collective-permute-done.14.refs_6_
  66.0 0.1 collective-permute-start.16
  66.1 0.0 collective-permute-done.6.refs_2_.refs_6_
  66.1 1.4 %collective-permute-start.11 = (bf16[2,256,128]{2,1,0:T(8,128)(2,1)S(1)}, bf16[2,256,128]{2,1,0:T(8,128)(2,1)S(1)}, u32[]{:S(2)}, u32[]{:S(2)}) collective-permute-start(bf16[2,256,128]{2,1,0:T(8,128)(2,1)S(1)} %get-tuple-element.49), channel_id=1, source_target_pairs={{0,2},{2,0},{4,6},{6,4},{8,10},{10,8},{12,14},{14,12},{1,3},{3,1},... | collective-permute-start | bytes 393224 | tf_op jit(solution)/shard_map/ppermute | solution.py:495
  67.5 0.0 collective-permute-done.7.refs_3_.refs_7_
  67.5 2.0 %collective-permute-start.12 = (bf16[2,256,128]{2,1,0:T(8,128)(2,1)S(1)}, bf16[2,256,128]{2,1,0:T(8,128)(2,1)S(1)}, u32[]{:S(2)}, u32[]{:S(2)}) collective-permute-start(bf16[2,256,128]{2,1,0:T(8,128)(2,1)S(1)} %get-tuple-element.50), channel_id=1, source_target_pairs={{0,4},{2,6},{4,0},{6,2},{8,12},{10,14},{12,8},{14,10},{1,5},{3,7},... | collective-permute-start | bytes 393224 | tf_op jit(solution)/shard_map/ppermute | solution.py:495
  69.6 0.0 collective-permute-done.8.refs_4_.refs_8_
  69.6 0.1 collective-permute-start.13
  69.6 3.9 %late.3.refs_21_ = bf16[2,256,4096]{2,1,0:T(8,128)(2,1)} custom-call(s32[1]{0:T(128)} %bitcast.place_ref.refs_0_, bf16[2,544,128]{2,1,0:T(8,128)(2,1)S(1)} %get-tuple-element.43.refs_5_.refs_1_, bf16[2,544,128]{2,1,0:T(8,128)(2,1)S(1)} %collective-permute-done.6.refs_2_.refs_6_, bf16[2,544,128]{2,1,0:T(8,128)(2,1)S(1)} %collective-permute-done.7.refs_3_.refs_7_, ...), custom_call_target="tpu_custom_call" | custom-call | flops 1 | bytes 1 | tf_op jit(solution)/shard_map/late/pallas_call | solution.py:631
  73.6 0.0 collective-permute-done.15.refs_7_
  73.6 0.0 collective-permute-done.16.refs_8_
  73.6 2.9 %late.4.refs_21_ = bf16[2,256,4096]{2,1,0:T(8,128)(2,1)} custom-call(s32[1]{0:T(128)} %bitcast.place_ref.refs_0_, bf16[2,544,128]{2,1,0:T(8,128)(2,1)S(1)} %get-tuple-element.43.refs_5_.refs_1_, bf16[2,544,128]{2,1,0:T(8,128)(2,1)S(1)} %collective-permute-done.6.refs_2_.refs_6_, ...), custom_call_target="tpu_custom_call", output_to_operand_aliasing={{}: (21, {})} | custom-call | flops 1 | bytes 1 | tf_op jit(solution)/shard_map/late/pallas_call | solution.py:631
  76.6 0.0 collective-permute-done.13.refs_8_
  76.6 2.9 %late.5 = bf16[2,256,4096]{2,1,0:T(8,128)(2,1)} custom-call(s32[1]{0:T(128)} %bitcast.place_ref.refs_0_, bf16[2,544,128]{2,1,0:T(8,128)(2,1)S(1)} %get-tuple-element.43.refs_5_.refs_1_, bf16[2,544,128]{2,1,0:T(8,128)(2,1)S(1)} %collective-permute-done.6.refs_2_.refs_6_, ...), custom_call_target="tpu_custom_call", output_to_operand_aliasing={{}: (21, {})} | custom-call | flops 1 | bytes 1 | tf_op jit(solution)/shard_map/late/pallas_call | solution.py:631
  (17 shorter events, 0.1 us)
Async XLA Ops:
  0.0 10.8 %copy-start.3 = (s32[8]{0:T(128)S(1)}, s32[8]{0:T(128)}, u32[]{:S(2)}) copy-start(s32[8]{0:T(128)} %param.26) | copy-start | bytes 100
  0.0 10.9 %copy-start.4 = (s32[16]{0:T(128)S(1)}, s32[16]{0:T(128)}, u32[]{:S(2)}) copy-start(s32[16]{0:T(128)} %param.27) | copy-start | bytes 196
  0.0 11.2 %copy-start = (f32[64]{0:T(128)S(1)}, f32[64]{0:T(128)}, u32[]{:S(2)}) copy-start(f32[64]{0:T(128)} %param.18) | copy-start | bytes 772
  0.0 11.3 %copy-start.1 = (f32[64]{0:T(128)S(1)}, f32[64]{0:T(128)}, u32[]{:S(2)}) copy-start(f32[64]{0:T(128)} %param.19) | copy-start | bytes 772
  0.0 11.4 %copy-start.2 = (f32[64]{0:T(128)S(1)}, f32[64]{0:T(128)}, u32[]{:S(2)}) copy-start(f32[64]{0:T(128)} %param.20) | copy-start | bytes 772
  1.8 29.1 %collective-permute-start.3 = (bf16[2,544,128]{2,1,0:T(8,128)(2,1)S(1)}, bf16[2,544,128]{2,1,0:T(8,128)(2,1)S(1)}, u32[]{:S(2)}, u32[]{:S(2)}) collective-permute-start(bf16[2,544,128]{2,1,0:T(8,128)(2,1)S(1)} %get-tuple-element.39), channel_id=1, source_target_pairs={{0,8},{2,10},{4,12},{6,14},{8,0},{10,2},{12,4},{14,6},{1,9},{3,11}... | collective-permute-start | bytes 835592 | tf_op jit(solution)/shard_map/ppermute | solution.py:495
  6.0 25.0 %collective-permute-start.4 = (bf16[2,544,128]{2,1,0:T(8,128)(2,1)S(1)}, bf16[2,544,128]{2,1,0:T(8,128)(2,1)S(1)}, u32[]{:S(2)}, u32[]{:S(2)}) collective-permute-start(bf16[2,544,128]{2,1,0:T(8,128)(2,1)S(1)} %get-tuple-element.40), channel_id=1, source_target_pairs={{0,12},{2,14},{4,8},{6,10},{8,4},{10,6},{12,0},{14,2},{1,13},{3,15... | collective-permute-start | bytes 835592 | tf_op jit(solution)/shard_map/ppermute | solution.py:495
  7.3 25.2 %collective-permute-start = (bf16[1104,128]{1,0:T(8,128)(2,1)S(1)}, bf16[1104,128]{1,0:T(8,128)(2,1)S(1)}, u32[]{:S(2)}, u32[]{:S(2)}) collective-permute-start(bf16[1104,128]{1,0:T(8,128)(2,1)S(1)} %get-tuple-element.36), channel_id=1, source_target_pairs={{0,2},{2,0},{4,6},{6,4},{8,10},{10,8},{12,14},{14,12},{1,3},{3,1},... | collective-permute-start | bytes 847880 | tf_op jit(solution)/shard_map/ppermute | solution.py:495
  8.8 23.7 %collective-permute-start.1 = (bf16[1104,128]{1,0:T(8,128)(2,1)S(1)}, bf16[1104,128]{1,0:T(8,128)(2,1)S(1)}, u32[]{:S(2)}, u32[]{:S(2)}) collective-permute-start(bf16[1104,128]{1,0:T(8,128)(2,1)S(1)} %get-tuple-element.37), channel_id=1, source_target_pairs={{0,4},{2,6},{4,0},{6,2},{8,12},{10,14},{12,8},{14,10},{1,5},{3,7},... | collective-permute-start | bytes 847880 | tf_op jit(solution)/shard_map/ppermute | solution.py:495
  9.1 24.4 %collective-permute-start.2 = (bf16[1104,128]{1,0:T(8,128)(2,1)S(1)}, bf16[1104,128]{1,0:T(8,128)(2,1)S(1)}, u32[]{:S(2)}, u32[]{:S(2)}) collective-permute-start(bf16[1104,128]{1,0:T(8,128)(2,1)S(1)} %get-tuple-element.38), channel_id=1, source_target_pairs={{0,6},{2,4},{4,2},{6,0},{8,14},{10,12},{12,10},{14,8},{1,7},{3,5},... | collective-permute-start | bytes 847880 | tf_op jit(solution)/shard_map/ppermute | solution.py:495
  31.0 8.3 %collective-permute-start.5 = (bf16[2,544,128]{2,1,0:T(8,128)(2,1)S(1)}, bf16[2,544,128]{2,1,0:T(8,128)(2,1)S(1)}, u32[]{:S(2)}, u32[]{:S(2)}) collective-permute-start(bf16[2,544,128]{2,1,0:T(8,128)(2,1)S(1)} %stack_first.1.refs_5_), channel_id=1, source_target_pairs={{0,2},{2,0},{4,6},{6,4},{8,10},{10,8},{12,14},{14,12},{1,3},{3,1},... | collective-permute-start | bytes 835592 | tf_op jit(solution)/shard_map/ppermute | solution.py:495
  33.4 13.4 %collective-permute-start.9 = (bf16[4,256,128]{2,1,0:T(8,128)(2,1)S(1)}, bf16[4,256,128]{2,1,0:T(8,128)(2,1)S(1)}, u32[]{:S(2)}, u32[]{:S(2)}) collective-permute-start(bf16[4,256,128]{2,1,0:T(8,128)(2,1)S(1)} %stack_later.2.refs_8_), channel_id=1, source_target_pairs={{0,8},{2,10},{4,12},{6,14},{8,0},{10,2},{12,4},{14,6},{1,9},{3,11}... | collective-permute-start | bytes 786440 | tf_op jit(solution)/shard_map/ppermute | solution.py:495
  40.4 25.7 %collective-permute-start.6 = (bf16[2,544,128]{2,1,0:T(8,128)(2,1)S(1)}, bf16[2,544,128]{2,1,0:T(8,128)(2,1)S(1)}, u32[]{:S(2)}, u32[]{:S(2)}) collective-permute-start(bf16[2,544,128]{2,1,0:T(8,128)(2,1)S(1)} %get-tuple-element.44), channel_id=1, source_target_pairs={{0,2},{2,0},{4,6},{6,4},{8,10},{10,8},{12,14},{14,12},{1,3},{3,1},... | collective-permute-start | bytes 835592 | tf_op jit(solution)/shard_map/ppermute | solution.py:495
  41.9 25.6 %collective-permute-start.7 = (bf16[2,544,128]{2,1,0:T(8,128)(2,1)S(1)}, bf16[2,544,128]{2,1,0:T(8,128)(2,1)S(1)}, u32[]{:S(2)}, u32[]{:S(2)}) collective-permute-start(bf16[2,544,128]{2,1,0:T(8,128)(2,1)S(1)} %get-tuple-element.45), channel_id=1, source_target_pairs={{0,4},{2,6},{4,0},{6,2},{8,12},{10,14},{12,8},{14,10},{1,5},{3,7},... | collective-permute-start | bytes 835592 | tf_op jit(solution)/shard_map/ppermute | solution.py:495
  42.6 26.9 %collective-permute-start.8 = (bf16[2,544,128]{2,1,0:T(8,128)(2,1)S(1)}, bf16[2,544,128]{2,1,0:T(8,128)(2,1)S(1)}, u32[]{:S(2)}, u32[]{:S(2)}) collective-permute-start(bf16[2,544,128]{2,1,0:T(8,128)(2,1)S(1)} %get-tuple-element.46), channel_id=1, source_target_pairs={{0,6},{2,4},{4,2},{6,0},{8,14},{10,12},{12,10},{14,8},{1,7},{3,5},... | collective-permute-start | bytes 835592 | tf_op jit(solution)/shard_map/ppermute | solution.py:495
  46.9 12.4 %collective-permute-start.10 = (bf16[4,256,128]{2,1,0:T(8,128)(2,1)S(1)}, bf16[4,256,128]{2,1,0:T(8,128)(2,1)S(1)}, u32[]{:S(2)}, u32[]{:S(2)}) collective-permute-start(bf16[4,256,128]{2,1,0:T(8,128)(2,1)S(1)} %stack_later.3.refs_6_), channel_id=1, source_target_pairs={{0,8},{2,10},{4,12},{6,14},{8,0},{10,2},{12,4},{14,6},{1,9},{3,11}... | collective-permute-start | bytes 786440 | tf_op jit(solution)/shard_map/ppermute | solution.py:495
  48.0 18.0 %collective-permute-start.14 = (bf16[2,256,128]{2,1,0:T(8,128)(2,1)S(1)}, bf16[2,256,128]{2,1,0:T(8,128)(2,1)S(1)}, u32[]{:S(2)}, u32[]{:S(2)}) collective-permute-start(bf16[2,256,128]{2,1,0:T(8,128)(2,1)S(1)} %get-tuple-element.62), channel_id=1, source_target_pairs={{0,2},{2,0},{4,6},{6,4},{8,10},{10,8},{12,14},{14,12},{1,3},{3,1},... | collective-permute-start | bytes 393224 | tf_op jit(solution)/shard_map/ppermute | solution.py:495
  59.2 14.3 %collective-permute-start.15 = (bf16[2,256,128]{2,1,0:T(8,128)(2,1)S(1)}, bf16[2,256,128]{2,1,0:T(8,128)(2,1)S(1)}, u32[]{:S(2)}, u32[]{:S(2)}) collective-permute-start(bf16[2,256,128]{2,1,0:T(8,128)(2,1)S(1)} %get-tuple-element.63), channel_id=1, source_target_pairs={{0,4},{2,6},{4,0},{6,2},{8,12},{10,14},{12,8},{14,10},{1,5},{3,7},... | collective-permute-start | bytes 393224 | tf_op jit(solution)/shard_map/ppermute | solution.py:495
  66.0 7.6 %collective-permute-start.16 = (bf16[2,256,128]{2,1,0:T(8,128)(2,1)S(1)}, bf16[2,256,128]{2,1,0:T(8,128)(2,1)S(1)}, u32[]{:S(2)}, u32[]{:S(2)}) collective-permute-start(bf16[2,256,128]{2,1,0:T(8,128)(2,1)S(1)} %get-tuple-element.64), channel_id=1, source_target_pairs={{0,6},{2,4},{4,2},{6,0},{8,14},{10,12},{12,10},{14,8},{1,7},{3,5},... | collective-permute-start | bytes 393224 | tf_op jit(solution)/shard_map/ppermute | solution.py:495
  66.1 10.5 %collective-permute-start.11 = (bf16[2,256,128]{2,1,0:T(8,128)(2,1)S(1)}, bf16[2,256,128]{2,1,0:T(8,128)(2,1)S(1)}, u32[]{:S(2)}, u32[]{:S(2)}) collective-permute-start(bf16[2,256,128]{2,1,0:T(8,128)(2,1)S(1)} %get-tuple-element.49), channel_id=1, source_target_pairs={{0,2},{2,0},{4,6},{6,4},{8,10},{10,8},{12,14},{14,12},{1,3},{3,1},... | collective-permute-start | bytes 393224 | tf_op jit(solution)/shard_map/ppermute | solution.py:495
  67.5 9.0 %collective-permute-start.12 = (bf16[2,256,128]{2,1,0:T(8,128)(2,1)S(1)}, bf16[2,256,128]{2,1,0:T(8,128)(2,1)S(1)}, u32[]{:S(2)}, u32[]{:S(2)}) collective-permute-start(bf16[2,256,128]{2,1,0:T(8,128)(2,1)S(1)} %get-tuple-element.50), channel_id=1, source_target_pairs={{0,4},{2,6},{4,0},{6,2},{8,12},{10,14},{12,8},{14,10},{1,5},{3,7},... | collective-permute-start | bytes 393224 | tf_op jit(solution)/shard_map/ppermute | solution.py:495
  69.6 7.0 %collective-permute-start.13 = (bf16[2,256,128]{2,1,0:T(8,128)(2,1)S(1)}, bf16[2,256,128]{2,1,0:T(8,128)(2,1)S(1)}, u32[]{:S(2)}, u32[]{:S(2)}) collective-permute-start(bf16[2,256,128]{2,1,0:T(8,128)(2,1)S(1)} %get-tuple-element.51), channel_id=1, source_target_pairs={{0,6},{2,4},{4,2},{6,0},{8,14},{10,12},{12,10},{14,8},{1,7},{3,5},... | collective-permute-start | bytes 393224 | tf_op jit(solution)/shard_map/ppermute | solution.py:495

commit v16 on v15

--- a/solution.py
+++ b/solution.py
@@ -8,7 +8,7 @@
 from jax.sharding import PartitionSpec as P
 
 VMEM_LIMIT = 12 * 1024 * 1024
-SPLIT = (8, 4, 4)
+SPLIT = (4, 8, 4)
 FIX = 16
 LOG2_E = 1.4426950408889634
 
@@ -495,21 +495,22 @@
         return lax.ppermute(value, "batch", perm=[(i, i ^ r) for i in range(8)])
 
     def cast():
-        rows = per_group * width + tail_lines + 48
+        rows = per_group * width + tail_lines
         rows_a = SPLIT[0] * width + tail_lines
-        count = len(SPLIT) + 2
+        blocks = [(0, SPLIT[0])] + [(at, 4) for at in range(SPLIT[0], per_group, 4)]
+        count = len(blocks) + 2
 
         def kernel(place_ref, *refs):
             ins, outs = refs[: 4 * count], refs[4 * count :]
             for n in range(4):
                 cast_kernel(
-                    len(SPLIT), [tail_lines], reach, lines, *ins[count * n : count * n + count], outs[n]
+                    len(blocks), [tail_lines], reach, lines, *ins[count * n : count * n + count], outs[n]
                 )
                 outs[4 + n // 2][n % 2] = outs[n][:rows_a]
 
         operands, specs = [], []
         for n in range(4):
-            for part, offset in zip(SPLIT, offsets):
+            for offset, part in blocks:
                 operands.append(state)
                 specs.append(
                     pl.BlockSpec(
@@ -665,20 +666,20 @@
         return pick(rows[k], [*inside, crossed], choices, tokens)
 
     parts = [early(0, [own[0], slots])]
-    parts.append(early(1, [parts[0][1]]))
     moves = [(0, n, None, [(n, 1)]) for n in range(2)]
     (spread,) = rearrange(
-        place, crossed_a, moves, [(2, rows[0], size)], [parts[1][1]], "stack_first"
+        place, crossed_a, moves, [(2, rows[0], size)], [parts[0][1]], "stack_first"
     )
     passed = swap(spread, 1)
     sent_b, crossed_b = cross(1, [spread])
+    parts.append(early(1, [sent_b]))
     choices = [(j, chunks[0]) for j in range(4)] + [(4, 0), (6, 0), (5, 0), (6, 1)]
-    states_a = pick(rows[0], [*inside, *crossed_a, passed], choices, [sent_b])
+    states_a = pick(rows[0], [*inside, *crossed_a, passed], choices, [parts[1][1]])
     sent_c, crossed_c = cross(2, [states_a[0], crossed_b])
     states_b = pick_later(1, crossed_b, [sent_c])
-    states_c = pick_later(2, crossed_c, [states_b[0]])
-    result = late(0, states_a, states_a, parts, None, [states_c[0]])
-    result = late(1, states_b, states_a, parts, result, [])
+    result = late(0, states_a, states_a, parts, None, [states_b[0]])
+    states_c = pick_later(2, crossed_c, [stay(result)])
+    result = late(1, states_b, states_a, parts, result, [states_c[0]])
     return late(2, states_c, states_a, parts, result, [])
 
 

time: 79.9 us -> 85.4 us (1.069)
  waiting for transfers between devices: 18 us -> 26.5 us
  starting transfers between devices: 26.2 us -> 23.3 us
    ppermute x17, waiting for transfers between devices: 18 us -> 26.5 us  [swap(): return lax.ppermute(value, 'batch', perm=[(i, i ^ r) for i in range(8)])]
    ppermute x17, starting transfers between devices: 26.2 us -> 23.3 us  [swap(): return lax.ppermute(value, 'batch', perm=[(i, i ^ r) for i in range(8)])]
  transfers between devices with their start and end apart: 17 -> 17, of which waited for: 4 -> 6; matrix products, arithmetic and copies ran while one was open for 1% -> 1% of each run, Pallas kernels for 37% -> 35%
where the time goes in v16:
time: 85.4 us; the launch traced here: 85.2 us
  Pallas kernels  34.3 us (40%)
  waiting for transfers between devices  26.5 us (31%)
  starting transfers between devices  23.3 us (27%)
    ppermute x17, waiting for transfers between devices, swap(): return lax.ppermute(value, 'batch', perm=[(i, i ^ r) for i in range(8)])  26.5 us
    ppermute x17, starting transfers between devices, swap(): return lax.ppermute(value, 'batch', perm=[(i, i ^ r) for i in range(8)])  23.3 us
    pallas_call x2, Pallas kernels, early(): pl.pallas_call(functools.partial(drop_tokens, early_kernel, len(operands)...  19.3 us
    pallas_call x3, Pallas kernels, late(): pl.pallas_call(functools.partial(drop_tokens, kernel, keep, 1 + len(opera...  9.71 us
    pallas_call x6, Pallas kernels, rearrange(): pl.pallas_call(functools.partial(drop_tokens, kernel, 1 + len(sources), l...  3.44 us
    pallas_call x1, Pallas kernels, cast(): pl.pallas_call(kernel, grid_spec=pltpu.PrefetchScalarGridSpec(num_scalar_...  1.86 us
  transfers between devices with their start and end apart: 17, of which 6 were waited for; matrix products, arithmetic and copies ran while one was open for 1% of the time, Pallas kernels for 35%

profile of v16, /device:TPU:0, one launch (start us, length us, event | category | flops | bytes accessed | tf_op | source)
XLA Modules:
  0.0 85.2 jit_solution(7041411945071944860)
XLA Ops:
  0.0 1.9 %cast_states.1 = (bf16[1056,128]{1,0:T(8,128)(2,1)S(1)}, bf16[1056,128]{1,0:T(8,128)(2,1)S(1)}, bf16[1056,128]{1,0:T(8,128)(2,1)S(1)}, bf16[1056,128]{1,0:T(8,12...) custom-call(s32[1]{0:T(128)} %bitcast.place_ref.refs_0_, f32[4,16,64,128]{3,2,1,0:T(8,128)} %bitcast.5, ...), custom_call_target="tpu_custom_call" | custom-call | flops 1 | bytes 1 | tf_op jit(solution)/shard_map/cast_states/pallas_call | solution.py:527
  1.9 3.0 %collective-permute-start = (bf16[1056,128]{1,0:T(8,128)(2,1)S(1)}, bf16[1056,128]{1,0:T(8,128)(2,1)S(1)}, u32[]{:S(2)}, u32[]{:S(2)}) collective-permute-start(bf16[1056,128]{1,0:T(8,128)(2,1)S(1)} %get-tuple-element.36), channel_id=1, source_target_pairs={{0,2},{2,0},{4,6},{6,4},{8,10},{10,8},{12,14},{14,12},{1,3},{3,1},... | collective-permute-start | bytes 811016 | tf_op jit(solution)/shard_map/ppermute | solution.py:495
  4.9 1.6 %collective-permute-start.1 = (bf16[1056,128]{1,0:T(8,128)(2,1)S(1)}, bf16[1056,128]{1,0:T(8,128)(2,1)S(1)}, u32[]{:S(2)}, u32[]{:S(2)}) collective-permute-start(bf16[1056,128]{1,0:T(8,128)(2,1)S(1)} %get-tuple-element.37), channel_id=1, source_target_pairs={{0,4},{2,6},{4,0},{6,2},{8,12},{10,14},{12,8},{14,10},{1,5},{3,7},... | collective-permute-start | bytes 811016 | tf_op jit(solution)/shard_map/ppermute | solution.py:495
  6.5 0.0 collective-permute-start.2
  6.5 3.0 %collective-permute-start.3 = (bf16[2,288,128]{2,1,0:T(8,128)(2,1)S(1)}, bf16[2,288,128]{2,1,0:T(8,128)(2,1)S(1)}, u32[]{:S(2)}, u32[]{:S(2)}) collective-permute-start(bf16[2,288,128]{2,1,0:T(8,128)(2,1)S(1)} %get-tuple-element.39), channel_id=1, source_target_pairs={{0,8},{2,10},{4,12},{6,14},{8,0},{10,2},{12,4},{14,6},{1,9},{3,11}... | collective-permute-start | bytes 442376 | tf_op jit(solution)/shard_map/ppermute | solution.py:495
  9.5 1.3 %collective-permute-start.4 = (bf16[2,288,128]{2,1,0:T(8,128)(2,1)S(1)}, bf16[2,288,128]{2,1,0:T(8,128)(2,1)S(1)}, u32[]{:S(2)}, u32[]{:S(2)}) collective-permute-start(bf16[2,288,128]{2,1,0:T(8,128)(2,1)S(1)} %get-tuple-element.40), channel_id=1, source_target_pairs={{0,12},{2,14},{4,8},{6,10},{8,4},{10,6},{12,0},{14,2},{1,13},{3,15... | collective-permute-start | bytes 442376 | tf_op jit(solution)/shard_map/ppermute | solution.py:495
  10.8 0.1 select_reduce_fusion.1
  11.0 0.1 convert_reduce_fusion
  11.0 0.2 select_reduce_fusion
  11.2 0.1 copy.21.refs_4_
  11.3 0.1 copy.22.refs_5_
  11.4 0.1 broadcast_in_dim.53
  11.5 0.1 broadcast_in_dim_reshape.3.refs_6_
  11.6 9.6 %early.2 = (f32[4,256,1024]{2,1,0:T(8,128)S(1)}, bf16[4,256,128]{2,1,0:T(8,128)(2,1)S(1)}, f32[4,16,256]{2,1,0:T(8,128)S(1)}, f32[4,256,256]{2,1,0:T(8,128)S(1)}...) custom-call(bf16[2,256,4096]{2,1,0:T(8,128)(2,1)} %refs_0_.3, bf16[2,256,512]{2,1,0:T(8,128)(2,1)} %refs_1_.3, ...), custom_call_target="tpu_custom_call" | custom-call | flops 1 | bytes 1 | tf_op jit(solution)/shard_map/early/pallas_call | solution.py:588
  21.3 1.1 %collective-permute-done.3.refs_1_.refs_5_ = bf16[2,288,128]{2,1,0:T(8,128)(2,1)S(1)} collective-permute-done((bf16[2,288,128]{2,1,0:T(8,128)(2,1)S(1)}, bf16[2,288,128]{2,1,0:T(8,128)(2,1)S(1)}, u32[]{:S(2)}, u32[]{:S(2)}) %collective-permute-start.3) | collective-permute-done | bytes 147488 | tf_op jit(solution)/shard_map/ppermute | solution.py:495
  22.4 4.6 %collective-permute-done.4.refs_2_.refs_6_ = bf16[2,288,128]{2,1,0:T(8,128)(2,1)S(1)} collective-permute-done((bf16[2,288,128]{2,1,0:T(8,128)(2,1)S(1)}, bf16[2,288,128]{2,1,0:T(8,128)(2,1)S(1)}, u32[]{:S(2)}, u32[]{:S(2)}) %collective-permute-start.4) | collective-permute-done | bytes 147488 | tf_op jit(solution)/shard_map/ppermute | solution.py:495
  27.0 0.0 collective-permute-done.refs_2_
  27.0 0.0 collective-permute-done.1.refs_3_
  27.0 0.0 collective-permute-done.2.refs_4_
  27.1 0.1 collective-permute-start.9
  27.2 0.6 collective-permute-start.5
  27.7 9.6 %early.3 = (f32[4,256,1024]{2,1,0:T(8,128)S(1)}, bf16[4,256,128]{2,1,0:T(8,128)(2,1)S(1)}, f32[4,16,256]{2,1,0:T(8,128)S(1)}, f32[4,256,256]{2,1,0:T(8,128)S(1)}...) custom-call(bf16[2,256,4096]{2,1,0:T(8,128)(2,1)} %refs_0_.3, bf16[2,256,512]{2,1,0:T(8,128)(2,1)} %refs_1_.3, ...), custom_call_target="tpu_custom_call" | custom-call | flops 1 | bytes 1 | tf_op jit(solution)/shard_map/early/pallas_call | solution.py:588
  37.4 0.0 collective-permute-done.5.refs_7_
  37.4 1.1 %pick_states.3 = (bf16[2,288,128]{2,1,0:T(8,128)(2,1)S(1)}, bf16[2,288,128]{2,1,0:T(8,128)(2,1)S(1)}, bf16[2,288,128]{2,1,0:T(8,128)(2,1)S(1)}, bf16[2,288,128]{2,1,0:T(8,128)(2,1)S(1)}) custom-call(s32[8]{0:T(128)S(1)} %broadcast_xor_fusion.refs_10_.refs_0_, bf16[1056,128]{1,0:T(8,128)(2,1)S(1)} %get-tuple-element.35.refs_9_.refs_1_, ...), custom_call_target="tpu_custom_call" | custom-call | flops 1 | bytes 1 | tf_op jit(solution)/shard_map/pick_states/pallas_call | solution.py:559
  38.5 1.6 %collective-permute-start.6 = (bf16[2,288,128]{2,1,0:T(8,128)(2,1)S(1)}, bf16[2,288,128]{2,1,0:T(8,128)(2,1)S(1)}, u32[]{:S(2)}, u32[]{:S(2)}) collective-permute-start(bf16[2,288,128]{2,1,0:T(8,128)(2,1)S(1)} %get-tuple-element.44), channel_id=1, source_target_pairs={{0,2},{2,0},{4,6},{6,4},{8,10},{10,8},{12,14},{14,12},{1,3},{3,1},... | collective-permute-start | bytes 442376 | tf_op jit(solution)/shard_map/ppermute | solution.py:495
  40.0 2.0 %collective-permute-start.7 = (bf16[2,288,128]{2,1,0:T(8,128)(2,1)S(1)}, bf16[2,288,128]{2,1,0:T(8,128)(2,1)S(1)}, u32[]{:S(2)}, u32[]{:S(2)}) collective-permute-start(bf16[2,288,128]{2,1,0:T(8,128)(2,1)S(1)} %get-tuple-element.45), channel_id=1, source_target_pairs={{0,4},{2,6},{4,0},{6,2},{8,12},{10,14},{12,8},{14,10},{1,5},{3,7},... | collective-permute-start | bytes 442376 | tf_op jit(solution)/shard_map/ppermute | solution.py:495
  42.0 8.6 %collective-permute-done.9.refs_6_.refs_5_ = bf16[4,512,128]{2,1,0:T(8,128)(2,1)S(1)} collective-permute-done((bf16[4,512,128]{2,1,0:T(8,128)(2,1)S(1)}, bf16[4,512,128]{2,1,0:T(8,128)(2,1)S(1)}, u32[]{:S(2)}, u32[]{:S(2)}) %collective-permute-start.9) | collective-permute-done | bytes 524320 | tf_op jit(solution)/shard_map/ppermute | solution.py:495
  50.6 0.1 collective-permute-start.10
  50.7 1.1 %pick_states.4 = (bf16[2,512,128]{2,1,0:T(8,128)(2,1)S(1)}, bf16[2,512,128]{2,1,0:T(8,128)(2,1)S(1)}, bf16[2,512,128]{2,1,0:T(8,128)(2,1)S(1)}, bf16[2,512,128]{2,1,0:T(8,128)(2,1)S(1)}) custom-call(s32[8]{0:T(128)S(1)} %broadcast_xor_fusion.refs_10_.refs_0_, bf16[1056,128]{1,0:T(8,128)(2,1)S(1)} %get-tuple-element.35.refs_9_.refs_1_, ...), custom_call_target="tpu_custom_call" | custom-call | flops 1 | bytes 1 | tf_op jit(solution)/shard_map/pick_states/pallas_call | solution.py:559
  51.8 0.6 collective-permute-start.14
  52.3 4.0 %collective-permute-start.8 = (bf16[2,288,128]{2,1,0:T(8,128)(2,1)S(1)}, bf16[2,288,128]{2,1,0:T(8,128)(2,1)S(1)}, u32[]{:S(2)}, u32[]{:S(2)}) collective-permute-start(bf16[2,288,128]{2,1,0:T(8,128)(2,1)S(1)} %get-tuple-element.46), channel_id=1, source_target_pairs={{0,6},{2,4},{4,2},{6,0},{8,14},{10,12},{12,10},{14,8},{1,7},{3,5},... | collective-permute-start | bytes 442376 | tf_op jit(solution)/shard_map/ppermute | solution.py:495
  56.3 0.0 collective-permute-done.6.refs_2_.refs_6_
  56.3 0.0 collective-permute-start.15
  56.3 0.0 collective-permute-done.7.refs_3_.refs_7_
  56.3 2.0 %collective-permute-start.16 = (bf16[2,512,128]{2,1,0:T(8,128)(2,1)S(1)}, bf16[2,512,128]{2,1,0:T(8,128)(2,1)S(1)}, u32[]{:S(2)}, u32[]{:S(2)}) collective-permute-start(bf16[2,512,128]{2,1,0:T(8,128)(2,1)S(1)} %get-tuple-element.64), channel_id=1, source_target_pairs={{0,6},{2,4},{4,2},{6,0},{8,14},{10,12},{12,10},{14,8},{1,7},{3,5},... | collective-permute-start | bytes 786440 | tf_op jit(solution)/shard_map/ppermute | solution.py:495
  58.3 8.3 %collective-permute-done.8.refs_4_.refs_8_ = bf16[2,288,128]{2,1,0:T(8,128)(2,1)S(1)} collective-permute-done((bf16[2,288,128]{2,1,0:T(8,128)(2,1)S(1)}, bf16[2,288,128]{2,1,0:T(8,128)(2,1)S(1)}, u32[]{:S(2)}, u32[]{:S(2)}) %collective-permute-start.8) | collective-permute-done | bytes 147488 | tf_op jit(solution)/shard_map/ppermute | solution.py:495
  66.6 2.9 %late.3.refs_6_.refs_22_ = bf16[2,256,4096]{2,1,0:T(8,128)(2,1)} custom-call(s32[1]{0:T(128)} %bitcast.place_ref.refs_0_, bf16[2,288,128]{2,1,0:T(8,128)(2,1)S(1)} %get-tuple-element.43.refs_5_.refs_1_, bf16[2,288,128]{2,1,0:T(8,128)(2,1)S(1)} %collective-permute-done.6.refs_2_.refs_6_, bf16[2,288,128]{2,1,0:T(8,128)(2,1)S(1)} %collective-permute-done.7.refs_3_.refs_7_, ...), custom_call_target="tpu_custom_call" | custom-call | flops 1 | bytes 1 | tf_op jit(solution)/shard_map/late/pallas_call | solution.py:632
  69.4 0.0 collective-permute-done.10.refs_5_
  69.5 1.2 %pick_states.5 = (bf16[2,256,128]{2,1,0:T(8,128)(2,1)S(1)}, bf16[2,256,128]{2,1,0:T(8,128)(2,1)S(1)}, bf16[2,256,128]{2,1,0:T(8,128)(2,1)S(1)}, bf16[2,256,128]{2,1,0:T(8,128)(2,1)S(1)}) custom-call(s32[8]{0:T(128)S(1)} %broadcast_xor_fusion.refs_10_.refs_0_, bf16[1056,128]{1,0:T(8,128)(2,1)S(1)} %get-tuple-element.35.refs_9_.refs_1_, ...), custom_call_target="tpu_custom_call" | custom-call | flops 1 | bytes 1 | tf_op jit(solution)/shard_map/pick_states/pallas_call | solution.py:559
  70.7 0.1 collective-permute-start.11
  70.8 0.1 collective-permute-start.12
  70.9 0.0 collective-permute-done.14.refs_6_
  70.9 3.4 %collective-permute-start.13 = (bf16[2,256,128]{2,1,0:T(8,128)(2,1)S(1)}, bf16[2,256,128]{2,1,0:T(8,128)(2,1)S(1)}, u32[]{:S(2)}, u32[]{:S(2)}) collective-permute-start(bf16[2,256,128]{2,1,0:T(8,128)(2,1)S(1)} %get-tuple-element.61), channel_id=1, source_target_pairs={{0,6},{2,4},{4,2},{6,0},{8,14},{10,12},{12,10},{14,8},{1,7},{3,5},... | collective-permute-start | bytes 393224 | tf_op jit(solution)/shard_map/ppermute | solution.py:495
  74.3 0.0 collective-permute-done.15.refs_7_
  74.3 3.5 %collective-permute-done.16.refs_8_ = bf16[2,512,128]{2,1,0:T(8,128)(2,1)S(1)} collective-permute-done((bf16[2,512,128]{2,1,0:T(8,128)(2,1)S(1)}, bf16[2,512,128]{2,1,0:T(8,128)(2,1)S(1)}, u32[]{:S(2)}, u32[]{:S(2)}) %collective-permute-start.16) | collective-permute-done | bytes 262176 | tf_op jit(solution)/shard_map/ppermute | solution.py:495
  77.8 3.9 %late.4.refs_21_ = bf16[2,256,4096]{2,1,0:T(8,128)(2,1)} custom-call(s32[1]{0:T(128)} %bitcast.place_ref.refs_0_, bf16[2,288,128]{2,1,0:T(8,128)(2,1)S(1)} %get-tuple-element.43.refs_5_.refs_1_, bf16[2,288,128]{2,1,0:T(8,128)(2,1)S(1)} %collective-permute-done.6.refs_2_.refs_6_, ...), custom_call_target="tpu_custom_call", output_to_operand_aliasing={{}: (22, {})} | custom-call | flops 1 | bytes 1 | tf_op jit(solution)/shard_map/late/pallas_call | solution.py:632
  81.8 0.4 collective-permute-done.13.refs_8_
  82.1 2.9 %late.5 = bf16[2,256,4096]{2,1,0:T(8,128)(2,1)} custom-call(s32[1]{0:T(128)} %bitcast.place_ref.refs_0_, bf16[2,288,128]{2,1,0:T(8,128)(2,1)S(1)} %get-tuple-element.43.refs_5_.refs_1_, bf16[2,288,128]{2,1,0:T(8,128)(2,1)S(1)} %collective-permute-done.6.refs_2_.refs_6_, ...), custom_call_target="tpu_custom_call", output_to_operand_aliasing={{}: (21, {})} | custom-call | flops 1 | bytes 1 | tf_op jit(solution)/shard_map/late/pallas_call | solution.py:632
  (17 shorter events, 0.1 us)
Async XLA Ops:
  0.0 10.8 %copy-start.3 = (s32[8]{0:T(128)S(1)}, s32[8]{0:T(128)}, u32[]{:S(2)}) copy-start(s32[8]{0:T(128)} %param.26) | copy-start | bytes 100
  0.0 10.9 %copy-start.4 = (s32[16]{0:T(128)S(1)}, s32[16]{0:T(128)}, u32[]{:S(2)}) copy-start(s32[16]{0:T(128)} %param.27) | copy-start | bytes 196
  0.0 11.2 %copy-start = (f32[64]{0:T(128)S(1)}, f32[64]{0:T(128)}, u32[]{:S(2)}) copy-start(f32[64]{0:T(128)} %param.18) | copy-start | bytes 772
  0.0 11.3 %copy-start.1 = (f32[64]{0:T(128)S(1)}, f32[64]{0:T(128)}, u32[]{:S(2)}) copy-start(f32[64]{0:T(128)} %param.19) | copy-start | bytes 772
  0.0 11.4 %copy-start.2 = (f32[64]{0:T(128)S(1)}, f32[64]{0:T(128)}, u32[]{:S(2)}) copy-start(f32[64]{0:T(128)} %param.20) | copy-start | bytes 772
  1.9 25.1 %collective-permute-start = (bf16[1056,128]{1,0:T(8,128)(2,1)S(1)}, bf16[1056,128]{1,0:T(8,128)(2,1)S(1)}, u32[]{:S(2)}, u32[]{:S(2)}) collective-permute-start(bf16[1056,128]{1,0:T(8,128)(2,1)S(1)} %get-tuple-element.36), channel_id=1, source_target_pairs={{0,2},{2,0},{4,6},{6,4},{8,10},{10,8},{12,14},{14,12},{1,3},{3,1},... | collective-permute-start | bytes 811016 | tf_op jit(solution)/shard_map/ppermute | solution.py:495
  4.9 22.1 %collective-permute-start.1 = (bf16[1056,128]{1,0:T(8,128)(2,1)S(1)}, bf16[1056,128]{1,0:T(8,128)(2,1)S(1)}, u32[]{:S(2)}, u32[]{:S(2)}) collective-permute-start(bf16[1056,128]{1,0:T(8,128)(2,1)S(1)} %get-tuple-element.37), channel_id=1, source_target_pairs={{0,4},{2,6},{4,0},{6,2},{8,12},{10,14},{12,8},{14,10},{1,5},{3,7},... | collective-permute-start | bytes 811016 | tf_op jit(solution)/shard_map/ppermute | solution.py:495
  6.5 20.5 %collective-permute-start.2 = (bf16[1056,128]{1,0:T(8,128)(2,1)S(1)}, bf16[1056,128]{1,0:T(8,128)(2,1)S(1)}, u32[]{:S(2)}, u32[]{:S(2)}) collective-permute-start(bf16[1056,128]{1,0:T(8,128)(2,1)S(1)} %get-tuple-element.38), channel_id=1, source_target_pairs={{0,6},{2,4},{4,2},{6,0},{8,14},{10,12},{12,10},{14,8},{1,7},{3,5},... | collective-permute-start | bytes 811016 | tf_op jit(solution)/shard_map/ppermute | solution.py:495
  6.5 15.9 %collective-permute-start.3 = (bf16[2,288,128]{2,1,0:T(8,128)(2,1)S(1)}, bf16[2,288,128]{2,1,0:T(8,128)(2,1)S(1)}, u32[]{:S(2)}, u32[]{:S(2)}) collective-permute-start(bf16[2,288,128]{2,1,0:T(8,128)(2,1)S(1)} %get-tuple-element.39), channel_id=1, source_target_pairs={{0,8},{2,10},{4,12},{6,14},{8,0},{10,2},{12,4},{14,6},{1,9},{3,11}... | collective-permute-start | bytes 442376 | tf_op jit(solution)/shard_map/ppermute | solution.py:495
  9.5 17.5 %collective-permute-start.4 = (bf16[2,288,128]{2,1,0:T(8,128)(2,1)S(1)}, bf16[2,288,128]{2,1,0:T(8,128)(2,1)S(1)}, u32[]{:S(2)}, u32[]{:S(2)}) collective-permute-start(bf16[2,288,128]{2,1,0:T(8,128)(2,1)S(1)} %get-tuple-element.40), channel_id=1, source_target_pairs={{0,12},{2,14},{4,8},{6,10},{8,4},{10,6},{12,0},{14,2},{1,13},{3,15... | collective-permute-start | bytes 442376 | tf_op jit(solution)/shard_map/ppermute | solution.py:495
  27.1 23.5 %collective-permute-start.9 = (bf16[4,512,128]{2,1,0:T(8,128)(2,1)S(1)}, bf16[4,512,128]{2,1,0:T(8,128)(2,1)S(1)}, u32[]{:S(2)}, u32[]{:S(2)}) collective-permute-start(bf16[4,512,128]{2,1,0:T(8,128)(2,1)S(1)} %stack_later.2.refs_9_), channel_id=1, source_target_pairs={{0,8},{2,10},{4,12},{6,14},{8,0},{10,2},{12,4},{14,6},{1,9},{3,11}... | collective-permute-start | bytes 1572872 | tf_op jit(solution)/shard_map/ppermute | solution.py:495
  27.2 10.2 %collective-permute-start.5 = (bf16[2,288,128]{2,1,0:T(8,128)(2,1)S(1)}, bf16[2,288,128]{2,1,0:T(8,128)(2,1)S(1)}, u32[]{:S(2)}, u32[]{:S(2)}) collective-permute-start(bf16[2,288,128]{2,1,0:T(8,128)(2,1)S(1)} %stack_first.1.refs_5_), channel_id=1, source_target_pairs={{0,2},{2,0},{4,6},{6,4},{8,10},{10,8},{12,14},{14,12},{1,3},{3,1},... | collective-permute-start | bytes 442376 | tf_op jit(solution)/shard_map/ppermute | solution.py:495
  38.5 17.9 %collective-permute-start.6 = (bf16[2,288,128]{2,1,0:T(8,128)(2,1)S(1)}, bf16[2,288,128]{2,1,0:T(8,128)(2,1)S(1)}, u32[]{:S(2)}, u32[]{:S(2)}) collective-permute-start(bf16[2,288,128]{2,1,0:T(8,128)(2,1)S(1)} %get-tuple-element.44), channel_id=1, source_target_pairs={{0,2},{2,0},{4,6},{6,4},{8,10},{10,8},{12,14},{14,12},{1,3},{3,1},... | collective-permute-start | bytes 442376 | tf_op jit(solution)/shard_map/ppermute | solution.py:495
  40.0 16.3 %collective-permute-start.7 = (bf16[2,288,128]{2,1,0:T(8,128)(2,1)S(1)}, bf16[2,288,128]{2,1,0:T(8,128)(2,1)S(1)}, u32[]{:S(2)}, u32[]{:S(2)}) collective-permute-start(bf16[2,288,128]{2,1,0:T(8,128)(2,1)S(1)} %get-tuple-element.45), channel_id=1, source_target_pairs={{0,4},{2,6},{4,0},{6,2},{8,12},{10,14},{12,8},{14,10},{1,5},{3,7},... | collective-permute-start | bytes 442376 | tf_op jit(solution)/shard_map/ppermute | solution.py:495
  50.6 18.9 %collective-permute-start.10 = (bf16[4,256,128]{2,1,0:T(8,128)(2,1)S(1)}, bf16[4,256,128]{2,1,0:T(8,128)(2,1)S(1)}, u32[]{:S(2)}, u32[]{:S(2)}) collective-permute-start(bf16[4,256,128]{2,1,0:T(8,128)(2,1)S(1)} %stack_later.3.refs_6_), channel_id=1, source_target_pairs={{0,8},{2,10},{4,12},{6,14},{8,0},{10,2},{12,4},{14,6},{1,9},{3,11}... | collective-permute-start | bytes 786440 | tf_op jit(solution)/shard_map/ppermute | solution.py:495
  51.8 19.1 %collective-permute-start.14 = (bf16[2,512,128]{2,1,0:T(8,128)(2,1)S(1)}, bf16[2,512,128]{2,1,0:T(8,128)(2,1)S(1)}, u32[]{:S(2)}, u32[]{:S(2)}) collective-permute-start(bf16[2,512,128]{2,1,0:T(8,128)(2,1)S(1)} %get-tuple-element.62), channel_id=1, source_target_pairs={{0,2},{2,0},{4,6},{6,4},{8,10},{10,8},{12,14},{14,12},{1,3},{3,1},... | collective-permute-start | bytes 786440 | tf_op jit(solution)/shard_map/ppermute | solution.py:495
  52.3 14.2 %collective-permute-start.8 = (bf16[2,288,128]{2,1,0:T(8,128)(2,1)S(1)}, bf16[2,288,128]{2,1,0:T(8,128)(2,1)S(1)}, u32[]{:S(2)}, u32[]{:S(2)}) collective-permute-start(bf16[2,288,128]{2,1,0:T(8,128)(2,1)S(1)} %get-tuple-element.46), channel_id=1, source_target_pairs={{0,6},{2,4},{4,2},{6,0},{8,14},{10,12},{12,10},{14,8},{1,7},{3,5},... | collective-permute-start | bytes 442376 | tf_op jit(solution)/shard_map/ppermute | solution.py:495
  56.3 17.9 %collective-permute-start.15 = (bf16[2,512,128]{2,1,0:T(8,128)(2,1)S(1)}, bf16[2,512,128]{2,1,0:T(8,128)(2,1)S(1)}, u32[]{:S(2)}, u32[]{:S(2)}) collective-permute-start(bf16[2,512,128]{2,1,0:T(8,128)(2,1)S(1)} %get-tuple-element.63), channel_id=1, source_target_pairs={{0,4},{2,6},{4,0},{6,2},{8,12},{10,14},{12,8},{14,10},{1,5},{3,7},... | collective-permute-start | bytes 786440 | tf_op jit(solution)/shard_map/ppermute | solution.py:495
  56.3 21.5 %collective-permute-start.16 = (bf16[2,512,128]{2,1,0:T(8,128)(2,1)S(1)}, bf16[2,512,128]{2,1,0:T(8,128)(2,1)S(1)}, u32[]{:S(2)}, u32[]{:S(2)}) collective-permute-start(bf16[2,512,128]{2,1,0:T(8,128)(2,1)S(1)} %get-tuple-element.64), channel_id=1, source_target_pairs={{0,6},{2,4},{4,2},{6,0},{8,14},{10,12},{12,10},{14,8},{1,7},{3,5},... | collective-permute-start | bytes 786440 | tf_op jit(solution)/shard_map/ppermute | solution.py:495
  70.7 11.0 %collective-permute-start.11 = (bf16[2,256,128]{2,1,0:T(8,128)(2,1)S(1)}, bf16[2,256,128]{2,1,0:T(8,128)(2,1)S(1)}, u32[]{:S(2)}, u32[]{:S(2)}) collective-permute-start(bf16[2,256,128]{2,1,0:T(8,128)(2,1)S(1)} %get-tuple-element.59), channel_id=1, source_target_pairs={{0,2},{2,0},{4,6},{6,4},{8,10},{10,8},{12,14},{14,12},{1,3},{3,1},... | collective-permute-start | bytes 393224 | tf_op jit(solution)/shard_map/ppermute | solution.py:495
  70.8 11.0 %collective-permute-start.12 = (bf16[2,256,128]{2,1,0:T(8,128)(2,1)S(1)}, bf16[2,256,128]{2,1,0:T(8,128)(2,1)S(1)}, u32[]{:S(2)}, u32[]{:S(2)}) collective-permute-start(bf16[2,256,128]{2,1,0:T(8,128)(2,1)S(1)} %get-tuple-element.60), channel_id=1, source_target_pairs={{0,4},{2,6},{4,0},{6,2},{8,12},{10,14},{12,8},{14,10},{1,5},{3,7},... | collective-permute-start | bytes 393224 | tf_op jit(solution)/shard_map/ppermute | solution.py:495
  70.9 11.3 %collective-permute-start.13 = (bf16[2,256,128]{2,1,0:T(8,128)(2,1)S(1)}, bf16[2,256,128]{2,1,0:T(8,128)(2,1)S(1)}, u32[]{:S(2)}, u32[]{:S(2)}) collective-permute-start(bf16[2,256,128]{2,1,0:T(8,128)(2,1)S(1)} %get-tuple-element.61), channel_id=1, source_target_pairs={{0,6},{2,4},{4,2},{6,0},{8,14},{10,12},{12,10},{14,8},{1,7},{3,5},... | collective-permute-start | bytes 393224 | tf_op jit(solution)/shard_map/ppermute | solution.py:495

commit v17 on v14

--- a/solution.py
+++ b/solution.py
@@ -123,10 +123,13 @@
 
 
 def late_kernel(offset, heads, lines, reach, tail_at, place_ref, *refs):
-    tails, states, parts = refs[:4], refs[4:8], refs[8:-4]
+    count = len(heads)
+    tails, states, parts = refs[:4], refs[4 : 4 + 4 * count], refs[4 + 4 * count : -4]
     y_ref, padded, y_part, sems = refs[-4:]
     _, kids, length, wide = y_part.shape
+    rows, heads = heads, sum(heads)
     width = wide // heads
+    rows = [part * width for part in rows]
     low_first = lax.broadcasted_iota(jnp.int32, (FIX, 2 * width), 1) < width
     contract = (((1,), (1,)), ((), ()))
 
@@ -140,7 +143,7 @@
         group_wide = opening_ref.shape[2] - 2 * size
         tail_rows = pl.ds(tail_at, -(-lines * reach // 16) * 16)
         tail = tails[j][kid, tail_rows].astype(jnp.float32)
-        state = states[j][kid, : heads * width]
+        state = jnp.concatenate([states[4 * n + j][kid, : rows[n]] for n in range(count)])
 
         def opening(start, stop, at):
             tap_rows = []
@@ -497,19 +500,21 @@
     def cast():
         rows = per_group * width + tail_lines
         rows_a = SPLIT[0] * width + tail_lines
-        count = len(SPLIT) + 2
+        blocks = [(0, SPLIT[0])] + [(at, 4) for at in range(SPLIT[0], per_group, 4)]
+        count = len(blocks) + 2
 
         def kernel(place_ref, *refs):
             ins, outs = refs[: 4 * count], refs[4 * count :]
-            for n in range(4):
+            quarters = [outs[0], outs[2].at[0], outs[1], outs[2].at[1]]
+            for n, out_ref in enumerate(quarters):
                 cast_kernel(
-                    len(SPLIT), [tail_lines], reach, lines, *ins[count * n : count * n + count], outs[n]
+                    len(blocks), [tail_lines], reach, lines, *ins[count * n : count * n + count], out_ref
                 )
-                outs[4 + n // 2][n % 2] = outs[n][:rows_a]
+                outs[3 + n // 2][n % 2] = out_ref[:rows_a]
 
         operands, specs = [], []
         for n in range(4):
-            for part, offset in zip(SPLIT, offsets):
+            for offset, part in blocks:
                 operands.append(state)
                 specs.append(
                     pl.BlockSpec(
@@ -522,7 +527,7 @@
                 pl.BlockSpec((1, reach, wide), lambda i, p, n=n: (0, 0, p[0] ^ n)),
                 pl.BlockSpec((1, reach, 2, size), lambda i, p, n=n: (0, 0, 0, p[0] ^ n)),
             ]
-        shapes = [(rows, size)] * 4 + [(2, rows_a, size)] * 2
+        shapes = [(rows, size)] * 2 + [(2, rows, size)] + [(2, rows_a, size)] * 2
         return pl.pallas_call(
             kernel,
             grid_spec=pltpu.PrefetchScalarGridSpec(
@@ -579,8 +584,8 @@
         )
         return [picked[0]] + [swap(picked[j], j) for j in range(1, 4)]
 
-    def early(c, piece, before, tokens):
-        per = groups // 2
+    def early(c, pieces, piece, before, tokens):
+        per = groups // pieces
         at = lambda q: (c, 0, per * piece + q)
         operands = [
             x_in, b_in, c_in, dt_in, dt_bias[:, None], a_log[:, None], skip_row, conv_x, conv_bc
@@ -621,10 +626,10 @@
             name="early",
         )(*operands, *tokens)
 
-    def late(k, states, states_first, parts, result, tokens):
-        part, offset = SPLIT[k], offsets[k]
-        chunk = part * width
-        operands = [keep_in_vmem(a) for a in (*states_first, *states, *parts[0], *parts[1])]
+    def late(ks, states, parts, result, tokens):
+        offset = offsets[ks[0]]
+        chunk = sum(SPLIT[k] for k in ks) * width
+        operands = [keep_in_vmem(a) for a in (*states[0], *sum((states[k] for k in ks), []), *parts[0], *parts[1])]
         specs = [pl.BlockSpec(memory_space=pltpu.VMEM)] * len(operands)
         keep = 1 + len(operands)
         operands += tokens
@@ -634,7 +639,9 @@
             alias = {1 + len(operands): 0}
             operands.append(result)
             specs.append(anywhere)
-        kernel = functools.partial(late_kernel, offset, part, lines, reach, SPLIT[0] * width)
+        kernel = functools.partial(
+            late_kernel, offset, [SPLIT[k] for k in ks], lines, reach, SPLIT[0] * width
+        )
         return pl.pallas_call(
             functools.partial(drop_tokens, kernel, keep, 1 + len(operands) - keep),
             grid_spec=pltpu.PrefetchScalarGridSpec(
@@ -658,36 +665,43 @@
     skip_row = jnp.repeat(d_skip, width)[None, :]
     rows = [SPLIT[0] * width + tail_lines] + [part * width for part in SPLIT[1:]]
     chunks = [pl.ds(sum(rows[:k]), rows[k]) for k in range(len(SPLIT))]
-    *own, sent_4, sent_6 = cast()
+    own, own_2, own_13, sent_4, sent_6 = cast()
     crossed_a = [swap(sent_4, 4), swap(sent_6, 6)]
-    inside = [own[0]] + [swap(own[j], j) for j in range(1, 4)]
+    along_y, along_z = swap(own_13, 1), swap(own_2, 2)
+    parts = [early(0, 1, 0, [], [own, slots])]
+    (turn,) = rearrange(
+        place, [along_y], [(0, None, None, [(0, 1)])], [own.shape], [parts[0][1]], "stack_turn"
+    )
+    inside = [own, along_y, along_z, swap(turn, 2)]
+
+    def inside_rows(k):
+        return [(0, chunks[k]), (1, (0, chunks[k])), (2, chunks[k]), (3, chunks[k])]
 
     def cross(k, tokens):
-        moves = [(0, j, None, [(j, chunks[k])]) for j in range(4)]
+        moves = [(0, j, None, [choice]) for j, choice in enumerate(inside_rows(k))]
         (sent,) = rearrange(place, inside, moves, [(4, rows[k], size)], tokens, "stack_later")
         return sent, swap(sent, 4)
 
     def pick_later(k, crossed, tokens):
-        choices = [(j, chunks[k]) for j in range(4)] + [(4, j) for j in range(4)]
+        choices = inside_rows(k) + [(4, j) for j in range(4)]
         return pick(rows[k], [*inside, crossed], choices, tokens)
 
-    first = early(0, 0, [], [own[0], slots])
-    first = early(0, 1, first, [])
-    second = early(1, 0, [], [first[1]])
-    sent_b, crossed_b = cross(1, [second[1], *crossed_a])
+    second = early(1, 2, 0, [], [turn])
     moves = [(0, n, None, [(n, 1)]) for n in range(2)]
-    (spread,) = rearrange(place, crossed_a, moves, [(2, rows[0], size)], [sent_b], "stack_first")
+    (spread,) = rearrange(
+        place, crossed_a, moves, [(2, rows[0], size)], [second[1]], "stack_first"
+    )
     passed = swap(spread, 1)
-    choices = [(j, chunks[0]) for j in range(4)] + [(4, 0), (6, 0), (5, 0), (6, 1)]
-    states_a = pick(rows[0], [*inside, *crossed_a, passed], choices, [])
-    sent_c, crossed_c = cross(2, [states_a[0], crossed_b])
-    states_b = pick_later(1, crossed_b, [sent_c])
-    second = early(1, 1, second, [states_b[0]])
-    parts = [first, second]
-    result = late(0, states_a, states_a, parts, None, [states_b[0]])
-    states_c = pick_later(2, crossed_c, [stay(result)])
-    result = late(1, states_b, states_a, parts, result, [states_c[0]])
-    return late(2, states_c, states_a, parts, result, [])
+    sent_b, crossed_b = cross(1, [spread])
+    second = early(1, 2, 1, second, [sent_b])
+    parts.append(second)
+    choices = inside_rows(0) + [(4, 0), (6, 0), (5, 0), (6, 1)]
+    states = [pick(rows[0], [*inside, *crossed_a, passed], choices, [second[1]])]
+    sent_c, crossed_c = cross(2, [states[0][0], crossed_b])
+    states.append(pick_later(1, crossed_b, [sent_c]))
+    states.append(pick_later(2, crossed_c, [states[1][0]]))
+    result = late([0, 1], states, parts, None, [states[2][0]])
+    return late([2], states, parts, result, [])
 
 
 def solution(mesh):

time: 82.8 us -> 79.4 us (0.959)
  waiting for transfers between devices: 19.9 us -> 17 us
  Pallas kernels: 36.5 us -> 34.3 us
  starting transfers between devices: 25.1 us -> 26.8 us
    ppermute x17, waiting for transfers between devices: 19.9 us -> 17 us  [swap(): return lax.ppermute(value, 'batch', perm=[(i, i ^ r) for i in range(8)])]
    ppermute x17, starting transfers between devices: 25.1 us -> 26.8 us  [swap(): return lax.ppermute(value, 'batch', perm=[(i, i ^ r) for i in range(8)])]
    pallas_call x4 -> x3, Pallas kernels: 21.5 us -> 20.4 us  [early(): pl.pallas_call(functools.partial(drop_tokens, functools.partial(early_ker...]
    pallas_call x3 -> x2, Pallas kernels: 9.74 us -> 8.65 us  [late(): pl.pallas_call(functools.partial(drop_tokens, kernel, keep, 1 + len(opera...]
    pallas_call x6 -> x7, Pallas kernels: 3.43 us -> 3.45 us  [rearrange(): pl.pallas_call(functools.partial(drop_tokens, kernel, 1 + len(sources), l...]
  transfers between devices with their start and end apart: 17 -> 17, of which waited for: 6 -> 6; matrix products, arithmetic and copies ran while one was open for 1% -> 1% of each run, Pallas kernels for 38% -> 37%
where the time goes in v17:
time: 79.4 us; the launch traced here: 79.2 us
  Pallas kernels  34.3 us (43%)
  starting transfers between devices  26.8 us (34%)
  waiting for transfers between devices  17 us (21%)
    ppermute x17, starting transfers between devices, swap(): return lax.ppermute(value, 'batch', perm=[(i, i ^ r) for i in range(8)])  26.8 us
    pallas_call x3, Pallas kernels, early(): pl.pallas_call(functools.partial(drop_tokens, functools.partial(early_ker...  20.4 us
    ppermute x17, waiting for transfers between devices, swap(): return lax.ppermute(value, 'batch', perm=[(i, i ^ r) for i in range(8)])  17 us
    pallas_call x2, Pallas kernels, late(): pl.pallas_call(functools.partial(drop_tokens, kernel, keep, 1 + len(opera...  8.65 us
    pallas_call x7, Pallas kernels, rearrange(): pl.pallas_call(functools.partial(drop_tokens, kernel, 1 + len(sources), l...  3.45 us
    pallas_call x1, Pallas kernels, cast(): pl.pallas_call(kernel, grid_spec=pltpu.PrefetchScalarGridSpec(num_scalar_...  1.82 us
  transfers between devices with their start and end apart: 17, of which 6 were waited for; matrix products, arithmetic and copies ran while one was open for 1% of the time, Pallas kernels for 37%

profile of v17, /device:TPU:0, one launch (start us, length us, event | category | flops | bytes accessed | tf_op | source)
XLA Modules:
  0.0 79.2 jit_solution(9175187956363360216)
XLA Ops:
  0.0 1.8 %cast_states.1 = (bf16[1056,128]{1,0:T(8,128)(2,1)S(1)}, bf16[1056,128]{1,0:T(8,128)(2,1)S(1)}, bf16[2,1056,128]{2,1,0:T(8,128)(2,1)S(1)}, bf16[2,544,128]{2,1,0:T(8,128)(2,1)S(1)}, bf16[2,544,128]{2,1,0:T(8,128)(2,1)S(1)}) custom-call(s32[1]{0:T(128)} %bitcast.place_ref.refs_0_, f32[4,16,64,128]{3,2,1,0:T(8,128)} %bitcast.5, f32[4,16,64,128]{3,2,1,0:T(8,128)} %bitcast.6, ...), custom_call_target="tpu_custom_call" | custom-call | flops 1 | bytes 1 | tf_op jit(solution)/shard_map/cast_states/pallas_call | solution.py:531
  1.8 3.1 %collective-permute-start.1 = (bf16[1056,128]{1,0:T(8,128)(2,1)S(1)}, bf16[1056,128]{1,0:T(8,128)(2,1)S(1)}, u32[]{:S(2)}, u32[]{:S(2)}) collective-permute-start(bf16[1056,128]{1,0:T(8,128)(2,1)S(1)} %get-tuple-element.42), channel_id=1, source_target_pairs={{0,4},{2,6},{4,0},{6,2},{8,12},{10,14},{12,8},{14,10},{1,5},{3,7},... | collective-permute-start | bytes 811016 | tf_op jit(solution)/shard_map/ppermute | solution.py:498
  4.9 2.6 %collective-permute-start.3 = (bf16[2,544,128]{2,1,0:T(8,128)(2,1)S(1)}, bf16[2,544,128]{2,1,0:T(8,128)(2,1)S(1)}, u32[]{:S(2)}, u32[]{:S(2)}) collective-permute-start(bf16[2,544,128]{2,1,0:T(8,128)(2,1)S(1)} %get-tuple-element.44), channel_id=1, source_target_pairs={{0,8},{2,10},{4,12},{6,14},{8,0},{10,2},{12,4},{14,6},{1,9},{3,11}... | collective-permute-start | bytes 835592 | tf_op jit(solution)/shard_map/ppermute | solution.py:498
  7.5 0.0 collective-permute-start.4
  7.5 1.7 %collective-permute-start = (bf16[2,1056,128]{2,1,0:T(8,128)(2,1)S(1)}, bf16[2,1056,128]{2,1,0:T(8,128)(2,1)S(1)}, u32[]{:S(2)}, u32[]{:S(2)}) collective-permute-start(bf16[2,1056,128]{2,1,0:T(8,128)(2,1)S(1)} %get-tuple-element.41), channel_id=1, source_target_pairs={{0,2},{2,0},{4,6},{6,4},{8,10},{10,8},{12,14},{14,12},{1,3},{3,1},... | collective-permute-start | bytes 1622024 | tf_op jit(solution)/shard_map/ppermute | solution.py:498
  9.3 0.1 select_reduce_fusion.1
  9.4 0.1 convert_reduce_fusion
  9.5 0.2 select_reduce_fusion
  9.7 0.1 copy.28.refs_4_
  9.8 0.1 copy.29.refs_5_
  9.9 0.1 broadcast_in_dim.55
  10.0 0.1 broadcast_in_dim_reshape.3.refs_6_
  10.1 9.6 %early.3 = (f32[4,256,1024]{2,1,0:T(8,128)S(1)}, bf16[4,256,128]{2,1,0:T(8,128)(2,1)S(1)}, f32[4,16,256]{2,1,0:T(8,128)S(1)}, f32[4,256,256]{2,1,0:T(8,128)S(1)}...) custom-call(bf16[2,256,4096]{2,1,0:T(8,128)(2,1)} %refs_0_.5, bf16[2,256,512]{2,1,0:T(8,128)(2,1)} %refs_1_.5, ...), custom_call_target="tpu_custom_call" | custom-call | flops 1 | bytes 1 | tf_op jit(solution)/shard_map/early/pallas_call | solution.py:596
  19.7 1.3 %collective-permute-done.refs_1_.refs_2_ = bf16[2,1056,128]{2,1,0:T(8,128)(2,1)S(1)} collective-permute-done((bf16[2,1056,128]{2,1,0:T(8,128)(2,1)S(1)}, bf16[2,1056,128]{2,1,0:T(8,128)(2,1)S(1)}, u32[]{:S(2)}, u32[]{:S(2)}) %collective-permute-start) | collective-permute-done | bytes 540704 | tf_op jit(solution)/shard_map/ppermute | solution.py:498
  21.0 0.7 collective-permute-start.2
  21.7 5.4 %early.4 = (f32[4,256,1024]{2,1,0:T(8,128)S(1)}, bf16[4,256,128]{2,1,0:T(8,128)(2,1)S(1)}, f32[4,16,256]{2,1,0:T(8,128)S(1)}, f32[4,256,256]{2,1,0:T(8,128)S(1)}...) custom-call(bf16[2,256,4096]{2,1,0:T(8,128)(2,1)} %refs_0_.5, bf16[2,256,512]{2,1,0:T(8,128)(2,1)} %refs_1_.5, ...), custom_call_target="tpu_custom_call" | custom-call | flops 1 | bytes 1 | tf_op jit(solution)/shard_map/early/pallas_call | solution.py:596
  27.1 0.3 collective-permute-done.3.refs_1_.refs_5_
  27.4 0.0 collective-permute-done.4.refs_2_.refs_6_
  27.4 1.6 %collective-permute-start.5 = (bf16[2,544,128]{2,1,0:T(8,128)(2,1)S(1)}, bf16[2,544,128]{2,1,0:T(8,128)(2,1)S(1)}, u32[]{:S(2)}, u32[]{:S(2)}) collective-permute-start(bf16[2,544,128]{2,1,0:T(8,128)(2,1)S(1)} %stack_first.1.refs_5_), channel_id=1, source_target_pairs={{0,2},{2,0},{4,6},{6,4},{8,10},{10,8},{12,14},{14,12},{1,3},{3,1},... | collective-permute-start | bytes 835592 | tf_op jit(solution)/shard_map/ppermute | solution.py:498
  29.0 0.0 collective-permute-done.1.refs_3_
  29.0 3.3 %collective-permute-done.2.refs_4_ = bf16[1056,128]{1,0:T(8,128)(2,1)S(1)} collective-permute-done((bf16[1056,128]{1,0:T(8,128)(2,1)S(1)}, bf16[1056,128]{1,0:T(8,128)(2,1)S(1)}, u32[]{:S(2)}, u32[]{:S(2)}) %collective-permute-start.2) | collective-permute-done | bytes 270368 | tf_op jit(solution)/shard_map/ppermute | solution.py:498
  32.3 2.9 %collective-permute-start.9 = (bf16[4,256,128]{2,1,0:T(8,128)(2,1)S(1)}, bf16[4,256,128]{2,1,0:T(8,128)(2,1)S(1)}, u32[]{:S(2)}, u32[]{:S(2)}) collective-permute-start(bf16[4,256,128]{2,1,0:T(8,128)(2,1)S(1)} %stack_later.2.refs_9_), channel_id=1, source_target_pairs={{0,8},{2,10},{4,12},{6,14},{8,0},{10,2},{12,4},{14,6},{1,9},{3,11}... | collective-permute-start | bytes 786440 | tf_op jit(solution)/shard_map/ppermute | solution.py:498
  35.2 5.4 %early.5 = (f32[4,256,1024]{2,1,0:T(8,128)S(1)}, bf16[4,256,128]{2,1,0:T(8,128)(2,1)S(1)}, f32[4,16,256]{2,1,0:T(8,128)S(1)}, f32[4,256,256]{2,1,0:T(8,128)S(1)}...) custom-call(bf16[2,256,4096]{2,1,0:T(8,128)(2,1)} %refs_0_.5, ...), custom_call_target="tpu_custom_call", output_to_operand_aliasing={{0}: (10, {}), {1}: (11, {}), {2}: (12, {}), {3}: (13, {}),... | custom-call | flops 1 | bytes 1 | tf_op jit(solution)/shard_map/early/pallas_call | solution.py:596
  40.6 0.0 collective-permute-done.5.refs_7_
  40.6 1.1 %pick_states.3 = (bf16[2,544,128]{2,1,0:T(8,128)(2,1)S(1)}, bf16[2,544,128]{2,1,0:T(8,128)(2,1)S(1)}, bf16[2,544,128]{2,1,0:T(8,128)(2,1)S(1)}, bf16[2,544,128]{2,1,0:T(8,128)(2,1)S(1)}) custom-call(s32[8]{0:T(128)S(1)} %broadcast_xor_fusion.refs_10_.refs_0_, bf16[1056,128]{1,0:T(8,128)(2,1)S(1)} %get-tuple-element.40.refs_9_.refs_1_, ...), custom_call_target="tpu_custom_call" | custom-call | flops 1 | bytes 1 | tf_op jit(solution)/shard_map/pick_states/pallas_call | solution.py:563
  41.7 0.6 collective-permute-start.6
  42.3 0.7 collective-permute-start.7
  42.9 2.3 %collective-permute-start.8 = (bf16[2,544,128]{2,1,0:T(8,128)(2,1)S(1)}, bf16[2,544,128]{2,1,0:T(8,128)(2,1)S(1)}, u32[]{:S(2)}, u32[]{:S(2)}) collective-permute-start(bf16[2,544,128]{2,1,0:T(8,128)(2,1)S(1)} %get-tuple-element.56), channel_id=1, source_target_pairs={{0,6},{2,4},{4,2},{6,0},{8,14},{10,12},{12,10},{14,8},{1,7},{3,5},... | collective-permute-start | bytes 835592 | tf_op jit(solution)/shard_map/ppermute | solution.py:498
  45.2 1.7 %collective-permute-done.9.refs_6_.refs_5_ = bf16[4,256,128]{2,1,0:T(8,128)(2,1)S(1)} collective-permute-done((bf16[4,256,128]{2,1,0:T(8,128)(2,1)S(1)}, bf16[4,256,128]{2,1,0:T(8,128)(2,1)S(1)}, u32[]{:S(2)}, u32[]{:S(2)}) %collective-permute-start.9) | collective-permute-done | bytes 262176 | tf_op jit(solution)/shard_map/ppermute | solution.py:498
  46.9 0.1 collective-permute-start.10
  47.0 1.1 %pick_states.4 = (bf16[2,256,128]{2,1,0:T(8,128)(2,1)S(1)}, bf16[2,256,128]{2,1,0:T(8,128)(2,1)S(1)}, bf16[2,256,128]{2,1,0:T(8,128)(2,1)S(1)}, bf16[2,256,128]{2,1,0:T(8,128)(2,1)S(1)}) custom-call(s32[8]{0:T(128)S(1)} %broadcast_xor_fusion.refs_10_.refs_0_, bf16[1056,128]{1,0:T(8,128)(2,1)S(1)} %get-tuple-element.40.refs_9_.refs_1_, ...), custom_call_target="tpu_custom_call" | custom-call | flops 1 | bytes 1 | tf_op jit(solution)/shard_map/pick_states/pallas_call | solution.py:563
  48.1 0.9 %collective-permute-start.14 = (bf16[2,256,128]{2,1,0:T(8,128)(2,1)S(1)}, bf16[2,256,128]{2,1,0:T(8,128)(2,1)S(1)}, u32[]{:S(2)}, u32[]{:S(2)}) collective-permute-start(bf16[2,256,128]{2,1,0:T(8,128)(2,1)S(1)} %get-tuple-element.72), channel_id=1, source_target_pairs={{0,2},{2,0},{4,6},{6,4},{8,10},{10,8},{12,14},{14,12},{1,3},{3,1},... | collective-permute-start | bytes 393224 | tf_op jit(solution)/shard_map/ppermute | solution.py:498
  49.0 0.0 collective-permute-done.6.refs_2_.refs_6_
  49.0 2.7 %collective-permute-start.15 = (bf16[2,256,128]{2,1,0:T(8,128)(2,1)S(1)}, bf16[2,256,128]{2,1,0:T(8,128)(2,1)S(1)}, u32[]{:S(2)}, u32[]{:S(2)}) collective-permute-start(bf16[2,256,128]{2,1,0:T(8,128)(2,1)S(1)} %get-tuple-element.73), channel_id=1, source_target_pairs={{0,4},{2,6},{4,0},{6,2},{8,12},{10,14},{12,8},{14,10},{1,5},{3,7},... | collective-permute-start | bytes 393224 | tf_op jit(solution)/shard_map/ppermute | solution.py:498
  51.7 9.2 %collective-permute-done.10.refs_5_ = bf16[4,256,128]{2,1,0:T(8,128)(2,1)S(1)} collective-permute-done((bf16[4,256,128]{2,1,0:T(8,128)(2,1)S(1)}, bf16[4,256,128]{2,1,0:T(8,128)(2,1)S(1)}, u32[]{:S(2)}, u32[]{:S(2)}) %collective-permute-start.10) | collective-permute-done | bytes 262176 | tf_op jit(solution)/shard_map/ppermute | solution.py:498
  61.0 3.4 %collective-permute-start.16 = (bf16[2,256,128]{2,1,0:T(8,128)(2,1)S(1)}, bf16[2,256,128]{2,1,0:T(8,128)(2,1)S(1)}, u32[]{:S(2)}, u32[]{:S(2)}) collective-permute-start(bf16[2,256,128]{2,1,0:T(8,128)(2,1)S(1)} %get-tuple-element.74), channel_id=1, source_target_pairs={{0,6},{2,4},{4,2},{6,0},{8,14},{10,12},{12,10},{14,8},{1,7},{3,5},... | collective-permute-start | bytes 393224 | tf_op jit(solution)/shard_map/ppermute | solution.py:498
  64.4 1.2 %pick_states.5 = (bf16[2,256,128]{2,1,0:T(8,128)(2,1)S(1)}, bf16[2,256,128]{2,1,0:T(8,128)(2,1)S(1)}, bf16[2,256,128]{2,1,0:T(8,128)(2,1)S(1)}, bf16[2,256,128]{2,1,0:T(8,128)(2,1)S(1)}) custom-call(s32[8]{0:T(128)S(1)} %broadcast_xor_fusion.refs_10_.refs_0_, bf16[1056,128]{1,0:T(8,128)(2,1)S(1)} %get-tuple-element.40.refs_9_.refs_1_, ...), custom_call_target="tpu_custom_call" | custom-call | flops 1 | bytes 1 | tf_op jit(solution)/shard_map/pick_states/pallas_call | solution.py:563
  65.6 0.0 collective-permute-done.7.refs_3_.refs_7_
  65.6 1.9 %collective-permute-start.11 = (bf16[2,256,128]{2,1,0:T(8,128)(2,1)S(1)}, bf16[2,256,128]{2,1,0:T(8,128)(2,1)S(1)}, u32[]{:S(2)}, u32[]{:S(2)}) collective-permute-start(bf16[2,256,128]{2,1,0:T(8,128)(2,1)S(1)} %get-tuple-element.59), channel_id=1, source_target_pairs={{0,2},{2,0},{4,6},{6,4},{8,10},{10,8},{12,14},{14,12},{1,3},{3,1},... | collective-permute-start | bytes 393224 | tf_op jit(solution)/shard_map/ppermute | solution.py:498
  67.5 0.0 collective-permute-done.8.refs_4_.refs_8_
  67.5 0.0 collective-permute-start.12
  67.5 0.0 collective-permute-done.14.refs_10_
  67.5 1.7 %collective-permute-start.13 = (bf16[2,256,128]{2,1,0:T(8,128)(2,1)S(1)}, bf16[2,256,128]{2,1,0:T(8,128)(2,1)S(1)}, u32[]{:S(2)}, u32[]{:S(2)}) collective-permute-start(bf16[2,256,128]{2,1,0:T(8,128)(2,1)S(1)} %get-tuple-element.61), channel_id=1, source_target_pairs={{0,6},{2,4},{4,2},{6,0},{8,14},{10,12},{12,10},{14,8},{1,7},{3,5},... | collective-permute-start | bytes 393224 | tf_op jit(solution)/shard_map/ppermute | solution.py:498
  69.2 1.1 %collective-permute-done.16.refs_12_ = bf16[2,256,128]{2,1,0:T(8,128)(2,1)S(1)} collective-permute-done((bf16[2,256,128]{2,1,0:T(8,128)(2,1)S(1)}, bf16[2,256,128]{2,1,0:T(8,128)(2,1)S(1)}, u32[]{:S(2)}, u32[]{:S(2)}) %collective-permute-start.16) | collective-permute-done | bytes 131104 | tf_op jit(solution)/shard_map/ppermute | solution.py:498
  70.4 5.7 %late.2.refs_21_ = bf16[2,256,4096]{2,1,0:T(8,128)(2,1)} custom-call(s32[1]{0:T(128)} %bitcast.place_ref.refs_0_, bf16[2,544,128]{2,1,0:T(8,128)(2,1)S(1)} %get-tuple-element.53.refs_5_.refs_1_, bf16[2,544,128]{2,1,0:T(8,128)(2,1)S(1)} %collective-permute-done.6.refs_2_.refs_6_, bf16[2,544,128]{2,1,0:T(8,128)(2,1)S(1)} %collective-permute-done.7.refs_3_.refs_7_, ...), custom_call_target="tpu_custom_call" | custom-call | flops 1 | bytes 1 | tf_op jit(solution)/shard_map/late/pallas_call | solution.py:645
  76.1 0.0 collective-permute-done.11.refs_6_
  76.1 0.0 collective-permute-done.12.refs_7_
  76.1 2.9 %late.3 = bf16[2,256,4096]{2,1,0:T(8,128)(2,1)} custom-call(s32[1]{0:T(128)} %bitcast.place_ref.refs_0_, bf16[2,544,128]{2,1,0:T(8,128)(2,1)S(1)} %get-tuple-element.53.refs_5_.refs_1_, bf16[2,544,128]{2,1,0:T(8,128)(2,1)S(1)} %collective-permute-done.6.refs_2_.refs_6_, ...), custom_call_target="tpu_custom_call", output_to_operand_aliasing={{}: (21, {})} | custom-call | flops 1 | bytes 1 | tf_op jit(solution)/shard_map/late/pallas_call | solution.py:645
  (18 shorter events, 0.1 us)
Async XLA Ops:
  0.0 9.3 %copy-start.3 = (s32[8]{0:T(128)S(1)}, s32[8]{0:T(128)}, u32[]{:S(2)}) copy-start(s32[8]{0:T(128)} %param.26) | copy-start | bytes 100
  0.0 9.4 %copy-start.4 = (s32[16]{0:T(128)S(1)}, s32[16]{0:T(128)}, u32[]{:S(2)}) copy-start(s32[16]{0:T(128)} %param.27) | copy-start | bytes 196
  0.0 9.7 %copy-start = (f32[64]{0:T(128)S(1)}, f32[64]{0:T(128)}, u32[]{:S(2)}) copy-start(f32[64]{0:T(128)} %param.18) | copy-start | bytes 772
  0.0 9.8 %copy-start.1 = (f32[64]{0:T(128)S(1)}, f32[64]{0:T(128)}, u32[]{:S(2)}) copy-start(f32[64]{0:T(128)} %param.19) | copy-start | bytes 772
  0.0 9.9 %copy-start.2 = (f32[64]{0:T(128)S(1)}, f32[64]{0:T(128)}, u32[]{:S(2)}) copy-start(f32[64]{0:T(128)} %param.20) | copy-start | bytes 772
  1.8 27.2 %collective-permute-start.1 = (bf16[1056,128]{1,0:T(8,128)(2,1)S(1)}, bf16[1056,128]{1,0:T(8,128)(2,1)S(1)}, u32[]{:S(2)}, u32[]{:S(2)}) collective-permute-start(bf16[1056,128]{1,0:T(8,128)(2,1)S(1)} %get-tuple-element.42), channel_id=1, source_target_pairs={{0,4},{2,6},{4,0},{6,2},{8,12},{10,14},{12,8},{14,10},{1,5},{3,7},... | collective-permute-start | bytes 811016 | tf_op jit(solution)/shard_map/ppermute | solution.py:498
  4.9 22.5 %collective-permute-start.3 = (bf16[2,544,128]{2,1,0:T(8,128)(2,1)S(1)}, bf16[2,544,128]{2,1,0:T(8,128)(2,1)S(1)}, u32[]{:S(2)}, u32[]{:S(2)}) collective-permute-start(bf16[2,544,128]{2,1,0:T(8,128)(2,1)S(1)} %get-tuple-element.44), channel_id=1, source_target_pairs={{0,8},{2,10},{4,12},{6,14},{8,0},{10,2},{12,4},{14,6},{1,9},{3,11}... | collective-permute-start | bytes 835592 | tf_op jit(solution)/shard_map/ppermute | solution.py:498
  7.5 19.9 %collective-permute-start.4 = (bf16[2,544,128]{2,1,0:T(8,128)(2,1)S(1)}, bf16[2,544,128]{2,1,0:T(8,128)(2,1)S(1)}, u32[]{:S(2)}, u32[]{:S(2)}) collective-permute-start(bf16[2,544,128]{2,1,0:T(8,128)(2,1)S(1)} %get-tuple-element.45), channel_id=1, source_target_pairs={{0,12},{2,14},{4,8},{6,10},{8,4},{10,6},{12,0},{14,2},{1,13},{3,15... | collective-permute-start | bytes 835592 | tf_op jit(solution)/shard_map/ppermute | solution.py:498
  7.5 13.5 %collective-permute-start = (bf16[2,1056,128]{2,1,0:T(8,128)(2,1)S(1)}, bf16[2,1056,128]{2,1,0:T(8,128)(2,1)S(1)}, u32[]{:S(2)}, u32[]{:S(2)}) collective-permute-start(bf16[2,1056,128]{2,1,0:T(8,128)(2,1)S(1)} %get-tuple-element.41), channel_id=1, source_target_pairs={{0,2},{2,0},{4,6},{6,4},{8,10},{10,8},{12,14},{14,12},{1,3},{3,1},... | collective-permute-start | bytes 1622024 | tf_op jit(solution)/shard_map/ppermute | solution.py:498
  21.0 11.3 %collective-permute-start.2 = (bf16[1056,128]{1,0:T(8,128)(2,1)S(1)}, bf16[1056,128]{1,0:T(8,128)(2,1)S(1)}, u32[]{:S(2)}, u32[]{:S(2)}) collective-permute-start(bf16[1056,128]{1,0:T(8,128)(2,1)S(1)} %stack_turn.1.refs_9_), channel_id=1, source_target_pairs={{0,4},{2,6},{4,0},{6,2},{8,12},{10,14},{12,8},{14,10},{1,5},{3,7},... | collective-permute-start | bytes 811016 | tf_op jit(solution)/shard_map/ppermute | solution.py:498
  27.4 13.1 %collective-permute-start.5 = (bf16[2,544,128]{2,1,0:T(8,128)(2,1)S(1)}, bf16[2,544,128]{2,1,0:T(8,128)(2,1)S(1)}, u32[]{:S(2)}, u32[]{:S(2)}) collective-permute-start(bf16[2,544,128]{2,1,0:T(8,128)(2,1)S(1)} %stack_first.1.refs_5_), channel_id=1, source_target_pairs={{0,2},{2,0},{4,6},{6,4},{8,10},{10,8},{12,14},{14,12},{1,3},{3,1},... | collective-permute-start | bytes 835592 | tf_op jit(solution)/shard_map/ppermute | solution.py:498
  32.3 14.6 %collective-permute-start.9 = (bf16[4,256,128]{2,1,0:T(8,128)(2,1)S(1)}, bf16[4,256,128]{2,1,0:T(8,128)(2,1)S(1)}, u32[]{:S(2)}, u32[]{:S(2)}) collective-permute-start(bf16[4,256,128]{2,1,0:T(8,128)(2,1)S(1)} %stack_later.2.refs_9_), channel_id=1, source_target_pairs={{0,8},{2,10},{4,12},{6,14},{8,0},{10,2},{12,4},{14,6},{1,9},{3,11}... | collective-permute-start | bytes 786440 | tf_op jit(solution)/shard_map/ppermute | solution.py:498
  41.7 7.3 %collective-permute-start.6 = (bf16[2,544,128]{2,1,0:T(8,128)(2,1)S(1)}, bf16[2,544,128]{2,1,0:T(8,128)(2,1)S(1)}, u32[]{:S(2)}, u32[]{:S(2)}) collective-permute-start(bf16[2,544,128]{2,1,0:T(8,128)(2,1)S(1)} %get-tuple-element.54), channel_id=1, source_target_pairs={{0,2},{2,0},{4,6},{6,4},{8,10},{10,8},{12,14},{14,12},{1,3},{3,1},... | collective-permute-start | bytes 835592 | tf_op jit(solution)/shard_map/ppermute | solution.py:498
  42.3 23.4 %collective-permute-start.7 = (bf16[2,544,128]{2,1,0:T(8,128)(2,1)S(1)}, bf16[2,544,128]{2,1,0:T(8,128)(2,1)S(1)}, u32[]{:S(2)}, u32[]{:S(2)}) collective-permute-start(bf16[2,544,128]{2,1,0:T(8,128)(2,1)S(1)} %get-tuple-element.55), channel_id=1, source_target_pairs={{0,4},{2,6},{4,0},{6,2},{8,12},{10,14},{12,8},{14,10},{1,5},{3,7},... | collective-permute-start | bytes 835592 | tf_op jit(solution)/shard_map/ppermute | solution.py:498
  42.9 24.6 %collective-permute-start.8 = (bf16[2,544,128]{2,1,0:T(8,128)(2,1)S(1)}, bf16[2,544,128]{2,1,0:T(8,128)(2,1)S(1)}, u32[]{:S(2)}, u32[]{:S(2)}) collective-permute-start(bf16[2,544,128]{2,1,0:T(8,128)(2,1)S(1)} %get-tuple-element.56), channel_id=1, source_target_pairs={{0,6},{2,4},{4,2},{6,0},{8,14},{10,12},{12,10},{14,8},{1,7},{3,5},... | collective-permute-start | bytes 835592 | tf_op jit(solution)/shard_map/ppermute | solution.py:498
  46.9 14.0 %collective-permute-start.10 = (bf16[4,256,128]{2,1,0:T(8,128)(2,1)S(1)}, bf16[4,256,128]{2,1,0:T(8,128)(2,1)S(1)}, u32[]{:S(2)}, u32[]{:S(2)}) collective-permute-start(bf16[4,256,128]{2,1,0:T(8,128)(2,1)S(1)} %stack_later.3.refs_6_), channel_id=1, source_target_pairs={{0,8},{2,10},{4,12},{6,14},{8,0},{10,2},{12,4},{14,6},{1,9},{3,11}... | collective-permute-start | bytes 786440 | tf_op jit(solution)/shard_map/ppermute | solution.py:498
  48.1 19.5 %collective-permute-start.14 = (bf16[2,256,128]{2,1,0:T(8,128)(2,1)S(1)}, bf16[2,256,128]{2,1,0:T(8,128)(2,1)S(1)}, u32[]{:S(2)}, u32[]{:S(2)}) collective-permute-start(bf16[2,256,128]{2,1,0:T(8,128)(2,1)S(1)} %get-tuple-element.72), channel_id=1, source_target_pairs={{0,2},{2,0},{4,6},{6,4},{8,10},{10,8},{12,14},{14,12},{1,3},{3,1},... | collective-permute-start | bytes 393224 | tf_op jit(solution)/shard_map/ppermute | solution.py:498
  49.0 20.2 %collective-permute-start.15 = (bf16[2,256,128]{2,1,0:T(8,128)(2,1)S(1)}, bf16[2,256,128]{2,1,0:T(8,128)(2,1)S(1)}, u32[]{:S(2)}, u32[]{:S(2)}) collective-permute-start(bf16[2,256,128]{2,1,0:T(8,128)(2,1)S(1)} %get-tuple-element.73), channel_id=1, source_target_pairs={{0,4},{2,6},{4,0},{6,2},{8,12},{10,14},{12,8},{14,10},{1,5},{3,7},... | collective-permute-start | bytes 393224 | tf_op jit(solution)/shard_map/ppermute | solution.py:498
  61.0 9.4 %collective-permute-start.16 = (bf16[2,256,128]{2,1,0:T(8,128)(2,1)S(1)}, bf16[2,256,128]{2,1,0:T(8,128)(2,1)S(1)}, u32[]{:S(2)}, u32[]{:S(2)}) collective-permute-start(bf16[2,256,128]{2,1,0:T(8,128)(2,1)S(1)} %get-tuple-element.74), channel_id=1, source_target_pairs={{0,6},{2,4},{4,2},{6,0},{8,14},{10,12},{12,10},{14,8},{1,7},{3,5},... | collective-permute-start | bytes 393224 | tf_op jit(solution)/shard_map/ppermute | solution.py:498
  65.6 10.4 %collective-permute-start.11 = (bf16[2,256,128]{2,1,0:T(8,128)(2,1)S(1)}, bf16[2,256,128]{2,1,0:T(8,128)(2,1)S(1)}, u32[]{:S(2)}, u32[]{:S(2)}) collective-permute-start(bf16[2,256,128]{2,1,0:T(8,128)(2,1)S(1)} %get-tuple-element.59), channel_id=1, source_target_pairs={{0,2},{2,0},{4,6},{6,4},{8,10},{10,8},{12,14},{14,12},{1,3},{3,1},... | collective-permute-start | bytes 393224 | tf_op jit(solution)/shard_map/ppermute | solution.py:498
  67.5 8.6 %collective-permute-start.12 = (bf16[2,256,128]{2,1,0:T(8,128)(2,1)S(1)}, bf16[2,256,128]{2,1,0:T(8,128)(2,1)S(1)}, u32[]{:S(2)}, u32[]{:S(2)}) collective-permute-start(bf16[2,256,128]{2,1,0:T(8,128)(2,1)S(1)} %get-tuple-element.60), channel_id=1, source_target_pairs={{0,4},{2,6},{4,0},{6,2},{8,12},{10,14},{12,8},{14,10},{1,5},{3,7},... | collective-permute-start | bytes 393224 | tf_op jit(solution)/shard_map/ppermute | solution.py:498
  67.5 8.6 %collective-permute-start.13 = (bf16[2,256,128]{2,1,0:T(8,128)(2,1)S(1)}, bf16[2,256,128]{2,1,0:T(8,128)(2,1)S(1)}, u32[]{:S(2)}, u32[]{:S(2)}) collective-permute-start(bf16[2,256,128]{2,1,0:T(8,128)(2,1)S(1)} %get-tuple-element.61), channel_id=1, source_target_pairs={{0,6},{2,4},{4,2},{6,0},{8,14},{10,12},{12,10},{14,8},{1,7},{3,5},... | collective-permute-start | bytes 393224 | tf_op jit(solution)/shard_map/ppermute | solution.py:498

commit v18 on v17

--- a/solution.py
+++ b/solution.py
@@ -668,9 +668,9 @@
     own, own_2, own_13, sent_4, sent_6 = cast()
     crossed_a = [swap(sent_4, 4), swap(sent_6, 6)]
     along_y, along_z = swap(own_13, 1), swap(own_2, 2)
-    parts = [early(0, 1, 0, [], [own, slots])]
+    first = early(0, 2, 0, [], [own, slots])
     (turn,) = rearrange(
-        place, [along_y], [(0, None, None, [(0, 1)])], [own.shape], [parts[0][1]], "stack_turn"
+        place, [along_y], [(0, None, None, [(0, 1)])], [own.shape], [first[1]], "stack_turn"
     )
     inside = [own, along_y, along_z, swap(turn, 2)]
 
@@ -686,20 +686,21 @@
         choices = inside_rows(k) + [(4, j) for j in range(4)]
         return pick(rows[k], [*inside, crossed], choices, tokens)
 
-    second = early(1, 2, 0, [], [turn])
+    first = early(0, 2, 1, first, [turn])
+    sent_b, crossed_b = cross(1, [first[1]])
+    second = early(1, 2, 0, [], [sent_b])
     moves = [(0, n, None, [(n, 1)]) for n in range(2)]
     (spread,) = rearrange(
         place, crossed_a, moves, [(2, rows[0], size)], [second[1]], "stack_first"
     )
     passed = swap(spread, 1)
-    sent_b, crossed_b = cross(1, [spread])
-    second = early(1, 2, 1, second, [sent_b])
-    parts.append(second)
+    sent_c, crossed_c = cross(2, [spread])
+    second = early(1, 2, 1, second, [sent_c])
     choices = inside_rows(0) + [(4, 0), (6, 0), (5, 0), (6, 1)]
     states = [pick(rows[0], [*inside, *crossed_a, passed], choices, [second[1]])]
-    sent_c, crossed_c = cross(2, [states[0][0], crossed_b])
-    states.append(pick_later(1, crossed_b, [sent_c]))
-    states.append(pick_later(2, crossed_c, [states[1][0]]))
+    states.append(pick_later(1, crossed_b, [states[0][0]]))
+    states.append(pick_later(2, crossed_c, [states[1][0], *states[0]]))
+    parts = [first, second]
     result = late([0, 1], states, parts, None, [states[2][0]])
     return late([2], states, parts, result, [])
 

time: 79.4 us -> 85.4 us (1.076)
  waiting for transfers between devices: 17 us -> 26.2 us
  starting transfers between devices: 26.8 us -> 22.4 us
  Pallas kernels: 34.3 us -> 35.4 us
    ppermute x17, waiting for transfers between devices: 17 us -> 26.2 us  [swap(): return lax.ppermute(value, 'batch', perm=[(i, i ^ r) for i in range(8)])]
    ppermute x17, starting transfers between devices: 26.8 us -> 22.4 us  [swap(): return lax.ppermute(value, 'batch', perm=[(i, i ^ r) for i in range(8)])]
    pallas_call x3 -> x4, Pallas kernels: 20.4 us -> 21.6 us  [early(): pl.pallas_call(functools.partial(drop_tokens, functools.partial(early_ker...]
  transfers between devices with their start and end apart: 17 -> 17, of which waited for: 6 -> 7; matrix products, arithmetic and copies ran while one was open for 1% -> 1% of each run, Pallas kernels for 37% -> 36%
where the time goes in v18:
time: 85.4 us; the launch traced here: 85.2 us
  Pallas kernels  35.4 us (41%)
  waiting for transfers between devices  26.2 us (31%)
  starting transfers between devices  22.4 us (26%)
    ppermute x17, waiting for transfers between devices, swap(): return lax.ppermute(value, 'batch', perm=[(i, i ^ r) for i in range(8)])  26.2 us
    ppermute x17, starting transfers between devices, swap(): return lax.ppermute(value, 'batch', perm=[(i, i ^ r) for i in range(8)])  22.4 us
    pallas_call x4, Pallas kernels, early(): pl.pallas_call(functools.partial(drop_tokens, functools.partial(early_ker...  21.6 us
    pallas_call x2, Pallas kernels, late(): pl.pallas_call(functools.partial(drop_tokens, kernel, keep, 1 + len(opera...  8.63 us
    pallas_call x7, Pallas kernels, rearrange(): pl.pallas_call(functools.partial(drop_tokens, kernel, 1 + len(sources), l...  3.44 us
    pallas_call x1, Pallas kernels, cast(): pl.pallas_call(kernel, grid_spec=pltpu.PrefetchScalarGridSpec(num_scalar_...  1.82 us
  transfers between devices with their start and end apart: 17, of which 7 were waited for; matrix products, arithmetic and copies ran while one was open for 1% of the time, Pallas kernels for 36%

profile of v18, /device:TPU:0, one launch (start us, length us, event | category | flops | bytes accessed | tf_op | source)
XLA Modules:
  0.0 85.2 jit_solution(2954253017670594310)
XLA Ops:
  0.0 1.8 %cast_states.1 = (bf16[1056,128]{1,0:T(8,128)(2,1)S(1)}, bf16[1056,128]{1,0:T(8,128)(2,1)S(1)}, bf16[2,1056,128]{2,1,0:T(8,128)(2,1)S(1)}, bf16[2,544,128]{2,1,0:T(8,128)(2,1)S(1)}, bf16[2,544,128]{2,1,0:T(8,128)(2,1)S(1)}) custom-call(s32[1]{0:T(128)} %bitcast.place_ref.refs_0_, f32[4,16,64,128]{3,2,1,0:T(8,128)} %bitcast.5, f32[4,16,64,128]{3,2,1,0:T(8,128)} %bitcast.6, ...), custom_call_target="tpu_custom_call" | custom-call | flops 1 | bytes 1 | tf_op jit(solution)/shard_map/cast_states/pallas_call | solution.py:531
  1.8 3.1 %collective-permute-start.1 = (bf16[1056,128]{1,0:T(8,128)(2,1)S(1)}, bf16[1056,128]{1,0:T(8,128)(2,1)S(1)}, u32[]{:S(2)}, u32[]{:S(2)}) collective-permute-start(bf16[1056,128]{1,0:T(8,128)(2,1)S(1)} %get-tuple-element.48), channel_id=1, source_target_pairs={{0,4},{2,6},{4,0},{6,2},{8,12},{10,14},{12,8},{14,10},{1,5},{3,7},... | collective-permute-start | bytes 811016 | tf_op jit(solution)/shard_map/ppermute | solution.py:498
  4.9 2.6 %collective-permute-start.3 = (bf16[2,544,128]{2,1,0:T(8,128)(2,1)S(1)}, bf16[2,544,128]{2,1,0:T(8,128)(2,1)S(1)}, u32[]{:S(2)}, u32[]{:S(2)}) collective-permute-start(bf16[2,544,128]{2,1,0:T(8,128)(2,1)S(1)} %get-tuple-element.50), channel_id=1, source_target_pairs={{0,8},{2,10},{4,12},{6,14},{8,0},{10,2},{12,4},{14,6},{1,9},{3,11}... | collective-permute-start | bytes 835592 | tf_op jit(solution)/shard_map/ppermute | solution.py:498
  7.5 0.0 collective-permute-start.4
  7.5 1.7 %collective-permute-start = (bf16[2,1056,128]{2,1,0:T(8,128)(2,1)S(1)}, bf16[2,1056,128]{2,1,0:T(8,128)(2,1)S(1)}, u32[]{:S(2)}, u32[]{:S(2)}) collective-permute-start(bf16[2,1056,128]{2,1,0:T(8,128)(2,1)S(1)} %get-tuple-element.47), channel_id=1, source_target_pairs={{0,2},{2,0},{4,6},{6,4},{8,10},{10,8},{12,14},{14,12},{1,3},{3,1},... | collective-permute-start | bytes 1622024 | tf_op jit(solution)/shard_map/ppermute | solution.py:498
  9.3 0.1 select_reduce_fusion.1
  9.4 0.1 convert_reduce_fusion
  9.5 0.2 select_reduce_fusion
  9.7 0.1 copy.36.refs_4_
  9.8 0.1 copy.37.refs_5_
  9.9 0.1 broadcast_in_dim.57
  10.0 0.1 broadcast_in_dim_reshape.3.refs_6_
  10.1 5.4 %early.4 = (f32[4,256,1024]{2,1,0:T(8,128)S(1)}, bf16[4,256,128]{2,1,0:T(8,128)(2,1)S(1)}, f32[4,16,256]{2,1,0:T(8,128)S(1)}, f32[4,256,256]{2,1,0:T(8,128)S(1)}...) custom-call(bf16[2,256,4096]{2,1,0:T(8,128)(2,1)} %refs_0_.7, bf16[2,256,512]{2,1,0:T(8,128)(2,1)} %refs_1_.7, ...), custom_call_target="tpu_custom_call" | custom-call | flops 1 | bytes 1 | tf_op jit(solution)/shard_map/early/pallas_call | solution.py:596
  15.5 5.5 %collective-permute-done.refs_1_.refs_2_ = bf16[2,1056,128]{2,1,0:T(8,128)(2,1)S(1)} collective-permute-done((bf16[2,1056,128]{2,1,0:T(8,128)(2,1)S(1)}, bf16[2,1056,128]{2,1,0:T(8,128)(2,1)S(1)}, u32[]{:S(2)}, u32[]{:S(2)}) %collective-permute-start) | collective-permute-done | bytes 540704 | tf_op jit(solution)/shard_map/ppermute | solution.py:498
  21.0 0.7 collective-permute-start.2
  21.7 5.4 %early.5 = (f32[4,256,1024]{2,1,0:T(8,128)S(1)}, bf16[4,256,128]{2,1,0:T(8,128)(2,1)S(1)}, f32[4,16,256]{2,1,0:T(8,128)S(1)}, f32[4,256,256]{2,1,0:T(8,128)S(1)}...) custom-call(bf16[2,256,4096]{2,1,0:T(8,128)(2,1)} %refs_0_.7, ...), custom_call_target="tpu_custom_call", output_to_operand_aliasing={{0}: (10, {}), {1}: (11, {}), {2}: (12, {}), {3}: (13, {}),... | custom-call | flops 1 | bytes 1 | tf_op jit(solution)/shard_map/early/pallas_call | solution.py:596
  27.1 0.0 collective-permute-done.1.refs_3_
  27.1 5.2 %collective-permute-done.2.refs_4_ = bf16[1056,128]{1,0:T(8,128)(2,1)S(1)} collective-permute-done((bf16[1056,128]{1,0:T(8,128)(2,1)S(1)}, bf16[1056,128]{1,0:T(8,128)(2,1)S(1)}, u32[]{:S(2)}, u32[]{:S(2)}) %collective-permute-start.2) | collective-permute-done | bytes 270368 | tf_op jit(solution)/shard_map/ppermute | solution.py:498
  32.3 5.4 %early.6 = (f32[4,256,1024]{2,1,0:T(8,128)S(1)}, bf16[4,256,128]{2,1,0:T(8,128)(2,1)S(1)}, f32[4,16,256]{2,1,0:T(8,128)S(1)}, f32[4,256,256]{2,1,0:T(8,128)S(1)}...) custom-call(bf16[2,256,4096]{2,1,0:T(8,128)(2,1)} %refs_0_.7, bf16[2,256,512]{2,1,0:T(8,128)(2,1)} %refs_1_.7, ...), custom_call_target="tpu_custom_call" | custom-call | flops 1 | bytes 1 | tf_op jit(solution)/shard_map/early/pallas_call | solution.py:596
  37.7 0.0 collective-permute-done.4.refs_2_.refs_6_
  37.8 1.6 %collective-permute-start.5 = (bf16[2,544,128]{2,1,0:T(8,128)(2,1)S(1)}, bf16[2,544,128]{2,1,0:T(8,128)(2,1)S(1)}, u32[]{:S(2)}, u32[]{:S(2)}) collective-permute-start(bf16[2,544,128]{2,1,0:T(8,128)(2,1)S(1)} %stack_first.1.refs_5_), channel_id=1, source_target_pairs={{0,2},{2,0},{4,6},{6,4},{8,10},{10,8},{12,14},{14,12},{1,3},{3,1},... | collective-permute-start | bytes 835592 | tf_op jit(solution)/shard_map/ppermute | solution.py:498
  39.4 0.0 collective-permute-start.10
  39.4 5.4 %early.7 = (f32[4,256,1024]{2,1,0:T(8,128)S(1)}, bf16[4,256,128]{2,1,0:T(8,128)(2,1)S(1)}, f32[4,16,256]{2,1,0:T(8,128)S(1)}, f32[4,256,256]{2,1,0:T(8,128)S(1)}...) custom-call(bf16[2,256,4096]{2,1,0:T(8,128)(2,1)} %refs_0_.7, ...), custom_call_target="tpu_custom_call", output_to_operand_aliasing={{0}: (10, {}), {1}: (11, {}), {2}: (12, {}), {3}: (13, {}),... | custom-call | flops 1 | bytes 1 | tf_op jit(solution)/shard_map/early/pallas_call | solution.py:596
  44.8 1.6 %collective-permute-done.5.refs_7_ = bf16[2,544,128]{2,1,0:T(8,128)(2,1)S(1)} collective-permute-done((bf16[2,544,128]{2,1,0:T(8,128)(2,1)S(1)}, bf16[2,544,128]{2,1,0:T(8,128)(2,1)S(1)}, u32[]{:S(2)}, u32[]{:S(2)}) %collective-permute-start.5) | collective-permute-done | bytes 278560 | tf_op jit(solution)/shard_map/ppermute | solution.py:498
  46.4 1.1 %pick_states.3 = (bf16[2,544,128]{2,1,0:T(8,128)(2,1)S(1)}, bf16[2,544,128]{2,1,0:T(8,128)(2,1)S(1)}, bf16[2,544,128]{2,1,0:T(8,128)(2,1)S(1)}, bf16[2,544,128]{2,1,0:T(8,128)(2,1)S(1)}) custom-call(s32[8]{0:T(128)S(1)} %broadcast_xor_fusion.refs_10_.refs_0_, bf16[1056,128]{1,0:T(8,128)(2,1)S(1)} %get-tuple-element.46.refs_9_.refs_1_, ...), custom_call_target="tpu_custom_call" | custom-call | flops 1 | bytes 1 | tf_op jit(solution)/shard_map/pick_states/pallas_call | solution.py:563
  47.5 1.6 %collective-permute-start.6 = (bf16[2,544,128]{2,1,0:T(8,128)(2,1)S(1)}, bf16[2,544,128]{2,1,0:T(8,128)(2,1)S(1)}, u32[]{:S(2)}, u32[]{:S(2)}) collective-permute-start(bf16[2,544,128]{2,1,0:T(8,128)(2,1)S(1)} %get-tuple-element.66), channel_id=1, source_target_pairs={{0,2},{2,0},{4,6},{6,4},{8,10},{10,8},{12,14},{14,12},{1,3},{3,1},... | collective-permute-start | bytes 835592 | tf_op jit(solution)/shard_map/ppermute | solution.py:498
  49.1 0.0 collective-permute-start.7
  49.1 2.0 %collective-permute-start.8 = (bf16[2,544,128]{2,1,0:T(8,128)(2,1)S(1)}, bf16[2,544,128]{2,1,0:T(8,128)(2,1)S(1)}, u32[]{:S(2)}, u32[]{:S(2)}) collective-permute-start(bf16[2,544,128]{2,1,0:T(8,128)(2,1)S(1)} %get-tuple-element.68), channel_id=1, source_target_pairs={{0,6},{2,4},{4,2},{6,0},{8,14},{10,12},{12,10},{14,8},{1,7},{3,5},... | collective-permute-start | bytes 835592 | tf_op jit(solution)/shard_map/ppermute | solution.py:498
  51.1 1.3 %collective-permute-start.9 = (bf16[4,256,128]{2,1,0:T(8,128)(2,1)S(1)}, bf16[4,256,128]{2,1,0:T(8,128)(2,1)S(1)}, u32[]{:S(2)}, u32[]{:S(2)}) collective-permute-start(bf16[4,256,128]{2,1,0:T(8,128)(2,1)S(1)} %stack_later.3.refs_9_), channel_id=1, source_target_pairs={{0,8},{2,10},{4,12},{6,14},{8,0},{10,2},{12,4},{14,6},{1,9},{3,11}... | collective-permute-start | bytes 786440 | tf_op jit(solution)/shard_map/ppermute | solution.py:498
  52.4 0.5 collective-permute-done.10.refs_5_
  52.9 1.0 %pick_states.4 = (bf16[2,256,128]{2,1,0:T(8,128)(2,1)S(1)}, bf16[2,256,128]{2,1,0:T(8,128)(2,1)S(1)}, bf16[2,256,128]{2,1,0:T(8,128)(2,1)S(1)}, bf16[2,256,128]{2,1,0:T(8,128)(2,1)S(1)}) custom-call(s32[8]{0:T(128)S(1)} %broadcast_xor_fusion.refs_10_.refs_0_, bf16[1056,128]{1,0:T(8,128)(2,1)S(1)} %get-tuple-element.46.refs_9_.refs_1_, ...), custom_call_target="tpu_custom_call" | custom-call | flops 1 | bytes 1 | tf_op jit(solution)/shard_map/pick_states/pallas_call | solution.py:563
  54.0 0.6 collective-permute-start.14
  54.5 11.4 %collective-permute-done.9.refs_5_ = bf16[4,256,128]{2,1,0:T(8,128)(2,1)S(1)} collective-permute-done((bf16[4,256,128]{2,1,0:T(8,128)(2,1)S(1)}, bf16[4,256,128]{2,1,0:T(8,128)(2,1)S(1)}, u32[]{:S(2)}, u32[]{:S(2)}) %collective-permute-start.9) | collective-permute-done | bytes 262176 | tf_op jit(solution)/shard_map/ppermute | solution.py:498
  66.0 2.8 %collective-permute-start.15 = (bf16[2,256,128]{2,1,0:T(8,128)(2,1)S(1)}, bf16[2,256,128]{2,1,0:T(8,128)(2,1)S(1)}, u32[]{:S(2)}, u32[]{:S(2)}) collective-permute-start(bf16[2,256,128]{2,1,0:T(8,128)(2,1)S(1)} %get-tuple-element.85), channel_id=1, source_target_pairs={{0,4},{2,6},{4,0},{6,2},{8,12},{10,14},{12,8},{14,10},{1,5},{3,7},... | collective-permute-start | bytes 393224 | tf_op jit(solution)/shard_map/ppermute | solution.py:498
  68.8 0.0 collective-permute-done.6.refs_8_.refs_2_.refs_6_
  68.8 1.0 %collective-permute-start.16 = (bf16[2,256,128]{2,1,0:T(8,128)(2,1)S(1)}, bf16[2,256,128]{2,1,0:T(8,128)(2,1)S(1)}, u32[]{:S(2)}, u32[]{:S(2)}) collective-permute-start(bf16[2,256,128]{2,1,0:T(8,128)(2,1)S(1)} %get-tuple-element.86), channel_id=1, source_target_pairs={{0,6},{2,4},{4,2},{6,0},{8,14},{10,12},{12,10},{14,8},{1,7},{3,5},... | collective-permute-start | bytes 393224 | tf_op jit(solution)/shard_map/ppermute | solution.py:498
  69.7 0.0 collective-permute-done.7.refs_9_.refs_3_.refs_7_
  69.7 0.7 collective-permute-done.8.refs_10_.refs_4_.refs_8_
  70.4 1.2 %pick_states.5 = (bf16[2,256,128]{2,1,0:T(8,128)(2,1)S(1)}, bf16[2,256,128]{2,1,0:T(8,128)(2,1)S(1)}, bf16[2,256,128]{2,1,0:T(8,128)(2,1)S(1)}, bf16[2,256,128]{2,1,0:T(8,128)(2,1)S(1)}) custom-call(s32[8]{0:T(128)S(1)} %broadcast_xor_fusion.refs_10_.refs_0_, bf16[1056,128]{1,0:T(8,128)(2,1)S(1)} %get-tuple-element.46.refs_9_.refs_1_, ...), custom_call_target="tpu_custom_call" | custom-call | flops 1 | bytes 1 | tf_op jit(solution)/shard_map/pick_states/pallas_call | solution.py:563
  71.6 1.6 %collective-permute-start.11 = (bf16[2,256,128]{2,1,0:T(8,128)(2,1)S(1)}, bf16[2,256,128]{2,1,0:T(8,128)(2,1)S(1)}, u32[]{:S(2)}, u32[]{:S(2)}) collective-permute-start(bf16[2,256,128]{2,1,0:T(8,128)(2,1)S(1)} %get-tuple-element.71), channel_id=1, source_target_pairs={{0,2},{2,0},{4,6},{6,4},{8,10},{10,8},{12,14},{14,12},{1,3},{3,1},... | collective-permute-start | bytes 393224 | tf_op jit(solution)/shard_map/ppermute | solution.py:498
  73.2 0.4 collective-permute-start.12
  73.6 0.0 collective-permute-done.14.refs_10_
  73.6 1.6 %collective-permute-start.13 = (bf16[2,256,128]{2,1,0:T(8,128)(2,1)S(1)}, bf16[2,256,128]{2,1,0:T(8,128)(2,1)S(1)}, u32[]{:S(2)}, u32[]{:S(2)}) collective-permute-start(bf16[2,256,128]{2,1,0:T(8,128)(2,1)S(1)} %get-tuple-element.73), channel_id=1, source_target_pairs={{0,6},{2,4},{4,2},{6,0},{8,14},{10,12},{12,10},{14,8},{1,7},{3,5},... | collective-permute-start | bytes 393224 | tf_op jit(solution)/shard_map/ppermute | solution.py:498
  75.2 0.0 collective-permute-done.15.refs_11_
  75.2 1.2 %collective-permute-done.16.refs_12_ = bf16[2,256,128]{2,1,0:T(8,128)(2,1)S(1)} collective-permute-done((bf16[2,256,128]{2,1,0:T(8,128)(2,1)S(1)}, bf16[2,256,128]{2,1,0:T(8,128)(2,1)S(1)}, u32[]{:S(2)}, u32[]{:S(2)}) %collective-permute-start.16) | collective-permute-done | bytes 131104 | tf_op jit(solution)/shard_map/ppermute | solution.py:498
  76.4 5.7 %late.2.refs_21_ = bf16[2,256,4096]{2,1,0:T(8,128)(2,1)} custom-call(s32[1]{0:T(128)} %bitcast.place_ref.refs_0_, bf16[2,544,128]{2,1,0:T(8,128)(2,1)S(1)} %get-tuple-element.65.refs_6_.refs_7_.refs_1_.refs_5_, bf16[2,544,128]{2,1,0:T(8,128)(2,1)S(1)} %collective-permute-done.6.refs_8_.refs_2_.refs_6_, ...), custom_call_target="tpu_custom_call" | custom-call | flops 1 | bytes 1 | tf_op jit(solution)/shard_map/late/pallas_call | solution.py:645
  82.1 0.0 collective-permute-done.11.refs_6_
  82.1 2.9 %late.3 = bf16[2,256,4096]{2,1,0:T(8,128)(2,1)} custom-call(s32[1]{0:T(128)} %bitcast.place_ref.refs_0_, bf16[2,544,128]{2,1,0:T(8,128)(2,1)S(1)} %get-tuple-element.65.refs_6_.refs_7_.refs_1_.refs_5_, bf16[2,544,128]{2,1,0:T(8,128)(2,1)S(1)} %collective-permute-done.6.refs_8_.refs_2_.refs_6_, ...), custom_call_target="tpu_custom_call", output_to_operand_aliasing={{}: (21, {})} | custom-call | flops 1 | bytes 1 | tf_op jit(solution)/shard_map/late/pallas_call | solution.py:645
  (19 shorter events, 0.1 us)
Async XLA Ops:
  0.0 9.3 %copy-start.3 = (s32[8]{0:T(128)S(1)}, s32[8]{0:T(128)}, u32[]{:S(2)}) copy-start(s32[8]{0:T(128)} %param.26) | copy-start | bytes 100
  0.0 9.4 %copy-start.4 = (s32[16]{0:T(128)S(1)}, s32[16]{0:T(128)}, u32[]{:S(2)}) copy-start(s32[16]{0:T(128)} %param.27) | copy-start | bytes 196
  0.0 9.7 %copy-start = (f32[64]{0:T(128)S(1)}, f32[64]{0:T(128)}, u32[]{:S(2)}) copy-start(f32[64]{0:T(128)} %param.18) | copy-start | bytes 772
  0.0 9.8 %copy-start.1 = (f32[64]{0:T(128)S(1)}, f32[64]{0:T(128)}, u32[]{:S(2)}) copy-start(f32[64]{0:T(128)} %param.19) | copy-start | bytes 772
  0.0 9.9 %copy-start.2 = (f32[64]{0:T(128)S(1)}, f32[64]{0:T(128)}, u32[]{:S(2)}) copy-start(f32[64]{0:T(128)} %param.20) | copy-start | bytes 772
  1.8 25.2 %collective-permute-start.1 = (bf16[1056,128]{1,0:T(8,128)(2,1)S(1)}, bf16[1056,128]{1,0:T(8,128)(2,1)S(1)}, u32[]{:S(2)}, u32[]{:S(2)}) collective-permute-start(bf16[1056,128]{1,0:T(8,128)(2,1)S(1)} %get-tuple-element.48), channel_id=1, source_target_pairs={{0,4},{2,6},{4,0},{6,2},{8,12},{10,14},{12,8},{14,10},{1,5},{3,7},... | collective-permute-start | bytes 811016 | tf_op jit(solution)/shard_map/ppermute | solution.py:498
  4.9 32.8 %collective-permute-start.3 = (bf16[2,544,128]{2,1,0:T(8,128)(2,1)S(1)}, bf16[2,544,128]{2,1,0:T(8,128)(2,1)S(1)}, u32[]{:S(2)}, u32[]{:S(2)}) collective-permute-start(bf16[2,544,128]{2,1,0:T(8,128)(2,1)S(1)} %get-tuple-element.50), channel_id=1, source_target_pairs={{0,8},{2,10},{4,12},{6,14},{8,0},{10,2},{12,4},{14,6},{1,9},{3,11}... | collective-permute-start | bytes 835592 | tf_op jit(solution)/shard_map/ppermute | solution.py:498
  7.5 30.2 %collective-permute-start.4 = (bf16[2,544,128]{2,1,0:T(8,128)(2,1)S(1)}, bf16[2,544,128]{2,1,0:T(8,128)(2,1)S(1)}, u32[]{:S(2)}, u32[]{:S(2)}) collective-permute-start(bf16[2,544,128]{2,1,0:T(8,128)(2,1)S(1)} %get-tuple-element.51), channel_id=1, source_target_pairs={{0,12},{2,14},{4,8},{6,10},{8,4},{10,6},{12,0},{14,2},{1,13},{3,15... | collective-permute-start | bytes 835592 | tf_op jit(solution)/shard_map/ppermute | solution.py:498
  7.5 13.5 %collective-permute-start = (bf16[2,1056,128]{2,1,0:T(8,128)(2,1)S(1)}, bf16[2,1056,128]{2,1,0:T(8,128)(2,1)S(1)}, u32[]{:S(2)}, u32[]{:S(2)}) collective-permute-start(bf16[2,1056,128]{2,1,0:T(8,128)(2,1)S(1)} %get-tuple-element.47), channel_id=1, source_target_pairs={{0,2},{2,0},{4,6},{6,4},{8,10},{10,8},{12,14},{14,12},{1,3},{3,1},... | collective-permute-start | bytes 1622024 | tf_op jit(solution)/shard_map/ppermute | solution.py:498
  21.0 11.3 %collective-permute-start.2 = (bf16[1056,128]{1,0:T(8,128)(2,1)S(1)}, bf16[1056,128]{1,0:T(8,128)(2,1)S(1)}, u32[]{:S(2)}, u32[]{:S(2)}) collective-permute-start(bf16[1056,128]{1,0:T(8,128)(2,1)S(1)} %stack_turn.1.refs_9_), channel_id=1, source_target_pairs={{0,4},{2,6},{4,0},{6,2},{8,12},{10,14},{12,8},{14,10},{1,5},{3,7},... | collective-permute-start | bytes 811016 | tf_op jit(solution)/shard_map/ppermute | solution.py:498
  37.8 8.6 %collective-permute-start.5 = (bf16[2,544,128]{2,1,0:T(8,128)(2,1)S(1)}, bf16[2,544,128]{2,1,0:T(8,128)(2,1)S(1)}, u32[]{:S(2)}, u32[]{:S(2)}) collective-permute-start(bf16[2,544,128]{2,1,0:T(8,128)(2,1)S(1)} %stack_first.1.refs_5_), channel_id=1, source_target_pairs={{0,2},{2,0},{4,6},{6,4},{8,10},{10,8},{12,14},{14,12},{1,3},{3,1},... | collective-permute-start | bytes 835592 | tf_op jit(solution)/shard_map/ppermute | solution.py:498
  39.4 13.5 %collective-permute-start.10 = (bf16[4,256,128]{2,1,0:T(8,128)(2,1)S(1)}, bf16[4,256,128]{2,1,0:T(8,128)(2,1)S(1)}, u32[]{:S(2)}, u32[]{:S(2)}) collective-permute-start(bf16[4,256,128]{2,1,0:T(8,128)(2,1)S(1)} %stack_later.2.refs_9_), channel_id=1, source_target_pairs={{0,8},{2,10},{4,12},{6,14},{8,0},{10,2},{12,4},{14,6},{1,9},{3,11}... | collective-permute-start | bytes 786440 | tf_op jit(solution)/shard_map/ppermute | solution.py:498
  47.5 21.3 %collective-permute-start.6 = (bf16[2,544,128]{2,1,0:T(8,128)(2,1)S(1)}, bf16[2,544,128]{2,1,0:T(8,128)(2,1)S(1)}, u32[]{:S(2)}, u32[]{:S(2)}) collective-permute-start(bf16[2,544,128]{2,1,0:T(8,128)(2,1)S(1)} %get-tuple-element.66), channel_id=1, source_target_pairs={{0,2},{2,0},{4,6},{6,4},{8,10},{10,8},{12,14},{14,12},{1,3},{3,1},... | collective-permute-start | bytes 835592 | tf_op jit(solution)/shard_map/ppermute | solution.py:498
  49.1 20.6 %collective-permute-start.7 = (bf16[2,544,128]{2,1,0:T(8,128)(2,1)S(1)}, bf16[2,544,128]{2,1,0:T(8,128)(2,1)S(1)}, u32[]{:S(2)}, u32[]{:S(2)}) collective-permute-start(bf16[2,544,128]{2,1,0:T(8,128)(2,1)S(1)} %get-tuple-element.67), channel_id=1, source_target_pairs={{0,4},{2,6},{4,0},{6,2},{8,12},{10,14},{12,8},{14,10},{1,5},{3,7},... | collective-permute-start | bytes 835592 | tf_op jit(solution)/shard_map/ppermute | solution.py:498
  49.1 21.3 %collective-permute-start.8 = (bf16[2,544,128]{2,1,0:T(8,128)(2,1)S(1)}, bf16[2,544,128]{2,1,0:T(8,128)(2,1)S(1)}, u32[]{:S(2)}, u32[]{:S(2)}) collective-permute-start(bf16[2,544,128]{2,1,0:T(8,128)(2,1)S(1)} %get-tuple-element.68), channel_id=1, source_target_pairs={{0,6},{2,4},{4,2},{6,0},{8,14},{10,12},{12,10},{14,8},{1,7},{3,5},... | collective-permute-start | bytes 835592 | tf_op jit(solution)/shard_map/ppermute | solution.py:498
  51.1 14.9 %collective-permute-start.9 = (bf16[4,256,128]{2,1,0:T(8,128)(2,1)S(1)}, bf16[4,256,128]{2,1,0:T(8,128)(2,1)S(1)}, u32[]{:S(2)}, u32[]{:S(2)}) collective-permute-start(bf16[4,256,128]{2,1,0:T(8,128)(2,1)S(1)} %stack_later.3.refs_9_), channel_id=1, source_target_pairs={{0,8},{2,10},{4,12},{6,14},{8,0},{10,2},{12,4},{14,6},{1,9},{3,11}... | collective-permute-start | bytes 786440 | tf_op jit(solution)/shard_map/ppermute | solution.py:498
  54.0 19.6 %collective-permute-start.14 = (bf16[2,256,128]{2,1,0:T(8,128)(2,1)S(1)}, bf16[2,256,128]{2,1,0:T(8,128)(2,1)S(1)}, u32[]{:S(2)}, u32[]{:S(2)}) collective-permute-start(bf16[2,256,128]{2,1,0:T(8,128)(2,1)S(1)} %get-tuple-element.84), channel_id=1, source_target_pairs={{0,2},{2,0},{4,6},{6,4},{8,10},{10,8},{12,14},{14,12},{1,3},{3,1},... | collective-permute-start | bytes 393224 | tf_op jit(solution)/shard_map/ppermute | solution.py:498
  66.0 9.2 %collective-permute-start.15 = (bf16[2,256,128]{2,1,0:T(8,128)(2,1)S(1)}, bf16[2,256,128]{2,1,0:T(8,128)(2,1)S(1)}, u32[]{:S(2)}, u32[]{:S(2)}) collective-permute-start(bf16[2,256,128]{2,1,0:T(8,128)(2,1)S(1)} %get-tuple-element.85), channel_id=1, source_target_pairs={{0,4},{2,6},{4,0},{6,2},{8,12},{10,14},{12,8},{14,10},{1,5},{3,7},... | collective-permute-start | bytes 393224 | tf_op jit(solution)/shard_map/ppermute | solution.py:498
  68.8 7.6 %collective-permute-start.16 = (bf16[2,256,128]{2,1,0:T(8,128)(2,1)S(1)}, bf16[2,256,128]{2,1,0:T(8,128)(2,1)S(1)}, u32[]{:S(2)}, u32[]{:S(2)}) collective-permute-start(bf16[2,256,128]{2,1,0:T(8,128)(2,1)S(1)} %get-tuple-element.86), channel_id=1, source_target_pairs={{0,6},{2,4},{4,2},{6,0},{8,14},{10,12},{12,10},{14,8},{1,7},{3,5},... | collective-permute-start | bytes 393224 | tf_op jit(solution)/shard_map/ppermute | solution.py:498
  71.6 10.5 %collective-permute-start.11 = (bf16[2,256,128]{2,1,0:T(8,128)(2,1)S(1)}, bf16[2,256,128]{2,1,0:T(8,128)(2,1)S(1)}, u32[]{:S(2)}, u32[]{:S(2)}) collective-permute-start(bf16[2,256,128]{2,1,0:T(8,128)(2,1)S(1)} %get-tuple-element.71), channel_id=1, source_target_pairs={{0,2},{2,0},{4,6},{6,4},{8,10},{10,8},{12,14},{14,12},{1,3},{3,1},... | collective-permute-start | bytes 393224 | tf_op jit(solution)/shard_map/ppermute | solution.py:498
  73.2 8.9 %collective-permute-start.12 = (bf16[2,256,128]{2,1,0:T(8,128)(2,1)S(1)}, bf16[2,256,128]{2,1,0:T(8,128)(2,1)S(1)}, u32[]{:S(2)}, u32[]{:S(2)}) collective-permute-start(bf16[2,256,128]{2,1,0:T(8,128)(2,1)S(1)} %get-tuple-element.72), channel_id=1, source_target_pairs={{0,4},{2,6},{4,0},{6,2},{8,12},{10,14},{12,8},{14,10},{1,5},{3,7},... | collective-permute-start | bytes 393224 | tf_op jit(solution)/shard_map/ppermute | solution.py:498
  73.6 8.5 %collective-permute-start.13 = (bf16[2,256,128]{2,1,0:T(8,128)(2,1)S(1)}, bf16[2,256,128]{2,1,0:T(8,128)(2,1)S(1)}, u32[]{:S(2)}, u32[]{:S(2)}) collective-permute-start(bf16[2,256,128]{2,1,0:T(8,128)(2,1)S(1)} %get-tuple-element.73), channel_id=1, source_target_pairs={{0,6},{2,4},{4,2},{6,0},{8,14},{10,12},{12,10},{14,8},{1,7},{3,5},... | collective-permute-start | bytes 393224 | tf_op jit(solution)/shard_map/ppermute | solution.py:498

commit v19 on v17

--- a/solution.py
+++ b/solution.py
@@ -8,7 +8,7 @@
 from jax.sharding import PartitionSpec as P
 
 VMEM_LIMIT = 12 * 1024 * 1024
-SPLIT = (8, 4, 4)
+SPLIT = (8, 6, 2)
 FIX = 16
 LOG2_E = 1.4426950408889634
 
@@ -500,7 +500,7 @@
     def cast():
         rows = per_group * width + tail_lines
         rows_a = SPLIT[0] * width + tail_lines
-        blocks = [(0, SPLIT[0])] + [(at, 4) for at in range(SPLIT[0], per_group, 4)]
+        blocks = [(0, SPLIT[0])] + [(at, 2) for at in range(SPLIT[0], per_group, 2)]
         count = len(blocks) + 2
 
         def kernel(place_ref, *refs):
@@ -700,8 +700,8 @@
     sent_c, crossed_c = cross(2, [states[0][0], crossed_b])
     states.append(pick_later(1, crossed_b, [sent_c]))
     states.append(pick_later(2, crossed_c, [states[1][0]]))
-    result = late([0, 1], states, parts, None, [states[2][0]])
-    return late([2], states, parts, result, [])
+    result = late([0], states, parts, None, [states[2][0]])
+    return late([1, 2], states, parts, result, [])
 
 
 def solution(mesh):

time: 79.4 us -> 82.2 us (1.035)
  waiting for transfers between devices: 17 us -> 24.3 us
  starting transfers between devices: 26.8 us -> 23.1 us
    ppermute x17, waiting for transfers between devices: 17 us -> 24.3 us  [swap(): return lax.ppermute(value, 'batch', perm=[(i, i ^ r) for i in range(8)])]
    ppermute x17, starting transfers between devices: 26.8 us -> 23.1 us  [swap(): return lax.ppermute(value, 'batch', perm=[(i, i ^ r) for i in range(8)])]
  transfers between devices with their start and end apart: 17 -> 17, of which waited for: 6 -> 9; matrix products, arithmetic and copies ran while one was open for 1% -> 1% of each run, Pallas kernels for 37% -> 34%
where the time goes in v19:
time: 82.2 us; the launch traced here: 82 us
  Pallas kernels  33.5 us (41%)
  waiting for transfers between devices  24.3 us (30%)
  starting transfers between devices  23.1 us (28%)
    ppermute x17, waiting for transfers between devices, swap(): return lax.ppermute(value, 'batch', perm=[(i, i ^ r) for i in range(8)])  24.3 us
    ppermute x17, starting transfers between devices, swap(): return lax.ppermute(value, 'batch', perm=[(i, i ^ r) for i in range(8)])  23.1 us
    pallas_call x3, Pallas kernels, early(): pl.pallas_call(functools.partial(drop_tokens, functools.partial(early_ker...  20.4 us
    pallas_call x2, Pallas kernels, late(): pl.pallas_call(functools.partial(drop_tokens, kernel, keep, 1 + len(opera...  7.83 us
    pallas_call x7, Pallas kernels, rearrange(): pl.pallas_call(functools.partial(drop_tokens, kernel, 1 + len(sources), l...  3.45 us
    pallas_call x1, Pallas kernels, cast(): pl.pallas_call(kernel, grid_spec=pltpu.PrefetchScalarGridSpec(num_scalar_...  1.79 us
  transfers between devices with their start and end apart: 17, of which 9 were waited for; matrix products, arithmetic and copies ran while one was open for 1% of the time, Pallas kernels for 34%

profile of v19, /device:TPU:0, one launch (start us, length us, event | category | flops | bytes accessed | tf_op | source)
XLA Modules:
  0.0 82.0 jit_solution(2378507764827610947)
XLA Ops:
  0.0 1.8 %cast_states.1 = (bf16[1056,128]{1,0:T(8,128)(2,1)S(1)}, bf16[1056,128]{1,0:T(8,128)(2,1)S(1)}, bf16[2,1056,128]{2,1,0:T(8,128)(2,1)S(1)}, bf16[2,544,128]{2,1,0:T(8,128)(2,1)S(1)}, bf16[2,544,128]{2,1,0:T(8,128)(2,1)S(1)}) custom-call(s32[1]{0:T(128)} %bitcast.place_ref.refs_0_, f32[4,16,64,128]{3,2,1,0:T(8,128)} %bitcast.5, f32[4,16,64,128]{3,2,1,0:T(8,128)} %bitcast.6, ...), custom_call_target="tpu_custom_call" | custom-call | flops 1 | bytes 1 | tf_op jit(solution)/shard_map/cast_states/pallas_call | solution.py:531
  1.8 3.1 %collective-permute-start.1 = (bf16[1056,128]{1,0:T(8,128)(2,1)S(1)}, bf16[1056,128]{1,0:T(8,128)(2,1)S(1)}, u32[]{:S(2)}, u32[]{:S(2)}) collective-permute-start(bf16[1056,128]{1,0:T(8,128)(2,1)S(1)} %get-tuple-element.42), channel_id=1, source_target_pairs={{0,4},{2,6},{4,0},{6,2},{8,12},{10,14},{12,8},{14,10},{1,5},{3,7},... | collective-permute-start | bytes 811016 | tf_op jit(solution)/shard_map/ppermute | solution.py:498
  4.9 2.6 %collective-permute-start.3 = (bf16[2,544,128]{2,1,0:T(8,128)(2,1)S(1)}, bf16[2,544,128]{2,1,0:T(8,128)(2,1)S(1)}, u32[]{:S(2)}, u32[]{:S(2)}) collective-permute-start(bf16[2,544,128]{2,1,0:T(8,128)(2,1)S(1)} %get-tuple-element.44), channel_id=1, source_target_pairs={{0,8},{2,10},{4,12},{6,14},{8,0},{10,2},{12,4},{14,6},{1,9},{3,11}... | collective-permute-start | bytes 835592 | tf_op jit(solution)/shard_map/ppermute | solution.py:498
  7.5 0.0 collective-permute-start.4
  7.5 1.7 %collective-permute-start = (bf16[2,1056,128]{2,1,0:T(8,128)(2,1)S(1)}, bf16[2,1056,128]{2,1,0:T(8,128)(2,1)S(1)}, u32[]{:S(2)}, u32[]{:S(2)}) collective-permute-start(bf16[2,1056,128]{2,1,0:T(8,128)(2,1)S(1)} %get-tuple-element.41), channel_id=1, source_target_pairs={{0,2},{2,0},{4,6},{6,4},{8,10},{10,8},{12,14},{14,12},{1,3},{3,1},... | collective-permute-start | bytes 1622024 | tf_op jit(solution)/shard_map/ppermute | solution.py:498
  9.2 0.1 select_reduce_fusion.1
  9.4 0.1 convert_reduce_fusion
  9.5 0.2 select_reduce_fusion
  9.7 0.1 copy.28.refs_4_
  9.8 0.1 copy.29.refs_5_
  9.9 0.1 broadcast_in_dim.55
  9.9 0.1 broadcast_in_dim_reshape.3.refs_6_
  10.0 9.6 %early.3 = (f32[4,256,1024]{2,1,0:T(8,128)S(1)}, bf16[4,256,128]{2,1,0:T(8,128)(2,1)S(1)}, f32[4,16,256]{2,1,0:T(8,128)S(1)}, f32[4,256,256]{2,1,0:T(8,128)S(1)}...) custom-call(bf16[2,256,4096]{2,1,0:T(8,128)(2,1)} %refs_0_.5, bf16[2,256,512]{2,1,0:T(8,128)(2,1)} %refs_1_.5, ...), custom_call_target="tpu_custom_call" | custom-call | flops 1 | bytes 1 | tf_op jit(solution)/shard_map/early/pallas_call | solution.py:596
  19.7 1.3 %collective-permute-done.refs_1_.refs_2_ = bf16[2,1056,128]{2,1,0:T(8,128)(2,1)S(1)} collective-permute-done((bf16[2,1056,128]{2,1,0:T(8,128)(2,1)S(1)}, bf16[2,1056,128]{2,1,0:T(8,128)(2,1)S(1)}, u32[]{:S(2)}, u32[]{:S(2)}) %collective-permute-start) | collective-permute-done | bytes 540704 | tf_op jit(solution)/shard_map/ppermute | solution.py:498
  21.0 0.7 collective-permute-start.2
  21.7 5.4 %early.4 = (f32[4,256,1024]{2,1,0:T(8,128)S(1)}, bf16[4,256,128]{2,1,0:T(8,128)(2,1)S(1)}, f32[4,16,256]{2,1,0:T(8,128)S(1)}, f32[4,256,256]{2,1,0:T(8,128)S(1)}...) custom-call(bf16[2,256,4096]{2,1,0:T(8,128)(2,1)} %refs_0_.5, bf16[2,256,512]{2,1,0:T(8,128)(2,1)} %refs_1_.5, ...), custom_call_target="tpu_custom_call" | custom-call | flops 1 | bytes 1 | tf_op jit(solution)/shard_map/early/pallas_call | solution.py:596
  27.0 0.3 collective-permute-done.3.refs_1_.refs_5_
  27.4 1.6 %collective-permute-start.5 = (bf16[2,544,128]{2,1,0:T(8,128)(2,1)S(1)}, bf16[2,544,128]{2,1,0:T(8,128)(2,1)S(1)}, u32[]{:S(2)}, u32[]{:S(2)}) collective-permute-start(bf16[2,544,128]{2,1,0:T(8,128)(2,1)S(1)} %stack_first.1.refs_5_), channel_id=1, source_target_pairs={{0,2},{2,0},{4,6},{6,4},{8,10},{10,8},{12,14},{14,12},{1,3},{3,1},... | collective-permute-start | bytes 835592 | tf_op jit(solution)/shard_map/ppermute | solution.py:498
  29.0 0.0 collective-permute-done.1.refs_3_
  29.0 3.3 %collective-permute-done.2.refs_4_ = bf16[1056,128]{1,0:T(8,128)(2,1)S(1)} collective-permute-done((bf16[1056,128]{1,0:T(8,128)(2,1)S(1)}, bf16[1056,128]{1,0:T(8,128)(2,1)S(1)}, u32[]{:S(2)}, u32[]{:S(2)}) %collective-permute-start.2) | collective-permute-done | bytes 270368 | tf_op jit(solution)/shard_map/ppermute | solution.py:498
  32.3 2.9 %collective-permute-start.9 = (bf16[4,384,128]{2,1,0:T(8,128)(2,1)S(1)}, bf16[4,384,128]{2,1,0:T(8,128)(2,1)S(1)}, u32[]{:S(2)}, u32[]{:S(2)}) collective-permute-start(bf16[4,384,128]{2,1,0:T(8,128)(2,1)S(1)} %stack_later.2.refs_9_), channel_id=1, source_target_pairs={{0,8},{2,10},{4,12},{6,14},{8,0},{10,2},{12,4},{14,6},{1,9},{3,11}... | collective-permute-start | bytes 1179656 | tf_op jit(solution)/shard_map/ppermute | solution.py:498
  35.2 5.4 %early.5 = (f32[4,256,1024]{2,1,0:T(8,128)S(1)}, bf16[4,256,128]{2,1,0:T(8,128)(2,1)S(1)}, f32[4,16,256]{2,1,0:T(8,128)S(1)}, f32[4,256,256]{2,1,0:T(8,128)S(1)}...) custom-call(bf16[2,256,4096]{2,1,0:T(8,128)(2,1)} %refs_0_.5, ...), custom_call_target="tpu_custom_call", output_to_operand_aliasing={{0}: (10, {}), {1}: (11, {}), {2}: (12, {}), {3}: (13, {}),... | custom-call | flops 1 | bytes 1 | tf_op jit(solution)/shard_map/early/pallas_call | solution.py:596
  40.5 0.0 collective-permute-done.5.refs_7_
  40.6 1.1 %pick_states.3 = (bf16[2,544,128]{2,1,0:T(8,128)(2,1)S(1)}, bf16[2,544,128]{2,1,0:T(8,128)(2,1)S(1)}, bf16[2,544,128]{2,1,0:T(8,128)(2,1)S(1)}, bf16[2,544,128]{2,1,0:T(8,128)(2,1)S(1)}) custom-call(s32[8]{0:T(128)S(1)} %broadcast_xor_fusion.refs_10_.refs_0_, bf16[1056,128]{1,0:T(8,128)(2,1)S(1)} %get-tuple-element.40.refs_9_.refs_1_, ...), custom_call_target="tpu_custom_call" | custom-call | flops 1 | bytes 1 | tf_op jit(solution)/shard_map/pick_states/pallas_call | solution.py:563
  41.7 0.6 collective-permute-start.6
  42.2 0.7 collective-permute-start.7
  42.9 2.3 %collective-permute-start.8 = (bf16[2,544,128]{2,1,0:T(8,128)(2,1)S(1)}, bf16[2,544,128]{2,1,0:T(8,128)(2,1)S(1)}, u32[]{:S(2)}, u32[]{:S(2)}) collective-permute-start(bf16[2,544,128]{2,1,0:T(8,128)(2,1)S(1)} %get-tuple-element.56), channel_id=1, source_target_pairs={{0,6},{2,4},{4,2},{6,0},{8,14},{10,12},{12,10},{14,8},{1,7},{3,5},... | collective-permute-start | bytes 835592 | tf_op jit(solution)/shard_map/ppermute | solution.py:498
  45.2 7.3 %collective-permute-done.9.refs_6_.refs_5_ = bf16[4,384,128]{2,1,0:T(8,128)(2,1)S(1)} collective-permute-done((bf16[4,384,128]{2,1,0:T(8,128)(2,1)S(1)}, bf16[4,384,128]{2,1,0:T(8,128)(2,1)S(1)}, u32[]{:S(2)}, u32[]{:S(2)}) %collective-permute-start.9) | collective-permute-done | bytes 393248 | tf_op jit(solution)/shard_map/ppermute | solution.py:498
  52.5 0.1 collective-permute-start.13
  52.6 1.1 %pick_states.4 = (bf16[2,384,128]{2,1,0:T(8,128)(2,1)S(1)}, bf16[2,384,128]{2,1,0:T(8,128)(2,1)S(1)}, bf16[2,384,128]{2,1,0:T(8,128)(2,1)S(1)}, bf16[2,384,128]{2,1,0:T(8,128)(2,1)S(1)}) custom-call(s32[8]{0:T(128)S(1)} %broadcast_xor_fusion.refs_10_.refs_0_, bf16[1056,128]{1,0:T(8,128)(2,1)S(1)} %get-tuple-element.40.refs_9_.refs_1_, ...), custom_call_target="tpu_custom_call" | custom-call | flops 1 | bytes 1 | tf_op jit(solution)/shard_map/pick_states/pallas_call | solution.py:563
  53.7 0.9 %collective-permute-start.10 = (bf16[2,384,128]{2,1,0:T(8,128)(2,1)S(1)}, bf16[2,384,128]{2,1,0:T(8,128)(2,1)S(1)}, u32[]{:S(2)}, u32[]{:S(2)}) collective-permute-start(bf16[2,384,128]{2,1,0:T(8,128)(2,1)S(1)} %get-tuple-element.58), channel_id=1, source_target_pairs={{0,2},{2,0},{4,6},{6,4},{8,10},{10,8},{12,14},{14,12},{1,3},{3,1},... | collective-permute-start | bytes 589832 | tf_op jit(solution)/shard_map/ppermute | solution.py:498
  54.6 0.0 collective-permute-done.6.refs_2_.refs_6_
  54.6 2.8 %collective-permute-start.11 = (bf16[2,384,128]{2,1,0:T(8,128)(2,1)S(1)}, bf16[2,384,128]{2,1,0:T(8,128)(2,1)S(1)}, u32[]{:S(2)}, u32[]{:S(2)}) collective-permute-start(bf16[2,384,128]{2,1,0:T(8,128)(2,1)S(1)} %get-tuple-element.59), channel_id=1, source_target_pairs={{0,4},{2,6},{4,0},{6,2},{8,12},{10,14},{12,8},{14,10},{1,5},{3,7},... | collective-permute-start | bytes 589832 | tf_op jit(solution)/shard_map/ppermute | solution.py:498
  57.3 4.0 %collective-permute-done.13.refs_5_ = bf16[4,128,128]{2,1,0:T(8,128)(2,1)S(1)} collective-permute-done((bf16[4,128,128]{2,1,0:T(8,128)(2,1)S(1)}, bf16[4,128,128]{2,1,0:T(8,128)(2,1)S(1)}, u32[]{:S(2)}, u32[]{:S(2)}) %collective-permute-start.13) | collective-permute-done | bytes 131104 | tf_op jit(solution)/shard_map/ppermute | solution.py:498
  61.3 0.0 collective-permute-start.12
  61.3 1.2 %pick_states.5 = (bf16[2,128,128]{2,1,0:T(8,128)(2,1)S(1)}, bf16[2,128,128]{2,1,0:T(8,128)(2,1)S(1)}, bf16[2,128,128]{2,1,0:T(8,128)(2,1)S(1)}, bf16[2,128,128]{2,1,0:T(8,128)(2,1)S(1)}) custom-call(s32[8]{0:T(128)S(1)} %broadcast_xor_fusion.refs_10_.refs_0_, bf16[1056,128]{1,0:T(8,128)(2,1)S(1)} %get-tuple-element.40.refs_9_.refs_1_, ...), custom_call_target="tpu_custom_call" | custom-call | flops 1 | bytes 1 | tf_op jit(solution)/shard_map/pick_states/pallas_call | solution.py:563
  62.5 0.0 collective-permute-done.7.refs_3_.refs_7_
  62.5 1.2 %collective-permute-start.14 = (bf16[2,128,128]{2,1,0:T(8,128)(2,1)S(1)}, bf16[2,128,128]{2,1,0:T(8,128)(2,1)S(1)}, u32[]{:S(2)}, u32[]{:S(2)}) collective-permute-start(bf16[2,128,128]{2,1,0:T(8,128)(2,1)S(1)} %get-tuple-element.62), channel_id=1, source_target_pairs={{0,2},{2,0},{4,6},{6,4},{8,10},{10,8},{12,14},{14,12},{1,3},{3,1},... | collective-permute-start | bytes 196616 | tf_op jit(solution)/shard_map/ppermute | solution.py:498
  63.7 3.9 %collective-permute-done.8.refs_4_.refs_8_ = bf16[2,544,128]{2,1,0:T(8,128)(2,1)S(1)} collective-permute-done((bf16[2,544,128]{2,1,0:T(8,128)(2,1)S(1)}, bf16[2,544,128]{2,1,0:T(8,128)(2,1)S(1)}, u32[]{:S(2)}, u32[]{:S(2)}) %collective-permute-start.8) | collective-permute-done | bytes 278560 | tf_op jit(solution)/shard_map/ppermute | solution.py:498
  67.6 0.0 collective-permute-start.15
  67.6 0.5 collective-permute-done.14.refs_10_
  68.1 2.1 %collective-permute-start.16 = (bf16[2,128,128]{2,1,0:T(8,128)(2,1)S(1)}, bf16[2,128,128]{2,1,0:T(8,128)(2,1)S(1)}, u32[]{:S(2)}, u32[]{:S(2)}) collective-permute-start(bf16[2,128,128]{2,1,0:T(8,128)(2,1)S(1)} %get-tuple-element.64), channel_id=1, source_target_pairs={{0,6},{2,4},{4,2},{6,0},{8,14},{10,12},{12,10},{14,8},{1,7},{3,5},... | collective-permute-start | bytes 196616 | tf_op jit(solution)/shard_map/ppermute | solution.py:498
  70.2 3.9 %late.2.refs_25_ = bf16[2,256,4096]{2,1,0:T(8,128)(2,1)} custom-call(s32[1]{0:T(128)} %bitcast.place_ref.refs_0_, bf16[2,544,128]{2,1,0:T(8,128)(2,1)S(1)} %get-tuple-element.53.refs_5_.refs_1_, bf16[2,544,128]{2,1,0:T(8,128)(2,1)S(1)} %collective-permute-done.6.refs_2_.refs_6_, bf16[2,544,128]{2,1,0:T(8,128)(2,1)S(1)} %collective-permute-done.7.refs_3_.refs_7_, ...), custom_call_target="tpu_custom_call" | custom-call | flops 1 | bytes 1 | tf_op jit(solution)/shard_map/late/pallas_call | solution.py:645
  74.1 2.3 %collective-permute-done.15.refs_11_ = bf16[2,128,128]{2,1,0:T(8,128)(2,1)S(1)} collective-permute-done((bf16[2,128,128]{2,1,0:T(8,128)(2,1)S(1)}, bf16[2,128,128]{2,1,0:T(8,128)(2,1)S(1)}, u32[]{:S(2)}, u32[]{:S(2)}) %collective-permute-start.15) | collective-permute-done | bytes 65568 | tf_op jit(solution)/shard_map/ppermute | solution.py:498
  76.4 1.5 %collective-permute-done.16.refs_12_ = bf16[2,128,128]{2,1,0:T(8,128)(2,1)S(1)} collective-permute-done((bf16[2,128,128]{2,1,0:T(8,128)(2,1)S(1)}, bf16[2,128,128]{2,1,0:T(8,128)(2,1)S(1)}, u32[]{:S(2)}, u32[]{:S(2)}) %collective-permute-start.16) | collective-permute-done | bytes 65568 | tf_op jit(solution)/shard_map/ppermute | solution.py:498
  77.9 0.0 collective-permute-done.10.refs_6_
  77.9 0.0 collective-permute-done.11.refs_7_
  77.9 3.9 %late.3 = bf16[2,256,4096]{2,1,0:T(8,128)(2,1)} custom-call(s32[1]{0:T(128)} %bitcast.place_ref.refs_0_, bf16[2,544,128]{2,1,0:T(8,128)(2,1)S(1)} %get-tuple-element.53.refs_5_.refs_1_, bf16[2,544,128]{2,1,0:T(8,128)(2,1)S(1)} %collective-permute-done.6.refs_2_.refs_6_, ...), custom_call_target="tpu_custom_call", output_to_operand_aliasing={{}: (25, {})} | custom-call | flops 1 | bytes 1 | tf_op jit(solution)/shard_map/late/pallas_call | solution.py:645
  (18 shorter events, 0.1 us)
Async XLA Ops:
  0.0 9.2 %copy-start.3 = (s32[8]{0:T(128)S(1)}, s32[8]{0:T(128)}, u32[]{:S(2)}) copy-start(s32[8]{0:T(128)} %param.26) | copy-start | bytes 100
  0.0 9.4 %copy-start.4 = (s32[16]{0:T(128)S(1)}, s32[16]{0:T(128)}, u32[]{:S(2)}) copy-start(s32[16]{0:T(128)} %param.27) | copy-start | bytes 196
  0.0 9.6 %copy-start = (f32[64]{0:T(128)S(1)}, f32[64]{0:T(128)}, u32[]{:S(2)}) copy-start(f32[64]{0:T(128)} %param.18) | copy-start | bytes 772
  0.0 9.7 %copy-start.1 = (f32[64]{0:T(128)S(1)}, f32[64]{0:T(128)}, u32[]{:S(2)}) copy-start(f32[64]{0:T(128)} %param.19) | copy-start | bytes 772
  0.0 9.8 %copy-start.2 = (f32[64]{0:T(128)S(1)}, f32[64]{0:T(128)}, u32[]{:S(2)}) copy-start(f32[64]{0:T(128)} %param.20) | copy-start | bytes 772
  1.8 27.2 %collective-permute-start.1 = (bf16[1056,128]{1,0:T(8,128)(2,1)S(1)}, bf16[1056,128]{1,0:T(8,128)(2,1)S(1)}, u32[]{:S(2)}, u32[]{:S(2)}) collective-permute-start(bf16[1056,128]{1,0:T(8,128)(2,1)S(1)} %get-tuple-element.42), channel_id=1, source_target_pairs={{0,4},{2,6},{4,0},{6,2},{8,12},{10,14},{12,8},{14,10},{1,5},{3,7},... | collective-permute-start | bytes 811016 | tf_op jit(solution)/shard_map/ppermute | solution.py:498
  4.9 22.5 %collective-permute-start.3 = (bf16[2,544,128]{2,1,0:T(8,128)(2,1)S(1)}, bf16[2,544,128]{2,1,0:T(8,128)(2,1)S(1)}, u32[]{:S(2)}, u32[]{:S(2)}) collective-permute-start(bf16[2,544,128]{2,1,0:T(8,128)(2,1)S(1)} %get-tuple-element.44), channel_id=1, source_target_pairs={{0,8},{2,10},{4,12},{6,14},{8,0},{10,2},{12,4},{14,6},{1,9},{3,11}... | collective-permute-start | bytes 835592 | tf_op jit(solution)/shard_map/ppermute | solution.py:498
  7.5 19.9 %collective-permute-start.4 = (bf16[2,544,128]{2,1,0:T(8,128)(2,1)S(1)}, bf16[2,544,128]{2,1,0:T(8,128)(2,1)S(1)}, u32[]{:S(2)}, u32[]{:S(2)}) collective-permute-start(bf16[2,544,128]{2,1,0:T(8,128)(2,1)S(1)} %get-tuple-element.45), channel_id=1, source_target_pairs={{0,12},{2,14},{4,8},{6,10},{8,4},{10,6},{12,0},{14,2},{1,13},{3,15... | collective-permute-start | bytes 835592 | tf_op jit(solution)/shard_map/ppermute | solution.py:498
  7.5 13.5 %collective-permute-start = (bf16[2,1056,128]{2,1,0:T(8,128)(2,1)S(1)}, bf16[2,1056,128]{2,1,0:T(8,128)(2,1)S(1)}, u32[]{:S(2)}, u32[]{:S(2)}) collective-permute-start(bf16[2,1056,128]{2,1,0:T(8,128)(2,1)S(1)} %get-tuple-element.41), channel_id=1, source_target_pairs={{0,2},{2,0},{4,6},{6,4},{8,10},{10,8},{12,14},{14,12},{1,3},{3,1},... | collective-permute-start | bytes 1622024 | tf_op jit(solution)/shard_map/ppermute | solution.py:498
  21.0 11.3 %collective-permute-start.2 = (bf16[1056,128]{1,0:T(8,128)(2,1)S(1)}, bf16[1056,128]{1,0:T(8,128)(2,1)S(1)}, u32[]{:S(2)}, u32[]{:S(2)}) collective-permute-start(bf16[1056,128]{1,0:T(8,128)(2,1)S(1)} %stack_turn.1.refs_9_), channel_id=1, source_target_pairs={{0,4},{2,6},{4,0},{6,2},{8,12},{10,14},{12,8},{14,10},{1,5},{3,7},... | collective-permute-start | bytes 811016 | tf_op jit(solution)/shard_map/ppermute | solution.py:498
  27.4 13.1 %collective-permute-start.5 = (bf16[2,544,128]{2,1,0:T(8,128)(2,1)S(1)}, bf16[2,544,128]{2,1,0:T(8,128)(2,1)S(1)}, u32[]{:S(2)}, u32[]{:S(2)}) collective-permute-start(bf16[2,544,128]{2,1,0:T(8,128)(2,1)S(1)} %stack_first.1.refs_5_), channel_id=1, source_target_pairs={{0,2},{2,0},{4,6},{6,4},{8,10},{10,8},{12,14},{14,12},{1,3},{3,1},... | collective-permute-start | bytes 835592 | tf_op jit(solution)/shard_map/ppermute | solution.py:498
  32.3 20.2 %collective-permute-start.9 = (bf16[4,384,128]{2,1,0:T(8,128)(2,1)S(1)}, bf16[4,384,128]{2,1,0:T(8,128)(2,1)S(1)}, u32[]{:S(2)}, u32[]{:S(2)}) collective-permute-start(bf16[4,384,128]{2,1,0:T(8,128)(2,1)S(1)} %stack_later.2.refs_9_), channel_id=1, source_target_pairs={{0,8},{2,10},{4,12},{6,14},{8,0},{10,2},{12,4},{14,6},{1,9},{3,11}... | collective-permute-start | bytes 1179656 | tf_op jit(solution)/shard_map/ppermute | solution.py:498
  41.7 12.9 %collective-permute-start.6 = (bf16[2,544,128]{2,1,0:T(8,128)(2,1)S(1)}, bf16[2,544,128]{2,1,0:T(8,128)(2,1)S(1)}, u32[]{:S(2)}, u32[]{:S(2)}) collective-permute-start(bf16[2,544,128]{2,1,0:T(8,128)(2,1)S(1)} %get-tuple-element.54), channel_id=1, source_target_pairs={{0,2},{2,0},{4,6},{6,4},{8,10},{10,8},{12,14},{14,12},{1,3},{3,1},... | collective-permute-start | bytes 835592 | tf_op jit(solution)/shard_map/ppermute | solution.py:498
  42.2 20.3 %collective-permute-start.7 = (bf16[2,544,128]{2,1,0:T(8,128)(2,1)S(1)}, bf16[2,544,128]{2,1,0:T(8,128)(2,1)S(1)}, u32[]{:S(2)}, u32[]{:S(2)}) collective-permute-start(bf16[2,544,128]{2,1,0:T(8,128)(2,1)S(1)} %get-tuple-element.55), channel_id=1, source_target_pairs={{0,4},{2,6},{4,0},{6,2},{8,12},{10,14},{12,8},{14,10},{1,5},{3,7},... | collective-permute-start | bytes 835592 | tf_op jit(solution)/shard_map/ppermute | solution.py:498
  42.9 24.6 %collective-permute-start.8 = (bf16[2,544,128]{2,1,0:T(8,128)(2,1)S(1)}, bf16[2,544,128]{2,1,0:T(8,128)(2,1)S(1)}, u32[]{:S(2)}, u32[]{:S(2)}) collective-permute-start(bf16[2,544,128]{2,1,0:T(8,128)(2,1)S(1)} %get-tuple-element.56), channel_id=1, source_target_pairs={{0,6},{2,4},{4,2},{6,0},{8,14},{10,12},{12,10},{14,8},{1,7},{3,5},... | collective-permute-start | bytes 835592 | tf_op jit(solution)/shard_map/ppermute | solution.py:498
  52.5 8.8 %collective-permute-start.13 = (bf16[4,128,128]{2,1,0:T(8,128)(2,1)S(1)}, bf16[4,128,128]{2,1,0:T(8,128)(2,1)S(1)}, u32[]{:S(2)}, u32[]{:S(2)}) collective-permute-start(bf16[4,128,128]{2,1,0:T(8,128)(2,1)S(1)} %stack_later.3.refs_6_), channel_id=1, source_target_pairs={{0,8},{2,10},{4,12},{6,14},{8,0},{10,2},{12,4},{14,6},{1,9},{3,11}... | collective-permute-start | bytes 393224 | tf_op jit(solution)/shard_map/ppermute | solution.py:498
  53.7 24.3 %collective-permute-start.10 = (bf16[2,384,128]{2,1,0:T(8,128)(2,1)S(1)}, bf16[2,384,128]{2,1,0:T(8,128)(2,1)S(1)}, u32[]{:S(2)}, u32[]{:S(2)}) collective-permute-start(bf16[2,384,128]{2,1,0:T(8,128)(2,1)S(1)} %get-tuple-element.58), channel_id=1, source_target_pairs={{0,2},{2,0},{4,6},{6,4},{8,10},{10,8},{12,14},{14,12},{1,3},{3,1},... | collective-permute-start | bytes 589832 | tf_op jit(solution)/shard_map/ppermute | solution.py:498
  54.6 23.4 %collective-permute-start.11 = (bf16[2,384,128]{2,1,0:T(8,128)(2,1)S(1)}, bf16[2,384,128]{2,1,0:T(8,128)(2,1)S(1)}, u32[]{:S(2)}, u32[]{:S(2)}) collective-permute-start(bf16[2,384,128]{2,1,0:T(8,128)(2,1)S(1)} %get-tuple-element.59), channel_id=1, source_target_pairs={{0,4},{2,6},{4,0},{6,2},{8,12},{10,14},{12,8},{14,10},{1,5},{3,7},... | collective-permute-start | bytes 589832 | tf_op jit(solution)/shard_map/ppermute | solution.py:498
  61.3 16.7 %collective-permute-start.12 = (bf16[2,384,128]{2,1,0:T(8,128)(2,1)S(1)}, bf16[2,384,128]{2,1,0:T(8,128)(2,1)S(1)}, u32[]{:S(2)}, u32[]{:S(2)}) collective-permute-start(bf16[2,384,128]{2,1,0:T(8,128)(2,1)S(1)} %get-tuple-element.60), channel_id=1, source_target_pairs={{0,6},{2,4},{4,2},{6,0},{8,14},{10,12},{12,10},{14,8},{1,7},{3,5},... | collective-permute-start | bytes 589832 | tf_op jit(solution)/shard_map/ppermute | solution.py:498
  62.5 5.6 %collective-permute-start.14 = (bf16[2,128,128]{2,1,0:T(8,128)(2,1)S(1)}, bf16[2,128,128]{2,1,0:T(8,128)(2,1)S(1)}, u32[]{:S(2)}, u32[]{:S(2)}) collective-permute-start(bf16[2,128,128]{2,1,0:T(8,128)(2,1)S(1)} %get-tuple-element.62), channel_id=1, source_target_pairs={{0,2},{2,0},{4,6},{6,4},{8,10},{10,8},{12,14},{14,12},{1,3},{3,1},... | collective-permute-start | bytes 196616 | tf_op jit(solution)/shard_map/ppermute | solution.py:498
  67.6 8.8 %collective-permute-start.15 = (bf16[2,128,128]{2,1,0:T(8,128)(2,1)S(1)}, bf16[2,128,128]{2,1,0:T(8,128)(2,1)S(1)}, u32[]{:S(2)}, u32[]{:S(2)}) collective-permute-start(bf16[2,128,128]{2,1,0:T(8,128)(2,1)S(1)} %get-tuple-element.63), channel_id=1, source_target_pairs={{0,4},{2,6},{4,0},{6,2},{8,12},{10,14},{12,8},{14,10},{1,5},{3,7},... | collective-permute-start | bytes 196616 | tf_op jit(solution)/shard_map/ppermute | solution.py:498
  68.1 9.8 %collective-permute-start.16 = (bf16[2,128,128]{2,1,0:T(8,128)(2,1)S(1)}, bf16[2,128,128]{2,1,0:T(8,128)(2,1)S(1)}, u32[]{:S(2)}, u32[]{:S(2)}) collective-permute-start(bf16[2,128,128]{2,1,0:T(8,128)(2,1)S(1)} %get-tuple-element.64), channel_id=1, source_target_pairs={{0,6},{2,4},{4,2},{6,0},{8,14},{10,12},{12,10},{14,8},{1,7},{3,5},... | collective-permute-start | bytes 196616 | tf_op jit(solution)/shard_map/ppermute | solution.py:498

commit v20 on v19

--- a/solution.py
+++ b/solution.py
@@ -8,7 +8,7 @@
 from jax.sharding import PartitionSpec as P
 
 VMEM_LIMIT = 12 * 1024 * 1024
-SPLIT = (8, 6, 2)
+SPLIT = (6, 6, 4)
 FIX = 16
 LOG2_E = 1.4426950408889634
 
@@ -669,13 +669,20 @@
     crossed_a = [swap(sent_4, 4), swap(sent_6, 6)]
     along_y, along_z = swap(own_13, 1), swap(own_2, 2)
     parts = [early(0, 1, 0, [], [own, slots])]
-    (turn,) = rearrange(
-        place, [along_y], [(0, None, None, [(0, 1)])], [own.shape], [parts[0][1]], "stack_turn"
-    )
-    inside = [own, along_y, along_z, swap(turn, 2)]
+    spare = sum(rows[1:])
+    turn = rearrange(
+        place,
+        [along_y],
+        [(0, None, None, [(0, (1, chunks[0]))]), (1, None, None, [(0, (1, pl.ds(rows[0], spare)))])],
+        [(rows[0], size), (spare, size)],
+        [parts[0][1]],
+        "stack_turn",
+    )
+    inside = [own, along_y, along_z, swap(turn[0], 2), swap(turn[1], 2)]
 
     def inside_rows(k):
-        return [(0, chunks[k]), (1, (0, chunks[k])), (2, chunks[k]), (3, chunks[k])]
+        last = (3, None) if k == 0 else (4, pl.ds(sum(rows[1:k]), rows[k]))
+        return [(0, chunks[k]), (1, (0, chunks[k])), (2, chunks[k]), last]
 
     def cross(k, tokens):
         moves = [(0, j, None, [choice]) for j, choice in enumerate(inside_rows(k))]
@@ -683,25 +690,24 @@
         return sent, swap(sent, 4)
 
     def pick_later(k, crossed, tokens):
-        choices = inside_rows(k) + [(4, j) for j in range(4)]
+        choices = inside_rows(k) + [(5, j) for j in range(4)]
         return pick(rows[k], [*inside, crossed], choices, tokens)
 
-    second = early(1, 2, 0, [], [turn])
     moves = [(0, n, None, [(n, 1)]) for n in range(2)]
-    (spread,) = rearrange(
-        place, crossed_a, moves, [(2, rows[0], size)], [second[1]], "stack_first"
-    )
+    (spread,) = rearrange(place, crossed_a, moves, [(2, rows[0], size)], [turn[0]], "stack_first")
     passed = swap(spread, 1)
-    sent_b, crossed_b = cross(1, [spread])
-    second = early(1, 2, 1, second, [sent_b])
+    second = early(1, 2, 0, [], [spread])
+    sent_b, crossed_b = cross(1, [second[1], passed])
+    choices = inside_rows(0) + [(5, 0), (7, 0), (6, 0), (7, 1)]
+    states = [pick(rows[0], [*inside, *crossed_a, passed], choices, [sent_b])]
+    second = early(1, 2, 1, second, [states[0][0]])
     parts.append(second)
-    choices = inside_rows(0) + [(4, 0), (6, 0), (5, 0), (6, 1)]
-    states = [pick(rows[0], [*inside, *crossed_a, passed], choices, [second[1]])]
-    sent_c, crossed_c = cross(2, [states[0][0], crossed_b])
-    states.append(pick_later(1, crossed_b, [sent_c]))
-    states.append(pick_later(2, crossed_c, [states[1][0]]))
-    result = late([0], states, parts, None, [states[2][0]])
-    return late([1, 2], states, parts, result, [])
+    sent_c, crossed_c = cross(2, [second[1], crossed_b])
+    states.append(pick_later(1, crossed_b, [sent_c, *states[0]]))
+    result = late([0], states, parts, None, [states[1][0]])
+    states.append(pick_later(2, crossed_c, [stay(result)]))
+    result = late([1], states, parts, result, [states[2][0]])
+    return late([2], states, parts, result, [])
 
 
 def solution(mesh):

time: 82.2 us -> 80.3 us (0.977)
  waiting for transfers between devices: 24.3 us -> 18.6 us
  starting transfers between devices: 23.1 us -> 25.3 us
  Pallas kernels: 33.5 us -> 35.2 us
    ppermute x17 -> x18, waiting for transfers between devices: 24.3 us -> 18.6 us  [swap(): return lax.ppermute(value, 'batch', perm=[(i, i ^ r) for i in range(8)])]
    ppermute x17 -> x18, starting transfers between devices: 23.1 us -> 25.3 us  [swap(): return lax.ppermute(value, 'batch', perm=[(i, i ^ r) for i in range(8)])]
    pallas_call x2 -> x3, Pallas kernels: 7.83 us -> 9.52 us  [late(): pl.pallas_call(functools.partial(drop_tokens, kernel, keep, 1 + len(opera...]
  transfers between devices with their start and end apart: 17 -> 18, of which waited for: 9 -> 9; matrix products, arithmetic and copies ran while one was open for 1% -> 1% of each run, Pallas kernels for 34% -> 38%
where the time goes in v20:
time: 80.3 us; the launch traced here: 80.1 us
  Pallas kernels  35.2 us (44%)
  starting transfers between devices  25.3 us (32%)
  waiting for transfers between devices  18.6 us (23%)
    ppermute x18, starting transfers between devices, swap(): return lax.ppermute(value, 'batch', perm=[(i, i ^ r) for i in range(8)])  25.3 us
    pallas_call x3, Pallas kernels, early(): pl.pallas_call(functools.partial(drop_tokens, functools.partial(early_ker...  20.4 us
    ppermute x18, waiting for transfers between devices, swap(): return lax.ppermute(value, 'batch', perm=[(i, i ^ r) for i in range(8)])  18.6 us
    pallas_call x3, Pallas kernels, late(): pl.pallas_call(functools.partial(drop_tokens, kernel, keep, 1 + len(opera...  9.52 us
    pallas_call x7, Pallas kernels, rearrange(): pl.pallas_call(functools.partial(drop_tokens, kernel, 1 + len(sources), l...  3.45 us
    pallas_call x1, Pallas kernels, cast(): pl.pallas_call(kernel, grid_spec=pltpu.PrefetchScalarGridSpec(num_scalar_...  1.85 us
  transfers between devices with their start and end apart: 18, of which 9 were waited for; matrix products, arithmetic and copies ran while one was open for 1% of the time, Pallas kernels for 38%

profile of v20, /device:TPU:0, one launch (start us, length us, event | category | flops | bytes accessed | tf_op | source)
XLA Modules:
  0.0 80.1 jit_solution(11850284866535862907)
XLA Ops:
  0.0 1.8 %cast_states.1 = (bf16[1056,128]{1,0:T(8,128)(2,1)S(1)}, bf16[1056,128]{1,0:T(8,128)(2,1)S(1)}, bf16[2,1056,128]{2,1,0:T(8,128)(2,1)S(1)}, bf16[2,416,128]{2,1,0:T(8,128)(2,1)S(1)}, bf16[2,416,128]{2,1,0:T(8,128)(2,1)S(1)}) custom-call(s32[1]{0:T(128)} %bitcast.place_ref.refs_0_, f32[4,16,64,128]{3,2,1,0:T(8,128)} %bitcast.16, f32[4,16,64,128]{3,2,1,0:T(8,128)} %bitcast.6, ...), custom_call_target="tpu_custom_call" | custom-call | flops 1 | bytes 1 | tf_op jit(solution)/shard_map/cast_states/pallas_call | solution.py:531
  1.9 3.0 %collective-permute-start = (bf16[2,1056,128]{2,1,0:T(8,128)(2,1)S(1)}, bf16[2,1056,128]{2,1,0:T(8,128)(2,1)S(1)}, u32[]{:S(2)}, u32[]{:S(2)}) collective-permute-start(bf16[2,1056,128]{2,1,0:T(8,128)(2,1)S(1)} %get-tuple-element.43), channel_id=1, source_target_pairs={{0,2},{2,0},{4,6},{6,4},{8,10},{10,8},{12,14},{14,12},{1,3},{3,1},... | collective-permute-start | bytes 1622024 | tf_op jit(solution)/shard_map/ppermute | solution.py:498
  4.9 1.6 %collective-permute-start.1 = (bf16[1056,128]{1,0:T(8,128)(2,1)S(1)}, bf16[1056,128]{1,0:T(8,128)(2,1)S(1)}, u32[]{:S(2)}, u32[]{:S(2)}) collective-permute-start(bf16[1056,128]{1,0:T(8,128)(2,1)S(1)} %get-tuple-element.44), channel_id=1, source_target_pairs={{0,4},{2,6},{4,0},{6,2},{8,12},{10,14},{12,8},{14,10},{1,5},{3,7},... | collective-permute-start | bytes 811016 | tf_op jit(solution)/shard_map/ppermute | solution.py:498
  6.5 2.6 %collective-permute-start.4 = (bf16[2,416,128]{2,1,0:T(8,128)(2,1)S(1)}, bf16[2,416,128]{2,1,0:T(8,128)(2,1)S(1)}, u32[]{:S(2)}, u32[]{:S(2)}) collective-permute-start(bf16[2,416,128]{2,1,0:T(8,128)(2,1)S(1)} %get-tuple-element.48), channel_id=1, source_target_pairs={{0,8},{2,10},{4,12},{6,14},{8,0},{10,2},{12,4},{14,6},{1,9},{3,11}... | collective-permute-start | bytes 638984 | tf_op jit(solution)/shard_map/ppermute | solution.py:498
  9.1 0.2 collective-permute-start.5
  9.3 0.1 select_reduce_fusion.1
  9.4 0.1 convert_reduce_fusion
  9.5 0.2 select_reduce_fusion
  9.7 0.1 copy.29.refs_4_
  9.8 0.1 copy.30.refs_5_
  9.9 0.1 broadcast_in_dim.55
  10.0 0.1 broadcast_in_dim_reshape.3.refs_6_
  10.1 9.6 %early.3 = (f32[4,256,1024]{2,1,0:T(8,128)S(1)}, bf16[4,256,128]{2,1,0:T(8,128)(2,1)S(1)}, f32[4,16,256]{2,1,0:T(8,128)S(1)}, f32[4,256,256]{2,1,0:T(8,128)S(1)}...) custom-call(bf16[2,256,4096]{2,1,0:T(8,128)(2,1)} %refs_0_.5, bf16[2,256,512]{2,1,0:T(8,128)(2,1)} %refs_1_.5, ...), custom_call_target="tpu_custom_call" | custom-call | flops 1 | bytes 1 | tf_op jit(solution)/shard_map/early/pallas_call | solution.py:596
  19.7 0.0 collective-permute-done.refs_1_.refs_2_
  19.8 4.9 %collective-permute-done.4.refs_1_.refs_6_ = bf16[2,416,128]{2,1,0:T(8,128)(2,1)S(1)} collective-permute-done((bf16[2,416,128]{2,1,0:T(8,128)(2,1)S(1)}, bf16[2,416,128]{2,1,0:T(8,128)(2,1)S(1)}, u32[]{:S(2)}, u32[]{:S(2)}) %collective-permute-start.4) | collective-permute-done | bytes 213024 | tf_op jit(solution)/shard_map/ppermute | solution.py:498
  24.7 0.0 collective-permute-done.5.refs_2_.refs_7_
  24.7 0.6 collective-permute-start.6
  25.3 3.4 %collective-permute-start.3 = (bf16[640,128]{1,0:T(8,128)(2,1)S(1)}, bf16[640,128]{1,0:T(8,128)(2,1)S(1)}, u32[]{:S(2)}, u32[]{:S(2)}) collective-permute-start(bf16[640,128]{1,0:T(8,128)(2,1)S(1)} %get-tuple-element.47), channel_id=1, source_target_pairs={{0,4},{2,6},{4,0},{6,2},{8,12},{10,14},{12,8},{14,10},{1,5},{3,7},... | collective-permute-start | bytes 491528 | tf_op jit(solution)/shard_map/ppermute | solution.py:498
  28.7 0.0 collective-permute-start.2
  28.8 5.4 %early.4 = (f32[4,256,1024]{2,1,0:T(8,128)S(1)}, bf16[4,256,128]{2,1,0:T(8,128)(2,1)S(1)}, f32[4,16,256]{2,1,0:T(8,128)S(1)}, f32[4,256,256]{2,1,0:T(8,128)S(1)}...) custom-call(bf16[2,256,4096]{2,1,0:T(8,128)(2,1)} %refs_0_.5, bf16[2,256,512]{2,1,0:T(8,128)(2,1)} %refs_1_.5, ...), custom_call_target="tpu_custom_call" | custom-call | flops 1 | bytes 1 | tf_op jit(solution)/shard_map/early/pallas_call | solution.py:596
  34.1 0.0 collective-permute-done.1.refs_3_
  34.1 0.0 collective-permute-done.3.refs_5_
  34.2 0.0 collective-permute-done.6.refs_7_.refs_8_
  34.2 3.1 %collective-permute-start.10 = (bf16[4,384,128]{2,1,0:T(8,128)(2,1)S(1)}, bf16[4,384,128]{2,1,0:T(8,128)(2,1)S(1)}, u32[]{:S(2)}, u32[]{:S(2)}) collective-permute-start(bf16[4,384,128]{2,1,0:T(8,128)(2,1)S(1)} %stack_later.2.refs_9_), channel_id=1, source_target_pairs={{0,8},{2,10},{4,12},{6,14},{8,0},{10,2},{12,4},{14,6},{1,9},{3,11}... | collective-permute-start | bytes 1179656 | tf_op jit(solution)/shard_map/ppermute | solution.py:498
  37.3 1.1 %pick_states.3 = (bf16[2,416,128]{2,1,0:T(8,128)(2,1)S(1)}, bf16[2,416,128]{2,1,0:T(8,128)(2,1)S(1)}, bf16[2,416,128]{2,1,0:T(8,128)(2,1)S(1)}, bf16[2,416,128]{2,1,0:T(8,128)(2,1)S(1)}) custom-call(s32[8]{0:T(128)S(1)} %broadcast_xor_fusion.refs_10_.refs_0_, bf16[1056,128]{1,0:T(8,128)(2,1)S(1)} %get-tuple-element.42.refs_9_.refs_1_, ...), custom_call_target="tpu_custom_call" | custom-call | flops 1 | bytes 1 | tf_op jit(solution)/shard_map/pick_states/pallas_call | solution.py:563
  38.4 1.6 %collective-permute-start.7 = (bf16[2,416,128]{2,1,0:T(8,128)(2,1)S(1)}, bf16[2,416,128]{2,1,0:T(8,128)(2,1)S(1)}, u32[]{:S(2)}, u32[]{:S(2)}) collective-permute-start(bf16[2,416,128]{2,1,0:T(8,128)(2,1)S(1)} %get-tuple-element.52), channel_id=1, source_target_pairs={{0,2},{2,0},{4,6},{6,4},{8,10},{10,8},{12,14},{14,12},{1,3},{3,1},... | collective-permute-start | bytes 638984 | tf_op jit(solution)/shard_map/ppermute | solution.py:498
  39.9 0.0 collective-permute-start.8
  40.0 1.9 %collective-permute-start.9 = (bf16[2,416,128]{2,1,0:T(8,128)(2,1)S(1)}, bf16[2,416,128]{2,1,0:T(8,128)(2,1)S(1)}, u32[]{:S(2)}, u32[]{:S(2)}) collective-permute-start(bf16[2,416,128]{2,1,0:T(8,128)(2,1)S(1)} %get-tuple-element.54), channel_id=1, source_target_pairs={{0,6},{2,4},{4,2},{6,0},{8,14},{10,12},{12,10},{14,8},{1,7},{3,5},... | collective-permute-start | bytes 638984 | tf_op jit(solution)/shard_map/ppermute | solution.py:498
  41.9 5.4 %early.5 = (f32[4,256,1024]{2,1,0:T(8,128)S(1)}, bf16[4,256,128]{2,1,0:T(8,128)(2,1)S(1)}, f32[4,16,256]{2,1,0:T(8,128)S(1)}, f32[4,256,256]{2,1,0:T(8,128)S(1)}...) custom-call(bf16[2,256,4096]{2,1,0:T(8,128)(2,1)} %refs_0_.5, ...), custom_call_target="tpu_custom_call", output_to_operand_aliasing={{0}: (10, {}), {1}: (11, {}), {2}: (12, {}), {3}: (13, {}),... | custom-call | flops 1 | bytes 1 | tf_op jit(solution)/shard_map/early/pallas_call | solution.py:596
  47.3 5.3 %collective-permute-done.10.refs_7_.refs_6_ = bf16[4,384,128]{2,1,0:T(8,128)(2,1)S(1)} collective-permute-done((bf16[4,384,128]{2,1,0:T(8,128)(2,1)S(1)}, bf16[4,384,128]{2,1,0:T(8,128)(2,1)S(1)}, u32[]{:S(2)}, u32[]{:S(2)}) %collective-permute-start.10) | collective-permute-done | bytes 393248 | tf_op jit(solution)/shard_map/ppermute | solution.py:498
  52.7 0.1 collective-permute-start.11
  52.7 0.0 collective-permute-done.7.refs_9_.refs_2_.refs_6_
  52.8 0.9 %collective-permute-done.8.refs_10_.refs_3_.refs_7_ = bf16[2,416,128]{2,1,0:T(8,128)(2,1)S(1)} collective-permute-done((bf16[2,416,128]{2,1,0:T(8,128)(2,1)S(1)}, bf16[2,416,128]{2,1,0:T(8,128)(2,1)S(1)}, u32[]{:S(2)}, u32[]{:S(2)}) %collective-permute-start.8) | collective-permute-done | bytes 213024 | tf_op jit(solution)/shard_map/ppermute | solution.py:498
  53.6 2.2 %collective-permute-done.9.refs_11_.refs_4_.refs_8_ = bf16[2,416,128]{2,1,0:T(8,128)(2,1)S(1)} collective-permute-done((bf16[2,416,128]{2,1,0:T(8,128)(2,1)S(1)}, bf16[2,416,128]{2,1,0:T(8,128)(2,1)S(1)}, u32[]{:S(2)}, u32[]{:S(2)}) %collective-permute-start.9) | collective-permute-done | bytes 213024 | tf_op jit(solution)/shard_map/ppermute | solution.py:498
  55.9 1.1 %pick_states.4 = (bf16[2,384,128]{2,1,0:T(8,128)(2,1)S(1)}, bf16[2,384,128]{2,1,0:T(8,128)(2,1)S(1)}, bf16[2,384,128]{2,1,0:T(8,128)(2,1)S(1)}, bf16[2,384,128]{2,1,0:T(8,128)(2,1)S(1)}) custom-call(s32[8]{0:T(128)S(1)} %broadcast_xor_fusion.refs_10_.refs_0_, bf16[1056,128]{1,0:T(8,128)(2,1)S(1)} %get-tuple-element.42.refs_9_.refs_1_, ...), custom_call_target="tpu_custom_call" | custom-call | flops 1 | bytes 1 | tf_op jit(solution)/shard_map/pick_states/pallas_call | solution.py:563
  56.9 1.7 %collective-permute-start.15 = (bf16[2,384,128]{2,1,0:T(8,128)(2,1)S(1)}, bf16[2,384,128]{2,1,0:T(8,128)(2,1)S(1)}, u32[]{:S(2)}, u32[]{:S(2)}) collective-permute-start(bf16[2,384,128]{2,1,0:T(8,128)(2,1)S(1)} %get-tuple-element.76), channel_id=1, source_target_pairs={{0,2},{2,0},{4,6},{6,4},{8,10},{10,8},{12,14},{14,12},{1,3},{3,1},... | collective-permute-start | bytes 589832 | tf_op jit(solution)/shard_map/ppermute | solution.py:498
  58.6 1.9 %collective-permute-start.17 = (bf16[2,384,128]{2,1,0:T(8,128)(2,1)S(1)}, bf16[2,384,128]{2,1,0:T(8,128)(2,1)S(1)}, u32[]{:S(2)}, u32[]{:S(2)}) collective-permute-start(bf16[2,384,128]{2,1,0:T(8,128)(2,1)S(1)} %get-tuple-element.78), channel_id=1, source_target_pairs={{0,6},{2,4},{4,2},{6,0},{8,14},{10,12},{12,10},{14,8},{1,7},{3,5},... | collective-permute-start | bytes 589832 | tf_op jit(solution)/shard_map/ppermute | solution.py:498
  60.5 3.3 %late.3.refs_7_.refs_22_ = bf16[2,256,4096]{2,1,0:T(8,128)(2,1)} custom-call(s32[1]{0:T(128)} %bitcast.place_ref.refs_0_, bf16[2,416,128]{2,1,0:T(8,128)(2,1)S(1)} %get-tuple-element.51.refs_9_.refs_8_.refs_1_.refs_5_, bf16[2,416,128]{2,1,0:T(8,128)(2,1)S(1)} %collective-permute-done.7.refs_9_.refs_2_.refs_6_, ...), custom_call_target="tpu_custom_call" | custom-call | flops 1 | bytes 1 | tf_op jit(solution)/shard_map/late/pallas_call | solution.py:645
  63.8 2.3 %collective-permute-done.11.refs_6_ = bf16[4,256,128]{2,1,0:T(8,128)(2,1)S(1)} collective-permute-done((bf16[4,256,128]{2,1,0:T(8,128)(2,1)S(1)}, bf16[4,256,128]{2,1,0:T(8,128)(2,1)S(1)}, u32[]{:S(2)}, u32[]{:S(2)}) %collective-permute-start.11) | collective-permute-done | bytes 262176 | tf_op jit(solution)/shard_map/ppermute | solution.py:498
  66.0 1.2 %pick_states.5 = (bf16[2,256,128]{2,1,0:T(8,128)(2,1)S(1)}, bf16[2,256,128]{2,1,0:T(8,128)(2,1)S(1)}, bf16[2,256,128]{2,1,0:T(8,128)(2,1)S(1)}, bf16[2,256,128]{2,1,0:T(8,128)(2,1)S(1)}) custom-call(s32[8]{0:T(128)S(1)} %broadcast_xor_fusion.refs_10_.refs_0_, bf16[1056,128]{1,0:T(8,128)(2,1)S(1)} %get-tuple-element.42.refs_9_.refs_1_, ...), custom_call_target="tpu_custom_call" | custom-call | flops 1 | bytes 1 | tf_op jit(solution)/shard_map/pick_states/pallas_call | solution.py:563
  67.3 1.6 %collective-permute-start.12 = (bf16[2,256,128]{2,1,0:T(8,128)(2,1)S(1)}, bf16[2,256,128]{2,1,0:T(8,128)(2,1)S(1)}, u32[]{:S(2)}, u32[]{:S(2)}) collective-permute-start(bf16[2,256,128]{2,1,0:T(8,128)(2,1)S(1)} %get-tuple-element.73), channel_id=1, source_target_pairs={{0,2},{2,0},{4,6},{6,4},{8,10},{10,8},{12,14},{14,12},{1,3},{3,1},... | collective-permute-start | bytes 393224 | tf_op jit(solution)/shard_map/ppermute | solution.py:498
  68.9 2.0 %collective-permute-start.14 = (bf16[2,256,128]{2,1,0:T(8,128)(2,1)S(1)}, bf16[2,256,128]{2,1,0:T(8,128)(2,1)S(1)}, u32[]{:S(2)}, u32[]{:S(2)}) collective-permute-start(bf16[2,256,128]{2,1,0:T(8,128)(2,1)S(1)} %get-tuple-element.75), channel_id=1, source_target_pairs={{0,6},{2,4},{4,2},{6,0},{8,14},{10,12},{12,10},{14,8},{1,7},{3,5},... | collective-permute-start | bytes 393224 | tf_op jit(solution)/shard_map/ppermute | solution.py:498
  70.8 0.9 %collective-permute-done.17.refs_8_ = bf16[2,384,128]{2,1,0:T(8,128)(2,1)S(1)} collective-permute-done((bf16[2,384,128]{2,1,0:T(8,128)(2,1)S(1)}, bf16[2,384,128]{2,1,0:T(8,128)(2,1)S(1)}, u32[]{:S(2)}, u32[]{:S(2)}) %collective-permute-start.17) | collective-permute-done | bytes 196640 | tf_op jit(solution)/shard_map/ppermute | solution.py:498
  71.7 3.3 %late.4.refs_21_ = bf16[2,256,4096]{2,1,0:T(8,128)(2,1)} custom-call(s32[1]{0:T(128)} %bitcast.place_ref.refs_0_, bf16[2,416,128]{2,1,0:T(8,128)(2,1)S(1)} %get-tuple-element.51.refs_9_.refs_8_.refs_1_.refs_5_, bf16[2,416,128]{2,1,0:T(8,128)(2,1)S(1)} %collective-permute-done.7.refs_9_.refs_2_.refs_6_, ...), custom_call_target="tpu_custom_call", output_to_operand_aliasing={{}: (22, {})} | custom-call | flops 1 | bytes 1 | tf_op jit(solution)/shard_map/late/pallas_call | solution.py:645
  75.0 0.2 collective-permute-done.12.refs_6_
  75.2 0.1 collective-permute-done.13.refs_7_
  75.3 1.8 %collective-permute-done.14.refs_8_ = bf16[2,256,128]{2,1,0:T(8,128)(2,1)S(1)} collective-permute-done((bf16[2,256,128]{2,1,0:T(8,128)(2,1)S(1)}, bf16[2,256,128]{2,1,0:T(8,128)(2,1)S(1)}, u32[]{:S(2)}, u32[]{:S(2)}) %collective-permute-start.14) | collective-permute-done | bytes 131104 | tf_op jit(solution)/shard_map/ppermute | solution.py:498
  77.1 2.9 %late.5 = bf16[2,256,4096]{2,1,0:T(8,128)(2,1)} custom-call(s32[1]{0:T(128)} %bitcast.place_ref.refs_0_, bf16[2,416,128]{2,1,0:T(8,128)(2,1)S(1)} %get-tuple-element.51.refs_9_.refs_8_.refs_1_.refs_5_, bf16[2,416,128]{2,1,0:T(8,128)(2,1)S(1)} %collective-permute-done.7.refs_9_.refs_2_.refs_6_, ...), custom_call_target="tpu_custom_call", output_to_operand_aliasing={{}: (21, {})} | custom-call | flops 1 | bytes 1 | tf_op jit(solution)/shard_map/late/pallas_call | solution.py:645
  (21 shorter events, 0.1 us)
Async XLA Ops:
  0.0 9.3 %copy-start.3 = (s32[8]{0:T(128)S(1)}, s32[8]{0:T(128)}, u32[]{:S(2)}) copy-start(s32[8]{0:T(128)} %param.26) | copy-start | bytes 100
  0.0 9.4 %copy-start.4 = (s32[16]{0:T(128)S(1)}, s32[16]{0:T(128)}, u32[]{:S(2)}) copy-start(s32[16]{0:T(128)} %param.27) | copy-start | bytes 196
  0.0 9.7 %copy-start = (f32[64]{0:T(128)S(1)}, f32[64]{0:T(128)}, u32[]{:S(2)}) copy-start(f32[64]{0:T(128)} %param.18) | copy-start | bytes 772
  0.0 9.8 %copy-start.1 = (f32[64]{0:T(128)S(1)}, f32[64]{0:T(128)}, u32[]{:S(2)}) copy-start(f32[64]{0:T(128)} %param.19) | copy-start | bytes 772
  0.0 9.9 %copy-start.2 = (f32[64]{0:T(128)S(1)}, f32[64]{0:T(128)}, u32[]{:S(2)}) copy-start(f32[64]{0:T(128)} %param.20) | copy-start | bytes 772
  1.9 17.9 %collective-permute-start = (bf16[2,1056,128]{2,1,0:T(8,128)(2,1)S(1)}, bf16[2,1056,128]{2,1,0:T(8,128)(2,1)S(1)}, u32[]{:S(2)}, u32[]{:S(2)}) collective-permute-start(bf16[2,1056,128]{2,1,0:T(8,128)(2,1)S(1)} %get-tuple-element.43), channel_id=1, source_target_pairs={{0,2},{2,0},{4,6},{6,4},{8,10},{10,8},{12,14},{14,12},{1,3},{3,1},... | collective-permute-start | bytes 1622024 | tf_op jit(solution)/shard_map/ppermute | solution.py:498
  4.9 29.2 %collective-permute-start.1 = (bf16[1056,128]{1,0:T(8,128)(2,1)S(1)}, bf16[1056,128]{1,0:T(8,128)(2,1)S(1)}, u32[]{:S(2)}, u32[]{:S(2)}) collective-permute-start(bf16[1056,128]{1,0:T(8,128)(2,1)S(1)} %get-tuple-element.44), channel_id=1, source_target_pairs={{0,4},{2,6},{4,0},{6,2},{8,12},{10,14},{12,8},{14,10},{1,5},{3,7},... | collective-permute-start | bytes 811016 | tf_op jit(solution)/shard_map/ppermute | solution.py:498
  6.5 18.2 %collective-permute-start.4 = (bf16[2,416,128]{2,1,0:T(8,128)(2,1)S(1)}, bf16[2,416,128]{2,1,0:T(8,128)(2,1)S(1)}, u32[]{:S(2)}, u32[]{:S(2)}) collective-permute-start(bf16[2,416,128]{2,1,0:T(8,128)(2,1)S(1)} %get-tuple-element.48), channel_id=1, source_target_pairs={{0,8},{2,10},{4,12},{6,14},{8,0},{10,2},{12,4},{14,6},{1,9},{3,11}... | collective-permute-start | bytes 638984 | tf_op jit(solution)/shard_map/ppermute | solution.py:498
  9.1 15.6 %collective-permute-start.5 = (bf16[2,416,128]{2,1,0:T(8,128)(2,1)S(1)}, bf16[2,416,128]{2,1,0:T(8,128)(2,1)S(1)}, u32[]{:S(2)}, u32[]{:S(2)}) collective-permute-start(bf16[2,416,128]{2,1,0:T(8,128)(2,1)S(1)} %get-tuple-element.49), channel_id=1, source_target_pairs={{0,12},{2,14},{4,8},{6,10},{8,4},{10,6},{12,0},{14,2},{1,13},{3,15... | collective-permute-start | bytes 638984 | tf_op jit(solution)/shard_map/ppermute | solution.py:498
  24.7 9.4 %collective-permute-start.6 = (bf16[2,416,128]{2,1,0:T(8,128)(2,1)S(1)}, bf16[2,416,128]{2,1,0:T(8,128)(2,1)S(1)}, u32[]{:S(2)}, u32[]{:S(2)}) collective-permute-start(bf16[2,416,128]{2,1,0:T(8,128)(2,1)S(1)} %stack_first.1.refs_9_), channel_id=1, source_target_pairs={{0,2},{2,0},{4,6},{6,4},{8,10},{10,8},{12,14},{14,12},{1,3},{3,1},... | collective-permute-start | bytes 638984 | tf_op jit(solution)/shard_map/ppermute | solution.py:498
  25.3 8.8 %collective-permute-start.3 = (bf16[640,128]{1,0:T(8,128)(2,1)S(1)}, bf16[640,128]{1,0:T(8,128)(2,1)S(1)}, u32[]{:S(2)}, u32[]{:S(2)}) collective-permute-start(bf16[640,128]{1,0:T(8,128)(2,1)S(1)} %get-tuple-element.47), channel_id=1, source_target_pairs={{0,4},{2,6},{4,0},{6,2},{8,12},{10,14},{12,8},{14,10},{1,5},{3,7},... | collective-permute-start | bytes 491528 | tf_op jit(solution)/shard_map/ppermute | solution.py:498
  28.7 5.4 %collective-permute-start.2 = (bf16[416,128]{1,0:T(8,128)(2,1)S(1)}, bf16[416,128]{1,0:T(8,128)(2,1)S(1)}, u32[]{:S(2)}, u32[]{:S(2)}) collective-permute-start(bf16[416,128]{1,0:T(8,128)(2,1)S(1)} %get-tuple-element.46.refs_3_), channel_id=1, source_target_pairs={{0,4},{2,6},{4,0},{6,2},{8,12},{10,14},{12,8},{14,10},{1,5},{3,7},... | collective-permute-start | bytes 319496 | tf_op jit(solution)/shard_map/ppermute | solution.py:498
  34.2 18.4 %collective-permute-start.10 = (bf16[4,384,128]{2,1,0:T(8,128)(2,1)S(1)}, bf16[4,384,128]{2,1,0:T(8,128)(2,1)S(1)}, u32[]{:S(2)}, u32[]{:S(2)}) collective-permute-start(bf16[4,384,128]{2,1,0:T(8,128)(2,1)S(1)} %stack_later.2.refs_9_), channel_id=1, source_target_pairs={{0,8},{2,10},{4,12},{6,14},{8,0},{10,2},{12,4},{14,6},{1,9},{3,11}... | collective-permute-start | bytes 1179656 | tf_op jit(solution)/shard_map/ppermute | solution.py:498
  38.4 14.4 %collective-permute-start.7 = (bf16[2,416,128]{2,1,0:T(8,128)(2,1)S(1)}, bf16[2,416,128]{2,1,0:T(8,128)(2,1)S(1)}, u32[]{:S(2)}, u32[]{:S(2)}) collective-permute-start(bf16[2,416,128]{2,1,0:T(8,128)(2,1)S(1)} %get-tuple-element.52), channel_id=1, source_target_pairs={{0,2},{2,0},{4,6},{6,4},{8,10},{10,8},{12,14},{14,12},{1,3},{3,1},... | collective-permute-start | bytes 638984 | tf_op jit(solution)/shard_map/ppermute | solution.py:498
  39.9 13.7 %collective-permute-start.8 = (bf16[2,416,128]{2,1,0:T(8,128)(2,1)S(1)}, bf16[2,416,128]{2,1,0:T(8,128)(2,1)S(1)}, u32[]{:S(2)}, u32[]{:S(2)}) collective-permute-start(bf16[2,416,128]{2,1,0:T(8,128)(2,1)S(1)} %get-tuple-element.53), channel_id=1, source_target_pairs={{0,4},{2,6},{4,0},{6,2},{8,12},{10,14},{12,8},{14,10},{1,5},{3,7},... | collective-permute-start | bytes 638984 | tf_op jit(solution)/shard_map/ppermute | solution.py:498
  40.0 15.9 %collective-permute-start.9 = (bf16[2,416,128]{2,1,0:T(8,128)(2,1)S(1)}, bf16[2,416,128]{2,1,0:T(8,128)(2,1)S(1)}, u32[]{:S(2)}, u32[]{:S(2)}) collective-permute-start(bf16[2,416,128]{2,1,0:T(8,128)(2,1)S(1)} %get-tuple-element.54), channel_id=1, source_target_pairs={{0,6},{2,4},{4,2},{6,0},{8,14},{10,12},{12,10},{14,8},{1,7},{3,5},... | collective-permute-start | bytes 638984 | tf_op jit(solution)/shard_map/ppermute | solution.py:498
  52.7 13.4 %collective-permute-start.11 = (bf16[4,256,128]{2,1,0:T(8,128)(2,1)S(1)}, bf16[4,256,128]{2,1,0:T(8,128)(2,1)S(1)}, u32[]{:S(2)}, u32[]{:S(2)}) collective-permute-start(bf16[4,256,128]{2,1,0:T(8,128)(2,1)S(1)} %stack_later.3.refs_7_), channel_id=1, source_target_pairs={{0,8},{2,10},{4,12},{6,14},{8,0},{10,2},{12,4},{14,6},{1,9},{3,11}... | collective-permute-start | bytes 786440 | tf_op jit(solution)/shard_map/ppermute | solution.py:498
  56.9 11.9 %collective-permute-start.15 = (bf16[2,384,128]{2,1,0:T(8,128)(2,1)S(1)}, bf16[2,384,128]{2,1,0:T(8,128)(2,1)S(1)}, u32[]{:S(2)}, u32[]{:S(2)}) collective-permute-start(bf16[2,384,128]{2,1,0:T(8,128)(2,1)S(1)} %get-tuple-element.76), channel_id=1, source_target_pairs={{0,2},{2,0},{4,6},{6,4},{8,10},{10,8},{12,14},{14,12},{1,3},{3,1},... | collective-permute-start | bytes 589832 | tf_op jit(solution)/shard_map/ppermute | solution.py:498
  58.6 12.2 %collective-permute-start.16 = (bf16[2,384,128]{2,1,0:T(8,128)(2,1)S(1)}, bf16[2,384,128]{2,1,0:T(8,128)(2,1)S(1)}, u32[]{:S(2)}, u32[]{:S(2)}) collective-permute-start(bf16[2,384,128]{2,1,0:T(8,128)(2,1)S(1)} %get-tuple-element.77), channel_id=1, source_target_pairs={{0,4},{2,6},{4,0},{6,2},{8,12},{10,14},{12,8},{14,10},{1,5},{3,7},... | collective-permute-start | bytes 589832 | tf_op jit(solution)/shard_map/ppermute | solution.py:498
  58.6 13.1 %collective-permute-start.17 = (bf16[2,384,128]{2,1,0:T(8,128)(2,1)S(1)}, bf16[2,384,128]{2,1,0:T(8,128)(2,1)S(1)}, u32[]{:S(2)}, u32[]{:S(2)}) collective-permute-start(bf16[2,384,128]{2,1,0:T(8,128)(2,1)S(1)} %get-tuple-element.78), channel_id=1, source_target_pairs={{0,6},{2,4},{4,2},{6,0},{8,14},{10,12},{12,10},{14,8},{1,7},{3,5},... | collective-permute-start | bytes 589832 | tf_op jit(solution)/shard_map/ppermute | solution.py:498
  67.3 7.9 %collective-permute-start.12 = (bf16[2,256,128]{2,1,0:T(8,128)(2,1)S(1)}, bf16[2,256,128]{2,1,0:T(8,128)(2,1)S(1)}, u32[]{:S(2)}, u32[]{:S(2)}) collective-permute-start(bf16[2,256,128]{2,1,0:T(8,128)(2,1)S(1)} %get-tuple-element.73), channel_id=1, source_target_pairs={{0,2},{2,0},{4,6},{6,4},{8,10},{10,8},{12,14},{14,12},{1,3},{3,1},... | collective-permute-start | bytes 393224 | tf_op jit(solution)/shard_map/ppermute | solution.py:498
  68.9 6.4 %collective-permute-start.13 = (bf16[2,256,128]{2,1,0:T(8,128)(2,1)S(1)}, bf16[2,256,128]{2,1,0:T(8,128)(2,1)S(1)}, u32[]{:S(2)}, u32[]{:S(2)}) collective-permute-start(bf16[2,256,128]{2,1,0:T(8,128)(2,1)S(1)} %get-tuple-element.74), channel_id=1, source_target_pairs={{0,4},{2,6},{4,0},{6,2},{8,12},{10,14},{12,8},{14,10},{1,5},{3,7},... | collective-permute-start | bytes 393224 | tf_op jit(solution)/shard_map/ppermute | solution.py:498
  68.9 8.2 %collective-permute-start.14 = (bf16[2,256,128]{2,1,0:T(8,128)(2,1)S(1)}, bf16[2,256,128]{2,1,0:T(8,128)(2,1)S(1)}, u32[]{:S(2)}, u32[]{:S(2)}) collective-permute-start(bf16[2,256,128]{2,1,0:T(8,128)(2,1)S(1)} %get-tuple-element.75), channel_id=1, source_target_pairs={{0,6},{2,4},{4,2},{6,0},{8,14},{10,12},{12,10},{14,8},{1,7},{3,5},... | collective-permute-start | bytes 393224 | tf_op jit(solution)/shard_map/ppermute | solution.py:498

commit v21 on v20

--- a/solution.py
+++ b/solution.py
@@ -700,13 +700,12 @@
     sent_b, crossed_b = cross(1, [second[1], passed])
     choices = inside_rows(0) + [(5, 0), (7, 0), (6, 0), (7, 1)]
     states = [pick(rows[0], [*inside, *crossed_a, passed], choices, [sent_b])]
-    second = early(1, 2, 1, second, [states[0][0]])
+    sent_c, crossed_c = cross(2, [states[0][0]])
+    second = early(1, 2, 1, second, [sent_c])
     parts.append(second)
-    sent_c, crossed_c = cross(2, [second[1], crossed_b])
-    states.append(pick_later(1, crossed_b, [sent_c, *states[0]]))
-    result = late([0], states, parts, None, [states[1][0]])
-    states.append(pick_later(2, crossed_c, [stay(result)]))
-    result = late([1], states, parts, result, [states[2][0]])
+    states.append(pick_later(1, crossed_b, [second[1], *states[0]]))
+    states.append(pick_later(2, crossed_c, [states[1][0]]))
+    result = late([0, 1], states, parts, None, [states[2][0]])
     return late([2], states, parts, result, [])
 
 

time: 80.3 us -> 83 us (1.034)
  starting transfers between devices: 25.3 us -> 27.8 us
  waiting for transfers between devices: 18.6 us -> 19.6 us
    ppermute x18, starting transfers between devices: 25.3 us -> 27.8 us  [swap(): return lax.ppermute(value, 'batch', perm=[(i, i ^ r) for i in range(8)])]
    ppermute x18, waiting for transfers between devices: 18.6 us -> 19.6 us  [swap(): return lax.ppermute(value, 'batch', perm=[(i, i ^ r) for i in range(8)])]
    pallas_call x3 -> x2, Pallas kernels: 9.52 us -> 8.67 us  [late(): pl.pallas_call(functools.partial(drop_tokens, kernel, keep, 1 + len(opera...]
  transfers between devices with their start and end apart: 18 -> 18, of which waited for: 9 -> 7; matrix products, arithmetic and copies ran while one was open for 1% -> 1% of each run, Pallas kernels for 38% -> 36%
where the time goes in v21:
time: 83 us; the launch traced here: 82.8 us
  Pallas kernels  34.4 us (41%)
  starting transfers between devices  27.8 us (33%)
  waiting for transfers between devices  19.6 us (24%)
    ppermute x18, starting transfers between devices, swap(): return lax.ppermute(value, 'batch', perm=[(i, i ^ r) for i in range(8)])  27.8 us
    pallas_call x3, Pallas kernels, early(): pl.pallas_call(functools.partial(drop_tokens, functools.partial(early_ker...  20.4 us
    ppermute x18, waiting for transfers between devices, swap(): return lax.ppermute(value, 'batch', perm=[(i, i ^ r) for i in range(8)])  19.6 us
    pallas_call x2, Pallas kernels, late(): pl.pallas_call(functools.partial(drop_tokens, kernel, keep, 1 + len(opera...  8.67 us
    pallas_call x7, Pallas kernels, rearrange(): pl.pallas_call(functools.partial(drop_tokens, kernel, 1 + len(sources), l...  3.44 us
    pallas_call x1, Pallas kernels, cast(): pl.pallas_call(kernel, grid_spec=pltpu.PrefetchScalarGridSpec(num_scalar_...  1.85 us
  transfers between devices with their start and end apart: 18, of which 7 were waited for; matrix products, arithmetic and copies ran while one was open for 1% of the time, Pallas kernels for 36%

profile of v21, /device:TPU:0, one launch (start us, length us, event | category | flops | bytes accessed | tf_op | source)
XLA Modules:
  0.0 82.8 jit_solution(15911351639273425438)
XLA Ops:
  0.0 1.8 %cast_states.1 = (bf16[1056,128]{1,0:T(8,128)(2,1)S(1)}, bf16[1056,128]{1,0:T(8,128)(2,1)S(1)}, bf16[2,1056,128]{2,1,0:T(8,128)(2,1)S(1)}, bf16[2,416,128]{2,1,0:T(8,128)(2,1)S(1)}, bf16[2,416,128]{2,1,0:T(8,128)(2,1)S(1)}) custom-call(s32[1]{0:T(128)} %bitcast.place_ref.refs_0_, f32[4,16,64,128]{3,2,1,0:T(8,128)} %bitcast.16, f32[4,16,64,128]{3,2,1,0:T(8,128)} %bitcast.6, ...), custom_call_target="tpu_custom_call" | custom-call | flops 1 | bytes 1 | tf_op jit(solution)/shard_map/cast_states/pallas_call | solution.py:531
  1.9 4.1 %collective-permute-start.4 = (bf16[2,416,128]{2,1,0:T(8,128)(2,1)S(1)}, bf16[2,416,128]{2,1,0:T(8,128)(2,1)S(1)}, u32[]{:S(2)}, u32[]{:S(2)}) collective-permute-start(bf16[2,416,128]{2,1,0:T(8,128)(2,1)S(1)} %get-tuple-element.48), channel_id=1, source_target_pairs={{0,8},{2,10},{4,12},{6,14},{8,0},{10,2},{12,4},{14,6},{1,9},{3,11}... | collective-permute-start | bytes 638984 | tf_op jit(solution)/shard_map/ppermute | solution.py:498
  6.0 1.3 %collective-permute-start.5 = (bf16[2,416,128]{2,1,0:T(8,128)(2,1)S(1)}, bf16[2,416,128]{2,1,0:T(8,128)(2,1)S(1)}, u32[]{:S(2)}, u32[]{:S(2)}) collective-permute-start(bf16[2,416,128]{2,1,0:T(8,128)(2,1)S(1)} %get-tuple-element.49), channel_id=1, source_target_pairs={{0,12},{2,14},{4,8},{6,10},{8,4},{10,6},{12,0},{14,2},{1,13},{3,15... | collective-permute-start | bytes 638984 | tf_op jit(solution)/shard_map/ppermute | solution.py:498
  7.3 0.2 collective-permute-start.1
  7.6 1.5 %collective-permute-start = (bf16[2,1056,128]{2,1,0:T(8,128)(2,1)S(1)}, bf16[2,1056,128]{2,1,0:T(8,128)(2,1)S(1)}, u32[]{:S(2)}, u32[]{:S(2)}) collective-permute-start(bf16[2,1056,128]{2,1,0:T(8,128)(2,1)S(1)} %get-tuple-element.43), channel_id=1, source_target_pairs={{0,2},{2,0},{4,6},{6,4},{8,10},{10,8},{12,14},{14,12},{1,3},{3,1},... | collective-permute-start | bytes 1622024 | tf_op jit(solution)/shard_map/ppermute | solution.py:498
  9.1 0.1 select_reduce_fusion.1
  9.2 0.1 convert_reduce_fusion
  9.3 0.2 select_reduce_fusion
  9.5 0.1 copy.28.refs_4_
  9.6 0.1 copy.29.refs_5_
  9.7 0.1 broadcast_in_dim.55
  9.8 0.1 broadcast_in_dim_reshape.3.refs_6_
  9.9 9.6 %early.3 = (f32[4,256,1024]{2,1,0:T(8,128)S(1)}, bf16[4,256,128]{2,1,0:T(8,128)(2,1)S(1)}, f32[4,16,256]{2,1,0:T(8,128)S(1)}, f32[4,256,256]{2,1,0:T(8,128)S(1)}...) custom-call(bf16[2,256,4096]{2,1,0:T(8,128)(2,1)} %refs_0_.5, bf16[2,256,512]{2,1,0:T(8,128)(2,1)} %refs_1_.5, ...), custom_call_target="tpu_custom_call" | custom-call | flops 1 | bytes 1 | tf_op jit(solution)/shard_map/early/pallas_call | solution.py:596
  19.5 1.5 %collective-permute-done.refs_1_.refs_2_ = bf16[2,1056,128]{2,1,0:T(8,128)(2,1)S(1)} collective-permute-done((bf16[2,1056,128]{2,1,0:T(8,128)(2,1)S(1)}, bf16[2,1056,128]{2,1,0:T(8,128)(2,1)S(1)}, u32[]{:S(2)}, u32[]{:S(2)}) %collective-permute-start) | collective-permute-done | bytes 540704 | tf_op jit(solution)/shard_map/ppermute | solution.py:498
  21.0 0.2 collective-permute-done.4.refs_1_.refs_6_
  21.2 0.0 collective-permute-done.5.refs_2_.refs_7_
  21.3 1.9 %collective-permute-start.6 = (bf16[2,416,128]{2,1,0:T(8,128)(2,1)S(1)}, bf16[2,416,128]{2,1,0:T(8,128)(2,1)S(1)}, u32[]{:S(2)}, u32[]{:S(2)}) collective-permute-start(bf16[2,416,128]{2,1,0:T(8,128)(2,1)S(1)} %stack_first.1.refs_9_), channel_id=1, source_target_pairs={{0,2},{2,0},{4,6},{6,4},{8,10},{10,8},{12,14},{14,12},{1,3},{3,1},... | collective-permute-start | bytes 638984 | tf_op jit(solution)/shard_map/ppermute | solution.py:498
  23.2 4.1 %collective-permute-start.3 = (bf16[640,128]{1,0:T(8,128)(2,1)S(1)}, bf16[640,128]{1,0:T(8,128)(2,1)S(1)}, u32[]{:S(2)}, u32[]{:S(2)}) collective-permute-start(bf16[640,128]{1,0:T(8,128)(2,1)S(1)} %get-tuple-element.47), channel_id=1, source_target_pairs={{0,4},{2,6},{4,0},{6,2},{8,12},{10,14},{12,8},{14,10},{1,5},{3,7},... | collective-permute-start | bytes 491528 | tf_op jit(solution)/shard_map/ppermute | solution.py:498
  27.3 0.0 collective-permute-start.2
  27.3 5.4 %early.4 = (f32[4,256,1024]{2,1,0:T(8,128)S(1)}, bf16[4,256,128]{2,1,0:T(8,128)(2,1)S(1)}, f32[4,16,256]{2,1,0:T(8,128)S(1)}, f32[4,256,256]{2,1,0:T(8,128)S(1)}...) custom-call(bf16[2,256,4096]{2,1,0:T(8,128)(2,1)} %refs_0_.5, bf16[2,256,512]{2,1,0:T(8,128)(2,1)} %refs_1_.5, ...), custom_call_target="tpu_custom_call" | custom-call | flops 1 | bytes 1 | tf_op jit(solution)/shard_map/early/pallas_call | solution.py:596
  32.7 0.0 collective-permute-done.1.refs_3_
  32.7 1.0 %collective-permute-done.2.refs_4_ = bf16[416,128]{1,0:T(8,128)(2,1)S(1)} collective-permute-done((bf16[416,128]{1,0:T(8,128)(2,1)S(1)}, bf16[416,128]{1,0:T(8,128)(2,1)S(1)}, u32[]{:S(2)}, u32[]{:S(2)}) %collective-permute-start.2) | collective-permute-done | bytes 106528 | tf_op jit(solution)/shard_map/ppermute | solution.py:498
  33.7 0.0 collective-permute-done.3.refs_5_
  33.7 0.0 collective-permute-done.6.refs_7_.refs_8_
  33.7 3.7 %collective-permute-start.11 = (bf16[4,384,128]{2,1,0:T(8,128)(2,1)S(1)}, bf16[4,384,128]{2,1,0:T(8,128)(2,1)S(1)}, u32[]{:S(2)}, u32[]{:S(2)}) collective-permute-start(bf16[4,384,128]{2,1,0:T(8,128)(2,1)S(1)} %stack_later.2.refs_9_), channel_id=1, source_target_pairs={{0,8},{2,10},{4,12},{6,14},{8,0},{10,2},{12,4},{14,6},{1,9},{3,11}... | collective-permute-start | bytes 1179656 | tf_op jit(solution)/shard_map/ppermute | solution.py:498
  37.4 1.1 %pick_states.3 = (bf16[2,416,128]{2,1,0:T(8,128)(2,1)S(1)}, bf16[2,416,128]{2,1,0:T(8,128)(2,1)S(1)}, bf16[2,416,128]{2,1,0:T(8,128)(2,1)S(1)}, bf16[2,416,128]{2,1,0:T(8,128)(2,1)S(1)}) custom-call(s32[8]{0:T(128)S(1)} %broadcast_xor_fusion.refs_10_.refs_0_, bf16[1056,128]{1,0:T(8,128)(2,1)S(1)} %get-tuple-element.42.refs_9_.refs_1_, ...), custom_call_target="tpu_custom_call" | custom-call | flops 1 | bytes 1 | tf_op jit(solution)/shard_map/pick_states/pallas_call | solution.py:563
  38.5 0.6 collective-permute-start.7
  39.1 0.3 collective-permute-start.8
  39.4 2.7 %collective-permute-start.9 = (bf16[2,416,128]{2,1,0:T(8,128)(2,1)S(1)}, bf16[2,416,128]{2,1,0:T(8,128)(2,1)S(1)}, u32[]{:S(2)}, u32[]{:S(2)}) collective-permute-start(bf16[2,416,128]{2,1,0:T(8,128)(2,1)S(1)} %get-tuple-element.54), channel_id=1, source_target_pairs={{0,6},{2,4},{4,2},{6,0},{8,14},{10,12},{12,10},{14,8},{1,7},{3,5},... | collective-permute-start | bytes 638984 | tf_op jit(solution)/shard_map/ppermute | solution.py:498
  42.1 0.1 collective-permute-start.10
  42.2 5.4 %early.5 = (f32[4,256,1024]{2,1,0:T(8,128)S(1)}, bf16[4,256,128]{2,1,0:T(8,128)(2,1)S(1)}, f32[4,16,256]{2,1,0:T(8,128)S(1)}, f32[4,256,256]{2,1,0:T(8,128)S(1)}...) custom-call(bf16[2,256,4096]{2,1,0:T(8,128)(2,1)} %refs_0_.5, ...), custom_call_target="tpu_custom_call", output_to_operand_aliasing={{0}: (10, {}), {1}: (11, {}), {2}: (12, {}), {3}: (13, {}),... | custom-call | flops 1 | bytes 1 | tf_op jit(solution)/shard_map/early/pallas_call | solution.py:596
  47.6 0.0 collective-permute-done.7.refs_9_.refs_2_.refs_6_
  47.6 7.1 %collective-permute-done.8.refs_10_.refs_3_.refs_7_ = bf16[2,416,128]{2,1,0:T(8,128)(2,1)S(1)} collective-permute-done((bf16[2,416,128]{2,1,0:T(8,128)(2,1)S(1)}, bf16[2,416,128]{2,1,0:T(8,128)(2,1)S(1)}, u32[]{:S(2)}, u32[]{:S(2)}) %collective-permute-start.8) | collective-permute-done | bytes 213024 | tf_op jit(solution)/shard_map/ppermute | solution.py:498
  54.7 4.6 %collective-permute-done.9.refs_11_.refs_4_.refs_8_ = bf16[2,416,128]{2,1,0:T(8,128)(2,1)S(1)} collective-permute-done((bf16[2,416,128]{2,1,0:T(8,128)(2,1)S(1)}, bf16[2,416,128]{2,1,0:T(8,128)(2,1)S(1)}, u32[]{:S(2)}, u32[]{:S(2)}) %collective-permute-start.9) | collective-permute-done | bytes 213024 | tf_op jit(solution)/shard_map/ppermute | solution.py:498
  59.2 0.0 collective-permute-done.11.refs_6_
  59.2 1.1 %pick_states.4 = (bf16[2,384,128]{2,1,0:T(8,128)(2,1)S(1)}, bf16[2,384,128]{2,1,0:T(8,128)(2,1)S(1)}, bf16[2,384,128]{2,1,0:T(8,128)(2,1)S(1)}, bf16[2,384,128]{2,1,0:T(8,128)(2,1)S(1)}) custom-call(s32[8]{0:T(128)S(1)} %broadcast_xor_fusion.refs_10_.refs_0_, bf16[1056,128]{1,0:T(8,128)(2,1)S(1)} %get-tuple-element.42.refs_9_.refs_1_, ...), custom_call_target="tpu_custom_call" | custom-call | flops 1 | bytes 1 | tf_op jit(solution)/shard_map/pick_states/pallas_call | solution.py:563
  60.3 0.6 collective-permute-start.15
  60.8 0.4 collective-permute-start.16
  61.2 2.6 %collective-permute-start.17 = (bf16[2,384,128]{2,1,0:T(8,128)(2,1)S(1)}, bf16[2,384,128]{2,1,0:T(8,128)(2,1)S(1)}, u32[]{:S(2)}, u32[]{:S(2)}) collective-permute-start(bf16[2,384,128]{2,1,0:T(8,128)(2,1)S(1)} %get-tuple-element.78), channel_id=1, source_target_pairs={{0,6},{2,4},{4,2},{6,0},{8,14},{10,12},{12,10},{14,8},{1,7},{3,5},... | collective-permute-start | bytes 589832 | tf_op jit(solution)/shard_map/ppermute | solution.py:498
  63.8 1.5 %collective-permute-done.10.refs_6_ = bf16[4,256,128]{2,1,0:T(8,128)(2,1)S(1)} collective-permute-done((bf16[4,256,128]{2,1,0:T(8,128)(2,1)S(1)}, bf16[4,256,128]{2,1,0:T(8,128)(2,1)S(1)}, u32[]{:S(2)}, u32[]{:S(2)}) %collective-permute-start.10) | collective-permute-done | bytes 262176 | tf_op jit(solution)/shard_map/ppermute | solution.py:498
  65.4 1.2 %pick_states.5 = (bf16[2,256,128]{2,1,0:T(8,128)(2,1)S(1)}, bf16[2,256,128]{2,1,0:T(8,128)(2,1)S(1)}, bf16[2,256,128]{2,1,0:T(8,128)(2,1)S(1)}, bf16[2,256,128]{2,1,0:T(8,128)(2,1)S(1)}) custom-call(s32[8]{0:T(128)S(1)} %broadcast_xor_fusion.refs_10_.refs_0_, bf16[1056,128]{1,0:T(8,128)(2,1)S(1)} %get-tuple-element.42.refs_9_.refs_1_, ...), custom_call_target="tpu_custom_call" | custom-call | flops 1 | bytes 1 | tf_op jit(solution)/shard_map/pick_states/pallas_call | solution.py:563
  66.6 0.6 collective-permute-start.12
  67.2 3.0 %collective-permute-start.14 = (bf16[2,256,128]{2,1,0:T(8,128)(2,1)S(1)}, bf16[2,256,128]{2,1,0:T(8,128)(2,1)S(1)}, u32[]{:S(2)}, u32[]{:S(2)}) collective-permute-start(bf16[2,256,128]{2,1,0:T(8,128)(2,1)S(1)} %get-tuple-element.65), channel_id=1, source_target_pairs={{0,6},{2,4},{4,2},{6,0},{8,14},{10,12},{12,10},{14,8},{1,7},{3,5},... | collective-permute-start | bytes 393224 | tf_op jit(solution)/shard_map/ppermute | solution.py:498
  70.2 3.7 %collective-permute-done.17.refs_12_ = bf16[2,384,128]{2,1,0:T(8,128)(2,1)S(1)} collective-permute-done((bf16[2,384,128]{2,1,0:T(8,128)(2,1)S(1)}, bf16[2,384,128]{2,1,0:T(8,128)(2,1)S(1)}, u32[]{:S(2)}, u32[]{:S(2)}) %collective-permute-start.17) | collective-permute-done | bytes 196640 | tf_op jit(solution)/shard_map/ppermute | solution.py:498
  73.9 5.7 %late.2.refs_21_ = bf16[2,256,4096]{2,1,0:T(8,128)(2,1)} custom-call(s32[1]{0:T(128)} %bitcast.place_ref.refs_0_, bf16[2,416,128]{2,1,0:T(8,128)(2,1)S(1)} %get-tuple-element.51.refs_6_.refs_8_.refs_1_.refs_5_, bf16[2,416,128]{2,1,0:T(8,128)(2,1)S(1)} %collective-permute-done.7.refs_9_.refs_2_.refs_6_, ...), custom_call_target="tpu_custom_call" | custom-call | flops 1 | bytes 1 | tf_op jit(solution)/shard_map/late/pallas_call | solution.py:645
  79.7 0.0 collective-permute-done.12.refs_6_
  79.7 0.0 collective-permute-done.13.refs_7_
  79.7 2.9 %late.3 = bf16[2,256,4096]{2,1,0:T(8,128)(2,1)} custom-call(s32[1]{0:T(128)} %bitcast.place_ref.refs_0_, bf16[2,416,128]{2,1,0:T(8,128)(2,1)S(1)} %get-tuple-element.51.refs_6_.refs_8_.refs_1_.refs_5_, bf16[2,416,128]{2,1,0:T(8,128)(2,1)S(1)} %collective-permute-done.7.refs_9_.refs_2_.refs_6_, ...), custom_call_target="tpu_custom_call", output_to_operand_aliasing={{}: (21, {})} | custom-call | flops 1 | bytes 1 | tf_op jit(solution)/shard_map/late/pallas_call | solution.py:645
  (20 shorter events, 0.1 us)
Async XLA Ops:
  0.0 9.1 %copy-start.3 = (s32[8]{0:T(128)S(1)}, s32[8]{0:T(128)}, u32[]{:S(2)}) copy-start(s32[8]{0:T(128)} %param.26) | copy-start | bytes 100
  0.0 9.2 %copy-start.4 = (s32[16]{0:T(128)S(1)}, s32[16]{0:T(128)}, u32[]{:S(2)}) copy-start(s32[16]{0:T(128)} %param.27) | copy-start | bytes 196
  0.0 9.5 %copy-start = (f32[64]{0:T(128)S(1)}, f32[64]{0:T(128)}, u32[]{:S(2)}) copy-start(f32[64]{0:T(128)} %param.18) | copy-start | bytes 772
  0.0 9.6 %copy-start.1 = (f32[64]{0:T(128)S(1)}, f32[64]{0:T(128)}, u32[]{:S(2)}) copy-start(f32[64]{0:T(128)} %param.19) | copy-start | bytes 772
  0.0 9.7 %copy-start.2 = (f32[64]{0:T(128)S(1)}, f32[64]{0:T(128)}, u32[]{:S(2)}) copy-start(f32[64]{0:T(128)} %param.20) | copy-start | bytes 772
  1.9 19.4 %collective-permute-start.4 = (bf16[2,416,128]{2,1,0:T(8,128)(2,1)S(1)}, bf16[2,416,128]{2,1,0:T(8,128)(2,1)S(1)}, u32[]{:S(2)}, u32[]{:S(2)}) collective-permute-start(bf16[2,416,128]{2,1,0:T(8,128)(2,1)S(1)} %get-tuple-element.48), channel_id=1, source_target_pairs={{0,8},{2,10},{4,12},{6,14},{8,0},{10,2},{12,4},{14,6},{1,9},{3,11}... | collective-permute-start | bytes 638984 | tf_op jit(solution)/shard_map/ppermute | solution.py:498
  6.0 15.3 %collective-permute-start.5 = (bf16[2,416,128]{2,1,0:T(8,128)(2,1)S(1)}, bf16[2,416,128]{2,1,0:T(8,128)(2,1)S(1)}, u32[]{:S(2)}, u32[]{:S(2)}) collective-permute-start(bf16[2,416,128]{2,1,0:T(8,128)(2,1)S(1)} %get-tuple-element.49), channel_id=1, source_target_pairs={{0,12},{2,14},{4,8},{6,10},{8,4},{10,6},{12,0},{14,2},{1,13},{3,15... | collective-permute-start | bytes 638984 | tf_op jit(solution)/shard_map/ppermute | solution.py:498
  7.3 25.4 %collective-permute-start.1 = (bf16[1056,128]{1,0:T(8,128)(2,1)S(1)}, bf16[1056,128]{1,0:T(8,128)(2,1)S(1)}, u32[]{:S(2)}, u32[]{:S(2)}) collective-permute-start(bf16[1056,128]{1,0:T(8,128)(2,1)S(1)} %get-tuple-element.44), channel_id=1, source_target_pairs={{0,4},{2,6},{4,0},{6,2},{8,12},{10,14},{12,8},{14,10},{1,5},{3,7},... | collective-permute-start | bytes 811016 | tf_op jit(solution)/shard_map/ppermute | solution.py:498
  7.6 13.5 %collective-permute-start = (bf16[2,1056,128]{2,1,0:T(8,128)(2,1)S(1)}, bf16[2,1056,128]{2,1,0:T(8,128)(2,1)S(1)}, u32[]{:S(2)}, u32[]{:S(2)}) collective-permute-start(bf16[2,1056,128]{2,1,0:T(8,128)(2,1)S(1)} %get-tuple-element.43), channel_id=1, source_target_pairs={{0,2},{2,0},{4,6},{6,4},{8,10},{10,8},{12,14},{14,12},{1,3},{3,1},... | collective-permute-start | bytes 1622024 | tf_op jit(solution)/shard_map/ppermute | solution.py:498
  21.3 12.4 %collective-permute-start.6 = (bf16[2,416,128]{2,1,0:T(8,128)(2,1)S(1)}, bf16[2,416,128]{2,1,0:T(8,128)(2,1)S(1)}, u32[]{:S(2)}, u32[]{:S(2)}) collective-permute-start(bf16[2,416,128]{2,1,0:T(8,128)(2,1)S(1)} %stack_first.1.refs_9_), channel_id=1, source_target_pairs={{0,2},{2,0},{4,6},{6,4},{8,10},{10,8},{12,14},{14,12},{1,3},{3,1},... | collective-permute-start | bytes 638984 | tf_op jit(solution)/shard_map/ppermute | solution.py:498
  23.2 10.5 %collective-permute-start.3 = (bf16[640,128]{1,0:T(8,128)(2,1)S(1)}, bf16[640,128]{1,0:T(8,128)(2,1)S(1)}, u32[]{:S(2)}, u32[]{:S(2)}) collective-permute-start(bf16[640,128]{1,0:T(8,128)(2,1)S(1)} %get-tuple-element.47), channel_id=1, source_target_pairs={{0,4},{2,6},{4,0},{6,2},{8,12},{10,14},{12,8},{14,10},{1,5},{3,7},... | collective-permute-start | bytes 491528 | tf_op jit(solution)/shard_map/ppermute | solution.py:498
  27.3 6.4 %collective-permute-start.2 = (bf16[416,128]{1,0:T(8,128)(2,1)S(1)}, bf16[416,128]{1,0:T(8,128)(2,1)S(1)}, u32[]{:S(2)}, u32[]{:S(2)}) collective-permute-start(bf16[416,128]{1,0:T(8,128)(2,1)S(1)} %get-tuple-element.46.refs_3_), channel_id=1, source_target_pairs={{0,4},{2,6},{4,0},{6,2},{8,12},{10,14},{12,8},{14,10},{1,5},{3,7},... | collective-permute-start | bytes 319496 | tf_op jit(solution)/shard_map/ppermute | solution.py:498
  33.7 25.5 %collective-permute-start.11 = (bf16[4,384,128]{2,1,0:T(8,128)(2,1)S(1)}, bf16[4,384,128]{2,1,0:T(8,128)(2,1)S(1)}, u32[]{:S(2)}, u32[]{:S(2)}) collective-permute-start(bf16[4,384,128]{2,1,0:T(8,128)(2,1)S(1)} %stack_later.2.refs_9_), channel_id=1, source_target_pairs={{0,8},{2,10},{4,12},{6,14},{8,0},{10,2},{12,4},{14,6},{1,9},{3,11}... | collective-permute-start | bytes 1179656 | tf_op jit(solution)/shard_map/ppermute | solution.py:498
  38.5 9.1 %collective-permute-start.7 = (bf16[2,416,128]{2,1,0:T(8,128)(2,1)S(1)}, bf16[2,416,128]{2,1,0:T(8,128)(2,1)S(1)}, u32[]{:S(2)}, u32[]{:S(2)}) collective-permute-start(bf16[2,416,128]{2,1,0:T(8,128)(2,1)S(1)} %get-tuple-element.52), channel_id=1, source_target_pairs={{0,2},{2,0},{4,6},{6,4},{8,10},{10,8},{12,14},{14,12},{1,3},{3,1},... | collective-permute-start | bytes 638984 | tf_op jit(solution)/shard_map/ppermute | solution.py:498
  39.1 15.6 %collective-permute-start.8 = (bf16[2,416,128]{2,1,0:T(8,128)(2,1)S(1)}, bf16[2,416,128]{2,1,0:T(8,128)(2,1)S(1)}, u32[]{:S(2)}, u32[]{:S(2)}) collective-permute-start(bf16[2,416,128]{2,1,0:T(8,128)(2,1)S(1)} %get-tuple-element.53), channel_id=1, source_target_pairs={{0,4},{2,6},{4,0},{6,2},{8,12},{10,14},{12,8},{14,10},{1,5},{3,7},... | collective-permute-start | bytes 638984 | tf_op jit(solution)/shard_map/ppermute | solution.py:498
  39.4 19.8 %collective-permute-start.9 = (bf16[2,416,128]{2,1,0:T(8,128)(2,1)S(1)}, bf16[2,416,128]{2,1,0:T(8,128)(2,1)S(1)}, u32[]{:S(2)}, u32[]{:S(2)}) collective-permute-start(bf16[2,416,128]{2,1,0:T(8,128)(2,1)S(1)} %get-tuple-element.54), channel_id=1, source_target_pairs={{0,6},{2,4},{4,2},{6,0},{8,14},{10,12},{12,10},{14,8},{1,7},{3,5},... | collective-permute-start | bytes 638984 | tf_op jit(solution)/shard_map/ppermute | solution.py:498
  42.1 23.3 %collective-permute-start.10 = (bf16[4,256,128]{2,1,0:T(8,128)(2,1)S(1)}, bf16[4,256,128]{2,1,0:T(8,128)(2,1)S(1)}, u32[]{:S(2)}, u32[]{:S(2)}) collective-permute-start(bf16[4,256,128]{2,1,0:T(8,128)(2,1)S(1)} %stack_later.3.refs_9_), channel_id=1, source_target_pairs={{0,8},{2,10},{4,12},{6,14},{8,0},{10,2},{12,4},{14,6},{1,9},{3,11}... | collective-permute-start | bytes 786440 | tf_op jit(solution)/shard_map/ppermute | solution.py:498
  60.3 6.9 %collective-permute-start.15 = (bf16[2,384,128]{2,1,0:T(8,128)(2,1)S(1)}, bf16[2,384,128]{2,1,0:T(8,128)(2,1)S(1)}, u32[]{:S(2)}, u32[]{:S(2)}) collective-permute-start(bf16[2,384,128]{2,1,0:T(8,128)(2,1)S(1)} %get-tuple-element.76), channel_id=1, source_target_pairs={{0,2},{2,0},{4,6},{6,4},{8,10},{10,8},{12,14},{14,12},{1,3},{3,1},... | collective-permute-start | bytes 589832 | tf_op jit(solution)/shard_map/ppermute | solution.py:498
  60.8 9.3 %collective-permute-start.16 = (bf16[2,384,128]{2,1,0:T(8,128)(2,1)S(1)}, bf16[2,384,128]{2,1,0:T(8,128)(2,1)S(1)}, u32[]{:S(2)}, u32[]{:S(2)}) collective-permute-start(bf16[2,384,128]{2,1,0:T(8,128)(2,1)S(1)} %get-tuple-element.77), channel_id=1, source_target_pairs={{0,4},{2,6},{4,0},{6,2},{8,12},{10,14},{12,8},{14,10},{1,5},{3,7},... | collective-permute-start | bytes 589832 | tf_op jit(solution)/shard_map/ppermute | solution.py:498
  61.2 12.7 %collective-permute-start.17 = (bf16[2,384,128]{2,1,0:T(8,128)(2,1)S(1)}, bf16[2,384,128]{2,1,0:T(8,128)(2,1)S(1)}, u32[]{:S(2)}, u32[]{:S(2)}) collective-permute-start(bf16[2,384,128]{2,1,0:T(8,128)(2,1)S(1)} %get-tuple-element.78), channel_id=1, source_target_pairs={{0,6},{2,4},{4,2},{6,0},{8,14},{10,12},{12,10},{14,8},{1,7},{3,5},... | collective-permute-start | bytes 589832 | tf_op jit(solution)/shard_map/ppermute | solution.py:498
  66.6 13.0 %collective-permute-start.12 = (bf16[2,256,128]{2,1,0:T(8,128)(2,1)S(1)}, bf16[2,256,128]{2,1,0:T(8,128)(2,1)S(1)}, u32[]{:S(2)}, u32[]{:S(2)}) collective-permute-start(bf16[2,256,128]{2,1,0:T(8,128)(2,1)S(1)} %get-tuple-element.63), channel_id=1, source_target_pairs={{0,2},{2,0},{4,6},{6,4},{8,10},{10,8},{12,14},{14,12},{1,3},{3,1},... | collective-permute-start | bytes 393224 | tf_op jit(solution)/shard_map/ppermute | solution.py:498
  67.2 12.5 %collective-permute-start.13 = (bf16[2,256,128]{2,1,0:T(8,128)(2,1)S(1)}, bf16[2,256,128]{2,1,0:T(8,128)(2,1)S(1)}, u32[]{:S(2)}, u32[]{:S(2)}) collective-permute-start(bf16[2,256,128]{2,1,0:T(8,128)(2,1)S(1)} %get-tuple-element.64), channel_id=1, source_target_pairs={{0,4},{2,6},{4,0},{6,2},{8,12},{10,14},{12,8},{14,10},{1,5},{3,7},... | collective-permute-start | bytes 393224 | tf_op jit(solution)/shard_map/ppermute | solution.py:498
  67.2 12.5 %collective-permute-start.14 = (bf16[2,256,128]{2,1,0:T(8,128)(2,1)S(1)}, bf16[2,256,128]{2,1,0:T(8,128)(2,1)S(1)}, u32[]{:S(2)}, u32[]{:S(2)}) collective-permute-start(bf16[2,256,128]{2,1,0:T(8,128)(2,1)S(1)} %get-tuple-element.65), channel_id=1, source_target_pairs={{0,6},{2,4},{4,2},{6,0},{8,14},{10,12},{12,10},{14,8},{1,7},{3,5},... | collective-permute-start | bytes 393224 | tf_op jit(solution)/shard_map/ppermute | solution.py:498

commit v22 on v17

--- a/solution.py
+++ b/solution.py
@@ -122,7 +122,7 @@
         ] * x_conv.astype(jnp.float32)
 
 
-def late_kernel(offset, heads, lines, reach, tail_at, place_ref, *refs):
+def late_kernel(places, offset, heads, lines, reach, tail_at, place_ref, *refs):
     count = len(heads)
     tails, states, parts = refs[:4], refs[4 : 4 + 4 * count], refs[4 + 4 * count : -4]
     y_ref, padded, y_part, sems = refs[-4:]
@@ -142,8 +142,9 @@
         per_group = column_ref.shape[1]
         group_wide = opening_ref.shape[2] - 2 * size
         tail_rows = pl.ds(tail_at, -(-lines * reach // 16) * 16)
-        tail = tails[j][kid, tail_rows].astype(jnp.float32)
-        state = jnp.concatenate([states[4 * n + j][kid, : rows[n]] for n in range(count)])
+        tail = tails[places[0].index(j)][kid, tail_rows].astype(jnp.float32)
+        blocks = [states[4 * n + places[1 + n].index(j)] for n in range(count)]
+        state = jnp.concatenate([ref[kid, : rows[n]] for n, ref in enumerate(blocks)])
 
         def opening(start, stop, at):
             tap_rows = []
@@ -575,14 +576,14 @@
             name=name,
         )(scalars, *map(keep_in_vmem, sources), *tokens)
 
-    def pick(rows, sources, choices, tokens):
+    def pick(rows, sources, choices, tokens, order=(1, 2, 3)):
         moves = [
             (j, kid, j * kids + kid, choices) for j in range(4) for kid in range(kids)
         ]
         picked = rearrange(
             slots, sources, moves, [(kids, rows, size)] * 4, tokens, "pick_states"
         )
-        return [picked[0]] + [swap(picked[j], j) for j in range(1, 4)]
+        return [(0, picked[0])] + [(j, swap(picked[j], j)) for j in order]
 
     def early(c, pieces, piece, before, tokens):
         per = groups // pieces
@@ -629,7 +630,9 @@
     def late(ks, states, parts, result, tokens):
         offset = offsets[ks[0]]
         chunk = sum(SPLIT[k] for k in ks) * width
-        operands = [keep_in_vmem(a) for a in (*states[0], *sum((states[k] for k in ks), []), *parts[0], *parts[1])]
+        places = [[j for j, _ in chunk_states] for chunk_states in states]
+        held = [array for chunk_states in states for _, array in chunk_states]
+        operands = [keep_in_vmem(a) for a in (*held[:4], *sum((held[4 * k : 4 * k + 4] for k in ks), []), *parts[0], *parts[1])]
         specs = [pl.BlockSpec(memory_space=pltpu.VMEM)] * len(operands)
         keep = 1 + len(operands)
         operands += tokens
@@ -640,7 +643,7 @@
             operands.append(result)
             specs.append(anywhere)
         kernel = functools.partial(
-            late_kernel, offset, [SPLIT[k] for k in ks], lines, reach, SPLIT[0] * width
+            late_kernel, [places[0]] + [places[k] for k in ks], offset, [SPLIT[k] for k in ks], lines, reach, SPLIT[0] * width
         )
         return pl.pallas_call(
             functools.partial(drop_tokens, kernel, keep, 1 + len(operands) - keep),
@@ -684,7 +687,7 @@
 
     def pick_later(k, crossed, tokens):
         choices = inside_rows(k) + [(4, j) for j in range(4)]
-        return pick(rows[k], [*inside, crossed], choices, tokens)
+        return pick(rows[k], [*inside, crossed], choices, tokens, (3, 2, 1))
 
     second = early(1, 2, 0, [], [turn])
     moves = [(0, n, None, [(n, 1)]) for n in range(2)]
@@ -697,10 +700,10 @@
     parts.append(second)
     choices = inside_rows(0) + [(4, 0), (6, 0), (5, 0), (6, 1)]
     states = [pick(rows[0], [*inside, *crossed_a, passed], choices, [second[1]])]
-    sent_c, crossed_c = cross(2, [states[0][0], crossed_b])
+    sent_c, crossed_c = cross(2, [states[0][0][1], crossed_b])
     states.append(pick_later(1, crossed_b, [sent_c]))
-    states.append(pick_later(2, crossed_c, [states[1][0]]))
-    result = late([0, 1], states, parts, None, [states[2][0]])
+    states.append(pick_later(2, crossed_c, [states[1][0][1]]))
+    result = late([0, 1], states, parts, None, [states[2][0][1]])
     return late([2], states, parts, result, [])
 
 

time: 79.4 us -> 79.5 us (level)
  starting transfers between devices: 26.8 us -> 25 us
  waiting for transfers between devices: 17 us -> 18.8 us
    ppermute x17, waiting for transfers between devices: 17 us -> 18.8 us  [swap(): return lax.ppermute(value, 'batch', perm=[(i, i ^ r) for i in range(8)])]
    ppermute x17, starting transfers between devices: 26.8 us -> 25 us  [swap(): return lax.ppermute(value, 'batch', perm=[(i, i ^ r) for i in range(8)])]
  transfers between devices with their start and end apart: 17 -> 17, of which waited for: 6 -> 8; matrix products, arithmetic and copies ran while one was open for 1% -> 1% of each run, Pallas kernels for 37% -> 37%
where the time goes in v22:
time: 79.5 us; the launch traced here: 79.3 us
  Pallas kernels  34.3 us (43%)
  starting transfers between devices  25 us (31%)
  waiting for transfers between devices  18.8 us (24%)
    ppermute x17, starting transfers between devices, swap(): return lax.ppermute(value, 'batch', perm=[(i, i ^ r) for i in range(8)])  25 us
    pallas_call x3, Pallas kernels, early(): pl.pallas_call(functools.partial(drop_tokens, functools.partial(early_ker...  20.4 us
    ppermute x17, waiting for transfers between devices, swap(): return lax.ppermute(value, 'batch', perm=[(i, i ^ r) for i in range(8)])  18.8 us
    pallas_call x2, Pallas kernels, late(): pl.pallas_call(functools.partial(drop_tokens, kernel, keep, 1 + len(opera...  8.66 us
    pallas_call x7, Pallas kernels, rearrange(): pl.pallas_call(functools.partial(drop_tokens, kernel, 1 + len(sources), l...  3.45 us
    pallas_call x1, Pallas kernels, cast(): pl.pallas_call(kernel, grid_spec=pltpu.PrefetchScalarGridSpec(num_scalar_...  1.82 us
  transfers between devices with their start and end apart: 17, of which 8 were waited for; matrix products, arithmetic and copies ran while one was open for 1% of the time, Pallas kernels for 37%

profile of v22, /device:TPU:0, one launch (start us, length us, event | category | flops | bytes accessed | tf_op | source)
XLA Modules:
  0.0 79.3 jit_solution(9468984075662499257)
XLA Ops:
  0.0 1.8 %cast_states.1 = (bf16[1056,128]{1,0:T(8,128)(2,1)S(1)}, bf16[1056,128]{1,0:T(8,128)(2,1)S(1)}, bf16[2,1056,128]{2,1,0:T(8,128)(2,1)S(1)}, bf16[2,544,128]{2,1,0:T(8,128)(2,1)S(1)}, bf16[2,544,128]{2,1,0:T(8,128)(2,1)S(1)}) custom-call(s32[1]{0:T(128)} %bitcast.place_ref.refs_0_, f32[4,16,64,128]{3,2,1,0:T(8,128)} %bitcast.5, f32[4,16,64,128]{3,2,1,0:T(8,128)} %bitcast.6, ...), custom_call_target="tpu_custom_call" | custom-call | flops 1 | bytes 1 | tf_op jit(solution)/shard_map/cast_states/pallas_call | solution.py:532
  1.8 3.1 %collective-permute-start.1 = (bf16[1056,128]{1,0:T(8,128)(2,1)S(1)}, bf16[1056,128]{1,0:T(8,128)(2,1)S(1)}, u32[]{:S(2)}, u32[]{:S(2)}) collective-permute-start(bf16[1056,128]{1,0:T(8,128)(2,1)S(1)} %get-tuple-element.42), channel_id=1, source_target_pairs={{0,4},{2,6},{4,0},{6,2},{8,12},{10,14},{12,8},{14,10},{1,5},{3,7},... | collective-permute-start | bytes 811016 | tf_op jit(solution)/shard_map/ppermute | solution.py:499
  4.9 2.6 %collective-permute-start.3 = (bf16[2,544,128]{2,1,0:T(8,128)(2,1)S(1)}, bf16[2,544,128]{2,1,0:T(8,128)(2,1)S(1)}, u32[]{:S(2)}, u32[]{:S(2)}) collective-permute-start(bf16[2,544,128]{2,1,0:T(8,128)(2,1)S(1)} %get-tuple-element.44), channel_id=1, source_target_pairs={{0,8},{2,10},{4,12},{6,14},{8,0},{10,2},{12,4},{14,6},{1,9},{3,11}... | collective-permute-start | bytes 835592 | tf_op jit(solution)/shard_map/ppermute | solution.py:499
  7.5 0.0 collective-permute-start.4
  7.5 1.7 %collective-permute-start = (bf16[2,1056,128]{2,1,0:T(8,128)(2,1)S(1)}, bf16[2,1056,128]{2,1,0:T(8,128)(2,1)S(1)}, u32[]{:S(2)}, u32[]{:S(2)}) collective-permute-start(bf16[2,1056,128]{2,1,0:T(8,128)(2,1)S(1)} %get-tuple-element.41), channel_id=1, source_target_pairs={{0,2},{2,0},{4,6},{6,4},{8,10},{10,8},{12,14},{14,12},{1,3},{3,1},... | collective-permute-start | bytes 1622024 | tf_op jit(solution)/shard_map/ppermute | solution.py:499
  9.3 0.1 select_reduce_fusion.1
  9.4 0.1 convert_reduce_fusion
  9.5 0.2 select_reduce_fusion
  9.7 0.1 copy.28.refs_4_
  9.8 0.1 copy.29.refs_5_
  9.9 0.1 broadcast_in_dim.55
  10.0 0.1 broadcast_in_dim_reshape.3.refs_6_
  10.1 9.6 %early.3 = (f32[4,256,1024]{2,1,0:T(8,128)S(1)}, bf16[4,256,128]{2,1,0:T(8,128)(2,1)S(1)}, f32[4,16,256]{2,1,0:T(8,128)S(1)}, f32[4,256,256]{2,1,0:T(8,128)S(1)}...) custom-call(bf16[2,256,4096]{2,1,0:T(8,128)(2,1)} %refs_0_.5, bf16[2,256,512]{2,1,0:T(8,128)(2,1)} %refs_1_.5, ...), custom_call_target="tpu_custom_call" | custom-call | flops 1 | bytes 1 | tf_op jit(solution)/shard_map/early/pallas_call | solution.py:597
  19.7 1.3 %collective-permute-done.refs_1_.refs_2_ = bf16[2,1056,128]{2,1,0:T(8,128)(2,1)S(1)} collective-permute-done((bf16[2,1056,128]{2,1,0:T(8,128)(2,1)S(1)}, bf16[2,1056,128]{2,1,0:T(8,128)(2,1)S(1)}, u32[]{:S(2)}, u32[]{:S(2)}) %collective-permute-start) | collective-permute-done | bytes 540704 | tf_op jit(solution)/shard_map/ppermute | solution.py:499
  21.0 0.7 collective-permute-start.2
  21.7 5.4 %early.4 = (f32[4,256,1024]{2,1,0:T(8,128)S(1)}, bf16[4,256,128]{2,1,0:T(8,128)(2,1)S(1)}, f32[4,16,256]{2,1,0:T(8,128)S(1)}, f32[4,256,256]{2,1,0:T(8,128)S(1)}...) custom-call(bf16[2,256,4096]{2,1,0:T(8,128)(2,1)} %refs_0_.5, bf16[2,256,512]{2,1,0:T(8,128)(2,1)} %refs_1_.5, ...), custom_call_target="tpu_custom_call" | custom-call | flops 1 | bytes 1 | tf_op jit(solution)/shard_map/early/pallas_call | solution.py:597
  27.1 0.3 collective-permute-done.3.refs_1_.refs_5_
  27.4 0.0 collective-permute-done.4.refs_2_.refs_6_
  27.4 1.6 %collective-permute-start.5 = (bf16[2,544,128]{2,1,0:T(8,128)(2,1)S(1)}, bf16[2,544,128]{2,1,0:T(8,128)(2,1)S(1)}, u32[]{:S(2)}, u32[]{:S(2)}) collective-permute-start(bf16[2,544,128]{2,1,0:T(8,128)(2,1)S(1)} %stack_first.1.refs_5_), channel_id=1, source_target_pairs={{0,2},{2,0},{4,6},{6,4},{8,10},{10,8},{12,14},{14,12},{1,3},{3,1},... | collective-permute-start | bytes 835592 | tf_op jit(solution)/shard_map/ppermute | solution.py:499
  29.0 0.0 collective-permute-done.1.refs_3_
  29.0 3.3 %collective-permute-done.2.refs_4_ = bf16[1056,128]{1,0:T(8,128)(2,1)S(1)} collective-permute-done((bf16[1056,128]{1,0:T(8,128)(2,1)S(1)}, bf16[1056,128]{1,0:T(8,128)(2,1)S(1)}, u32[]{:S(2)}, u32[]{:S(2)}) %collective-permute-start.2) | collective-permute-done | bytes 270368 | tf_op jit(solution)/shard_map/ppermute | solution.py:499
  32.3 2.9 %collective-permute-start.9 = (bf16[4,256,128]{2,1,0:T(8,128)(2,1)S(1)}, bf16[4,256,128]{2,1,0:T(8,128)(2,1)S(1)}, u32[]{:S(2)}, u32[]{:S(2)}) collective-permute-start(bf16[4,256,128]{2,1,0:T(8,128)(2,1)S(1)} %stack_later.2.refs_9_), channel_id=1, source_target_pairs={{0,8},{2,10},{4,12},{6,14},{8,0},{10,2},{12,4},{14,6},{1,9},{3,11}... | collective-permute-start | bytes 786440 | tf_op jit(solution)/shard_map/ppermute | solution.py:499
  35.2 5.4 %early.5 = (f32[4,256,1024]{2,1,0:T(8,128)S(1)}, bf16[4,256,128]{2,1,0:T(8,128)(2,1)S(1)}, f32[4,16,256]{2,1,0:T(8,128)S(1)}, f32[4,256,256]{2,1,0:T(8,128)S(1)}...) custom-call(bf16[2,256,4096]{2,1,0:T(8,128)(2,1)} %refs_0_.5, ...), custom_call_target="tpu_custom_call", output_to_operand_aliasing={{0}: (10, {}), {1}: (11, {}), {2}: (12, {}), {3}: (13, {}),... | custom-call | flops 1 | bytes 1 | tf_op jit(solution)/shard_map/early/pallas_call | solution.py:597
  40.6 0.0 collective-permute-done.5.refs_7_
  40.6 1.1 %pick_states.3 = (bf16[2,544,128]{2,1,0:T(8,128)(2,1)S(1)}, bf16[2,544,128]{2,1,0:T(8,128)(2,1)S(1)}, bf16[2,544,128]{2,1,0:T(8,128)(2,1)S(1)}, bf16[2,544,128]{2,1,0:T(8,128)(2,1)S(1)}) custom-call(s32[8]{0:T(128)S(1)} %broadcast_xor_fusion.refs_10_.refs_0_, bf16[1056,128]{1,0:T(8,128)(2,1)S(1)} %get-tuple-element.40.refs_9_.refs_1_, ...), custom_call_target="tpu_custom_call" | custom-call | flops 1 | bytes 1 | tf_op jit(solution)/shard_map/pick_states/pallas_call | solution.py:564
  41.7 0.6 collective-permute-start.6
  42.3 0.7 collective-permute-start.7
  42.9 2.3 %collective-permute-start.8 = (bf16[2,544,128]{2,1,0:T(8,128)(2,1)S(1)}, bf16[2,544,128]{2,1,0:T(8,128)(2,1)S(1)}, u32[]{:S(2)}, u32[]{:S(2)}) collective-permute-start(bf16[2,544,128]{2,1,0:T(8,128)(2,1)S(1)} %get-tuple-element.56), channel_id=1, source_target_pairs={{0,6},{2,4},{4,2},{6,0},{8,14},{10,12},{12,10},{14,8},{1,7},{3,5},... | collective-permute-start | bytes 835592 | tf_op jit(solution)/shard_map/ppermute | solution.py:499
  45.2 1.7 %collective-permute-done.9.refs_6_.refs_5_ = bf16[4,256,128]{2,1,0:T(8,128)(2,1)S(1)} collective-permute-done((bf16[4,256,128]{2,1,0:T(8,128)(2,1)S(1)}, bf16[4,256,128]{2,1,0:T(8,128)(2,1)S(1)}, u32[]{:S(2)}, u32[]{:S(2)}) %collective-permute-start.9) | collective-permute-done | bytes 262176 | tf_op jit(solution)/shard_map/ppermute | solution.py:499
  46.9 0.1 collective-permute-start.10
  47.0 1.1 %pick_states.4 = (bf16[2,256,128]{2,1,0:T(8,128)(2,1)S(1)}, bf16[2,256,128]{2,1,0:T(8,128)(2,1)S(1)}, bf16[2,256,128]{2,1,0:T(8,128)(2,1)S(1)}, bf16[2,256,128]{2,1,0:T(8,128)(2,1)S(1)}) custom-call(s32[8]{0:T(128)S(1)} %broadcast_xor_fusion.refs_10_.refs_0_, bf16[1056,128]{1,0:T(8,128)(2,1)S(1)} %get-tuple-element.40.refs_9_.refs_1_, ...), custom_call_target="tpu_custom_call" | custom-call | flops 1 | bytes 1 | tf_op jit(solution)/shard_map/pick_states/pallas_call | solution.py:564
  48.1 3.1 %collective-permute-start.14 = (bf16[2,256,128]{2,1,0:T(8,128)(2,1)S(1)}, bf16[2,256,128]{2,1,0:T(8,128)(2,1)S(1)}, u32[]{:S(2)}, u32[]{:S(2)}) collective-permute-start(bf16[2,256,128]{2,1,0:T(8,128)(2,1)S(1)} %get-tuple-element.72), channel_id=1, source_target_pairs={{0,6},{2,4},{4,2},{6,0},{8,14},{10,12},{12,10},{14,8},{1,7},{3,5},... | collective-permute-start | bytes 393224 | tf_op jit(solution)/shard_map/ppermute | solution.py:499
  51.2 0.0 collective-permute-done.6.refs_2_.refs_6_
  51.2 0.0 collective-permute-start.15
  51.2 10.5 %collective-permute-done.10.refs_5_ = bf16[4,256,128]{2,1,0:T(8,128)(2,1)S(1)} collective-permute-done((bf16[4,256,128]{2,1,0:T(8,128)(2,1)S(1)}, bf16[4,256,128]{2,1,0:T(8,128)(2,1)S(1)}, u32[]{:S(2)}, u32[]{:S(2)}) %collective-permute-start.10) | collective-permute-done | bytes 262176 | tf_op jit(solution)/shard_map/ppermute | solution.py:499
  61.6 0.8 %collective-permute-start.16 = (bf16[2,256,128]{2,1,0:T(8,128)(2,1)S(1)}, bf16[2,256,128]{2,1,0:T(8,128)(2,1)S(1)}, u32[]{:S(2)}, u32[]{:S(2)}) collective-permute-start(bf16[2,256,128]{2,1,0:T(8,128)(2,1)S(1)} %get-tuple-element.74), channel_id=1, source_target_pairs={{0,2},{2,0},{4,6},{6,4},{8,10},{10,8},{12,14},{14,12},{1,3},{3,1},... | collective-permute-start | bytes 393224 | tf_op jit(solution)/shard_map/ppermute | solution.py:499
  62.5 1.2 %pick_states.5 = (bf16[2,256,128]{2,1,0:T(8,128)(2,1)S(1)}, bf16[2,256,128]{2,1,0:T(8,128)(2,1)S(1)}, bf16[2,256,128]{2,1,0:T(8,128)(2,1)S(1)}, bf16[2,256,128]{2,1,0:T(8,128)(2,1)S(1)}) custom-call(s32[8]{0:T(128)S(1)} %broadcast_xor_fusion.refs_10_.refs_0_, bf16[1056,128]{1,0:T(8,128)(2,1)S(1)} %get-tuple-element.40.refs_9_.refs_1_, ...), custom_call_target="tpu_custom_call" | custom-call | flops 1 | bytes 1 | tf_op jit(solution)/shard_map/pick_states/pallas_call | solution.py:564
  63.7 0.0 collective-permute-done.7.refs_3_.refs_7_
  63.7 3.7 %collective-permute-start.11 = (bf16[2,256,128]{2,1,0:T(8,128)(2,1)S(1)}, bf16[2,256,128]{2,1,0:T(8,128)(2,1)S(1)}, u32[]{:S(2)}, u32[]{:S(2)}) collective-permute-start(bf16[2,256,128]{2,1,0:T(8,128)(2,1)S(1)} %get-tuple-element.59), channel_id=1, source_target_pairs={{0,6},{2,4},{4,2},{6,0},{8,14},{10,12},{12,10},{14,8},{1,7},{3,5},... | collective-permute-start | bytes 393224 | tf_op jit(solution)/shard_map/ppermute | solution.py:499
  67.5 0.0 collective-permute-done.8.refs_4_.refs_8_
  67.5 0.1 collective-permute-done.14.refs_10_
  67.6 1.2 %collective-permute-start.13 = (bf16[2,256,128]{2,1,0:T(8,128)(2,1)S(1)}, bf16[2,256,128]{2,1,0:T(8,128)(2,1)S(1)}, u32[]{:S(2)}, u32[]{:S(2)}) collective-permute-start(bf16[2,256,128]{2,1,0:T(8,128)(2,1)S(1)} %get-tuple-element.61), channel_id=1, source_target_pairs={{0,2},{2,0},{4,6},{6,4},{8,10},{10,8},{12,14},{14,12},{1,3},{3,1},... | collective-permute-start | bytes 393224 | tf_op jit(solution)/shard_map/ppermute | solution.py:499
  68.8 1.3 %collective-permute-done.15.refs_11_ = bf16[2,256,128]{2,1,0:T(8,128)(2,1)S(1)} collective-permute-done((bf16[2,256,128]{2,1,0:T(8,128)(2,1)S(1)}, bf16[2,256,128]{2,1,0:T(8,128)(2,1)S(1)}, u32[]{:S(2)}, u32[]{:S(2)}) %collective-permute-start.15) | collective-permute-done | bytes 131104 | tf_op jit(solution)/shard_map/ppermute | solution.py:499
  70.1 0.3 collective-permute-done.16.refs_12_
  70.4 5.7 %late.2.refs_21_ = bf16[2,256,4096]{2,1,0:T(8,128)(2,1)} custom-call(s32[1]{0:T(128)} %bitcast.place_ref.refs_0_, bf16[2,544,128]{2,1,0:T(8,128)(2,1)S(1)} %get-tuple-element.53.refs_5_.refs_1_, bf16[2,544,128]{2,1,0:T(8,128)(2,1)S(1)} %collective-permute-done.6.refs_2_.refs_6_, bf16[2,544,128]{2,1,0:T(8,128)(2,1)S(1)} %collective-permute-done.7.refs_3_.refs_7_, ...), custom_call_target="tpu_custom_call" | custom-call | flops 1 | bytes 1 | tf_op jit(solution)/shard_map/late/pallas_call | solution.py:648
  76.2 0.0 collective-permute-done.11.refs_6_
  76.2 0.0 collective-permute-done.12.refs_7_
  76.2 2.9 %late.3 = bf16[2,256,4096]{2,1,0:T(8,128)(2,1)} custom-call(s32[1]{0:T(128)} %bitcast.place_ref.refs_0_, bf16[2,544,128]{2,1,0:T(8,128)(2,1)S(1)} %get-tuple-element.53.refs_5_.refs_1_, bf16[2,544,128]{2,1,0:T(8,128)(2,1)S(1)} %collective-permute-done.6.refs_2_.refs_6_, ...), custom_call_target="tpu_custom_call", output_to_operand_aliasing={{}: (21, {})} | custom-call | flops 1 | bytes 1 | tf_op jit(solution)/shard_map/late/pallas_call | solution.py:648
  (18 shorter events, 0.1 us)
Async XLA Ops:
  0.0 9.3 %copy-start.3 = (s32[8]{0:T(128)S(1)}, s32[8]{0:T(128)}, u32[]{:S(2)}) copy-start(s32[8]{0:T(128)} %param.26) | copy-start | bytes 100
  0.0 9.4 %copy-start.4 = (s32[16]{0:T(128)S(1)}, s32[16]{0:T(128)}, u32[]{:S(2)}) copy-start(s32[16]{0:T(128)} %param.27) | copy-start | bytes 196
  0.0 9.7 %copy-start = (f32[64]{0:T(128)S(1)}, f32[64]{0:T(128)}, u32[]{:S(2)}) copy-start(f32[64]{0:T(128)} %param.18) | copy-start | bytes 772
  0.0 9.8 %copy-start.1 = (f32[64]{0:T(128)S(1)}, f32[64]{0:T(128)}, u32[]{:S(2)}) copy-start(f32[64]{0:T(128)} %param.19) | copy-start | bytes 772
  0.0 9.9 %copy-start.2 = (f32[64]{0:T(128)S(1)}, f32[64]{0:T(128)}, u32[]{:S(2)}) copy-start(f32[64]{0:T(128)} %param.20) | copy-start | bytes 772
  1.8 27.2 %collective-permute-start.1 = (bf16[1056,128]{1,0:T(8,128)(2,1)S(1)}, bf16[1056,128]{1,0:T(8,128)(2,1)S(1)}, u32[]{:S(2)}, u32[]{:S(2)}) collective-permute-start(bf16[1056,128]{1,0:T(8,128)(2,1)S(1)} %get-tuple-element.42), channel_id=1, source_target_pairs={{0,4},{2,6},{4,0},{6,2},{8,12},{10,14},{12,8},{14,10},{1,5},{3,7},... | collective-permute-start | bytes 811016 | tf_op jit(solution)/shard_map/ppermute | solution.py:499
  4.9 22.5 %collective-permute-start.3 = (bf16[2,544,128]{2,1,0:T(8,128)(2,1)S(1)}, bf16[2,544,128]{2,1,0:T(8,128)(2,1)S(1)}, u32[]{:S(2)}, u32[]{:S(2)}) collective-permute-start(bf16[2,544,128]{2,1,0:T(8,128)(2,1)S(1)} %get-tuple-element.44), channel_id=1, source_target_pairs={{0,8},{2,10},{4,12},{6,14},{8,0},{10,2},{12,4},{14,6},{1,9},{3,11}... | collective-permute-start | bytes 835592 | tf_op jit(solution)/shard_map/ppermute | solution.py:499
  7.5 19.9 %collective-permute-start.4 = (bf16[2,544,128]{2,1,0:T(8,128)(2,1)S(1)}, bf16[2,544,128]{2,1,0:T(8,128)(2,1)S(1)}, u32[]{:S(2)}, u32[]{:S(2)}) collective-permute-start(bf16[2,544,128]{2,1,0:T(8,128)(2,1)S(1)} %get-tuple-element.45), channel_id=1, source_target_pairs={{0,12},{2,14},{4,8},{6,10},{8,4},{10,6},{12,0},{14,2},{1,13},{3,15... | collective-permute-start | bytes 835592 | tf_op jit(solution)/shard_map/ppermute | solution.py:499
  7.5 13.5 %collective-permute-start = (bf16[2,1056,128]{2,1,0:T(8,128)(2,1)S(1)}, bf16[2,1056,128]{2,1,0:T(8,128)(2,1)S(1)}, u32[]{:S(2)}, u32[]{:S(2)}) collective-permute-start(bf16[2,1056,128]{2,1,0:T(8,128)(2,1)S(1)} %get-tuple-element.41), channel_id=1, source_target_pairs={{0,2},{2,0},{4,6},{6,4},{8,10},{10,8},{12,14},{14,12},{1,3},{3,1},... | collective-permute-start | bytes 1622024 | tf_op jit(solution)/shard_map/ppermute | solution.py:499
  21.0 11.3 %collective-permute-start.2 = (bf16[1056,128]{1,0:T(8,128)(2,1)S(1)}, bf16[1056,128]{1,0:T(8,128)(2,1)S(1)}, u32[]{:S(2)}, u32[]{:S(2)}) collective-permute-start(bf16[1056,128]{1,0:T(8,128)(2,1)S(1)} %stack_turn.1.refs_9_), channel_id=1, source_target_pairs={{0,4},{2,6},{4,0},{6,2},{8,12},{10,14},{12,8},{14,10},{1,5},{3,7},... | collective-permute-start | bytes 811016 | tf_op jit(solution)/shard_map/ppermute | solution.py:499
  27.4 13.1 %collective-permute-start.5 = (bf16[2,544,128]{2,1,0:T(8,128)(2,1)S(1)}, bf16[2,544,128]{2,1,0:T(8,128)(2,1)S(1)}, u32[]{:S(2)}, u32[]{:S(2)}) collective-permute-start(bf16[2,544,128]{2,1,0:T(8,128)(2,1)S(1)} %stack_first.1.refs_5_), channel_id=1, source_target_pairs={{0,2},{2,0},{4,6},{6,4},{8,10},{10,8},{12,14},{14,12},{1,3},{3,1},... | collective-permute-start | bytes 835592 | tf_op jit(solution)/shard_map/ppermute | solution.py:499
  32.3 14.6 %collective-permute-start.9 = (bf16[4,256,128]{2,1,0:T(8,128)(2,1)S(1)}, bf16[4,256,128]{2,1,0:T(8,128)(2,1)S(1)}, u32[]{:S(2)}, u32[]{:S(2)}) collective-permute-start(bf16[4,256,128]{2,1,0:T(8,128)(2,1)S(1)} %stack_later.2.refs_9_), channel_id=1, source_target_pairs={{0,8},{2,10},{4,12},{6,14},{8,0},{10,2},{12,4},{14,6},{1,9},{3,11}... | collective-permute-start | bytes 786440 | tf_op jit(solution)/shard_map/ppermute | solution.py:499
  41.7 9.5 %collective-permute-start.6 = (bf16[2,544,128]{2,1,0:T(8,128)(2,1)S(1)}, bf16[2,544,128]{2,1,0:T(8,128)(2,1)S(1)}, u32[]{:S(2)}, u32[]{:S(2)}) collective-permute-start(bf16[2,544,128]{2,1,0:T(8,128)(2,1)S(1)} %get-tuple-element.54), channel_id=1, source_target_pairs={{0,2},{2,0},{4,6},{6,4},{8,10},{10,8},{12,14},{14,12},{1,3},{3,1},... | collective-permute-start | bytes 835592 | tf_op jit(solution)/shard_map/ppermute | solution.py:499
  42.3 21.5 %collective-permute-start.7 = (bf16[2,544,128]{2,1,0:T(8,128)(2,1)S(1)}, bf16[2,544,128]{2,1,0:T(8,128)(2,1)S(1)}, u32[]{:S(2)}, u32[]{:S(2)}) collective-permute-start(bf16[2,544,128]{2,1,0:T(8,128)(2,1)S(1)} %get-tuple-element.55), channel_id=1, source_target_pairs={{0,4},{2,6},{4,0},{6,2},{8,12},{10,14},{12,8},{14,10},{1,5},{3,7},... | collective-permute-start | bytes 835592 | tf_op jit(solution)/shard_map/ppermute | solution.py:499
  42.9 24.5 %collective-permute-start.8 = (bf16[2,544,128]{2,1,0:T(8,128)(2,1)S(1)}, bf16[2,544,128]{2,1,0:T(8,128)(2,1)S(1)}, u32[]{:S(2)}, u32[]{:S(2)}) collective-permute-start(bf16[2,544,128]{2,1,0:T(8,128)(2,1)S(1)} %get-tuple-element.56), channel_id=1, source_target_pairs={{0,6},{2,4},{4,2},{6,0},{8,14},{10,12},{12,10},{14,8},{1,7},{3,5},... | collective-permute-start | bytes 835592 | tf_op jit(solution)/shard_map/ppermute | solution.py:499
  46.9 14.7 %collective-permute-start.10 = (bf16[4,256,128]{2,1,0:T(8,128)(2,1)S(1)}, bf16[4,256,128]{2,1,0:T(8,128)(2,1)S(1)}, u32[]{:S(2)}, u32[]{:S(2)}) collective-permute-start(bf16[4,256,128]{2,1,0:T(8,128)(2,1)S(1)} %stack_later.3.refs_6_), channel_id=1, source_target_pairs={{0,8},{2,10},{4,12},{6,14},{8,0},{10,2},{12,4},{14,6},{1,9},{3,11}... | collective-permute-start | bytes 786440 | tf_op jit(solution)/shard_map/ppermute | solution.py:499
  48.1 19.5 %collective-permute-start.14 = (bf16[2,256,128]{2,1,0:T(8,128)(2,1)S(1)}, bf16[2,256,128]{2,1,0:T(8,128)(2,1)S(1)}, u32[]{:S(2)}, u32[]{:S(2)}) collective-permute-start(bf16[2,256,128]{2,1,0:T(8,128)(2,1)S(1)} %get-tuple-element.72), channel_id=1, source_target_pairs={{0,6},{2,4},{4,2},{6,0},{8,14},{10,12},{12,10},{14,8},{1,7},{3,5},... | collective-permute-start | bytes 393224 | tf_op jit(solution)/shard_map/ppermute | solution.py:499
  51.2 18.9 %collective-permute-start.15 = (bf16[2,256,128]{2,1,0:T(8,128)(2,1)S(1)}, bf16[2,256,128]{2,1,0:T(8,128)(2,1)S(1)}, u32[]{:S(2)}, u32[]{:S(2)}) collective-permute-start(bf16[2,256,128]{2,1,0:T(8,128)(2,1)S(1)} %get-tuple-element.73), channel_id=1, source_target_pairs={{0,4},{2,6},{4,0},{6,2},{8,12},{10,14},{12,8},{14,10},{1,5},{3,7},... | collective-permute-start | bytes 393224 | tf_op jit(solution)/shard_map/ppermute | solution.py:499
  61.6 8.8 %collective-permute-start.16 = (bf16[2,256,128]{2,1,0:T(8,128)(2,1)S(1)}, bf16[2,256,128]{2,1,0:T(8,128)(2,1)S(1)}, u32[]{:S(2)}, u32[]{:S(2)}) collective-permute-start(bf16[2,256,128]{2,1,0:T(8,128)(2,1)S(1)} %get-tuple-element.74), channel_id=1, source_target_pairs={{0,2},{2,0},{4,6},{6,4},{8,10},{10,8},{12,14},{14,12},{1,3},{3,1},... | collective-permute-start | bytes 393224 | tf_op jit(solution)/shard_map/ppermute | solution.py:499
  63.7 12.4 %collective-permute-start.11 = (bf16[2,256,128]{2,1,0:T(8,128)(2,1)S(1)}, bf16[2,256,128]{2,1,0:T(8,128)(2,1)S(1)}, u32[]{:S(2)}, u32[]{:S(2)}) collective-permute-start(bf16[2,256,128]{2,1,0:T(8,128)(2,1)S(1)} %get-tuple-element.59), channel_id=1, source_target_pairs={{0,6},{2,4},{4,2},{6,0},{8,14},{10,12},{12,10},{14,8},{1,7},{3,5},... | collective-permute-start | bytes 393224 | tf_op jit(solution)/shard_map/ppermute | solution.py:499
  67.5 8.7 %collective-permute-start.12 = (bf16[2,256,128]{2,1,0:T(8,128)(2,1)S(1)}, bf16[2,256,128]{2,1,0:T(8,128)(2,1)S(1)}, u32[]{:S(2)}, u32[]{:S(2)}) collective-permute-start(bf16[2,256,128]{2,1,0:T(8,128)(2,1)S(1)} %get-tuple-element.60), channel_id=1, source_target_pairs={{0,4},{2,6},{4,0},{6,2},{8,12},{10,14},{12,8},{14,10},{1,5},{3,7},... | collective-permute-start | bytes 393224 | tf_op jit(solution)/shard_map/ppermute | solution.py:499
  67.6 8.6 %collective-permute-start.13 = (bf16[2,256,128]{2,1,0:T(8,128)(2,1)S(1)}, bf16[2,256,128]{2,1,0:T(8,128)(2,1)S(1)}, u32[]{:S(2)}, u32[]{:S(2)}) collective-permute-start(bf16[2,256,128]{2,1,0:T(8,128)(2,1)S(1)} %get-tuple-element.61), channel_id=1, source_target_pairs={{0,2},{2,0},{4,6},{6,4},{8,10},{10,8},{12,14},{14,12},{1,3},{3,1},... | collective-permute-start | bytes 393224 | tf_op jit(solution)/shard_map/ppermute | solution.py:499

commit v23 on v22

--- a/solution.py
+++ b/solution.py
@@ -8,7 +8,7 @@
 from jax.sharding import PartitionSpec as P
 
 VMEM_LIMIT = 12 * 1024 * 1024
-SPLIT = (8, 4, 4)
+SPLIT = (8, 8)
 FIX = 16
 LOG2_E = 1.4426950408889634
 
@@ -700,11 +700,9 @@
     parts.append(second)
     choices = inside_rows(0) + [(4, 0), (6, 0), (5, 0), (6, 1)]
     states = [pick(rows[0], [*inside, *crossed_a, passed], choices, [second[1]])]
-    sent_c, crossed_c = cross(2, [states[0][0][1], crossed_b])
-    states.append(pick_later(1, crossed_b, [sent_c]))
-    states.append(pick_later(2, crossed_c, [states[1][0][1]]))
-    result = late([0, 1], states, parts, None, [states[2][0][1]])
-    return late([2], states, parts, result, [])
+    states.append(pick_later(1, crossed_b, [states[0][0][1]]))
+    result = late([0], states, parts, None, [states[1][0][1]])
+    return late([1], states, parts, result, [])
 
 
 def solution(mesh):

time: 79.5 us -> 82.3 us (1.035)
  waiting for transfers between devices: 18.8 us -> 28.9 us
  starting transfers between devices: 25 us -> 19.7 us
  Pallas kernels: 34.3 us -> 32.5 us
    ppermute x17 -> x13, waiting for transfers between devices: 18.8 us -> 28.9 us  [swap(): return lax.ppermute(value, 'batch', perm=[(i, i ^ r) for i in range(8)])]
    ppermute x17 -> x13, starting transfers between devices: 25 us -> 19.7 us  [swap(): return lax.ppermute(value, 'batch', perm=[(i, i ^ r) for i in range(8)])]
    pallas_call x7 -> x5, Pallas kernels: 3.45 us -> 2.43 us  [rearrange(): pl.pallas_call(functools.partial(drop_tokens, kernel, 1 + len(sources), l...]
  transfers between devices with their start and end apart: 17 -> 13, of which waited for: 8 -> 8; matrix products, arithmetic and copies ran while one was open for 1% -> 1% of each run, Pallas kernels for 37% -> 33%
where the time goes in v23:
time: 82.3 us; the launch traced here: 82.1 us
  Pallas kernels  32.5 us (39%)
  waiting for transfers between devices  28.9 us (35%)
  starting transfers between devices  19.7 us (24%)
    ppermute x13, waiting for transfers between devices, swap(): return lax.ppermute(value, 'batch', perm=[(i, i ^ r) for i in range(8)])  28.9 us
    pallas_call x3, Pallas kernels, early(): pl.pallas_call(functools.partial(drop_tokens, functools.partial(early_ker...  20.4 us
    ppermute x13, starting transfers between devices, swap(): return lax.ppermute(value, 'batch', perm=[(i, i ^ r) for i in range(8)])  19.7 us
    pallas_call x2, Pallas kernels, late(): pl.pallas_call(functools.partial(drop_tokens, kernel, keep, 1 + len(opera...  7.85 us
    pallas_call x5, Pallas kernels, rearrange(): pl.pallas_call(functools.partial(drop_tokens, kernel, 1 + len(sources), l...  2.43 us
    pallas_call x1, Pallas kernels, cast(): pl.pallas_call(kernel, grid_spec=pltpu.PrefetchScalarGridSpec(num_scalar_...  1.82 us
  transfers between devices with their start and end apart: 13, of which 8 were waited for; matrix products, arithmetic and copies ran while one was open for 1% of the time, Pallas kernels for 33%

profile of v23, /device:TPU:0, one launch (start us, length us, event | category | flops | bytes accessed | tf_op | source)
XLA Modules:
  0.0 82.1 jit_solution(6971989371711093007)
XLA Ops:
  0.0 0.0 copy-start.4
  0.0 0.0 copy-start
  0.0 1.8 %cast_states.1 = (bf16[1056,128]{1,0:T(8,128)(2,1)S(1)}, bf16[1056,128]{1,0:T(8,128)(2,1)S(1)}, bf16[2,1056,128]{2,1,0:T(8,128)(2,1)S(1)}, bf16[2,544,128]{2,1,0:T(8,128)(2,1)S(1)}, bf16[2,544,128]{2,1,0:T(8,128)(2,1)S(1)}) custom-call(s32[1]{0:T(128)} %bitcast.place_ref.refs_0_, f32[4,16,64,128]{3,2,1,0:T(8,128)} %bitcast.5, f32[4,16,64,128]{3,2,1,0:T(8,128)} %bitcast.6, ...), custom_call_target="tpu_custom_call" | custom-call | flops 1 | bytes 1 | tf_op jit(solution)/shard_map/cast_states/pallas_call | solution.py:532
  1.8 3.1 %collective-permute-start.1 = (bf16[1056,128]{1,0:T(8,128)(2,1)S(1)}, bf16[1056,128]{1,0:T(8,128)(2,1)S(1)}, u32[]{:S(2)}, u32[]{:S(2)}) collective-permute-start(bf16[1056,128]{1,0:T(8,128)(2,1)S(1)} %get-tuple-element.38), channel_id=1, source_target_pairs={{0,4},{2,6},{4,0},{6,2},{8,12},{10,14},{12,8},{14,10},{1,5},{3,7},... | collective-permute-start | bytes 811016 | tf_op jit(solution)/shard_map/ppermute | solution.py:499
  4.9 2.6 %collective-permute-start.3 = (bf16[2,544,128]{2,1,0:T(8,128)(2,1)S(1)}, bf16[2,544,128]{2,1,0:T(8,128)(2,1)S(1)}, u32[]{:S(2)}, u32[]{:S(2)}) collective-permute-start(bf16[2,544,128]{2,1,0:T(8,128)(2,1)S(1)} %get-tuple-element.40), channel_id=1, source_target_pairs={{0,8},{2,10},{4,12},{6,14},{8,0},{10,2},{12,4},{14,6},{1,9},{3,11}... | collective-permute-start | bytes 835592 | tf_op jit(solution)/shard_map/ppermute | solution.py:499
  7.5 0.0 collective-permute-start.4
  7.5 1.7 %collective-permute-start = (bf16[2,1056,128]{2,1,0:T(8,128)(2,1)S(1)}, bf16[2,1056,128]{2,1,0:T(8,128)(2,1)S(1)}, u32[]{:S(2)}, u32[]{:S(2)}) collective-permute-start(bf16[2,1056,128]{2,1,0:T(8,128)(2,1)S(1)} %get-tuple-element.37), channel_id=1, source_target_pairs={{0,2},{2,0},{4,6},{6,4},{8,10},{10,8},{12,14},{14,12},{1,3},{3,1},... | collective-permute-start | bytes 1622024 | tf_op jit(solution)/shard_map/ppermute | solution.py:499
  9.3 0.0 copy-done.3
  9.3 0.1 select_reduce_fusion.1
  9.4 0.0 copy-done.4
  9.4 0.1 convert_reduce_fusion
  9.5 0.2 select_reduce_fusion
  9.7 0.0 copy-done
  9.7 0.1 copy.28.refs_4_
  9.8 0.0 copy-done.1
  9.8 0.1 copy.29.refs_5_
  9.9 0.0 copy-done.2
  9.9 0.1 broadcast_in_dim.55
  10.0 0.1 broadcast_in_dim_reshape.3.refs_6_
  10.1 9.6 %early.3 = (f32[4,256,1024]{2,1,0:T(8,128)S(1)}, bf16[4,256,128]{2,1,0:T(8,128)(2,1)S(1)}, f32[4,16,256]{2,1,0:T(8,128)S(1)}, f32[4,256,256]{2,1,0:T(8,128)S(1)}...) custom-call(bf16[2,256,4096]{2,1,0:T(8,128)(2,1)} %refs_0_.5, bf16[2,256,512]{2,1,0:T(8,128)(2,1)} %refs_1_.5, ...), custom_call_target="tpu_custom_call" | custom-call | flops 1 | bytes 1 | tf_op jit(solution)/shard_map/early/pallas_call | solution.py:597
  19.7 1.3 %collective-permute-done.refs_1_.refs_2_ = bf16[2,1056,128]{2,1,0:T(8,128)(2,1)S(1)} collective-permute-done((bf16[2,1056,128]{2,1,0:T(8,128)(2,1)S(1)}, bf16[2,1056,128]{2,1,0:T(8,128)(2,1)S(1)}, u32[]{:S(2)}, u32[]{:S(2)}) %collective-permute-start) | collective-permute-done | bytes 540704 | tf_op jit(solution)/shard_map/ppermute | solution.py:499
  21.0 0.7 collective-permute-start.2
  21.7 5.4 %early.4 = (f32[4,256,1024]{2,1,0:T(8,128)S(1)}, bf16[4,256,128]{2,1,0:T(8,128)(2,1)S(1)}, f32[4,16,256]{2,1,0:T(8,128)S(1)}, f32[4,256,256]{2,1,0:T(8,128)S(1)}...) custom-call(bf16[2,256,4096]{2,1,0:T(8,128)(2,1)} %refs_0_.5, bf16[2,256,512]{2,1,0:T(8,128)(2,1)} %refs_1_.5, ...), custom_call_target="tpu_custom_call" | custom-call | flops 1 | bytes 1 | tf_op jit(solution)/shard_map/early/pallas_call | solution.py:597
  27.1 0.3 collective-permute-done.3.refs_1_.refs_5_
  27.4 0.0 collective-permute-done.4.refs_2_.refs_6_
  27.4 1.6 %collective-permute-start.5 = (bf16[2,544,128]{2,1,0:T(8,128)(2,1)S(1)}, bf16[2,544,128]{2,1,0:T(8,128)(2,1)S(1)}, u32[]{:S(2)}, u32[]{:S(2)}) collective-permute-start(bf16[2,544,128]{2,1,0:T(8,128)(2,1)S(1)} %stack_first.1.refs_5_), channel_id=1, source_target_pairs={{0,2},{2,0},{4,6},{6,4},{8,10},{10,8},{12,14},{14,12},{1,3},{3,1},... | collective-permute-start | bytes 835592 | tf_op jit(solution)/shard_map/ppermute | solution.py:499
  29.0 0.0 collective-permute-done.1.refs_3_
  29.0 3.3 %collective-permute-done.2.refs_4_ = bf16[1056,128]{1,0:T(8,128)(2,1)S(1)} collective-permute-done((bf16[1056,128]{1,0:T(8,128)(2,1)S(1)}, bf16[1056,128]{1,0:T(8,128)(2,1)S(1)}, u32[]{:S(2)}, u32[]{:S(2)}) %collective-permute-start.2) | collective-permute-done | bytes 270368 | tf_op jit(solution)/shard_map/ppermute | solution.py:499
  32.3 2.9 %collective-permute-start.9 = (bf16[4,512,128]{2,1,0:T(8,128)(2,1)S(1)}, bf16[4,512,128]{2,1,0:T(8,128)(2,1)S(1)}, u32[]{:S(2)}, u32[]{:S(2)}) collective-permute-start(bf16[4,512,128]{2,1,0:T(8,128)(2,1)S(1)} %stack_later.1.refs_9_), channel_id=1, source_target_pairs={{0,8},{2,10},{4,12},{6,14},{8,0},{10,2},{12,4},{14,6},{1,9},{3,11}... | collective-permute-start | bytes 1572872 | tf_op jit(solution)/shard_map/ppermute | solution.py:499
  35.2 5.4 %early.5 = (f32[4,256,1024]{2,1,0:T(8,128)S(1)}, bf16[4,256,128]{2,1,0:T(8,128)(2,1)S(1)}, f32[4,16,256]{2,1,0:T(8,128)S(1)}, f32[4,256,256]{2,1,0:T(8,128)S(1)}...) custom-call(bf16[2,256,4096]{2,1,0:T(8,128)(2,1)} %refs_0_.5, ...), custom_call_target="tpu_custom_call", output_to_operand_aliasing={{0}: (10, {}), {1}: (11, {}), {2}: (12, {}), {3}: (13, {}),... | custom-call | flops 1 | bytes 1 | tf_op jit(solution)/shard_map/early/pallas_call | solution.py:597
  40.6 0.0 collective-permute-done.5.refs_7_
  40.6 1.1 %pick_states.2 = (bf16[2,544,128]{2,1,0:T(8,128)(2,1)S(1)}, bf16[2,544,128]{2,1,0:T(8,128)(2,1)S(1)}, bf16[2,544,128]{2,1,0:T(8,128)(2,1)S(1)}, bf16[2,544,128]{2,1,0:T(8,128)(2,1)S(1)}) custom-call(s32[8]{0:T(128)S(1)} %broadcast_xor_fusion.refs_10_.refs_0_, bf16[1056,128]{1,0:T(8,128)(2,1)S(1)} %get-tuple-element.36.refs_9_.refs_1_, ...), custom_call_target="tpu_custom_call" | custom-call | flops 1 | bytes 1 | tf_op jit(solution)/shard_map/pick_states/pallas_call | solution.py:564
  41.7 0.6 collective-permute-start.6
  42.3 0.7 collective-permute-start.7
  43.0 2.3 %collective-permute-start.8 = (bf16[2,544,128]{2,1,0:T(8,128)(2,1)S(1)}, bf16[2,544,128]{2,1,0:T(8,128)(2,1)S(1)}, u32[]{:S(2)}, u32[]{:S(2)}) collective-permute-start(bf16[2,544,128]{2,1,0:T(8,128)(2,1)S(1)} %get-tuple-element.52), channel_id=1, source_target_pairs={{0,6},{2,4},{4,2},{6,0},{8,14},{10,12},{12,10},{14,8},{1,7},{3,5},... | collective-permute-start | bytes 835592 | tf_op jit(solution)/shard_map/ppermute | solution.py:499
  45.3 12.9 %collective-permute-done.9.refs_5_ = bf16[4,512,128]{2,1,0:T(8,128)(2,1)S(1)} collective-permute-done((bf16[4,512,128]{2,1,0:T(8,128)(2,1)S(1)}, bf16[4,512,128]{2,1,0:T(8,128)(2,1)S(1)}, u32[]{:S(2)}, u32[]{:S(2)}) %collective-permute-start.9) | collective-permute-done | bytes 524320 | tf_op jit(solution)/shard_map/ppermute | solution.py:499
  58.1 1.3 %pick_states.3 = (bf16[2,512,128]{2,1,0:T(8,128)(2,1)S(1)}, bf16[2,512,128]{2,1,0:T(8,128)(2,1)S(1)}, bf16[2,512,128]{2,1,0:T(8,128)(2,1)S(1)}, bf16[2,512,128]{2,1,0:T(8,128)(2,1)S(1)}) custom-call(s32[8]{0:T(128)S(1)} %broadcast_xor_fusion.refs_10_.refs_0_, bf16[1056,128]{1,0:T(8,128)(2,1)S(1)} %get-tuple-element.36.refs_9_.refs_1_, ...), custom_call_target="tpu_custom_call" | custom-call | flops 1 | bytes 1 | tf_op jit(solution)/shard_map/pick_states/pallas_call | solution.py:564
  59.4 0.1 collective-permute-start.10
  59.5 2.3 %collective-permute-start.11 = (bf16[2,512,128]{2,1,0:T(8,128)(2,1)S(1)}, bf16[2,512,128]{2,1,0:T(8,128)(2,1)S(1)}, u32[]{:S(2)}, u32[]{:S(2)}) collective-permute-start(bf16[2,512,128]{2,1,0:T(8,128)(2,1)S(1)} %get-tuple-element.55), channel_id=1, source_target_pairs={{0,4},{2,6},{4,0},{6,2},{8,12},{10,14},{12,8},{14,10},{1,5},{3,7},... | collective-permute-start | bytes 786440 | tf_op jit(solution)/shard_map/ppermute | solution.py:499
  61.8 0.0 collective-permute-done.6.refs_2_.refs_6_
  61.8 1.2 %collective-permute-start.12 = (bf16[2,512,128]{2,1,0:T(8,128)(2,1)S(1)}, bf16[2,512,128]{2,1,0:T(8,128)(2,1)S(1)}, u32[]{:S(2)}, u32[]{:S(2)}) collective-permute-start(bf16[2,512,128]{2,1,0:T(8,128)(2,1)S(1)} %get-tuple-element.56), channel_id=1, source_target_pairs={{0,2},{2,0},{4,6},{6,4},{8,10},{10,8},{12,14},{14,12},{1,3},{3,1},... | collective-permute-start | bytes 786440 | tf_op jit(solution)/shard_map/ppermute | solution.py:499
  63.0 0.0 collective-permute-done.7.refs_3_.refs_7_
  63.0 6.1 %collective-permute-done.8.refs_4_.refs_8_ = bf16[2,544,128]{2,1,0:T(8,128)(2,1)S(1)} collective-permute-done((bf16[2,544,128]{2,1,0:T(8,128)(2,1)S(1)}, bf16[2,544,128]{2,1,0:T(8,128)(2,1)S(1)}, u32[]{:S(2)}, u32[]{:S(2)}) %collective-permute-start.8) | collective-permute-done | bytes 278560 | tf_op jit(solution)/shard_map/ppermute | solution.py:499
  69.1 3.9 %late.2.refs_21_ = bf16[2,256,4096]{2,1,0:T(8,128)(2,1)} custom-call(s32[1]{0:T(128)} %bitcast.place_ref.refs_0_, bf16[2,544,128]{2,1,0:T(8,128)(2,1)S(1)} %get-tuple-element.49.refs_6_.refs_1_.refs_5_, bf16[2,544,128]{2,1,0:T(8,128)(2,1)S(1)} %collective-permute-done.6.refs_2_.refs_6_, bf16[2,544,128]{2,1,0:T(8,128)(2,1)S(1)} %collective-permute-done.7.refs_3_.refs_7_, ...), custom_call_target="tpu_custom_call" | custom-call | flops 1 | bytes 1 | tf_op jit(solution)/shard_map/late/pallas_call | solution.py:648
  73.1 1.6 %collective-permute-done.10.refs_6_ = bf16[2,512,128]{2,1,0:T(8,128)(2,1)S(1)} collective-permute-done((bf16[2,512,128]{2,1,0:T(8,128)(2,1)S(1)}, bf16[2,512,128]{2,1,0:T(8,128)(2,1)S(1)}, u32[]{:S(2)}, u32[]{:S(2)}) %collective-permute-start.10) | collective-permute-done | bytes 262176 | tf_op jit(solution)/shard_map/ppermute | solution.py:499
  74.7 2.5 %collective-permute-done.11.refs_7_ = bf16[2,512,128]{2,1,0:T(8,128)(2,1)S(1)} collective-permute-done((bf16[2,512,128]{2,1,0:T(8,128)(2,1)S(1)}, bf16[2,512,128]{2,1,0:T(8,128)(2,1)S(1)}, u32[]{:S(2)}, u32[]{:S(2)}) %collective-permute-start.11) | collective-permute-done | bytes 262176 | tf_op jit(solution)/shard_map/ppermute | solution.py:499
  77.2 0.8 collective-permute-done.12.refs_8_
  78.0 3.9 %late.3 = bf16[2,256,4096]{2,1,0:T(8,128)(2,1)} custom-call(s32[1]{0:T(128)} %bitcast.place_ref.refs_0_, bf16[2,544,128]{2,1,0:T(8,128)(2,1)S(1)} %get-tuple-element.49.refs_6_.refs_1_.refs_5_, bf16[2,544,128]{2,1,0:T(8,128)(2,1)S(1)} %collective-permute-done.6.refs_2_.refs_6_, ...), custom_call_target="tpu_custom_call", output_to_operand_aliasing={{}: (21, {})} | custom-call | flops 1 | bytes 1 | tf_op jit(solution)/shard_map/late/pallas_call | solution.py:648
  (8 shorter events, 0.1 us)
Async XLA Ops:
  0.0 9.3 %copy-start.3 = (s32[8]{0:T(128)S(1)}, s32[8]{0:T(128)}, u32[]{:S(2)}) copy-start(s32[8]{0:T(128)} %param.26) | copy-start | bytes 100
  0.0 9.4 %copy-start.4 = (s32[16]{0:T(128)S(1)}, s32[16]{0:T(128)}, u32[]{:S(2)}) copy-start(s32[16]{0:T(128)} %param.27) | copy-start | bytes 196
  0.0 9.7 %copy-start = (f32[64]{0:T(128)S(1)}, f32[64]{0:T(128)}, u32[]{:S(2)}) copy-start(f32[64]{0:T(128)} %param.18) | copy-start | bytes 772
  0.0 9.8 %copy-start.1 = (f32[64]{0:T(128)S(1)}, f32[64]{0:T(128)}, u32[]{:S(2)}) copy-start(f32[64]{0:T(128)} %param.19) | copy-start | bytes 772
  0.0 9.9 %copy-start.2 = (f32[64]{0:T(128)S(1)}, f32[64]{0:T(128)}, u32[]{:S(2)}) copy-start(f32[64]{0:T(128)} %param.20) | copy-start | bytes 772
  1.8 27.2 %collective-permute-start.1 = (bf16[1056,128]{1,0:T(8,128)(2,1)S(1)}, bf16[1056,128]{1,0:T(8,128)(2,1)S(1)}, u32[]{:S(2)}, u32[]{:S(2)}) collective-permute-start(bf16[1056,128]{1,0:T(8,128)(2,1)S(1)} %get-tuple-element.38), channel_id=1, source_target_pairs={{0,4},{2,6},{4,0},{6,2},{8,12},{10,14},{12,8},{14,10},{1,5},{3,7},... | collective-permute-start | bytes 811016 | tf_op jit(solution)/shard_map/ppermute | solution.py:499
  4.9 22.5 %collective-permute-start.3 = (bf16[2,544,128]{2,1,0:T(8,128)(2,1)S(1)}, bf16[2,544,128]{2,1,0:T(8,128)(2,1)S(1)}, u32[]{:S(2)}, u32[]{:S(2)}) collective-permute-start(bf16[2,544,128]{2,1,0:T(8,128)(2,1)S(1)} %get-tuple-element.40), channel_id=1, source_target_pairs={{0,8},{2,10},{4,12},{6,14},{8,0},{10,2},{12,4},{14,6},{1,9},{3,11}... | collective-permute-start | bytes 835592 | tf_op jit(solution)/shard_map/ppermute | solution.py:499
  7.5 19.9 %collective-permute-start.4 = (bf16[2,544,128]{2,1,0:T(8,128)(2,1)S(1)}, bf16[2,544,128]{2,1,0:T(8,128)(2,1)S(1)}, u32[]{:S(2)}, u32[]{:S(2)}) collective-permute-start(bf16[2,544,128]{2,1,0:T(8,128)(2,1)S(1)} %get-tuple-element.41), channel_id=1, source_target_pairs={{0,12},{2,14},{4,8},{6,10},{8,4},{10,6},{12,0},{14,2},{1,13},{3,15... | collective-permute-start | bytes 835592 | tf_op jit(solution)/shard_map/ppermute | solution.py:499
  7.5 13.5 %collective-permute-start = (bf16[2,1056,128]{2,1,0:T(8,128)(2,1)S(1)}, bf16[2,1056,128]{2,1,0:T(8,128)(2,1)S(1)}, u32[]{:S(2)}, u32[]{:S(2)}) collective-permute-start(bf16[2,1056,128]{2,1,0:T(8,128)(2,1)S(1)} %get-tuple-element.37), channel_id=1, source_target_pairs={{0,2},{2,0},{4,6},{6,4},{8,10},{10,8},{12,14},{14,12},{1,3},{3,1},... | collective-permute-start | bytes 1622024 | tf_op jit(solution)/shard_map/ppermute | solution.py:499
  21.0 11.3 %collective-permute-start.2 = (bf16[1056,128]{1,0:T(8,128)(2,1)S(1)}, bf16[1056,128]{1,0:T(8,128)(2,1)S(1)}, u32[]{:S(2)}, u32[]{:S(2)}) collective-permute-start(bf16[1056,128]{1,0:T(8,128)(2,1)S(1)} %stack_turn.1.refs_9_), channel_id=1, source_target_pairs={{0,4},{2,6},{4,0},{6,2},{8,12},{10,14},{12,8},{14,10},{1,5},{3,7},... | collective-permute-start | bytes 811016 | tf_op jit(solution)/shard_map/ppermute | solution.py:499
  27.4 13.2 %collective-permute-start.5 = (bf16[2,544,128]{2,1,0:T(8,128)(2,1)S(1)}, bf16[2,544,128]{2,1,0:T(8,128)(2,1)S(1)}, u32[]{:S(2)}, u32[]{:S(2)}) collective-permute-start(bf16[2,544,128]{2,1,0:T(8,128)(2,1)S(1)} %stack_first.1.refs_5_), channel_id=1, source_target_pairs={{0,2},{2,0},{4,6},{6,4},{8,10},{10,8},{12,14},{14,12},{1,3},{3,1},... | collective-permute-start | bytes 835592 | tf_op jit(solution)/shard_map/ppermute | solution.py:499
  32.3 25.8 %collective-permute-start.9 = (bf16[4,512,128]{2,1,0:T(8,128)(2,1)S(1)}, bf16[4,512,128]{2,1,0:T(8,128)(2,1)S(1)}, u32[]{:S(2)}, u32[]{:S(2)}) collective-permute-start(bf16[4,512,128]{2,1,0:T(8,128)(2,1)S(1)} %stack_later.1.refs_9_), channel_id=1, source_target_pairs={{0,8},{2,10},{4,12},{6,14},{8,0},{10,2},{12,4},{14,6},{1,9},{3,11}... | collective-permute-start | bytes 1572872 | tf_op jit(solution)/shard_map/ppermute | solution.py:499
  41.7 20.1 %collective-permute-start.6 = (bf16[2,544,128]{2,1,0:T(8,128)(2,1)S(1)}, bf16[2,544,128]{2,1,0:T(8,128)(2,1)S(1)}, u32[]{:S(2)}, u32[]{:S(2)}) collective-permute-start(bf16[2,544,128]{2,1,0:T(8,128)(2,1)S(1)} %get-tuple-element.50), channel_id=1, source_target_pairs={{0,2},{2,0},{4,6},{6,4},{8,10},{10,8},{12,14},{14,12},{1,3},{3,1},... | collective-permute-start | bytes 835592 | tf_op jit(solution)/shard_map/ppermute | solution.py:499
  42.3 20.7 %collective-permute-start.7 = (bf16[2,544,128]{2,1,0:T(8,128)(2,1)S(1)}, bf16[2,544,128]{2,1,0:T(8,128)(2,1)S(1)}, u32[]{:S(2)}, u32[]{:S(2)}) collective-permute-start(bf16[2,544,128]{2,1,0:T(8,128)(2,1)S(1)} %get-tuple-element.51), channel_id=1, source_target_pairs={{0,4},{2,6},{4,0},{6,2},{8,12},{10,14},{12,8},{14,10},{1,5},{3,7},... | collective-permute-start | bytes 835592 | tf_op jit(solution)/shard_map/ppermute | solution.py:499
  43.0 26.1 %collective-permute-start.8 = (bf16[2,544,128]{2,1,0:T(8,128)(2,1)S(1)}, bf16[2,544,128]{2,1,0:T(8,128)(2,1)S(1)}, u32[]{:S(2)}, u32[]{:S(2)}) collective-permute-start(bf16[2,544,128]{2,1,0:T(8,128)(2,1)S(1)} %get-tuple-element.52), channel_id=1, source_target_pairs={{0,6},{2,4},{4,2},{6,0},{8,14},{10,12},{12,10},{14,8},{1,7},{3,5},... | collective-permute-start | bytes 835592 | tf_op jit(solution)/shard_map/ppermute | solution.py:499
  59.4 15.3 %collective-permute-start.10 = (bf16[2,512,128]{2,1,0:T(8,128)(2,1)S(1)}, bf16[2,512,128]{2,1,0:T(8,128)(2,1)S(1)}, u32[]{:S(2)}, u32[]{:S(2)}) collective-permute-start(bf16[2,512,128]{2,1,0:T(8,128)(2,1)S(1)} %get-tuple-element.54), channel_id=1, source_target_pairs={{0,6},{2,4},{4,2},{6,0},{8,14},{10,12},{12,10},{14,8},{1,7},{3,5},... | collective-permute-start | bytes 786440 | tf_op jit(solution)/shard_map/ppermute | solution.py:499
  59.5 17.7 %collective-permute-start.11 = (bf16[2,512,128]{2,1,0:T(8,128)(2,1)S(1)}, bf16[2,512,128]{2,1,0:T(8,128)(2,1)S(1)}, u32[]{:S(2)}, u32[]{:S(2)}) collective-permute-start(bf16[2,512,128]{2,1,0:T(8,128)(2,1)S(1)} %get-tuple-element.55), channel_id=1, source_target_pairs={{0,4},{2,6},{4,0},{6,2},{8,12},{10,14},{12,8},{14,10},{1,5},{3,7},... | collective-permute-start | bytes 786440 | tf_op jit(solution)/shard_map/ppermute | solution.py:499
  61.8 16.2 %collective-permute-start.12 = (bf16[2,512,128]{2,1,0:T(8,128)(2,1)S(1)}, bf16[2,512,128]{2,1,0:T(8,128)(2,1)S(1)}, u32[]{:S(2)}, u32[]{:S(2)}) collective-permute-start(bf16[2,512,128]{2,1,0:T(8,128)(2,1)S(1)} %get-tuple-element.56), channel_id=1, source_target_pairs={{0,2},{2,0},{4,6},{6,4},{8,10},{10,8},{12,14},{14,12},{1,3},{3,1},... | collective-permute-start | bytes 786440 | tf_op jit(solution)/shard_map/ppermute | solution.py:499

commit v24 on v23

--- a/solution.py
+++ b/solution.py
@@ -8,7 +8,7 @@
 from jax.sharding import PartitionSpec as P
 
 VMEM_LIMIT = 12 * 1024 * 1024
-SPLIT = (8, 8)
+SPLIT = (10, 6)
 FIX = 16
 LOG2_E = 1.4426950408889634
 
@@ -501,7 +501,7 @@
     def cast():
         rows = per_group * width + tail_lines
         rows_a = SPLIT[0] * width + tail_lines
-        blocks = [(0, SPLIT[0])] + [(at, 4) for at in range(SPLIT[0], per_group, 4)]
+        blocks = [(0, SPLIT[0])] + [(at, 2) for at in range(SPLIT[0], per_group, 2)]
         count = len(blocks) + 2
 
         def kernel(place_ref, *refs):

time: 82.3 us -> 97.5 us (1.18)
  waiting for transfers between devices: 28.9 us -> 36.6 us
  starting transfers between devices: 19.7 us -> 26.7 us
    ppermute x13, waiting for transfers between devices: 28.9 us -> 36.6 us  [swap(): return lax.ppermute(value, 'batch', perm=[(i, i ^ r) for i in range(8)])]
    ppermute x13, starting transfers between devices: 19.7 us -> 26.7 us  [swap(): return lax.ppermute(value, 'batch', perm=[(i, i ^ r) for i in range(8)])]
  transfers between devices with their start and end apart: 13 -> 13, of which waited for: 8 -> 8; matrix products, arithmetic and copies ran while one was open for 1% -> 1% of each run, Pallas kernels for 33% -> 28%
where the time goes in v24:
time: 97.5 us; the launch traced here: 97.3 us
  waiting for transfers between devices  36.6 us (38%)
  Pallas kernels  33 us (34%)
  starting transfers between devices  26.7 us (27%)
    ppermute x13, waiting for transfers between devices, swap(): return lax.ppermute(value, 'batch', perm=[(i, i ^ r) for i in range(8)])  36.6 us
    ppermute x13, starting transfers between devices, swap(): return lax.ppermute(value, 'batch', perm=[(i, i ^ r) for i in range(8)])  26.7 us
    pallas_call x3, Pallas kernels, early(): pl.pallas_call(functools.partial(drop_tokens, functools.partial(early_ker...  20.4 us
    pallas_call x2, Pallas kernels, late(): pl.pallas_call(functools.partial(drop_tokens, kernel, keep, 1 + len(opera...  8.24 us
    pallas_call x5, Pallas kernels, rearrange(): pl.pallas_call(functools.partial(drop_tokens, kernel, 1 + len(sources), l...  2.42 us
  transfers between devices with their start and end apart: 13, of which 8 were waited for; matrix products, arithmetic and copies ran while one was open for 1% of the time, Pallas kernels for 28%

profile of v24, /device:TPU:0, one launch (start us, length us, event | category | flops | bytes accessed | tf_op | source)
XLA Modules:
  0.0 97.3 jit_solution(10130339054921675623)
XLA Ops:
  0.0 0.0 copy-start.3
  0.0 0.0 copy-start.4
  0.0 1.9 %cast_states.1 = (bf16[1056,128]{1,0:T(8,128)(2,1)S(1)}, bf16[1056,128]{1,0:T(8,128)(2,1)S(1)}, bf16[2,1056,128]{2,1,0:T(8,128)(2,1)S(1)}, bf16[2,672,128]{2,1,0:T(8,128)(2,1)S(1)}, bf16[2,672,128]{2,1,0:T(8,128)(2,1)S(1)}) custom-call(s32[1]{0:T(128)} %bitcast.place_ref.refs_0_, f32[4,16,64,128]{3,2,1,0:T(8,128)} %bitcast.5, f32[4,16,64,128]{3,2,1,0:T(8,128)} %bitcast.6, ...), custom_call_target="tpu_custom_call" | custom-call | flops 1 | bytes 1 | tf_op jit(solution)/shard_map/cast_states/pallas_call | solution.py:532
  1.9 4.1 %collective-permute-start.3 = (bf16[2,672,128]{2,1,0:T(8,128)(2,1)S(1)}, bf16[2,672,128]{2,1,0:T(8,128)(2,1)S(1)}, u32[]{:S(2)}, u32[]{:S(2)}) collective-permute-start(bf16[2,672,128]{2,1,0:T(8,128)(2,1)S(1)} %get-tuple-element.40), channel_id=1, source_target_pairs={{0,8},{2,10},{4,12},{6,14},{8,0},{10,2},{12,4},{14,6},{1,9},{3,11}... | collective-permute-start | bytes 1032200 | tf_op jit(solution)/shard_map/ppermute | solution.py:499
  6.0 1.3 %collective-permute-start.4 = (bf16[2,672,128]{2,1,0:T(8,128)(2,1)S(1)}, bf16[2,672,128]{2,1,0:T(8,128)(2,1)S(1)}, u32[]{:S(2)}, u32[]{:S(2)}) collective-permute-start(bf16[2,672,128]{2,1,0:T(8,128)(2,1)S(1)} %get-tuple-element.41), channel_id=1, source_target_pairs={{0,12},{2,14},{4,8},{6,10},{8,4},{10,6},{12,0},{14,2},{1,13},{3,15... | collective-permute-start | bytes 1032200 | tf_op jit(solution)/shard_map/ppermute | solution.py:499
  7.4 1.5 %collective-permute-start = (bf16[2,1056,128]{2,1,0:T(8,128)(2,1)S(1)}, bf16[2,1056,128]{2,1,0:T(8,128)(2,1)S(1)}, u32[]{:S(2)}, u32[]{:S(2)}) collective-permute-start(bf16[2,1056,128]{2,1,0:T(8,128)(2,1)S(1)} %get-tuple-element.37), channel_id=1, source_target_pairs={{0,2},{2,0},{4,6},{6,4},{8,10},{10,8},{12,14},{14,12},{1,3},{3,1},... | collective-permute-start | bytes 1622024 | tf_op jit(solution)/shard_map/ppermute | solution.py:499
  8.9 0.0 copy-done.3
  8.9 0.1 select_reduce_fusion.1
  9.0 0.0 copy-done.4
  9.0 0.1 convert_reduce_fusion
  9.1 0.0 copy-done
  9.1 0.1 copy.28.refs_4_
  9.2 0.0 copy-done.1
  9.2 0.1 copy.29.refs_5_
  9.3 0.0 copy-done.2
  9.3 0.1 broadcast_in_dim.55
  9.4 0.1 broadcast_in_dim_reshape.3.refs_6_
  9.5 0.2 select_reduce_fusion
  9.7 9.7 %early.3 = (f32[4,256,1024]{2,1,0:T(8,128)S(1)}, bf16[4,256,128]{2,1,0:T(8,128)(2,1)S(1)}, f32[4,16,256]{2,1,0:T(8,128)S(1)}, f32[4,256,256]{2,1,0:T(8,128)S(1)}...) custom-call(bf16[2,256,4096]{2,1,0:T(8,128)(2,1)} %refs_0_.5, bf16[2,256,512]{2,1,0:T(8,128)(2,1)} %refs_1_.5, ...), custom_call_target="tpu_custom_call" | custom-call | flops 1 | bytes 1 | tf_op jit(solution)/shard_map/early/pallas_call | solution.py:597
  19.3 1.5 %collective-permute-done.refs_1_.refs_2_ = bf16[2,1056,128]{2,1,0:T(8,128)(2,1)S(1)} collective-permute-done((bf16[2,1056,128]{2,1,0:T(8,128)(2,1)S(1)}, bf16[2,1056,128]{2,1,0:T(8,128)(2,1)S(1)}, u32[]{:S(2)}, u32[]{:S(2)}) %collective-permute-start) | collective-permute-done | bytes 540704 | tf_op jit(solution)/shard_map/ppermute | solution.py:499
  20.9 5.4 %early.4 = (f32[4,256,1024]{2,1,0:T(8,128)S(1)}, bf16[4,256,128]{2,1,0:T(8,128)(2,1)S(1)}, f32[4,16,256]{2,1,0:T(8,128)S(1)}, f32[4,256,256]{2,1,0:T(8,128)S(1)}...) custom-call(bf16[2,256,4096]{2,1,0:T(8,128)(2,1)} %refs_0_.5, bf16[2,256,512]{2,1,0:T(8,128)(2,1)} %refs_1_.5, ...), custom_call_target="tpu_custom_call" | custom-call | flops 1 | bytes 1 | tf_op jit(solution)/shard_map/early/pallas_call | solution.py:597
  26.3 3.4 %collective-permute-done.3.refs_1_.refs_5_ = bf16[2,672,128]{2,1,0:T(8,128)(2,1)S(1)} collective-permute-done((bf16[2,672,128]{2,1,0:T(8,128)(2,1)S(1)}, bf16[2,672,128]{2,1,0:T(8,128)(2,1)S(1)}, u32[]{:S(2)}, u32[]{:S(2)}) %collective-permute-start.3) | collective-permute-done | bytes 344096 | tf_op jit(solution)/shard_map/ppermute | solution.py:499
  29.6 0.0 collective-permute-done.4.refs_2_.refs_6_
  29.7 1.9 %collective-permute-start.5 = (bf16[2,672,128]{2,1,0:T(8,128)(2,1)S(1)}, bf16[2,672,128]{2,1,0:T(8,128)(2,1)S(1)}, u32[]{:S(2)}, u32[]{:S(2)}) collective-permute-start(bf16[2,672,128]{2,1,0:T(8,128)(2,1)S(1)} %stack_first.1.refs_5_), channel_id=1, source_target_pairs={{0,2},{2,0},{4,6},{6,4},{8,10},{10,8},{12,14},{14,12},{1,3},{3,1},... | collective-permute-start | bytes 1032200 | tf_op jit(solution)/shard_map/ppermute | solution.py:499
  31.6 6.9 %collective-permute-start.1 = (bf16[1056,128]{1,0:T(8,128)(2,1)S(1)}, bf16[1056,128]{1,0:T(8,128)(2,1)S(1)}, u32[]{:S(2)}, u32[]{:S(2)}) collective-permute-start(bf16[1056,128]{1,0:T(8,128)(2,1)S(1)} %get-tuple-element.38), channel_id=1, source_target_pairs={{0,4},{2,6},{4,0},{6,2},{8,12},{10,14},{12,8},{14,10},{1,5},{3,7},... | collective-permute-start | bytes 811016 | tf_op jit(solution)/shard_map/ppermute | solution.py:499
  38.5 0.0 collective-permute-start.2
  38.6 7.3 %collective-permute-done.1.refs_3_ = bf16[1056,128]{1,0:T(8,128)(2,1)S(1)} collective-permute-done((bf16[1056,128]{1,0:T(8,128)(2,1)S(1)}, bf16[1056,128]{1,0:T(8,128)(2,1)S(1)}, u32[]{:S(2)}, u32[]{:S(2)}) %collective-permute-start.1) | collective-permute-done | bytes 270368 | tf_op jit(solution)/shard_map/ppermute | solution.py:499
  45.8 4.9 %collective-permute-done.2.refs_4_ = bf16[1056,128]{1,0:T(8,128)(2,1)S(1)} collective-permute-done((bf16[1056,128]{1,0:T(8,128)(2,1)S(1)}, bf16[1056,128]{1,0:T(8,128)(2,1)S(1)}, u32[]{:S(2)}, u32[]{:S(2)}) %collective-permute-start.2) | collective-permute-done | bytes 270368 | tf_op jit(solution)/shard_map/ppermute | solution.py:499
  50.7 3.7 %collective-permute-start.9 = (bf16[4,384,128]{2,1,0:T(8,128)(2,1)S(1)}, bf16[4,384,128]{2,1,0:T(8,128)(2,1)S(1)}, u32[]{:S(2)}, u32[]{:S(2)}) collective-permute-start(bf16[4,384,128]{2,1,0:T(8,128)(2,1)S(1)} %stack_later.1.refs_9_), channel_id=1, source_target_pairs={{0,8},{2,10},{4,12},{6,14},{8,0},{10,2},{12,4},{14,6},{1,9},{3,11}... | collective-permute-start | bytes 1179656 | tf_op jit(solution)/shard_map/ppermute | solution.py:499
  54.5 5.4 %early.5 = (f32[4,256,1024]{2,1,0:T(8,128)S(1)}, bf16[4,256,128]{2,1,0:T(8,128)(2,1)S(1)}, f32[4,16,256]{2,1,0:T(8,128)S(1)}, f32[4,256,256]{2,1,0:T(8,128)S(1)}...) custom-call(bf16[2,256,4096]{2,1,0:T(8,128)(2,1)} %refs_0_.5, ...), custom_call_target="tpu_custom_call", output_to_operand_aliasing={{0}: (10, {}), {1}: (11, {}), {2}: (12, {}), {3}: (13, {}),... | custom-call | flops 1 | bytes 1 | tf_op jit(solution)/shard_map/early/pallas_call | solution.py:597
  59.8 0.0 collective-permute-done.5.refs_7_
  59.8 1.1 %pick_states.2 = (bf16[2,672,128]{2,1,0:T(8,128)(2,1)S(1)}, bf16[2,672,128]{2,1,0:T(8,128)(2,1)S(1)}, bf16[2,672,128]{2,1,0:T(8,128)(2,1)S(1)}, bf16[2,672,128]{2,1,0:T(8,128)(2,1)S(1)}) custom-call(s32[8]{0:T(128)S(1)} %broadcast_xor_fusion.refs_10_.refs_0_, bf16[1056,128]{1,0:T(8,128)(2,1)S(1)} %get-tuple-element.36.refs_9_.refs_1_, ...), custom_call_target="tpu_custom_call" | custom-call | flops 1 | bytes 1 | tf_op jit(solution)/shard_map/pick_states/pallas_call | solution.py:564
  61.0 0.6 collective-permute-start.6
  61.5 0.3 collective-permute-start.7
  61.8 2.7 %collective-permute-start.8 = (bf16[2,672,128]{2,1,0:T(8,128)(2,1)S(1)}, bf16[2,672,128]{2,1,0:T(8,128)(2,1)S(1)}, u32[]{:S(2)}, u32[]{:S(2)}) collective-permute-start(bf16[2,672,128]{2,1,0:T(8,128)(2,1)S(1)} %get-tuple-element.52), channel_id=1, source_target_pairs={{0,6},{2,4},{4,2},{6,0},{8,14},{10,12},{12,10},{14,8},{1,7},{3,5},... | collective-permute-start | bytes 1032200 | tf_op jit(solution)/shard_map/ppermute | solution.py:499
  64.5 6.6 %collective-permute-done.9.refs_5_ = bf16[4,384,128]{2,1,0:T(8,128)(2,1)S(1)} collective-permute-done((bf16[4,384,128]{2,1,0:T(8,128)(2,1)S(1)}, bf16[4,384,128]{2,1,0:T(8,128)(2,1)S(1)}, u32[]{:S(2)}, u32[]{:S(2)}) %collective-permute-start.9) | collective-permute-done | bytes 393248 | tf_op jit(solution)/shard_map/ppermute | solution.py:499
  71.1 1.2 %pick_states.3 = (bf16[2,384,128]{2,1,0:T(8,128)(2,1)S(1)}, bf16[2,384,128]{2,1,0:T(8,128)(2,1)S(1)}, bf16[2,384,128]{2,1,0:T(8,128)(2,1)S(1)}, bf16[2,384,128]{2,1,0:T(8,128)(2,1)S(1)}) custom-call(s32[8]{0:T(128)S(1)} %broadcast_xor_fusion.refs_10_.refs_0_, bf16[1056,128]{1,0:T(8,128)(2,1)S(1)} %get-tuple-element.36.refs_9_.refs_1_, ...), custom_call_target="tpu_custom_call" | custom-call | flops 1 | bytes 1 | tf_op jit(solution)/shard_map/pick_states/pallas_call | solution.py:564
  72.4 0.1 collective-permute-start.10
  72.4 2.0 %collective-permute-start.11 = (bf16[2,384,128]{2,1,0:T(8,128)(2,1)S(1)}, bf16[2,384,128]{2,1,0:T(8,128)(2,1)S(1)}, u32[]{:S(2)}, u32[]{:S(2)}) collective-permute-start(bf16[2,384,128]{2,1,0:T(8,128)(2,1)S(1)} %get-tuple-element.55), channel_id=1, source_target_pairs={{0,4},{2,6},{4,0},{6,2},{8,12},{10,14},{12,8},{14,10},{1,5},{3,7},... | collective-permute-start | bytes 589832 | tf_op jit(solution)/shard_map/ppermute | solution.py:499
  74.4 0.0 collective-permute-done.6.refs_2_.refs_6_
  74.4 1.5 %collective-permute-start.12 = (bf16[2,384,128]{2,1,0:T(8,128)(2,1)S(1)}, bf16[2,384,128]{2,1,0:T(8,128)(2,1)S(1)}, u32[]{:S(2)}, u32[]{:S(2)}) collective-permute-start(bf16[2,384,128]{2,1,0:T(8,128)(2,1)S(1)} %get-tuple-element.56), channel_id=1, source_target_pairs={{0,2},{2,0},{4,6},{6,4},{8,10},{10,8},{12,14},{14,12},{1,3},{3,1},... | collective-permute-start | bytes 589832 | tf_op jit(solution)/shard_map/ppermute | solution.py:499
  75.9 2.6 %collective-permute-done.7.refs_3_.refs_7_ = bf16[2,672,128]{2,1,0:T(8,128)(2,1)S(1)} collective-permute-done((bf16[2,672,128]{2,1,0:T(8,128)(2,1)S(1)}, bf16[2,672,128]{2,1,0:T(8,128)(2,1)S(1)}, u32[]{:S(2)}, u32[]{:S(2)}) %collective-permute-start.7) | collective-permute-done | bytes 344096 | tf_op jit(solution)/shard_map/ppermute | solution.py:499
  78.5 7.3 %collective-permute-done.8.refs_4_.refs_8_ = bf16[2,672,128]{2,1,0:T(8,128)(2,1)S(1)} collective-permute-done((bf16[2,672,128]{2,1,0:T(8,128)(2,1)S(1)}, bf16[2,672,128]{2,1,0:T(8,128)(2,1)S(1)}, u32[]{:S(2)}, u32[]{:S(2)}) %collective-permute-start.8) | collective-permute-done | bytes 344096 | tf_op jit(solution)/shard_map/ppermute | solution.py:499
  85.9 4.9 %late.2.refs_21_ = bf16[2,256,4096]{2,1,0:T(8,128)(2,1)} custom-call(s32[1]{0:T(128)} %bitcast.place_ref.refs_0_, bf16[2,672,128]{2,1,0:T(8,128)(2,1)S(1)} %get-tuple-element.49.refs_6_.refs_1_.refs_5_, bf16[2,672,128]{2,1,0:T(8,128)(2,1)S(1)} %collective-permute-done.6.refs_2_.refs_6_, bf16[2,672,128]{2,1,0:T(8,128)(2,1)S(1)} %collective-permute-done.7.refs_3_.refs_7_, ...), custom_call_target="tpu_custom_call" | custom-call | flops 1 | bytes 1 | tf_op jit(solution)/shard_map/late/pallas_call | solution.py:648
  90.8 0.0 collective-permute-done.10.refs_6_
  90.8 3.0 %collective-permute-done.11.refs_7_ = bf16[2,384,128]{2,1,0:T(8,128)(2,1)S(1)} collective-permute-done((bf16[2,384,128]{2,1,0:T(8,128)(2,1)S(1)}, bf16[2,384,128]{2,1,0:T(8,128)(2,1)S(1)}, u32[]{:S(2)}, u32[]{:S(2)}) %collective-permute-start.11) | collective-permute-done | bytes 196640 | tf_op jit(solution)/shard_map/ppermute | solution.py:499
  93.8 0.0 collective-permute-done.12.refs_8_
  93.8 3.3 %late.3 = bf16[2,256,4096]{2,1,0:T(8,128)(2,1)} custom-call(s32[1]{0:T(128)} %bitcast.place_ref.refs_0_, bf16[2,672,128]{2,1,0:T(8,128)(2,1)S(1)} %get-tuple-element.49.refs_6_.refs_1_.refs_5_, bf16[2,672,128]{2,1,0:T(8,128)(2,1)S(1)} %collective-permute-done.6.refs_2_.refs_6_, ...), custom_call_target="tpu_custom_call", output_to_operand_aliasing={{}: (21, {})} | custom-call | flops 1 | bytes 1 | tf_op jit(solution)/shard_map/late/pallas_call | solution.py:648
  (8 shorter events, 0.1 us)
Async XLA Ops:
  0.0 8.9 %copy-start.3 = (s32[8]{0:T(128)S(1)}, s32[8]{0:T(128)}, u32[]{:S(2)}) copy-start(s32[8]{0:T(128)} %param.26) | copy-start | bytes 100
  0.0 9.0 %copy-start.4 = (s32[16]{0:T(128)S(1)}, s32[16]{0:T(128)}, u32[]{:S(2)}) copy-start(s32[16]{0:T(128)} %param.27) | copy-start | bytes 196
  0.0 9.1 %copy-start = (f32[64]{0:T(128)S(1)}, f32[64]{0:T(128)}, u32[]{:S(2)}) copy-start(f32[64]{0:T(128)} %param.18) | copy-start | bytes 772
  0.0 9.2 %copy-start.1 = (f32[64]{0:T(128)S(1)}, f32[64]{0:T(128)}, u32[]{:S(2)}) copy-start(f32[64]{0:T(128)} %param.19) | copy-start | bytes 772
  0.0 9.3 %copy-start.2 = (f32[64]{0:T(128)S(1)}, f32[64]{0:T(128)}, u32[]{:S(2)}) copy-start(f32[64]{0:T(128)} %param.20) | copy-start | bytes 772
  1.9 27.7 %collective-permute-start.3 = (bf16[2,672,128]{2,1,0:T(8,128)(2,1)S(1)}, bf16[2,672,128]{2,1,0:T(8,128)(2,1)S(1)}, u32[]{:S(2)}, u32[]{:S(2)}) collective-permute-start(bf16[2,672,128]{2,1,0:T(8,128)(2,1)S(1)} %get-tuple-element.40), channel_id=1, source_target_pairs={{0,8},{2,10},{4,12},{6,14},{8,0},{10,2},{12,4},{14,6},{1,9},{3,11}... | collective-permute-start | bytes 1032200 | tf_op jit(solution)/shard_map/ppermute | solution.py:499
  6.0 23.6 %collective-permute-start.4 = (bf16[2,672,128]{2,1,0:T(8,128)(2,1)S(1)}, bf16[2,672,128]{2,1,0:T(8,128)(2,1)S(1)}, u32[]{:S(2)}, u32[]{:S(2)}) collective-permute-start(bf16[2,672,128]{2,1,0:T(8,128)(2,1)S(1)} %get-tuple-element.41), channel_id=1, source_target_pairs={{0,12},{2,14},{4,8},{6,10},{8,4},{10,6},{12,0},{14,2},{1,13},{3,15... | collective-permute-start | bytes 1032200 | tf_op jit(solution)/shard_map/ppermute | solution.py:499
  7.4 13.5 %collective-permute-start = (bf16[2,1056,128]{2,1,0:T(8,128)(2,1)S(1)}, bf16[2,1056,128]{2,1,0:T(8,128)(2,1)S(1)}, u32[]{:S(2)}, u32[]{:S(2)}) collective-permute-start(bf16[2,1056,128]{2,1,0:T(8,128)(2,1)S(1)} %get-tuple-element.37), channel_id=1, source_target_pairs={{0,2},{2,0},{4,6},{6,4},{8,10},{10,8},{12,14},{14,12},{1,3},{3,1},... | collective-permute-start | bytes 1622024 | tf_op jit(solution)/shard_map/ppermute | solution.py:499
  29.7 30.2 %collective-permute-start.5 = (bf16[2,672,128]{2,1,0:T(8,128)(2,1)S(1)}, bf16[2,672,128]{2,1,0:T(8,128)(2,1)S(1)}, u32[]{:S(2)}, u32[]{:S(2)}) collective-permute-start(bf16[2,672,128]{2,1,0:T(8,128)(2,1)S(1)} %stack_first.1.refs_5_), channel_id=1, source_target_pairs={{0,2},{2,0},{4,6},{6,4},{8,10},{10,8},{12,14},{14,12},{1,3},{3,1},... | collective-permute-start | bytes 1032200 | tf_op jit(solution)/shard_map/ppermute | solution.py:499
  31.6 14.2 %collective-permute-start.1 = (bf16[1056,128]{1,0:T(8,128)(2,1)S(1)}, bf16[1056,128]{1,0:T(8,128)(2,1)S(1)}, u32[]{:S(2)}, u32[]{:S(2)}) collective-permute-start(bf16[1056,128]{1,0:T(8,128)(2,1)S(1)} %get-tuple-element.38), channel_id=1, source_target_pairs={{0,4},{2,6},{4,0},{6,2},{8,12},{10,14},{12,8},{14,10},{1,5},{3,7},... | collective-permute-start | bytes 811016 | tf_op jit(solution)/shard_map/ppermute | solution.py:499
  38.5 12.2 %collective-permute-start.2 = (bf16[1056,128]{1,0:T(8,128)(2,1)S(1)}, bf16[1056,128]{1,0:T(8,128)(2,1)S(1)}, u32[]{:S(2)}, u32[]{:S(2)}) collective-permute-start(bf16[1056,128]{1,0:T(8,128)(2,1)S(1)} %stack_turn.1.refs_9_), channel_id=1, source_target_pairs={{0,4},{2,6},{4,0},{6,2},{8,12},{10,14},{12,8},{14,10},{1,5},{3,7},... | collective-permute-start | bytes 811016 | tf_op jit(solution)/shard_map/ppermute | solution.py:499
  50.7 20.4 %collective-permute-start.9 = (bf16[4,384,128]{2,1,0:T(8,128)(2,1)S(1)}, bf16[4,384,128]{2,1,0:T(8,128)(2,1)S(1)}, u32[]{:S(2)}, u32[]{:S(2)}) collective-permute-start(bf16[4,384,128]{2,1,0:T(8,128)(2,1)S(1)} %stack_later.1.refs_9_), channel_id=1, source_target_pairs={{0,8},{2,10},{4,12},{6,14},{8,0},{10,2},{12,4},{14,6},{1,9},{3,11}... | collective-permute-start | bytes 1179656 | tf_op jit(solution)/shard_map/ppermute | solution.py:499
  61.0 13.4 %collective-permute-start.6 = (bf16[2,672,128]{2,1,0:T(8,128)(2,1)S(1)}, bf16[2,672,128]{2,1,0:T(8,128)(2,1)S(1)}, u32[]{:S(2)}, u32[]{:S(2)}) collective-permute-start(bf16[2,672,128]{2,1,0:T(8,128)(2,1)S(1)} %get-tuple-element.50), channel_id=1, source_target_pairs={{0,2},{2,0},{4,6},{6,4},{8,10},{10,8},{12,14},{14,12},{1,3},{3,1},... | collective-permute-start | bytes 1032200 | tf_op jit(solution)/shard_map/ppermute | solution.py:499
  61.5 17.0 %collective-permute-start.7 = (bf16[2,672,128]{2,1,0:T(8,128)(2,1)S(1)}, bf16[2,672,128]{2,1,0:T(8,128)(2,1)S(1)}, u32[]{:S(2)}, u32[]{:S(2)}) collective-permute-start(bf16[2,672,128]{2,1,0:T(8,128)(2,1)S(1)} %get-tuple-element.51), channel_id=1, source_target_pairs={{0,4},{2,6},{4,0},{6,2},{8,12},{10,14},{12,8},{14,10},{1,5},{3,7},... | collective-permute-start | bytes 1032200 | tf_op jit(solution)/shard_map/ppermute | solution.py:499
  61.8 24.1 %collective-permute-start.8 = (bf16[2,672,128]{2,1,0:T(8,128)(2,1)S(1)}, bf16[2,672,128]{2,1,0:T(8,128)(2,1)S(1)}, u32[]{:S(2)}, u32[]{:S(2)}) collective-permute-start(bf16[2,672,128]{2,1,0:T(8,128)(2,1)S(1)} %get-tuple-element.52), channel_id=1, source_target_pairs={{0,6},{2,4},{4,2},{6,0},{8,14},{10,12},{12,10},{14,8},{1,7},{3,5},... | collective-permute-start | bytes 1032200 | tf_op jit(solution)/shard_map/ppermute | solution.py:499
  72.4 18.4 %collective-permute-start.10 = (bf16[2,384,128]{2,1,0:T(8,128)(2,1)S(1)}, bf16[2,384,128]{2,1,0:T(8,128)(2,1)S(1)}, u32[]{:S(2)}, u32[]{:S(2)}) collective-permute-start(bf16[2,384,128]{2,1,0:T(8,128)(2,1)S(1)} %get-tuple-element.54), channel_id=1, source_target_pairs={{0,6},{2,4},{4,2},{6,0},{8,14},{10,12},{12,10},{14,8},{1,7},{3,5},... | collective-permute-start | bytes 589832 | tf_op jit(solution)/shard_map/ppermute | solution.py:499
  72.4 21.3 %collective-permute-start.11 = (bf16[2,384,128]{2,1,0:T(8,128)(2,1)S(1)}, bf16[2,384,128]{2,1,0:T(8,128)(2,1)S(1)}, u32[]{:S(2)}, u32[]{:S(2)}) collective-permute-start(bf16[2,384,128]{2,1,0:T(8,128)(2,1)S(1)} %get-tuple-element.55), channel_id=1, source_target_pairs={{0,4},{2,6},{4,0},{6,2},{8,12},{10,14},{12,8},{14,10},{1,5},{3,7},... | collective-permute-start | bytes 589832 | tf_op jit(solution)/shard_map/ppermute | solution.py:499
  74.4 19.4 %collective-permute-start.12 = (bf16[2,384,128]{2,1,0:T(8,128)(2,1)S(1)}, bf16[2,384,128]{2,1,0:T(8,128)(2,1)S(1)}, u32[]{:S(2)}, u32[]{:S(2)}) collective-permute-start(bf16[2,384,128]{2,1,0:T(8,128)(2,1)S(1)} %get-tuple-element.56), channel_id=1, source_target_pairs={{0,2},{2,0},{4,6},{6,4},{8,10},{10,8},{12,14},{14,12},{1,3},{3,1},... | collective-permute-start | bytes 589832 | tf_op jit(solution)/shard_map/ppermute | solution.py:499

commit v25 on v24

--- a/solution.py
+++ b/solution.py
@@ -690,16 +690,16 @@
         return pick(rows[k], [*inside, crossed], choices, tokens, (3, 2, 1))
 
     second = early(1, 2, 0, [], [turn])
-    moves = [(0, n, None, [(n, 1)]) for n in range(2)]
-    (spread,) = rearrange(
-        place, crossed_a, moves, [(2, rows[0], size)], [second[1]], "stack_first"
-    )
-    passed = swap(spread, 1)
-    sent_b, crossed_b = cross(1, [spread])
+    moves = [(n, None, None, [(n, 1)]) for n in range(2)]
+    spread = rearrange(
+        place, crossed_a, moves, [(rows[0], size)] * 2, [second[1]], "stack_first"
+    )
+    passed = [swap(spread[n], 1) for n in range(2)]
+    sent_b, crossed_b = cross(1, [spread[0]])
     second = early(1, 2, 1, second, [sent_b])
     parts.append(second)
-    choices = inside_rows(0) + [(4, 0), (6, 0), (5, 0), (6, 1)]
-    states = [pick(rows[0], [*inside, *crossed_a, passed], choices, [second[1]])]
+    choices = inside_rows(0) + [(4, 0), (6, None), (5, 0), (7, None)]
+    states = [pick(rows[0], [*inside, *crossed_a, *passed], choices, [second[1]])]
     states.append(pick_later(1, crossed_b, [states[0][0][1]]))
     result = late([0], states, parts, None, [states[1][0][1]])
     return late([1], states, parts, result, [])

time: 97.5 us -> 83.9 us (0.86)
  waiting for transfers between devices: 36.6 us -> 26.8 us
  starting transfers between devices: 26.7 us -> 22.8 us
    ppermute x13 -> x14, waiting for transfers between devices: 36.6 us -> 26.8 us  [swap(): return lax.ppermute(value, 'batch', perm=[(i, i ^ r) for i in range(8)])]
    ppermute x13 -> x14, starting transfers between devices: 26.7 us -> 22.8 us  [swap(): return lax.ppermute(value, 'batch', perm=[(i, i ^ r) for i in range(8)])]
  transfers between devices with their start and end apart: 13 -> 14, of which waited for: 8 -> 7; matrix products, arithmetic and copies ran while one was open for 1% -> 1% of each run, Pallas kernels for 28% -> 33%
where the time goes in v25:
time: 83.9 us; the launch traced here: 83.6 us
  Pallas kernels  32.9 us (39%)
  waiting for transfers between devices  26.8 us (32%)
  starting transfers between devices  22.8 us (27%)
    ppermute x14, waiting for transfers between devices, swap(): return lax.ppermute(value, 'batch', perm=[(i, i ^ r) for i in range(8)])  26.8 us
    ppermute x14, starting transfers between devices, swap(): return lax.ppermute(value, 'batch', perm=[(i, i ^ r) for i in range(8)])  22.8 us
    pallas_call x3, Pallas kernels, early(): pl.pallas_call(functools.partial(drop_tokens, functools.partial(early_ker...  20.4 us
    pallas_call x2, Pallas kernels, late(): pl.pallas_call(functools.partial(drop_tokens, kernel, keep, 1 + len(opera...  8.23 us
    pallas_call x5, Pallas kernels, rearrange(): pl.pallas_call(functools.partial(drop_tokens, kernel, 1 + len(sources), l...  2.42 us
    pallas_call x1, Pallas kernels, cast(): pl.pallas_call(kernel, grid_spec=pltpu.PrefetchScalarGridSpec(num_scalar_...  1.88 us
  transfers between devices with their start and end apart: 14, of which 7 were waited for; matrix products, arithmetic and copies ran while one was open for 1% of the time, Pallas kernels for 33%

profile of v25, /device:TPU:0, one launch (start us, length us, event | category | flops | bytes accessed | tf_op | source)
XLA Modules:
  0.0 83.6 jit_solution(17074614256203492779)
XLA Ops:
  0.0 1.9 %cast_states.1 = (bf16[1056,128]{1,0:T(8,128)(2,1)S(1)}, bf16[1056,128]{1,0:T(8,128)(2,1)S(1)}, bf16[2,1056,128]{2,1,0:T(8,128)(2,1)S(1)}, bf16[2,672,128]{2,1,0:T(8,128)(2,1)S(1)}, bf16[2,672,128]{2,1,0:T(8,128)(2,1)S(1)}) custom-call(s32[1]{0:T(128)} %bitcast.place_ref.refs_0_, f32[4,16,64,128]{3,2,1,0:T(8,128)} %bitcast.5, f32[4,16,64,128]{3,2,1,0:T(8,128)} %bitcast.6, ...), custom_call_target="tpu_custom_call" | custom-call | flops 1 | bytes 1 | tf_op jit(solution)/shard_map/cast_states/pallas_call | solution.py:532
  1.9 3.1 %collective-permute-start.1 = (bf16[1056,128]{1,0:T(8,128)(2,1)S(1)}, bf16[1056,128]{1,0:T(8,128)(2,1)S(1)}, u32[]{:S(2)}, u32[]{:S(2)}) collective-permute-start(bf16[1056,128]{1,0:T(8,128)(2,1)S(1)} %get-tuple-element.40), channel_id=1, source_target_pairs={{0,4},{2,6},{4,0},{6,2},{8,12},{10,14},{12,8},{14,10},{1,5},{3,7},... | collective-permute-start | bytes 811016 | tf_op jit(solution)/shard_map/ppermute | solution.py:499
  5.0 2.6 %collective-permute-start.3 = (bf16[2,672,128]{2,1,0:T(8,128)(2,1)S(1)}, bf16[2,672,128]{2,1,0:T(8,128)(2,1)S(1)}, u32[]{:S(2)}, u32[]{:S(2)}) collective-permute-start(bf16[2,672,128]{2,1,0:T(8,128)(2,1)S(1)} %get-tuple-element.42), channel_id=1, source_target_pairs={{0,8},{2,10},{4,12},{6,14},{8,0},{10,2},{12,4},{14,6},{1,9},{3,11}... | collective-permute-start | bytes 1032200 | tf_op jit(solution)/shard_map/ppermute | solution.py:499
  7.6 0.0 collective-permute-start.4
  7.6 1.7 %collective-permute-start = (bf16[2,1056,128]{2,1,0:T(8,128)(2,1)S(1)}, bf16[2,1056,128]{2,1,0:T(8,128)(2,1)S(1)}, u32[]{:S(2)}, u32[]{:S(2)}) collective-permute-start(bf16[2,1056,128]{2,1,0:T(8,128)(2,1)S(1)} %get-tuple-element.39), channel_id=1, source_target_pairs={{0,2},{2,0},{4,6},{6,4},{8,10},{10,8},{12,14},{14,12},{1,3},{3,1},... | collective-permute-start | bytes 1622024 | tf_op jit(solution)/shard_map/ppermute | solution.py:499
  9.3 0.0 copy-done.3
  9.3 0.1 select_reduce_fusion.1
  9.4 0.0 copy-done
  9.4 0.1 copy.28.refs_4_
  9.5 0.0 copy-done.1
  9.5 0.1 copy.29.refs_5_
  9.6 0.0 copy-done.2
  9.6 0.1 broadcast_in_dim.55
  9.7 0.1 broadcast_in_dim_reshape.3.refs_6_
  9.8 0.0 copy-done.4
  9.8 0.1 convert_reduce_fusion
  9.9 0.2 select_reduce_fusion
  10.1 9.7 %early.3 = (f32[4,256,1024]{2,1,0:T(8,128)S(1)}, bf16[4,256,128]{2,1,0:T(8,128)(2,1)S(1)}, f32[4,16,256]{2,1,0:T(8,128)S(1)}, f32[4,256,256]{2,1,0:T(8,128)S(1)}...) custom-call(bf16[2,256,4096]{2,1,0:T(8,128)(2,1)} %refs_0_.5, bf16[2,256,512]{2,1,0:T(8,128)(2,1)} %refs_1_.5, ...), custom_call_target="tpu_custom_call" | custom-call | flops 1 | bytes 1 | tf_op jit(solution)/shard_map/early/pallas_call | solution.py:597
  19.8 1.3 %collective-permute-done.refs_1_.refs_2_ = bf16[2,1056,128]{2,1,0:T(8,128)(2,1)S(1)} collective-permute-done((bf16[2,1056,128]{2,1,0:T(8,128)(2,1)S(1)}, bf16[2,1056,128]{2,1,0:T(8,128)(2,1)S(1)}, u32[]{:S(2)}, u32[]{:S(2)}) %collective-permute-start) | collective-permute-done | bytes 540704 | tf_op jit(solution)/shard_map/ppermute | solution.py:499
  21.1 0.7 collective-permute-start.2
  21.7 5.4 %early.4 = (f32[4,256,1024]{2,1,0:T(8,128)S(1)}, bf16[4,256,128]{2,1,0:T(8,128)(2,1)S(1)}, f32[4,16,256]{2,1,0:T(8,128)S(1)}, f32[4,256,256]{2,1,0:T(8,128)S(1)}...) custom-call(bf16[2,256,4096]{2,1,0:T(8,128)(2,1)} %refs_0_.5, bf16[2,256,512]{2,1,0:T(8,128)(2,1)} %refs_1_.5, ...), custom_call_target="tpu_custom_call" | custom-call | flops 1 | bytes 1 | tf_op jit(solution)/shard_map/early/pallas_call | solution.py:597
  27.1 4.5 %collective-permute-done.3.refs_1_.refs_5_ = bf16[2,672,128]{2,1,0:T(8,128)(2,1)S(1)} collective-permute-done((bf16[2,672,128]{2,1,0:T(8,128)(2,1)S(1)}, bf16[2,672,128]{2,1,0:T(8,128)(2,1)S(1)}, u32[]{:S(2)}, u32[]{:S(2)}) %collective-permute-start.3) | collective-permute-done | bytes 344096 | tf_op jit(solution)/shard_map/ppermute | solution.py:499
  31.7 0.0 collective-permute-done.4.refs_2_.refs_6_
  31.7 1.6 %collective-permute-start.6 = (bf16[672,128]{1,0:T(8,128)(2,1)S(1)}, bf16[672,128]{1,0:T(8,128)(2,1)S(1)}, u32[]{:S(2)}, u32[]{:S(2)}) collective-permute-start(bf16[672,128]{1,0:T(8,128)(2,1)S(1)} %get-tuple-element.46), channel_id=1, source_target_pairs={{0,2},{2,0},{4,6},{6,4},{8,10},{10,8},{12,14},{14,12},{1,3},{3,1},... | collective-permute-start | bytes 516104 | tf_op jit(solution)/shard_map/ppermute | solution.py:499
  33.3 0.5 collective-permute-start.5
  33.8 0.0 collective-permute-done.1.refs_3_
  33.8 2.1 %collective-permute-done.2.refs_4_ = bf16[1056,128]{1,0:T(8,128)(2,1)S(1)} collective-permute-done((bf16[1056,128]{1,0:T(8,128)(2,1)S(1)}, bf16[1056,128]{1,0:T(8,128)(2,1)S(1)}, u32[]{:S(2)}, u32[]{:S(2)}) %collective-permute-start.2) | collective-permute-done | bytes 270368 | tf_op jit(solution)/shard_map/ppermute | solution.py:499
  35.9 5.5 %collective-permute-start.10 = (bf16[4,384,128]{2,1,0:T(8,128)(2,1)S(1)}, bf16[4,384,128]{2,1,0:T(8,128)(2,1)S(1)}, u32[]{:S(2)}, u32[]{:S(2)}) collective-permute-start(bf16[4,384,128]{2,1,0:T(8,128)(2,1)S(1)} %stack_later.1.refs_9_), channel_id=1, source_target_pairs={{0,8},{2,10},{4,12},{6,14},{8,0},{10,2},{12,4},{14,6},{1,9},{3,11}... | collective-permute-start | bytes 1179656 | tf_op jit(solution)/shard_map/ppermute | solution.py:499
  41.4 5.4 %early.5 = (f32[4,256,1024]{2,1,0:T(8,128)S(1)}, bf16[4,256,128]{2,1,0:T(8,128)(2,1)S(1)}, f32[4,16,256]{2,1,0:T(8,128)S(1)}, f32[4,256,256]{2,1,0:T(8,128)S(1)}...) custom-call(bf16[2,256,4096]{2,1,0:T(8,128)(2,1)} %refs_0_.5, ...), custom_call_target="tpu_custom_call", output_to_operand_aliasing={{0}: (10, {}), {1}: (11, {}), {2}: (12, {}), {3}: (13, {}),... | custom-call | flops 1 | bytes 1 | tf_op jit(solution)/shard_map/early/pallas_call | solution.py:597
  46.8 0.0 collective-permute-done.6.refs_8_
  46.8 0.0 collective-permute-done.5.refs_7_
  46.8 1.1 %pick_states.2 = (bf16[2,672,128]{2,1,0:T(8,128)(2,1)S(1)}, bf16[2,672,128]{2,1,0:T(8,128)(2,1)S(1)}, bf16[2,672,128]{2,1,0:T(8,128)(2,1)S(1)}, bf16[2,672,128]{2,1,0:T(8,128)(2,1)S(1)}) custom-call(s32[8]{0:T(128)S(1)} %broadcast_xor_fusion.refs_10_.refs_0_, bf16[1056,128]{1,0:T(8,128)(2,1)S(1)} %get-tuple-element.38.refs_9_.refs_1_, ...), custom_call_target="tpu_custom_call" | custom-call | flops 1 | bytes 1 | tf_op jit(solution)/shard_map/pick_states/pallas_call | solution.py:564
  47.9 1.6 %collective-permute-start.7 = (bf16[2,672,128]{2,1,0:T(8,128)(2,1)S(1)}, bf16[2,672,128]{2,1,0:T(8,128)(2,1)S(1)}, u32[]{:S(2)}, u32[]{:S(2)}) collective-permute-start(bf16[2,672,128]{2,1,0:T(8,128)(2,1)S(1)} %get-tuple-element.54), channel_id=1, source_target_pairs={{0,2},{2,0},{4,6},{6,4},{8,10},{10,8},{12,14},{14,12},{1,3},{3,1},... | collective-permute-start | bytes 1032200 | tf_op jit(solution)/shard_map/ppermute | solution.py:499
  49.5 0.1 collective-permute-start.8
  49.6 1.9 %collective-permute-start.9 = (bf16[2,672,128]{2,1,0:T(8,128)(2,1)S(1)}, bf16[2,672,128]{2,1,0:T(8,128)(2,1)S(1)}, u32[]{:S(2)}, u32[]{:S(2)}) collective-permute-start(bf16[2,672,128]{2,1,0:T(8,128)(2,1)S(1)} %get-tuple-element.56), channel_id=1, source_target_pairs={{0,6},{2,4},{4,2},{6,0},{8,14},{10,12},{12,10},{14,8},{1,7},{3,5},... | collective-permute-start | bytes 1032200 | tf_op jit(solution)/shard_map/ppermute | solution.py:499
  51.5 5.9 %collective-permute-done.10.refs_5_ = bf16[4,384,128]{2,1,0:T(8,128)(2,1)S(1)} collective-permute-done((bf16[4,384,128]{2,1,0:T(8,128)(2,1)S(1)}, bf16[4,384,128]{2,1,0:T(8,128)(2,1)S(1)}, u32[]{:S(2)}, u32[]{:S(2)}) %collective-permute-start.10) | collective-permute-done | bytes 393248 | tf_op jit(solution)/shard_map/ppermute | solution.py:499
  57.4 1.2 %pick_states.3 = (bf16[2,384,128]{2,1,0:T(8,128)(2,1)S(1)}, bf16[2,384,128]{2,1,0:T(8,128)(2,1)S(1)}, bf16[2,384,128]{2,1,0:T(8,128)(2,1)S(1)}, bf16[2,384,128]{2,1,0:T(8,128)(2,1)S(1)}) custom-call(s32[8]{0:T(128)S(1)} %broadcast_xor_fusion.refs_10_.refs_0_, bf16[1056,128]{1,0:T(8,128)(2,1)S(1)} %get-tuple-element.38.refs_9_.refs_1_, ...), custom_call_target="tpu_custom_call" | custom-call | flops 1 | bytes 1 | tf_op jit(solution)/shard_map/pick_states/pallas_call | solution.py:564
  58.6 0.1 collective-permute-start.11
  58.7 3.0 %collective-permute-start.12 = (bf16[2,384,128]{2,1,0:T(8,128)(2,1)S(1)}, bf16[2,384,128]{2,1,0:T(8,128)(2,1)S(1)}, u32[]{:S(2)}, u32[]{:S(2)}) collective-permute-start(bf16[2,384,128]{2,1,0:T(8,128)(2,1)S(1)} %get-tuple-element.59), channel_id=1, source_target_pairs={{0,4},{2,6},{4,0},{6,2},{8,12},{10,14},{12,8},{14,10},{1,5},{3,7},... | collective-permute-start | bytes 589832 | tf_op jit(solution)/shard_map/ppermute | solution.py:499
  61.7 0.0 collective-permute-done.7.refs_2_.refs_6_
  61.7 0.5 collective-permute-start.13
  62.2 2.6 %collective-permute-done.8.refs_3_.refs_7_ = bf16[2,672,128]{2,1,0:T(8,128)(2,1)S(1)} collective-permute-done((bf16[2,672,128]{2,1,0:T(8,128)(2,1)S(1)}, bf16[2,672,128]{2,1,0:T(8,128)(2,1)S(1)}, u32[]{:S(2)}, u32[]{:S(2)}) %collective-permute-start.8) | collective-permute-done | bytes 344096 | tf_op jit(solution)/shard_map/ppermute | solution.py:499
  64.8 8.4 %collective-permute-done.9.refs_4_.refs_8_ = bf16[2,672,128]{2,1,0:T(8,128)(2,1)S(1)} collective-permute-done((bf16[2,672,128]{2,1,0:T(8,128)(2,1)S(1)}, bf16[2,672,128]{2,1,0:T(8,128)(2,1)S(1)}, u32[]{:S(2)}, u32[]{:S(2)}) %collective-permute-start.9) | collective-permute-done | bytes 344096 | tf_op jit(solution)/shard_map/ppermute | solution.py:499
  73.2 4.9 %late.2.refs_21_ = bf16[2,256,4096]{2,1,0:T(8,128)(2,1)} custom-call(s32[1]{0:T(128)} %bitcast.place_ref.refs_0_, bf16[2,672,128]{2,1,0:T(8,128)(2,1)S(1)} %get-tuple-element.53.refs_6_.refs_1_.refs_5_, bf16[2,672,128]{2,1,0:T(8,128)(2,1)S(1)} %collective-permute-done.7.refs_2_.refs_6_, bf16[2,672,128]{2,1,0:T(8,128)(2,1)S(1)} %collective-permute-done.8.refs_3_.refs_7_, ...), custom_call_target="tpu_custom_call" | custom-call | flops 1 | bytes 1 | tf_op jit(solution)/shard_map/late/pallas_call | solution.py:648
  78.1 0.0 collective-permute-done.11.refs_6_
  78.1 2.0 %collective-permute-done.12.refs_7_ = bf16[2,384,128]{2,1,0:T(8,128)(2,1)S(1)} collective-permute-done((bf16[2,384,128]{2,1,0:T(8,128)(2,1)S(1)}, bf16[2,384,128]{2,1,0:T(8,128)(2,1)S(1)}, u32[]{:S(2)}, u32[]{:S(2)}) %collective-permute-start.12) | collective-permute-done | bytes 196640 | tf_op jit(solution)/shard_map/ppermute | solution.py:499
  80.2 0.0 collective-permute-done.13.refs_8_
  80.2 3.3 %late.3 = bf16[2,256,4096]{2,1,0:T(8,128)(2,1)} custom-call(s32[1]{0:T(128)} %bitcast.place_ref.refs_0_, bf16[2,672,128]{2,1,0:T(8,128)(2,1)S(1)} %get-tuple-element.53.refs_6_.refs_1_.refs_5_, bf16[2,672,128]{2,1,0:T(8,128)(2,1)S(1)} %collective-permute-done.7.refs_2_.refs_6_, ...), custom_call_target="tpu_custom_call", output_to_operand_aliasing={{}: (21, {})} | custom-call | flops 1 | bytes 1 | tf_op jit(solution)/shard_map/late/pallas_call | solution.py:648
  (10 shorter events, 0.1 us)
Async XLA Ops:
  0.0 9.3 %copy-start.3 = (s32[8]{0:T(128)S(1)}, s32[8]{0:T(128)}, u32[]{:S(2)}) copy-start(s32[8]{0:T(128)} %param.26) | copy-start | bytes 100
  0.0 9.4 %copy-start = (f32[64]{0:T(128)S(1)}, f32[64]{0:T(128)}, u32[]{:S(2)}) copy-start(f32[64]{0:T(128)} %param.18) | copy-start | bytes 772
  0.0 9.5 %copy-start.1 = (f32[64]{0:T(128)S(1)}, f32[64]{0:T(128)}, u32[]{:S(2)}) copy-start(f32[64]{0:T(128)} %param.19) | copy-start | bytes 772
  0.0 9.6 %copy-start.2 = (f32[64]{0:T(128)S(1)}, f32[64]{0:T(128)}, u32[]{:S(2)}) copy-start(f32[64]{0:T(128)} %param.20) | copy-start | bytes 772
  0.0 9.8 %copy-start.4 = (s32[16]{0:T(128)S(1)}, s32[16]{0:T(128)}, u32[]{:S(2)}) copy-start(s32[16]{0:T(128)} %param.27) | copy-start | bytes 196
  1.9 31.9 %collective-permute-start.1 = (bf16[1056,128]{1,0:T(8,128)(2,1)S(1)}, bf16[1056,128]{1,0:T(8,128)(2,1)S(1)}, u32[]{:S(2)}, u32[]{:S(2)}) collective-permute-start(bf16[1056,128]{1,0:T(8,128)(2,1)S(1)} %get-tuple-element.40), channel_id=1, source_target_pairs={{0,4},{2,6},{4,0},{6,2},{8,12},{10,14},{12,8},{14,10},{1,5},{3,7},... | collective-permute-start | bytes 811016 | tf_op jit(solution)/shard_map/ppermute | solution.py:499
  5.0 26.7 %collective-permute-start.3 = (bf16[2,672,128]{2,1,0:T(8,128)(2,1)S(1)}, bf16[2,672,128]{2,1,0:T(8,128)(2,1)S(1)}, u32[]{:S(2)}, u32[]{:S(2)}) collective-permute-start(bf16[2,672,128]{2,1,0:T(8,128)(2,1)S(1)} %get-tuple-element.42), channel_id=1, source_target_pairs={{0,8},{2,10},{4,12},{6,14},{8,0},{10,2},{12,4},{14,6},{1,9},{3,11}... | collective-permute-start | bytes 1032200 | tf_op jit(solution)/shard_map/ppermute | solution.py:499
  7.6 24.1 %collective-permute-start.4 = (bf16[2,672,128]{2,1,0:T(8,128)(2,1)S(1)}, bf16[2,672,128]{2,1,0:T(8,128)(2,1)S(1)}, u32[]{:S(2)}, u32[]{:S(2)}) collective-permute-start(bf16[2,672,128]{2,1,0:T(8,128)(2,1)S(1)} %get-tuple-element.43), channel_id=1, source_target_pairs={{0,12},{2,14},{4,8},{6,10},{8,4},{10,6},{12,0},{14,2},{1,13},{3,15... | collective-permute-start | bytes 1032200 | tf_op jit(solution)/shard_map/ppermute | solution.py:499
  7.6 13.5 %collective-permute-start = (bf16[2,1056,128]{2,1,0:T(8,128)(2,1)S(1)}, bf16[2,1056,128]{2,1,0:T(8,128)(2,1)S(1)}, u32[]{:S(2)}, u32[]{:S(2)}) collective-permute-start(bf16[2,1056,128]{2,1,0:T(8,128)(2,1)S(1)} %get-tuple-element.39), channel_id=1, source_target_pairs={{0,2},{2,0},{4,6},{6,4},{8,10},{10,8},{12,14},{14,12},{1,3},{3,1},... | collective-permute-start | bytes 1622024 | tf_op jit(solution)/shard_map/ppermute | solution.py:499
  21.1 14.8 %collective-permute-start.2 = (bf16[1056,128]{1,0:T(8,128)(2,1)S(1)}, bf16[1056,128]{1,0:T(8,128)(2,1)S(1)}, u32[]{:S(2)}, u32[]{:S(2)}) collective-permute-start(bf16[1056,128]{1,0:T(8,128)(2,1)S(1)} %stack_turn.1.refs_9_), channel_id=1, source_target_pairs={{0,4},{2,6},{4,0},{6,2},{8,12},{10,14},{12,8},{14,10},{1,5},{3,7},... | collective-permute-start | bytes 811016 | tf_op jit(solution)/shard_map/ppermute | solution.py:499
  31.7 15.1 %collective-permute-start.6 = (bf16[672,128]{1,0:T(8,128)(2,1)S(1)}, bf16[672,128]{1,0:T(8,128)(2,1)S(1)}, u32[]{:S(2)}, u32[]{:S(2)}) collective-permute-start(bf16[672,128]{1,0:T(8,128)(2,1)S(1)} %get-tuple-element.46), channel_id=1, source_target_pairs={{0,2},{2,0},{4,6},{6,4},{8,10},{10,8},{12,14},{14,12},{1,3},{3,1},... | collective-permute-start | bytes 516104 | tf_op jit(solution)/shard_map/ppermute | solution.py:499
  33.3 13.5 %collective-permute-start.5 = (bf16[672,128]{1,0:T(8,128)(2,1)S(1)}, bf16[672,128]{1,0:T(8,128)(2,1)S(1)}, u32[]{:S(2)}, u32[]{:S(2)}) collective-permute-start(bf16[672,128]{1,0:T(8,128)(2,1)S(1)} %get-tuple-element.45.refs_5_), channel_id=1, source_target_pairs={{0,2},{2,0},{4,6},{6,4},{8,10},{10,8},{12,14},{14,12},{1,3},{3,1},... | collective-permute-start | bytes 516104 | tf_op jit(solution)/shard_map/ppermute | solution.py:499
  35.9 21.4 %collective-permute-start.10 = (bf16[4,384,128]{2,1,0:T(8,128)(2,1)S(1)}, bf16[4,384,128]{2,1,0:T(8,128)(2,1)S(1)}, u32[]{:S(2)}, u32[]{:S(2)}) collective-permute-start(bf16[4,384,128]{2,1,0:T(8,128)(2,1)S(1)} %stack_later.1.refs_9_), channel_id=1, source_target_pairs={{0,8},{2,10},{4,12},{6,14},{8,0},{10,2},{12,4},{14,6},{1,9},{3,11}... | collective-permute-start | bytes 1179656 | tf_op jit(solution)/shard_map/ppermute | solution.py:499
  47.9 13.7 %collective-permute-start.7 = (bf16[2,672,128]{2,1,0:T(8,128)(2,1)S(1)}, bf16[2,672,128]{2,1,0:T(8,128)(2,1)S(1)}, u32[]{:S(2)}, u32[]{:S(2)}) collective-permute-start(bf16[2,672,128]{2,1,0:T(8,128)(2,1)S(1)} %get-tuple-element.54), channel_id=1, source_target_pairs={{0,2},{2,0},{4,6},{6,4},{8,10},{10,8},{12,14},{14,12},{1,3},{3,1},... | collective-permute-start | bytes 1032200 | tf_op jit(solution)/shard_map/ppermute | solution.py:499
  49.5 15.3 %collective-permute-start.8 = (bf16[2,672,128]{2,1,0:T(8,128)(2,1)S(1)}, bf16[2,672,128]{2,1,0:T(8,128)(2,1)S(1)}, u32[]{:S(2)}, u32[]{:S(2)}) collective-permute-start(bf16[2,672,128]{2,1,0:T(8,128)(2,1)S(1)} %get-tuple-element.55), channel_id=1, source_target_pairs={{0,4},{2,6},{4,0},{6,2},{8,12},{10,14},{12,8},{14,10},{1,5},{3,7},... | collective-permute-start | bytes 1032200 | tf_op jit(solution)/shard_map/ppermute | solution.py:499
  49.6 23.6 %collective-permute-start.9 = (bf16[2,672,128]{2,1,0:T(8,128)(2,1)S(1)}, bf16[2,672,128]{2,1,0:T(8,128)(2,1)S(1)}, u32[]{:S(2)}, u32[]{:S(2)}) collective-permute-start(bf16[2,672,128]{2,1,0:T(8,128)(2,1)S(1)} %get-tuple-element.56), channel_id=1, source_target_pairs={{0,6},{2,4},{4,2},{6,0},{8,14},{10,12},{12,10},{14,8},{1,7},{3,5},... | collective-permute-start | bytes 1032200 | tf_op jit(solution)/shard_map/ppermute | solution.py:499
  58.6 19.5 %collective-permute-start.11 = (bf16[2,384,128]{2,1,0:T(8,128)(2,1)S(1)}, bf16[2,384,128]{2,1,0:T(8,128)(2,1)S(1)}, u32[]{:S(2)}, u32[]{:S(2)}) collective-permute-start(bf16[2,384,128]{2,1,0:T(8,128)(2,1)S(1)} %get-tuple-element.58), channel_id=1, source_target_pairs={{0,6},{2,4},{4,2},{6,0},{8,14},{10,12},{12,10},{14,8},{1,7},{3,5},... | collective-permute-start | bytes 589832 | tf_op jit(solution)/shard_map/ppermute | solution.py:499
  58.7 21.5 %collective-permute-start.12 = (bf16[2,384,128]{2,1,0:T(8,128)(2,1)S(1)}, bf16[2,384,128]{2,1,0:T(8,128)(2,1)S(1)}, u32[]{:S(2)}, u32[]{:S(2)}) collective-permute-start(bf16[2,384,128]{2,1,0:T(8,128)(2,1)S(1)} %get-tuple-element.59), channel_id=1, source_target_pairs={{0,4},{2,6},{4,0},{6,2},{8,12},{10,14},{12,8},{14,10},{1,5},{3,7},... | collective-permute-start | bytes 589832 | tf_op jit(solution)/shard_map/ppermute | solution.py:499
  61.7 18.5 %collective-permute-start.13 = (bf16[2,384,128]{2,1,0:T(8,128)(2,1)S(1)}, bf16[2,384,128]{2,1,0:T(8,128)(2,1)S(1)}, u32[]{:S(2)}, u32[]{:S(2)}) collective-permute-start(bf16[2,384,128]{2,1,0:T(8,128)(2,1)S(1)} %get-tuple-element.60), channel_id=1, source_target_pairs={{0,2},{2,0},{4,6},{6,4},{8,10},{10,8},{12,14},{14,12},{1,3},{3,1},... | collective-permute-start | bytes 589832 | tf_op jit(solution)/shard_map/ppermute | solution.py:499

commit v26 on v22

--- a/solution.py
+++ b/solution.py
@@ -703,8 +703,8 @@
     sent_c, crossed_c = cross(2, [states[0][0][1], crossed_b])
     states.append(pick_later(1, crossed_b, [sent_c]))
     states.append(pick_later(2, crossed_c, [states[1][0][1]]))
-    result = late([0, 1], states, parts, None, [states[2][0][1]])
-    return late([2], states, parts, result, [])
+    result = late([0], states, parts, None, [states[2][0][1]])
+    return late([1, 2], states, parts, result, [])
 
 
 def solution(mesh):

time: 79.5 us -> 80.9 us (1.018)
  starting transfers between devices: 25 us -> 27.1 us
    ppermute x17, starting transfers between devices: 25 us -> 27.1 us  [swap(): return lax.ppermute(value, 'batch', perm=[(i, i ^ r) for i in range(8)])]
    pallas_call x2, Pallas kernels: 8.66 us -> 7.83 us  [late(): pl.pallas_call(functools.partial(drop_tokens, kernel, keep, 1 + len(opera...]
  transfers between devices with their start and end apart: 17 -> 17, of which waited for: 8 -> 8; matrix products, arithmetic and copies ran while one was open for 1% -> 1% of each run, Pallas kernels for 37% -> 34%
where the time goes in v26:
time: 80.9 us; the launch traced here: 80.7 us
  Pallas kernels  33.5 us (41%)
  starting transfers between devices  27.1 us (33%)
  waiting for transfers between devices  19 us (23%)
    ppermute x17, starting transfers between devices, swap(): return lax.ppermute(value, 'batch', perm=[(i, i ^ r) for i in range(8)])  27.1 us
    pallas_call x3, Pallas kernels, early(): pl.pallas_call(functools.partial(drop_tokens, functools.partial(early_ker...  20.4 us
    ppermute x17, waiting for transfers between devices, swap(): return lax.ppermute(value, 'batch', perm=[(i, i ^ r) for i in range(8)])  19 us
    pallas_call x2, Pallas kernels, late(): pl.pallas_call(functools.partial(drop_tokens, kernel, keep, 1 + len(opera...  7.83 us
    pallas_call x7, Pallas kernels, rearrange(): pl.pallas_call(functools.partial(drop_tokens, kernel, 1 + len(sources), l...  3.45 us
    pallas_call x1, Pallas kernels, cast(): pl.pallas_call(kernel, grid_spec=pltpu.PrefetchScalarGridSpec(num_scalar_...  1.82 us
  transfers between devices with their start and end apart: 17, of which 8 were waited for; matrix products, arithmetic and copies ran while one was open for 1% of the time, Pallas kernels for 34%

profile of v26, /device:TPU:0, one launch (start us, length us, event | category | flops | bytes accessed | tf_op | source)
XLA Modules:
  0.0 80.7 jit_solution(7674562815089252292)
XLA Ops:
  0.0 1.8 %cast_states.1 = (bf16[1056,128]{1,0:T(8,128)(2,1)S(1)}, bf16[1056,128]{1,0:T(8,128)(2,1)S(1)}, bf16[2,1056,128]{2,1,0:T(8,128)(2,1)S(1)}, bf16[2,544,128]{2,1,0:T(8,128)(2,1)S(1)}, bf16[2,544,128]{2,1,0:T(8,128)(2,1)S(1)}) custom-call(s32[1]{0:T(128)} %bitcast.place_ref.refs_0_, f32[4,16,64,128]{3,2,1,0:T(8,128)} %bitcast.5, f32[4,16,64,128]{3,2,1,0:T(8,128)} %bitcast.6, ...), custom_call_target="tpu_custom_call" | custom-call | flops 1 | bytes 1 | tf_op jit(solution)/shard_map/cast_states/pallas_call | solution.py:532
  1.8 3.1 %collective-permute-start.1 = (bf16[1056,128]{1,0:T(8,128)(2,1)S(1)}, bf16[1056,128]{1,0:T(8,128)(2,1)S(1)}, u32[]{:S(2)}, u32[]{:S(2)}) collective-permute-start(bf16[1056,128]{1,0:T(8,128)(2,1)S(1)} %get-tuple-element.42), channel_id=1, source_target_pairs={{0,4},{2,6},{4,0},{6,2},{8,12},{10,14},{12,8},{14,10},{1,5},{3,7},... | collective-permute-start | bytes 811016 | tf_op jit(solution)/shard_map/ppermute | solution.py:499
  4.9 2.6 %collective-permute-start.3 = (bf16[2,544,128]{2,1,0:T(8,128)(2,1)S(1)}, bf16[2,544,128]{2,1,0:T(8,128)(2,1)S(1)}, u32[]{:S(2)}, u32[]{:S(2)}) collective-permute-start(bf16[2,544,128]{2,1,0:T(8,128)(2,1)S(1)} %get-tuple-element.44), channel_id=1, source_target_pairs={{0,8},{2,10},{4,12},{6,14},{8,0},{10,2},{12,4},{14,6},{1,9},{3,11}... | collective-permute-start | bytes 835592 | tf_op jit(solution)/shard_map/ppermute | solution.py:499
  7.5 0.0 collective-permute-start.4
  7.5 1.7 %collective-permute-start = (bf16[2,1056,128]{2,1,0:T(8,128)(2,1)S(1)}, bf16[2,1056,128]{2,1,0:T(8,128)(2,1)S(1)}, u32[]{:S(2)}, u32[]{:S(2)}) collective-permute-start(bf16[2,1056,128]{2,1,0:T(8,128)(2,1)S(1)} %get-tuple-element.41), channel_id=1, source_target_pairs={{0,2},{2,0},{4,6},{6,4},{8,10},{10,8},{12,14},{14,12},{1,3},{3,1},... | collective-permute-start | bytes 1622024 | tf_op jit(solution)/shard_map/ppermute | solution.py:499
  9.3 0.1 select_reduce_fusion.1
  9.4 0.1 convert_reduce_fusion
  9.5 0.2 select_reduce_fusion
  9.7 0.1 copy.28.refs_4_
  9.8 0.1 copy.29.refs_5_
  9.9 0.1 broadcast_in_dim.55
  10.0 0.1 broadcast_in_dim_reshape.3.refs_6_
  10.1 9.6 %early.3 = (f32[4,256,1024]{2,1,0:T(8,128)S(1)}, bf16[4,256,128]{2,1,0:T(8,128)(2,1)S(1)}, f32[4,16,256]{2,1,0:T(8,128)S(1)}, f32[4,256,256]{2,1,0:T(8,128)S(1)}...) custom-call(bf16[2,256,4096]{2,1,0:T(8,128)(2,1)} %refs_0_.5, bf16[2,256,512]{2,1,0:T(8,128)(2,1)} %refs_1_.5, ...), custom_call_target="tpu_custom_call" | custom-call | flops 1 | bytes 1 | tf_op jit(solution)/shard_map/early/pallas_call | solution.py:597
  19.7 1.3 %collective-permute-done.refs_1_.refs_2_ = bf16[2,1056,128]{2,1,0:T(8,128)(2,1)S(1)} collective-permute-done((bf16[2,1056,128]{2,1,0:T(8,128)(2,1)S(1)}, bf16[2,1056,128]{2,1,0:T(8,128)(2,1)S(1)}, u32[]{:S(2)}, u32[]{:S(2)}) %collective-permute-start) | collective-permute-done | bytes 540704 | tf_op jit(solution)/shard_map/ppermute | solution.py:499
  21.0 0.7 collective-permute-start.2
  21.7 5.4 %early.4 = (f32[4,256,1024]{2,1,0:T(8,128)S(1)}, bf16[4,256,128]{2,1,0:T(8,128)(2,1)S(1)}, f32[4,16,256]{2,1,0:T(8,128)S(1)}, f32[4,256,256]{2,1,0:T(8,128)S(1)}...) custom-call(bf16[2,256,4096]{2,1,0:T(8,128)(2,1)} %refs_0_.5, bf16[2,256,512]{2,1,0:T(8,128)(2,1)} %refs_1_.5, ...), custom_call_target="tpu_custom_call" | custom-call | flops 1 | bytes 1 | tf_op jit(solution)/shard_map/early/pallas_call | solution.py:597
  27.1 0.3 collective-permute-done.3.refs_1_.refs_5_
  27.4 0.0 collective-permute-done.4.refs_2_.refs_6_
  27.4 1.6 %collective-permute-start.5 = (bf16[2,544,128]{2,1,0:T(8,128)(2,1)S(1)}, bf16[2,544,128]{2,1,0:T(8,128)(2,1)S(1)}, u32[]{:S(2)}, u32[]{:S(2)}) collective-permute-start(bf16[2,544,128]{2,1,0:T(8,128)(2,1)S(1)} %stack_first.1.refs_5_), channel_id=1, source_target_pairs={{0,2},{2,0},{4,6},{6,4},{8,10},{10,8},{12,14},{14,12},{1,3},{3,1},... | collective-permute-start | bytes 835592 | tf_op jit(solution)/shard_map/ppermute | solution.py:499
  29.0 0.0 collective-permute-done.1.refs_3_
  29.0 3.3 %collective-permute-done.2.refs_4_ = bf16[1056,128]{1,0:T(8,128)(2,1)S(1)} collective-permute-done((bf16[1056,128]{1,0:T(8,128)(2,1)S(1)}, bf16[1056,128]{1,0:T(8,128)(2,1)S(1)}, u32[]{:S(2)}, u32[]{:S(2)}) %collective-permute-start.2) | collective-permute-done | bytes 270368 | tf_op jit(solution)/shard_map/ppermute | solution.py:499
  32.3 2.9 %collective-permute-start.9 = (bf16[4,256,128]{2,1,0:T(8,128)(2,1)S(1)}, bf16[4,256,128]{2,1,0:T(8,128)(2,1)S(1)}, u32[]{:S(2)}, u32[]{:S(2)}) collective-permute-start(bf16[4,256,128]{2,1,0:T(8,128)(2,1)S(1)} %stack_later.2.refs_9_), channel_id=1, source_target_pairs={{0,8},{2,10},{4,12},{6,14},{8,0},{10,2},{12,4},{14,6},{1,9},{3,11}... | collective-permute-start | bytes 786440 | tf_op jit(solution)/shard_map/ppermute | solution.py:499
  35.2 5.4 %early.5 = (f32[4,256,1024]{2,1,0:T(8,128)S(1)}, bf16[4,256,128]{2,1,0:T(8,128)(2,1)S(1)}, f32[4,16,256]{2,1,0:T(8,128)S(1)}, f32[4,256,256]{2,1,0:T(8,128)S(1)}...) custom-call(bf16[2,256,4096]{2,1,0:T(8,128)(2,1)} %refs_0_.5, ...), custom_call_target="tpu_custom_call", output_to_operand_aliasing={{0}: (10, {}), {1}: (11, {}), {2}: (12, {}), {3}: (13, {}),... | custom-call | flops 1 | bytes 1 | tf_op jit(solution)/shard_map/early/pallas_call | solution.py:597
  40.6 0.0 collective-permute-done.5.refs_7_
  40.6 1.1 %pick_states.3 = (bf16[2,544,128]{2,1,0:T(8,128)(2,1)S(1)}, bf16[2,544,128]{2,1,0:T(8,128)(2,1)S(1)}, bf16[2,544,128]{2,1,0:T(8,128)(2,1)S(1)}, bf16[2,544,128]{2,1,0:T(8,128)(2,1)S(1)}) custom-call(s32[8]{0:T(128)S(1)} %broadcast_xor_fusion.refs_10_.refs_0_, bf16[1056,128]{1,0:T(8,128)(2,1)S(1)} %get-tuple-element.40.refs_9_.refs_1_, ...), custom_call_target="tpu_custom_call" | custom-call | flops 1 | bytes 1 | tf_op jit(solution)/shard_map/pick_states/pallas_call | solution.py:564
  41.7 0.6 collective-permute-start.6
  42.3 0.7 collective-permute-start.7
  42.9 2.3 %collective-permute-start.8 = (bf16[2,544,128]{2,1,0:T(8,128)(2,1)S(1)}, bf16[2,544,128]{2,1,0:T(8,128)(2,1)S(1)}, u32[]{:S(2)}, u32[]{:S(2)}) collective-permute-start(bf16[2,544,128]{2,1,0:T(8,128)(2,1)S(1)} %get-tuple-element.56), channel_id=1, source_target_pairs={{0,6},{2,4},{4,2},{6,0},{8,14},{10,12},{12,10},{14,8},{1,7},{3,5},... | collective-permute-start | bytes 835592 | tf_op jit(solution)/shard_map/ppermute | solution.py:499
  45.2 1.7 %collective-permute-done.9.refs_6_.refs_5_ = bf16[4,256,128]{2,1,0:T(8,128)(2,1)S(1)} collective-permute-done((bf16[4,256,128]{2,1,0:T(8,128)(2,1)S(1)}, bf16[4,256,128]{2,1,0:T(8,128)(2,1)S(1)}, u32[]{:S(2)}, u32[]{:S(2)}) %collective-permute-start.9) | collective-permute-done | bytes 262176 | tf_op jit(solution)/shard_map/ppermute | solution.py:499
  46.9 0.1 collective-permute-start.13
  47.0 1.1 %pick_states.4 = (bf16[2,256,128]{2,1,0:T(8,128)(2,1)S(1)}, bf16[2,256,128]{2,1,0:T(8,128)(2,1)S(1)}, bf16[2,256,128]{2,1,0:T(8,128)(2,1)S(1)}, bf16[2,256,128]{2,1,0:T(8,128)(2,1)S(1)}) custom-call(s32[8]{0:T(128)S(1)} %broadcast_xor_fusion.refs_10_.refs_0_, bf16[1056,128]{1,0:T(8,128)(2,1)S(1)} %get-tuple-element.40.refs_9_.refs_1_, ...), custom_call_target="tpu_custom_call" | custom-call | flops 1 | bytes 1 | tf_op jit(solution)/shard_map/pick_states/pallas_call | solution.py:564
  48.1 3.1 %collective-permute-start.10 = (bf16[2,256,128]{2,1,0:T(8,128)(2,1)S(1)}, bf16[2,256,128]{2,1,0:T(8,128)(2,1)S(1)}, u32[]{:S(2)}, u32[]{:S(2)}) collective-permute-start(bf16[2,256,128]{2,1,0:T(8,128)(2,1)S(1)} %get-tuple-element.58), channel_id=1, source_target_pairs={{0,6},{2,4},{4,2},{6,0},{8,14},{10,12},{12,10},{14,8},{1,7},{3,5},... | collective-permute-start | bytes 393224 | tf_op jit(solution)/shard_map/ppermute | solution.py:499
  51.2 9.8 %collective-permute-done.13.refs_5_ = bf16[4,256,128]{2,1,0:T(8,128)(2,1)S(1)} collective-permute-done((bf16[4,256,128]{2,1,0:T(8,128)(2,1)S(1)}, bf16[4,256,128]{2,1,0:T(8,128)(2,1)S(1)}, u32[]{:S(2)}, u32[]{:S(2)}) %collective-permute-start.13) | collective-permute-done | bytes 262176 | tf_op jit(solution)/shard_map/ppermute | solution.py:499
  60.9 3.8 %collective-permute-start.11 = (bf16[2,256,128]{2,1,0:T(8,128)(2,1)S(1)}, bf16[2,256,128]{2,1,0:T(8,128)(2,1)S(1)}, u32[]{:S(2)}, u32[]{:S(2)}) collective-permute-start(bf16[2,256,128]{2,1,0:T(8,128)(2,1)S(1)} %get-tuple-element.59), channel_id=1, source_target_pairs={{0,4},{2,6},{4,0},{6,2},{8,12},{10,14},{12,8},{14,10},{1,5},{3,7},... | collective-permute-start | bytes 393224 | tf_op jit(solution)/shard_map/ppermute | solution.py:499
  64.7 1.2 %pick_states.5 = (bf16[2,256,128]{2,1,0:T(8,128)(2,1)S(1)}, bf16[2,256,128]{2,1,0:T(8,128)(2,1)S(1)}, bf16[2,256,128]{2,1,0:T(8,128)(2,1)S(1)}, bf16[2,256,128]{2,1,0:T(8,128)(2,1)S(1)}) custom-call(s32[8]{0:T(128)S(1)} %broadcast_xor_fusion.refs_10_.refs_0_, bf16[1056,128]{1,0:T(8,128)(2,1)S(1)} %get-tuple-element.40.refs_9_.refs_1_, ...), custom_call_target="tpu_custom_call" | custom-call | flops 1 | bytes 1 | tf_op jit(solution)/shard_map/pick_states/pallas_call | solution.py:564
  65.9 0.0 collective-permute-done.6.refs_2_.refs_6_
  65.9 0.6 collective-permute-start.12
  66.5 0.0 collective-permute-done.7.refs_3_.refs_7_
  66.5 1.0 %collective-permute-start.14 = (bf16[2,256,128]{2,1,0:T(8,128)(2,1)S(1)}, bf16[2,256,128]{2,1,0:T(8,128)(2,1)S(1)}, u32[]{:S(2)}, u32[]{:S(2)}) collective-permute-start(bf16[2,256,128]{2,1,0:T(8,128)(2,1)S(1)} %get-tuple-element.62), channel_id=1, source_target_pairs={{0,6},{2,4},{4,2},{6,0},{8,14},{10,12},{12,10},{14,8},{1,7},{3,5},... | collective-permute-start | bytes 393224 | tf_op jit(solution)/shard_map/ppermute | solution.py:499
  67.5 0.0 collective-permute-done.8.refs_4_.refs_8_
  67.5 2.0 %collective-permute-start.15 = (bf16[2,256,128]{2,1,0:T(8,128)(2,1)S(1)}, bf16[2,256,128]{2,1,0:T(8,128)(2,1)S(1)}, u32[]{:S(2)}, u32[]{:S(2)}) collective-permute-start(bf16[2,256,128]{2,1,0:T(8,128)(2,1)S(1)} %get-tuple-element.63), channel_id=1, source_target_pairs={{0,4},{2,6},{4,0},{6,2},{8,12},{10,14},{12,8},{14,10},{1,5},{3,7},... | collective-permute-start | bytes 393224 | tf_op jit(solution)/shard_map/ppermute | solution.py:499
  69.5 0.0 collective-permute-done.10.refs_6_
  69.5 0.5 collective-permute-start.16
  70.0 3.9 %late.2.refs_25_ = bf16[2,256,4096]{2,1,0:T(8,128)(2,1)} custom-call(s32[1]{0:T(128)} %bitcast.place_ref.refs_0_, bf16[2,544,128]{2,1,0:T(8,128)(2,1)S(1)} %get-tuple-element.53.refs_5_.refs_1_, bf16[2,544,128]{2,1,0:T(8,128)(2,1)S(1)} %collective-permute-done.6.refs_2_.refs_6_, bf16[2,544,128]{2,1,0:T(8,128)(2,1)S(1)} %collective-permute-done.7.refs_3_.refs_7_, ...), custom_call_target="tpu_custom_call" | custom-call | flops 1 | bytes 1 | tf_op jit(solution)/shard_map/late/pallas_call | solution.py:648
  74.0 0.8 collective-permute-done.12.refs_8_
  74.7 0.9 %collective-permute-done.15.refs_11_ = bf16[2,256,128]{2,1,0:T(8,128)(2,1)S(1)} collective-permute-done((bf16[2,256,128]{2,1,0:T(8,128)(2,1)S(1)}, bf16[2,256,128]{2,1,0:T(8,128)(2,1)S(1)}, u32[]{:S(2)}, u32[]{:S(2)}) %collective-permute-start.15) | collective-permute-done | bytes 131104 | tf_op jit(solution)/shard_map/ppermute | solution.py:499
  75.7 0.9 %collective-permute-done.16.refs_12_ = bf16[2,256,128]{2,1,0:T(8,128)(2,1)S(1)} collective-permute-done((bf16[2,256,128]{2,1,0:T(8,128)(2,1)S(1)}, bf16[2,256,128]{2,1,0:T(8,128)(2,1)S(1)}, u32[]{:S(2)}, u32[]{:S(2)}) %collective-permute-start.16) | collective-permute-done | bytes 131104 | tf_op jit(solution)/shard_map/ppermute | solution.py:499
  76.6 3.9 %late.3 = bf16[2,256,4096]{2,1,0:T(8,128)(2,1)} custom-call(s32[1]{0:T(128)} %bitcast.place_ref.refs_0_, bf16[2,544,128]{2,1,0:T(8,128)(2,1)S(1)} %get-tuple-element.53.refs_5_.refs_1_, bf16[2,544,128]{2,1,0:T(8,128)(2,1)S(1)} %collective-permute-done.6.refs_2_.refs_6_, ...), custom_call_target="tpu_custom_call", output_to_operand_aliasing={{}: (25, {})} | custom-call | flops 1 | bytes 1 | tf_op jit(solution)/shard_map/late/pallas_call | solution.py:648
  (18 shorter events, 0.1 us)
Async XLA Ops:
  0.0 9.3 %copy-start.3 = (s32[8]{0:T(128)S(1)}, s32[8]{0:T(128)}, u32[]{:S(2)}) copy-start(s32[8]{0:T(128)} %param.26) | copy-start | bytes 100
  0.0 9.4 %copy-start.4 = (s32[16]{0:T(128)S(1)}, s32[16]{0:T(128)}, u32[]{:S(2)}) copy-start(s32[16]{0:T(128)} %param.27) | copy-start | bytes 196
  0.0 9.7 %copy-start = (f32[64]{0:T(128)S(1)}, f32[64]{0:T(128)}, u32[]{:S(2)}) copy-start(f32[64]{0:T(128)} %param.18) | copy-start | bytes 772
  0.0 9.8 %copy-start.1 = (f32[64]{0:T(128)S(1)}, f32[64]{0:T(128)}, u32[]{:S(2)}) copy-start(f32[64]{0:T(128)} %param.19) | copy-start | bytes 772
  0.0 9.9 %copy-start.2 = (f32[64]{0:T(128)S(1)}, f32[64]{0:T(128)}, u32[]{:S(2)}) copy-start(f32[64]{0:T(128)} %param.20) | copy-start | bytes 772
  1.8 27.2 %collective-permute-start.1 = (bf16[1056,128]{1,0:T(8,128)(2,1)S(1)}, bf16[1056,128]{1,0:T(8,128)(2,1)S(1)}, u32[]{:S(2)}, u32[]{:S(2)}) collective-permute-start(bf16[1056,128]{1,0:T(8,128)(2,1)S(1)} %get-tuple-element.42), channel_id=1, source_target_pairs={{0,4},{2,6},{4,0},{6,2},{8,12},{10,14},{12,8},{14,10},{1,5},{3,7},... | collective-permute-start | bytes 811016 | tf_op jit(solution)/shard_map/ppermute | solution.py:499
  4.9 22.5 %collective-permute-start.3 = (bf16[2,544,128]{2,1,0:T(8,128)(2,1)S(1)}, bf16[2,544,128]{2,1,0:T(8,128)(2,1)S(1)}, u32[]{:S(2)}, u32[]{:S(2)}) collective-permute-start(bf16[2,544,128]{2,1,0:T(8,128)(2,1)S(1)} %get-tuple-element.44), channel_id=1, source_target_pairs={{0,8},{2,10},{4,12},{6,14},{8,0},{10,2},{12,4},{14,6},{1,9},{3,11}... | collective-permute-start | bytes 835592 | tf_op jit(solution)/shard_map/ppermute | solution.py:499
  7.5 19.9 %collective-permute-start.4 = (bf16[2,544,128]{2,1,0:T(8,128)(2,1)S(1)}, bf16[2,544,128]{2,1,0:T(8,128)(2,1)S(1)}, u32[]{:S(2)}, u32[]{:S(2)}) collective-permute-start(bf16[2,544,128]{2,1,0:T(8,128)(2,1)S(1)} %get-tuple-element.45), channel_id=1, source_target_pairs={{0,12},{2,14},{4,8},{6,10},{8,4},{10,6},{12,0},{14,2},{1,13},{3,15... | collective-permute-start | bytes 835592 | tf_op jit(solution)/shard_map/ppermute | solution.py:499
  7.5 13.5 %collective-permute-start = (bf16[2,1056,128]{2,1,0:T(8,128)(2,1)S(1)}, bf16[2,1056,128]{2,1,0:T(8,128)(2,1)S(1)}, u32[]{:S(2)}, u32[]{:S(2)}) collective-permute-start(bf16[2,1056,128]{2,1,0:T(8,128)(2,1)S(1)} %get-tuple-element.41), channel_id=1, source_target_pairs={{0,2},{2,0},{4,6},{6,4},{8,10},{10,8},{12,14},{14,12},{1,3},{3,1},... | collective-permute-start | bytes 1622024 | tf_op jit(solution)/shard_map/ppermute | solution.py:499
  21.0 11.3 %collective-permute-start.2 = (bf16[1056,128]{1,0:T(8,128)(2,1)S(1)}, bf16[1056,128]{1,0:T(8,128)(2,1)S(1)}, u32[]{:S(2)}, u32[]{:S(2)}) collective-permute-start(bf16[1056,128]{1,0:T(8,128)(2,1)S(1)} %stack_turn.1.refs_9_), channel_id=1, source_target_pairs={{0,4},{2,6},{4,0},{6,2},{8,12},{10,14},{12,8},{14,10},{1,5},{3,7},... | collective-permute-start | bytes 811016 | tf_op jit(solution)/shard_map/ppermute | solution.py:499
  27.4 13.1 %collective-permute-start.5 = (bf16[2,544,128]{2,1,0:T(8,128)(2,1)S(1)}, bf16[2,544,128]{2,1,0:T(8,128)(2,1)S(1)}, u32[]{:S(2)}, u32[]{:S(2)}) collective-permute-start(bf16[2,544,128]{2,1,0:T(8,128)(2,1)S(1)} %stack_first.1.refs_5_), channel_id=1, source_target_pairs={{0,2},{2,0},{4,6},{6,4},{8,10},{10,8},{12,14},{14,12},{1,3},{3,1},... | collective-permute-start | bytes 835592 | tf_op jit(solution)/shard_map/ppermute | solution.py:499
  32.3 14.6 %collective-permute-start.9 = (bf16[4,256,128]{2,1,0:T(8,128)(2,1)S(1)}, bf16[4,256,128]{2,1,0:T(8,128)(2,1)S(1)}, u32[]{:S(2)}, u32[]{:S(2)}) collective-permute-start(bf16[4,256,128]{2,1,0:T(8,128)(2,1)S(1)} %stack_later.2.refs_9_), channel_id=1, source_target_pairs={{0,8},{2,10},{4,12},{6,14},{8,0},{10,2},{12,4},{14,6},{1,9},{3,11}... | collective-permute-start | bytes 786440 | tf_op jit(solution)/shard_map/ppermute | solution.py:499
  41.7 24.2 %collective-permute-start.6 = (bf16[2,544,128]{2,1,0:T(8,128)(2,1)S(1)}, bf16[2,544,128]{2,1,0:T(8,128)(2,1)S(1)}, u32[]{:S(2)}, u32[]{:S(2)}) collective-permute-start(bf16[2,544,128]{2,1,0:T(8,128)(2,1)S(1)} %get-tuple-element.54), channel_id=1, source_target_pairs={{0,2},{2,0},{4,6},{6,4},{8,10},{10,8},{12,14},{14,12},{1,3},{3,1},... | collective-permute-start | bytes 835592 | tf_op jit(solution)/shard_map/ppermute | solution.py:499
  42.3 24.3 %collective-permute-start.7 = (bf16[2,544,128]{2,1,0:T(8,128)(2,1)S(1)}, bf16[2,544,128]{2,1,0:T(8,128)(2,1)S(1)}, u32[]{:S(2)}, u32[]{:S(2)}) collective-permute-start(bf16[2,544,128]{2,1,0:T(8,128)(2,1)S(1)} %get-tuple-element.55), channel_id=1, source_target_pairs={{0,4},{2,6},{4,0},{6,2},{8,12},{10,14},{12,8},{14,10},{1,5},{3,7},... | collective-permute-start | bytes 835592 | tf_op jit(solution)/shard_map/ppermute | solution.py:499
  42.9 24.5 %collective-permute-start.8 = (bf16[2,544,128]{2,1,0:T(8,128)(2,1)S(1)}, bf16[2,544,128]{2,1,0:T(8,128)(2,1)S(1)}, u32[]{:S(2)}, u32[]{:S(2)}) collective-permute-start(bf16[2,544,128]{2,1,0:T(8,128)(2,1)S(1)} %get-tuple-element.56), channel_id=1, source_target_pairs={{0,6},{2,4},{4,2},{6,0},{8,14},{10,12},{12,10},{14,8},{1,7},{3,5},... | collective-permute-start | bytes 835592 | tf_op jit(solution)/shard_map/ppermute | solution.py:499
  46.9 14.0 %collective-permute-start.13 = (bf16[4,256,128]{2,1,0:T(8,128)(2,1)S(1)}, bf16[4,256,128]{2,1,0:T(8,128)(2,1)S(1)}, u32[]{:S(2)}, u32[]{:S(2)}) collective-permute-start(bf16[4,256,128]{2,1,0:T(8,128)(2,1)S(1)} %stack_later.3.refs_6_), channel_id=1, source_target_pairs={{0,8},{2,10},{4,12},{6,14},{8,0},{10,2},{12,4},{14,6},{1,9},{3,11}... | collective-permute-start | bytes 786440 | tf_op jit(solution)/shard_map/ppermute | solution.py:499
  48.1 21.4 %collective-permute-start.10 = (bf16[2,256,128]{2,1,0:T(8,128)(2,1)S(1)}, bf16[2,256,128]{2,1,0:T(8,128)(2,1)S(1)}, u32[]{:S(2)}, u32[]{:S(2)}) collective-permute-start(bf16[2,256,128]{2,1,0:T(8,128)(2,1)S(1)} %get-tuple-element.58), channel_id=1, source_target_pairs={{0,6},{2,4},{4,2},{6,0},{8,14},{10,12},{12,10},{14,8},{1,7},{3,5},... | collective-permute-start | bytes 393224 | tf_op jit(solution)/shard_map/ppermute | solution.py:499
  60.9 13.0 %collective-permute-start.11 = (bf16[2,256,128]{2,1,0:T(8,128)(2,1)S(1)}, bf16[2,256,128]{2,1,0:T(8,128)(2,1)S(1)}, u32[]{:S(2)}, u32[]{:S(2)}) collective-permute-start(bf16[2,256,128]{2,1,0:T(8,128)(2,1)S(1)} %get-tuple-element.59), channel_id=1, source_target_pairs={{0,4},{2,6},{4,0},{6,2},{8,12},{10,14},{12,8},{14,10},{1,5},{3,7},... | collective-permute-start | bytes 393224 | tf_op jit(solution)/shard_map/ppermute | solution.py:499
  65.9 8.8 %collective-permute-start.12 = (bf16[2,256,128]{2,1,0:T(8,128)(2,1)S(1)}, bf16[2,256,128]{2,1,0:T(8,128)(2,1)S(1)}, u32[]{:S(2)}, u32[]{:S(2)}) collective-permute-start(bf16[2,256,128]{2,1,0:T(8,128)(2,1)S(1)} %get-tuple-element.60), channel_id=1, source_target_pairs={{0,2},{2,0},{4,6},{6,4},{8,10},{10,8},{12,14},{14,12},{1,3},{3,1},... | collective-permute-start | bytes 393224 | tf_op jit(solution)/shard_map/ppermute | solution.py:499
  66.5 8.2 %collective-permute-start.14 = (bf16[2,256,128]{2,1,0:T(8,128)(2,1)S(1)}, bf16[2,256,128]{2,1,0:T(8,128)(2,1)S(1)}, u32[]{:S(2)}, u32[]{:S(2)}) collective-permute-start(bf16[2,256,128]{2,1,0:T(8,128)(2,1)S(1)} %get-tuple-element.62), channel_id=1, source_target_pairs={{0,6},{2,4},{4,2},{6,0},{8,14},{10,12},{12,10},{14,8},{1,7},{3,5},... | collective-permute-start | bytes 393224 | tf_op jit(solution)/shard_map/ppermute | solution.py:499
  67.5 8.2 %collective-permute-start.15 = (bf16[2,256,128]{2,1,0:T(8,128)(2,1)S(1)}, bf16[2,256,128]{2,1,0:T(8,128)(2,1)S(1)}, u32[]{:S(2)}, u32[]{:S(2)}) collective-permute-start(bf16[2,256,128]{2,1,0:T(8,128)(2,1)S(1)} %get-tuple-element.63), channel_id=1, source_target_pairs={{0,4},{2,6},{4,0},{6,2},{8,12},{10,14},{12,8},{14,10},{1,5},{3,7},... | collective-permute-start | bytes 393224 | tf_op jit(solution)/shard_map/ppermute | solution.py:499
  69.5 7.1 %collective-permute-start.16 = (bf16[2,256,128]{2,1,0:T(8,128)(2,1)S(1)}, bf16[2,256,128]{2,1,0:T(8,128)(2,1)S(1)}, u32[]{:S(2)}, u32[]{:S(2)}) collective-permute-start(bf16[2,256,128]{2,1,0:T(8,128)(2,1)S(1)} %get-tuple-element.64), channel_id=1, source_target_pairs={{0,2},{2,0},{4,6},{6,4},{8,10},{10,8},{12,14},{14,12},{1,3},{3,1},... | collective-permute-start | bytes 393224 | tf_op jit(solution)/shard_map/ppermute | solution.py:499

commit v27 on v22

--- a/solution.py
+++ b/solution.py
@@ -576,7 +576,7 @@
             name=name,
         )(scalars, *map(keep_in_vmem, sources), *tokens)
 
-    def pick(rows, sources, choices, tokens, order=(1, 2, 3)):
+    def pick(rows, sources, choices, tokens, order=(1, 3, 2)):
         moves = [
             (j, kid, j * kids + kid, choices) for j in range(4) for kid in range(kids)
         ]

time: 79.5 us -> 79.2 us (level)
  waiting for transfers between devices: 18.8 us -> 15.2 us
  starting transfers between devices: 25 us -> 28.4 us
    ppermute x17, waiting for transfers between devices: 18.8 us -> 15.2 us  [swap(): return lax.ppermute(value, 'batch', perm=[(i, i ^ r) for i in range(8)])]
    ppermute x17, starting transfers between devices: 25 us -> 28.4 us  [swap(): return lax.ppermute(value, 'batch', perm=[(i, i ^ r) for i in range(8)])]
where the time goes in v27:
time: 79.2 us; the launch traced here: 79 us
  Pallas kernels  34.3 us (43%)
  starting transfers between devices  28.4 us (36%)
  waiting for transfers between devices  15.2 us (19%)
    ppermute x17, starting transfers between devices, swap(): return lax.ppermute(value, 'batch', perm=[(i, i ^ r) for i in range(8)])  28.4 us
    pallas_call x3, Pallas kernels, early(): pl.pallas_call(functools.partial(drop_tokens, functools.partial(early_ker...  20.4 us
    ppermute x17, waiting for transfers between devices, swap(): return lax.ppermute(value, 'batch', perm=[(i, i ^ r) for i in range(8)])  15.2 us
    pallas_call x2, Pallas kernels, late(): pl.pallas_call(functools.partial(drop_tokens, kernel, keep, 1 + len(opera...  8.66 us
    pallas_call x7, Pallas kernels, rearrange(): pl.pallas_call(functools.partial(drop_tokens, kernel, 1 + len(sources), l...  3.45 us
    pallas_call x1, Pallas kernels, cast(): pl.pallas_call(kernel, grid_spec=pltpu.PrefetchScalarGridSpec(num_scalar_...  1.82 us
  transfers between devices with their start and end apart: 17, of which 8 were waited for; matrix products, arithmetic and copies ran while one was open for 1% of the time, Pallas kernels for 37%

profile of v27, /device:TPU:0, one launch (start us, length us, event | category | flops | bytes accessed | tf_op | source)
XLA Modules:
  0.0 79.0 jit_solution(6299615406191324353)
XLA Ops:
  0.0 1.8 %cast_states.1 = (bf16[1056,128]{1,0:T(8,128)(2,1)S(1)}, bf16[1056,128]{1,0:T(8,128)(2,1)S(1)}, bf16[2,1056,128]{2,1,0:T(8,128)(2,1)S(1)}, bf16[2,544,128]{2,1,0:T(8,128)(2,1)S(1)}, bf16[2,544,128]{2,1,0:T(8,128)(2,1)S(1)}) custom-call(s32[1]{0:T(128)} %bitcast.place_ref.refs_0_, f32[4,16,64,128]{3,2,1,0:T(8,128)} %bitcast.5, f32[4,16,64,128]{3,2,1,0:T(8,128)} %bitcast.6, ...), custom_call_target="tpu_custom_call" | custom-call | flops 1 | bytes 1 | tf_op jit(solution)/shard_map/cast_states/pallas_call | solution.py:532
  1.8 3.1 %collective-permute-start.1 = (bf16[1056,128]{1,0:T(8,128)(2,1)S(1)}, bf16[1056,128]{1,0:T(8,128)(2,1)S(1)}, u32[]{:S(2)}, u32[]{:S(2)}) collective-permute-start(bf16[1056,128]{1,0:T(8,128)(2,1)S(1)} %get-tuple-element.42), channel_id=1, source_target_pairs={{0,4},{2,6},{4,0},{6,2},{8,12},{10,14},{12,8},{14,10},{1,5},{3,7},... | collective-permute-start | bytes 811016 | tf_op jit(solution)/shard_map/ppermute | solution.py:499
  4.9 2.6 %collective-permute-start.3 = (bf16[2,544,128]{2,1,0:T(8,128)(2,1)S(1)}, bf16[2,544,128]{2,1,0:T(8,128)(2,1)S(1)}, u32[]{:S(2)}, u32[]{:S(2)}) collective-permute-start(bf16[2,544,128]{2,1,0:T(8,128)(2,1)S(1)} %get-tuple-element.44), channel_id=1, source_target_pairs={{0,8},{2,10},{4,12},{6,14},{8,0},{10,2},{12,4},{14,6},{1,9},{3,11}... | collective-permute-start | bytes 835592 | tf_op jit(solution)/shard_map/ppermute | solution.py:499
  7.5 0.0 collective-permute-start.4
  7.5 1.7 %collective-permute-start = (bf16[2,1056,128]{2,1,0:T(8,128)(2,1)S(1)}, bf16[2,1056,128]{2,1,0:T(8,128)(2,1)S(1)}, u32[]{:S(2)}, u32[]{:S(2)}) collective-permute-start(bf16[2,1056,128]{2,1,0:T(8,128)(2,1)S(1)} %get-tuple-element.41), channel_id=1, source_target_pairs={{0,2},{2,0},{4,6},{6,4},{8,10},{10,8},{12,14},{14,12},{1,3},{3,1},... | collective-permute-start | bytes 1622024 | tf_op jit(solution)/shard_map/ppermute | solution.py:499
  9.3 0.1 select_reduce_fusion.1
  9.4 0.1 convert_reduce_fusion
  9.5 0.2 select_reduce_fusion
  9.7 0.1 copy.28.refs_4_
  9.8 0.1 copy.29.refs_5_
  9.9 0.1 broadcast_in_dim.55
  10.0 0.1 broadcast_in_dim_reshape.3.refs_6_
  10.1 9.6 %early.3 = (f32[4,256,1024]{2,1,0:T(8,128)S(1)}, bf16[4,256,128]{2,1,0:T(8,128)(2,1)S(1)}, f32[4,16,256]{2,1,0:T(8,128)S(1)}, f32[4,256,256]{2,1,0:T(8,128)S(1)}...) custom-call(bf16[2,256,4096]{2,1,0:T(8,128)(2,1)} %refs_0_.5, bf16[2,256,512]{2,1,0:T(8,128)(2,1)} %refs_1_.5, ...), custom_call_target="tpu_custom_call" | custom-call | flops 1 | bytes 1 | tf_op jit(solution)/shard_map/early/pallas_call | solution.py:597
  19.7 1.3 %collective-permute-done.refs_1_.refs_2_ = bf16[2,1056,128]{2,1,0:T(8,128)(2,1)S(1)} collective-permute-done((bf16[2,1056,128]{2,1,0:T(8,128)(2,1)S(1)}, bf16[2,1056,128]{2,1,0:T(8,128)(2,1)S(1)}, u32[]{:S(2)}, u32[]{:S(2)}) %collective-permute-start) | collective-permute-done | bytes 540704 | tf_op jit(solution)/shard_map/ppermute | solution.py:499
  21.0 0.7 collective-permute-start.2
  21.7 5.4 %early.4 = (f32[4,256,1024]{2,1,0:T(8,128)S(1)}, bf16[4,256,128]{2,1,0:T(8,128)(2,1)S(1)}, f32[4,16,256]{2,1,0:T(8,128)S(1)}, f32[4,256,256]{2,1,0:T(8,128)S(1)}...) custom-call(bf16[2,256,4096]{2,1,0:T(8,128)(2,1)} %refs_0_.5, bf16[2,256,512]{2,1,0:T(8,128)(2,1)} %refs_1_.5, ...), custom_call_target="tpu_custom_call" | custom-call | flops 1 | bytes 1 | tf_op jit(solution)/shard_map/early/pallas_call | solution.py:597
  27.1 0.3 collective-permute-done.3.refs_1_.refs_5_
  27.4 0.0 collective-permute-done.4.refs_2_.refs_6_
  27.4 1.6 %collective-permute-start.5 = (bf16[2,544,128]{2,1,0:T(8,128)(2,1)S(1)}, bf16[2,544,128]{2,1,0:T(8,128)(2,1)S(1)}, u32[]{:S(2)}, u32[]{:S(2)}) collective-permute-start(bf16[2,544,128]{2,1,0:T(8,128)(2,1)S(1)} %stack_first.1.refs_5_), channel_id=1, source_target_pairs={{0,2},{2,0},{4,6},{6,4},{8,10},{10,8},{12,14},{14,12},{1,3},{3,1},... | collective-permute-start | bytes 835592 | tf_op jit(solution)/shard_map/ppermute | solution.py:499
  29.0 0.0 collective-permute-done.1.refs_3_
  29.0 3.3 %collective-permute-done.2.refs_4_ = bf16[1056,128]{1,0:T(8,128)(2,1)S(1)} collective-permute-done((bf16[1056,128]{1,0:T(8,128)(2,1)S(1)}, bf16[1056,128]{1,0:T(8,128)(2,1)S(1)}, u32[]{:S(2)}, u32[]{:S(2)}) %collective-permute-start.2) | collective-permute-done | bytes 270368 | tf_op jit(solution)/shard_map/ppermute | solution.py:499
  32.3 2.9 %collective-permute-start.9 = (bf16[4,256,128]{2,1,0:T(8,128)(2,1)S(1)}, bf16[4,256,128]{2,1,0:T(8,128)(2,1)S(1)}, u32[]{:S(2)}, u32[]{:S(2)}) collective-permute-start(bf16[4,256,128]{2,1,0:T(8,128)(2,1)S(1)} %stack_later.2.refs_9_), channel_id=1, source_target_pairs={{0,8},{2,10},{4,12},{6,14},{8,0},{10,2},{12,4},{14,6},{1,9},{3,11}... | collective-permute-start | bytes 786440 | tf_op jit(solution)/shard_map/ppermute | solution.py:499
  35.2 5.4 %early.5 = (f32[4,256,1024]{2,1,0:T(8,128)S(1)}, bf16[4,256,128]{2,1,0:T(8,128)(2,1)S(1)}, f32[4,16,256]{2,1,0:T(8,128)S(1)}, f32[4,256,256]{2,1,0:T(8,128)S(1)}...) custom-call(bf16[2,256,4096]{2,1,0:T(8,128)(2,1)} %refs_0_.5, ...), custom_call_target="tpu_custom_call", output_to_operand_aliasing={{0}: (10, {}), {1}: (11, {}), {2}: (12, {}), {3}: (13, {}),... | custom-call | flops 1 | bytes 1 | tf_op jit(solution)/shard_map/early/pallas_call | solution.py:597
  40.6 0.0 collective-permute-done.5.refs_7_
  40.6 1.1 %pick_states.3 = (bf16[2,544,128]{2,1,0:T(8,128)(2,1)S(1)}, bf16[2,544,128]{2,1,0:T(8,128)(2,1)S(1)}, bf16[2,544,128]{2,1,0:T(8,128)(2,1)S(1)}, bf16[2,544,128]{2,1,0:T(8,128)(2,1)S(1)}) custom-call(s32[8]{0:T(128)S(1)} %broadcast_xor_fusion.refs_10_.refs_0_, bf16[1056,128]{1,0:T(8,128)(2,1)S(1)} %get-tuple-element.40.refs_9_.refs_1_, ...), custom_call_target="tpu_custom_call" | custom-call | flops 1 | bytes 1 | tf_op jit(solution)/shard_map/pick_states/pallas_call | solution.py:564
  41.7 0.6 collective-permute-start.6
  42.3 0.6 collective-permute-start.7
  42.9 2.3 %collective-permute-start.8 = (bf16[2,544,128]{2,1,0:T(8,128)(2,1)S(1)}, bf16[2,544,128]{2,1,0:T(8,128)(2,1)S(1)}, u32[]{:S(2)}, u32[]{:S(2)}) collective-permute-start(bf16[2,544,128]{2,1,0:T(8,128)(2,1)S(1)} %get-tuple-element.56), channel_id=1, source_target_pairs={{0,4},{2,6},{4,0},{6,2},{8,12},{10,14},{12,8},{14,10},{1,5},{3,7},... | collective-permute-start | bytes 835592 | tf_op jit(solution)/shard_map/ppermute | solution.py:499
  45.2 1.7 %collective-permute-done.9.refs_6_.refs_5_ = bf16[4,256,128]{2,1,0:T(8,128)(2,1)S(1)} collective-permute-done((bf16[4,256,128]{2,1,0:T(8,128)(2,1)S(1)}, bf16[4,256,128]{2,1,0:T(8,128)(2,1)S(1)}, u32[]{:S(2)}, u32[]{:S(2)}) %collective-permute-start.9) | collective-permute-done | bytes 262176 | tf_op jit(solution)/shard_map/ppermute | solution.py:499
  46.9 0.1 collective-permute-start.10
  47.0 1.1 %pick_states.4 = (bf16[2,256,128]{2,1,0:T(8,128)(2,1)S(1)}, bf16[2,256,128]{2,1,0:T(8,128)(2,1)S(1)}, bf16[2,256,128]{2,1,0:T(8,128)(2,1)S(1)}, bf16[2,256,128]{2,1,0:T(8,128)(2,1)S(1)}) custom-call(s32[8]{0:T(128)S(1)} %broadcast_xor_fusion.refs_10_.refs_0_, bf16[1056,128]{1,0:T(8,128)(2,1)S(1)} %get-tuple-element.40.refs_9_.refs_1_, ...), custom_call_target="tpu_custom_call" | custom-call | flops 1 | bytes 1 | tf_op jit(solution)/shard_map/pick_states/pallas_call | solution.py:564
  48.1 3.1 %collective-permute-start.14 = (bf16[2,256,128]{2,1,0:T(8,128)(2,1)S(1)}, bf16[2,256,128]{2,1,0:T(8,128)(2,1)S(1)}, u32[]{:S(2)}, u32[]{:S(2)}) collective-permute-start(bf16[2,256,128]{2,1,0:T(8,128)(2,1)S(1)} %get-tuple-element.72), channel_id=1, source_target_pairs={{0,6},{2,4},{4,2},{6,0},{8,14},{10,12},{12,10},{14,8},{1,7},{3,5},... | collective-permute-start | bytes 393224 | tf_op jit(solution)/shard_map/ppermute | solution.py:499
  51.1 1.0 %collective-permute-done.6.refs_2_.refs_6_ = bf16[2,544,128]{2,1,0:T(8,128)(2,1)S(1)} collective-permute-done((bf16[2,544,128]{2,1,0:T(8,128)(2,1)S(1)}, bf16[2,544,128]{2,1,0:T(8,128)(2,1)S(1)}, u32[]{:S(2)}, u32[]{:S(2)}) %collective-permute-start.6) | collective-permute-done | bytes 278560 | tf_op jit(solution)/shard_map/ppermute | solution.py:499
  52.1 3.0 %collective-permute-start.15 = (bf16[2,256,128]{2,1,0:T(8,128)(2,1)S(1)}, bf16[2,256,128]{2,1,0:T(8,128)(2,1)S(1)}, u32[]{:S(2)}, u32[]{:S(2)}) collective-permute-start(bf16[2,256,128]{2,1,0:T(8,128)(2,1)S(1)} %get-tuple-element.73), channel_id=1, source_target_pairs={{0,4},{2,6},{4,0},{6,2},{8,12},{10,14},{12,8},{14,10},{1,5},{3,7},... | collective-permute-start | bytes 393224 | tf_op jit(solution)/shard_map/ppermute | solution.py:499
  55.1 6.5 %collective-permute-done.10.refs_5_ = bf16[4,256,128]{2,1,0:T(8,128)(2,1)S(1)} collective-permute-done((bf16[4,256,128]{2,1,0:T(8,128)(2,1)S(1)}, bf16[4,256,128]{2,1,0:T(8,128)(2,1)S(1)}, u32[]{:S(2)}, u32[]{:S(2)}) %collective-permute-start.10) | collective-permute-done | bytes 262176 | tf_op jit(solution)/shard_map/ppermute | solution.py:499
  61.6 1.5 %collective-permute-start.16 = (bf16[2,256,128]{2,1,0:T(8,128)(2,1)S(1)}, bf16[2,256,128]{2,1,0:T(8,128)(2,1)S(1)}, u32[]{:S(2)}, u32[]{:S(2)}) collective-permute-start(bf16[2,256,128]{2,1,0:T(8,128)(2,1)S(1)} %get-tuple-element.74), channel_id=1, source_target_pairs={{0,2},{2,0},{4,6},{6,4},{8,10},{10,8},{12,14},{14,12},{1,3},{3,1},... | collective-permute-start | bytes 393224 | tf_op jit(solution)/shard_map/ppermute | solution.py:499
  63.1 1.2 %pick_states.5 = (bf16[2,256,128]{2,1,0:T(8,128)(2,1)S(1)}, bf16[2,256,128]{2,1,0:T(8,128)(2,1)S(1)}, bf16[2,256,128]{2,1,0:T(8,128)(2,1)S(1)}, bf16[2,256,128]{2,1,0:T(8,128)(2,1)S(1)}) custom-call(s32[8]{0:T(128)S(1)} %broadcast_xor_fusion.refs_10_.refs_0_, bf16[1056,128]{1,0:T(8,128)(2,1)S(1)} %get-tuple-element.40.refs_9_.refs_1_, ...), custom_call_target="tpu_custom_call" | custom-call | flops 1 | bytes 1 | tf_op jit(solution)/shard_map/pick_states/pallas_call | solution.py:564
  64.3 0.0 collective-permute-done.7.refs_3_.refs_7_
  64.4 3.1 %collective-permute-start.11 = (bf16[2,256,128]{2,1,0:T(8,128)(2,1)S(1)}, bf16[2,256,128]{2,1,0:T(8,128)(2,1)S(1)}, u32[]{:S(2)}, u32[]{:S(2)}) collective-permute-start(bf16[2,256,128]{2,1,0:T(8,128)(2,1)S(1)} %get-tuple-element.59), channel_id=1, source_target_pairs={{0,6},{2,4},{4,2},{6,0},{8,14},{10,12},{12,10},{14,8},{1,7},{3,5},... | collective-permute-start | bytes 393224 | tf_op jit(solution)/shard_map/ppermute | solution.py:499
  67.4 0.0 collective-permute-done.8.refs_4_.refs_8_
  67.4 0.1 collective-permute-start.12
  67.6 0.1 collective-permute-done.14.refs_10_
  67.6 1.4 %collective-permute-start.13 = (bf16[2,256,128]{2,1,0:T(8,128)(2,1)S(1)}, bf16[2,256,128]{2,1,0:T(8,128)(2,1)S(1)}, u32[]{:S(2)}, u32[]{:S(2)}) collective-permute-start(bf16[2,256,128]{2,1,0:T(8,128)(2,1)S(1)} %get-tuple-element.61), channel_id=1, source_target_pairs={{0,2},{2,0},{4,6},{6,4},{8,10},{10,8},{12,14},{14,12},{1,3},{3,1},... | collective-permute-start | bytes 393224 | tf_op jit(solution)/shard_map/ppermute | solution.py:499
  69.0 1.1 %collective-permute-done.15.refs_11_ = bf16[2,256,128]{2,1,0:T(8,128)(2,1)S(1)} collective-permute-done((bf16[2,256,128]{2,1,0:T(8,128)(2,1)S(1)}, bf16[2,256,128]{2,1,0:T(8,128)(2,1)S(1)}, u32[]{:S(2)}, u32[]{:S(2)}) %collective-permute-start.15) | collective-permute-done | bytes 131104 | tf_op jit(solution)/shard_map/ppermute | solution.py:499
  70.2 5.7 %late.2.refs_21_ = bf16[2,256,4096]{2,1,0:T(8,128)(2,1)} custom-call(s32[1]{0:T(128)} %bitcast.place_ref.refs_0_, bf16[2,544,128]{2,1,0:T(8,128)(2,1)S(1)} %get-tuple-element.53.refs_5_.refs_1_, bf16[2,544,128]{2,1,0:T(8,128)(2,1)S(1)} %collective-permute-done.6.refs_2_.refs_6_, bf16[2,544,128]{2,1,0:T(8,128)(2,1)S(1)} %collective-permute-done.7.refs_3_.refs_7_, ...), custom_call_target="tpu_custom_call" | custom-call | flops 1 | bytes 1 | tf_op jit(solution)/shard_map/late/pallas_call | solution.py:648
  75.9 0.0 collective-permute-done.12.refs_7_
  75.9 0.0 collective-permute-done.13.refs_8_
  75.9 2.9 %late.3 = bf16[2,256,4096]{2,1,0:T(8,128)(2,1)} custom-call(s32[1]{0:T(128)} %bitcast.place_ref.refs_0_, bf16[2,544,128]{2,1,0:T(8,128)(2,1)S(1)} %get-tuple-element.53.refs_5_.refs_1_, bf16[2,544,128]{2,1,0:T(8,128)(2,1)S(1)} %collective-permute-done.6.refs_2_.refs_6_, ...), custom_call_target="tpu_custom_call", output_to_operand_aliasing={{}: (21, {})} | custom-call | flops 1 | bytes 1 | tf_op jit(solution)/shard_map/late/pallas_call | solution.py:648
  (18 shorter events, 0.1 us)
Async XLA Ops:
  0.0 9.3 %copy-start.3 = (s32[8]{0:T(128)S(1)}, s32[8]{0:T(128)}, u32[]{:S(2)}) copy-start(s32[8]{0:T(128)} %param.26) | copy-start | bytes 100
  0.0 9.4 %copy-start.4 = (s32[16]{0:T(128)S(1)}, s32[16]{0:T(128)}, u32[]{:S(2)}) copy-start(s32[16]{0:T(128)} %param.27) | copy-start | bytes 196
  0.0 9.7 %copy-start = (f32[64]{0:T(128)S(1)}, f32[64]{0:T(128)}, u32[]{:S(2)}) copy-start(f32[64]{0:T(128)} %param.18) | copy-start | bytes 772
  0.0 9.8 %copy-start.1 = (f32[64]{0:T(128)S(1)}, f32[64]{0:T(128)}, u32[]{:S(2)}) copy-start(f32[64]{0:T(128)} %param.19) | copy-start | bytes 772
  0.0 9.9 %copy-start.2 = (f32[64]{0:T(128)S(1)}, f32[64]{0:T(128)}, u32[]{:S(2)}) copy-start(f32[64]{0:T(128)} %param.20) | copy-start | bytes 772
  1.8 27.2 %collective-permute-start.1 = (bf16[1056,128]{1,0:T(8,128)(2,1)S(1)}, bf16[1056,128]{1,0:T(8,128)(2,1)S(1)}, u32[]{:S(2)}, u32[]{:S(2)}) collective-permute-start(bf16[1056,128]{1,0:T(8,128)(2,1)S(1)} %get-tuple-element.42), channel_id=1, source_target_pairs={{0,4},{2,6},{4,0},{6,2},{8,12},{10,14},{12,8},{14,10},{1,5},{3,7},... | collective-permute-start | bytes 811016 | tf_op jit(solution)/shard_map/ppermute | solution.py:499
  4.9 22.5 %collective-permute-start.3 = (bf16[2,544,128]{2,1,0:T(8,128)(2,1)S(1)}, bf16[2,544,128]{2,1,0:T(8,128)(2,1)S(1)}, u32[]{:S(2)}, u32[]{:S(2)}) collective-permute-start(bf16[2,544,128]{2,1,0:T(8,128)(2,1)S(1)} %get-tuple-element.44), channel_id=1, source_target_pairs={{0,8},{2,10},{4,12},{6,14},{8,0},{10,2},{12,4},{14,6},{1,9},{3,11}... | collective-permute-start | bytes 835592 | tf_op jit(solution)/shard_map/ppermute | solution.py:499
  7.5 19.9 %collective-permute-start.4 = (bf16[2,544,128]{2,1,0:T(8,128)(2,1)S(1)}, bf16[2,544,128]{2,1,0:T(8,128)(2,1)S(1)}, u32[]{:S(2)}, u32[]{:S(2)}) collective-permute-start(bf16[2,544,128]{2,1,0:T(8,128)(2,1)S(1)} %get-tuple-element.45), channel_id=1, source_target_pairs={{0,12},{2,14},{4,8},{6,10},{8,4},{10,6},{12,0},{14,2},{1,13},{3,15... | collective-permute-start | bytes 835592 | tf_op jit(solution)/shard_map/ppermute | solution.py:499
  7.5 13.5 %collective-permute-start = (bf16[2,1056,128]{2,1,0:T(8,128)(2,1)S(1)}, bf16[2,1056,128]{2,1,0:T(8,128)(2,1)S(1)}, u32[]{:S(2)}, u32[]{:S(2)}) collective-permute-start(bf16[2,1056,128]{2,1,0:T(8,128)(2,1)S(1)} %get-tuple-element.41), channel_id=1, source_target_pairs={{0,2},{2,0},{4,6},{6,4},{8,10},{10,8},{12,14},{14,12},{1,3},{3,1},... | collective-permute-start | bytes 1622024 | tf_op jit(solution)/shard_map/ppermute | solution.py:499
  21.0 11.3 %collective-permute-start.2 = (bf16[1056,128]{1,0:T(8,128)(2,1)S(1)}, bf16[1056,128]{1,0:T(8,128)(2,1)S(1)}, u32[]{:S(2)}, u32[]{:S(2)}) collective-permute-start(bf16[1056,128]{1,0:T(8,128)(2,1)S(1)} %stack_turn.1.refs_9_), channel_id=1, source_target_pairs={{0,4},{2,6},{4,0},{6,2},{8,12},{10,14},{12,8},{14,10},{1,5},{3,7},... | collective-permute-start | bytes 811016 | tf_op jit(solution)/shard_map/ppermute | solution.py:499
  27.4 13.1 %collective-permute-start.5 = (bf16[2,544,128]{2,1,0:T(8,128)(2,1)S(1)}, bf16[2,544,128]{2,1,0:T(8,128)(2,1)S(1)}, u32[]{:S(2)}, u32[]{:S(2)}) collective-permute-start(bf16[2,544,128]{2,1,0:T(8,128)(2,1)S(1)} %stack_first.1.refs_5_), channel_id=1, source_target_pairs={{0,2},{2,0},{4,6},{6,4},{8,10},{10,8},{12,14},{14,12},{1,3},{3,1},... | collective-permute-start | bytes 835592 | tf_op jit(solution)/shard_map/ppermute | solution.py:499
  32.3 14.6 %collective-permute-start.9 = (bf16[4,256,128]{2,1,0:T(8,128)(2,1)S(1)}, bf16[4,256,128]{2,1,0:T(8,128)(2,1)S(1)}, u32[]{:S(2)}, u32[]{:S(2)}) collective-permute-start(bf16[4,256,128]{2,1,0:T(8,128)(2,1)S(1)} %stack_later.2.refs_9_), channel_id=1, source_target_pairs={{0,8},{2,10},{4,12},{6,14},{8,0},{10,2},{12,4},{14,6},{1,9},{3,11}... | collective-permute-start | bytes 786440 | tf_op jit(solution)/shard_map/ppermute | solution.py:499
  41.7 10.5 %collective-permute-start.6 = (bf16[2,544,128]{2,1,0:T(8,128)(2,1)S(1)}, bf16[2,544,128]{2,1,0:T(8,128)(2,1)S(1)}, u32[]{:S(2)}, u32[]{:S(2)}) collective-permute-start(bf16[2,544,128]{2,1,0:T(8,128)(2,1)S(1)} %get-tuple-element.54), channel_id=1, source_target_pairs={{0,2},{2,0},{4,6},{6,4},{8,10},{10,8},{12,14},{14,12},{1,3},{3,1},... | collective-permute-start | bytes 835592 | tf_op jit(solution)/shard_map/ppermute | solution.py:499
  42.3 22.1 %collective-permute-start.7 = (bf16[2,544,128]{2,1,0:T(8,128)(2,1)S(1)}, bf16[2,544,128]{2,1,0:T(8,128)(2,1)S(1)}, u32[]{:S(2)}, u32[]{:S(2)}) collective-permute-start(bf16[2,544,128]{2,1,0:T(8,128)(2,1)S(1)} %get-tuple-element.55), channel_id=1, source_target_pairs={{0,6},{2,4},{4,2},{6,0},{8,14},{10,12},{12,10},{14,8},{1,7},{3,5},... | collective-permute-start | bytes 835592 | tf_op jit(solution)/shard_map/ppermute | solution.py:499
  42.9 24.5 %collective-permute-start.8 = (bf16[2,544,128]{2,1,0:T(8,128)(2,1)S(1)}, bf16[2,544,128]{2,1,0:T(8,128)(2,1)S(1)}, u32[]{:S(2)}, u32[]{:S(2)}) collective-permute-start(bf16[2,544,128]{2,1,0:T(8,128)(2,1)S(1)} %get-tuple-element.56), channel_id=1, source_target_pairs={{0,4},{2,6},{4,0},{6,2},{8,12},{10,14},{12,8},{14,10},{1,5},{3,7},... | collective-permute-start | bytes 835592 | tf_op jit(solution)/shard_map/ppermute | solution.py:499
  46.9 14.7 %collective-permute-start.10 = (bf16[4,256,128]{2,1,0:T(8,128)(2,1)S(1)}, bf16[4,256,128]{2,1,0:T(8,128)(2,1)S(1)}, u32[]{:S(2)}, u32[]{:S(2)}) collective-permute-start(bf16[4,256,128]{2,1,0:T(8,128)(2,1)S(1)} %stack_later.3.refs_6_), channel_id=1, source_target_pairs={{0,8},{2,10},{4,12},{6,14},{8,0},{10,2},{12,4},{14,6},{1,9},{3,11}... | collective-permute-start | bytes 786440 | tf_op jit(solution)/shard_map/ppermute | solution.py:499
  48.1 19.6 %collective-permute-start.14 = (bf16[2,256,128]{2,1,0:T(8,128)(2,1)S(1)}, bf16[2,256,128]{2,1,0:T(8,128)(2,1)S(1)}, u32[]{:S(2)}, u32[]{:S(2)}) collective-permute-start(bf16[2,256,128]{2,1,0:T(8,128)(2,1)S(1)} %get-tuple-element.72), channel_id=1, source_target_pairs={{0,6},{2,4},{4,2},{6,0},{8,14},{10,12},{12,10},{14,8},{1,7},{3,5},... | collective-permute-start | bytes 393224 | tf_op jit(solution)/shard_map/ppermute | solution.py:499
  52.1 18.0 %collective-permute-start.15 = (bf16[2,256,128]{2,1,0:T(8,128)(2,1)S(1)}, bf16[2,256,128]{2,1,0:T(8,128)(2,1)S(1)}, u32[]{:S(2)}, u32[]{:S(2)}) collective-permute-start(bf16[2,256,128]{2,1,0:T(8,128)(2,1)S(1)} %get-tuple-element.73), channel_id=1, source_target_pairs={{0,4},{2,6},{4,0},{6,2},{8,12},{10,14},{12,8},{14,10},{1,5},{3,7},... | collective-permute-start | bytes 393224 | tf_op jit(solution)/shard_map/ppermute | solution.py:499
  61.6 8.6 %collective-permute-start.16 = (bf16[2,256,128]{2,1,0:T(8,128)(2,1)S(1)}, bf16[2,256,128]{2,1,0:T(8,128)(2,1)S(1)}, u32[]{:S(2)}, u32[]{:S(2)}) collective-permute-start(bf16[2,256,128]{2,1,0:T(8,128)(2,1)S(1)} %get-tuple-element.74), channel_id=1, source_target_pairs={{0,2},{2,0},{4,6},{6,4},{8,10},{10,8},{12,14},{14,12},{1,3},{3,1},... | collective-permute-start | bytes 393224 | tf_op jit(solution)/shard_map/ppermute | solution.py:499
  64.4 11.5 %collective-permute-start.11 = (bf16[2,256,128]{2,1,0:T(8,128)(2,1)S(1)}, bf16[2,256,128]{2,1,0:T(8,128)(2,1)S(1)}, u32[]{:S(2)}, u32[]{:S(2)}) collective-permute-start(bf16[2,256,128]{2,1,0:T(8,128)(2,1)S(1)} %get-tuple-element.59), channel_id=1, source_target_pairs={{0,6},{2,4},{4,2},{6,0},{8,14},{10,12},{12,10},{14,8},{1,7},{3,5},... | collective-permute-start | bytes 393224 | tf_op jit(solution)/shard_map/ppermute | solution.py:499
  67.4 8.5 %collective-permute-start.12 = (bf16[2,256,128]{2,1,0:T(8,128)(2,1)S(1)}, bf16[2,256,128]{2,1,0:T(8,128)(2,1)S(1)}, u32[]{:S(2)}, u32[]{:S(2)}) collective-permute-start(bf16[2,256,128]{2,1,0:T(8,128)(2,1)S(1)} %get-tuple-element.60), channel_id=1, source_target_pairs={{0,4},{2,6},{4,0},{6,2},{8,12},{10,14},{12,8},{14,10},{1,5},{3,7},... | collective-permute-start | bytes 393224 | tf_op jit(solution)/shard_map/ppermute | solution.py:499
  67.6 8.3 %collective-permute-start.13 = (bf16[2,256,128]{2,1,0:T(8,128)(2,1)S(1)}, bf16[2,256,128]{2,1,0:T(8,128)(2,1)S(1)}, u32[]{:S(2)}, u32[]{:S(2)}) collective-permute-start(bf16[2,256,128]{2,1,0:T(8,128)(2,1)S(1)} %get-tuple-element.61), channel_id=1, source_target_pairs={{0,2},{2,0},{4,6},{6,4},{8,10},{10,8},{12,14},{14,12},{1,3},{3,1},... | collective-permute-start | bytes 393224 | tf_op jit(solution)/shard_map/ppermute | solution.py:499
